TPU v7x, 32 devices: a whole 2x2x4 slice. The times are simulated.
32 devices in a mesh: grp: 2 (over x), rows: 16 (over z, y, core).
Axes of the slice: x: 2, y: 2, z: 4, core: 2. Of those that a mesh axis runs over, the one named last changes fastest.
Arguments:
- probes: float32 [64, 262144], P(None, ('grp', 'rows')), parts along dimension 1, may hold values from -6 to 6
- worker_len: int32 [32768], P(('grp', 'rows')), parts along dimension 0, may hold values from 1 to 8, as said below
- spell_to_slot: int32 [262144], P(('grp', 'rows')), parts along dimension 0, may hold values from 0 to 255, as said below
- slot_to_firm: int32 [8192], P(('grp', 'rows')), parts along dimension 0, may hold values from 0 to 1023, as said below
Outputs:
- demeaned: float32 [64, 262144], P(None, ('grp', 'rows')), parts along dimension 1
There are 2 independent parts, one for each index of `grp`. A program takes and returns all parts, laid end to end along the dimension named above; each array names one. Nothing has to cross between parts.
Inputs may be any that keep to these rules, and one draw needn't show every extreme that they name: `worker_len`: at least one worker of every device has 8 spells and one has a single spell. `spell_to_slot`: every device has a row of slot 0 and a row of slot 255. `slot_to_firm`: firms may repeat across slots and devices.
All inputs are finite; a program needn't handle non-finite values.
Results may differ from a plain program's by a relative error of at most 0.0001.
Values sent between devices are 32-bit elements; how exact they have to be, the bound alone decides.
No kernel may reach another device: no remote copies, remote signals or barrier semaphores. Data moves between devices by JAX's collectives and lax.ppermute only.
A program may use at most 64 MiB of HBM per device.

v0:
```python
import math

import jax
import jax.numpy as jnp
from jax import lax
from jax.sharding import PartitionSpec as P

FIRMS_PER_SHARD = 1024
SWEEPS = 2


def worker_step(block, valid_mask, row_len, table):
    columns, rows_dev = block.shape
    lanes = table.shape[0]
    flat = block.reshape(columns * rows_dev // lanes, lanes)
    totals = jnp.dot(flat, table, precision=lax.Precision.HIGHEST).reshape(columns, rows_dev)
    return (block - totals / row_len[None, :]) * valid_mask[None, :]


def slot_table(ids, slot_total):
    return (ids[:, None] == lax.broadcasted_iota(jnp.int32, (ids.shape[0], slot_total), 1)).astype(
        jnp.float32
    )


def slot_sums(block, spell_to_slot, slot_total, width):
    columns, rows_dev = block.shape
    turns = rows_dev // width

    def add_block(index, total):
        start = index * width
        piece = lax.dynamic_slice_in_dim(block, start, width, 1)
        ids = lax.dynamic_slice_in_dim(spell_to_slot, start, width, 0)
        return total + jnp.dot(piece, slot_table(ids, slot_total), precision=lax.Precision.HIGHEST)

    return lax.fori_loop(0, turns, add_block, jnp.zeros((columns, slot_total), jnp.float32))


def firm_step(block, slot_means, spell_to_slot, valid_mask, width):
    columns, rows_dev = block.shape
    slot_total = slot_means.shape[1]
    turns = rows_dev // width

    def take_block(index, result):
        start = index * width
        piece = lax.dynamic_slice_in_dim(block, start, width, 1)
        ids = lax.dynamic_slice_in_dim(spell_to_slot, start, width, 0)
        mask_piece = lax.dynamic_slice_in_dim(valid_mask, start, width, 0)
        spread = lax.dot_general(
            slot_means,
            slot_table(ids, slot_total),
            (((1,), (1,)), ((), ())),
            precision=lax.Precision.HIGHEST,
        )
        return lax.dynamic_update_slice_in_dim(
            result, (piece - spread) * mask_piece[None, :], start, 1
        )

    return lax.fori_loop(0, turns, take_block, jnp.zeros_like(block))


def owner_means(received, recv_firm, denom):
    table = (
        recv_firm[:, None]
        == lax.broadcasted_iota(jnp.int32, (recv_firm.shape[0], FIRMS_PER_SHARD), 1)
    ).astype(jnp.float32)
    sums = jnp.dot(received, table, precision=lax.Precision.HIGHEST)
    means = sums / denom[None, :]
    return lax.dot_general(means, table, (((1,), (1,)), ((), ())), precision=lax.Precision.HIGHEST)


def body(probes, worker_len, spell_to_slot, slot_to_firm):
    columns, rows_dev = probes.shape
    workers = worker_len.shape[0]
    shard_slots = rows_dev // workers
    slot_total = slot_to_firm.shape[0]
    width = math.gcd(rows_dev, 1024)
    lengths_wide = jnp.broadcast_to(worker_len[:, None], (workers, shard_slots))
    inside = lax.broadcasted_iota(jnp.int32, (workers, shard_slots), 1) < lengths_wide
    valid_mask = inside.astype(jnp.float32).reshape(rows_dev)
    row_len = lengths_wide.reshape(rows_dev).astype(jnp.float32)
    lane_index = lax.broadcasted_iota(jnp.int32, (128, 128), 0) // shard_slots
    lane_other = lax.broadcasted_iota(jnp.int32, (128, 128), 1) // shard_slots
    table = (lane_index == lane_other).astype(jnp.float32)
    slot_spell_count = slot_sums(valid_mask[None, :], spell_to_slot, slot_total, width)[0].astype(
        jnp.int32
    )
    recv_firm, recv_count = (
        lax.all_to_all(slot_to_firm, "rows", split_axis=0, concat_axis=0, tiled=True),
        lax.all_to_all(slot_spell_count, "rows", split_axis=0, concat_axis=0, tiled=True),
    )
    count = jax.ops.segment_sum(recv_count, recv_firm, FIRMS_PER_SHARD)
    denom = jnp.maximum(count.astype(jnp.float32), 1.0)
    demeaned = probes * valid_mask[None, :]
    for sweep in range(SWEEPS):
        demeaned = worker_step(demeaned, valid_mask, row_len, table)
        back = owner_means(
            lax.all_to_all(
                slot_sums(demeaned, spell_to_slot, slot_total, width),
                "rows",
                split_axis=1,
                concat_axis=1,
                tiled=True,
            ),
            recv_firm,
            denom,
        )
        slot_means = lax.all_to_all(back, "rows", split_axis=1, concat_axis=1, tiled=True)
        demeaned = firm_step(demeaned, slot_means, spell_to_slot, valid_mask, width)
    return demeaned


def solution(mesh):
    placed = (P(None, ("grp", "rows")), P(("grp", "rows")), P(("grp", "rows")), P(("grp", "rows")))
    return jax.shard_map(
        body, mesh=mesh, in_specs=placed, out_specs=P(None, ("grp", "rows")), check_vma=False
    )
```

profile of v0, /device:TPU:0, one launch (start us, length us, event | category | flops | bytes accessed | tf_op | source)
XLA Modules:
  0.0 154.6 jit_solution(1853574671404409794)
XLA Ops:
  1.4 7.4 %all-to-all-start.1 = ((s32[16,16,1]{1,2,0:T(1,128)}), s32[16,16,1]{1,2,0:T(1,128)S(1)}, u32[]{:S(2)}, u32[]{:S(2)}) async-start(s32[16,16,1]{1,2,0:T(1,128)} %bitcast.4), calls=%async_computation.1 | async-start | bytes 16384 | tf_op jit(solution)/shard_map/all_to_all | solution.py:89
  10.9 3.1 %broadcast_multiply_fusion = f32[64,8192]{1,0:T(8,128)} fusion(f32[64,8192]{1,0:T(8,128)} %param.14, f32[8192]{0:T(1024)S(1)} %reshape.100), kind=kLoop, calls=%fused_computation.37 | loop fusion | flops 524288 | bytes 4227072 | tf_op jit(solution)/shard_map/mul | solution.py:94
  14.0 1.7 %reshape.96 = f32[4096,128]{1,0:T(8,128)S(1)} reshape(f32[64,8192]{1,0:T(8,128)} %broadcast_multiply_fusion) | data formatting | bytes 4194304 | tf_op jit(solution)/shard_map/reshape | solution.py:15
  15.7 2.5 %fusion.26 = f32[4096,128]{1,0:T(8,128)} fusion(f32[4096,128]{1,0:T(8,128)S(1)} %reshape.96, s32[128]{0:T(128)S(1)} %get-tuple-element.582, s32[128]{0:T(128)S(1)} %get-tuple-element.583, pred[128]{0:T(512)(128)(4,1)S(1)} %compare_and_fusion), kind=kOutput, calls=%fused_computation.46 | convolution fusion | flops 805355520 | bytes 4195456 | tf_op jit(solution)/shard_map/dot_general | solution.py:16
  18.2 2.9 %reshape.97 = f32[64,8192]{1,0:T(8,128)} reshape(f32[4096,128]{1,0:T(8,128)} %fusion.26) | data formatting | bytes 4194304 | tf_op jit(solution)/shard_map/reshape | solution.py:16
  21.5 4.1 %while.71 = (s32[]{:T(128)}, f32[1,256]{1,0:T(1,128)S(1)}, f32[1,8192]{1,0:T(1,128)S(1)}, s32[8192]{0:T(1024)S(1)}, s32[]{:T(128)}, /*index=5*/s32[]{:T(128)}, s32[]{:T(128)}, s32[]{:T(128)}) while((s32[]{:T(128)}, f32[1,256]{1,0:T(1,128)S(1)}, f32[1,8192]{1,0:T(1,128)S(1)}, s32[8192]{0:T(1024)S(1)}, s32[]{:T(128)}, ...), condition=%wide.region_3.4_spmd.clone, body=%wide.region_2.3_spmd.clone.sunk | while | flops 3408391 | bytes 18581 | solution.py:36
  25.6 3.2 %subtract_multiply_fusion.1 = f32[64,8192]{1,0:T(8,128)} fusion(f32[64,8192]{1,0:T(8,128)} %reshape.97, f32[8192]{0:T(1024)S(1)} %convert_element_type.68, f32[8192]{0:T(1024)S(1)} %reshape.100, f32[64,8192]{1,0:T(8,128)S(1)} %copy-done), kind=kLoop, calls=%fused_computation.31 | loop fusion | flops 2097152 | bytes 6356992 | tf_op jit(solution)/shard_map/mul | solution.py:17
  29.6 6.0 %all-to-all-start.2 = ((s32[16,16,1]{1,2,0:T(1,128)}), s32[16,16,1]{1,2,0:T(1,128)S(1)}, u32[]{:S(2)}, u32[]{:S(2)}) async-start(s32[16,16,1]{1,2,0:T(1,128)} %convert_element_type.72), calls=%async_computation.2 | async-start | bytes 16384 | tf_op jit(solution)/shard_map/all_to_all | solution.py:90
  35.6 12.5 %while.70 = (s32[]{:T(128)}, f32[64,256]{1,0:T(8,128)S(1)}, f32[64,8192]{1,0:T(8,128)}, s32[8192]{0:T(1024)S(1)}, s32[]{:T(128)}, /*index=5*/s32[]{:T(128)}, s32[]{:T(128)}, s32[]{:T(128)}) while((s32[]{:T(128)}, f32[64,256]{1,0:T(8,128)S(1)}, f32[64,8192]{1,0:T(8,128)}, s32[8192]{0:T(1024)S(1)}, s32[]{:T(128)}, ...), condition=%wide.region_1.2_spmd.clone, body=%wide.region_0.1_spmd.clone.sunk | while | flops 201621504 | bytes 405653 | solution.py:36
  35.6 1.5 convolution_add_fusion.6
  37.2 1.5 convolution_add_fusion.6
  38.7 1.5 convolution_add_fusion.6
  40.3 1.5 convolution_add_fusion.6
  41.9 1.5 convolution_add_fusion.6
  50.2 6.0 %all-to-all-start = ((f32[16,1,1024]{2,1,0:T(1,128)}), f32[16,1,1024]{2,1,0:T(1,128)S(1)}, u32[]{:S(2)}, u32[]{:S(2)}) async-start(f32[16,1,1024]{2,1,0:T(1,128)} %reshape.137), calls=%async_computation | async-start | bytes 131072 | tf_op jit(solution)/shard_map/all_to_all | solution.py:98
  56.9 2.3 %scatter_custom_fusion = s32[1024]{0:T(1024)S(1)} fusion(s32[256]{0:T(256)S(1)} %eq.120, s32[256]{0:T(256)S(1)} %reshape.106, s32[]{:T(128)} %constant.172.clone.1), kind=kCustom, calls=%fused_computation.60 | custom fusion | flops 256 | bytes 4100 | tf_op jit(solution)/shard_map/scatter-add | solution.py:92
  59.3 3.8 %all-to-all-done = f32[16,1,1024]{2,1,0:T(1,128)S(1)} async-done(((f32[16,1,1024]{2,1,0:T(1,128)}), f32[16,1,1024]{2,1,0:T(1,128)S(1)}, u32[]{:S(2)}, u32[]{:S(2)}) %all-to-all-start) | async-done | bytes 65568 | tf_op jit(solution)/shard_map/all_to_all | solution.py:98
  66.5 3.5 %all-to-all-start.3 = ((f32[16,1,1024]{2,1,0:T(1,128)}), f32[16,1,1024]{2,1,0:T(1,128)S(1)}, u32[]{:S(2)}, u32[]{:S(2)}) async-start(f32[16,1,1024]{2,1,0:T(1,128)} %reshape.139), calls=%async_computation.3 | async-start | bytes 131072 | tf_op jit(solution)/shard_map/all_to_all | solution.py:108
  70.0 6.8 %all-to-all-done.3 = f32[16,1,1024]{2,1,0:T(1,128)S(1)} async-done(((f32[16,1,1024]{2,1,0:T(1,128)}), f32[16,1,1024]{2,1,0:T(1,128)S(1)}, u32[]{:S(2)}, u32[]{:S(2)}) %all-to-all-start.3) | async-done | bytes 65568 | tf_op jit(solution)/shard_map/all_to_all | solution.py:108
  77.9 13.7 %while.68 = (s32[]{:T(128)}, f32[64,8192]{1,0:T(8,128)S(1)}, f32[64,8192]{1,0:T(8,128)}, s32[8192]{0:T(1024)S(1)}, f32[64,256]{1,0:T(8,128)S(1)}, /*index=5*/f32...) while((s32[]{:T(128)}, f32[64,8192]{1,0:T(8,128)S(1)}, f32[64,8192]{1,0:T(8,128)}, ...), condition=%wide.region_6.7_spmd, body=%wide.region_5.6_spmd.sunk | while | flops 201719808 | bytes 614559 | solution.py:59
  78.0 1.7 %fusion.57 = f32[64,8192]{1,0:T(8,128)S(1)} fusion(f32[64,8192]{1,0:T(8,128)S(1)} %get-tuple-element.792, s32[]{:T(128)S(6)} %select_n.72, f32[64,256]{1,0:T(8,128)S(1)} %get-tuple-element.805, s32[1024]{0:T(1024)S(1)} %dynamic_slice.113, f32[64,8192]{1,0:T(8,128)} %get-tuple-element.803, f32[1024]{0:T(1024)S(1)} %dynamic_slice.114), kind=kOutput, calls=%fused_computation.4.clone.1 | convolution fusion | flops 201719808 | bytes 598020 | tf_op jit(solution)/shard_map/while/body/eval_jaxpr/dot_general | solution.py:49
  79.7 1.7 %fusion.57 = f32[64,8192]{1,0:T(8,128)S(1)} fusion(f32[64,8192]{1,0:T(8,128)S(1)} %get-tuple-element.792, s32[]{:T(128)S(6)} %select_n.72, f32[64,256]{1,0:T(8,128)S(1)} %get-tuple-element.805, s32[1024]{0:T(1024)S(1)} %dynamic_slice.113, f32[64,8192]{1,0:T(8,128)} %get-tuple-element.803, f32[1024]{0:T(1024)S(1)} %dynamic_slice.114), kind=kOutput, calls=%fused_computation.4.clone.1 | convolution fusion | flops 201719808 | bytes 598020 | tf_op jit(solution)/shard_map/while/body/eval_jaxpr/dot_general | solution.py:49
  81.4 1.7 %fusion.57 = f32[64,8192]{1,0:T(8,128)S(1)} fusion(f32[64,8192]{1,0:T(8,128)S(1)} %get-tuple-element.792, s32[]{:T(128)S(6)} %select_n.72, f32[64,256]{1,0:T(8,128)S(1)} %get-tuple-element.805, s32[1024]{0:T(1024)S(1)} %dynamic_slice.113, f32[64,8192]{1,0:T(8,128)} %get-tuple-element.803, f32[1024]{0:T(1024)S(1)} %dynamic_slice.114), kind=kOutput, calls=%fused_computation.4.clone.1 | convolution fusion | flops 201719808 | bytes 598020 | tf_op jit(solution)/shard_map/while/body/eval_jaxpr/dot_general | solution.py:49
  83.1 1.7 %fusion.57 = f32[64,8192]{1,0:T(8,128)S(1)} fusion(f32[64,8192]{1,0:T(8,128)S(1)} %get-tuple-element.792, s32[]{:T(128)S(6)} %select_n.72, f32[64,256]{1,0:T(8,128)S(1)} %get-tuple-element.805, s32[1024]{0:T(1024)S(1)} %dynamic_slice.113, f32[64,8192]{1,0:T(8,128)} %get-tuple-element.803, f32[1024]{0:T(1024)S(1)} %dynamic_slice.114), kind=kOutput, calls=%fused_computation.4.clone.1 | convolution fusion | flops 201719808 | bytes 598020 | tf_op jit(solution)/shard_map/while/body/eval_jaxpr/dot_general | solution.py:49
  84.8 1.7 %fusion.57 = f32[64,8192]{1,0:T(8,128)S(1)} fusion(f32[64,8192]{1,0:T(8,128)S(1)} %get-tuple-element.792, s32[]{:T(128)S(6)} %select_n.72, f32[64,256]{1,0:T(8,128)S(1)} %get-tuple-element.805, s32[1024]{0:T(1024)S(1)} %dynamic_slice.113, f32[64,8192]{1,0:T(8,128)} %get-tuple-element.803, f32[1024]{0:T(1024)S(1)} %dynamic_slice.114), kind=kOutput, calls=%fused_computation.4.clone.1 | convolution fusion | flops 201719808 | bytes 598020 | tf_op jit(solution)/shard_map/while/body/eval_jaxpr/dot_general | solution.py:49
  86.5 1.7 %fusion.57 = f32[64,8192]{1,0:T(8,128)S(1)} fusion(f32[64,8192]{1,0:T(8,128)S(1)} %get-tuple-element.792, s32[]{:T(128)S(6)} %select_n.72, f32[64,256]{1,0:T(8,128)S(1)} %get-tuple-element.805, s32[1024]{0:T(1024)S(1)} %dynamic_slice.113, f32[64,8192]{1,0:T(8,128)} %get-tuple-element.803, f32[1024]{0:T(1024)S(1)} %dynamic_slice.114), kind=kOutput, calls=%fused_computation.4.clone.1 | convolution fusion | flops 201719808 | bytes 598020 | tf_op jit(solution)/shard_map/while/body/eval_jaxpr/dot_general | solution.py:49
  88.2 1.7 %fusion.57 = f32[64,8192]{1,0:T(8,128)S(1)} fusion(f32[64,8192]{1,0:T(8,128)S(1)} %get-tuple-element.792, s32[]{:T(128)S(6)} %select_n.72, f32[64,256]{1,0:T(8,128)S(1)} %get-tuple-element.805, s32[1024]{0:T(1024)S(1)} %dynamic_slice.113, f32[64,8192]{1,0:T(8,128)} %get-tuple-element.803, f32[1024]{0:T(1024)S(1)} %dynamic_slice.114), kind=kOutput, calls=%fused_computation.4.clone.1 | convolution fusion | flops 201719808 | bytes 598020 | tf_op jit(solution)/shard_map/while/body/eval_jaxpr/dot_general | solution.py:49
  90.0 1.7 %fusion.57 = f32[64,8192]{1,0:T(8,128)S(1)} fusion(f32[64,8192]{1,0:T(8,128)S(1)} %get-tuple-element.792, s32[]{:T(128)S(6)} %select_n.72, f32[64,256]{1,0:T(8,128)S(1)} %get-tuple-element.805, s32[1024]{0:T(1024)S(1)} %dynamic_slice.113, f32[64,8192]{1,0:T(8,128)} %get-tuple-element.803, f32[1024]{0:T(1024)S(1)} %dynamic_slice.114), kind=kOutput, calls=%fused_computation.4.clone.1 | convolution fusion | flops 201719808 | bytes 598020 | tf_op jit(solution)/shard_map/while/body/eval_jaxpr/dot_general | solution.py:49
  93.1 4.1 %fusion.25 = f32[4096,128]{1,0:T(8,128)} fusion(f32[4096,128]{1,0:T(8,128)} %reshape.98, s32[128]{0:T(128)S(1)} %get-tuple-element.582, s32[128]{0:T(128)S(1)} %get-tuple-element.583, pred[128]{0:T(512)(128)(4,1)S(1)} %compare_and_fusion), kind=kOutput, calls=%fused_computation.45 | convolution fusion | flops 805355520 | bytes 4195456 | tf_op jit(solution)/shard_map/dot_general | solution.py:16
  97.2 2.7 %reshape.99 = f32[64,8192]{1,0:T(8,128)} reshape(f32[4096,128]{1,0:T(8,128)} %fusion.25) | data formatting | bytes 4194304 | tf_op jit(solution)/shard_map/reshape | solution.py:16
  99.9 3.2 %subtract_multiply_fusion = f32[64,8192]{1,0:T(8,128)} fusion(f32[64,8192]{1,0:T(8,128)S(1)} %get-tuple-element.462, f32[64,8192]{1,0:T(8,128)} %reshape.99, f32[8192]{0:T(1024)S(1)} %convert_element_type.68, f32[8192]{0:T(1024)S(1)} %get-tuple-element.877), kind=kLoop, calls=%fused_computation.30 | loop fusion | flops 1572864 | bytes 6356992 | tf_op jit(solution)/shard_map/mul | solution.py:17
  103.1 12.5 %while.72 = (s32[]{:T(128)}, f32[64,256]{1,0:T(8,128)S(1)}, f32[64,8192]{1,0:T(8,128)}, s32[8192]{0:T(1024)S(1)}, s32[]{:T(128)}, /*index=5*/s32[]{:T(128)}, s32[]{:T(128)}, s32[]{:T(128)}) while((s32[]{:T(128)}, f32[64,256]{1,0:T(8,128)S(1)}, f32[64,8192]{1,0:T(8,128)}, s32[8192]{0:T(1024)S(1)}, s32[]{:T(128)}, ...), condition=%wide.region_8.9_spmd.clone, body=%wide.region_7.8_spmd.clone.sunk | while | flops 201621504 | bytes 405653 | solution.py:36
  106.2 1.5 convolution_add_fusion.8
  107.8 1.5 convolution_add_fusion.8
  110.9 1.5 convolution_add_fusion.8
  112.5 1.5 convolution_add_fusion.8
  115.8 9.5 %all_to_all.66 = f32[16,1,1024]{2,1,0:T(1,128)S(1)} all-to-all(f32[16,1,1024]{2,1,0:T(1,128)S(1)} %reshape.141), channel_id=1, replica_groups=mesh['grp'=2,'rows'=16] {'rows'}, dimensions={0} | all-to-all | bytes 131072 | tf_op jit(solution)/shard_map/all_to_all | solution.py:98
  128.2 3.5 %all-to-all-start.5 = ((f32[16,1,1024]{2,1,0:T(1,128)}), f32[16,1,1024]{2,1,0:T(1,128)S(1)}, u32[]{:S(2)}, u32[]{:S(2)}) async-start(f32[16,1,1024]{2,1,0:T(1,128)} %reshape.143), calls=%async_computation.5 | async-start | bytes 131072 | tf_op jit(solution)/shard_map/all_to_all | solution.py:108
  131.7 6.9 %all-to-all-done.5 = f32[16,1,1024]{2,1,0:T(1,128)S(1)} async-done(((f32[16,1,1024]{2,1,0:T(1,128)}), f32[16,1,1024]{2,1,0:T(1,128)S(1)}, u32[]{:S(2)}, u32[]{:S(2)}) %all-to-all-start.5) | async-done | bytes 65568 | tf_op jit(solution)/shard_map/all_to_all | solution.py:108
  139.6 13.7 %while.69 = (s32[]{:T(128)}, f32[64,8192]{1,0:T(8,128)S(1)}, f32[64,8192]{1,0:T(8,128)}, s32[8192]{0:T(1024)S(1)}, f32[64,256]{1,0:T(8,128)S(1)}, /*index=5*/f32...) while((s32[]{:T(128)}, f32[64,8192]{1,0:T(8,128)S(1)}, f32[64,8192]{1,0:T(8,128)}, ...), condition=%wide.region_10.11_spmd, body=%wide.region_9.10_spmd.sunk | while | flops 201719808 | bytes 614559 | solution.py:59
  139.7 1.7 %fusion.59 = f32[64,8192]{1,0:T(8,128)S(1)} fusion(f32[64,8192]{1,0:T(8,128)S(1)} %get-tuple-element.846, s32[]{:T(128)S(6)} %select_n.73, f32[64,256]{1,0:T(8,128)S(1)} %get-tuple-element.859, s32[1024]{0:T(1024)S(1)} %dynamic_slice.116, f32[64,8192]{1,0:T(8,128)} %get-tuple-element.857, f32[1024]{0:T(1024)S(1)} %dynamic_slice.117), kind=kOutput, calls=%fused_computation.10.clone.1 | convolution fusion | flops 201719808 | bytes 598020 | tf_op jit(solution)/shard_map/while/body/eval_jaxpr/dot_general | solution.py:49
  141.4 1.7 %fusion.59 = f32[64,8192]{1,0:T(8,128)S(1)} fusion(f32[64,8192]{1,0:T(8,128)S(1)} %get-tuple-element.846, s32[]{:T(128)S(6)} %select_n.73, f32[64,256]{1,0:T(8,128)S(1)} %get-tuple-element.859, s32[1024]{0:T(1024)S(1)} %dynamic_slice.116, f32[64,8192]{1,0:T(8,128)} %get-tuple-element.857, f32[1024]{0:T(1024)S(1)} %dynamic_slice.117), kind=kOutput, calls=%fused_computation.10.clone.1 | convolution fusion | flops 201719808 | bytes 598020 | tf_op jit(solution)/shard_map/while/body/eval_jaxpr/dot_general | solution.py:49
  143.1 1.7 %fusion.59 = f32[64,8192]{1,0:T(8,128)S(1)} fusion(f32[64,8192]{1,0:T(8,128)S(1)} %get-tuple-element.846, s32[]{:T(128)S(6)} %select_n.73, f32[64,256]{1,0:T(8,128)S(1)} %get-tuple-element.859, s32[1024]{0:T(1024)S(1)} %dynamic_slice.116, f32[64,8192]{1,0:T(8,128)} %get-tuple-element.857, f32[1024]{0:T(1024)S(1)} %dynamic_slice.117), kind=kOutput, calls=%fused_computation.10.clone.1 | convolution fusion | flops 201719808 | bytes 598020 | tf_op jit(solution)/shard_map/while/body/eval_jaxpr/dot_general | solution.py:49
  144.8 1.7 %fusion.59 = f32[64,8192]{1,0:T(8,128)S(1)} fusion(f32[64,8192]{1,0:T(8,128)S(1)} %get-tuple-element.846, s32[]{:T(128)S(6)} %select_n.73, f32[64,256]{1,0:T(8,128)S(1)} %get-tuple-element.859, s32[1024]{0:T(1024)S(1)} %dynamic_slice.116, f32[64,8192]{1,0:T(8,128)} %get-tuple-element.857, f32[1024]{0:T(1024)S(1)} %dynamic_slice.117), kind=kOutput, calls=%fused_computation.10.clone.1 | convolution fusion | flops 201719808 | bytes 598020 | tf_op jit(solution)/shard_map/while/body/eval_jaxpr/dot_general | solution.py:49
  146.5 1.7 %fusion.59 = f32[64,8192]{1,0:T(8,128)S(1)} fusion(f32[64,8192]{1,0:T(8,128)S(1)} %get-tuple-element.846, s32[]{:T(128)S(6)} %select_n.73, f32[64,256]{1,0:T(8,128)S(1)} %get-tuple-element.859, s32[1024]{0:T(1024)S(1)} %dynamic_slice.116, f32[64,8192]{1,0:T(8,128)} %get-tuple-element.857, f32[1024]{0:T(1024)S(1)} %dynamic_slice.117), kind=kOutput, calls=%fused_computation.10.clone.1 | convolution fusion | flops 201719808 | bytes 598020 | tf_op jit(solution)/shard_map/while/body/eval_jaxpr/dot_general | solution.py:49
  148.2 1.7 %fusion.59 = f32[64,8192]{1,0:T(8,128)S(1)} fusion(f32[64,8192]{1,0:T(8,128)S(1)} %get-tuple-element.846, s32[]{:T(128)S(6)} %select_n.73, f32[64,256]{1,0:T(8,128)S(1)} %get-tuple-element.859, s32[1024]{0:T(1024)S(1)} %dynamic_slice.116, f32[64,8192]{1,0:T(8,128)} %get-tuple-element.857, f32[1024]{0:T(1024)S(1)} %dynamic_slice.117), kind=kOutput, calls=%fused_computation.10.clone.1 | convolution fusion | flops 201719808 | bytes 598020 | tf_op jit(solution)/shard_map/while/body/eval_jaxpr/dot_general | solution.py:49
  149.9 1.7 %fusion.59 = f32[64,8192]{1,0:T(8,128)S(1)} fusion(f32[64,8192]{1,0:T(8,128)S(1)} %get-tuple-element.846, s32[]{:T(128)S(6)} %select_n.73, f32[64,256]{1,0:T(8,128)S(1)} %get-tuple-element.859, s32[1024]{0:T(1024)S(1)} %dynamic_slice.116, f32[64,8192]{1,0:T(8,128)} %get-tuple-element.857, f32[1024]{0:T(1024)S(1)} %dynamic_slice.117), kind=kOutput, calls=%fused_computation.10.clone.1 | convolution fusion | flops 201719808 | bytes 598020 | tf_op jit(solution)/shard_map/while/body/eval_jaxpr/dot_general | solution.py:49
  151.6 1.7 %fusion.59 = f32[64,8192]{1,0:T(8,128)S(1)} fusion(f32[64,8192]{1,0:T(8,128)S(1)} %get-tuple-element.846, s32[]{:T(128)S(6)} %select_n.73, f32[64,256]{1,0:T(8,128)S(1)} %get-tuple-element.859, s32[1024]{0:T(1024)S(1)} %dynamic_slice.116, f32[64,8192]{1,0:T(8,128)} %get-tuple-element.857, f32[1024]{0:T(1024)S(1)} %dynamic_slice.117), kind=kOutput, calls=%fused_computation.10.clone.1 | convolution fusion | flops 201719808 | bytes 598020 | tf_op jit(solution)/shard_map/while/body/eval_jaxpr/dot_general | solution.py:49
  (123 shorter events, 33.9 us)
Async XLA Ops:
  1.4 28.2 %all-to-all-start.1 = ((s32[16,16,1]{1,2,0:T(1,128)}), s32[16,16,1]{1,2,0:T(1,128)S(1)}, u32[]{:S(2)}, u32[]{:S(2)}) async-start(s32[16,16,1]{1,2,0:T(1,128)} %bitcast.4), calls=%async_computation.1 | async-start | bytes 16384 | tf_op jit(solution)/shard_map/all_to_all | solution.py:89
  18.2 3.4 %copy-start.2 = (s32[8192]{0:T(1024)S(1)}, s32[8192]{0:T(1024)}, u32[]{:S(2)}) copy-start(s32[8192]{0:T(1024)} %param.16) | copy-start | bytes 98308
  18.2 7.4 %copy-start = (f32[64,8192]{1,0:T(8,128)S(1)}, f32[64,8192]{1,0:T(8,128)}, u32[]{:S(2)}) copy-start(f32[64,8192]{1,0:T(8,128)} %param.14) | copy-start | bytes 6291460
  29.6 20.7 %all-to-all-start.2 = ((s32[16,16,1]{1,2,0:T(1,128)}), s32[16,16,1]{1,2,0:T(1,128)S(1)}, u32[]{:S(2)}, u32[]{:S(2)}) async-start(s32[16,16,1]{1,2,0:T(1,128)} %convert_element_type.72), calls=%async_computation.2 | async-start | bytes 16384 | tf_op jit(solution)/shard_map/all_to_all | solution.py:90
  50.2 12.9 %all-to-all-start = ((f32[16,1,1024]{2,1,0:T(1,128)}), f32[16,1,1024]{2,1,0:T(1,128)S(1)}, u32[]{:S(2)}, u32[]{:S(2)}) async-start(f32[16,1,1024]{2,1,0:T(1,128)} %reshape.137), calls=%async_computation | async-start | bytes 131072 | tf_op jit(solution)/shard_map/all_to_all | solution.py:98
  66.5 10.4 %all-to-all-start.3 = ((f32[16,1,1024]{2,1,0:T(1,128)}), f32[16,1,1024]{2,1,0:T(1,128)S(1)}, u32[]{:S(2)}, u32[]{:S(2)}) async-start(f32[16,1,1024]{2,1,0:T(1,128)} %reshape.139), calls=%async_computation.3 | async-start | bytes 131072 | tf_op jit(solution)/shard_map/all_to_all | solution.py:108
  128.2 10.4 %all-to-all-start.5 = ((f32[16,1,1024]{2,1,0:T(1,128)}), f32[16,1,1024]{2,1,0:T(1,128)S(1)}, u32[]{:S(2)}, u32[]{:S(2)}) async-start(f32[16,1,1024]{2,1,0:T(1,128)} %reshape.143), calls=%async_computation.5 | async-start | bytes 131072 | tf_op jit(solution)/shard_map/all_to_all | solution.py:108
  153.3 1.3 copy-start.1
where the time goes:
time: 156 us; the launch traced here: 155 us
  matrix products  63.7 us (41%)
  starting transfers between devices  26.4 us (17%)
  local copies, waits for them, and re-layouts  18.2 us (12%)
  other arithmetic  17.8 us (11%)
  waiting for transfers between devices  17.5 us (11%)
  blocking collectives  9.48 us (6%)
    dot_general x24, matrix products, add_block(): jnp.dot(piece, slot_table(ids, slot_total), precision=lax.Precision.HIGHEST)  28.3 us
    dot_general x16, matrix products, take_block(): lax.dot_general(slot_means, slot_table(ids, slot_total), (((1,), (1,)), (...  26.5 us
    all_to_all x2, waiting for transfers between devices, body(): lax.all_to_all(back, 'rows', split_axis=1, concat_axis=1, tiled=True)  13.7 us
    all_to_all x1, blocking collectives, body(): lax.all_to_all(slot_sums(demeaned, spell_to_slot, slot_total, width), 'ro...  9.48 us
    all_to_all x1, starting transfers between devices, body(): lax.all_to_all(slot_to_firm, 'rows', split_axis=0, concat_axis=0, tiled=T...  7.39 us
    all_to_all x2, starting transfers between devices, body(): lax.all_to_all(back, 'rows', split_axis=1, concat_axis=1, tiled=True)  6.99 us
    dot_general x2, matrix products, worker_step(): jnp.dot(flat, table, precision=lax.Precision.HIGHEST)  6.53 us
    mul x2, other arithmetic, worker_step(): return (block - totals / row_len[None, :]) * valid_mask[None, :]  6.41 us
  transfers between devices with their start and end apart: 5, of which 3 were waited for; matrix products, arithmetic and copies ran while one was open for 25% of the time, Pallas kernels for 0%

commit v1 on v0

v1 whole, which is shorter than its diff:
```python
import functools

import jax
import jax.numpy as jnp
from jax import lax
from jax.experimental import pallas as pl
from jax.experimental.pallas import tpu as pltpu
from jax.sharding import PartitionSpec as P

FIRMS_PER_SHARD = 1024
LANES = 128
BLOCK = 1024
VMEM_BYTES = 48 * 1024 * 1024
F32, BF16 = jnp.float32, jnp.bfloat16
NT = (((1,), (1,)), ((), ()))
NN = (((1,), (0,)), ((), ()))


def dot(a, b, dims=NN):
    return lax.dot_general(a, b, dims, preferred_element_type=F32)


def iota(shape, dim):
    return lax.broadcasted_iota(jnp.int32, shape, dim)


def split(x):
    hi = x.astype(BF16)
    return hi, (x - hi.astype(F32)).astype(BF16)


def row(ref, block, size):
    per = size // LANES
    return jnp.concatenate([ref[block * per + k : block * per + k + 1, :] for k in range(per)], axis=1)


def one_hot(ids, slots):
    return (iota((slots, ids.shape[1]), 0) == ids).astype(F32).astype(BF16)


def same_worker(pad, width):
    return (iota((width, width), 0) // pad == iota((width, width), 1) // pad).astype(F32).astype(BF16)


def by_worker(x, table):
    rows, width = x.shape
    hi, lo = split(x)
    both = jnp.concatenate([hi, lo], axis=0)
    step = table.shape[0]
    total = jnp.concatenate([dot(both[:, k : k + step], table) for k in range(0, width, step)], axis=1)
    return total[:rows] + total[rows:]


def fold(x):
    return x + pltpu.roll(x, x.shape[1] // 2, axis=1)


def halves(x):
    hi, lo = split(x)
    return jnp.where(iota(x.shape, 1) < x.shape[1] // 2, hi.astype(F32), lo.astype(F32))


def sums_kernel(pad, cap, probes, lengths, ids, firms, send, own, own_count, mask_ids, weight, valid, x, acc, sems):
    blocks = x.shape[1] // BLOCK
    slots = own.shape[0]
    copies = [
        pltpu.make_async_copy(probes.at[:, pl.ds(b * BLOCK, BLOCK)], x.at[:, pl.ds(b * BLOCK, BLOCK)], sems.at[b])
        for b in range(blocks)
    ]
    for copy in copies:
        copy.start()
    total_rows = ids.shape[0]
    here = iota((total_rows, LANES), 0)
    lane = iota((total_rows, LANES), 1)
    wide = jnp.broadcast_to(
        lengths[...].astype(F32)[:, None, :], (lengths.shape[0], total_rows // lengths.shape[0], LANES)
    ).reshape(total_rows, LANES)
    per = LANES // pad
    wide = jnp.where(lane // per == here % pad, wide, 0.0).astype(BF16)
    spread = (iota((LANES, LANES), 0) % per == iota((LANES, LANES), 1) // pad).astype(F32).astype(BF16)
    row_len = dot(wide, spread)
    inside = (lane % pad).astype(F32) < row_len
    valid[...] = jnp.where(inside, 1.0, 0.0)
    weight[...] = jnp.where(inside, 1.0 / row_len, 0.0)
    mask_ids[...] = jnp.where(inside, ids[...], -1)

    table = same_worker(pad, 256)
    for b in range(blocks):
        copies[b].wait()
        ok = row(valid, b, BLOCK)
        x0 = x[:, b * BLOCK : (b + 1) * BLOCK] * ok
        x1 = x0 - by_worker(x0, table) * row(weight, b, BLOCK)
        hi, lo = split(x1)
        counted = jnp.broadcast_to(ok, (16, BLOCK)).astype(BF16)
        data = jnp.concatenate([hi, lo, counted], axis=0)
        part = dot(one_hot(row(mask_ids, b, BLOCK), slots), data, NT)
        if b == 0:
            acc[...] = part
        else:
            acc[...] += part
    both = fold(acc[:, :LANES])
    own[...] = both
    count = jnp.broadcast_to(acc[:, LANES : LANES + 1], (slots, LANES))
    own_count[...] = count
    half = slots // 2
    send[:half] = jnp.where(iota((half, LANES), 1) < LANES // 2, both[:half], both[half:])
    tiles = slots // LANES
    slot = iota((tiles, LANES), 0) * LANES + iota((tiles, LANES), 1)
    keys = ((slot // cap) * FIRMS_PER_SHARD + firms[...]).astype(F32)
    send[half : half + tiles] = keys
    for k in range(tiles):
        send[half + tiles + k : half + tiles + k + 1] = count[k * LANES : (k + 1) * LANES].T[:1]


def worker_kernel(pad, lengths, mask_ids, out):
    slots = out.shape[1]
    workers = lengths.shape[0] * LANES
    group = 256
    rows_group = group * pad
    pick = (iota((rows_group, group), 0) // pad == iota((rows_group, group), 1)).astype(F32).astype(BF16)
    total = jnp.zeros((2 * slots, slots), F32)
    for g in range(workers // group):
        counts = dot(one_hot(row(mask_ids, g, rows_group), slots), pick)
        inverse = 1.0 / row(lengths, g, group).astype(F32)
        hi, lo = split(counts * inverse)
        total += dot(jnp.concatenate([hi, lo], axis=0), counts.astype(BF16), NT)
    hi, lo = split(total[:slots] + total[slots:])
    out[:slots] = hi
    out[slots:] = lo


def column(ref, tiles):
    return jnp.concatenate([jnp.broadcast_to(ref[k : k + 1, :], (LANES, LANES)).T for k in range(tiles)], axis=0)


def own_keys(firms, cap):
    tiles = firms.shape[0]
    slots = tiles * LANES
    return (iota((slots, LANES), 0) // cap * FIRMS_PER_SHARD).astype(F32) + column(firms[...].astype(F32), tiles)


def firm_sums(n, received, info, mine, tiles, count=None):
    slots = tiles * LANES
    half = slots // 2
    rows, info_rows = received.shape[0] // n, info.shape[0] // n
    left = iota((half, LANES), 1) < LANES // 2

    def from_device(d, carry):
        total, count = carry
        start = pl.multiple_of(d * rows, 8)
        about = info[pl.ds(pl.multiple_of(d * info_rows, 8), info_rows), :]
        match = []
        for k in range(tiles):
            same = mine == about[k : k + 1]
            if count is not None:
                count += jnp.where(same, about[tiles + k : tiles + k + 1], 0.0)
            match.append(same.astype(F32).astype(BF16))
        block = received[pl.ds(start, half), :]
        turned = pltpu.roll(block, LANES // 2, axis=1)
        data = jnp.concatenate(
            [halves(jnp.where(left, block, turned)), halves(jnp.where(left, turned, block))], axis=0
        ).astype(BF16)
        return total + dot(jnp.concatenate(match, axis=1), data), count

    total, count = lax.fori_loop(0, n, from_device, (jnp.zeros((slots, LANES), F32), count), unroll=4)
    return fold(total), count


def means_kernel(n, cap, received, firms, own, own_count, pairs, mean, send, inverse, info):
    tiles = firms.shape[0]
    slots = tiles * LANES
    half = slots // 2
    rows, info_rows = received.shape[0] // n, info.shape[0] // n
    for d in range(n):
        info[d * info_rows : (d + 1) * info_rows] = received[d * rows + half : (d + 1) * rows]
    total, count = firm_sums(n, received, info, own_keys(firms, cap), tiles, jnp.zeros((slots, LANES), F32))
    scale = 1.0 / jnp.maximum(jnp.sum(count, axis=1, keepdims=True), 1.0)
    inverse[...] = jnp.broadcast_to(scale, (slots, LANES))
    found = total * scale
    mean[...] = found
    change = dot(pairs[...], halves(found).astype(BF16))
    new = own[...] - own_count[...] * found + fold(change[:slots] + change[slots:])
    left = iota((half, LANES), 1) < LANES // 2
    send[...] = jnp.where(left, new[:half], new[half:])


def column_copies(source, target, sems):
    width = source.shape[1]
    cuts = [pl.ds(start, BLOCK) for start in range(0, width, BLOCK)]
    return [pltpu.make_async_copy(source.at[:, cut], target.at[:, cut], sems.at[b]) for b, cut in enumerate(cuts)]


def take(parts, ids, slots):
    spread = dot(parts, one_hot(ids, slots))
    columns = parts.shape[0] // 2
    return spread[:columns] + spread[columns:]


def first_kernel(pad, probes, mean, mask_ids, weight, out, x, y, in_sems, out_sems):
    ins, outs = column_copies(probes, x, in_sems), column_copies(y, out, out_sems)
    for copy in ins:
        copy.start()
    slots = mean.shape[0]
    parts = halves(mean[...]).T.astype(BF16)
    table = same_worker(pad, 256)
    for b in range(len(ins)):
        ids = row(mask_ids, b, BLOCK)
        spread = take(parts, ids, slots)
        ins[b].wait()
        rest = jnp.where(ids >= 0, x[:, b * BLOCK : (b + 1) * BLOCK] - spread, 0.0)
        y[:, b * BLOCK : (b + 1) * BLOCK] = rest - by_worker(rest, table) * row(weight, b, BLOCK)
        outs[b].start()
    for copy in outs:
        copy.wait()


def last_kernel(n, cap, received, before, firms, info, inverse, mask_ids, out, x, y, in_sems, out_sems):
    ins, outs = column_copies(before, x, in_sems), column_copies(y, out, out_sems)
    for copy in ins:
        copy.start()
    tiles = firms.shape[0]
    slots = tiles * LANES
    total, _ = firm_sums(n, received, info, own_keys(firms, cap), tiles)
    parts = halves(total * inverse[...]).T.astype(BF16)
    for b in range(len(ins)):
        spread = take(parts, row(mask_ids, b, BLOCK), slots)
        ins[b].wait()
        y[:, b * BLOCK : (b + 1) * BLOCK] = x[:, b * BLOCK : (b + 1) * BLOCK] - spread
        outs[b].start()
    for copy in outs:
        copy.wait()


def call(kernel, out_shape, in_specs, out_specs, scratch, flops, moved):
    return pl.pallas_call(
        kernel,
        out_shape=out_shape,
        in_specs=in_specs,
        out_specs=out_specs,
        scratch_shapes=scratch,
        compiler_params=pltpu.CompilerParams(vmem_limit_bytes=VMEM_BYTES),
        cost_estimate=pl.CostEstimate(flops=flops, bytes_accessed=moved, transcendentals=0),
    )


def body(probes, worker_len, spell_to_slot, slot_to_firm, *, n):
    columns, rows_dev = probes.shape
    workers = worker_len.shape[0]
    pad = rows_dev // workers
    slots = slot_to_firm.shape[0]
    cap = slots // n
    half = slots // 2
    tiles = slots // LANES
    info_rows = -(-2 * tiles // 8) * 8
    blocks = rows_dev // BLOCK
    vmem, anywhere = pl.BlockSpec(memory_space=pltpu.VMEM), pl.BlockSpec(memory_space=pl.ANY)
    lengths = worker_len.reshape(workers // LANES, LANES)
    ids = spell_to_slot.reshape(rows_dev // LANES, LANES)
    firms = slot_to_firm.reshape(tiles, LANES)
    array = jax.ShapeDtypeStruct
    of_rows = (rows_dev // LANES, LANES)
    work = 2 * rows_dev * slots * 2 * columns
    sems = pltpu.SemaphoreType.DMA((blocks,))
    whole = pltpu.VMEM((columns, rows_dev), F32)

    send, own, own_count, mask_ids, weight = call(
        functools.partial(sums_kernel, pad, cap),
        [
            array((half + info_rows, LANES), F32),
            array((slots, LANES), F32),
            array((slots, LANES), F32),
            array(of_rows, jnp.int32),
            array(of_rows, F32),
        ],
        [anywhere, vmem, vmem, vmem],
        [vmem] * 5,
        [pltpu.VMEM(of_rows, F32), whole, pltpu.VMEM((slots, 2 * columns + 16), F32), sems],
        2 * work,
        4 * columns * rows_dev,
    )(probes, lengths, ids, firms)
    received = lax.all_gather(send, "rows", axis=0, tiled=True)
    pairs = call(
        functools.partial(worker_kernel, pad),
        array((2 * slots, slots), BF16),
        [vmem, vmem],
        vmem,
        [],
        2 * work,
        4 * slots * slots,
    )(lengths, mask_ids)
    mean, again, inverse, info = call(
        functools.partial(means_kernel, n, cap),
        [
            array((slots, LANES), F32),
            array((half, LANES), F32),
            array((slots, LANES), F32),
            array((n * info_rows, LANES), F32),
        ],
        [vmem] * 5,
        [vmem] * 4,
        [],
        work // 4,
        received.size * 4,
    )(received, firms, own, own_count, pairs)
    second = lax.all_gather(again, "rows", axis=0, tiled=True)
    before = call(
        functools.partial(first_kernel, pad),
        array((columns, rows_dev), F32),
        [anywhere, vmem, vmem, vmem],
        anywhere,
        [whole, whole, sems, sems],
        2 * work,
        8 * columns * rows_dev,
    )(probes, mean, mask_ids, weight)
    return call(
        functools.partial(last_kernel, n, cap),
        array((columns, rows_dev), F32),
        [vmem, anywhere, vmem, vmem, vmem, vmem],
        anywhere,
        [whole, whole, sems, sems],
        work,
        8 * columns * rows_dev,
    )(second, before, firms, info, inverse, mask_ids)


def solution(mesh):
    placed = (P(None, ("grp", "rows")), P(("grp", "rows")), P(("grp", "rows")), P(("grp", "rows")))
    return jax.shard_map(
        functools.partial(body, n=mesh.shape["rows"]),
        mesh=mesh,
        in_specs=placed,
        out_specs=P(None, ("grp", "rows")),
        check_vma=False,
    )
```

time: 156 us -> 112 us (0.72)
  matrix products: 63.7 us -> 0 us
  waiting for transfers between devices: 17.5 us -> 69.6 us
  starting transfers between devices: 26.4 us -> 0.04 us
  Pallas kernels: 0 us -> 20.6 us
  other arithmetic: 17.8 us -> 0 us
  between operations: 0.28 us -> 13.5 us
  local copies, waits for them, and re-layouts: 18.2 us -> 7.79 us
  blocking collectives: 9.48 us -> 0 us
    all_gather x0 -> x2, waiting for transfers between devices: none -> 69.5 us  [the longest x1 38.4 us: body(): received = lax.all_gather(send, 'rows', axis=0, tiled=True)]
    dot_general x46 -> x0, matrix products: 63.7 us -> none  [the longest x24 28.3 us: add_block(): jnp.dot(piece, slot_table(ids, slot_total), precision=lax.Precision.HIGHEST)]
    all_to_all x5 -> x0, starting transfers between devices: 26.4 us -> none  [the longest x1 7.39 us: body(): lax.all_to_all(slot_to_firm, 'rows', split_axis=0, concat_axis=0, tiled=T...]
    pallas_call x0 -> x5, Pallas kernels: none -> 20.6 us  [the longest x1 5.86 us: body(): call(functools.partial(sums_kernel, pad, cap), [array((half + info_rows,...]
    all_to_all x5 -> x0, waiting for transfers between devices: 17.5 us -> none  [the longest x2 13.7 us: body(): lax.all_to_all(back, 'rows', split_axis=1, concat_axis=1, tiled=True)]
    all_to_all x1 -> x0, blocking collectives: 9.48 us -> none  [body(): lax.all_to_all(slot_sums(demeaned, spell_to_slot, slot_total, width), 'ro...]
    mul x3 -> x0, other arithmetic: 9.47 us -> none  [the longest x2 6.41 us: worker_step(): return (block - totals / row_len[None, :]) * valid_mask[None, :]]
    reshape x4 -> x0, local copies, waits for them, and re-layouts: 8.85 us -> none  [the longest x2 5.65 us: worker_step(): jnp.dot(flat, table, precision=lax.Precision.HIGHEST)]
  transfers between devices with their start and end apart: 5 -> 2, of which waited for: 3 -> 2; matrix products, arithmetic and copies ran while one was open for 25% -> 0% of each run, Pallas kernels for 0% -> 6%
where the time goes in v1:
time: 112 us; the launch traced here: 111 us
  waiting for transfers between devices  69.6 us (62%)
  Pallas kernels  20.6 us (18%)
  between operations  13.5 us (12%)
  local copies, waits for them, and re-layouts  7.79 us (7%)
    all_gather x1, waiting for transfers between devices, body(): received = lax.all_gather(send, 'rows', axis=0, tiled=True)  38.4 us
    all_gather x1, waiting for transfers between devices, body(): second = lax.all_gather(again, 'rows', axis=0, tiled=True)  31.2 us
    unnamed x18, local copies, waits for them, and re-layouts  7.79 us
    pallas_call x1, Pallas kernels, body(): call(functools.partial(sums_kernel, pad, cap), [array((half + info_rows,...  5.86 us
    pallas_call x1, Pallas kernels, body(): call(functools.partial(last_kernel, n, cap), array((columns, rows_dev), F...  4.77 us
    pallas_call x1, Pallas kernels, body(): call(functools.partial(first_kernel, pad), array((columns, rows_dev), F32...  4.32 us
    pallas_call x1, Pallas kernels, body(): call(functools.partial(means_kernel, n, cap), [array((slots, LANES), F32)...  3.08 us
    pallas_call x1, Pallas kernels, body(): call(functools.partial(worker_kernel, pad), array((2 * slots, slots), BF1...  2.57 us
  transfers between devices with their start and end apart: 2, of which 2 were waited for; matrix products, arithmetic and copies ran while one was open for 0% of the time, Pallas kernels for 6%

profile of v1, /device:TPU:0, one launch (start us, length us, event | category | flops | bytes accessed | tf_op | source)
XLA Modules:
  0.0 111.5 jit_solution(16547248790844624826)
XLA Ops:
  6.5 0.0 copy-start.8
  6.5 0.0 all-gather.3.cloned.1.call-start
  6.5 0.0 copy-start
  6.5 1.6 %copy-done = f32[64,8192]{1,0:T(8,128)S(1)} copy-done((f32[64,8192]{1,0:T(8,128)S(1)}, f32[64,8192]{1,0:T(8,128)}, u32[]{:S(2)}) %copy-start) | copy-done | bytes 2097176
  8.1 0.0 copy-start.4
  8.1 0.7 copy-done.4
  8.8 0.0 copy-start.6
  8.8 0.8 copy-done.6
  9.6 0.0 copy-start.7
  9.6 0.7 copy-done.7
  10.3 5.9 %shard_map.46 = (f32[136,128]{1,0:T(8,128)}, f32[256,128]{1,0:T(8,128)S(1)}, f32[256,128]{1,0:T(8,128)S(1)}, s32[64,128]{1,0:T(8,128)S(1)}, f32[64,128]{1,0:T(8,128)S(1)}) custom-call(f32[64,8192]{1,0:T(8,128)S(1)} %copy-done, s32[8,128]{1,0:T(8,128)S(1)} %bitcast.7, s32[64,128]{1,0:T(8,128)S(1)} %bitcast.6, s32[2,128]{1,0:T(2,128)S(1)} %bitcast.3), custom_call_target="tpu_custom_call" | custom-call | flops 1073741824 | bytes 2097152 | tf_op jit(solution)/shard_map/pallas_call | solution.py:266
  16.1 0.0 copy-start.5
  16.1 0.0 all-gather.3.cloned.1.call-update
  16.2 0.0 all-gather.5.cloned.1.call-start
  16.2 0.0 copy-done.8
  16.2 2.6 %shard_map.47.pairs = bf16[512,256]{1,0:T(8,128)(2,1)S(1)} custom-call(s32[8,128]{1,0:T(8,128)S(1)} %bitcast.8, s32[64,128]{1,0:T(8,128)S(1)} %get-tuple-element.17.mask_ids), custom_call_target="tpu_custom_call" | custom-call | flops 1073741824 | bytes 262144 | tf_op jit(solution)/shard_map/pallas_call | solution.py:282
  18.8 38.4 %all-gather.3.cloned.1.call-done.received = f32[2176,128]{1,0:T(8,128)} async-done(((f32[136,128]{1,0:T(8,128)}), f32[2176,128]{1,0:T(8,128)}) %all-gather.3.cloned.1.call-update) | async-done | bytes 1114128 | tf_op jit(solution)/shard_map/all_gather | solution.py:281
  57.2 0.0 copy-done.5
  57.2 0.0 copy-start.2
  57.2 1.2 %copy-done.2 = f32[2176,128]{1,0:T(8,128)S(1)} copy-done((f32[2176,128]{1,0:T(8,128)S(1)}, f32[2176,128]{1,0:T(8,128)}, u32[]{:S(2)}) %copy-start.2) | copy-done | bytes 1114136
  58.4 3.1 %shard_map.48 = (f32[256,128]{1,0:T(8,128)S(1)}, f32[128,128]{1,0:T(8,128)}, f32[256,128]{1,0:T(8,128)S(1)}, f32[128,128]{1,0:T(8,128)S(1)}) custom-call(f32[2176,128]{1,0:T(8,128)S(1)} %copy-done.2, s32[2,128]{1,0:T(2,128)S(1)} %bitcast.4, f32[256,128]{1,0:T(8,128)S(1)} %get-tuple-element.15.own, f32[256,128]{1,0:T(8,128)S(1)} %get-tuple-element.16.own_count, ...), custom_call_target="tpu_custom_call" | custom-call | flops 134217728 | bytes 1114112 | tf_op jit(solution)/shard_map/pallas_call | solution.py:291
  61.5 0.0 all-gather.5.cloned.1.call-update
  61.5 0.0 copy-start.1
  61.6 1.6 %copy-done.1 = f32[64,8192]{1,0:T(8,128)S(1)} copy-done((f32[64,8192]{1,0:T(8,128)S(1)}, f32[64,8192]{1,0:T(8,128)}, u32[]{:S(2)}) %copy-start.1) | copy-done | bytes 2097176
  63.1 4.3 %shard_map.49.before = f32[64,8192]{1,0:T(8,128)S(1)} custom-call(f32[64,8192]{1,0:T(8,128)S(1)} %copy-done.1, f32[256,128]{1,0:T(8,128)S(1)} %get-tuple-element.19.mean, s32[64,128]{1,0:T(8,128)S(1)} %get-tuple-element.17.mask_ids, f32[64,128]{1,0:T(8,128)S(1)} %get-tuple-element.20.weight), custom_call_target="tpu_custom_call" | custom-call | flops 1073741824 | bytes 4194304 | tf_op jit(solution)/shard_map/pallas_call | solution.py:306
  67.5 31.2 %all-gather.5.cloned.1.call-done.received = f32[2048,128]{1,0:T(8,128)} async-done(((f32[128,128]{1,0:T(8,128)}), f32[2048,128]{1,0:T(8,128)}) %all-gather.5.cloned.1.call-update) | async-done | bytes 1048592 | tf_op jit(solution)/shard_map/all_gather | solution.py:305
  98.6 0.0 copy-start.3
  98.6 1.2 %copy-done.3 = f32[2048,128]{1,0:T(8,128)S(1)} copy-done((f32[2048,128]{1,0:T(8,128)S(1)}, f32[2048,128]{1,0:T(8,128)}, u32[]{:S(2)}) %copy-start.3) | copy-done | bytes 1048600
  99.9 4.8 %shard_map.50 = f32[64,8192]{1,0:T(8,128)} custom-call(f32[2048,128]{1,0:T(8,128)S(1)} %copy-done.3, f32[64,8192]{1,0:T(8,128)S(1)} %shard_map.49.before, s32[2,128]{1,0:T(2,128)S(1)} %bitcast.5, f32[128,128]{1,0:T(8,128)S(1)} %get-tuple-element.21.info, f32[256,128]{1,0:T(8,128)S(1)} %get-tuple-element.22.inverse, s32[64,128]{1,0:T(8,128)S(1)} %get-tuple-element.17.mask_ids), custom_call_target="tpu_custom_call" | custom-call | flops 536870912 | bytes 4194304 | tf_op jit(solution)/shard_map/pallas_call | solution.py:315
Async XLA Ops:
  6.5 9.7 %copy-start.8 = (s32[1024]{0:T(1024)S(1)}, s32[1024]{0:T(1024)}, u32[]{:S(2)}) copy-start(s32[1024]{0:T(1024)} %param.5) | copy-start | bytes 12292
  6.5 50.6 %all-gather.3.cloned.1.call-start = ((), (), s32[]{:S(2)}) async-start(), calls=%async_computation | async-start | bytes 1183744 | tf_op jit(solution)/shard_map/all_gather | solution.py:281
  6.5 1.6 %copy-start = (f32[64,8192]{1,0:T(8,128)S(1)}, f32[64,8192]{1,0:T(8,128)}, u32[]{:S(2)}) copy-start(f32[64,8192]{1,0:T(8,128)} %probes.3) | copy-start | bytes 6291460
  8.1 0.7 copy-start.4
  8.8 0.8 copy-start.6
  9.6 0.7 copy-start.7
  16.1 41.1 %copy-start.5 = (s32[256]{0:T(256)S(1)}, s32[256]{0:T(256)}, u32[]{:S(2)}) copy-start(s32[256]{0:T(256)} %param.7) | copy-start | bytes 3076
  16.2 82.5 %all-gather.5.cloned.1.call-start = ((), (), s32[]{:S(2)}) async-start(), calls=%async_computation.1 | async-start | bytes 1114112 | tf_op jit(solution)/shard_map/all_gather | solution.py:305
  57.2 1.2 %copy-start.2 = (f32[2176,128]{1,0:T(8,128)S(1)}, f32[2176,128]{1,0:T(8,128)}, u32[]{:S(2)}) copy-start(f32[2176,128]{1,0:T(8,128)} %all-gather.3.cloned.1.call-done.received) | copy-start | bytes 3342340
  61.5 1.6 %copy-start.1 = (f32[64,8192]{1,0:T(8,128)S(1)}, f32[64,8192]{1,0:T(8,128)}, u32[]{:S(2)}) copy-start(f32[64,8192]{1,0:T(8,128)} %probes.3) | copy-start | bytes 6291460
  98.6 1.2 %copy-start.3 = (f32[2048,128]{1,0:T(8,128)S(1)}, f32[2048,128]{1,0:T(8,128)}, u32[]{:S(2)}) copy-start(f32[2048,128]{1,0:T(8,128)} %all-gather.5.cloned.1.call-done.received) | copy-start | bytes 3145732
Sparse Core Ops, SparseCore 0:
  16.3 40.8 all-gather.2
  61.7 36.9 all-gather.4

commit v2 on v1

v2 whole, which is shorter than its diff:
```python
import functools

import jax
import jax.numpy as jnp
from jax import lax
from jax.experimental import pallas as pl
from jax.experimental.pallas import tpu as pltpu
from jax.sharding import PartitionSpec as P

FIRMS_PER_SHARD = 1024
LANES = 128
BLOCK = 1024
VMEM_BYTES = 60 * 1024 * 1024
F32, BF16 = jnp.float32, jnp.bfloat16
NT = (((1,), (1,)), ((), ()))
NN = (((1,), (0,)), ((), ()))


def dot(a, b, dims=NN):
    return lax.dot_general(a, b, dims, preferred_element_type=F32)


def iota(shape, dim):
    return lax.broadcasted_iota(jnp.int32, shape, dim)


def split(x):
    hi = x.astype(BF16)
    return hi, (x - hi.astype(F32)).astype(BF16)


def row(ref, block, size):
    per = size // LANES
    return jnp.concatenate([ref[block * per + k : block * per + k + 1, :] for k in range(per)], axis=1)


def one_hot(ids, slots):
    return (iota((slots, ids.shape[1]), 0) == ids).astype(F32).astype(BF16)


def same_worker(pad, width):
    return (iota((width, width), 0) // pad == iota((width, width), 1) // pad).astype(F32).astype(BF16)


def by_worker(x, table):
    rows, width = x.shape
    hi, lo = split(x)
    both = jnp.concatenate([hi, lo], axis=0)
    step = table.shape[0]
    total = jnp.concatenate([dot(both[:, k : k + step], table) for k in range(0, width, step)], axis=1)
    return total[:rows] + total[rows:]


def fold(x):
    return x + pltpu.roll(x, x.shape[1] // 2, axis=1)


def halves(x):
    hi, lo = split(x)
    return jnp.where(iota(x.shape, 1) < x.shape[1] // 2, hi.astype(F32), lo.astype(F32))


def column(firms):
    return jnp.concatenate(
        [jnp.broadcast_to(firms[k : k + 1, :], (LANES, LANES)).T for k in range(firms.shape[0])], axis=0
    )


def along(x):
    return jnp.concatenate([x[k : k + LANES].T[:1] for k in range(0, x.shape[0], LANES)], axis=1)


def left_of(shape):
    return iota(shape, len(shape) - 1) < LANES // 2


def to_tiles(x, n):
    x = x.reshape(n, 2, 8, LANES)
    return jnp.where(left_of((n, 8, LANES)), x[:, 0], x[:, 1])


def apart(tiles):
    turned = pltpu.roll(tiles, LANES // 2, axis=tiles.ndim - 1)
    left = left_of(tiles.shape)
    return jnp.where(left, tiles, turned), jnp.where(left, turned, tiles)


def from_tiles(tiles):
    n = tiles.shape[0]
    return jnp.stack(apart(tiles), axis=1).reshape(2 * 8 * n, LANES)


def start_all(copies):
    for copy in copies:
        copy.start()


def wait_all(copies):
    for copy in copies:
        copy.wait()


def tiles_out(n, buffer, outs, sem):
    me = lax.axis_index("rows")
    return [pltpu.make_async_copy(buffer.at[me ^ k], outs[k], sem.at[k]) for k in range(n)]


def tiles_in(n, ins, buffer, sem, by_device):
    me = lax.axis_index("rows")
    return [
        pltpu.make_async_copy(ins[k], buffer.at[me ^ k] if by_device else buffer.at[k], sem.at[k]) for k in range(n)
    ]


def column_copies(source, target, sems):
    width = source.shape[1]
    cuts = [pl.ds(start, BLOCK) for start in range(0, width, BLOCK)]
    return [pltpu.make_async_copy(source.at[:, cut], target.at[:, cut], sems.at[b]) for b, cut in enumerate(cuts)]


def sums_kernel(n, pad, probes, lengths_in, ids_in, firms_in, *refs):
    outs, (own, own_count, mask_ids, weight) = refs[:n], refs[n : n + 4]
    valid, x, acc, lengths, ids, firms, buffer, sems, small, sem = refs[n + 4 :]
    copies = column_copies(probes, x, sems)
    first = [
        pltpu.make_async_copy(source, target, small.at[k])
        for k, (source, target) in enumerate(((lengths_in, lengths), (ids_in, ids), (firms_in, firms)))
    ]
    start_all(first)
    start_all(copies)
    slots = own.shape[0]
    total_rows = ids.shape[0]
    here = iota((total_rows, LANES), 0)
    lane = iota((total_rows, LANES), 1)
    wait_all(first)
    wide = jnp.broadcast_to(
        lengths[...].astype(F32)[:, None, :], (lengths.shape[0], total_rows // lengths.shape[0], LANES)
    ).reshape(total_rows, LANES)
    per = LANES // pad
    wide = jnp.where(lane // per == here % pad, wide, 0.0).astype(BF16)
    spread = (iota((LANES, LANES), 0) % per == iota((LANES, LANES), 1) // pad).astype(F32).astype(BF16)
    row_len = dot(wide, spread)
    inside = (lane % pad).astype(F32) < row_len
    valid[...] = jnp.where(inside, 1.0, 0.0)
    weight[...] = jnp.where(inside, 1.0 / row_len, 0.0)
    mask_ids[...] = jnp.where(inside, ids[...], -1)

    table = same_worker(pad, 256)
    for b in range(len(copies)):
        copies[b].wait()
        ok = row(valid, b, BLOCK)
        x0 = x[:, b * BLOCK : (b + 1) * BLOCK] * ok
        x1 = x0 - by_worker(x0, table) * row(weight, b, BLOCK)
        hi, lo = split(x1)
        counted = jnp.broadcast_to(ok, (16, BLOCK)).astype(BF16)
        data = jnp.concatenate([hi, lo, counted], axis=0)
        part = dot(one_hot(row(mask_ids, b, BLOCK), slots), data, NT)
        if b == 0:
            acc[...] = part
        else:
            acc[...] += part
    both = fold(acc[:, :LANES])
    own[...] = both
    count = jnp.broadcast_to(acc[:, LANES : LANES + 1], (slots, LANES))
    own_count[...] = count
    buffer[:, :8] = to_tiles(both, n)
    about = jnp.where(left_of((slots, LANES)), column(firms[...].astype(F32)), count).reshape(n, 2, 8, LANES)
    even = iota((n, 8, LANES), 2) // (LANES // 4) % 2 == 0
    buffer[:, 8:] = jnp.where(even, about[:, 0], about[:, 1])
    copies = tiles_out(n, buffer, outs, sem)
    start_all(copies)
    wait_all(copies)


def worker_kernel(pad, lengths, mask_ids, out):
    slots = out.shape[1]
    workers = lengths.shape[0] * LANES
    group = 256
    rows_group = group * pad
    pick = (iota((rows_group, group), 0) // pad == iota((rows_group, group), 1)).astype(F32).astype(BF16)
    total = jnp.zeros((2 * slots, slots), F32)
    for g in range(workers // group):
        counts = dot(one_hot(row(mask_ids, g, rows_group), slots), pick)
        inverse = 1.0 / row(lengths, g, group).astype(F32)
        hi, lo = split(counts * inverse)
        total += dot(jnp.concatenate([hi, lo], axis=0), counts.astype(BF16), NT)
    hi, lo = split(total[:slots] + total[slots:])
    out[:slots] = hi
    out[slots:] = lo


def owner_means(tiles, table, scale):
    n = tiles.shape[0]
    left, right = apart(tiles.reshape(8 * n, LANES))
    data = jnp.concatenate([halves(left), halves(right)], axis=0).astype(BF16)
    total = fold(dot(table, data)) * scale
    return jnp.where(left_of((8 * n, LANES)), total[: 8 * n], total[8 * n :]).reshape(n, 8, LANES)


def owner_first_kernel(n, *refs):
    ins, outs, (table, scale) = refs[:n], refs[n : 2 * n], refs[2 * n : 2 * n + 2]
    buffer, back, in_sem, sem = refs[2 * n + 2 :]
    copies = tiles_in(n, ins, buffer, in_sem, False)
    start_all(copies)
    wait_all(copies)
    about = buffer[:, 8:].reshape(8 * n, LANES)
    quarter = LANES // 4

    def both(at):
        return jnp.concatenate(
            [jnp.broadcast_to(about[:, k : k + 1], (8 * n, LANES)) for k in (at, at + quarter)], axis=0
        )

    keys, counts = both(0), both(2 * quarter)
    same = keys[:, :1] == along(keys)
    table[...] = same.astype(F32).astype(BF16)
    count = jnp.sum(jnp.where(same, along(counts), 0.0), axis=1, keepdims=True)
    scale[...] = jnp.broadcast_to(1.0 / jnp.maximum(count, 1.0), scale.shape)
    back[...] = owner_means(buffer[:, :8], table[...], scale[...])
    copies = tiles_out_in_place(n, back, outs, sem)
    start_all(copies)
    wait_all(copies)


def owner_second_kernel(n, *refs):
    ins, (table, scale), outs = refs[:n], refs[n : n + 2], refs[n + 2 : 2 * n + 2]
    buffer, back, in_sem, sem = refs[2 * n + 2 :]
    copies = tiles_in(n, ins, buffer, in_sem, False)
    start_all(copies)
    wait_all(copies)
    back[...] = owner_means(buffer[...], table[...], scale[...])
    copies = tiles_out_in_place(n, back, outs, sem)
    start_all(copies)
    wait_all(copies)


def tiles_out_in_place(n, buffer, outs, sem):
    return [pltpu.make_async_copy(buffer.at[k], outs[k], sem.at[k]) for k in range(n)]


def change_kernel(n, *refs):
    ins, (own, own_count, pairs), outs, mean = refs[:n], refs[n : n + 3], refs[n + 3 : 2 * n + 3], refs[2 * n + 3]
    buffer, back, in_sem, sem = refs[2 * n + 4 :]
    copies = tiles_in(n, ins, buffer, in_sem, True)
    start_all(copies)
    wait_all(copies)
    slots = own.shape[0]
    found = from_tiles(buffer[...])
    mean[...] = found
    change = dot(pairs[...], halves(found).astype(BF16))
    new = own[...] - own_count[...] * found + fold(change[:slots] + change[slots:])
    back[...] = to_tiles(new, n)
    copies = tiles_out(n, back, outs, sem)
    start_all(copies)
    wait_all(copies)


def take(parts, ids, slots):
    spread = dot(parts, one_hot(ids, slots))
    columns = parts.shape[0] // 2
    return spread[:columns] + spread[columns:]


def first_kernel(pad, probes, mean, mask_ids, weight, out, x, y, in_sems, out_sems):
    ins, outs = column_copies(probes, x, in_sems), column_copies(y, out, out_sems)
    start_all(ins)
    slots = mean.shape[0]
    parts = halves(mean[...]).T.astype(BF16)
    table = same_worker(pad, 256)
    for b in range(len(ins)):
        ids = row(mask_ids, b, BLOCK)
        spread = take(parts, ids, slots)
        ins[b].wait()
        rest = jnp.where(ids >= 0, x[:, b * BLOCK : (b + 1) * BLOCK] - spread, 0.0)
        y[:, b * BLOCK : (b + 1) * BLOCK] = rest - by_worker(rest, table) * row(weight, b, BLOCK)
        outs[b].start()
    wait_all(outs)


def last_kernel(n, *refs):
    arrived, (before, mask_ids, out) = refs[:n], refs[n : n + 3]
    buffer, x, y, tile_sem, in_sems, out_sems = refs[n + 3 :]
    ins, outs = column_copies(before, x, in_sems), column_copies(y, out, out_sems)
    copies = tiles_in(n, arrived, buffer, tile_sem, True)
    start_all(copies)
    start_all(ins)
    wait_all(copies)
    mean = from_tiles(buffer[...])
    parts = halves(mean).T.astype(BF16)
    for b in range(len(ins)):
        spread = take(parts, row(mask_ids, b, BLOCK), mean.shape[0])
        ins[b].wait()
        y[:, b * BLOCK : (b + 1) * BLOCK] = x[:, b * BLOCK : (b + 1) * BLOCK] - spread
        outs[b].start()
    wait_all(outs)


def exchange(tiles):
    n = len(tiles)
    return [tiles[0]] + [lax.ppermute(tiles[k], "rows", [(i, i ^ k) for i in range(n)]) for k in range(1, n)]


def call(kernel, out_shape, in_specs, out_specs, scratch, flops, moved):
    return pl.pallas_call(
        kernel,
        out_shape=out_shape,
        in_specs=in_specs,
        out_specs=out_specs,
        scratch_shapes=scratch,
        compiler_params=pltpu.CompilerParams(vmem_limit_bytes=VMEM_BYTES),
        cost_estimate=pl.CostEstimate(flops=flops, bytes_accessed=moved, transcendentals=0),
    )


def body(probes, worker_len, spell_to_slot, slot_to_firm, *, n):
    columns, rows_dev = probes.shape
    workers = worker_len.shape[0]
    pad = rows_dev // workers
    slots = slot_to_firm.shape[0]
    firm_tiles = slots // LANES
    blocks = rows_dev // BLOCK
    vmem, anywhere = pl.BlockSpec(memory_space=pltpu.VMEM), pl.BlockSpec(memory_space=pl.ANY)
    lengths = worker_len.reshape(workers // LANES, LANES)
    ids = spell_to_slot.reshape(rows_dev // LANES, LANES)
    firms = slot_to_firm.reshape(firm_tiles, LANES)
    array = jax.ShapeDtypeStruct
    of_rows = (rows_dev // LANES, LANES)
    work = 2 * rows_dev * slots * 2 * columns
    sems = pltpu.SemaphoreType.DMA((blocks,))
    sem = pltpu.SemaphoreType.DMA((n,))
    whole = pltpu.VMEM((columns, rows_dev), F32)
    of_slots = array((slots, LANES), F32)
    tile, tall = array((8, LANES), F32), array((16, LANES), F32)
    tiles, talls = pltpu.VMEM((n, 8, LANES), F32), pltpu.VMEM((n, 16, LANES), F32)

    *send, own, own_count, mask_ids, weight = call(
        functools.partial(sums_kernel, n, pad),
        [tall] * n + [of_slots, of_slots, array(of_rows, jnp.int32), array(of_rows, F32)],
        [anywhere] * 4,
        [anywhere] * n + [vmem] * 4,
        [
            pltpu.VMEM(of_rows, F32),
            whole,
            pltpu.VMEM((slots, 2 * columns + 16), F32),
            pltpu.VMEM(lengths.shape, jnp.int32),
            pltpu.VMEM(ids.shape, jnp.int32),
            pltpu.VMEM(firms.shape, jnp.int32),
            talls,
            sems,
            pltpu.SemaphoreType.DMA((3,)),
            sem,
        ],
        2 * work,
        4 * columns * rows_dev,
    )(probes, lengths, ids, firms)
    received = exchange(send)
    pairs = call(
        functools.partial(worker_kernel, pad),
        array((2 * slots, slots), BF16),
        [vmem, vmem],
        vmem,
        [],
        2 * work,
        4 * slots * slots,
    )(lengths, mask_ids)
    *send, table, scale = call(
        functools.partial(owner_first_kernel, n),
        [tile] * n + [array((slots, slots), BF16), of_slots],
        [anywhere] * n,
        [anywhere] * n + [vmem] * 2,
        [talls, tiles, sem, sem],
        work // 16,
        slots * slots * 4,
    )(*received)
    received = exchange(send)
    *send, mean = call(
        functools.partial(change_kernel, n),
        [tile] * n + [of_slots],
        [anywhere] * n + [vmem] * 3,
        [anywhere] * n + [vmem],
        [tiles, tiles, sem, sem],
        work // 16,
        slots * slots * 4,
    )(*received, own, own_count, pairs)
    received = exchange(send)
    before = call(
        functools.partial(first_kernel, pad),
        array((columns, rows_dev), F32),
        [anywhere, vmem, vmem, vmem],
        anywhere,
        [whole, whole, sems, sems],
        2 * work,
        8 * columns * rows_dev,
    )(probes, mean, mask_ids, weight)
    send = call(
        functools.partial(owner_second_kernel, n),
        [tile] * n,
        [anywhere] * n + [vmem] * 2,
        [anywhere] * n,
        [tiles, tiles, sem, sem],
        work // 16,
        slots * slots * 4,
    )(*received, table, scale)
    received = exchange(send)
    return call(
        functools.partial(last_kernel, n),
        array((columns, rows_dev), F32),
        [anywhere] * n + [anywhere, vmem],
        anywhere,
        [tiles, whole, whole, sem, sems, sems],
        work,
        8 * columns * rows_dev,
    )(*received, before, mask_ids)


def solution(mesh):
    placed = (P(None, ("grp", "rows")), P(("grp", "rows")), P(("grp", "rows")), P(("grp", "rows")))
    return jax.shard_map(
        functools.partial(body, n=mesh.shape["rows"]),
        mesh=mesh,
        in_specs=placed,
        out_specs=P(None, ("grp", "rows")),
        check_vma=False,
    )
```

time: 112 us -> 129 us (1.15)
  starting transfers between devices: 0.04 us -> 83.5 us
  waiting for transfers between devices: 69.6 us -> 9.76 us
  between operations: 13.5 us -> 0.83 us
  Pallas kernels: 20.6 us -> 32.7 us
  local copies, waits for them, and re-layouts: 7.79 us -> 2.2 us
    ppermute x0 -> x60, starting transfers between devices: none -> 83.5 us  [exchange(): lax.ppermute(tiles[k], 'rows', [(i, i ^ k) for i in range(n)])]
    all_gather x2 -> x0, waiting for transfers between devices: 69.5 us -> none  [the longest x1 38.4 us: body(): received = lax.all_gather(send, 'rows', axis=0, tiled=True)]
    ppermute x0 -> x60, waiting for transfers between devices: none -> 9.76 us  [exchange(): lax.ppermute(tiles[k], 'rows', [(i, i ^ k) for i in range(n)])]
    pallas_call x3 -> x5, Pallas kernels: 13.7 us -> 23 us  [the longest x1 7.97 us: body(): call(functools.partial(sums_kernel, n, pad), [tall] * n + [of_slots, of_s...]
    unnamed x18 -> x120, local copies, waits for them, and re-layouts: 7.79 us -> 2.2 us
    pallas_call x1, Pallas kernels: 2.57 us -> 4.07 us  [body(): call(functools.partial(worker_kernel, pad), array((2 * slots, slots), BF1...]
    pallas_call x1, Pallas kernels: 4.32 us -> 5.66 us  [body(): call(functools.partial(first_kernel, pad), array((columns, rows_dev), F32...]
  transfers between devices with their start and end apart: 2 -> 60, of which waited for: 2 -> 8; matrix products, arithmetic and copies ran while one was open for 0% -> 0% of each run, Pallas kernels for 6% -> 8%
where the time goes in v2:
time: 129 us
  starting transfers between devices  83.5 us (65%)
  Pallas kernels  32.7 us (25%)
  waiting for transfers between devices  9.76 us (8%)
  local copies, waits for them, and re-layouts  2.2 us (2%)
    ppermute x60, starting transfers between devices, exchange(): lax.ppermute(tiles[k], 'rows', [(i, i ^ k) for i in range(n)])  83.5 us
    ppermute x60, waiting for transfers between devices, exchange(): lax.ppermute(tiles[k], 'rows', [(i, i ^ k) for i in range(n)])  9.76 us
    pallas_call x1, Pallas kernels, body(): call(functools.partial(sums_kernel, n, pad), [tall] * n + [of_slots, of_s...  7.97 us
    pallas_call x1, Pallas kernels, body(): call(functools.partial(first_kernel, pad), array((columns, rows_dev), F32...  5.66 us
    pallas_call x1, Pallas kernels, body(): call(functools.partial(last_kernel, n), array((columns, rows_dev), F32),...  5.23 us
    pallas_call x1, Pallas kernels, body(): call(functools.partial(worker_kernel, pad), array((2 * slots, slots), BF1...  4.07 us
    pallas_call x1, Pallas kernels, body(): call(functools.partial(change_kernel, n), [tile] * n + [of_slots], [anywh...  3.78 us
    pallas_call x1, Pallas kernels, body(): call(functools.partial(owner_first_kernel, n), [tile] * n + [array((slots...  3.02 us
  transfers between devices with their start and end apart: 60, of which 8 were waited for; matrix products, arithmetic and copies ran while one was open for 0% of the time, Pallas kernels for 8%

profile of v2, /device:TPU:0, one launch (start us, length us, event | category | flops | bytes accessed | tf_op | source)
XLA Modules:
  0.0 129.0 jit_solution(1319883960107547510)
XLA Ops:
  0.0 8.0 %shard_map.46 = (f32[16,128]{1,0:T(8,128)}, f32[16,128]{1,0:T(8,128)}, f32[16,128]{1,0:T(8,128)}, f32[16,128]{1,0:T(8,128)}, f32[16,128]{1,0:T(8,128)}, /*index=...) custom-call(f32[64,8192]{1,0:T(8,128)} %probes.3, ...), custom_call_target="tpu_custom_call" | custom-call | flops 1073741824 | bytes 2097152 | tf_op jit(solution)/shard_map/pallas_call | solution.py:336
  8.5 2.6 %collective-permute-start.1 = (f32[16,128]{1,0:T(8,128)}, f32[16,128]{1,0:T(8,128)S(1)}, u32[]{:S(2)}, u32[]{:S(2)}) collective-permute-start(f32[16,128]{1,0:T(8,128)} %get-tuple-element.78), channel_id=1, source_target_pairs={{0,2},{1,3},{2,0},{3,1},{4,6},{5,7},{6,4},{7,5},{8,10},{9,11},{10,... | collective-permute-start | bytes 24584 | tf_op jit(solution)/shard_map/ppermute | solution.py:300
  11.2 1.8 %collective-permute-start.3 = (f32[16,128]{1,0:T(8,128)}, f32[16,128]{1,0:T(8,128)S(1)}, u32[]{:S(2)}, u32[]{:S(2)}) collective-permute-start(f32[16,128]{1,0:T(8,128)} %get-tuple-element.80), channel_id=1, source_target_pairs={{0,4},{1,5},{2,6},{3,7},{4,0},{5,1},{6,2},{7,3},{8,12},{9,13},{10,... | collective-permute-start | bytes 24584 | tf_op jit(solution)/shard_map/ppermute | solution.py:300
  13.0 2.6 %collective-permute-start.5 = (f32[16,128]{1,0:T(8,128)}, f32[16,128]{1,0:T(8,128)S(1)}, u32[]{:S(2)}, u32[]{:S(2)}) collective-permute-start(f32[16,128]{1,0:T(8,128)} %get-tuple-element.82), channel_id=1, source_target_pairs={{0,6},{1,7},{2,4},{3,5},{4,2},{5,3},{6,0},{7,1},{8,14},{9,15},{10,... | collective-permute-start | bytes 24584 | tf_op jit(solution)/shard_map/ppermute | solution.py:300
  15.7 2.6 %collective-permute-start.7 = (f32[16,128]{1,0:T(8,128)}, f32[16,128]{1,0:T(8,128)S(1)}, u32[]{:S(2)}, u32[]{:S(2)}) collective-permute-start(f32[16,128]{1,0:T(8,128)} %get-tuple-element.84), channel_id=1, source_target_pairs={{0,8},{1,9},{2,10},{3,11},{4,12},{5,13},{6,14},{7,15},{8,0},{9,1},... | collective-permute-start | bytes 24584 | tf_op jit(solution)/shard_map/ppermute | solution.py:300
  18.4 3.5 %collective-permute-start.9 = (f32[16,128]{1,0:T(8,128)}, f32[16,128]{1,0:T(8,128)S(1)}, u32[]{:S(2)}, u32[]{:S(2)}) collective-permute-start(f32[16,128]{1,0:T(8,128)} %get-tuple-element.86), channel_id=1, source_target_pairs={{0,10},{1,11},{2,8},{3,9},{4,14},{5,15},{6,12},{7,13},{8,2},{9,3},... | collective-permute-start | bytes 24584 | tf_op jit(solution)/shard_map/ppermute | solution.py:300
  22.1 3.5 %collective-permute-start.11 = (f32[16,128]{1,0:T(8,128)}, f32[16,128]{1,0:T(8,128)S(1)}, u32[]{:S(2)}, u32[]{:S(2)}) collective-permute-start(f32[16,128]{1,0:T(8,128)} %get-tuple-element.88), channel_id=1, source_target_pairs={{0,12},{1,13},{2,14},{3,15},{4,8},{5,9},{6,10},{7,11},{8,4},{9,5},... | collective-permute-start | bytes 24584 | tf_op jit(solution)/shard_map/ppermute | solution.py:300
  25.6 4.4 %collective-permute-start.13 = (f32[16,128]{1,0:T(8,128)}, f32[16,128]{1,0:T(8,128)S(1)}, u32[]{:S(2)}, u32[]{:S(2)}) collective-permute-start(f32[16,128]{1,0:T(8,128)} %get-tuple-element.90), channel_id=1, source_target_pairs={{0,14},{1,15},{2,12},{3,13},{4,10},{5,11},{6,8},{7,9},{8,6},{9,7},... | collective-permute-start | bytes 24584 | tf_op jit(solution)/shard_map/ppermute | solution.py:300
  30.7 1.6 %collective-permute-done.13.refs_14_ = f32[16,128]{1,0:T(8,128)S(1)} collective-permute-done((f32[16,128]{1,0:T(8,128)}, f32[16,128]{1,0:T(8,128)S(1)}, u32[]{:S(2)}, u32[]{:S(2)}) %collective-permute-start.13) | collective-permute-done | bytes 8224 | tf_op jit(solution)/shard_map/ppermute | solution.py:300
  32.2 3.8 %collective-permute-done.14.refs_15_ = f32[16,128]{1,0:T(8,128)S(1)} collective-permute-done((f32[16,128]{1,0:T(8,128)}, f32[16,128]{1,0:T(8,128)S(1)}, u32[]{:S(2)}, u32[]{:S(2)}) %collective-permute-start.14) | collective-permute-done | bytes 8224 | tf_op jit(solution)/shard_map/ppermute | solution.py:300
  36.6 3.0 %shard_map.47 = (f32[8,128]{1,0:T(8,128)}, f32[8,128]{1,0:T(8,128)}, f32[8,128]{1,0:T(8,128)}, f32[8,128]{1,0:T(8,128)}, f32[8,128]{1,0:T(8,128)}, /*index=5*/f3...) custom-call(f32[16,128]{1,0:T(8,128)} %get-tuple-element.76.refs_0_,, ...), custom_call_target="tpu_custom_call" | custom-call | flops 33554432 | bytes 262144 | tf_op jit(solution)/shard_map/pallas_call | solution.py:366
  40.4 1.2 collective-permute-start.17
  41.6 1.8 %collective-permute-start.19 = (f32[8,128]{1,0:T(8,128)}, f32[8,128]{1,0:T(8,128)S(1)}, u32[]{:S(2)}, u32[]{:S(2)}) collective-permute-start(f32[8,128]{1,0:T(8,128)} %get-tuple-element.97), channel_id=1, source_target_pairs={{0,5},{1,4},{2,7},{3,6},{4,1},{5,0},{6,3},{7,2},{8,13},{9,12},{10,... | collective-permute-start | bytes 12296 | tf_op jit(solution)/shard_map/ppermute | solution.py:300
  43.7 2.3 %collective-permute-start.21 = (f32[8,128]{1,0:T(8,128)}, f32[8,128]{1,0:T(8,128)S(1)}, u32[]{:S(2)}, u32[]{:S(2)}) collective-permute-start(f32[8,128]{1,0:T(8,128)} %get-tuple-element.99), channel_id=1, source_target_pairs={{0,7},{1,6},{2,5},{3,4},{4,3},{5,2},{6,1},{7,0},{8,15},{9,14},{10,... | collective-permute-start | bytes 12296 | tf_op jit(solution)/shard_map/ppermute | solution.py:300
  46.0 2.7 %collective-permute-start.23 = (f32[8,128]{1,0:T(8,128)}, f32[8,128]{1,0:T(8,128)S(1)}, u32[]{:S(2)}, u32[]{:S(2)}) collective-permute-start(f32[8,128]{1,0:T(8,128)} %get-tuple-element.101), channel_id=1, source_target_pairs={{0,9},{1,8},{2,11},{3,10},{4,13},{5,12},{6,15},{7,14},{8,1},{9,0},... | collective-permute-start | bytes 12296 | tf_op jit(solution)/shard_map/ppermute | solution.py:300
  49.0 3.2 %collective-permute-start.25 = (f32[8,128]{1,0:T(8,128)}, f32[8,128]{1,0:T(8,128)S(1)}, u32[]{:S(2)}, u32[]{:S(2)}) collective-permute-start(f32[8,128]{1,0:T(8,128)} %get-tuple-element.103), channel_id=1, source_target_pairs={{0,11},{1,10},{2,9},{3,8},{4,15},{5,14},{6,13},{7,12},{8,3},{9,2},... | collective-permute-start | bytes 12296 | tf_op jit(solution)/shard_map/ppermute | solution.py:300
  52.6 3.2 %collective-permute-start.27 = (f32[8,128]{1,0:T(8,128)}, f32[8,128]{1,0:T(8,128)S(1)}, u32[]{:S(2)}, u32[]{:S(2)}) collective-permute-start(f32[8,128]{1,0:T(8,128)} %get-tuple-element.105), channel_id=1, source_target_pairs={{0,13},{1,12},{2,15},{3,14},{4,9},{5,8},{6,11},{7,10},{8,5},{9,4},... | collective-permute-start | bytes 12296 | tf_op jit(solution)/shard_map/ppermute | solution.py:300
  56.3 3.9 %collective-permute-start.29 = (f32[8,128]{1,0:T(8,128)}, f32[8,128]{1,0:T(8,128)S(1)}, u32[]{:S(2)}, u32[]{:S(2)}) collective-permute-start(f32[8,128]{1,0:T(8,128)} %get-tuple-element.107), channel_id=1, source_target_pairs={{0,15},{1,14},{2,13},{3,12},{4,11},{5,10},{6,9},{7,8},{8,7},{9,6},... | collective-permute-start | bytes 12296 | tf_op jit(solution)/shard_map/ppermute | solution.py:300
  60.2 4.1 %shard_map.48.refs_18_ = bf16[512,256]{1,0:T(8,128)(2,1)} custom-call(s32[8,128]{1,0:T(8,128)} %bitcast.5, s32[64,128]{1,0:T(8,128)} %get-tuple-element.110.mask_ids.refs_17_), custom_call_target="tpu_custom_call" | custom-call | flops 1073741824 | bytes 262144 | tf_op jit(solution)/shard_map/pallas_call | solution.py:357
  65.0 3.8 %shard_map.49 = (f32[8,128]{1,0:T(8,128)}, f32[8,128]{1,0:T(8,128)}, f32[8,128]{1,0:T(8,128)}, f32[8,128]{1,0:T(8,128)}, f32[8,128]{1,0:T(8,128)}, /*index=5*/f3...) custom-call(f32[8,128]{1,0:T(8,128)} %get-tuple-element.92.refs_0_, ...), custom_call_target="tpu_custom_call" | custom-call | flops 33554432 | bytes 262144 | tf_op jit(solution)/shard_map/pallas_call | solution.py:376
  68.7 0.5 collective-permute-start.30
  69.8 0.9 collective-permute-start.32
  70.7 2.1 %collective-permute-start.34 = (f32[8,128]{1,0:T(8,128)}, f32[8,128]{1,0:T(8,128)S(1)}, u32[]{:S(2)}, u32[]{:S(2)}) collective-permute-start(f32[8,128]{1,0:T(8,128)} %get-tuple-element.116), channel_id=1, source_target_pairs={{0,5},{1,4},{2,7},{3,6},{4,1},{5,0},{6,3},{7,2},{8,13},{9,12},{10,... | collective-permute-start | bytes 12296 | tf_op jit(solution)/shard_map/ppermute | solution.py:300
  73.1 2.0 %collective-permute-start.36 = (f32[8,128]{1,0:T(8,128)}, f32[8,128]{1,0:T(8,128)S(1)}, u32[]{:S(2)}, u32[]{:S(2)}) collective-permute-start(f32[8,128]{1,0:T(8,128)} %get-tuple-element.118), channel_id=1, source_target_pairs={{0,7},{1,6},{2,5},{3,4},{4,3},{5,2},{6,1},{7,0},{8,15},{9,14},{10,... | collective-permute-start | bytes 12296 | tf_op jit(solution)/shard_map/ppermute | solution.py:300
  75.3 2.8 %collective-permute-start.38 = (f32[8,128]{1,0:T(8,128)}, f32[8,128]{1,0:T(8,128)S(1)}, u32[]{:S(2)}, u32[]{:S(2)}) collective-permute-start(f32[8,128]{1,0:T(8,128)} %get-tuple-element.120), channel_id=1, source_target_pairs={{0,9},{1,8},{2,11},{3,10},{4,13},{5,12},{6,15},{7,14},{8,1},{9,0},... | collective-permute-start | bytes 12296 | tf_op jit(solution)/shard_map/ppermute | solution.py:300
  78.1 0.7 collective-permute-start.39
  78.8 2.5 %collective-permute-start.40 = (f32[8,128]{1,0:T(8,128)}, f32[8,128]{1,0:T(8,128)S(1)}, u32[]{:S(2)}, u32[]{:S(2)}) collective-permute-start(f32[8,128]{1,0:T(8,128)} %get-tuple-element.122), channel_id=1, source_target_pairs={{0,11},{1,10},{2,9},{3,8},{4,15},{5,14},{6,13},{7,12},{8,3},{9,2},... | collective-permute-start | bytes 12296 | tf_op jit(solution)/shard_map/ppermute | solution.py:300
  81.3 1.2 collective-permute-start.41
  82.5 2.7 %collective-permute-start.42 = (f32[8,128]{1,0:T(8,128)}, f32[8,128]{1,0:T(8,128)S(1)}, u32[]{:S(2)}, u32[]{:S(2)}) collective-permute-start(f32[8,128]{1,0:T(8,128)} %get-tuple-element.124), channel_id=1, source_target_pairs={{0,13},{1,12},{2,15},{3,14},{4,9},{5,8},{6,11},{7,10},{8,5},{9,4},... | collective-permute-start | bytes 12296 | tf_op jit(solution)/shard_map/ppermute | solution.py:300
  85.2 1.8 %collective-permute-start.43 = (f32[8,128]{1,0:T(8,128)}, f32[8,128]{1,0:T(8,128)S(1)}, u32[]{:S(2)}, u32[]{:S(2)}) collective-permute-start(f32[8,128]{1,0:T(8,128)} %get-tuple-element.125), channel_id=1, source_target_pairs={{0,14},{1,15},{2,12},{3,13},{4,10},{5,11},{6,8},{7,9},{8,6},{9,7},... | collective-permute-start | bytes 12296 | tf_op jit(solution)/shard_map/ppermute | solution.py:300
  87.1 2.3 %collective-permute-start.44 = (f32[8,128]{1,0:T(8,128)}, f32[8,128]{1,0:T(8,128)S(1)}, u32[]{:S(2)}, u32[]{:S(2)}) collective-permute-start(f32[8,128]{1,0:T(8,128)} %get-tuple-element.126), channel_id=1, source_target_pairs={{0,15},{1,14},{2,13},{3,12},{4,11},{5,10},{6,9},{7,8},{8,7},{9,6},... | collective-permute-start | bytes 12296 | tf_op jit(solution)/shard_map/ppermute | solution.py:300
  89.4 2.4 %collective-permute-done.43.refs_14_ = f32[8,128]{1,0:T(8,128)S(1)} collective-permute-done((f32[8,128]{1,0:T(8,128)}, f32[8,128]{1,0:T(8,128)S(1)}, u32[]{:S(2)}, u32[]{:S(2)}) %collective-permute-start.43) | collective-permute-done | bytes 4128 | tf_op jit(solution)/shard_map/ppermute | solution.py:300
  91.7 1.3 collective-permute-done.44.refs_15_
  93.6 3.0 %shard_map.50 = (f32[8,128]{1,0:T(8,128)}, f32[8,128]{1,0:T(8,128)}, f32[8,128]{1,0:T(8,128)}, f32[8,128]{1,0:T(8,128)}, f32[8,128]{1,0:T(8,128)}, /*index=5*/f3...) custom-call(f32[8,128]{1,0:T(8,128)} %get-tuple-element.111.refs_0_,, ...), custom_call_target="tpu_custom_call" | custom-call | flops 33554432 | bytes 262144 | tf_op jit(solution)/shard_map/pallas_call | solution.py:395
  96.8 0.5 collective-permute-start.46
  97.3 1.2 collective-permute-start.47
  98.5 1.8 %collective-permute-start.49 = (f32[8,128]{1,0:T(8,128)}, f32[8,128]{1,0:T(8,128)S(1)}, u32[]{:S(2)}, u32[]{:S(2)}) collective-permute-start(f32[8,128]{1,0:T(8,128)} %get-tuple-element.134), channel_id=1, source_target_pairs={{0,5},{1,4},{2,7},{3,6},{4,1},{5,0},{6,3},{7,2},{8,13},{9,12},{10,... | collective-permute-start | bytes 12296 | tf_op jit(solution)/shard_map/ppermute | solution.py:300
  100.6 2.3 %collective-permute-start.51 = (f32[8,128]{1,0:T(8,128)}, f32[8,128]{1,0:T(8,128)S(1)}, u32[]{:S(2)}, u32[]{:S(2)}) collective-permute-start(f32[8,128]{1,0:T(8,128)} %get-tuple-element.136), channel_id=1, source_target_pairs={{0,7},{1,6},{2,5},{3,4},{4,3},{5,2},{6,1},{7,0},{8,15},{9,14},{10,... | collective-permute-start | bytes 12296 | tf_op jit(solution)/shard_map/ppermute | solution.py:300
  102.9 0.9 collective-permute-start.52
  103.8 1.8 %collective-permute-start.53 = (f32[8,128]{1,0:T(8,128)}, f32[8,128]{1,0:T(8,128)S(1)}, u32[]{:S(2)}, u32[]{:S(2)}) collective-permute-start(f32[8,128]{1,0:T(8,128)} %get-tuple-element.138), channel_id=1, source_target_pairs={{0,9},{1,8},{2,11},{3,10},{4,13},{5,12},{6,15},{7,14},{8,1},{9,0},... | collective-permute-start | bytes 12296 | tf_op jit(solution)/shard_map/ppermute | solution.py:300
  105.6 1.8 %collective-permute-start.54 = (f32[8,128]{1,0:T(8,128)}, f32[8,128]{1,0:T(8,128)S(1)}, u32[]{:S(2)}, u32[]{:S(2)}) collective-permute-start(f32[8,128]{1,0:T(8,128)} %get-tuple-element.139), channel_id=1, source_target_pairs={{0,10},{1,11},{2,8},{3,9},{4,14},{5,15},{6,12},{7,13},{8,2},{9,3},... | collective-permute-start | bytes 12296 | tf_op jit(solution)/shard_map/ppermute | solution.py:300
  107.4 1.7 %collective-permute-start.55 = (f32[8,128]{1,0:T(8,128)}, f32[8,128]{1,0:T(8,128)S(1)}, u32[]{:S(2)}, u32[]{:S(2)}) collective-permute-start(f32[8,128]{1,0:T(8,128)} %get-tuple-element.140), channel_id=1, source_target_pairs={{0,11},{1,10},{2,9},{3,8},{4,15},{5,14},{6,13},{7,12},{8,3},{9,2},... | collective-permute-start | bytes 12296 | tf_op jit(solution)/shard_map/ppermute | solution.py:300
  109.1 2.0 %collective-permute-start.56 = (f32[8,128]{1,0:T(8,128)}, f32[8,128]{1,0:T(8,128)S(1)}, u32[]{:S(2)}, u32[]{:S(2)}) collective-permute-start(f32[8,128]{1,0:T(8,128)} %get-tuple-element.141), channel_id=1, source_target_pairs={{0,12},{1,13},{2,14},{3,15},{4,8},{5,9},{6,10},{7,11},{8,4},{9,5},... | collective-permute-start | bytes 12296 | tf_op jit(solution)/shard_map/ppermute | solution.py:300
  111.1 1.6 %collective-permute-start.57 = (f32[8,128]{1,0:T(8,128)}, f32[8,128]{1,0:T(8,128)S(1)}, u32[]{:S(2)}, u32[]{:S(2)}) collective-permute-start(f32[8,128]{1,0:T(8,128)} %get-tuple-element.142), channel_id=1, source_target_pairs={{0,13},{1,12},{2,15},{3,14},{4,9},{5,8},{6,11},{7,10},{8,5},{9,4},... | collective-permute-start | bytes 12296 | tf_op jit(solution)/shard_map/ppermute | solution.py:300
  112.7 2.8 %collective-permute-start.58 = (f32[8,128]{1,0:T(8,128)}, f32[8,128]{1,0:T(8,128)S(1)}, u32[]{:S(2)}, u32[]{:S(2)}) collective-permute-start(f32[8,128]{1,0:T(8,128)} %get-tuple-element.143), channel_id=1, source_target_pairs={{0,14},{1,15},{2,12},{3,13},{4,10},{5,11},{6,8},{7,9},{8,6},{9,7},... | collective-permute-start | bytes 12296 | tf_op jit(solution)/shard_map/ppermute | solution.py:300
  115.5 1.6 %collective-permute-start.59 = (f32[8,128]{1,0:T(8,128)}, f32[8,128]{1,0:T(8,128)S(1)}, u32[]{:S(2)}, u32[]{:S(2)}) collective-permute-start(f32[8,128]{1,0:T(8,128)} %get-tuple-element.144), channel_id=1, source_target_pairs={{0,15},{1,14},{2,13},{3,12},{4,11},{5,10},{6,9},{7,8},{8,7},{9,6},... | collective-permute-start | bytes 12296 | tf_op jit(solution)/shard_map/ppermute | solution.py:300
  117.1 5.7 %shard_map.51.refs_16_ = f32[64,8192]{1,0:T(8,128)} custom-call(f32[64,8192]{1,0:T(8,128)} %probes.3, f32[256,128]{1,0:T(8,128)} %get-tuple-element.145.mean, s32[64,128]{1,0:T(8,128)} %get-tuple-element.110.mask_ids.refs_17_, f32[64,128]{1,0:T(8,128)} %get-tuple-element.146.weight), custom_call_target="tpu_custom_call" | custom-call | flops 1073741824 | bytes 4194304 | tf_op jit(solution)/shard_map/pallas_call | solution.py:386
  123.6 5.2 %shard_map.52 = f32[64,8192]{1,0:T(8,128)} custom-call(f32[8,128]{1,0:T(8,128)} %get-tuple-element.129.refs_0_, f32[8,128]{1,0:T(8,128)} %copy-done.45, f32[8,128]{1,0:T(8,128)} %copy-done.46, f32[8,128]{1,0:T(8,128)} %copy-done.47, f32[8,128]{1,0:T(8,128)} %copy-done.48, f32[8,128]{1,0:T(8,128)} %copy-done.49, f32[8,128]{1,0:T(8,128)} %copy-done.50, ...), custom_call_target="tpu_custom_call" | custom-call | flops 536870912 | bytes 4194304 | tf_op jit(solution)/shard_map/pallas_call | solution.py:405
  (199 shorter events, 7.6 us)
Async XLA Ops:
  8.5 7.1 %collective-permute-start.1 = (f32[16,128]{1,0:T(8,128)}, f32[16,128]{1,0:T(8,128)S(1)}, u32[]{:S(2)}, u32[]{:S(2)}) collective-permute-start(f32[16,128]{1,0:T(8,128)} %get-tuple-element.78), channel_id=1, source_target_pairs={{0,2},{1,3},{2,0},{3,1},{4,6},{5,7},{6,4},{7,5},{8,10},{9,11},{10,... | collective-permute-start | bytes 24584 | tf_op jit(solution)/shard_map/ppermute | solution.py:300
  11.2 7.2 %collective-permute-start.3 = (f32[16,128]{1,0:T(8,128)}, f32[16,128]{1,0:T(8,128)S(1)}, u32[]{:S(2)}, u32[]{:S(2)}) collective-permute-start(f32[16,128]{1,0:T(8,128)} %get-tuple-element.80), channel_id=1, source_target_pairs={{0,4},{1,5},{2,6},{3,7},{4,0},{5,1},{6,2},{7,3},{8,12},{9,13},{10,... | collective-permute-start | bytes 24584 | tf_op jit(solution)/shard_map/ppermute | solution.py:300
  13.0 5.5 %collective-permute-start.4 = (f32[16,128]{1,0:T(8,128)}, f32[16,128]{1,0:T(8,128)S(1)}, u32[]{:S(2)}, u32[]{:S(2)}) collective-permute-start(f32[16,128]{1,0:T(8,128)} %get-tuple-element.81), channel_id=1, source_target_pairs={{0,5},{1,4},{2,7},{3,6},{4,1},{5,0},{6,3},{7,2},{8,13},{9,12},{10,... | collective-permute-start | bytes 24584 | tf_op jit(solution)/shard_map/ppermute | solution.py:300
  13.0 9.0 %collective-permute-start.5 = (f32[16,128]{1,0:T(8,128)}, f32[16,128]{1,0:T(8,128)S(1)}, u32[]{:S(2)}, u32[]{:S(2)}) collective-permute-start(f32[16,128]{1,0:T(8,128)} %get-tuple-element.82), channel_id=1, source_target_pairs={{0,6},{1,7},{2,4},{3,5},{4,2},{5,3},{6,0},{7,1},{8,14},{9,15},{10,... | collective-permute-start | bytes 24584 | tf_op jit(solution)/shard_map/ppermute | solution.py:300
  15.6 6.5 %collective-permute-start.6 = (f32[16,128]{1,0:T(8,128)}, f32[16,128]{1,0:T(8,128)S(1)}, u32[]{:S(2)}, u32[]{:S(2)}) collective-permute-start(f32[16,128]{1,0:T(8,128)} %get-tuple-element.83), channel_id=1, source_target_pairs={{0,7},{1,6},{2,5},{3,4},{4,3},{5,2},{6,1},{7,0},{8,15},{9,14},{10,... | collective-permute-start | bytes 24584 | tf_op jit(solution)/shard_map/ppermute | solution.py:300
  15.7 9.8 %collective-permute-start.7 = (f32[16,128]{1,0:T(8,128)}, f32[16,128]{1,0:T(8,128)S(1)}, u32[]{:S(2)}, u32[]{:S(2)}) collective-permute-start(f32[16,128]{1,0:T(8,128)} %get-tuple-element.84), channel_id=1, source_target_pairs={{0,8},{1,9},{2,10},{3,11},{4,12},{5,13},{6,14},{7,15},{8,0},{9,1},... | collective-permute-start | bytes 24584 | tf_op jit(solution)/shard_map/ppermute | solution.py:300
  18.4 7.3 %collective-permute-start.8 = (f32[16,128]{1,0:T(8,128)}, f32[16,128]{1,0:T(8,128)S(1)}, u32[]{:S(2)}, u32[]{:S(2)}) collective-permute-start(f32[16,128]{1,0:T(8,128)} %get-tuple-element.85), channel_id=1, source_target_pairs={{0,9},{1,8},{2,11},{3,10},{4,13},{5,12},{6,15},{7,14},{8,1},{9,0},... | collective-permute-start | bytes 24584 | tf_op jit(solution)/shard_map/ppermute | solution.py:300
  18.4 11.6 %collective-permute-start.9 = (f32[16,128]{1,0:T(8,128)}, f32[16,128]{1,0:T(8,128)S(1)}, u32[]{:S(2)}, u32[]{:S(2)}) collective-permute-start(f32[16,128]{1,0:T(8,128)} %get-tuple-element.86), channel_id=1, source_target_pairs={{0,10},{1,11},{2,8},{3,9},{4,14},{5,15},{6,12},{7,13},{8,2},{9,3},... | collective-permute-start | bytes 24584 | tf_op jit(solution)/shard_map/ppermute | solution.py:300
  21.9 8.3 %collective-permute-start.10 = (f32[16,128]{1,0:T(8,128)}, f32[16,128]{1,0:T(8,128)S(1)}, u32[]{:S(2)}, u32[]{:S(2)}) collective-permute-start(f32[16,128]{1,0:T(8,128)} %get-tuple-element.87), channel_id=1, source_target_pairs={{0,11},{1,10},{2,9},{3,8},{4,15},{5,14},{6,13},{7,12},{8,3},{9,2},... | collective-permute-start | bytes 24584 | tf_op jit(solution)/shard_map/ppermute | solution.py:300
  22.1 8.1 %collective-permute-start.11 = (f32[16,128]{1,0:T(8,128)}, f32[16,128]{1,0:T(8,128)S(1)}, u32[]{:S(2)}, u32[]{:S(2)}) collective-permute-start(f32[16,128]{1,0:T(8,128)} %get-tuple-element.88), channel_id=1, source_target_pairs={{0,12},{1,13},{2,14},{3,15},{4,8},{5,9},{6,10},{7,11},{8,4},{9,5},... | collective-permute-start | bytes 24584 | tf_op jit(solution)/shard_map/ppermute | solution.py:300
  25.6 6.6 %collective-permute-start.13 = (f32[16,128]{1,0:T(8,128)}, f32[16,128]{1,0:T(8,128)S(1)}, u32[]{:S(2)}, u32[]{:S(2)}) collective-permute-start(f32[16,128]{1,0:T(8,128)} %get-tuple-element.90), channel_id=1, source_target_pairs={{0,14},{1,15},{2,12},{3,13},{4,10},{5,11},{6,8},{7,9},{8,6},{9,7},... | collective-permute-start | bytes 24584 | tf_op jit(solution)/shard_map/ppermute | solution.py:300
  30.1 6.0 %collective-permute-start.14 = (f32[16,128]{1,0:T(8,128)}, f32[16,128]{1,0:T(8,128)S(1)}, u32[]{:S(2)}, u32[]{:S(2)}) collective-permute-start(f32[16,128]{1,0:T(8,128)} %get-tuple-element.91), channel_id=1, source_target_pairs={{0,15},{1,14},{2,13},{3,12},{4,11},{5,10},{6,9},{7,8},{8,7},{9,6},... | collective-permute-start | bytes 24584 | tf_op jit(solution)/shard_map/ppermute | solution.py:300
  40.4 5.6 %collective-permute-start.17 = (f32[8,128]{1,0:T(8,128)}, f32[8,128]{1,0:T(8,128)S(1)}, u32[]{:S(2)}, u32[]{:S(2)}) collective-permute-start(f32[8,128]{1,0:T(8,128)} %get-tuple-element.95), channel_id=1, source_target_pairs={{0,3},{1,2},{2,1},{3,0},{4,7},{5,6},{6,5},{7,4},{8,11},{9,10},{10,... | collective-permute-start | bytes 12296 | tf_op jit(solution)/shard_map/ppermute | solution.py:300
  41.6 7.1 %collective-permute-start.19 = (f32[8,128]{1,0:T(8,128)}, f32[8,128]{1,0:T(8,128)S(1)}, u32[]{:S(2)}, u32[]{:S(2)}) collective-permute-start(f32[8,128]{1,0:T(8,128)} %get-tuple-element.97), channel_id=1, source_target_pairs={{0,5},{1,4},{2,7},{3,6},{4,1},{5,0},{6,3},{7,2},{8,13},{9,12},{10,... | collective-permute-start | bytes 12296 | tf_op jit(solution)/shard_map/ppermute | solution.py:300
  43.4 5.6 %collective-permute-start.20 = (f32[8,128]{1,0:T(8,128)}, f32[8,128]{1,0:T(8,128)S(1)}, u32[]{:S(2)}, u32[]{:S(2)}) collective-permute-start(f32[8,128]{1,0:T(8,128)} %get-tuple-element.98), channel_id=1, source_target_pairs={{0,6},{1,7},{2,4},{3,5},{4,2},{5,3},{6,0},{7,1},{8,14},{9,15},{10,... | collective-permute-start | bytes 12296 | tf_op jit(solution)/shard_map/ppermute | solution.py:300
  43.7 8.5 %collective-permute-start.21 = (f32[8,128]{1,0:T(8,128)}, f32[8,128]{1,0:T(8,128)S(1)}, u32[]{:S(2)}, u32[]{:S(2)}) collective-permute-start(f32[8,128]{1,0:T(8,128)} %get-tuple-element.99), channel_id=1, source_target_pairs={{0,7},{1,6},{2,5},{3,4},{4,3},{5,2},{6,1},{7,0},{8,15},{9,14},{10,... | collective-permute-start | bytes 12296 | tf_op jit(solution)/shard_map/ppermute | solution.py:300
  46.0 6.6 %collective-permute-start.22 = (f32[8,128]{1,0:T(8,128)}, f32[8,128]{1,0:T(8,128)S(1)}, u32[]{:S(2)}, u32[]{:S(2)}) collective-permute-start(f32[8,128]{1,0:T(8,128)} %get-tuple-element.100), channel_id=1, source_target_pairs={{0,8},{1,9},{2,10},{3,11},{4,12},{5,13},{6,14},{7,15},{8,0},{9,1},... | collective-permute-start | bytes 12296 | tf_op jit(solution)/shard_map/ppermute | solution.py:300
  46.0 9.8 %collective-permute-start.23 = (f32[8,128]{1,0:T(8,128)}, f32[8,128]{1,0:T(8,128)S(1)}, u32[]{:S(2)}, u32[]{:S(2)}) collective-permute-start(f32[8,128]{1,0:T(8,128)} %get-tuple-element.101), channel_id=1, source_target_pairs={{0,9},{1,8},{2,11},{3,10},{4,13},{5,12},{6,15},{7,14},{8,1},{9,0},... | collective-permute-start | bytes 12296 | tf_op jit(solution)/shard_map/ppermute | solution.py:300
  48.7 7.6 %collective-permute-start.24 = (f32[8,128]{1,0:T(8,128)}, f32[8,128]{1,0:T(8,128)S(1)}, u32[]{:S(2)}, u32[]{:S(2)}) collective-permute-start(f32[8,128]{1,0:T(8,128)} %get-tuple-element.102), channel_id=1, source_target_pairs={{0,10},{1,11},{2,8},{3,9},{4,14},{5,15},{6,12},{7,13},{8,2},{9,3},... | collective-permute-start | bytes 12296 | tf_op jit(solution)/shard_map/ppermute | solution.py:300
  49.0 15.2 %collective-permute-start.25 = (f32[8,128]{1,0:T(8,128)}, f32[8,128]{1,0:T(8,128)S(1)}, u32[]{:S(2)}, u32[]{:S(2)}) collective-permute-start(f32[8,128]{1,0:T(8,128)} %get-tuple-element.103), channel_id=1, source_target_pairs={{0,11},{1,10},{2,9},{3,8},{4,15},{5,14},{6,13},{7,12},{8,3},{9,2},... | collective-permute-start | bytes 12296 | tf_op jit(solution)/shard_map/ppermute | solution.py:300
  52.2 12.1 %collective-permute-start.26 = (f32[8,128]{1,0:T(8,128)}, f32[8,128]{1,0:T(8,128)S(1)}, u32[]{:S(2)}, u32[]{:S(2)}) collective-permute-start(f32[8,128]{1,0:T(8,128)} %get-tuple-element.104), channel_id=1, source_target_pairs={{0,12},{1,13},{2,14},{3,15},{4,8},{5,9},{6,10},{7,11},{8,4},{9,5},... | collective-permute-start | bytes 12296 | tf_op jit(solution)/shard_map/ppermute | solution.py:300
  52.6 11.7 %collective-permute-start.27 = (f32[8,128]{1,0:T(8,128)}, f32[8,128]{1,0:T(8,128)S(1)}, u32[]{:S(2)}, u32[]{:S(2)}) collective-permute-start(f32[8,128]{1,0:T(8,128)} %get-tuple-element.105), channel_id=1, source_target_pairs={{0,13},{1,12},{2,15},{3,14},{4,9},{5,8},{6,11},{7,10},{8,5},{9,4},... | collective-permute-start | bytes 12296 | tf_op jit(solution)/shard_map/ppermute | solution.py:300
  55.8 8.5 %collective-permute-start.28 = (f32[8,128]{1,0:T(8,128)}, f32[8,128]{1,0:T(8,128)S(1)}, u32[]{:S(2)}, u32[]{:S(2)}) collective-permute-start(f32[8,128]{1,0:T(8,128)} %get-tuple-element.106), channel_id=1, source_target_pairs={{0,14},{1,15},{2,12},{3,13},{4,10},{5,11},{6,8},{7,9},{8,6},{9,7},... | collective-permute-start | bytes 12296 | tf_op jit(solution)/shard_map/ppermute | solution.py:300
  56.3 8.0 %collective-permute-start.29 = (f32[8,128]{1,0:T(8,128)}, f32[8,128]{1,0:T(8,128)S(1)}, u32[]{:S(2)}, u32[]{:S(2)}) collective-permute-start(f32[8,128]{1,0:T(8,128)} %get-tuple-element.107), channel_id=1, source_target_pairs={{0,15},{1,14},{2,13},{3,12},{4,11},{5,10},{6,9},{7,8},{8,7},{9,6},... | collective-permute-start | bytes 12296 | tf_op jit(solution)/shard_map/ppermute | solution.py:300
  70.7 7.4 %collective-permute-start.34 = (f32[8,128]{1,0:T(8,128)}, f32[8,128]{1,0:T(8,128)S(1)}, u32[]{:S(2)}, u32[]{:S(2)}) collective-permute-start(f32[8,128]{1,0:T(8,128)} %get-tuple-element.116), channel_id=1, source_target_pairs={{0,5},{1,4},{2,7},{3,6},{4,1},{5,0},{6,3},{7,2},{8,13},{9,12},{10,... | collective-permute-start | bytes 12296 | tf_op jit(solution)/shard_map/ppermute | solution.py:300
  72.8 6.0 %collective-permute-start.35 = (f32[8,128]{1,0:T(8,128)}, f32[8,128]{1,0:T(8,128)S(1)}, u32[]{:S(2)}, u32[]{:S(2)}) collective-permute-start(f32[8,128]{1,0:T(8,128)} %get-tuple-element.117), channel_id=1, source_target_pairs={{0,6},{1,7},{2,4},{3,5},{4,2},{5,3},{6,0},{7,1},{8,14},{9,15},{10,... | collective-permute-start | bytes 12296 | tf_op jit(solution)/shard_map/ppermute | solution.py:300
  73.1 8.2 %collective-permute-start.36 = (f32[8,128]{1,0:T(8,128)}, f32[8,128]{1,0:T(8,128)S(1)}, u32[]{:S(2)}, u32[]{:S(2)}) collective-permute-start(f32[8,128]{1,0:T(8,128)} %get-tuple-element.118), channel_id=1, source_target_pairs={{0,7},{1,6},{2,5},{3,4},{4,3},{5,2},{6,1},{7,0},{8,15},{9,14},{10,... | collective-permute-start | bytes 12296 | tf_op jit(solution)/shard_map/ppermute | solution.py:300
  75.1 7.4 %collective-permute-start.37 = (f32[8,128]{1,0:T(8,128)}, f32[8,128]{1,0:T(8,128)S(1)}, u32[]{:S(2)}, u32[]{:S(2)}) collective-permute-start(f32[8,128]{1,0:T(8,128)} %get-tuple-element.119), channel_id=1, source_target_pairs={{0,8},{1,9},{2,10},{3,11},{4,12},{5,13},{6,14},{7,15},{8,0},{9,1},... | collective-permute-start | bytes 12296 | tf_op jit(solution)/shard_map/ppermute | solution.py:300
  75.3 9.9 %collective-permute-start.38 = (f32[8,128]{1,0:T(8,128)}, f32[8,128]{1,0:T(8,128)S(1)}, u32[]{:S(2)}, u32[]{:S(2)}) collective-permute-start(f32[8,128]{1,0:T(8,128)} %get-tuple-element.120), channel_id=1, source_target_pairs={{0,9},{1,8},{2,11},{3,10},{4,13},{5,12},{6,15},{7,14},{8,1},{9,0},... | collective-permute-start | bytes 12296 | tf_op jit(solution)/shard_map/ppermute | solution.py:300
  78.1 9.0 %collective-permute-start.39 = (f32[8,128]{1,0:T(8,128)}, f32[8,128]{1,0:T(8,128)S(1)}, u32[]{:S(2)}, u32[]{:S(2)}) collective-permute-start(f32[8,128]{1,0:T(8,128)} %get-tuple-element.121), channel_id=1, source_target_pairs={{0,10},{1,11},{2,8},{3,9},{4,14},{5,15},{6,12},{7,13},{8,2},{9,3},... | collective-permute-start | bytes 12296 | tf_op jit(solution)/shard_map/ppermute | solution.py:300
  78.8 10.6 %collective-permute-start.40 = (f32[8,128]{1,0:T(8,128)}, f32[8,128]{1,0:T(8,128)S(1)}, u32[]{:S(2)}, u32[]{:S(2)}) collective-permute-start(f32[8,128]{1,0:T(8,128)} %get-tuple-element.122), channel_id=1, source_target_pairs={{0,11},{1,10},{2,9},{3,8},{4,15},{5,14},{6,13},{7,12},{8,3},{9,2},... | collective-permute-start | bytes 12296 | tf_op jit(solution)/shard_map/ppermute | solution.py:300
  81.3 8.0 %collective-permute-start.41 = (f32[8,128]{1,0:T(8,128)}, f32[8,128]{1,0:T(8,128)S(1)}, u32[]{:S(2)}, u32[]{:S(2)}) collective-permute-start(f32[8,128]{1,0:T(8,128)} %get-tuple-element.123), channel_id=1, source_target_pairs={{0,12},{1,13},{2,14},{3,15},{4,8},{5,9},{6,10},{7,11},{8,4},{9,5},... | collective-permute-start | bytes 12296 | tf_op jit(solution)/shard_map/ppermute | solution.py:300
  82.5 6.9 %collective-permute-start.42 = (f32[8,128]{1,0:T(8,128)}, f32[8,128]{1,0:T(8,128)S(1)}, u32[]{:S(2)}, u32[]{:S(2)}) collective-permute-start(f32[8,128]{1,0:T(8,128)} %get-tuple-element.124), channel_id=1, source_target_pairs={{0,13},{1,12},{2,15},{3,14},{4,9},{5,8},{6,11},{7,10},{8,5},{9,4},... | collective-permute-start | bytes 12296 | tf_op jit(solution)/shard_map/ppermute | solution.py:300
  85.2 6.5 %collective-permute-start.43 = (f32[8,128]{1,0:T(8,128)}, f32[8,128]{1,0:T(8,128)S(1)}, u32[]{:S(2)}, u32[]{:S(2)}) collective-permute-start(f32[8,128]{1,0:T(8,128)} %get-tuple-element.125), channel_id=1, source_target_pairs={{0,14},{1,15},{2,12},{3,13},{4,10},{5,11},{6,8},{7,9},{8,6},{9,7},... | collective-permute-start | bytes 12296 | tf_op jit(solution)/shard_map/ppermute | solution.py:300
  87.1 5.9 %collective-permute-start.44 = (f32[8,128]{1,0:T(8,128)}, f32[8,128]{1,0:T(8,128)S(1)}, u32[]{:S(2)}, u32[]{:S(2)}) collective-permute-start(f32[8,128]{1,0:T(8,128)} %get-tuple-element.126), channel_id=1, source_target_pairs={{0,15},{1,14},{2,13},{3,12},{4,11},{5,10},{6,9},{7,8},{8,7},{9,6},... | collective-permute-start | bytes 12296 | tf_op jit(solution)/shard_map/ppermute | solution.py:300
  97.3 5.6 %collective-permute-start.47 = (f32[8,128]{1,0:T(8,128)}, f32[8,128]{1,0:T(8,128)S(1)}, u32[]{:S(2)}, u32[]{:S(2)}) collective-permute-start(f32[8,128]{1,0:T(8,128)} %get-tuple-element.132), channel_id=1, source_target_pairs={{0,3},{1,2},{2,1},{3,0},{4,7},{5,6},{6,5},{7,4},{8,11},{9,10},{10,... | collective-permute-start | bytes 12296 | tf_op jit(solution)/shard_map/ppermute | solution.py:300
  98.5 5.3 %collective-permute-start.48 = (f32[8,128]{1,0:T(8,128)}, f32[8,128]{1,0:T(8,128)S(1)}, u32[]{:S(2)}, u32[]{:S(2)}) collective-permute-start(f32[8,128]{1,0:T(8,128)} %get-tuple-element.133), channel_id=1, source_target_pairs={{0,4},{1,5},{2,6},{3,7},{4,0},{5,1},{6,2},{7,3},{8,12},{9,13},{10,... | collective-permute-start | bytes 12296 | tf_op jit(solution)/shard_map/ppermute | solution.py:300
  98.5 7.1 %collective-permute-start.49 = (f32[8,128]{1,0:T(8,128)}, f32[8,128]{1,0:T(8,128)S(1)}, u32[]{:S(2)}, u32[]{:S(2)}) collective-permute-start(f32[8,128]{1,0:T(8,128)} %get-tuple-element.134), channel_id=1, source_target_pairs={{0,5},{1,4},{2,7},{3,6},{4,1},{5,0},{6,3},{7,2},{8,13},{9,12},{10,... | collective-permute-start | bytes 12296 | tf_op jit(solution)/shard_map/ppermute | solution.py:300
  100.3 7.1 %collective-permute-start.50 = (f32[8,128]{1,0:T(8,128)}, f32[8,128]{1,0:T(8,128)S(1)}, u32[]{:S(2)}, u32[]{:S(2)}) collective-permute-start(f32[8,128]{1,0:T(8,128)} %get-tuple-element.135), channel_id=1, source_target_pairs={{0,6},{1,7},{2,4},{3,5},{4,2},{5,3},{6,0},{7,1},{8,14},{9,15},{10,... | collective-permute-start | bytes 12296 | tf_op jit(solution)/shard_map/ppermute | solution.py:300
  100.6 8.5 %collective-permute-start.51 = (f32[8,128]{1,0:T(8,128)}, f32[8,128]{1,0:T(8,128)S(1)}, u32[]{:S(2)}, u32[]{:S(2)}) collective-permute-start(f32[8,128]{1,0:T(8,128)} %get-tuple-element.136), channel_id=1, source_target_pairs={{0,7},{1,6},{2,5},{3,4},{4,3},{5,2},{6,1},{7,0},{8,15},{9,14},{10,... | collective-permute-start | bytes 12296 | tf_op jit(solution)/shard_map/ppermute | solution.py:300
  102.9 8.2 %collective-permute-start.52 = (f32[8,128]{1,0:T(8,128)}, f32[8,128]{1,0:T(8,128)S(1)}, u32[]{:S(2)}, u32[]{:S(2)}) collective-permute-start(f32[8,128]{1,0:T(8,128)} %get-tuple-element.137), channel_id=1, source_target_pairs={{0,8},{1,9},{2,10},{3,11},{4,12},{5,13},{6,14},{7,15},{8,0},{9,1},... | collective-permute-start | bytes 12296 | tf_op jit(solution)/shard_map/ppermute | solution.py:300
  103.8 8.9 %collective-permute-start.53 = (f32[8,128]{1,0:T(8,128)}, f32[8,128]{1,0:T(8,128)S(1)}, u32[]{:S(2)}, u32[]{:S(2)}) collective-permute-start(f32[8,128]{1,0:T(8,128)} %get-tuple-element.138), channel_id=1, source_target_pairs={{0,9},{1,8},{2,11},{3,10},{4,13},{5,12},{6,15},{7,14},{8,1},{9,0},... | collective-permute-start | bytes 12296 | tf_op jit(solution)/shard_map/ppermute | solution.py:300
  105.6 9.9 %collective-permute-start.54 = (f32[8,128]{1,0:T(8,128)}, f32[8,128]{1,0:T(8,128)S(1)}, u32[]{:S(2)}, u32[]{:S(2)}) collective-permute-start(f32[8,128]{1,0:T(8,128)} %get-tuple-element.139), channel_id=1, source_target_pairs={{0,10},{1,11},{2,8},{3,9},{4,14},{5,15},{6,12},{7,13},{8,2},{9,3},... | collective-permute-start | bytes 12296 | tf_op jit(solution)/shard_map/ppermute | solution.py:300
  107.4 15.5 %collective-permute-start.55 = (f32[8,128]{1,0:T(8,128)}, f32[8,128]{1,0:T(8,128)S(1)}, u32[]{:S(2)}, u32[]{:S(2)}) collective-permute-start(f32[8,128]{1,0:T(8,128)} %get-tuple-element.140), channel_id=1, source_target_pairs={{0,11},{1,10},{2,9},{3,8},{4,15},{5,14},{6,13},{7,12},{8,3},{9,2},... | collective-permute-start | bytes 12296 | tf_op jit(solution)/shard_map/ppermute | solution.py:300
  109.1 13.8 %collective-permute-start.56 = (f32[8,128]{1,0:T(8,128)}, f32[8,128]{1,0:T(8,128)S(1)}, u32[]{:S(2)}, u32[]{:S(2)}) collective-permute-start(f32[8,128]{1,0:T(8,128)} %get-tuple-element.141), channel_id=1, source_target_pairs={{0,12},{1,13},{2,14},{3,15},{4,8},{5,9},{6,10},{7,11},{8,4},{9,5},... | collective-permute-start | bytes 12296 | tf_op jit(solution)/shard_map/ppermute | solution.py:300
  111.1 11.8 %collective-permute-start.57 = (f32[8,128]{1,0:T(8,128)}, f32[8,128]{1,0:T(8,128)S(1)}, u32[]{:S(2)}, u32[]{:S(2)}) collective-permute-start(f32[8,128]{1,0:T(8,128)} %get-tuple-element.142), channel_id=1, source_target_pairs={{0,13},{1,12},{2,15},{3,14},{4,9},{5,8},{6,11},{7,10},{8,5},{9,4},... | collective-permute-start | bytes 12296 | tf_op jit(solution)/shard_map/ppermute | solution.py:300
  112.7 10.2 %collective-permute-start.58 = (f32[8,128]{1,0:T(8,128)}, f32[8,128]{1,0:T(8,128)S(1)}, u32[]{:S(2)}, u32[]{:S(2)}) collective-permute-start(f32[8,128]{1,0:T(8,128)} %get-tuple-element.143), channel_id=1, source_target_pairs={{0,14},{1,15},{2,12},{3,13},{4,10},{5,11},{6,8},{7,9},{8,6},{9,7},... | collective-permute-start | bytes 12296 | tf_op jit(solution)/shard_map/ppermute | solution.py:300
  115.5 7.4 %collective-permute-start.59 = (f32[8,128]{1,0:T(8,128)}, f32[8,128]{1,0:T(8,128)S(1)}, u32[]{:S(2)}, u32[]{:S(2)}) collective-permute-start(f32[8,128]{1,0:T(8,128)} %get-tuple-element.144), channel_id=1, source_target_pairs={{0,15},{1,14},{2,13},{3,12},{4,11},{5,10},{6,9},{7,8},{8,7},{9,6},... | collective-permute-start | bytes 12296 | tf_op jit(solution)/shard_map/ppermute | solution.py:300
  (72 other events, 698.1 us)

commit v3 on v2

--- a/solution.py
+++ b/solution.py
@@ -100,16 +100,10 @@
         copy.wait()
 
 
-def tiles_out(n, buffer, outs, sem):
-    me = lax.axis_index("rows")
-    return [pltpu.make_async_copy(buffer.at[me ^ k], outs[k], sem.at[k]) for k in range(n)]
-
-
-def tiles_in(n, ins, buffer, sem, by_device):
-    me = lax.axis_index("rows")
-    return [
-        pltpu.make_async_copy(ins[k], buffer.at[me ^ k] if by_device else buffer.at[k], sem.at[k]) for k in range(n)
-    ]
+def move(source, target, sem):
+    copy = pltpu.make_async_copy(source, target, sem)
+    copy.start()
+    copy.wait()
 
 
 def column_copies(source, target, sems):
@@ -118,9 +112,9 @@
     return [pltpu.make_async_copy(source.at[:, cut], target.at[:, cut], sems.at[b]) for b, cut in enumerate(cuts)]
 
 
-def sums_kernel(n, pad, probes, lengths_in, ids_in, firms_in, *refs):
-    outs, (own, own_count, mask_ids, weight) = refs[:n], refs[n : n + 4]
-    valid, x, acc, lengths, ids, firms, buffer, sems, small, sem = refs[n + 4 :]
+def sums_kernel(n, pad, *refs):
+    probes, lengths_in, ids_in, firms_in, send, own, own_count, mask_ids, weight = refs[:9]
+    valid, x, acc, lengths, ids, firms, buffer, sems, small, sem = refs[9:]
     copies = column_copies(probes, x, sems)
     first = [
         pltpu.make_async_copy(source, target, small.at[k])
@@ -167,9 +161,7 @@
     about = jnp.where(left_of((slots, LANES)), column(firms[...].astype(F32)), count).reshape(n, 2, 8, LANES)
     even = iota((n, 8, LANES), 2) // (LANES // 4) % 2 == 0
     buffer[:, 8:] = jnp.where(even, about[:, 0], about[:, 1])
-    copies = tiles_out(n, buffer, outs, sem)
-    start_all(copies)
-    wait_all(copies)
+    move(buffer, send, sem)
 
 
 def worker_kernel(pad, lengths, mask_ids, out):
@@ -197,12 +189,9 @@
     return jnp.where(left_of((8 * n, LANES)), total[: 8 * n], total[8 * n :]).reshape(n, 8, LANES)
 
 
-def owner_first_kernel(n, *refs):
-    ins, outs, (table, scale) = refs[:n], refs[n : 2 * n], refs[2 * n : 2 * n + 2]
-    buffer, back, in_sem, sem = refs[2 * n + 2 :]
-    copies = tiles_in(n, ins, buffer, in_sem, False)
-    start_all(copies)
-    wait_all(copies)
+def owner_first_kernel(received, send, table, scale, buffer, back, in_sem, sem):
+    n = buffer.shape[0]
+    move(received, buffer, in_sem)
     about = buffer[:, 8:].reshape(8 * n, LANES)
     quarter = LANES // 4
 
@@ -217,42 +206,24 @@
     count = jnp.sum(jnp.where(same, along(counts), 0.0), axis=1, keepdims=True)
     scale[...] = jnp.broadcast_to(1.0 / jnp.maximum(count, 1.0), scale.shape)
     back[...] = owner_means(buffer[:, :8], table[...], scale[...])
-    copies = tiles_out_in_place(n, back, outs, sem)
-    start_all(copies)
-    wait_all(copies)
-
-
-def owner_second_kernel(n, *refs):
-    ins, (table, scale), outs = refs[:n], refs[n : n + 2], refs[n + 2 : 2 * n + 2]
-    buffer, back, in_sem, sem = refs[2 * n + 2 :]
-    copies = tiles_in(n, ins, buffer, in_sem, False)
-    start_all(copies)
-    wait_all(copies)
+    move(back, send, sem)
+
+
+def owner_second_kernel(received, table, scale, send, buffer, back, in_sem, sem):
+    move(received, buffer, in_sem)
     back[...] = owner_means(buffer[...], table[...], scale[...])
-    copies = tiles_out_in_place(n, back, outs, sem)
-    start_all(copies)
-    wait_all(copies)
-
-
-def tiles_out_in_place(n, buffer, outs, sem):
-    return [pltpu.make_async_copy(buffer.at[k], outs[k], sem.at[k]) for k in range(n)]
-
-
-def change_kernel(n, *refs):
-    ins, (own, own_count, pairs), outs, mean = refs[:n], refs[n : n + 3], refs[n + 3 : 2 * n + 3], refs[2 * n + 3]
-    buffer, back, in_sem, sem = refs[2 * n + 4 :]
-    copies = tiles_in(n, ins, buffer, in_sem, True)
-    start_all(copies)
-    wait_all(copies)
+    move(back, send, sem)
+
+
+def change_kernel(received, own, own_count, pairs, send, mean, buffer, back, in_sem, sem):
+    move(received, buffer, in_sem)
     slots = own.shape[0]
     found = from_tiles(buffer[...])
     mean[...] = found
     change = dot(pairs[...], halves(found).astype(BF16))
     new = own[...] - own_count[...] * found + fold(change[:slots] + change[slots:])
-    back[...] = to_tiles(new, n)
-    copies = tiles_out(n, back, outs, sem)
-    start_all(copies)
-    wait_all(copies)
+    back[...] = to_tiles(new, buffer.shape[0])
+    move(back, send, sem)
 
 
 def take(parts, ids, slots):
@@ -277,14 +248,12 @@
     wait_all(outs)
 
 
-def last_kernel(n, *refs):
-    arrived, (before, mask_ids, out) = refs[:n], refs[n : n + 3]
-    buffer, x, y, tile_sem, in_sems, out_sems = refs[n + 3 :]
+def last_kernel(received, before, mask_ids, out, buffer, x, y, tile_sem, in_sems, out_sems):
     ins, outs = column_copies(before, x, in_sems), column_copies(y, out, out_sems)
-    copies = tiles_in(n, arrived, buffer, tile_sem, True)
-    start_all(copies)
+    copy = pltpu.make_async_copy(received, buffer, tile_sem)
+    copy.start()
     start_all(ins)
-    wait_all(copies)
+    copy.wait()
     mean = from_tiles(buffer[...])
     parts = halves(mean).T.astype(BF16)
     for b in range(len(ins)):
@@ -296,8 +265,7 @@
 
 
 def exchange(tiles):
-    n = len(tiles)
-    return [tiles[0]] + [lax.ppermute(tiles[k], "rows", [(i, i ^ k) for i in range(n)]) for k in range(1, n)]
+    return lax.all_to_all(tiles, "rows", split_axis=0, concat_axis=0, tiled=True)
 
 
 def call(kernel, out_shape, in_specs, out_specs, scratch, flops, moved):
@@ -327,17 +295,17 @@
     of_rows = (rows_dev // LANES, LANES)
     work = 2 * rows_dev * slots * 2 * columns
     sems = pltpu.SemaphoreType.DMA((blocks,))
-    sem = pltpu.SemaphoreType.DMA((n,))
+    sem = pltpu.SemaphoreType.DMA
     whole = pltpu.VMEM((columns, rows_dev), F32)
     of_slots = array((slots, LANES), F32)
-    tile, tall = array((8, LANES), F32), array((16, LANES), F32)
+    all_tiles, all_talls = array((n, 8, LANES), F32), array((n, 16, LANES), F32)
     tiles, talls = pltpu.VMEM((n, 8, LANES), F32), pltpu.VMEM((n, 16, LANES), F32)
 
-    *send, own, own_count, mask_ids, weight = call(
+    send, own, own_count, mask_ids, weight = call(
         functools.partial(sums_kernel, n, pad),
-        [tall] * n + [of_slots, of_slots, array(of_rows, jnp.int32), array(of_rows, F32)],
+        [all_talls, of_slots, of_slots, array(of_rows, jnp.int32), array(of_rows, F32)],
         [anywhere] * 4,
-        [anywhere] * n + [vmem] * 4,
+        [anywhere] + [vmem] * 4,
         [
             pltpu.VMEM(of_rows, F32),
             whole,
@@ -363,25 +331,25 @@
         2 * work,
         4 * slots * slots,
     )(lengths, mask_ids)
-    *send, table, scale = call(
-        functools.partial(owner_first_kernel, n),
-        [tile] * n + [array((slots, slots), BF16), of_slots],
-        [anywhere] * n,
-        [anywhere] * n + [vmem] * 2,
+    send, table, scale = call(
+        owner_first_kernel,
+        [all_tiles, array((slots, slots), BF16), of_slots],
+        [anywhere],
+        [anywhere] + [vmem] * 2,
         [talls, tiles, sem, sem],
         work // 16,
         slots * slots * 4,
-    )(*received)
+    )(received)
     received = exchange(send)
-    *send, mean = call(
-        functools.partial(change_kernel, n),
-        [tile] * n + [of_slots],
-        [anywhere] * n + [vmem] * 3,
-        [anywhere] * n + [vmem],
+    send, mean = call(
+        change_kernel,
+        [all_tiles, of_slots],
+        [anywhere] + [vmem] * 3,
+        [anywhere, vmem],
         [tiles, tiles, sem, sem],
         work // 16,
         slots * slots * 4,
-    )(*received, own, own_count, pairs)
+    )(received, own, own_count, pairs)
     received = exchange(send)
     before = call(
         functools.partial(first_kernel, pad),
@@ -393,24 +361,24 @@
         8 * columns * rows_dev,
     )(probes, mean, mask_ids, weight)
     send = call(
-        functools.partial(owner_second_kernel, n),
-        [tile] * n,
-        [anywhere] * n + [vmem] * 2,
-        [anywhere] * n,
+        owner_second_kernel,
+        all_tiles,
+        [anywhere] + [vmem] * 2,
+        anywhere,
         [tiles, tiles, sem, sem],
         work // 16,
         slots * slots * 4,
-    )(*received, table, scale)
+    )(received, table, scale)
     received = exchange(send)
     return call(
-        functools.partial(last_kernel, n),
+        last_kernel,
         array((columns, rows_dev), F32),
-        [anywhere] * n + [anywhere, vmem],
+        [anywhere, anywhere, vmem],
         anywhere,
         [tiles, whole, whole, sem, sems, sems],
         work,
         8 * columns * rows_dev,
-    )(*received, before, mask_ids)
+    )(received, before, mask_ids)
 
 
 def solution(mesh):

time: 129 us -> 71.3 us (0.55)
  starting transfers between devices: 83.5 us -> 7.01 us
  blocking collectives: 0 us -> 26.5 us
  waiting for transfers between devices: 9.76 us -> 3.99 us
    ppermute x60 -> x0, starting transfers between devices: 83.5 us -> none  [exchange(): lax.ppermute(tiles[k], 'rows', [(i, i ^ k) for i in range(n)])]
    all_to_all x0 -> x2, blocking collectives: none -> 26.5 us  [exchange(): lax.all_to_all(tiles, 'rows', split_axis=0, concat_axis=0, tiled=True)]
    ppermute x60 -> x0, waiting for transfers between devices: 9.76 us -> none  [exchange(): lax.ppermute(tiles[k], 'rows', [(i, i ^ k) for i in range(n)])]
    all_to_all x0 -> x2, starting transfers between devices: none -> 7.01 us  [exchange(): lax.all_to_all(tiles, 'rows', split_axis=0, concat_axis=0, tiled=True)]
    all_to_all x0 -> x2, waiting for transfers between devices: none -> 3.99 us  [exchange(): lax.all_to_all(tiles, 'rows', split_axis=0, concat_axis=0, tiled=True)]
  transfers between devices with their start and end apart: 60 -> 2, of which waited for: 8 -> 2; matrix products, arithmetic and copies ran while one was open for 0% -> 0% of each run, Pallas kernels for 8% -> 14%
where the time goes in v3:
time: 71.3 us; the launch traced here: 70.6 us
  Pallas kernels  31.7 us (44%)
  blocking collectives  26.5 us (37%)
  starting transfers between devices  7.01 us (10%)
  waiting for transfers between devices  3.99 us (6%)
  local copies, waits for them, and re-layouts  1.25 us (2%)
    all_to_all x2, blocking collectives, exchange(): lax.all_to_all(tiles, 'rows', split_axis=0, concat_axis=0, tiled=True)  26.5 us
    pallas_call x1, Pallas kernels, body(): call(functools.partial(sums_kernel, n, pad), [all_talls, of_slots, of_slo...  7.79 us
    all_to_all x2, starting transfers between devices, exchange(): lax.all_to_all(tiles, 'rows', split_axis=0, concat_axis=0, tiled=True)  7.01 us
    pallas_call x1, Pallas kernels, body(): call(functools.partial(first_kernel, pad), array((columns, rows_dev), F32...  5.65 us
    pallas_call x1, Pallas kernels, body(): call(last_kernel, array((columns, rows_dev), F32), [anywhere, anywhere, v...  5.11 us
    pallas_call x1, Pallas kernels, body(): call(functools.partial(worker_kernel, pad), array((2 * slots, slots), BF1...  4.06 us
    all_to_all x2, waiting for transfers between devices, exchange(): lax.all_to_all(tiles, 'rows', split_axis=0, concat_axis=0, tiled=True)  3.99 us
    pallas_call x1, Pallas kernels, body(): call(change_kernel, [all_tiles, of_slots], [anywhere] + [vmem] * 3, [anyw...  3.57 us
  transfers between devices with their start and end apart: 2, of which 2 were waited for; matrix products, arithmetic and copies ran while one was open for 0% of the time, Pallas kernels for 14%

profile of v3, /device:TPU:0, one launch (start us, length us, event | category | flops | bytes accessed | tf_op | source)
XLA Modules:
  0.0 70.6 jit_solution(1950563778124328148)
XLA Ops:
  0.0 7.8 %shard_map.46 = (f32[16,16,128]{2,1,0:T(8,128)}, f32[256,128]{1,0:T(8,128)}, f32[256,128]{1,0:T(8,128)}, s32[64,128]{1,0:T(8,128)}, f32[64,128]{1,0:T(8,128)}) custom-call(f32[64,8192]{1,0:T(8,128)} %probes.1, s32[8,128]{1,0:T(8,128)} %bitcast.4, s32[64,128]{1,0:T(8,128)} %bitcast.3, s32[2,128]{1,0:T(2,128)} %bitcast.6), custom_call_target="tpu_custom_call" | custom-call | flops 1073741824 | bytes 2097152 | tf_op jit(solution)/shard_map/pallas_call | solution.py:304
  7.8 15.4 %all_to_all.20.received = f32[16,16,128]{2,1,0:T(8,128)} all-to-all(f32[16,16,128]{2,1,0:T(8,128)} %get-tuple-element.15), channel_id=1, replica_groups=mesh['grp'=2,'rows'=16] {'rows'}, dimensions={0} | all-to-all | bytes 262144 | tf_op jit(solution)/shard_map/all_to_all | solution.py:268
  23.2 2.8 %shard_map.47 = (f32[16,8,128]{2,1,0:T(8,128)}, bf16[256,256]{1,0:T(8,128)(2,1)}, f32[256,128]{1,0:T(8,128)}) custom-call(f32[16,16,128]{2,1,0:T(8,128)} %all_to_all.20.received), custom_call_target="tpu_custom_call" | custom-call | flops 33554432 | bytes 262144 | tf_op jit(solution)/shard_map/pallas_call | solution.py:334
  26.0 3.5 %all-to-all-start.1 = ((f32[16,8,128]{2,1,0:T(8,128)}), f32[16,8,128]{2,1,0:T(8,128)S(1)}, u32[]{:S(2)}, u32[]{:S(2)}) async-start(f32[16,8,128]{2,1,0:T(8,128)} %get-tuple-element.16), calls=%async_computation.1 | async-start | bytes 131072 | tf_op jit(solution)/shard_map/all_to_all | solution.py:268
  29.5 4.1 %shard_map.48.pairs = bf16[512,256]{1,0:T(8,128)(2,1)} custom-call(s32[8,128]{1,0:T(8,128)} %bitcast.5, s32[64,128]{1,0:T(8,128)} %get-tuple-element.19.mask_ids), custom_call_target="tpu_custom_call" | custom-call | flops 1073741824 | bytes 262144 | tf_op jit(solution)/shard_map/pallas_call | solution.py:325
  33.6 2.8 %all-to-all-done.1.received = f32[16,8,128]{2,1,0:T(8,128)S(1)} async-done(((f32[16,8,128]{2,1,0:T(8,128)}), f32[16,8,128]{2,1,0:T(8,128)S(1)}, u32[]{:S(2)}, u32[]{:S(2)}) %all-to-all-start.1) | async-done | bytes 65568 | tf_op jit(solution)/shard_map/all_to_all | solution.py:268
  36.4 0.0 copy-start.1
  36.4 0.6 copy-done.1
  37.0 3.6 %shard_map.49 = (f32[16,8,128]{2,1,0:T(8,128)}, f32[256,128]{1,0:T(8,128)}) custom-call(f32[16,8,128]{2,1,0:T(8,128)} %copy-done.1, f32[256,128]{1,0:T(8,128)} %get-tuple-element.17.own, f32[256,128]{1,0:T(8,128)} %get-tuple-element.18.own_count, bf16[512,256]{1,0:T(8,128)(2,1)} %shard_map.48.pairs), custom_call_target="tpu_custom_call" | custom-call | flops 33554432 | bytes 262144 | tf_op jit(solution)/shard_map/pallas_call | solution.py:344
  40.6 11.1 %all_to_all.21.received = f32[16,8,128]{2,1,0:T(8,128)} all-to-all(f32[16,8,128]{2,1,0:T(8,128)} %get-tuple-element.20), channel_id=1, replica_groups=mesh['grp'=2,'rows'=16] {'rows'}, dimensions={0} | all-to-all | bytes 131072 | tf_op jit(solution)/shard_map/all_to_all | solution.py:268
  51.7 2.8 %shard_map.50 = f32[16,8,128]{2,1,0:T(8,128)} custom-call(f32[16,8,128]{2,1,0:T(8,128)} %all_to_all.21.received, bf16[256,256]{1,0:T(8,128)(2,1)} %get-tuple-element.21.table, f32[256,128]{1,0:T(8,128)} %get-tuple-element.22.scale), custom_call_target="tpu_custom_call" | custom-call | flops 33554432 | bytes 262144 | tf_op jit(solution)/shard_map/pallas_call | solution.py:363
  54.4 3.5 %all-to-all-start.3 = ((f32[16,8,128]{2,1,0:T(8,128)}), f32[16,8,128]{2,1,0:T(8,128)S(1)}, u32[]{:S(2)}, u32[]{:S(2)}) async-start(f32[16,8,128]{2,1,0:T(8,128)} %shard_map.50), calls=%async_computation.3 | async-start | bytes 131072 | tf_op jit(solution)/shard_map/all_to_all | solution.py:268
  58.0 5.7 %shard_map.51.before = f32[64,8192]{1,0:T(8,128)} custom-call(f32[64,8192]{1,0:T(8,128)} %probes.1, f32[256,128]{1,0:T(8,128)} %get-tuple-element.23.mean, s32[64,128]{1,0:T(8,128)} %get-tuple-element.19.mask_ids, f32[64,128]{1,0:T(8,128)} %get-tuple-element.24.weight), custom_call_target="tpu_custom_call" | custom-call | flops 1073741824 | bytes 4194304 | tf_op jit(solution)/shard_map/pallas_call | solution.py:354
  63.6 1.2 %all-to-all-done.3.received = f32[16,8,128]{2,1,0:T(8,128)S(1)} async-done(((f32[16,8,128]{2,1,0:T(8,128)}), f32[16,8,128]{2,1,0:T(8,128)S(1)}, u32[]{:S(2)}, u32[]{:S(2)}) %all-to-all-start.3) | async-done | bytes 65568 | tf_op jit(solution)/shard_map/all_to_all | solution.py:268
  64.8 0.0 copy-start
  64.8 0.6 copy-done
  65.4 5.1 %shard_map.52 = f32[64,8192]{1,0:T(8,128)} custom-call(f32[16,8,128]{2,1,0:T(8,128)} %copy-done, f32[64,8192]{1,0:T(8,128)} %shard_map.51.before, s32[64,128]{1,0:T(8,128)} %get-tuple-element.19.mask_ids), custom_call_target="tpu_custom_call" | custom-call | flops 536870912 | bytes 4194304 | tf_op jit(solution)/shard_map/pallas_call | solution.py:373
Async XLA Ops:
  26.0 10.4 %all-to-all-start.1 = ((f32[16,8,128]{2,1,0:T(8,128)}), f32[16,8,128]{2,1,0:T(8,128)S(1)}, u32[]{:S(2)}, u32[]{:S(2)}) async-start(f32[16,8,128]{2,1,0:T(8,128)} %get-tuple-element.16), calls=%async_computation.1 | async-start | bytes 131072 | tf_op jit(solution)/shard_map/all_to_all | solution.py:268
  36.4 0.6 copy-start.1
  54.4 10.4 %all-to-all-start.3 = ((f32[16,8,128]{2,1,0:T(8,128)}), f32[16,8,128]{2,1,0:T(8,128)S(1)}, u32[]{:S(2)}, u32[]{:S(2)}) async-start(f32[16,8,128]{2,1,0:T(8,128)} %shard_map.50), calls=%async_computation.3 | async-start | bytes 131072 | tf_op jit(solution)/shard_map/all_to_all | solution.py:268
  64.8 0.6 copy-start

commit v4 on v3

--- a/solution.py
+++ b/solution.py
@@ -10,7 +10,8 @@
 FIRMS_PER_SHARD = 1024
 LANES = 128
 BLOCK = 1024
-VMEM_BYTES = 60 * 1024 * 1024
+VMEM_BYTES = 40 * 1024 * 1024
+NEAR = 4
 F32, BF16 = jnp.float32, jnp.bfloat16
 NT = (((1,), (1,)), ((), ()))
 NN = (((1,), (0,)), ((), ()))
@@ -100,12 +101,6 @@
         copy.wait()
 
 
-def move(source, target, sem):
-    copy = pltpu.make_async_copy(source, target, sem)
-    copy.start()
-    copy.wait()
-
-
 def column_copies(source, target, sems):
     width = source.shape[1]
     cuts = [pl.ds(start, BLOCK) for start in range(0, width, BLOCK)]
@@ -114,7 +109,7 @@
 
 def sums_kernel(n, pad, *refs):
     probes, lengths_in, ids_in, firms_in, send, own, own_count, mask_ids, weight = refs[:9]
-    valid, x, acc, lengths, ids, firms, buffer, sems, small, sem = refs[9:]
+    valid, x, acc, lengths, ids, firms, sems, small = refs[9:]
     copies = column_copies(probes, x, sems)
     first = [
         pltpu.make_async_copy(source, target, small.at[k])
@@ -157,11 +152,16 @@
     own[...] = both
     count = jnp.broadcast_to(acc[:, LANES : LANES + 1], (slots, LANES))
     own_count[...] = count
-    buffer[:, :8] = to_tiles(both, n)
-    about = jnp.where(left_of((slots, LANES)), column(firms[...].astype(F32)), count).reshape(n, 2, 8, LANES)
-    even = iota((n, 8, LANES), 2) // (LANES // 4) % 2 == 0
-    buffer[:, 8:] = jnp.where(even, about[:, 0], about[:, 1])
-    move(buffer, send, sem)
+    far = n // NEAR
+    send[:, : 8 * NEAR] = to_tiles(both, n).reshape(far, 8 * NEAR, LANES)
+    about = jnp.where(iota((slots, LANES), 1) % 16 < 8, column(firms[...].astype(F32)), count)
+    about = about.reshape(far, NEAR, 2, 8, LANES)
+    eighth = iota((far, 8, LANES), 2) // 8
+    packed = about[:, 0, 0]
+    for owner in range(NEAR):
+        for side in range(2):
+            packed = jnp.where(eighth // 2 == 2 * owner + side, about[:, owner, side], packed)
+    send[:, 8 * NEAR :] = packed
 
 
 def worker_kernel(pad, lengths, mask_ids, out):
@@ -181,49 +181,58 @@
     out[slots:] = lo
 
 
-def owner_means(tiles, table, scale):
-    n = tiles.shape[0]
-    left, right = apart(tiles.reshape(8 * n, LANES))
-    data = jnp.concatenate([halves(left), halves(right)], axis=0).astype(BF16)
-    total = fold(dot(table, data)) * scale
-    return jnp.where(left_of((8 * n, LANES)), total[: 8 * n], total[8 * n :]).reshape(n, 8, LANES)
-
-
-def owner_first_kernel(received, send, table, scale, buffer, back, in_sem, sem):
-    n = buffer.shape[0]
-    move(received, buffer, in_sem)
-    about = buffer[:, 8:].reshape(8 * n, LANES)
-    quarter = LANES // 4
-
-    def both(at):
-        return jnp.concatenate(
-            [jnp.broadcast_to(about[:, k : k + 1], (8 * n, LANES)) for k in (at, at + quarter)], axis=0
-        )
-
-    keys, counts = both(0), both(2 * quarter)
-    same = keys[:, :1] == along(keys)
-    table[...] = same.astype(F32).astype(BF16)
-    count = jnp.sum(jnp.where(same, along(counts), 0.0), axis=1, keepdims=True)
-    scale[...] = jnp.broadcast_to(1.0 / jnp.maximum(count, 1.0), scale.shape)
-    back[...] = owner_means(buffer[:, :8], table[...], scale[...])
-    move(back, send, sem)
-
-
-def owner_second_kernel(received, table, scale, send, buffer, back, in_sem, sem):
-    move(received, buffer, in_sem)
-    back[...] = owner_means(buffer[...], table[...], scale[...])
-    move(back, send, sem)
-
-
-def change_kernel(received, own, own_count, pairs, send, mean, buffer, back, in_sem, sem):
-    move(received, buffer, in_sem)
+def owner_means(parts, table, scale):
+    rows = 8 * NEAR * parts[0].shape[0]
+    data = [apart(part.reshape(rows, LANES)) for part in parts]
+    data = [halves(side) for sides in data for side in sides]
+    total = fold(dot(table, jnp.concatenate(data, axis=0).astype(BF16))) * scale
+    return jnp.where(left_of((rows, LANES)), total[:rows], total[rows:]).reshape(parts[0].shape)
+
+
+def owner_first_kernel(*refs):
+    parts, (send, table, scale) = refs[:NEAR], refs[NEAR:]
+    far = send.shape[0]
+
+    def sides(part, kind):
+        about = part[:, 8 * NEAR :].reshape(8 * far, LANES)
+        found = []
+        for side in range(2):
+            one = [
+                jnp.broadcast_to(about[:, at : at + 1], (8 * far, LANES)).reshape(far, 1, 8, LANES)
+                for at in (16 * (2 * owner + side) + 8 * kind for owner in range(NEAR))
+            ]
+            found.append(jnp.concatenate(one, axis=1).reshape(8 * NEAR * far, LANES))
+        return found
+
+    keys = [sides(part, 0) for part in parts]
+    counts = [along(side) for part in parts for side in sides(part, 1)]
+    rows = 8 * NEAR * far
+    owner = iota((rows, LANES), 0) // 8 % NEAR * FIRMS_PER_SHARD
+    keys = [[side + owner.astype(F32) for side in part] for part in keys]
+    mine = jnp.concatenate(keys[0], axis=0)
+    same = [mine[:, :1] == along(side) for part in keys for side in part]
+    total = jnp.zeros((2 * rows, rows), F32)
+    for k, (hit, count) in enumerate(zip(same, counts)):
+        table[:, k * rows : (k + 1) * rows] = hit.astype(F32).astype(BF16)
+        total += jnp.where(hit, count, 0.0)
+    total = jnp.sum(total, axis=1, keepdims=True)
+    scale[...] = jnp.broadcast_to(1.0 / jnp.maximum(total, 1.0), scale.shape)
+    send[...] = owner_means([part[:, : 8 * NEAR] for part in parts], table[...], scale[...])
+
+
+def owner_second_kernel(*refs):
+    parts, (table, scale, send) = refs[:NEAR], refs[NEAR:]
+    send[...] = owner_means([part[...] for part in parts], table[...], scale[...])
+
+
+def change_kernel(received, own, own_count, pairs, send, mean):
     slots = own.shape[0]
-    found = from_tiles(buffer[...])
+    n = slots // 16
+    found = from_tiles(received[...].reshape(n, 8, LANES))
     mean[...] = found
     change = dot(pairs[...], halves(found).astype(BF16))
     new = own[...] - own_count[...] * found + fold(change[:slots] + change[slots:])
-    back[...] = to_tiles(new, buffer.shape[0])
-    move(back, send, sem)
+    send[...] = to_tiles(new, n).reshape(send.shape)
 
 
 def take(parts, ids, slots):
@@ -248,13 +257,10 @@
     wait_all(outs)
 
 
-def last_kernel(received, before, mask_ids, out, buffer, x, y, tile_sem, in_sems, out_sems):
+def last_kernel(received, before, mask_ids, out, x, y, in_sems, out_sems):
     ins, outs = column_copies(before, x, in_sems), column_copies(y, out, out_sems)
-    copy = pltpu.make_async_copy(received, buffer, tile_sem)
-    copy.start()
     start_all(ins)
-    copy.wait()
-    mean = from_tiles(buffer[...])
+    mean = from_tiles(received[...].reshape(-1, 8, LANES))
     parts = halves(mean).T.astype(BF16)
     for b in range(len(ins)):
         spread = take(parts, row(mask_ids, b, BLOCK), mean.shape[0])
@@ -264,8 +270,13 @@
     wait_all(outs)
 
 
-def exchange(tiles):
-    return lax.all_to_all(tiles, "rows", split_axis=0, concat_axis=0, tiled=True)
+def exchange(tiles, n):
+    groups = [list(range(k, n, NEAR)) for k in range(NEAR)]
+    return lax.all_to_all(tiles, "rows", split_axis=0, concat_axis=0, axis_index_groups=groups, tiled=True)
+
+
+def share(part, n):
+    return [part] + [lax.ppermute(part, "rows", [(i, i ^ k) for i in range(n)]) for k in range(1, NEAR)]
 
 
 def call(kernel, out_shape, in_specs, out_specs, scratch, flops, moved):
@@ -287,7 +298,7 @@
     slots = slot_to_firm.shape[0]
     firm_tiles = slots // LANES
     blocks = rows_dev // BLOCK
-    vmem, anywhere = pl.BlockSpec(memory_space=pltpu.VMEM), pl.BlockSpec(memory_space=pl.ANY)
+    vmem, hbm = pl.BlockSpec(memory_space=pltpu.VMEM), pl.BlockSpec(memory_space=pltpu.HBM)
     lengths = worker_len.reshape(workers // LANES, LANES)
     ids = spell_to_slot.reshape(rows_dev // LANES, LANES)
     firms = slot_to_firm.reshape(firm_tiles, LANES)
@@ -295,17 +306,17 @@
     of_rows = (rows_dev // LANES, LANES)
     work = 2 * rows_dev * slots * 2 * columns
     sems = pltpu.SemaphoreType.DMA((blocks,))
-    sem = pltpu.SemaphoreType.DMA
     whole = pltpu.VMEM((columns, rows_dev), F32)
     of_slots = array((slots, LANES), F32)
-    all_tiles, all_talls = array((n, 8, LANES), F32), array((n, 16, LANES), F32)
-    tiles, talls = pltpu.VMEM((n, 8, LANES), F32), pltpu.VMEM((n, 16, LANES), F32)
+    far = n // NEAR
+    tiles, tiles_about = array((far, 8 * NEAR, LANES), F32), array((far, 8 * NEAR + 8, LANES), F32)
+    mine = 16 * NEAR * far
 
     send, own, own_count, mask_ids, weight = call(
         functools.partial(sums_kernel, n, pad),
-        [all_talls, of_slots, of_slots, array(of_rows, jnp.int32), array(of_rows, F32)],
-        [anywhere] * 4,
-        [anywhere] + [vmem] * 4,
+        [tiles_about, of_slots, of_slots, array(of_rows, jnp.int32), array(of_rows, F32)],
+        [hbm] * 4,
+        [vmem] * 5,
         [
             pltpu.VMEM(of_rows, F32),
             whole,
@@ -313,15 +324,13 @@
             pltpu.VMEM(lengths.shape, jnp.int32),
             pltpu.VMEM(ids.shape, jnp.int32),
             pltpu.VMEM(firms.shape, jnp.int32),
-            talls,
             sems,
             pltpu.SemaphoreType.DMA((3,)),
-            sem,
         ],
         2 * work,
         4 * columns * rows_dev,
     )(probes, lengths, ids, firms)
-    received = exchange(send)
+    received = share(exchange(send, n), n)
     pairs = call(
         functools.partial(worker_kernel, pad),
         array((2 * slots, slots), BF16),
@@ -333,49 +342,49 @@
     )(lengths, mask_ids)
     send, table, scale = call(
         owner_first_kernel,
-        [all_tiles, array((slots, slots), BF16), of_slots],
-        [anywhere],
-        [anywhere] + [vmem] * 2,
-        [talls, tiles, sem, sem],
+        [tiles, array((mine, NEAR * mine), BF16), array((mine, LANES), F32)],
+        [vmem] * NEAR,
+        [vmem] * 3,
+        [],
         work // 16,
         slots * slots * 4,
-    )(received)
-    received = exchange(send)
+    )(*received)
+    received = exchange(send, n)
     send, mean = call(
         change_kernel,
-        [all_tiles, of_slots],
-        [anywhere] + [vmem] * 3,
-        [anywhere, vmem],
-        [tiles, tiles, sem, sem],
+        [tiles, of_slots],
+        [vmem] * 4,
+        [vmem] * 2,
+        [],
         work // 16,
         slots * slots * 4,
     )(received, own, own_count, pairs)
-    received = exchange(send)
+    received = share(exchange(send, n), n)
     before = call(
         functools.partial(first_kernel, pad),
         array((columns, rows_dev), F32),
-        [anywhere, vmem, vmem, vmem],
-        anywhere,
+        [hbm, vmem, vmem, vmem],
+        hbm,
         [whole, whole, sems, sems],
         2 * work,
         8 * columns * rows_dev,
     )(probes, mean, mask_ids, weight)
     send = call(
         owner_second_kernel,
-        all_tiles,
-        [anywhere] + [vmem] * 2,
-        anywhere,
-        [tiles, tiles, sem, sem],
+        tiles,
+        [vmem] * (NEAR + 2),
+        vmem,
+        [],
         work // 16,
         slots * slots * 4,
-    )(received, table, scale)
-    received = exchange(send)
+    )(*received, table, scale)
+    received = exchange(send, n)
     return call(
         last_kernel,
         array((columns, rows_dev), F32),
-        [anywhere, anywhere, vmem],
-        anywhere,
-        [tiles, whole, whole, sem, sems, sems],
+        [vmem, hbm, vmem],
+        hbm,
+        [whole, whole, sems, sems],
         work,
         8 * columns * rows_dev,
     )(received, before, mask_ids)

time: 71.3 us -> 65.7 us (0.921)
  Pallas kernels: 31.7 us -> 18.6 us
  waiting for transfers between devices: 3.99 us -> 10.8 us
  blocking collectives: 26.5 us -> 20 us
  local copies, waits for them, and re-layouts: 1.25 us -> 5.3 us
  starting transfers between devices: 7.01 us -> 10.3 us
    pallas_call x5, Pallas kernels: 22 us -> 11.7 us  [the longest x1 5.31 us: body(): call(functools.partial(sums_kernel, n, pad), [tiles_about, of_slots, of_s...]
    ppermute x0 -> x6, waiting for transfers between devices: none -> 7.72 us  [share(): lax.ppermute(part, 'rows', [(i, i ^ k) for i in range(n)])]
    all_to_all x2, blocking collectives: 26.5 us -> 20 us  [exchange(): lax.all_to_all(tiles, 'rows', split_axis=0, concat_axis=0, axis_index_gro...]
    unnamed x4 -> x12, local copies, waits for them, and re-layouts: 1.25 us -> 5.3 us
    ppermute x0 -> x6, starting transfers between devices: none -> 3.72 us  [share(): lax.ppermute(part, 'rows', [(i, i ^ k) for i in range(n)])]
    pallas_call x1, Pallas kernels: 4.06 us -> 2.57 us  [body(): call(functools.partial(worker_kernel, pad), array((2 * slots, slots), BF1...]
    pallas_call x1, Pallas kernels: 5.65 us -> 4.31 us  [body(): call(functools.partial(first_kernel, pad), array((columns, rows_dev), F32...]
    all_to_all x2, waiting for transfers between devices: 3.99 us -> 3.12 us  [exchange(): lax.all_to_all(tiles, 'rows', split_axis=0, concat_axis=0, axis_index_gro...]
  transfers between devices with their start and end apart: 2 -> 8, of which waited for: 2 -> 5; matrix products, arithmetic and copies ran while one was open for 0% -> 0% of each run, Pallas kernels for 14% -> 11%
where the time goes in v4:
time: 65.7 us; the launch traced here: 65.1 us
  blocking collectives  20 us (30%)
  Pallas kernels  18.6 us (28%)
  waiting for transfers between devices  10.8 us (16%)
  starting transfers between devices  10.3 us (16%)
  local copies, waits for them, and re-layouts  5.3 us (8%)
    all_to_all x2, blocking collectives, exchange(): lax.all_to_all(tiles, 'rows', split_axis=0, concat_axis=0, axis_index_gro...  20 us
    ppermute x6, waiting for transfers between devices, share(): lax.ppermute(part, 'rows', [(i, i ^ k) for i in range(n)])  7.72 us
    all_to_all x2, starting transfers between devices, exchange(): lax.all_to_all(tiles, 'rows', split_axis=0, concat_axis=0, axis_index_gro...  6.57 us
    pallas_call x1, Pallas kernels, body(): call(functools.partial(sums_kernel, n, pad), [tiles_about, of_slots, of_s...  5.31 us
    unnamed x12, local copies, waits for them, and re-layouts  5.3 us
    pallas_call x1, Pallas kernels, body(): call(functools.partial(first_kernel, pad), array((columns, rows_dev), F32...  4.31 us
    ppermute x6, starting transfers between devices, share(): lax.ppermute(part, 'rows', [(i, i ^ k) for i in range(n)])  3.72 us
    all_to_all x2, waiting for transfers between devices, exchange(): lax.all_to_all(tiles, 'rows', split_axis=0, concat_axis=0, axis_index_gro...  3.12 us
  transfers between devices with their start and end apart: 8, of which 5 were waited for; matrix products, arithmetic and copies ran while one was open for 0% of the time, Pallas kernels for 11%

profile of v4, /device:TPU:0, one launch (start us, length us, event | category | flops | bytes accessed | tf_op | source)
XLA Modules:
  0.0 65.1 jit_solution(10001833225415242758)
XLA Ops:
  0.0 0.0 copy-start
  0.0 1.6 %copy-done = f32[64,8192]{1,0:T(8,128)S(1)} copy-done((f32[64,8192]{1,0:T(8,128)S(1)}, f32[64,8192]{1,0:T(8,128)}, u32[]{:S(2)}) %copy-start) | copy-done | bytes 2097176
  1.6 0.0 copy-start.2
  1.6 0.8 %copy-done.2 = s32[8192]{0:T(1024)S(1)} copy-done((s32[8192]{0:T(1024)S(1)}, s32[8192]{0:T(1024)}, u32[]{:S(2)}) %copy-start.2) | copy-done | bytes 32792
  2.4 0.0 copy-start.3
  2.4 0.7 %copy-done.3 = s32[1024]{0:T(1024)S(1)} copy-done((s32[1024]{0:T(1024)S(1)}, s32[1024]{0:T(1024)}, u32[]{:S(2)}) %copy-start.3) | copy-done | bytes 4120
  3.0 0.0 copy-start.5
  3.0 0.7 %copy-done.5 = s32[256]{0:T(256)S(1)} copy-done((s32[256]{0:T(256)S(1)}, s32[256]{0:T(256)}, u32[]{:S(2)}) %copy-start.5) | copy-done | bytes 1048
  3.7 0.0 copy-start.4
  3.7 5.3 %shard_map.46 = (f32[4,40,128]{2,1,0:T(8,128)S(1)}, f32[256,128]{1,0:T(8,128)S(1)}, f32[256,128]{1,0:T(8,128)S(1)}, s32[64,128]{1,0:T(8,128)S(1)}, f32[64,128]{1,0:T(8,128)S(1)}) custom-call(f32[64,8192]{1,0:T(8,128)S(1)} %copy-done, s32[8,128]{1,0:T(8,128)S(1)} %bitcast.4, s32[64,128]{1,0:T(8,128)S(1)} %bitcast.3, s32[2,128]{1,0:T(2,128)S(1)} %bitcast.6), custom_call_target="tpu_custom_call" | custom-call | flops 1073741824 | bytes 2097152 | tf_op jit(solution)/shard_map/pallas_call | solution.py:315
  9.0 11.9 %all_to_all.20.refs_0_ = f32[4,40,128]{2,1,0:T(8,128)S(1)} all-to-all(f32[4,40,128]{2,1,0:T(8,128)S(1)} %get-tuple-element.15), channel_id=1, replica_groups={{0,4,8,12},{1,5,9,13},{2,6,10,14},{3,7,11,15},{16,20,24,28},{17,21,25,2..., dimensions={0} | all-to-all | bytes 163840 | tf_op jit(solution)/shard_map/all_to_all | solution.py:275
  21.0 0.0 collective-permute-start.2
  21.0 1.5 %collective-permute-start.1 = (f32[4,40,128]{2,1,0:T(8,128)S(1)}, f32[4,40,128]{2,1,0:T(8,128)S(1)}, u32[]{:S(2)}, u32[]{:S(2)}) collective-permute-start(f32[4,40,128]{2,1,0:T(8,128)S(1)} %all_to_all.20.refs_0_), channel_id=1, source_target_pairs={{0,2},{1,3},{2,0},{3,1},{4,6},{5,7},{6,4},{7,5},{8,10},{9,11},{10,... | collective-permute-start | bytes 245768 | tf_op jit(solution)/shard_map/ppermute | solution.py:279
  22.5 0.3 collective-permute-start
  22.8 2.8 %collective-permute-done.2.refs_3_ = f32[4,40,128]{2,1,0:T(8,128)S(1)} collective-permute-done((f32[4,40,128]{2,1,0:T(8,128)S(1)}, f32[4,40,128]{2,1,0:T(8,128)S(1)}, u32[]{:S(2)}, u32[]{:S(2)}) %collective-permute-start.2) | collective-permute-done | bytes 81952 | tf_op jit(solution)/shard_map/ppermute | solution.py:279
  25.6 1.8 %collective-permute-done.1.refs_2_ = f32[4,40,128]{2,1,0:T(8,128)S(1)} collective-permute-done((f32[4,40,128]{2,1,0:T(8,128)S(1)}, f32[4,40,128]{2,1,0:T(8,128)S(1)}, u32[]{:S(2)}, u32[]{:S(2)}) %collective-permute-start.1) | collective-permute-done | bytes 81952 | tf_op jit(solution)/shard_map/ppermute | solution.py:279
  27.5 0.0 collective-permute-done.refs_1_
  27.5 1.9 %shard_map.47 = (f32[4,32,128]{2,1,0:T(8,128)}, bf16[256,1024]{1,0:T(8,128)(2,1)S(1)}, f32[256,128]{1,0:T(8,128)S(1)}) custom-call(f32[4,40,128]{2,1,0:T(8,128)S(1)} %all_to_all.20.refs_0_, f32[4,40,128]{2,1,0:T(8,128)S(1)} %collective-permute-done.refs_1_, f32[4,40,128]{2,1,0:T(8,128)S(1)} %collective-permute-done.1.refs_2_, ...), custom_call_target="tpu_custom_call" | custom-call | flops 33554432 | bytes 262144 | tf_op jit(solution)/shard_map/pallas_call | solution.py:343
  29.3 3.3 %all-to-all-start.1 = ((f32[4,32,128]{2,1,0:T(8,128)}), f32[4,32,128]{2,1,0:T(8,128)S(1)}, u32[]{:S(2)}, u32[]{:S(2)}) async-start(f32[4,32,128]{2,1,0:T(8,128)} %get-tuple-element.16), calls=%async_computation.1 | async-start | bytes 131072 | tf_op jit(solution)/shard_map/all_to_all | solution.py:275
  32.6 0.0 copy-done.4
  32.6 2.6 %shard_map.48.pairs = bf16[512,256]{1,0:T(8,128)(2,1)S(1)} custom-call(s32[8,128]{1,0:T(8,128)S(1)} %bitcast.5, s32[64,128]{1,0:T(8,128)S(1)} %get-tuple-element.19.mask_ids), custom_call_target="tpu_custom_call" | custom-call | flops 1073741824 | bytes 262144 | tf_op jit(solution)/shard_map/pallas_call | solution.py:334
  35.2 3.1 %all-to-all-done.1.received = f32[4,32,128]{2,1,0:T(8,128)S(1)} async-done(((f32[4,32,128]{2,1,0:T(8,128)}), f32[4,32,128]{2,1,0:T(8,128)S(1)}, u32[]{:S(2)}, u32[]{:S(2)}) %all-to-all-start.1) | async-done | bytes 65568 | tf_op jit(solution)/shard_map/all_to_all | solution.py:275
  38.3 0.4 shard_map.49
  38.7 8.1 %all_to_all.21.refs_0_ = f32[4,32,128]{2,1,0:T(8,128)S(1)} all-to-all(f32[4,32,128]{2,1,0:T(8,128)S(1)} %get-tuple-element.20), channel_id=1, replica_groups={{0,4,8,12},{1,5,9,13},{2,6,10,14},{3,7,11,15},{16,20,24,28},{17,21,25,2..., dimensions={0} | all-to-all | bytes 131072 | tf_op jit(solution)/shard_map/all_to_all | solution.py:275
  46.8 0.0 collective-permute-start.5
  46.8 0.3 collective-permute-start.4
  47.1 1.5 %collective-permute-start.3 = (f32[4,32,128]{2,1,0:T(8,128)S(1)}, f32[4,32,128]{2,1,0:T(8,128)S(1)}, u32[]{:S(2)}, u32[]{:S(2)}) collective-permute-start(f32[4,32,128]{2,1,0:T(8,128)S(1)} %all_to_all.21.refs_0_), channel_id=1, source_target_pairs={{0,1},{1,0},{2,3},{3,2},{4,5},{5,4},{6,7},{7,6},{8,9},{9,8},{10,11... | collective-permute-start | bytes 196616 | tf_op jit(solution)/shard_map/ppermute | solution.py:279
  48.7 2.0 %collective-permute-done.5.refs_3_ = f32[4,32,128]{2,1,0:T(8,128)S(1)} collective-permute-done((f32[4,32,128]{2,1,0:T(8,128)S(1)}, f32[4,32,128]{2,1,0:T(8,128)S(1)}, u32[]{:S(2)}, u32[]{:S(2)}) %collective-permute-start.5) | collective-permute-done | bytes 65568 | tf_op jit(solution)/shard_map/ppermute | solution.py:279
  50.6 1.1 %collective-permute-done.4.refs_2_ = f32[4,32,128]{2,1,0:T(8,128)S(1)} collective-permute-done((f32[4,32,128]{2,1,0:T(8,128)S(1)}, f32[4,32,128]{2,1,0:T(8,128)S(1)}, u32[]{:S(2)}, u32[]{:S(2)}) %collective-permute-start.4) | collective-permute-done | bytes 65568 | tf_op jit(solution)/shard_map/ppermute | solution.py:279
  51.7 0.0 collective-permute-done.3.refs_1_
  51.7 1.1 %shard_map.50 = f32[4,32,128]{2,1,0:T(8,128)} custom-call(f32[4,32,128]{2,1,0:T(8,128)S(1)} %all_to_all.21.refs_0_, f32[4,32,128]{2,1,0:T(8,128)S(1)} %collective-permute-done.3.refs_1_, f32[4,32,128]{2,1,0:T(8,128)S(1)} %collective-permute-done.4.refs_2_, f32[4,32,128]{2,1,0:T(8,128)S(1)} %collective-permute-done.5.refs_3_, ...), custom_call_target="tpu_custom_call" | custom-call | flops 33554432 | bytes 262144 | tf_op jit(solution)/shard_map/pallas_call | solution.py:372
  52.8 3.3 %all-to-all-start.3 = ((f32[4,32,128]{2,1,0:T(8,128)}), f32[4,32,128]{2,1,0:T(8,128)S(1)}, u32[]{:S(2)}, u32[]{:S(2)}) async-start(f32[4,32,128]{2,1,0:T(8,128)} %shard_map.50), calls=%async_computation.3 | async-start | bytes 131072 | tf_op jit(solution)/shard_map/all_to_all | solution.py:275
  56.1 0.0 copy-start.1
  56.1 1.6 %copy-done.1 = f32[64,8192]{1,0:T(8,128)S(1)} copy-done((f32[64,8192]{1,0:T(8,128)S(1)}, f32[64,8192]{1,0:T(8,128)}, u32[]{:S(2)}) %copy-start.1) | copy-done | bytes 2097176
  57.7 4.3 %shard_map.51.before = f32[64,8192]{1,0:T(8,128)S(1)} custom-call(f32[64,8192]{1,0:T(8,128)S(1)} %copy-done.1, f32[256,128]{1,0:T(8,128)S(1)} %get-tuple-element.23.mean, s32[64,128]{1,0:T(8,128)S(1)} %get-tuple-element.19.mask_ids, f32[64,128]{1,0:T(8,128)S(1)} %get-tuple-element.24.weight), custom_call_target="tpu_custom_call" | custom-call | flops 1073741824 | bytes 4194304 | tf_op jit(solution)/shard_map/pallas_call | solution.py:363
  62.0 0.0 all-to-all-done.3.received
  62.0 3.1 %shard_map.52 = f32[64,8192]{1,0:T(8,128)} custom-call(f32[4,32,128]{2,1,0:T(8,128)S(1)} %all-to-all-done.3.received, f32[64,8192]{1,0:T(8,128)S(1)} %shard_map.51.before, s32[64,128]{1,0:T(8,128)S(1)} %get-tuple-element.19.mask_ids), custom_call_target="tpu_custom_call" | custom-call | flops 536870912 | bytes 4194304 | tf_op jit(solution)/shard_map/pallas_call | solution.py:382
Async XLA Ops:
  0.0 1.6 %copy-start = (f32[64,8192]{1,0:T(8,128)S(1)}, f32[64,8192]{1,0:T(8,128)}, u32[]{:S(2)}) copy-start(f32[64,8192]{1,0:T(8,128)} %probes.1) | copy-start | bytes 6291460
  1.6 0.8 %copy-start.2 = (s32[8192]{0:T(1024)S(1)}, s32[8192]{0:T(1024)}, u32[]{:S(2)}) copy-start(s32[8192]{0:T(1024)} %param.6) | copy-start | bytes 98308
  2.4 0.7 %copy-start.3 = (s32[1024]{0:T(1024)S(1)}, s32[1024]{0:T(1024)}, u32[]{:S(2)}) copy-start(s32[1024]{0:T(1024)} %param.5) | copy-start | bytes 12292
  3.0 0.7 %copy-start.5 = (s32[256]{0:T(256)S(1)}, s32[256]{0:T(256)}, u32[]{:S(2)}) copy-start(s32[256]{0:T(256)} %param.7) | copy-start | bytes 3076
  3.7 28.9 %copy-start.4 = (s32[1024]{0:T(1024)S(1)}, s32[1024]{0:T(1024)}, u32[]{:S(2)}) copy-start(s32[1024]{0:T(1024)} %param.5) | copy-start | bytes 12292
  21.0 4.7 %collective-permute-start.2 = (f32[4,40,128]{2,1,0:T(8,128)S(1)}, f32[4,40,128]{2,1,0:T(8,128)S(1)}, u32[]{:S(2)}, u32[]{:S(2)}) collective-permute-start(f32[4,40,128]{2,1,0:T(8,128)S(1)} %all_to_all.20.refs_0_), channel_id=1, source_target_pairs={{0,3},{1,2},{2,1},{3,0},{4,7},{5,6},{6,5},{7,4},{8,11},{9,10},{10,... | collective-permute-start | bytes 245768 | tf_op jit(solution)/shard_map/ppermute | solution.py:279
  21.0 6.5 %collective-permute-start.1 = (f32[4,40,128]{2,1,0:T(8,128)S(1)}, f32[4,40,128]{2,1,0:T(8,128)S(1)}, u32[]{:S(2)}, u32[]{:S(2)}) collective-permute-start(f32[4,40,128]{2,1,0:T(8,128)S(1)} %all_to_all.20.refs_0_), channel_id=1, source_target_pairs={{0,2},{1,3},{2,0},{3,1},{4,6},{5,7},{6,4},{7,5},{8,10},{9,11},{10,... | collective-permute-start | bytes 245768 | tf_op jit(solution)/shard_map/ppermute | solution.py:279
  22.5 5.0 %collective-permute-start = (f32[4,40,128]{2,1,0:T(8,128)S(1)}, f32[4,40,128]{2,1,0:T(8,128)S(1)}, u32[]{:S(2)}, u32[]{:S(2)}) collective-permute-start(f32[4,40,128]{2,1,0:T(8,128)S(1)} %all_to_all.20.refs_0_), channel_id=1, source_target_pairs={{0,1},{1,0},{2,3},{3,2},{4,5},{5,4},{6,7},{7,6},{8,9},{9,8},{10,11... | collective-permute-start | bytes 245768 | tf_op jit(solution)/shard_map/ppermute | solution.py:279
  29.3 9.0 %all-to-all-start.1 = ((f32[4,32,128]{2,1,0:T(8,128)}), f32[4,32,128]{2,1,0:T(8,128)S(1)}, u32[]{:S(2)}, u32[]{:S(2)}) async-start(f32[4,32,128]{2,1,0:T(8,128)} %get-tuple-element.16), calls=%async_computation.1 | async-start | bytes 131072 | tf_op jit(solution)/shard_map/all_to_all | solution.py:275
  46.8 3.8 %collective-permute-start.5 = (f32[4,32,128]{2,1,0:T(8,128)S(1)}, f32[4,32,128]{2,1,0:T(8,128)S(1)}, u32[]{:S(2)}, u32[]{:S(2)}) collective-permute-start(f32[4,32,128]{2,1,0:T(8,128)S(1)} %all_to_all.21.refs_0_), channel_id=1, source_target_pairs={{0,3},{1,2},{2,1},{3,0},{4,7},{5,6},{6,5},{7,4},{8,11},{9,10},{10,... | collective-permute-start | bytes 196616 | tf_op jit(solution)/shard_map/ppermute | solution.py:279
  46.8 4.9 %collective-permute-start.4 = (f32[4,32,128]{2,1,0:T(8,128)S(1)}, f32[4,32,128]{2,1,0:T(8,128)S(1)}, u32[]{:S(2)}, u32[]{:S(2)}) collective-permute-start(f32[4,32,128]{2,1,0:T(8,128)S(1)} %all_to_all.21.refs_0_), channel_id=1, source_target_pairs={{0,2},{1,3},{2,0},{3,1},{4,6},{5,7},{6,4},{7,5},{8,10},{9,11},{10,... | collective-permute-start | bytes 196616 | tf_op jit(solution)/shard_map/ppermute | solution.py:279
  47.1 4.6 %collective-permute-start.3 = (f32[4,32,128]{2,1,0:T(8,128)S(1)}, f32[4,32,128]{2,1,0:T(8,128)S(1)}, u32[]{:S(2)}, u32[]{:S(2)}) collective-permute-start(f32[4,32,128]{2,1,0:T(8,128)S(1)} %all_to_all.21.refs_0_), channel_id=1, source_target_pairs={{0,1},{1,0},{2,3},{3,2},{4,5},{5,4},{6,7},{7,6},{8,9},{9,8},{10,11... | collective-permute-start | bytes 196616 | tf_op jit(solution)/shard_map/ppermute | solution.py:279
  52.8 9.2 %all-to-all-start.3 = ((f32[4,32,128]{2,1,0:T(8,128)}), f32[4,32,128]{2,1,0:T(8,128)S(1)}, u32[]{:S(2)}, u32[]{:S(2)}) async-start(f32[4,32,128]{2,1,0:T(8,128)} %shard_map.50), calls=%async_computation.3 | async-start | bytes 131072 | tf_op jit(solution)/shard_map/all_to_all | solution.py:275
  56.1 1.6 %copy-start.1 = (f32[64,8192]{1,0:T(8,128)S(1)}, f32[64,8192]{1,0:T(8,128)}, u32[]{:S(2)}) copy-start(f32[64,8192]{1,0:T(8,128)} %probes.1) | copy-start | bytes 6291460

commit v5 on v4

--- a/solution.py
+++ b/solution.py
@@ -101,6 +101,12 @@
         copy.wait()
 
 
+def place(tiles, sends):
+    me = lax.axis_index("rows") // NEAR
+    for k, send in enumerate(sends):
+        send[...] = tiles[me ^ k]
+
+
 def column_copies(source, target, sems):
     width = source.shape[1]
     cuts = [pl.ds(start, BLOCK) for start in range(0, width, BLOCK)]
@@ -108,8 +114,9 @@
 
 
 def sums_kernel(n, pad, *refs):
-    probes, lengths_in, ids_in, firms_in, send, own, own_count, mask_ids, weight = refs[:9]
-    valid, x, acc, lengths, ids, firms, sems, small = refs[9:]
+    far = n // NEAR
+    (probes, lengths_in, ids_in, firms_in), sends = refs[:4], refs[4 : 4 + far]
+    own, own_count, mask_ids, weight, valid, x, acc, lengths, ids, firms, tiles, sems, small = refs[4 + far :]
     copies = column_copies(probes, x, sems)
     first = [
         pltpu.make_async_copy(source, target, small.at[k])
@@ -152,8 +159,7 @@
     own[...] = both
     count = jnp.broadcast_to(acc[:, LANES : LANES + 1], (slots, LANES))
     own_count[...] = count
-    far = n // NEAR
-    send[:, : 8 * NEAR] = to_tiles(both, n).reshape(far, 8 * NEAR, LANES)
+    tiles[:, : 8 * NEAR] = to_tiles(both, n).reshape(far, 8 * NEAR, LANES)
     about = jnp.where(iota((slots, LANES), 1) % 16 < 8, column(firms[...].astype(F32)), count)
     about = about.reshape(far, NEAR, 2, 8, LANES)
     eighth = iota((far, 8, LANES), 2) // 8
@@ -161,7 +167,13 @@
     for owner in range(NEAR):
         for side in range(2):
             packed = jnp.where(eighth // 2 == 2 * owner + side, about[:, owner, side], packed)
-    send[:, 8 * NEAR :] = packed
+    tiles[:, 8 * NEAR :] = packed
+    place(tiles, sends)
+
+
+def join_kernel(*refs):
+    for k, part in enumerate(refs[:-1]):
+        refs[-1][k] = part[...]
 
 
 def worker_kernel(pad, lengths, mask_ids, out):
@@ -190,8 +202,8 @@
 
 
 def owner_first_kernel(*refs):
-    parts, (send, table, scale) = refs[:NEAR], refs[NEAR:]
-    far = send.shape[0]
+    parts, sends, (table, scale) = refs[:NEAR], refs[NEAR:-2], refs[-2:]
+    far = len(sends)
 
     def sides(part, kind):
         about = part[:, 8 * NEAR :].reshape(8 * far, LANES)
@@ -217,22 +229,36 @@
         total += jnp.where(hit, count, 0.0)
     total = jnp.sum(total, axis=1, keepdims=True)
     scale[...] = jnp.broadcast_to(1.0 / jnp.maximum(total, 1.0), scale.shape)
-    send[...] = owner_means([part[:, : 8 * NEAR] for part in parts], table[...], scale[...])
+    means = owner_means([part[:, : 8 * NEAR] for part in parts], table[...], scale[...])
+    for k, send in enumerate(sends):
+        send[...] = means[k]
 
 
 def owner_second_kernel(*refs):
-    parts, (table, scale, send) = refs[:NEAR], refs[NEAR:]
-    send[...] = owner_means([part[...] for part in parts], table[...], scale[...])
-
-
-def change_kernel(received, own, own_count, pairs, send, mean):
+    parts, (table, scale), sends = refs[:NEAR], refs[NEAR : NEAR + 2], refs[NEAR + 2 :]
+    means = owner_means([part[...] for part in parts], table[...], scale[...])
+    for k, send in enumerate(sends):
+        send[...] = means[k]
+
+
+def own_means(parts, tiles):
+    me = lax.axis_index("rows") // NEAR
+    for k, part in enumerate(parts):
+        tiles[me ^ k] = part[...]
+    return from_tiles(tiles[...].reshape(len(parts) * NEAR, 8, LANES))
+
+
+def change_kernel(far, *refs):
+    parts, (own, own_count, pairs), sends, (mean, tiles) = (
+        refs[:far], refs[far : far + 3], refs[far + 3 : 2 * far + 3], refs[2 * far + 3 :]
+    )
     slots = own.shape[0]
-    n = slots // 16
-    found = from_tiles(received[...].reshape(n, 8, LANES))
+    found = own_means(parts, tiles)
     mean[...] = found
     change = dot(pairs[...], halves(found).astype(BF16))
     new = own[...] - own_count[...] * found + fold(change[:slots] + change[slots:])
-    send[...] = to_tiles(new, n).reshape(send.shape)
+    tiles[...] = to_tiles(new, far * NEAR).reshape(tiles.shape)
+    place(tiles, sends)
 
 
 def take(parts, ids, slots):
@@ -241,8 +267,8 @@
     return spread[:columns] + spread[columns:]
 
 
-def first_kernel(pad, probes, mean, mask_ids, weight, out, x, y, in_sems, out_sems):
-    ins, outs = column_copies(probes, x, in_sems), column_copies(y, out, out_sems)
+def first_kernel(pad, probes, mean, mask_ids, weight, y, x, sems):
+    ins = column_copies(probes, x, sems)
     start_all(ins)
     slots = mean.shape[0]
     parts = halves(mean[...]).T.astype(BF16)
@@ -253,30 +279,31 @@
         ins[b].wait()
         rest = jnp.where(ids >= 0, x[:, b * BLOCK : (b + 1) * BLOCK] - spread, 0.0)
         y[:, b * BLOCK : (b + 1) * BLOCK] = rest - by_worker(rest, table) * row(weight, b, BLOCK)
+
+
+def last_kernel(far, *refs):
+    parts, (before, mask_ids, out, tiles, y, sems) = refs[:far], refs[far:]
+    outs = column_copies(y, out, sems)
+    mean = own_means(parts, tiles)
+    split_mean = halves(mean).T.astype(BF16)
+    for b in range(len(outs)):
+        spread = take(split_mean, row(mask_ids, b, BLOCK), mean.shape[0])
+        y[:, b * BLOCK : (b + 1) * BLOCK] = before[:, b * BLOCK : (b + 1) * BLOCK] - spread
         outs[b].start()
     wait_all(outs)
 
 
-def last_kernel(received, before, mask_ids, out, x, y, in_sems, out_sems):
-    ins, outs = column_copies(before, x, in_sems), column_copies(y, out, out_sems)
-    start_all(ins)
-    mean = from_tiles(received[...].reshape(-1, 8, LANES))
-    parts = halves(mean).T.astype(BF16)
-    for b in range(len(ins)):
-        spread = take(parts, row(mask_ids, b, BLOCK), mean.shape[0])
-        ins[b].wait()
-        y[:, b * BLOCK : (b + 1) * BLOCK] = x[:, b * BLOCK : (b + 1) * BLOCK] - spread
-        outs[b].start()
-    wait_all(outs)
-
-
-def exchange(tiles, n):
-    groups = [list(range(k, n, NEAR)) for k in range(NEAR)]
-    return lax.all_to_all(tiles, "rows", split_axis=0, concat_axis=0, axis_index_groups=groups, tiled=True)
+def exchange(parts, n):
+    steps = [[(i, i ^ (k * NEAR)) for i in range(n)] for k in range(len(parts))]
+    return [parts[0]] + [lax.ppermute(part, "rows", step) for part, step in zip(parts[1:], steps[1:])]
 
 
 def share(part, n):
     return [part] + [lax.ppermute(part, "rows", [(i, i ^ k) for i in range(n)]) for k in range(1, NEAR)]
+
+
+def in_hbm(x):
+    return pltpu.with_memory_space_constraint(x, pltpu.HBM)
 
 
 def call(kernel, out_shape, in_specs, out_specs, scratch, flops, moved):
@@ -309,14 +336,15 @@
     whole = pltpu.VMEM((columns, rows_dev), F32)
     of_slots = array((slots, LANES), F32)
     far = n // NEAR
-    tiles, tiles_about = array((far, 8 * NEAR, LANES), F32), array((far, 8 * NEAR + 8, LANES), F32)
+    tile, tile_about = array((8 * NEAR, LANES), F32), array((8 * NEAR + 8, LANES), F32)
+    tiles = pltpu.VMEM((far, 8 * NEAR, LANES), F32)
     mine = 16 * NEAR * far
 
-    send, own, own_count, mask_ids, weight = call(
+    *sends, own, own_count, mask_ids, weight = call(
         functools.partial(sums_kernel, n, pad),
-        [tiles_about, of_slots, of_slots, array(of_rows, jnp.int32), array(of_rows, F32)],
+        [tile_about] * far + [of_slots, of_slots, array(of_rows, jnp.int32), array(of_rows, F32)],
         [hbm] * 4,
-        [vmem] * 5,
+        [vmem] * (far + 4),
         [
             pltpu.VMEM(of_rows, F32),
             whole,
@@ -324,13 +352,19 @@
             pltpu.VMEM(lengths.shape, jnp.int32),
             pltpu.VMEM(ids.shape, jnp.int32),
             pltpu.VMEM(firms.shape, jnp.int32),
+            pltpu.VMEM((far, 8 * NEAR + 8, LANES), F32),
             sems,
             pltpu.SemaphoreType.DMA((3,)),
         ],
         2 * work,
         4 * columns * rows_dev,
-    )(probes, lengths, ids, firms)
-    received = share(exchange(send, n), n)
+    )(in_hbm(probes), in_hbm(lengths), in_hbm(ids), in_hbm(firms))
+
+    def join(parts):
+        shape = array((far, *parts[0].shape), F32)
+        return call(join_kernel, shape, [vmem] * far, vmem, [], 0, shape.size * 8)(*parts)
+
+    received = share(join(exchange(sends, n)), n)
     pairs = call(
         functools.partial(worker_kernel, pad),
         array((2 * slots, slots), BF16),
@@ -340,54 +374,54 @@
         2 * work,
         4 * slots * slots,
     )(lengths, mask_ids)
-    send, table, scale = call(
+    *sends, table, scale = call(
         owner_first_kernel,
-        [tiles, array((mine, NEAR * mine), BF16), array((mine, LANES), F32)],
+        [tile] * far + [array((mine, NEAR * mine), BF16), array((mine, LANES), F32)],
         [vmem] * NEAR,
-        [vmem] * 3,
+        [vmem] * (far + 2),
         [],
         work // 16,
         slots * slots * 4,
     )(*received)
-    received = exchange(send, n)
-    send, mean = call(
-        change_kernel,
-        [tiles, of_slots],
-        [vmem] * 4,
-        [vmem] * 2,
-        [],
+    received = exchange(sends, n)
+    *sends, mean = call(
+        functools.partial(change_kernel, far),
+        [tile] * far + [of_slots],
+        [vmem] * (far + 3),
+        [vmem] * (far + 1),
+        [tiles],
         work // 16,
         slots * slots * 4,
-    )(received, own, own_count, pairs)
-    received = share(exchange(send, n), n)
+    )(*received, own, own_count, pairs)
+    received = share(join(exchange(sends, n)), n)
     before = call(
         functools.partial(first_kernel, pad),
         array((columns, rows_dev), F32),
         [hbm, vmem, vmem, vmem],
-        hbm,
-        [whole, whole, sems, sems],
+        vmem,
+        [whole, sems],
         2 * work,
         8 * columns * rows_dev,
-    )(probes, mean, mask_ids, weight)
-    send = call(
+    )(in_hbm(probes), mean, mask_ids, weight)
+    sends = call(
         owner_second_kernel,
-        tiles,
+        [tile] * far,
         [vmem] * (NEAR + 2),
-        vmem,
+        [vmem] * far,
         [],
         work // 16,
         slots * slots * 4,
     )(*received, table, scale)
-    received = exchange(send, n)
+    received = exchange(sends, n)
     return call(
-        last_kernel,
+        functools.partial(last_kernel, far),
         array((columns, rows_dev), F32),
-        [vmem, hbm, vmem],
+        [vmem] * (far + 2),
         hbm,
-        [whole, whole, sems, sems],
+        [tiles, whole, sems],
         work,
         8 * columns * rows_dev,
-    )(received, before, mask_ids)
+    )(*received, before, mask_ids)
 
 
 def solution(mesh):

time: 65.7 us -> 58.2 us (0.89)
  blocking collectives: 20 us -> 0 us
  starting transfers between devices: 10.3 us -> 22.7 us
  waiting for transfers between devices: 10.8 us -> 18 us
  local copies, waits for them, and re-layouts: 5.3 us -> 0.01 us
  Pallas kernels: 18.6 us -> 17.2 us
    all_to_all x2 -> x0, blocking collectives: 20 us -> none  [exchange(): lax.all_to_all(tiles, 'rows', split_axis=0, concat_axis=0, axis_index_gro...]
    ppermute x0 -> x12, starting transfers between devices: none -> 19 us  [exchange(): lax.ppermute(part, 'rows', step)]
    ppermute x0 -> x12, waiting for transfers between devices: none -> 10.2 us  [exchange(): lax.ppermute(part, 'rows', step)]
    all_to_all x2 -> x0, starting transfers between devices: 6.57 us -> none  [exchange(): lax.all_to_all(tiles, 'rows', split_axis=0, concat_axis=0, axis_index_gro...]
    unnamed x12 -> x2, local copies, waits for them, and re-layouts: 5.3 us -> 0.01 us
    all_to_all x2 -> x0, waiting for transfers between devices: 3.12 us -> none  [exchange(): lax.all_to_all(tiles, 'rows', split_axis=0, concat_axis=0, axis_index_gro...]
    pallas_call x5 -> x7, Pallas kernels: 11.7 us -> 10.6 us  [the longest x1 6.44 us: body(): call(functools.partial(sums_kernel, n, pad), [tile_about] * far + [of_slo...]
  transfers between devices with their start and end apart: 8 -> 18, of which waited for: 5 -> 8; matrix products, arithmetic and copies ran while one was open for 0% -> 0% of each run, Pallas kernels for 11% -> 11%
where the time goes in v5:
time: 58.2 us; the launch traced here: 58 us
  starting transfers between devices  22.7 us (39%)
  waiting for transfers between devices  18 us (31%)
  Pallas kernels  17.2 us (30%)
    ppermute x12, starting transfers between devices, exchange(): lax.ppermute(part, 'rows', step)  19 us
    ppermute x12, waiting for transfers between devices, exchange(): lax.ppermute(part, 'rows', step)  10.2 us
    ppermute x6, waiting for transfers between devices, share(): lax.ppermute(part, 'rows', [(i, i ^ k) for i in range(n)])  7.77 us
    pallas_call x1, Pallas kernels, body(): call(functools.partial(sums_kernel, n, pad), [tile_about] * far + [of_slo...  6.44 us
    pallas_call x1, Pallas kernels, body(): call(functools.partial(first_kernel, pad), array((columns, rows_dev), F32...  3.95 us
    ppermute x6, starting transfers between devices, share(): lax.ppermute(part, 'rows', [(i, i ^ k) for i in range(n)])  3.71 us
    pallas_call x1, Pallas kernels, body(): call(functools.partial(worker_kernel, pad), array((2 * slots, slots), BF1...  2.57 us
    pallas_call x1, Pallas kernels, body(): call(functools.partial(last_kernel, far), array((columns, rows_dev), F32)...  2.1 us
  transfers between devices with their start and end apart: 18, of which 8 were waited for; matrix products, arithmetic and copies ran while one was open for 0% of the time, Pallas kernels for 11%

profile of v5, /device:TPU:0, one launch (start us, length us, event | category | flops | bytes accessed | tf_op | source)
XLA Modules:
  0.0 58.0 jit_solution(8986123414006895009)
XLA Ops:
  0.0 0.0 copy-start
  0.0 6.4 %shard_map.46 = (f32[40,128]{1,0:T(8,128)S(1)}, f32[40,128]{1,0:T(8,128)S(1)}, f32[40,128]{1,0:T(8,128)S(1)}, f32[40,128]{1,0:T(8,128)S(1)}, f32[256,128]{1,0:T(...) custom-call(f32[64,8192]{1,0:T(8,128)} %probes.1, s32[8,128]{1,0:T(8,128)} %bitcast.3, ...), custom_call_target="tpu_custom_call" | custom-call | flops 1073741824 | bytes 2097152 | tf_op jit(solution)/shard_map/pallas_call | solution.py:343
  6.4 3.1 %collective-permute-start = (f32[40,128]{1,0:T(8,128)S(1)}, f32[40,128]{1,0:T(8,128)S(1)}, u32[]{:S(2)}, u32[]{:S(2)}) collective-permute-start(f32[40,128]{1,0:T(8,128)S(1)} %get-tuple-element.29), channel_id=1, source_target_pairs={{0,4},{1,5},{2,6},{3,7},{4,0},{5,1},{6,2},{7,3},{8,12},{9,13},{10,... | collective-permute-start | bytes 61448 | tf_op jit(solution)/shard_map/ppermute | solution.py:298
  9.5 2.6 %collective-permute-start.1 = (f32[40,128]{1,0:T(8,128)S(1)}, f32[40,128]{1,0:T(8,128)S(1)}, u32[]{:S(2)}, u32[]{:S(2)}) collective-permute-start(f32[40,128]{1,0:T(8,128)S(1)} %get-tuple-element.30), channel_id=1, source_target_pairs={{0,8},{1,9},{2,10},{3,11},{4,12},{5,13},{6,14},{7,15},{8,0},{9,1},... | collective-permute-start | bytes 61448 | tf_op jit(solution)/shard_map/ppermute | solution.py:298
  12.1 0.0 collective-permute-start.2
  12.1 0.0 collective-permute-done.refs_1_
  12.1 2.3 %collective-permute-done.1.refs_2_ = f32[40,128]{1,0:T(8,128)S(1)} collective-permute-done((f32[40,128]{1,0:T(8,128)S(1)}, f32[40,128]{1,0:T(8,128)S(1)}, u32[]{:S(2)}, u32[]{:S(2)}) %collective-permute-start.1) | collective-permute-done | bytes 20512 | tf_op jit(solution)/shard_map/ppermute | solution.py:298
  14.4 3.3 %collective-permute-done.2.refs_3_ = f32[40,128]{1,0:T(8,128)S(1)} collective-permute-done((f32[40,128]{1,0:T(8,128)S(1)}, f32[40,128]{1,0:T(8,128)S(1)}, u32[]{:S(2)}, u32[]{:S(2)}) %collective-permute-start.2) | collective-permute-done | bytes 20512 | tf_op jit(solution)/shard_map/ppermute | solution.py:298
  17.7 0.0 collective-permute-start.5
  17.7 1.6 %collective-permute-start.4 = (f32[4,40,128]{2,1,0:T(8,128)S(1)}, f32[4,40,128]{2,1,0:T(8,128)S(1)}, u32[]{:S(2)}, u32[]{:S(2)}) collective-permute-start(f32[4,40,128]{2,1,0:T(8,128)S(1)} %shard_map.47.refs_0_), channel_id=1, source_target_pairs={{0,2},{1,3},{2,0},{3,1},{4,6},{5,7},{6,4},{7,5},{8,10},{9,11},{10,... | collective-permute-start | bytes 245768 | tf_op jit(solution)/shard_map/ppermute | solution.py:302
  19.3 0.3 collective-permute-start.3
  19.6 2.8 %collective-permute-done.5.refs_3_ = f32[4,40,128]{2,1,0:T(8,128)S(1)} collective-permute-done((f32[4,40,128]{2,1,0:T(8,128)S(1)}, f32[4,40,128]{2,1,0:T(8,128)S(1)}, u32[]{:S(2)}, u32[]{:S(2)}) %collective-permute-start.5) | collective-permute-done | bytes 81952 | tf_op jit(solution)/shard_map/ppermute | solution.py:302
  22.4 1.8 %collective-permute-done.4.refs_2_ = f32[4,40,128]{2,1,0:T(8,128)S(1)} collective-permute-done((f32[4,40,128]{2,1,0:T(8,128)S(1)}, f32[4,40,128]{2,1,0:T(8,128)S(1)}, u32[]{:S(2)}, u32[]{:S(2)}) %collective-permute-start.4) | collective-permute-done | bytes 81952 | tf_op jit(solution)/shard_map/ppermute | solution.py:302
  24.2 0.0 collective-permute-done.3.refs_1_
  24.2 1.2 %shard_map.48 = (f32[32,128]{1,0:T(8,128)S(1)}, f32[32,128]{1,0:T(8,128)S(1)}, f32[32,128]{1,0:T(8,128)S(1)}, f32[32,128]{1,0:T(8,128)S(1)}, bf16[256,1024]{1,0:T(8,128)(2,1)S(1)}, /*index=5*/f32[256,128]{1,0:T(8,128)S(1)}) custom-call(f32[4,40,128]{2,1,0:T(8,128)S(1)} %shard_map.47.refs_0_, f32[4,40,128]{2,1,0:T(8,128)S(1)} %collective-permute-done.3.refs_1_, ...), custom_call_target="tpu_custom_call" | custom-call | flops 33554432 | bytes 262144 | tf_op jit(solution)/shard_map/pallas_call | solution.py:377
  25.4 0.1 collective-permute-start.6
  25.5 0.8 %collective-permute-start.7 = (f32[32,128]{1,0:T(8,128)S(1)}, f32[32,128]{1,0:T(8,128)S(1)}, u32[]{:S(2)}, u32[]{:S(2)}) collective-permute-start(f32[32,128]{1,0:T(8,128)S(1)} %get-tuple-element.34), channel_id=1, source_target_pairs={{0,8},{1,9},{2,10},{3,11},{4,12},{5,13},{6,14},{7,15},{8,0},{9,1},... | collective-permute-start | bytes 49160 | tf_op jit(solution)/shard_map/ppermute | solution.py:298
  26.3 3.6 %collective-permute-start.8 = (f32[32,128]{1,0:T(8,128)S(1)}, f32[32,128]{1,0:T(8,128)S(1)}, u32[]{:S(2)}, u32[]{:S(2)}) collective-permute-start(f32[32,128]{1,0:T(8,128)S(1)} %get-tuple-element.35), channel_id=1, source_target_pairs={{0,12},{1,13},{2,14},{3,15},{4,8},{5,9},{6,10},{7,11},{8,4},{9,5},... | collective-permute-start | bytes 49160 | tf_op jit(solution)/shard_map/ppermute | solution.py:298
  29.9 0.0 copy-done
  29.9 2.6 %shard_map.49.refs_6_ = bf16[512,256]{1,0:T(8,128)(2,1)S(1)} custom-call(s32[8,128]{1,0:T(8,128)S(1)} %bitcast.4, s32[64,128]{1,0:T(8,128)S(1)} %get-tuple-element.38.mask_ids.refs_5_), custom_call_target="tpu_custom_call" | custom-call | flops 1073741824 | bytes 262144 | tf_op jit(solution)/shard_map/pallas_call | solution.py:368
  32.5 0.0 collective-permute-done.6.refs_1_
  32.5 0.0 collective-permute-done.7.refs_2_
  32.5 0.0 collective-permute-done.8.refs_3_
  32.5 0.4 shard_map.50
  32.9 0.1 collective-permute-start.9
  33.0 3.5 %collective-permute-start.10 = (f32[32,128]{1,0:T(8,128)S(1)}, f32[32,128]{1,0:T(8,128)S(1)}, u32[]{:S(2)}, u32[]{:S(2)}) collective-permute-start(f32[32,128]{1,0:T(8,128)S(1)} %get-tuple-element.41), channel_id=1, source_target_pairs={{0,8},{1,9},{2,10},{3,11},{4,12},{5,13},{6,14},{7,15},{8,0},{9,1},... | collective-permute-start | bytes 49160 | tf_op jit(solution)/shard_map/ppermute | solution.py:298
  36.5 0.9 %collective-permute-start.11 = (f32[32,128]{1,0:T(8,128)S(1)}, f32[32,128]{1,0:T(8,128)S(1)}, u32[]{:S(2)}, u32[]{:S(2)}) collective-permute-start(f32[32,128]{1,0:T(8,128)S(1)} %get-tuple-element.42), channel_id=1, source_target_pairs={{0,12},{1,13},{2,14},{3,15},{4,8},{5,9},{6,10},{7,11},{8,4},{9,5},... | collective-permute-start | bytes 49160 | tf_op jit(solution)/shard_map/ppermute | solution.py:298
  37.4 0.0 collective-permute-done.9.refs_1_
  37.4 0.8 %collective-permute-done.10.refs_2_ = f32[32,128]{1,0:T(8,128)S(1)} collective-permute-done((f32[32,128]{1,0:T(8,128)S(1)}, f32[32,128]{1,0:T(8,128)S(1)}, u32[]{:S(2)}, u32[]{:S(2)}) %collective-permute-start.10) | collective-permute-done | bytes 16416 | tf_op jit(solution)/shard_map/ppermute | solution.py:298
  38.2 3.8 %collective-permute-done.11.refs_3_ = f32[32,128]{1,0:T(8,128)S(1)} collective-permute-done((f32[32,128]{1,0:T(8,128)S(1)}, f32[32,128]{1,0:T(8,128)S(1)}, u32[]{:S(2)}, u32[]{:S(2)}) %collective-permute-start.11) | collective-permute-done | bytes 16416 | tf_op jit(solution)/shard_map/ppermute | solution.py:298
  42.0 0.0 collective-permute-start.14
  42.0 0.4 collective-permute-start.13
  42.4 1.4 %collective-permute-start.12 = (f32[4,32,128]{2,1,0:T(8,128)S(1)}, f32[4,32,128]{2,1,0:T(8,128)S(1)}, u32[]{:S(2)}, u32[]{:S(2)}) collective-permute-start(f32[4,32,128]{2,1,0:T(8,128)S(1)} %shard_map.51.refs_0_), channel_id=1, source_target_pairs={{0,1},{1,0},{2,3},{3,2},{4,5},{5,4},{6,7},{7,6},{8,9},{9,8},{10,11... | collective-permute-start | bytes 196616 | tf_op jit(solution)/shard_map/ppermute | solution.py:302
  43.9 1.9 %collective-permute-done.14.refs_3_ = f32[4,32,128]{2,1,0:T(8,128)S(1)} collective-permute-done((f32[4,32,128]{2,1,0:T(8,128)S(1)}, f32[4,32,128]{2,1,0:T(8,128)S(1)}, u32[]{:S(2)}, u32[]{:S(2)}) %collective-permute-start.14) | collective-permute-done | bytes 65568 | tf_op jit(solution)/shard_map/ppermute | solution.py:302
  45.8 1.2 %collective-permute-done.13.refs_2_ = f32[4,32,128]{2,1,0:T(8,128)S(1)} collective-permute-done((f32[4,32,128]{2,1,0:T(8,128)S(1)}, f32[4,32,128]{2,1,0:T(8,128)S(1)}, u32[]{:S(2)}, u32[]{:S(2)}) %collective-permute-start.13) | collective-permute-done | bytes 65568 | tf_op jit(solution)/shard_map/ppermute | solution.py:302
  47.0 0.0 collective-permute-done.12.refs_1_
  47.0 0.5 shard_map.52
  47.5 0.1 collective-permute-start.15
  47.5 1.5 %collective-permute-start.16 = (f32[32,128]{1,0:T(8,128)S(1)}, f32[32,128]{1,0:T(8,128)S(1)}, u32[]{:S(2)}, u32[]{:S(2)}) collective-permute-start(f32[32,128]{1,0:T(8,128)S(1)} %get-tuple-element.47), channel_id=1, source_target_pairs={{0,8},{1,9},{2,10},{3,11},{4,12},{5,13},{6,14},{7,15},{8,0},{9,1},... | collective-permute-start | bytes 49160 | tf_op jit(solution)/shard_map/ppermute | solution.py:298
  49.0 2.9 %collective-permute-start.17 = (f32[32,128]{1,0:T(8,128)S(1)}, f32[32,128]{1,0:T(8,128)S(1)}, u32[]{:S(2)}, u32[]{:S(2)}) collective-permute-start(f32[32,128]{1,0:T(8,128)S(1)} %get-tuple-element.48), channel_id=1, source_target_pairs={{0,12},{1,13},{2,14},{3,15},{4,8},{5,9},{6,10},{7,11},{8,4},{9,5},... | collective-permute-start | bytes 49160 | tf_op jit(solution)/shard_map/ppermute | solution.py:298
  51.9 4.0 %shard_map.53.refs_4_ = f32[64,8192]{1,0:T(8,128)S(1)} custom-call(f32[64,8192]{1,0:T(8,128)} %probes.1, f32[256,128]{1,0:T(8,128)S(1)} %get-tuple-element.49.mean, s32[64,128]{1,0:T(8,128)S(1)} %get-tuple-element.38.mask_ids.refs_5_, f32[64,128]{1,0:T(8,128)S(1)} %get-tuple-element.50.weight), custom_call_target="tpu_custom_call" | custom-call | flops 1073741824 | bytes 4194304 | tf_op jit(solution)/shard_map/pallas_call | solution.py:397
  55.9 0.0 collective-permute-done.15.refs_1_
  55.9 0.0 collective-permute-done.16.refs_2_
  55.9 0.0 collective-permute-done.17.refs_3_
  55.9 2.1 %shard_map.54 = f32[64,8192]{1,0:T(8,128)} custom-call(f32[32,128]{1,0:T(8,128)S(1)} %get-tuple-element.45.refs_0_, f32[32,128]{1,0:T(8,128)S(1)} %collective-permute-done.15.refs_1_, f32[32,128]{1,0:T(8,128)S(1)} %collective-permute-done.16.refs_2_, f32[32,128]{1,0:T(8,128)S(1)} %collective-permute-done.17.refs_3_, f32[64,8192]{1,0:T(8,128)S(1)} %shard_map.53.refs_4_, ...), custom_call_target="tpu_custom_call" | custom-call | flops 536870912 | bytes 4194304 | tf_op jit(solution)/shard_map/pallas_call | solution.py:416
  (2 shorter events, 0.0 us)
Async XLA Ops:
  0.0 29.9 %copy-start = (s32[1024]{0:T(1024)S(1)}, s32[1024]{0:T(1024)}, u32[]{:S(2)}) copy-start(s32[1024]{0:T(1024)} %param.5) | copy-start | bytes 12292
  6.4 5.7 %collective-permute-start = (f32[40,128]{1,0:T(8,128)S(1)}, f32[40,128]{1,0:T(8,128)S(1)}, u32[]{:S(2)}, u32[]{:S(2)}) collective-permute-start(f32[40,128]{1,0:T(8,128)S(1)} %get-tuple-element.29), channel_id=1, source_target_pairs={{0,4},{1,5},{2,6},{3,7},{4,0},{5,1},{6,2},{7,3},{8,12},{9,13},{10,... | collective-permute-start | bytes 61448 | tf_op jit(solution)/shard_map/ppermute | solution.py:298
  9.5 4.9 %collective-permute-start.1 = (f32[40,128]{1,0:T(8,128)S(1)}, f32[40,128]{1,0:T(8,128)S(1)}, u32[]{:S(2)}, u32[]{:S(2)}) collective-permute-start(f32[40,128]{1,0:T(8,128)S(1)} %get-tuple-element.30), channel_id=1, source_target_pairs={{0,8},{1,9},{2,10},{3,11},{4,12},{5,13},{6,14},{7,15},{8,0},{9,1},... | collective-permute-start | bytes 61448 | tf_op jit(solution)/shard_map/ppermute | solution.py:298
  12.1 5.6 %collective-permute-start.2 = (f32[40,128]{1,0:T(8,128)S(1)}, f32[40,128]{1,0:T(8,128)S(1)}, u32[]{:S(2)}, u32[]{:S(2)}) collective-permute-start(f32[40,128]{1,0:T(8,128)S(1)} %get-tuple-element.31), channel_id=1, source_target_pairs={{0,12},{1,13},{2,14},{3,15},{4,8},{5,9},{6,10},{7,11},{8,4},{9,5},... | collective-permute-start | bytes 61448 | tf_op jit(solution)/shard_map/ppermute | solution.py:298
  17.7 4.7 %collective-permute-start.5 = (f32[4,40,128]{2,1,0:T(8,128)S(1)}, f32[4,40,128]{2,1,0:T(8,128)S(1)}, u32[]{:S(2)}, u32[]{:S(2)}) collective-permute-start(f32[4,40,128]{2,1,0:T(8,128)S(1)} %shard_map.47.refs_0_), channel_id=1, source_target_pairs={{0,3},{1,2},{2,1},{3,0},{4,7},{5,6},{6,5},{7,4},{8,11},{9,10},{10,... | collective-permute-start | bytes 245768 | tf_op jit(solution)/shard_map/ppermute | solution.py:302
  17.7 6.5 %collective-permute-start.4 = (f32[4,40,128]{2,1,0:T(8,128)S(1)}, f32[4,40,128]{2,1,0:T(8,128)S(1)}, u32[]{:S(2)}, u32[]{:S(2)}) collective-permute-start(f32[4,40,128]{2,1,0:T(8,128)S(1)} %shard_map.47.refs_0_), channel_id=1, source_target_pairs={{0,2},{1,3},{2,0},{3,1},{4,6},{5,7},{6,4},{7,5},{8,10},{9,11},{10,... | collective-permute-start | bytes 245768 | tf_op jit(solution)/shard_map/ppermute | solution.py:302
  19.3 4.9 %collective-permute-start.3 = (f32[4,40,128]{2,1,0:T(8,128)S(1)}, f32[4,40,128]{2,1,0:T(8,128)S(1)}, u32[]{:S(2)}, u32[]{:S(2)}) collective-permute-start(f32[4,40,128]{2,1,0:T(8,128)S(1)} %shard_map.47.refs_0_), channel_id=1, source_target_pairs={{0,1},{1,0},{2,3},{3,2},{4,5},{5,4},{6,7},{7,6},{8,9},{9,8},{10,11... | collective-permute-start | bytes 245768 | tf_op jit(solution)/shard_map/ppermute | solution.py:302
  25.4 7.0 %collective-permute-start.6 = (f32[32,128]{1,0:T(8,128)S(1)}, f32[32,128]{1,0:T(8,128)S(1)}, u32[]{:S(2)}, u32[]{:S(2)}) collective-permute-start(f32[32,128]{1,0:T(8,128)S(1)} %get-tuple-element.33), channel_id=1, source_target_pairs={{0,4},{1,5},{2,6},{3,7},{4,0},{5,1},{6,2},{7,3},{8,12},{9,13},{10,... | collective-permute-start | bytes 49160 | tf_op jit(solution)/shard_map/ppermute | solution.py:298
  25.5 7.0 %collective-permute-start.7 = (f32[32,128]{1,0:T(8,128)S(1)}, f32[32,128]{1,0:T(8,128)S(1)}, u32[]{:S(2)}, u32[]{:S(2)}) collective-permute-start(f32[32,128]{1,0:T(8,128)S(1)} %get-tuple-element.34), channel_id=1, source_target_pairs={{0,8},{1,9},{2,10},{3,11},{4,12},{5,13},{6,14},{7,15},{8,0},{9,1},... | collective-permute-start | bytes 49160 | tf_op jit(solution)/shard_map/ppermute | solution.py:298
  26.3 6.2 %collective-permute-start.8 = (f32[32,128]{1,0:T(8,128)S(1)}, f32[32,128]{1,0:T(8,128)S(1)}, u32[]{:S(2)}, u32[]{:S(2)}) collective-permute-start(f32[32,128]{1,0:T(8,128)S(1)} %get-tuple-element.35), channel_id=1, source_target_pairs={{0,12},{1,13},{2,14},{3,15},{4,8},{5,9},{6,10},{7,11},{8,4},{9,5},... | collective-permute-start | bytes 49160 | tf_op jit(solution)/shard_map/ppermute | solution.py:298
  32.9 4.5 %collective-permute-start.9 = (f32[32,128]{1,0:T(8,128)S(1)}, f32[32,128]{1,0:T(8,128)S(1)}, u32[]{:S(2)}, u32[]{:S(2)}) collective-permute-start(f32[32,128]{1,0:T(8,128)S(1)} %get-tuple-element.40), channel_id=1, source_target_pairs={{0,4},{1,5},{2,6},{3,7},{4,0},{5,1},{6,2},{7,3},{8,12},{9,13},{10,... | collective-permute-start | bytes 49160 | tf_op jit(solution)/shard_map/ppermute | solution.py:298
  33.0 5.2 %collective-permute-start.10 = (f32[32,128]{1,0:T(8,128)S(1)}, f32[32,128]{1,0:T(8,128)S(1)}, u32[]{:S(2)}, u32[]{:S(2)}) collective-permute-start(f32[32,128]{1,0:T(8,128)S(1)} %get-tuple-element.41), channel_id=1, source_target_pairs={{0,8},{1,9},{2,10},{3,11},{4,12},{5,13},{6,14},{7,15},{8,0},{9,1},... | collective-permute-start | bytes 49160 | tf_op jit(solution)/shard_map/ppermute | solution.py:298
  36.5 5.5 %collective-permute-start.11 = (f32[32,128]{1,0:T(8,128)S(1)}, f32[32,128]{1,0:T(8,128)S(1)}, u32[]{:S(2)}, u32[]{:S(2)}) collective-permute-start(f32[32,128]{1,0:T(8,128)S(1)} %get-tuple-element.42), channel_id=1, source_target_pairs={{0,12},{1,13},{2,14},{3,15},{4,8},{5,9},{6,10},{7,11},{8,4},{9,5},... | collective-permute-start | bytes 49160 | tf_op jit(solution)/shard_map/ppermute | solution.py:298
  42.0 3.8 %collective-permute-start.14 = (f32[4,32,128]{2,1,0:T(8,128)S(1)}, f32[4,32,128]{2,1,0:T(8,128)S(1)}, u32[]{:S(2)}, u32[]{:S(2)}) collective-permute-start(f32[4,32,128]{2,1,0:T(8,128)S(1)} %shard_map.51.refs_0_), channel_id=1, source_target_pairs={{0,3},{1,2},{2,1},{3,0},{4,7},{5,6},{6,5},{7,4},{8,11},{9,10},{10,... | collective-permute-start | bytes 196616 | tf_op jit(solution)/shard_map/ppermute | solution.py:302
  42.0 5.0 %collective-permute-start.13 = (f32[4,32,128]{2,1,0:T(8,128)S(1)}, f32[4,32,128]{2,1,0:T(8,128)S(1)}, u32[]{:S(2)}, u32[]{:S(2)}) collective-permute-start(f32[4,32,128]{2,1,0:T(8,128)S(1)} %shard_map.51.refs_0_), channel_id=1, source_target_pairs={{0,2},{1,3},{2,0},{3,1},{4,6},{5,7},{6,4},{7,5},{8,10},{9,11},{10,... | collective-permute-start | bytes 196616 | tf_op jit(solution)/shard_map/ppermute | solution.py:302
  42.4 4.6 %collective-permute-start.12 = (f32[4,32,128]{2,1,0:T(8,128)S(1)}, f32[4,32,128]{2,1,0:T(8,128)S(1)}, u32[]{:S(2)}, u32[]{:S(2)}) collective-permute-start(f32[4,32,128]{2,1,0:T(8,128)S(1)} %shard_map.51.refs_0_), channel_id=1, source_target_pairs={{0,1},{1,0},{2,3},{3,2},{4,5},{5,4},{6,7},{7,6},{8,9},{9,8},{10,11... | collective-permute-start | bytes 196616 | tf_op jit(solution)/shard_map/ppermute | solution.py:302
  47.5 8.4 %collective-permute-start.15 = (f32[32,128]{1,0:T(8,128)S(1)}, f32[32,128]{1,0:T(8,128)S(1)}, u32[]{:S(2)}, u32[]{:S(2)}) collective-permute-start(f32[32,128]{1,0:T(8,128)S(1)} %get-tuple-element.46), channel_id=1, source_target_pairs={{0,4},{1,5},{2,6},{3,7},{4,0},{5,1},{6,2},{7,3},{8,12},{9,13},{10,... | collective-permute-start | bytes 49160 | tf_op jit(solution)/shard_map/ppermute | solution.py:298
  47.5 8.3 %collective-permute-start.16 = (f32[32,128]{1,0:T(8,128)S(1)}, f32[32,128]{1,0:T(8,128)S(1)}, u32[]{:S(2)}, u32[]{:S(2)}) collective-permute-start(f32[32,128]{1,0:T(8,128)S(1)} %get-tuple-element.47), channel_id=1, source_target_pairs={{0,8},{1,9},{2,10},{3,11},{4,12},{5,13},{6,14},{7,15},{8,0},{9,1},... | collective-permute-start | bytes 49160 | tf_op jit(solution)/shard_map/ppermute | solution.py:298
  49.0 6.9 %collective-permute-start.17 = (f32[32,128]{1,0:T(8,128)S(1)}, f32[32,128]{1,0:T(8,128)S(1)}, u32[]{:S(2)}, u32[]{:S(2)}) collective-permute-start(f32[32,128]{1,0:T(8,128)S(1)} %get-tuple-element.48), channel_id=1, source_target_pairs={{0,12},{1,13},{2,14},{3,15},{4,8},{5,9},{6,10},{7,11},{8,4},{9,5},... | collective-permute-start | bytes 49160 | tf_op jit(solution)/shard_map/ppermute | solution.py:298

commit v6 on v5

--- a/solution.py
+++ b/solution.py
@@ -36,7 +36,12 @@
 
 
 def one_hot(ids, slots):
-    return (iota((slots, ids.shape[1]), 0) == ids).astype(F32).astype(BF16)
+    kind = BF16 if slots <= 256 else F32
+    slot = iota((slots, LANES), 0).astype(F32).astype(kind)
+    ids = ids.astype(F32).astype(kind)
+    one, zero = jnp.ones((slots, LANES), kind), jnp.zeros((slots, LANES), kind)
+    parts = [jnp.where(slot == ids[:, k : k + LANES], one, zero) for k in range(0, ids.shape[1], LANES)]
+    return jnp.concatenate(parts, axis=1).astype(BF16)
 
 
 def same_worker(pad, width):
@@ -202,7 +207,7 @@
 
 
 def owner_first_kernel(*refs):
-    parts, sends, (table, scale) = refs[:NEAR], refs[NEAR:-2], refs[-2:]
+    parts, sends, (table, scale) = refs[:NEAR], refs[NEAR + 1 : -2], refs[-2:]
     far = len(sends)
 
     def sides(part, kind):
@@ -235,7 +240,7 @@
 
 
 def owner_second_kernel(*refs):
-    parts, (table, scale), sends = refs[:NEAR], refs[NEAR : NEAR + 2], refs[NEAR + 2 :]
+    parts, (table, scale), sends = refs[:NEAR], refs[NEAR : NEAR + 2], refs[NEAR + 3 :]
     means = owner_means([part[...] for part in parts], table[...], scale[...])
     for k, send in enumerate(sends):
         send[...] = means[k]
@@ -267,28 +272,30 @@
     return spread[:columns] + spread[columns:]
 
 
-def first_kernel(pad, probes, mean, mask_ids, weight, y, x, sems):
-    ins = column_copies(probes, x, sems)
+def first_kernel(pad, start, probes, mean, mask_ids, weight, y, x, sems):
+    ins = column_copies(probes.at[:, pl.ds(start * BLOCK, y.shape[1])], x, sems)
     start_all(ins)
     slots = mean.shape[0]
     parts = halves(mean[...]).T.astype(BF16)
     table = same_worker(pad, 256)
     for b in range(len(ins)):
-        ids = row(mask_ids, b, BLOCK)
+        ids = row(mask_ids, start + b, BLOCK)
         spread = take(parts, ids, slots)
         ins[b].wait()
         rest = jnp.where(ids >= 0, x[:, b * BLOCK : (b + 1) * BLOCK] - spread, 0.0)
-        y[:, b * BLOCK : (b + 1) * BLOCK] = rest - by_worker(rest, table) * row(weight, b, BLOCK)
+        y[:, b * BLOCK : (b + 1) * BLOCK] = rest - by_worker(rest, table) * row(weight, start + b, BLOCK)
 
 
 def last_kernel(far, *refs):
-    parts, (before, mask_ids, out, tiles, y, sems) = refs[:far], refs[far:]
+    parts, (before, after, mask_ids, out, tiles, y, sems) = refs[:far], refs[far:]
+    cut = before.shape[1] // BLOCK
     outs = column_copies(y, out, sems)
     mean = own_means(parts, tiles)
     split_mean = halves(mean).T.astype(BF16)
     for b in range(len(outs)):
         spread = take(split_mean, row(mask_ids, b, BLOCK), mean.shape[0])
-        y[:, b * BLOCK : (b + 1) * BLOCK] = before[:, b * BLOCK : (b + 1) * BLOCK] - spread
+        source, at = (before, b) if b < cut else (after, b - cut)
+        y[:, b * BLOCK : (b + 1) * BLOCK] = source[:, at * BLOCK : (at + 1) * BLOCK] - spread
         outs[b].start()
     wait_all(outs)
 
@@ -377,12 +384,12 @@
     *sends, table, scale = call(
         owner_first_kernel,
         [tile] * far + [array((mine, NEAR * mine), BF16), array((mine, LANES), F32)],
-        [vmem] * NEAR,
+        [vmem] * (NEAR + 1),
         [vmem] * (far + 2),
         [],
         work // 16,
         slots * slots * 4,
-    )(*received)
+    )(*received, pairs)
     received = exchange(sends, n)
     *sends, mean = call(
         functools.partial(change_kernel, far),
@@ -394,34 +401,39 @@
         slots * slots * 4,
     )(*received, own, own_count, pairs)
     received = share(join(exchange(sends, n)), n)
-    before = call(
-        functools.partial(first_kernel, pad),
-        array((columns, rows_dev), F32),
-        [hbm, vmem, vmem, vmem],
-        vmem,
-        [whole, sems],
-        2 * work,
-        8 * columns * rows_dev,
-    )(in_hbm(probes), mean, mask_ids, weight)
+
+    def first(start, stop):
+        width = (stop - start) * BLOCK
+        return call(
+            functools.partial(first_kernel, pad, start),
+            array((columns, width), F32),
+            [hbm, vmem, vmem, vmem],
+            vmem,
+            [pltpu.VMEM((columns, width), F32), sems],
+            2 * work * (stop - start) // blocks,
+            8 * columns * width,
+        )(in_hbm(probes), mean, mask_ids, weight)
+
+    before, after = first(0, 5 * blocks // 8), first(5 * blocks // 8, blocks)
     sends = call(
         owner_second_kernel,
         [tile] * far,
-        [vmem] * (NEAR + 2),
+        [vmem] * (NEAR + 3),
         [vmem] * far,
         [],
         work // 16,
         slots * slots * 4,
-    )(*received, table, scale)
+    )(*received, table, scale, before)
     received = exchange(sends, n)
     return call(
         functools.partial(last_kernel, far),
         array((columns, rows_dev), F32),
-        [vmem] * (far + 2),
+        [vmem] * (far + 3),
         hbm,
         [tiles, whole, sems],
         work,
         8 * columns * rows_dev,
-    )(*received, before, mask_ids)
+    )(*received, before, after, mask_ids)
 
 
 def solution(mesh):

time: 58.2 us -> 55.8 us (0.959)
  waiting for transfers between devices: 18 us -> 15.5 us
    ppermute x6, waiting for transfers between devices: 7.77 us -> 2.66 us  [share(): lax.ppermute(part, 'rows', [(i, i ^ k) for i in range(n)])]
    ppermute x12, waiting for transfers between devices: 10.2 us -> 12.8 us  [exchange(): lax.ppermute(part, 'rows', step)]
    pallas_call x2 -> x3, Pallas kernels: 4.41 us -> 4.87 us  [the longest x2 4.4 us: first(): call(functools.partial(first_kernel, pad, start), array((columns, width),...]
  transfers between devices with their start and end apart: 18 -> 18, of which waited for: 8 -> 9; matrix products, arithmetic and copies ran while one was open for 0% -> 0% of each run, Pallas kernels for 11% -> 13%
where the time goes in v6:
time: 55.8 us; the launch traced here: 55.6 us
  starting transfers between devices  22.7 us (41%)
  Pallas kernels  17.2 us (31%)
  waiting for transfers between devices  15.5 us (28%)
    ppermute x12, starting transfers between devices, exchange(): lax.ppermute(part, 'rows', step)  19 us
    ppermute x12, waiting for transfers between devices, exchange(): lax.ppermute(part, 'rows', step)  12.8 us
    pallas_call x1, Pallas kernels, body(): call(functools.partial(sums_kernel, n, pad), [tile_about] * far + [of_slo...  6.45 us
    pallas_call x2, Pallas kernels, first(): call(functools.partial(first_kernel, pad, start), array((columns, width),...  4.4 us
    ppermute x6, starting transfers between devices, share(): lax.ppermute(part, 'rows', [(i, i ^ k) for i in range(n)])  3.71 us
    ppermute x6, waiting for transfers between devices, share(): lax.ppermute(part, 'rows', [(i, i ^ k) for i in range(n)])  2.66 us
    pallas_call x1, Pallas kernels, body(): call(functools.partial(worker_kernel, pad), array((2 * slots, slots), BF1...  2.57 us
    pallas_call x1, Pallas kernels, body(): call(functools.partial(last_kernel, far), array((columns, rows_dev), F32)...  1.76 us
  transfers between devices with their start and end apart: 18, of which 9 were waited for; matrix products, arithmetic and copies ran while one was open for 0% of the time, Pallas kernels for 13%

profile of v6, /device:TPU:0, one launch (start us, length us, event | category | flops | bytes accessed | tf_op | source)
XLA Modules:
  0.0 55.6 jit_solution(1262714615928977259)
XLA Ops:
  0.0 0.0 copy-start
  0.0 6.4 %shard_map.46 = (f32[40,128]{1,0:T(8,128)S(1)}, f32[40,128]{1,0:T(8,128)S(1)}, f32[40,128]{1,0:T(8,128)S(1)}, f32[40,128]{1,0:T(8,128)S(1)}, f32[256,128]{1,0:T(...) custom-call(f32[64,8192]{1,0:T(8,128)} %probes.3, s32[8,128]{1,0:T(8,128)} %bitcast.3, ...), custom_call_target="tpu_custom_call" | custom-call | flops 1073741824 | bytes 2097152 | tf_op jit(solution)/shard_map/pallas_call | solution.py:350
  6.5 3.1 %collective-permute-start = (f32[40,128]{1,0:T(8,128)S(1)}, f32[40,128]{1,0:T(8,128)S(1)}, u32[]{:S(2)}, u32[]{:S(2)}) collective-permute-start(f32[40,128]{1,0:T(8,128)S(1)} %get-tuple-element.29), channel_id=1, source_target_pairs={{0,4},{1,5},{2,6},{3,7},{4,0},{5,1},{6,2},{7,3},{8,12},{9,13},{10,... | collective-permute-start | bytes 61448 | tf_op jit(solution)/shard_map/ppermute | solution.py:305
  9.6 2.6 %collective-permute-start.1 = (f32[40,128]{1,0:T(8,128)S(1)}, f32[40,128]{1,0:T(8,128)S(1)}, u32[]{:S(2)}, u32[]{:S(2)}) collective-permute-start(f32[40,128]{1,0:T(8,128)S(1)} %get-tuple-element.30), channel_id=1, source_target_pairs={{0,8},{1,9},{2,10},{3,11},{4,12},{5,13},{6,14},{7,15},{8,0},{9,1},... | collective-permute-start | bytes 61448 | tf_op jit(solution)/shard_map/ppermute | solution.py:305
  12.1 0.0 collective-permute-start.2
  12.1 0.0 collective-permute-done.refs_1_
  12.1 2.3 %collective-permute-done.1.refs_2_ = f32[40,128]{1,0:T(8,128)S(1)} collective-permute-done((f32[40,128]{1,0:T(8,128)S(1)}, f32[40,128]{1,0:T(8,128)S(1)}, u32[]{:S(2)}, u32[]{:S(2)}) %collective-permute-start.1) | collective-permute-done | bytes 20512 | tf_op jit(solution)/shard_map/ppermute | solution.py:305
  14.4 3.3 %collective-permute-done.2.refs_3_ = f32[40,128]{1,0:T(8,128)S(1)} collective-permute-done((f32[40,128]{1,0:T(8,128)S(1)}, f32[40,128]{1,0:T(8,128)S(1)}, u32[]{:S(2)}, u32[]{:S(2)}) %collective-permute-start.2) | collective-permute-done | bytes 20512 | tf_op jit(solution)/shard_map/ppermute | solution.py:305
  17.7 0.0 collective-permute-start.5
  17.7 1.6 %collective-permute-start.4 = (f32[4,40,128]{2,1,0:T(8,128)S(1)}, f32[4,40,128]{2,1,0:T(8,128)S(1)}, u32[]{:S(2)}, u32[]{:S(2)}) collective-permute-start(f32[4,40,128]{2,1,0:T(8,128)S(1)} %shard_map.47.refs_0_), channel_id=1, source_target_pairs={{0,2},{1,3},{2,0},{3,1},{4,6},{5,7},{6,4},{7,5},{8,10},{9,11},{10,... | collective-permute-start | bytes 245768 | tf_op jit(solution)/shard_map/ppermute | solution.py:309
  19.3 0.3 collective-permute-start.3
  19.6 0.0 copy-done
  19.6 2.6 %shard_map.48.refs_4_.refs_6_ = bf16[512,256]{1,0:T(8,128)(2,1)S(1)} custom-call(s32[8,128]{1,0:T(8,128)S(1)} %bitcast.4, s32[64,128]{1,0:T(8,128)S(1)} %get-tuple-element.32.mask_ids.refs_6_), custom_call_target="tpu_custom_call" | custom-call | flops 1073741824 | bytes 262144 | tf_op jit(solution)/shard_map/pallas_call | solution.py:375
  22.2 0.2 collective-permute-done.5.refs_3_
  22.4 1.8 %collective-permute-done.4.refs_2_ = f32[4,40,128]{2,1,0:T(8,128)S(1)} collective-permute-done((f32[4,40,128]{2,1,0:T(8,128)S(1)}, f32[4,40,128]{2,1,0:T(8,128)S(1)}, u32[]{:S(2)}, u32[]{:S(2)}) %collective-permute-start.4) | collective-permute-done | bytes 81952 | tf_op jit(solution)/shard_map/ppermute | solution.py:309
  24.2 0.0 collective-permute-done.3.refs_1_
  24.2 1.2 %shard_map.49 = (f32[32,128]{1,0:T(8,128)S(1)}, f32[32,128]{1,0:T(8,128)S(1)}, f32[32,128]{1,0:T(8,128)S(1)}, f32[32,128]{1,0:T(8,128)S(1)}, bf16[256,1024]{1,0:T(8,128)(2,1)S(1)}, /*index=5*/f32[256,128]{1,0:T(8,128)S(1)}) custom-call(f32[4,40,128]{2,1,0:T(8,128)S(1)} %shard_map.47.refs_0_, f32[4,40,128]{2,1,0:T(8,128)S(1)} %collective-permute-done.3.refs_1_, ...), custom_call_target="tpu_custom_call" | custom-call | flops 33554432 | bytes 262144 | tf_op jit(solution)/shard_map/pallas_call | solution.py:384
  25.5 0.1 collective-permute-start.6
  25.5 0.8 %collective-permute-start.7 = (f32[32,128]{1,0:T(8,128)S(1)}, f32[32,128]{1,0:T(8,128)S(1)}, u32[]{:S(2)}, u32[]{:S(2)}) collective-permute-start(f32[32,128]{1,0:T(8,128)S(1)} %get-tuple-element.35), channel_id=1, source_target_pairs={{0,8},{1,9},{2,10},{3,11},{4,12},{5,13},{6,14},{7,15},{8,0},{9,1},... | collective-permute-start | bytes 49160 | tf_op jit(solution)/shard_map/ppermute | solution.py:305
  26.3 3.6 %collective-permute-start.8 = (f32[32,128]{1,0:T(8,128)S(1)}, f32[32,128]{1,0:T(8,128)S(1)}, u32[]{:S(2)}, u32[]{:S(2)}) collective-permute-start(f32[32,128]{1,0:T(8,128)S(1)} %get-tuple-element.36), channel_id=1, source_target_pairs={{0,12},{1,13},{2,14},{3,15},{4,8},{5,9},{6,10},{7,11},{8,4},{9,5},... | collective-permute-start | bytes 49160 | tf_op jit(solution)/shard_map/ppermute | solution.py:305
  29.9 0.0 collective-permute-done.6.refs_1_
  29.9 0.3 collective-permute-done.7.refs_2_
  30.2 1.6 %collective-permute-done.8.refs_3_ = f32[32,128]{1,0:T(8,128)S(1)} collective-permute-done((f32[32,128]{1,0:T(8,128)S(1)}, f32[32,128]{1,0:T(8,128)S(1)}, u32[]{:S(2)}, u32[]{:S(2)}) %collective-permute-start.8) | collective-permute-done | bytes 16416 | tf_op jit(solution)/shard_map/ppermute | solution.py:305
  31.8 0.4 shard_map.50
  32.2 0.4 collective-permute-start.9
  32.6 3.8 %collective-permute-start.10 = (f32[32,128]{1,0:T(8,128)S(1)}, f32[32,128]{1,0:T(8,128)S(1)}, u32[]{:S(2)}, u32[]{:S(2)}) collective-permute-start(f32[32,128]{1,0:T(8,128)S(1)} %get-tuple-element.41), channel_id=1, source_target_pairs={{0,8},{1,9},{2,10},{3,11},{4,12},{5,13},{6,14},{7,15},{8,0},{9,1},... | collective-permute-start | bytes 49160 | tf_op jit(solution)/shard_map/ppermute | solution.py:305
  36.5 0.2 collective-permute-start.11
  36.7 0.0 collective-permute-done.9.refs_1_
  36.7 1.5 %collective-permute-done.10.refs_2_ = f32[32,128]{1,0:T(8,128)S(1)} collective-permute-done((f32[32,128]{1,0:T(8,128)S(1)}, f32[32,128]{1,0:T(8,128)S(1)}, u32[]{:S(2)}, u32[]{:S(2)}) %collective-permute-start.10) | collective-permute-done | bytes 16416 | tf_op jit(solution)/shard_map/ppermute | solution.py:305
  38.2 3.8 %collective-permute-done.11.refs_3_ = f32[32,128]{1,0:T(8,128)S(1)} collective-permute-done((f32[32,128]{1,0:T(8,128)S(1)}, f32[32,128]{1,0:T(8,128)S(1)}, u32[]{:S(2)}, u32[]{:S(2)}) %collective-permute-start.11) | collective-permute-done | bytes 16416 | tf_op jit(solution)/shard_map/ppermute | solution.py:305
  42.0 0.0 collective-permute-start.14
  42.0 0.4 collective-permute-start.13
  42.4 1.4 %collective-permute-start.12 = (f32[4,32,128]{2,1,0:T(8,128)S(1)}, f32[4,32,128]{2,1,0:T(8,128)S(1)}, u32[]{:S(2)}, u32[]{:S(2)}) collective-permute-start(f32[4,32,128]{2,1,0:T(8,128)S(1)} %shard_map.51.refs_0_), channel_id=1, source_target_pairs={{0,1},{1,0},{2,3},{3,2},{4,5},{5,4},{6,7},{7,6},{8,9},{9,8},{10,11... | collective-permute-start | bytes 196616 | tf_op jit(solution)/shard_map/ppermute | solution.py:309
  43.9 2.5 %shard_map.52.refs_6_.refs_4_ = f32[64,5120]{1,0:T(8,128)S(1)} custom-call(f32[64,8192]{1,0:T(8,128)} %probes.3, f32[256,128]{1,0:T(8,128)S(1)} %get-tuple-element.45.mean, s32[64,128]{1,0:T(8,128)S(1)} %get-tuple-element.32.mask_ids.refs_6_, f32[64,128]{1,0:T(8,128)S(1)} %get-tuple-element.46.weight), custom_call_target="tpu_custom_call" | custom-call | flops 671088640 | bytes 2621440 | tf_op jit(solution)/shard_map/pallas_call | solution.py:407
  46.4 0.0 collective-permute-done.14.refs_3_
  46.4 0.6 %collective-permute-done.13.refs_2_ = f32[4,32,128]{2,1,0:T(8,128)S(1)} collective-permute-done((f32[4,32,128]{2,1,0:T(8,128)S(1)}, f32[4,32,128]{2,1,0:T(8,128)S(1)}, u32[]{:S(2)}, u32[]{:S(2)}) %collective-permute-start.13) | collective-permute-done | bytes 65568 | tf_op jit(solution)/shard_map/ppermute | solution.py:309
  47.0 0.0 collective-permute-done.12.refs_1_
  47.0 0.5 shard_map.53
  47.5 0.1 collective-permute-start.15
  47.5 0.8 %collective-permute-start.16 = (f32[32,128]{1,0:T(8,128)S(1)}, f32[32,128]{1,0:T(8,128)S(1)}, u32[]{:S(2)}, u32[]{:S(2)}) collective-permute-start(f32[32,128]{1,0:T(8,128)S(1)} %get-tuple-element.49), channel_id=1, source_target_pairs={{0,8},{1,9},{2,10},{3,11},{4,12},{5,13},{6,14},{7,15},{8,0},{9,1},... | collective-permute-start | bytes 49160 | tf_op jit(solution)/shard_map/ppermute | solution.py:305
  48.3 3.6 %collective-permute-start.17 = (f32[32,128]{1,0:T(8,128)S(1)}, f32[32,128]{1,0:T(8,128)S(1)}, u32[]{:S(2)}, u32[]{:S(2)}) collective-permute-start(f32[32,128]{1,0:T(8,128)S(1)} %get-tuple-element.50), channel_id=1, source_target_pairs={{0,12},{1,13},{2,14},{3,15},{4,8},{5,9},{6,10},{7,11},{8,4},{9,5},... | collective-permute-start | bytes 49160 | tf_op jit(solution)/shard_map/ppermute | solution.py:305
  51.9 1.9 %shard_map.54.refs_5_ = f32[64,3072]{1,0:T(8,128)S(1)} custom-call(f32[64,8192]{1,0:T(8,128)} %probes.3, f32[256,128]{1,0:T(8,128)S(1)} %get-tuple-element.45.mean, s32[64,128]{1,0:T(8,128)S(1)} %get-tuple-element.32.mask_ids.refs_6_, f32[64,128]{1,0:T(8,128)S(1)} %get-tuple-element.46.weight), custom_call_target="tpu_custom_call" | custom-call | flops 402653184 | bytes 1572864 | tf_op jit(solution)/shard_map/pallas_call | solution.py:407
  53.8 0.0 collective-permute-done.15.refs_1_
  53.8 0.0 collective-permute-done.16.refs_2_
  53.8 0.0 collective-permute-done.17.refs_3_
  53.8 1.8 %shard_map.55 = f32[64,8192]{1,0:T(8,128)} custom-call(f32[32,128]{1,0:T(8,128)S(1)} %get-tuple-element.47.refs_0_, f32[32,128]{1,0:T(8,128)S(1)} %collective-permute-done.15.refs_1_, f32[32,128]{1,0:T(8,128)S(1)} %collective-permute-done.16.refs_2_, f32[32,128]{1,0:T(8,128)S(1)} %collective-permute-done.17.refs_3_, ...), custom_call_target="tpu_custom_call" | custom-call | flops 536870912 | bytes 4194304 | tf_op jit(solution)/shard_map/pallas_call | solution.py:428
  (2 shorter events, 0.0 us)
Async XLA Ops:
  0.0 19.6 %copy-start = (s32[1024]{0:T(1024)S(1)}, s32[1024]{0:T(1024)}, u32[]{:S(2)}) copy-start(s32[1024]{0:T(1024)} %param.5) | copy-start | bytes 12292
  6.5 5.7 %collective-permute-start = (f32[40,128]{1,0:T(8,128)S(1)}, f32[40,128]{1,0:T(8,128)S(1)}, u32[]{:S(2)}, u32[]{:S(2)}) collective-permute-start(f32[40,128]{1,0:T(8,128)S(1)} %get-tuple-element.29), channel_id=1, source_target_pairs={{0,4},{1,5},{2,6},{3,7},{4,0},{5,1},{6,2},{7,3},{8,12},{9,13},{10,... | collective-permute-start | bytes 61448 | tf_op jit(solution)/shard_map/ppermute | solution.py:305
  9.6 4.9 %collective-permute-start.1 = (f32[40,128]{1,0:T(8,128)S(1)}, f32[40,128]{1,0:T(8,128)S(1)}, u32[]{:S(2)}, u32[]{:S(2)}) collective-permute-start(f32[40,128]{1,0:T(8,128)S(1)} %get-tuple-element.30), channel_id=1, source_target_pairs={{0,8},{1,9},{2,10},{3,11},{4,12},{5,13},{6,14},{7,15},{8,0},{9,1},... | collective-permute-start | bytes 61448 | tf_op jit(solution)/shard_map/ppermute | solution.py:305
  12.1 5.6 %collective-permute-start.2 = (f32[40,128]{1,0:T(8,128)S(1)}, f32[40,128]{1,0:T(8,128)S(1)}, u32[]{:S(2)}, u32[]{:S(2)}) collective-permute-start(f32[40,128]{1,0:T(8,128)S(1)} %get-tuple-element.31), channel_id=1, source_target_pairs={{0,12},{1,13},{2,14},{3,15},{4,8},{5,9},{6,10},{7,11},{8,4},{9,5},... | collective-permute-start | bytes 61448 | tf_op jit(solution)/shard_map/ppermute | solution.py:305
  17.7 4.7 %collective-permute-start.5 = (f32[4,40,128]{2,1,0:T(8,128)S(1)}, f32[4,40,128]{2,1,0:T(8,128)S(1)}, u32[]{:S(2)}, u32[]{:S(2)}) collective-permute-start(f32[4,40,128]{2,1,0:T(8,128)S(1)} %shard_map.47.refs_0_), channel_id=1, source_target_pairs={{0,3},{1,2},{2,1},{3,0},{4,7},{5,6},{6,5},{7,4},{8,11},{9,10},{10,... | collective-permute-start | bytes 245768 | tf_op jit(solution)/shard_map/ppermute | solution.py:309
  17.7 6.5 %collective-permute-start.4 = (f32[4,40,128]{2,1,0:T(8,128)S(1)}, f32[4,40,128]{2,1,0:T(8,128)S(1)}, u32[]{:S(2)}, u32[]{:S(2)}) collective-permute-start(f32[4,40,128]{2,1,0:T(8,128)S(1)} %shard_map.47.refs_0_), channel_id=1, source_target_pairs={{0,2},{1,3},{2,0},{3,1},{4,6},{5,7},{6,4},{7,5},{8,10},{9,11},{10,... | collective-permute-start | bytes 245768 | tf_op jit(solution)/shard_map/ppermute | solution.py:309
  19.3 4.9 %collective-permute-start.3 = (f32[4,40,128]{2,1,0:T(8,128)S(1)}, f32[4,40,128]{2,1,0:T(8,128)S(1)}, u32[]{:S(2)}, u32[]{:S(2)}) collective-permute-start(f32[4,40,128]{2,1,0:T(8,128)S(1)} %shard_map.47.refs_0_), channel_id=1, source_target_pairs={{0,1},{1,0},{2,3},{3,2},{4,5},{5,4},{6,7},{7,6},{8,9},{9,8},{10,11... | collective-permute-start | bytes 245768 | tf_op jit(solution)/shard_map/ppermute | solution.py:309
  25.5 4.5 %collective-permute-start.6 = (f32[32,128]{1,0:T(8,128)S(1)}, f32[32,128]{1,0:T(8,128)S(1)}, u32[]{:S(2)}, u32[]{:S(2)}) collective-permute-start(f32[32,128]{1,0:T(8,128)S(1)} %get-tuple-element.34), channel_id=1, source_target_pairs={{0,4},{1,5},{2,6},{3,7},{4,0},{5,1},{6,2},{7,3},{8,12},{9,13},{10,... | collective-permute-start | bytes 49160 | tf_op jit(solution)/shard_map/ppermute | solution.py:305
  25.5 4.7 %collective-permute-start.7 = (f32[32,128]{1,0:T(8,128)S(1)}, f32[32,128]{1,0:T(8,128)S(1)}, u32[]{:S(2)}, u32[]{:S(2)}) collective-permute-start(f32[32,128]{1,0:T(8,128)S(1)} %get-tuple-element.35), channel_id=1, source_target_pairs={{0,8},{1,9},{2,10},{3,11},{4,12},{5,13},{6,14},{7,15},{8,0},{9,1},... | collective-permute-start | bytes 49160 | tf_op jit(solution)/shard_map/ppermute | solution.py:305
  26.3 5.5 %collective-permute-start.8 = (f32[32,128]{1,0:T(8,128)S(1)}, f32[32,128]{1,0:T(8,128)S(1)}, u32[]{:S(2)}, u32[]{:S(2)}) collective-permute-start(f32[32,128]{1,0:T(8,128)S(1)} %get-tuple-element.36), channel_id=1, source_target_pairs={{0,12},{1,13},{2,14},{3,15},{4,8},{5,9},{6,10},{7,11},{8,4},{9,5},... | collective-permute-start | bytes 49160 | tf_op jit(solution)/shard_map/ppermute | solution.py:305
  32.2 4.5 %collective-permute-start.9 = (f32[32,128]{1,0:T(8,128)S(1)}, f32[32,128]{1,0:T(8,128)S(1)}, u32[]{:S(2)}, u32[]{:S(2)}) collective-permute-start(f32[32,128]{1,0:T(8,128)S(1)} %get-tuple-element.40), channel_id=1, source_target_pairs={{0,4},{1,5},{2,6},{3,7},{4,0},{5,1},{6,2},{7,3},{8,12},{9,13},{10,... | collective-permute-start | bytes 49160 | tf_op jit(solution)/shard_map/ppermute | solution.py:305
  32.6 5.5 %collective-permute-start.10 = (f32[32,128]{1,0:T(8,128)S(1)}, f32[32,128]{1,0:T(8,128)S(1)}, u32[]{:S(2)}, u32[]{:S(2)}) collective-permute-start(f32[32,128]{1,0:T(8,128)S(1)} %get-tuple-element.41), channel_id=1, source_target_pairs={{0,8},{1,9},{2,10},{3,11},{4,12},{5,13},{6,14},{7,15},{8,0},{9,1},... | collective-permute-start | bytes 49160 | tf_op jit(solution)/shard_map/ppermute | solution.py:305
  36.5 5.5 %collective-permute-start.11 = (f32[32,128]{1,0:T(8,128)S(1)}, f32[32,128]{1,0:T(8,128)S(1)}, u32[]{:S(2)}, u32[]{:S(2)}) collective-permute-start(f32[32,128]{1,0:T(8,128)S(1)} %get-tuple-element.42), channel_id=1, source_target_pairs={{0,12},{1,13},{2,14},{3,15},{4,8},{5,9},{6,10},{7,11},{8,4},{9,5},... | collective-permute-start | bytes 49160 | tf_op jit(solution)/shard_map/ppermute | solution.py:305
  42.0 4.4 %collective-permute-start.14 = (f32[4,32,128]{2,1,0:T(8,128)S(1)}, f32[4,32,128]{2,1,0:T(8,128)S(1)}, u32[]{:S(2)}, u32[]{:S(2)}) collective-permute-start(f32[4,32,128]{2,1,0:T(8,128)S(1)} %shard_map.51.refs_0_), channel_id=1, source_target_pairs={{0,3},{1,2},{2,1},{3,0},{4,7},{5,6},{6,5},{7,4},{8,11},{9,10},{10,... | collective-permute-start | bytes 196616 | tf_op jit(solution)/shard_map/ppermute | solution.py:309
  42.0 5.0 %collective-permute-start.13 = (f32[4,32,128]{2,1,0:T(8,128)S(1)}, f32[4,32,128]{2,1,0:T(8,128)S(1)}, u32[]{:S(2)}, u32[]{:S(2)}) collective-permute-start(f32[4,32,128]{2,1,0:T(8,128)S(1)} %shard_map.51.refs_0_), channel_id=1, source_target_pairs={{0,2},{1,3},{2,0},{3,1},{4,6},{5,7},{6,4},{7,5},{8,10},{9,11},{10,... | collective-permute-start | bytes 196616 | tf_op jit(solution)/shard_map/ppermute | solution.py:309
  42.4 4.6 %collective-permute-start.12 = (f32[4,32,128]{2,1,0:T(8,128)S(1)}, f32[4,32,128]{2,1,0:T(8,128)S(1)}, u32[]{:S(2)}, u32[]{:S(2)}) collective-permute-start(f32[4,32,128]{2,1,0:T(8,128)S(1)} %shard_map.51.refs_0_), channel_id=1, source_target_pairs={{0,1},{1,0},{2,3},{3,2},{4,5},{5,4},{6,7},{7,6},{8,9},{9,8},{10,11... | collective-permute-start | bytes 196616 | tf_op jit(solution)/shard_map/ppermute | solution.py:309
  47.5 6.3 %collective-permute-start.15 = (f32[32,128]{1,0:T(8,128)S(1)}, f32[32,128]{1,0:T(8,128)S(1)}, u32[]{:S(2)}, u32[]{:S(2)}) collective-permute-start(f32[32,128]{1,0:T(8,128)S(1)} %get-tuple-element.48), channel_id=1, source_target_pairs={{0,4},{1,5},{2,6},{3,7},{4,0},{5,1},{6,2},{7,3},{8,12},{9,13},{10,... | collective-permute-start | bytes 49160 | tf_op jit(solution)/shard_map/ppermute | solution.py:305
  47.5 6.3 %collective-permute-start.16 = (f32[32,128]{1,0:T(8,128)S(1)}, f32[32,128]{1,0:T(8,128)S(1)}, u32[]{:S(2)}, u32[]{:S(2)}) collective-permute-start(f32[32,128]{1,0:T(8,128)S(1)} %get-tuple-element.49), channel_id=1, source_target_pairs={{0,8},{1,9},{2,10},{3,11},{4,12},{5,13},{6,14},{7,15},{8,0},{9,1},... | collective-permute-start | bytes 49160 | tf_op jit(solution)/shard_map/ppermute | solution.py:305
  48.3 5.5 %collective-permute-start.17 = (f32[32,128]{1,0:T(8,128)S(1)}, f32[32,128]{1,0:T(8,128)S(1)}, u32[]{:S(2)}, u32[]{:S(2)}) collective-permute-start(f32[32,128]{1,0:T(8,128)S(1)} %get-tuple-element.50), channel_id=1, source_target_pairs={{0,12},{1,13},{2,14},{3,15},{4,8},{5,9},{6,10},{7,11},{8,4},{9,5},... | collective-permute-start | bytes 49160 | tf_op jit(solution)/shard_map/ppermute | solution.py:305

commit v7 on v6

--- a/solution.py
+++ b/solution.py
@@ -106,10 +106,30 @@
         copy.wait()
 
 
-def place(tiles, sends):
+def senders(far):
+    left = [group for group in range(far) if group != far // 2 - 1]
+    return left, [far - 1 - group for group in left]
+
+
+def place(halves_of, sends):
+    far = len(sends)
     me = lax.axis_index("rows") // NEAR
-    for k, send in enumerate(sends):
-        send[...] = tiles[me ^ k]
+    for send, group in zip(sends, [far // 2 - 1] + senders(far)[0]):
+        send[...] = halves_of[jnp.where(me == group, 0, 1)]
+
+
+def own_means(parts, tiles):
+    far = len(parts)
+    me = lax.axis_index("rows") // NEAR
+    for k, part in enumerate(parts):
+        tiles[k] = part[...]
+    found = []
+    for steps in senders(far):
+        at = 0
+        for k, group in enumerate(steps):
+            at += jnp.where(me == group, k + 1, 0)
+        found.append(tiles[at])
+    return from_tiles(jnp.concatenate(found, axis=0).reshape(-1, 8, LANES))
 
 
 def column_copies(source, target, sems):
@@ -164,15 +184,16 @@
     own[...] = both
     count = jnp.broadcast_to(acc[:, LANES : LANES + 1], (slots, LANES))
     own_count[...] = count
-    tiles[:, : 8 * NEAR] = to_tiles(both, n).reshape(far, 8 * NEAR, LANES)
+    data = 4 * n
+    tiles[:, :data] = to_tiles(both, n).reshape(2, data, LANES)
     about = jnp.where(iota((slots, LANES), 1) % 16 < 8, column(firms[...].astype(F32)), count)
-    about = about.reshape(far, NEAR, 2, 8, LANES)
-    eighth = iota((far, 8, LANES), 2) // 8
+    about = about.reshape(n // 4, 4, 2, 8, LANES)
+    sixteenth = iota((n // 4, 8, LANES), 2) // 16
     packed = about[:, 0, 0]
-    for owner in range(NEAR):
+    for owner in range(4):
         for side in range(2):
-            packed = jnp.where(eighth // 2 == 2 * owner + side, about[:, owner, side], packed)
-    tiles[:, 8 * NEAR :] = packed
+            packed = jnp.where(sixteenth == 2 * owner + side, about[:, owner, side], packed)
+    tiles[:, data:] = packed.reshape(2, n, LANES)
     place(tiles, sends)
 
 
@@ -198,59 +219,43 @@
     out[slots:] = lo
 
 
-def owner_means(parts, table, scale):
-    rows = 8 * NEAR * parts[0].shape[0]
-    data = [apart(part.reshape(rows, LANES)) for part in parts]
-    data = [halves(side) for sides in data for side in sides]
-    total = fold(dot(table, jnp.concatenate(data, axis=0).astype(BF16))) * scale
-    return jnp.where(left_of((rows, LANES)), total[:rows], total[rows:]).reshape(parts[0].shape)
+def owner_means(parts, table, scale, sends):
+    far = len(sends)
+    rows = 8 * far
+    for owner in range(table.shape[0]):
+        at = slice(8 * owner, 8 * owner + 8)
+        block = jnp.concatenate([part[:, at].reshape(rows, LANES) for part in parts], axis=0)
+        data = jnp.concatenate([halves(side) for side in apart(block)], axis=0).astype(BF16)
+        means = fold(dot(table[owner], data)) * scale[owner]
+        means = jnp.where(left_of((rows, LANES)), means[:rows], means[rows:])
+        for k, send in enumerate(sends):
+            send[at] = means[8 * k : 8 * k + 8]
 
 
 def owner_first_kernel(*refs):
     parts, sends, (table, scale) = refs[:NEAR], refs[NEAR + 1 : -2], refs[-2:]
     far = len(sends)
-
-    def sides(part, kind):
-        about = part[:, 8 * NEAR :].reshape(8 * far, LANES)
-        found = []
-        for side in range(2):
-            one = [
-                jnp.broadcast_to(about[:, at : at + 1], (8 * far, LANES)).reshape(far, 1, 8, LANES)
-                for at in (16 * (2 * owner + side) + 8 * kind for owner in range(NEAR))
-            ]
-            found.append(jnp.concatenate(one, axis=1).reshape(8 * NEAR * far, LANES))
-        return found
-
-    keys = [sides(part, 0) for part in parts]
-    counts = [along(side) for part in parts for side in sides(part, 1)]
-    rows = 8 * NEAR * far
-    owner = iota((rows, LANES), 0) // 8 % NEAR * FIRMS_PER_SHARD
-    keys = [[side + owner.astype(F32) for side in part] for part in keys]
-    mine = jnp.concatenate(keys[0], axis=0)
-    same = [mine[:, :1] == along(side) for part in keys for side in part]
-    total = jnp.zeros((2 * rows, rows), F32)
-    for k, (hit, count) in enumerate(zip(same, counts)):
-        table[:, k * rows : (k + 1) * rows] = hit.astype(F32).astype(BF16)
-        total += jnp.where(hit, count, 0.0)
-    total = jnp.sum(total, axis=1, keepdims=True)
-    scale[...] = jnp.broadcast_to(1.0 / jnp.maximum(total, 1.0), scale.shape)
-    means = owner_means([part[:, : 8 * NEAR] for part in parts], table[...], scale[...])
-    for k, send in enumerate(sends):
-        send[...] = means[k]
+    rows = 8 * far
+    owners = table.shape[0]
+    for four in range(owners // 4):
+        start = 8 * owners + 8 * four
+        about = [part[:, start : start + 8].reshape(rows, LANES) for part in parts]
+        turned = jnp.concatenate(about, axis=0).T
+        for k in range(4):
+            at = [32 * k, 32 * k + 16]
+            mine = jnp.concatenate([jnp.broadcast_to(about[0][:, i : i + 1], (rows, LANES)) for i in at], axis=0)
+            keys = jnp.concatenate([turned[i : i + 1] for i in at], axis=1)
+            counts = jnp.concatenate([turned[i + 8 : i + 9] for i in at], axis=1)
+            same = mine[:, :1] == keys
+            total = jnp.sum(jnp.where(same, counts, 0.0), axis=1, keepdims=True)
+            table[4 * four + k] = same.astype(F32).astype(BF16)
+            scale[4 * four + k] = jnp.broadcast_to(1.0 / jnp.maximum(total, 1.0), (2 * rows, LANES))
+    owner_means(parts, table, scale, sends)
 
 
 def owner_second_kernel(*refs):
     parts, (table, scale), sends = refs[:NEAR], refs[NEAR : NEAR + 2], refs[NEAR + 3 :]
-    means = owner_means([part[...] for part in parts], table[...], scale[...])
-    for k, send in enumerate(sends):
-        send[...] = means[k]
-
-
-def own_means(parts, tiles):
-    me = lax.axis_index("rows") // NEAR
-    for k, part in enumerate(parts):
-        tiles[me ^ k] = part[...]
-    return from_tiles(tiles[...].reshape(len(parts) * NEAR, 8, LANES))
+    owner_means(parts, table, scale, sends)
 
 
 def change_kernel(far, *refs):
@@ -262,7 +267,8 @@
     mean[...] = found
     change = dot(pairs[...], halves(found).astype(BF16))
     new = own[...] - own_count[...] * found + fold(change[:slots] + change[slots:])
-    tiles[...] = to_tiles(new, far * NEAR).reshape(tiles.shape)
+    for half in range(2):
+        tiles[half] = to_tiles(new, far * NEAR).reshape(2, -1, LANES)[half]
     place(tiles, sends)
 
 
@@ -300,13 +306,32 @@
     wait_all(outs)
 
 
-def exchange(parts, n):
-    steps = [[(i, i ^ (k * NEAR)) for i in range(n)] for k in range(len(parts))]
-    return [parts[0]] + [lax.ppermute(part, "rows", step) for part, step in zip(parts[1:], steps[1:])]
+def steps_to_hubs(n):
+    far = n // NEAR
+    left, right = far // 2 - 1, far // 2
+    return [
+        [(NEAR * group + k, NEAR * hub + k) for group, hub in ((one, left), (other, right)) for k in range(NEAR)]
+        for one, other in zip(*senders(far))
+    ]
+
+
+def to_hubs(parts, n):
+    return [parts[0]] + [lax.ppermute(part, "rows", step) for part, step in zip(parts[1:], steps_to_hubs(n))]
+
+
+def from_hubs(parts, n):
+    steps = [[(hub, group) for group, hub in step] for step in steps_to_hubs(n)]
+    return [parts[0]] + [lax.ppermute(part, "rows", step) for part, step in zip(parts[1:], steps)]
 
 
 def share(part, n):
-    return [part] + [lax.ppermute(part, "rows", [(i, i ^ k) for i in range(n)]) for k in range(1, NEAR)]
+    hubs = range(n // 2 - NEAR, n // 2 + NEAR)
+
+    def swap(part, k):
+        return lax.ppermute(part, "rows", [(i, i ^ k) for i in hubs])
+
+    far_side = swap(part, 2)
+    return [part, swap(part, 1), far_side, swap(far_side, 1)]
 
 
 def in_hbm(x):
@@ -343,9 +368,9 @@
     whole = pltpu.VMEM((columns, rows_dev), F32)
     of_slots = array((slots, LANES), F32)
     far = n // NEAR
-    tile, tile_about = array((8 * NEAR, LANES), F32), array((8 * NEAR + 8, LANES), F32)
-    tiles = pltpu.VMEM((far, 8 * NEAR, LANES), F32)
-    mine = 16 * NEAR * far
+    tile, tile_about = array((4 * n, LANES), F32), array((5 * n, LANES), F32)
+    tiles = pltpu.VMEM((far, 4 * n, LANES), F32)
+    mine = 16 * far
 
     *sends, own, own_count, mask_ids, weight = call(
         functools.partial(sums_kernel, n, pad),
@@ -359,7 +384,7 @@
             pltpu.VMEM(lengths.shape, jnp.int32),
             pltpu.VMEM(ids.shape, jnp.int32),
             pltpu.VMEM(firms.shape, jnp.int32),
-            pltpu.VMEM((far, 8 * NEAR + 8, LANES), F32),
+            pltpu.VMEM((2, 5 * n, LANES), F32),
             sems,
             pltpu.SemaphoreType.DMA((3,)),
         ],
@@ -371,7 +396,7 @@
         shape = array((far, *parts[0].shape), F32)
         return call(join_kernel, shape, [vmem] * far, vmem, [], 0, shape.size * 8)(*parts)
 
-    received = share(join(exchange(sends, n)), n)
+    received = share(join(to_hubs(sends, n)), n)
     pairs = call(
         functools.partial(worker_kernel, pad),
         array((2 * slots, slots), BF16),
@@ -383,14 +408,14 @@
     )(lengths, mask_ids)
     *sends, table, scale = call(
         owner_first_kernel,
-        [tile] * far + [array((mine, NEAR * mine), BF16), array((mine, LANES), F32)],
+        [tile] * far + [array((n // 2, mine, NEAR * mine), BF16), array((n // 2, mine, LANES), F32)],
         [vmem] * (NEAR + 1),
         [vmem] * (far + 2),
         [],
         work // 16,
         slots * slots * 4,
     )(*received, pairs)
-    received = exchange(sends, n)
+    received = from_hubs(sends, n)
     *sends, mean = call(
         functools.partial(change_kernel, far),
         [tile] * far + [of_slots],
@@ -400,7 +425,7 @@
         work // 16,
         slots * slots * 4,
     )(*received, own, own_count, pairs)
-    received = share(join(exchange(sends, n)), n)
+    received = share(join(to_hubs(sends, n)), n)
 
     def first(start, stop):
         width = (stop - start) * BLOCK
@@ -424,7 +449,7 @@
         work // 16,
         slots * slots * 4,
     )(*received, table, scale, before)
-    received = exchange(sends, n)
+    received = from_hubs(sends, n)
     return call(
         functools.partial(last_kernel, far),
         array((columns, rows_dev), F32),

time: 55.8 us -> 74.8 us (1.34)
  waiting for transfers between devices: 15.5 us -> 30.4 us
  starting transfers between devices: 22.7 us -> 25.9 us
    ppermute x18, waiting for transfers between devices: 15.5 us -> 30.4 us  [the longest x6 27.2 us: from_hubs(): lax.ppermute(part, 'rows', step)]
    ppermute x18, starting transfers between devices: 22.7 us -> 25.9 us  [the longest x6 15.4 us: to_hubs(): lax.ppermute(part, 'rows', step)]
  transfers between devices with their start and end apart: 18 -> 18, of which waited for: 9 -> 6; matrix products, arithmetic and copies ran while one was open for 0% -> 0% of each run, Pallas kernels for 13% -> 9%
where the time goes in v7:
time: 74.8 us; the launch traced here: 74.2 us
  waiting for transfers between devices  30.4 us (41%)
  starting transfers between devices  25.9 us (35%)
  Pallas kernels  17.6 us (24%)
    ppermute x6, waiting for transfers between devices, from_hubs(): lax.ppermute(part, 'rows', step)  27.2 us
    ppermute x6, starting transfers between devices, to_hubs(): lax.ppermute(part, 'rows', step)  15.4 us
    ppermute x6, starting transfers between devices, from_hubs(): lax.ppermute(part, 'rows', step)  6.49 us
    pallas_call x1, Pallas kernels, body(): call(functools.partial(sums_kernel, n, pad), [tile_about] * far + [of_slo...  6.46 us
    pallas_call x2, Pallas kernels, first(): call(functools.partial(first_kernel, pad, start), array((columns, width),...  4.41 us
    ppermute x6, starting transfers between devices, swap(): return lax.ppermute(part, 'rows', [(i, i ^ k) for i in hubs])  4.02 us
    ppermute x6, waiting for transfers between devices, to_hubs(): lax.ppermute(part, 'rows', step)  3.2 us
    pallas_call x1, Pallas kernels, body(): call(functools.partial(worker_kernel, pad), array((2 * slots, slots), BF1...  2.57 us
  transfers between devices with their start and end apart: 18, of which 6 were waited for; matrix products, arithmetic and copies ran while one was open for 0% of the time, Pallas kernels for 9%

profile of v7, /device:TPU:0, one launch (start us, length us, event | category | flops | bytes accessed | tf_op | source)
XLA Modules:
  0.0 74.2 jit_solution(17395694577440225172)
XLA Ops:
  0.0 0.0 copy-start
  0.0 6.5 %shard_map.46 = (f32[80,128]{1,0:T(8,128)S(1)}, f32[80,128]{1,0:T(8,128)S(1)}, f32[80,128]{1,0:T(8,128)S(1)}, f32[80,128]{1,0:T(8,128)S(1)}, f32[256,128]{1,0:T(...) custom-call(f32[64,8192]{1,0:T(8,128)} %probes.3, s32[8,128]{1,0:T(8,128)} %bitcast.3, ...), custom_call_target="tpu_custom_call" | custom-call | flops 1073741824 | bytes 2097152 | tf_op jit(solution)/shard_map/pallas_call | solution.py:375
  6.5 4.9 %collective-permute-start = (f32[80,128]{1,0:T(8,128)S(1)}, f32[80,128]{1,0:T(8,128)S(1)}, u32[]{:S(2)}, u32[]{:S(2)}) collective-permute-start(f32[80,128]{1,0:T(8,128)S(1)} %get-tuple-element.29), channel_id=1, source_target_pairs={{0,4},{1,5},{2,6},{3,7},{12,8},{13,9},{14,10},{15,11},{16,20},{17,... | collective-permute-start | bytes 122888 | tf_op jit(solution)/shard_map/ppermute | solution.py:319
  11.4 0.7 collective-permute-start.1
  12.1 4.0 %collective-permute-start.2 = (f32[80,128]{1,0:T(8,128)S(1)}, f32[80,128]{1,0:T(8,128)S(1)}, u32[]{:S(2)}, u32[]{:S(2)}) collective-permute-start(f32[80,128]{1,0:T(8,128)S(1)} %get-tuple-element.31), channel_id=1, source_target_pairs={{12,4},{13,5},{14,6},{15,7},{0,8},{1,9},{2,10},{3,11},{28,20},{29,... | collective-permute-start | bytes 122888 | tf_op jit(solution)/shard_map/ppermute | solution.py:319
  16.1 0.0 collective-permute-done.refs_1_
  16.1 0.0 collective-permute-done.1.refs_2_
  16.1 1.6 %collective-permute-done.2.refs_3_ = f32[80,128]{1,0:T(8,128)S(1)} collective-permute-done((f32[80,128]{1,0:T(8,128)S(1)}, f32[80,128]{1,0:T(8,128)S(1)}, u32[]{:S(2)}, u32[]{:S(2)}) %collective-permute-start.2) | collective-permute-done | bytes 40992 | tf_op jit(solution)/shard_map/ppermute | solution.py:319
  17.8 0.7 collective-permute-start.4
  18.4 0.7 collective-permute-start.3
  19.1 0.0 collective-permute-done.4.refs_2_
  19.1 0.7 collective-permute-start.5
  19.8 0.0 copy-done
  19.8 2.6 %shard_map.48.refs_4_.refs_6_ = bf16[512,256]{1,0:T(8,128)(2,1)S(1)} custom-call(s32[8,128]{1,0:T(8,128)S(1)} %bitcast.4, s32[64,128]{1,0:T(8,128)S(1)} %get-tuple-element.32.mask_ids.refs_6_), custom_call_target="tpu_custom_call" | custom-call | flops 1073741824 | bytes 262144 | tf_op jit(solution)/shard_map/pallas_call | solution.py:400
  22.4 0.0 collective-permute-done.3.refs_1_
  22.4 0.0 collective-permute-done.5.refs_3_
  22.4 1.5 %shard_map.49 = (f32[64,128]{1,0:T(8,128)S(1)}, f32[64,128]{1,0:T(8,128)S(1)}, f32[64,128]{1,0:T(8,128)S(1)}, f32[64,128]{1,0:T(8,128)S(1)}, bf16[8,64,256]{2,1,0:T(8,128)(2,1)S(1)}, /*index=5*/f32[8,64,128]{2,1,0:T(8,128)S(1)}) custom-call(f32[4,80,128]{2,1,0:T(8,128)S(1)} %shard_map.47.refs_0_, f32[4,80,128]{2,1,0:T(8,128)S(1)} %collective-permute-done.3.refs_1_, ...), custom_call_target="tpu_custom_call" | custom-call | flops 33554432 | bytes 262144 | tf_op jit(solution)/shard_map/pallas_call | solution.py:409
  23.9 1.3 %collective-permute-start.6 = (f32[64,128]{1,0:T(8,128)S(1)}, f32[64,128]{1,0:T(8,128)S(1)}, u32[]{:S(2)}, u32[]{:S(2)}) collective-permute-start(f32[64,128]{1,0:T(8,128)S(1)} %get-tuple-element.34), channel_id=1, source_target_pairs={{4,0},{5,1},{6,2},{7,3},{8,12},{9,13},{10,14},{11,15},{20,16},{21,... | collective-permute-start | bytes 98312 | tf_op jit(solution)/shard_map/ppermute | solution.py:324
  25.2 0.7 collective-permute-start.7
  25.9 1.3 %collective-permute-start.8 = (f32[64,128]{1,0:T(8,128)S(1)}, f32[64,128]{1,0:T(8,128)S(1)}, u32[]{:S(2)}, u32[]{:S(2)}) collective-permute-start(f32[64,128]{1,0:T(8,128)S(1)} %get-tuple-element.36), channel_id=1, source_target_pairs={{4,12},{5,13},{6,14},{7,15},{8,0},{9,1},{10,2},{11,3},{20,28},{21,... | collective-permute-start | bytes 98312 | tf_op jit(solution)/shard_map/ppermute | solution.py:324
  27.2 10.5 %collective-permute-done.6.refs_1_ = f32[64,128]{1,0:T(8,128)S(1)} collective-permute-done((f32[64,128]{1,0:T(8,128)S(1)}, f32[64,128]{1,0:T(8,128)S(1)}, u32[]{:S(2)}, u32[]{:S(2)}) %collective-permute-start.6) | collective-permute-done | bytes 32800 | tf_op jit(solution)/shard_map/ppermute | solution.py:324
  37.7 0.0 collective-permute-done.7.refs_2_
  37.7 4.5 %collective-permute-done.8.refs_3_ = f32[64,128]{1,0:T(8,128)S(1)} collective-permute-done((f32[64,128]{1,0:T(8,128)S(1)}, f32[64,128]{1,0:T(8,128)S(1)}, u32[]{:S(2)}, u32[]{:S(2)}) %collective-permute-start.8) | collective-permute-done | bytes 32800 | tf_op jit(solution)/shard_map/ppermute | solution.py:324
  42.2 0.4 shard_map.50
  42.6 1.3 %collective-permute-start.9 = (f32[64,128]{1,0:T(8,128)S(1)}, f32[64,128]{1,0:T(8,128)S(1)}, u32[]{:S(2)}, u32[]{:S(2)}) collective-permute-start(f32[64,128]{1,0:T(8,128)S(1)} %get-tuple-element.40), channel_id=1, source_target_pairs={{0,4},{1,5},{2,6},{3,7},{12,8},{13,9},{14,10},{15,11},{16,20},{17,... | collective-permute-start | bytes 98312 | tf_op jit(solution)/shard_map/ppermute | solution.py:319
  43.9 0.7 collective-permute-start.10
  44.6 3.9 %collective-permute-start.11 = (f32[64,128]{1,0:T(8,128)S(1)}, f32[64,128]{1,0:T(8,128)S(1)}, u32[]{:S(2)}, u32[]{:S(2)}) collective-permute-start(f32[64,128]{1,0:T(8,128)S(1)} %get-tuple-element.42), channel_id=1, source_target_pairs={{12,4},{13,5},{14,6},{15,7},{0,8},{1,9},{2,10},{3,11},{28,20},{29,... | collective-permute-start | bytes 98312 | tf_op jit(solution)/shard_map/ppermute | solution.py:319
  48.5 0.0 collective-permute-done.9.refs_1_
  48.5 0.0 collective-permute-done.10.refs_2_
  48.5 1.6 %collective-permute-done.11.refs_3_ = f32[64,128]{1,0:T(8,128)S(1)} collective-permute-done((f32[64,128]{1,0:T(8,128)S(1)}, f32[64,128]{1,0:T(8,128)S(1)}, u32[]{:S(2)}, u32[]{:S(2)}) %collective-permute-start.11) | collective-permute-done | bytes 32800 | tf_op jit(solution)/shard_map/ppermute | solution.py:319
  50.1 0.7 collective-permute-start.13
  50.7 0.7 collective-permute-start.12
  51.4 0.0 collective-permute-done.13.refs_2_
  51.4 0.7 collective-permute-start.14
  52.1 2.5 %shard_map.52.refs_6_.refs_4_ = f32[64,5120]{1,0:T(8,128)S(1)} custom-call(f32[64,8192]{1,0:T(8,128)} %probes.3, f32[256,128]{1,0:T(8,128)S(1)} %get-tuple-element.45.mean, s32[64,128]{1,0:T(8,128)S(1)} %get-tuple-element.32.mask_ids.refs_6_, f32[64,128]{1,0:T(8,128)S(1)} %get-tuple-element.46.weight), custom_call_target="tpu_custom_call" | custom-call | flops 671088640 | bytes 2621440 | tf_op jit(solution)/shard_map/pallas_call | solution.py:432
  54.6 0.0 collective-permute-done.12.refs_1_
  54.6 0.0 collective-permute-done.14.refs_3_
  54.6 0.5 shard_map.53
  55.1 1.3 %collective-permute-start.15 = (f32[64,128]{1,0:T(8,128)S(1)}, f32[64,128]{1,0:T(8,128)S(1)}, u32[]{:S(2)}, u32[]{:S(2)}) collective-permute-start(f32[64,128]{1,0:T(8,128)S(1)} %get-tuple-element.48), channel_id=1, source_target_pairs={{4,0},{5,1},{6,2},{7,3},{8,12},{9,13},{10,14},{11,15},{20,16},{21,... | collective-permute-start | bytes 98312 | tf_op jit(solution)/shard_map/ppermute | solution.py:324
  56.4 0.7 collective-permute-start.16
  57.1 1.3 %collective-permute-start.17 = (f32[64,128]{1,0:T(8,128)S(1)}, f32[64,128]{1,0:T(8,128)S(1)}, u32[]{:S(2)}, u32[]{:S(2)}) collective-permute-start(f32[64,128]{1,0:T(8,128)S(1)} %get-tuple-element.50), channel_id=1, source_target_pairs={{4,12},{5,13},{6,14},{7,15},{8,0},{9,1},{10,2},{11,3},{20,28},{21,... | collective-permute-start | bytes 98312 | tf_op jit(solution)/shard_map/ppermute | solution.py:324
  58.4 1.9 %shard_map.54.refs_5_ = f32[64,3072]{1,0:T(8,128)S(1)} custom-call(f32[64,8192]{1,0:T(8,128)} %probes.3, f32[256,128]{1,0:T(8,128)S(1)} %get-tuple-element.45.mean, s32[64,128]{1,0:T(8,128)S(1)} %get-tuple-element.32.mask_ids.refs_6_, f32[64,128]{1,0:T(8,128)S(1)} %get-tuple-element.46.weight), custom_call_target="tpu_custom_call" | custom-call | flops 402653184 | bytes 1572864 | tf_op jit(solution)/shard_map/pallas_call | solution.py:432
  60.3 7.7 %collective-permute-done.15.refs_1_ = f32[64,128]{1,0:T(8,128)S(1)} collective-permute-done((f32[64,128]{1,0:T(8,128)S(1)}, f32[64,128]{1,0:T(8,128)S(1)}, u32[]{:S(2)}, u32[]{:S(2)}) %collective-permute-start.15) | collective-permute-done | bytes 32800 | tf_op jit(solution)/shard_map/ppermute | solution.py:324
  68.0 0.0 collective-permute-done.16.refs_2_
  68.0 4.5 %collective-permute-done.17.refs_3_ = f32[64,128]{1,0:T(8,128)S(1)} collective-permute-done((f32[64,128]{1,0:T(8,128)S(1)}, f32[64,128]{1,0:T(8,128)S(1)}, u32[]{:S(2)}, u32[]{:S(2)}) %collective-permute-start.17) | collective-permute-done | bytes 32800 | tf_op jit(solution)/shard_map/ppermute | solution.py:324
  72.5 1.8 %shard_map.55 = f32[64,8192]{1,0:T(8,128)} custom-call(f32[64,128]{1,0:T(8,128)S(1)} %get-tuple-element.47.refs_0_, f32[64,128]{1,0:T(8,128)S(1)} %collective-permute-done.15.refs_1_, f32[64,128]{1,0:T(8,128)S(1)} %collective-permute-done.16.refs_2_, f32[64,128]{1,0:T(8,128)S(1)} %collective-permute-done.17.refs_3_, ...), custom_call_target="tpu_custom_call" | custom-call | flops 536870912 | bytes 4194304 | tf_op jit(solution)/shard_map/pallas_call | solution.py:453
  (2 shorter events, 0.0 us)
Async XLA Ops:
  0.0 19.8 %copy-start = (s32[1024]{0:T(1024)S(1)}, s32[1024]{0:T(1024)}, u32[]{:S(2)}) copy-start(s32[1024]{0:T(1024)} %param.5) | copy-start | bytes 12292
  6.5 9.6 %collective-permute-start = (f32[80,128]{1,0:T(8,128)S(1)}, f32[80,128]{1,0:T(8,128)S(1)}, u32[]{:S(2)}, u32[]{:S(2)}) collective-permute-start(f32[80,128]{1,0:T(8,128)S(1)} %get-tuple-element.29), channel_id=1, source_target_pairs={{0,4},{1,5},{2,6},{3,7},{12,8},{13,9},{14,10},{15,11},{16,20},{17,... | collective-permute-start | bytes 122888 | tf_op jit(solution)/shard_map/ppermute | solution.py:319
  11.4 4.7 %collective-permute-start.1 = (f32[80,128]{1,0:T(8,128)S(1)}, f32[80,128]{1,0:T(8,128)S(1)}, u32[]{:S(2)}, u32[]{:S(2)}) collective-permute-start(f32[80,128]{1,0:T(8,128)S(1)} %get-tuple-element.30), channel_id=1, source_target_pairs={{8,4},{9,5},{10,6},{11,7},{4,8},{5,9},{6,10},{7,11},{24,20},{25,21... | collective-permute-start | bytes 122888 | tf_op jit(solution)/shard_map/ppermute | solution.py:319
  12.1 5.7 %collective-permute-start.2 = (f32[80,128]{1,0:T(8,128)S(1)}, f32[80,128]{1,0:T(8,128)S(1)}, u32[]{:S(2)}, u32[]{:S(2)}) collective-permute-start(f32[80,128]{1,0:T(8,128)S(1)} %get-tuple-element.31), channel_id=1, source_target_pairs={{12,4},{13,5},{14,6},{15,7},{0,8},{1,9},{2,10},{3,11},{28,20},{29,... | collective-permute-start | bytes 122888 | tf_op jit(solution)/shard_map/ppermute | solution.py:319
  17.8 1.4 %collective-permute-start.4 = (f32[4,80,128]{2,1,0:T(8,128)S(1)}, f32[4,80,128]{2,1,0:T(8,128)S(1)}, u32[]{:S(2)}, u32[]{:S(2)}) collective-permute-start(f32[4,80,128]{2,1,0:T(8,128)S(1)} %shard_map.47.refs_0_), channel_id=1, source_target_pairs={{4,6},{5,7},{6,4},{7,5},{8,10},{9,11},{10,8},{11,9},{20,22},{21,23... | collective-permute-start | bytes 491528 | tf_op jit(solution)/shard_map/ppermute | solution.py:331
  18.4 4.0 %collective-permute-start.3 = (f32[4,80,128]{2,1,0:T(8,128)S(1)}, f32[4,80,128]{2,1,0:T(8,128)S(1)}, u32[]{:S(2)}, u32[]{:S(2)}) collective-permute-start(f32[4,80,128]{2,1,0:T(8,128)S(1)} %shard_map.47.refs_0_), channel_id=1, source_target_pairs={{4,5},{5,4},{6,7},{7,6},{8,9},{9,8},{10,11},{11,10},{20,21},{21,20... | collective-permute-start | bytes 491528 | tf_op jit(solution)/shard_map/ppermute | solution.py:331
  19.1 3.3 %collective-permute-start.5 = (f32[4,80,128]{2,1,0:T(8,128)S(1)}, f32[4,80,128]{2,1,0:T(8,128)S(1)}, u32[]{:S(2)}, u32[]{:S(2)}) collective-permute-start(f32[4,80,128]{2,1,0:T(8,128)S(1)} %collective-permute-done.4.refs_2_), channel_id=1, source_target_pairs={{4,5},{5,4},{6,7},{7,6},{8,9},{9,8},{10,11},{11,10},{20,21},{21,20... | collective-permute-start | bytes 491528 | tf_op jit(solution)/shard_map/ppermute | solution.py:331
  23.9 13.8 %collective-permute-start.6 = (f32[64,128]{1,0:T(8,128)S(1)}, f32[64,128]{1,0:T(8,128)S(1)}, u32[]{:S(2)}, u32[]{:S(2)}) collective-permute-start(f32[64,128]{1,0:T(8,128)S(1)} %get-tuple-element.34), channel_id=1, source_target_pairs={{4,0},{5,1},{6,2},{7,3},{8,12},{9,13},{10,14},{11,15},{20,16},{21,... | collective-permute-start | bytes 98312 | tf_op jit(solution)/shard_map/ppermute | solution.py:324
  25.2 12.5 %collective-permute-start.7 = (f32[64,128]{1,0:T(8,128)S(1)}, f32[64,128]{1,0:T(8,128)S(1)}, u32[]{:S(2)}, u32[]{:S(2)}) collective-permute-start(f32[64,128]{1,0:T(8,128)S(1)} %get-tuple-element.35), channel_id=1, source_target_pairs={{4,8},{5,9},{6,10},{7,11},{8,4},{9,5},{10,6},{11,7},{20,24},{21,25... | collective-permute-start | bytes 98312 | tf_op jit(solution)/shard_map/ppermute | solution.py:324
  25.9 16.3 %collective-permute-start.8 = (f32[64,128]{1,0:T(8,128)S(1)}, f32[64,128]{1,0:T(8,128)S(1)}, u32[]{:S(2)}, u32[]{:S(2)}) collective-permute-start(f32[64,128]{1,0:T(8,128)S(1)} %get-tuple-element.36), channel_id=1, source_target_pairs={{4,12},{5,13},{6,14},{7,15},{8,0},{9,1},{10,2},{11,3},{20,28},{21,... | collective-permute-start | bytes 98312 | tf_op jit(solution)/shard_map/ppermute | solution.py:324
  42.6 5.9 %collective-permute-start.9 = (f32[64,128]{1,0:T(8,128)S(1)}, f32[64,128]{1,0:T(8,128)S(1)}, u32[]{:S(2)}, u32[]{:S(2)}) collective-permute-start(f32[64,128]{1,0:T(8,128)S(1)} %get-tuple-element.40), channel_id=1, source_target_pairs={{0,4},{1,5},{2,6},{3,7},{12,8},{13,9},{14,10},{15,11},{16,20},{17,... | collective-permute-start | bytes 98312 | tf_op jit(solution)/shard_map/ppermute | solution.py:319
  43.9 4.6 %collective-permute-start.10 = (f32[64,128]{1,0:T(8,128)S(1)}, f32[64,128]{1,0:T(8,128)S(1)}, u32[]{:S(2)}, u32[]{:S(2)}) collective-permute-start(f32[64,128]{1,0:T(8,128)S(1)} %get-tuple-element.41), channel_id=1, source_target_pairs={{8,4},{9,5},{10,6},{11,7},{4,8},{5,9},{6,10},{7,11},{24,20},{25,21... | collective-permute-start | bytes 98312 | tf_op jit(solution)/shard_map/ppermute | solution.py:319
  44.6 5.5 %collective-permute-start.11 = (f32[64,128]{1,0:T(8,128)S(1)}, f32[64,128]{1,0:T(8,128)S(1)}, u32[]{:S(2)}, u32[]{:S(2)}) collective-permute-start(f32[64,128]{1,0:T(8,128)S(1)} %get-tuple-element.42), channel_id=1, source_target_pairs={{12,4},{13,5},{14,6},{15,7},{0,8},{1,9},{2,10},{3,11},{28,20},{29,... | collective-permute-start | bytes 98312 | tf_op jit(solution)/shard_map/ppermute | solution.py:319
  50.1 1.4 %collective-permute-start.13 = (f32[4,64,128]{2,1,0:T(8,128)S(1)}, f32[4,64,128]{2,1,0:T(8,128)S(1)}, u32[]{:S(2)}, u32[]{:S(2)}) collective-permute-start(f32[4,64,128]{2,1,0:T(8,128)S(1)} %shard_map.51.refs_0_), channel_id=1, source_target_pairs={{4,6},{5,7},{6,4},{7,5},{8,10},{9,11},{10,8},{11,9},{20,22},{21,23... | collective-permute-start | bytes 393224 | tf_op jit(solution)/shard_map/ppermute | solution.py:331
  50.7 3.9 %collective-permute-start.12 = (f32[4,64,128]{2,1,0:T(8,128)S(1)}, f32[4,64,128]{2,1,0:T(8,128)S(1)}, u32[]{:S(2)}, u32[]{:S(2)}) collective-permute-start(f32[4,64,128]{2,1,0:T(8,128)S(1)} %shard_map.51.refs_0_), channel_id=1, source_target_pairs={{4,5},{5,4},{6,7},{7,6},{8,9},{9,8},{10,11},{11,10},{20,21},{21,20... | collective-permute-start | bytes 393224 | tf_op jit(solution)/shard_map/ppermute | solution.py:331
  51.4 3.2 %collective-permute-start.14 = (f32[4,64,128]{2,1,0:T(8,128)S(1)}, f32[4,64,128]{2,1,0:T(8,128)S(1)}, u32[]{:S(2)}, u32[]{:S(2)}) collective-permute-start(f32[4,64,128]{2,1,0:T(8,128)S(1)} %collective-permute-done.13.refs_2_), channel_id=1, source_target_pairs={{4,5},{5,4},{6,7},{7,6},{8,9},{9,8},{10,11},{11,10},{20,21},{21,20... | collective-permute-start | bytes 393224 | tf_op jit(solution)/shard_map/ppermute | solution.py:331
  55.1 12.8 %collective-permute-start.15 = (f32[64,128]{1,0:T(8,128)S(1)}, f32[64,128]{1,0:T(8,128)S(1)}, u32[]{:S(2)}, u32[]{:S(2)}) collective-permute-start(f32[64,128]{1,0:T(8,128)S(1)} %get-tuple-element.48), channel_id=1, source_target_pairs={{4,0},{5,1},{6,2},{7,3},{8,12},{9,13},{10,14},{11,15},{20,16},{21,... | collective-permute-start | bytes 98312 | tf_op jit(solution)/shard_map/ppermute | solution.py:324
  56.4 11.5 %collective-permute-start.16 = (f32[64,128]{1,0:T(8,128)S(1)}, f32[64,128]{1,0:T(8,128)S(1)}, u32[]{:S(2)}, u32[]{:S(2)}) collective-permute-start(f32[64,128]{1,0:T(8,128)S(1)} %get-tuple-element.49), channel_id=1, source_target_pairs={{4,8},{5,9},{6,10},{7,11},{8,4},{9,5},{10,6},{11,7},{20,24},{21,25... | collective-permute-start | bytes 98312 | tf_op jit(solution)/shard_map/ppermute | solution.py:324
  57.1 15.4 %collective-permute-start.17 = (f32[64,128]{1,0:T(8,128)S(1)}, f32[64,128]{1,0:T(8,128)S(1)}, u32[]{:S(2)}, u32[]{:S(2)}) collective-permute-start(f32[64,128]{1,0:T(8,128)S(1)} %get-tuple-element.50), channel_id=1, source_target_pairs={{4,12},{5,13},{6,14},{7,15},{8,0},{9,1},{10,2},{11,3},{20,28},{21,... | collective-permute-start | bytes 98312 | tf_op jit(solution)/shard_map/ppermute | solution.py:324

commit v8 on v6

--- a/solution.py
+++ b/solution.py
@@ -155,14 +155,16 @@
         hi, lo = split(x1)
         counted = jnp.broadcast_to(ok, (16, BLOCK)).astype(BF16)
         data = jnp.concatenate([hi, lo, counted], axis=0)
-        part = dot(one_hot(row(mask_ids, b, BLOCK), slots), data, NT)
+        part = dot(data, one_hot(row(mask_ids, b, BLOCK), slots), NT)
         if b == 0:
             acc[...] = part
         else:
             acc[...] += part
-    both = fold(acc[:, :LANES])
+    columns = x.shape[0]
+    sums = acc[:columns] + acc[columns : 2 * columns]
+    both = jnp.concatenate([sums, sums], axis=0).T
     own[...] = both
-    count = jnp.broadcast_to(acc[:, LANES : LANES + 1], (slots, LANES))
+    count = jnp.broadcast_to(acc[2 * columns : 2 * columns + 1], (LANES, slots)).T
     own_count[...] = count
     tiles[:, : 8 * NEAR] = to_tiles(both, n).reshape(far, 8 * NEAR, LANES)
     about = jnp.where(iota((slots, LANES), 1) % 16 < 8, column(firms[...].astype(F32)), count)
@@ -355,7 +357,7 @@
         [
             pltpu.VMEM(of_rows, F32),
             whole,
-            pltpu.VMEM((slots, 2 * columns + 16), F32),
+            pltpu.VMEM((2 * columns + 16, slots), F32),
             pltpu.VMEM(lengths.shape, jnp.int32),
             pltpu.VMEM(ids.shape, jnp.int32),
             pltpu.VMEM(firms.shape, jnp.int32),

time: 55.8 us -> 54.6 us (0.978)
  Pallas kernels: 17.2 us -> 16 us
    pallas_call x1, Pallas kernels: 6.45 us -> 5.22 us  [body(): call(functools.partial(sums_kernel, n, pad), [tile_about] * far + [of_slo...]
where the time goes in v8:
time: 54.6 us; the launch traced here: 54.4 us
  starting transfers between devices  22.7 us (42%)
  Pallas kernels  16 us (29%)
  waiting for transfers between devices  15.5 us (28%)
    ppermute x12, starting transfers between devices, exchange(): lax.ppermute(part, 'rows', step)  19 us
    ppermute x12, waiting for transfers between devices, exchange(): lax.ppermute(part, 'rows', step)  12.8 us
    pallas_call x1, Pallas kernels, body(): call(functools.partial(sums_kernel, n, pad), [tile_about] * far + [of_slo...  5.22 us
    pallas_call x2, Pallas kernels, first(): call(functools.partial(first_kernel, pad, start), array((columns, width),...  4.4 us
    ppermute x6, starting transfers between devices, share(): lax.ppermute(part, 'rows', [(i, i ^ k) for i in range(n)])  3.71 us
    ppermute x6, waiting for transfers between devices, share(): lax.ppermute(part, 'rows', [(i, i ^ k) for i in range(n)])  2.69 us
    pallas_call x1, Pallas kernels, body(): call(functools.partial(worker_kernel, pad), array((2 * slots, slots), BF1...  2.57 us
    pallas_call x1, Pallas kernels, body(): call(functools.partial(last_kernel, far), array((columns, rows_dev), F32)...  1.76 us
  transfers between devices with their start and end apart: 18, of which 9 were waited for; matrix products, arithmetic and copies ran while one was open for 0% of the time, Pallas kernels for 13%

profile of v8, /device:TPU:0, one launch (start us, length us, event | category | flops | bytes accessed | tf_op | source)
XLA Modules:
  0.0 54.4 jit_solution(3222746637074616490)
XLA Ops:
  0.0 0.0 copy-start
  0.0 5.2 %shard_map.46 = (f32[40,128]{1,0:T(8,128)S(1)}, f32[40,128]{1,0:T(8,128)S(1)}, f32[40,128]{1,0:T(8,128)S(1)}, f32[40,128]{1,0:T(8,128)S(1)}, f32[256,128]{1,0:T(...) custom-call(f32[64,8192]{1,0:T(8,128)} %probes.3, s32[8,128]{1,0:T(8,128)} %bitcast.3, ...), custom_call_target="tpu_custom_call" | custom-call | flops 1073741824 | bytes 2097152 | tf_op jit(solution)/shard_map/pallas_call | solution.py:352
  5.2 3.1 %collective-permute-start = (f32[40,128]{1,0:T(8,128)S(1)}, f32[40,128]{1,0:T(8,128)S(1)}, u32[]{:S(2)}, u32[]{:S(2)}) collective-permute-start(f32[40,128]{1,0:T(8,128)S(1)} %get-tuple-element.29), channel_id=1, source_target_pairs={{0,4},{1,5},{2,6},{3,7},{4,0},{5,1},{6,2},{7,3},{8,12},{9,13},{10,... | collective-permute-start | bytes 61448 | tf_op jit(solution)/shard_map/ppermute | solution.py:307
  8.3 2.6 %collective-permute-start.1 = (f32[40,128]{1,0:T(8,128)S(1)}, f32[40,128]{1,0:T(8,128)S(1)}, u32[]{:S(2)}, u32[]{:S(2)}) collective-permute-start(f32[40,128]{1,0:T(8,128)S(1)} %get-tuple-element.30), channel_id=1, source_target_pairs={{0,8},{1,9},{2,10},{3,11},{4,12},{5,13},{6,14},{7,15},{8,0},{9,1},... | collective-permute-start | bytes 61448 | tf_op jit(solution)/shard_map/ppermute | solution.py:307
  10.9 0.0 collective-permute-start.2
  10.9 0.0 collective-permute-done.refs_1_
  10.9 2.3 %collective-permute-done.1.refs_2_ = f32[40,128]{1,0:T(8,128)S(1)} collective-permute-done((f32[40,128]{1,0:T(8,128)S(1)}, f32[40,128]{1,0:T(8,128)S(1)}, u32[]{:S(2)}, u32[]{:S(2)}) %collective-permute-start.1) | collective-permute-done | bytes 20512 | tf_op jit(solution)/shard_map/ppermute | solution.py:307
  13.2 3.3 %collective-permute-done.2.refs_3_ = f32[40,128]{1,0:T(8,128)S(1)} collective-permute-done((f32[40,128]{1,0:T(8,128)S(1)}, f32[40,128]{1,0:T(8,128)S(1)}, u32[]{:S(2)}, u32[]{:S(2)}) %collective-permute-start.2) | collective-permute-done | bytes 20512 | tf_op jit(solution)/shard_map/ppermute | solution.py:307
  16.5 0.0 collective-permute-start.5
  16.5 1.6 %collective-permute-start.4 = (f32[4,40,128]{2,1,0:T(8,128)S(1)}, f32[4,40,128]{2,1,0:T(8,128)S(1)}, u32[]{:S(2)}, u32[]{:S(2)}) collective-permute-start(f32[4,40,128]{2,1,0:T(8,128)S(1)} %shard_map.47.refs_0_), channel_id=1, source_target_pairs={{0,2},{1,3},{2,0},{3,1},{4,6},{5,7},{6,4},{7,5},{8,10},{9,11},{10,... | collective-permute-start | bytes 245768 | tf_op jit(solution)/shard_map/ppermute | solution.py:311
  18.1 0.3 collective-permute-start.3
  18.4 0.0 copy-done
  18.4 2.6 %shard_map.48.refs_4_.refs_6_ = bf16[512,256]{1,0:T(8,128)(2,1)S(1)} custom-call(s32[8,128]{1,0:T(8,128)S(1)} %bitcast.4, s32[64,128]{1,0:T(8,128)S(1)} %get-tuple-element.32.mask_ids.refs_6_), custom_call_target="tpu_custom_call" | custom-call | flops 1073741824 | bytes 262144 | tf_op jit(solution)/shard_map/pallas_call | solution.py:377
  20.9 0.2 collective-permute-done.5.refs_3_
  21.2 1.8 %collective-permute-done.4.refs_2_ = f32[4,40,128]{2,1,0:T(8,128)S(1)} collective-permute-done((f32[4,40,128]{2,1,0:T(8,128)S(1)}, f32[4,40,128]{2,1,0:T(8,128)S(1)}, u32[]{:S(2)}, u32[]{:S(2)}) %collective-permute-start.4) | collective-permute-done | bytes 81952 | tf_op jit(solution)/shard_map/ppermute | solution.py:311
  23.0 0.0 collective-permute-done.3.refs_1_
  23.0 1.2 %shard_map.49 = (f32[32,128]{1,0:T(8,128)S(1)}, f32[32,128]{1,0:T(8,128)S(1)}, f32[32,128]{1,0:T(8,128)S(1)}, f32[32,128]{1,0:T(8,128)S(1)}, bf16[256,1024]{1,0:T(8,128)(2,1)S(1)}, /*index=5*/f32[256,128]{1,0:T(8,128)S(1)}) custom-call(f32[4,40,128]{2,1,0:T(8,128)S(1)} %shard_map.47.refs_0_, f32[4,40,128]{2,1,0:T(8,128)S(1)} %collective-permute-done.3.refs_1_, ...), custom_call_target="tpu_custom_call" | custom-call | flops 33554432 | bytes 262144 | tf_op jit(solution)/shard_map/pallas_call | solution.py:386
  24.2 0.1 collective-permute-start.6
  24.3 0.8 %collective-permute-start.7 = (f32[32,128]{1,0:T(8,128)S(1)}, f32[32,128]{1,0:T(8,128)S(1)}, u32[]{:S(2)}, u32[]{:S(2)}) collective-permute-start(f32[32,128]{1,0:T(8,128)S(1)} %get-tuple-element.35), channel_id=1, source_target_pairs={{0,8},{1,9},{2,10},{3,11},{4,12},{5,13},{6,14},{7,15},{8,0},{9,1},... | collective-permute-start | bytes 49160 | tf_op jit(solution)/shard_map/ppermute | solution.py:307
  25.1 3.6 %collective-permute-start.8 = (f32[32,128]{1,0:T(8,128)S(1)}, f32[32,128]{1,0:T(8,128)S(1)}, u32[]{:S(2)}, u32[]{:S(2)}) collective-permute-start(f32[32,128]{1,0:T(8,128)S(1)} %get-tuple-element.36), channel_id=1, source_target_pairs={{0,12},{1,13},{2,14},{3,15},{4,8},{5,9},{6,10},{7,11},{8,4},{9,5},... | collective-permute-start | bytes 49160 | tf_op jit(solution)/shard_map/ppermute | solution.py:307
  28.7 0.0 collective-permute-done.6.refs_1_
  28.7 0.3 collective-permute-done.7.refs_2_
  29.0 1.6 %collective-permute-done.8.refs_3_ = f32[32,128]{1,0:T(8,128)S(1)} collective-permute-done((f32[32,128]{1,0:T(8,128)S(1)}, f32[32,128]{1,0:T(8,128)S(1)}, u32[]{:S(2)}, u32[]{:S(2)}) %collective-permute-start.8) | collective-permute-done | bytes 16416 | tf_op jit(solution)/shard_map/ppermute | solution.py:307
  30.6 0.4 shard_map.50
  31.0 0.4 collective-permute-start.9
  31.4 3.8 %collective-permute-start.10 = (f32[32,128]{1,0:T(8,128)S(1)}, f32[32,128]{1,0:T(8,128)S(1)}, u32[]{:S(2)}, u32[]{:S(2)}) collective-permute-start(f32[32,128]{1,0:T(8,128)S(1)} %get-tuple-element.41), channel_id=1, source_target_pairs={{0,8},{1,9},{2,10},{3,11},{4,12},{5,13},{6,14},{7,15},{8,0},{9,1},... | collective-permute-start | bytes 49160 | tf_op jit(solution)/shard_map/ppermute | solution.py:307
  35.3 0.2 collective-permute-start.11
  35.5 0.0 collective-permute-done.9.refs_1_
  35.5 1.5 %collective-permute-done.10.refs_2_ = f32[32,128]{1,0:T(8,128)S(1)} collective-permute-done((f32[32,128]{1,0:T(8,128)S(1)}, f32[32,128]{1,0:T(8,128)S(1)}, u32[]{:S(2)}, u32[]{:S(2)}) %collective-permute-start.10) | collective-permute-done | bytes 16416 | tf_op jit(solution)/shard_map/ppermute | solution.py:307
  37.0 3.8 %collective-permute-done.11.refs_3_ = f32[32,128]{1,0:T(8,128)S(1)} collective-permute-done((f32[32,128]{1,0:T(8,128)S(1)}, f32[32,128]{1,0:T(8,128)S(1)}, u32[]{:S(2)}, u32[]{:S(2)}) %collective-permute-start.11) | collective-permute-done | bytes 16416 | tf_op jit(solution)/shard_map/ppermute | solution.py:307
  40.8 0.0 collective-permute-start.14
  40.8 0.4 collective-permute-start.13
  41.2 1.4 %collective-permute-start.12 = (f32[4,32,128]{2,1,0:T(8,128)S(1)}, f32[4,32,128]{2,1,0:T(8,128)S(1)}, u32[]{:S(2)}, u32[]{:S(2)}) collective-permute-start(f32[4,32,128]{2,1,0:T(8,128)S(1)} %shard_map.51.refs_0_), channel_id=1, source_target_pairs={{0,1},{1,0},{2,3},{3,2},{4,5},{5,4},{6,7},{7,6},{8,9},{9,8},{10,11... | collective-permute-start | bytes 196616 | tf_op jit(solution)/shard_map/ppermute | solution.py:311
  42.7 2.5 %shard_map.52.refs_6_.refs_4_ = f32[64,5120]{1,0:T(8,128)S(1)} custom-call(f32[64,8192]{1,0:T(8,128)} %probes.3, f32[256,128]{1,0:T(8,128)S(1)} %get-tuple-element.45.mean, s32[64,128]{1,0:T(8,128)S(1)} %get-tuple-element.32.mask_ids.refs_6_, f32[64,128]{1,0:T(8,128)S(1)} %get-tuple-element.46.weight), custom_call_target="tpu_custom_call" | custom-call | flops 671088640 | bytes 2621440 | tf_op jit(solution)/shard_map/pallas_call | solution.py:409
  45.2 0.0 collective-permute-done.14.refs_3_
  45.2 0.6 %collective-permute-done.13.refs_2_ = f32[4,32,128]{2,1,0:T(8,128)S(1)} collective-permute-done((f32[4,32,128]{2,1,0:T(8,128)S(1)}, f32[4,32,128]{2,1,0:T(8,128)S(1)}, u32[]{:S(2)}, u32[]{:S(2)}) %collective-permute-start.13) | collective-permute-done | bytes 65568 | tf_op jit(solution)/shard_map/ppermute | solution.py:311
  45.8 0.0 collective-permute-done.12.refs_1_
  45.8 0.5 shard_map.53
  46.3 0.1 collective-permute-start.15
  46.4 0.7 %collective-permute-start.16 = (f32[32,128]{1,0:T(8,128)S(1)}, f32[32,128]{1,0:T(8,128)S(1)}, u32[]{:S(2)}, u32[]{:S(2)}) collective-permute-start(f32[32,128]{1,0:T(8,128)S(1)} %get-tuple-element.49), channel_id=1, source_target_pairs={{0,8},{1,9},{2,10},{3,11},{4,12},{5,13},{6,14},{7,15},{8,0},{9,1},... | collective-permute-start | bytes 49160 | tf_op jit(solution)/shard_map/ppermute | solution.py:307
  47.1 3.6 %collective-permute-start.17 = (f32[32,128]{1,0:T(8,128)S(1)}, f32[32,128]{1,0:T(8,128)S(1)}, u32[]{:S(2)}, u32[]{:S(2)}) collective-permute-start(f32[32,128]{1,0:T(8,128)S(1)} %get-tuple-element.50), channel_id=1, source_target_pairs={{0,12},{1,13},{2,14},{3,15},{4,8},{5,9},{6,10},{7,11},{8,4},{9,5},... | collective-permute-start | bytes 49160 | tf_op jit(solution)/shard_map/ppermute | solution.py:307
  50.7 1.9 %shard_map.54.refs_5_ = f32[64,3072]{1,0:T(8,128)S(1)} custom-call(f32[64,8192]{1,0:T(8,128)} %probes.3, f32[256,128]{1,0:T(8,128)S(1)} %get-tuple-element.45.mean, s32[64,128]{1,0:T(8,128)S(1)} %get-tuple-element.32.mask_ids.refs_6_, f32[64,128]{1,0:T(8,128)S(1)} %get-tuple-element.46.weight), custom_call_target="tpu_custom_call" | custom-call | flops 402653184 | bytes 1572864 | tf_op jit(solution)/shard_map/pallas_call | solution.py:409
  52.6 0.0 collective-permute-done.15.refs_1_
  52.6 0.0 collective-permute-done.16.refs_2_
  52.7 0.0 collective-permute-done.17.refs_3_
  52.7 1.8 %shard_map.55 = f32[64,8192]{1,0:T(8,128)} custom-call(f32[32,128]{1,0:T(8,128)S(1)} %get-tuple-element.47.refs_0_, f32[32,128]{1,0:T(8,128)S(1)} %collective-permute-done.15.refs_1_, f32[32,128]{1,0:T(8,128)S(1)} %collective-permute-done.16.refs_2_, f32[32,128]{1,0:T(8,128)S(1)} %collective-permute-done.17.refs_3_, ...), custom_call_target="tpu_custom_call" | custom-call | flops 536870912 | bytes 4194304 | tf_op jit(solution)/shard_map/pallas_call | solution.py:430
  (2 shorter events, 0.0 us)
Async XLA Ops:
  0.0 18.4 %copy-start = (s32[1024]{0:T(1024)S(1)}, s32[1024]{0:T(1024)}, u32[]{:S(2)}) copy-start(s32[1024]{0:T(1024)} %param.5) | copy-start | bytes 12292
  5.2 5.7 %collective-permute-start = (f32[40,128]{1,0:T(8,128)S(1)}, f32[40,128]{1,0:T(8,128)S(1)}, u32[]{:S(2)}, u32[]{:S(2)}) collective-permute-start(f32[40,128]{1,0:T(8,128)S(1)} %get-tuple-element.29), channel_id=1, source_target_pairs={{0,4},{1,5},{2,6},{3,7},{4,0},{5,1},{6,2},{7,3},{8,12},{9,13},{10,... | collective-permute-start | bytes 61448 | tf_op jit(solution)/shard_map/ppermute | solution.py:307
  8.3 4.9 %collective-permute-start.1 = (f32[40,128]{1,0:T(8,128)S(1)}, f32[40,128]{1,0:T(8,128)S(1)}, u32[]{:S(2)}, u32[]{:S(2)}) collective-permute-start(f32[40,128]{1,0:T(8,128)S(1)} %get-tuple-element.30), channel_id=1, source_target_pairs={{0,8},{1,9},{2,10},{3,11},{4,12},{5,13},{6,14},{7,15},{8,0},{9,1},... | collective-permute-start | bytes 61448 | tf_op jit(solution)/shard_map/ppermute | solution.py:307
  10.9 5.6 %collective-permute-start.2 = (f32[40,128]{1,0:T(8,128)S(1)}, f32[40,128]{1,0:T(8,128)S(1)}, u32[]{:S(2)}, u32[]{:S(2)}) collective-permute-start(f32[40,128]{1,0:T(8,128)S(1)} %get-tuple-element.31), channel_id=1, source_target_pairs={{0,12},{1,13},{2,14},{3,15},{4,8},{5,9},{6,10},{7,11},{8,4},{9,5},... | collective-permute-start | bytes 61448 | tf_op jit(solution)/shard_map/ppermute | solution.py:307
  16.5 4.7 %collective-permute-start.5 = (f32[4,40,128]{2,1,0:T(8,128)S(1)}, f32[4,40,128]{2,1,0:T(8,128)S(1)}, u32[]{:S(2)}, u32[]{:S(2)}) collective-permute-start(f32[4,40,128]{2,1,0:T(8,128)S(1)} %shard_map.47.refs_0_), channel_id=1, source_target_pairs={{0,3},{1,2},{2,1},{3,0},{4,7},{5,6},{6,5},{7,4},{8,11},{9,10},{10,... | collective-permute-start | bytes 245768 | tf_op jit(solution)/shard_map/ppermute | solution.py:311
  16.5 6.5 %collective-permute-start.4 = (f32[4,40,128]{2,1,0:T(8,128)S(1)}, f32[4,40,128]{2,1,0:T(8,128)S(1)}, u32[]{:S(2)}, u32[]{:S(2)}) collective-permute-start(f32[4,40,128]{2,1,0:T(8,128)S(1)} %shard_map.47.refs_0_), channel_id=1, source_target_pairs={{0,2},{1,3},{2,0},{3,1},{4,6},{5,7},{6,4},{7,5},{8,10},{9,11},{10,... | collective-permute-start | bytes 245768 | tf_op jit(solution)/shard_map/ppermute | solution.py:311
  18.1 4.9 %collective-permute-start.3 = (f32[4,40,128]{2,1,0:T(8,128)S(1)}, f32[4,40,128]{2,1,0:T(8,128)S(1)}, u32[]{:S(2)}, u32[]{:S(2)}) collective-permute-start(f32[4,40,128]{2,1,0:T(8,128)S(1)} %shard_map.47.refs_0_), channel_id=1, source_target_pairs={{0,1},{1,0},{2,3},{3,2},{4,5},{5,4},{6,7},{7,6},{8,9},{9,8},{10,11... | collective-permute-start | bytes 245768 | tf_op jit(solution)/shard_map/ppermute | solution.py:311
  24.2 4.5 %collective-permute-start.6 = (f32[32,128]{1,0:T(8,128)S(1)}, f32[32,128]{1,0:T(8,128)S(1)}, u32[]{:S(2)}, u32[]{:S(2)}) collective-permute-start(f32[32,128]{1,0:T(8,128)S(1)} %get-tuple-element.34), channel_id=1, source_target_pairs={{0,4},{1,5},{2,6},{3,7},{4,0},{5,1},{6,2},{7,3},{8,12},{9,13},{10,... | collective-permute-start | bytes 49160 | tf_op jit(solution)/shard_map/ppermute | solution.py:307
  24.3 4.7 %collective-permute-start.7 = (f32[32,128]{1,0:T(8,128)S(1)}, f32[32,128]{1,0:T(8,128)S(1)}, u32[]{:S(2)}, u32[]{:S(2)}) collective-permute-start(f32[32,128]{1,0:T(8,128)S(1)} %get-tuple-element.35), channel_id=1, source_target_pairs={{0,8},{1,9},{2,10},{3,11},{4,12},{5,13},{6,14},{7,15},{8,0},{9,1},... | collective-permute-start | bytes 49160 | tf_op jit(solution)/shard_map/ppermute | solution.py:307
  25.1 5.5 %collective-permute-start.8 = (f32[32,128]{1,0:T(8,128)S(1)}, f32[32,128]{1,0:T(8,128)S(1)}, u32[]{:S(2)}, u32[]{:S(2)}) collective-permute-start(f32[32,128]{1,0:T(8,128)S(1)} %get-tuple-element.36), channel_id=1, source_target_pairs={{0,12},{1,13},{2,14},{3,15},{4,8},{5,9},{6,10},{7,11},{8,4},{9,5},... | collective-permute-start | bytes 49160 | tf_op jit(solution)/shard_map/ppermute | solution.py:307
  31.0 4.5 %collective-permute-start.9 = (f32[32,128]{1,0:T(8,128)S(1)}, f32[32,128]{1,0:T(8,128)S(1)}, u32[]{:S(2)}, u32[]{:S(2)}) collective-permute-start(f32[32,128]{1,0:T(8,128)S(1)} %get-tuple-element.40), channel_id=1, source_target_pairs={{0,4},{1,5},{2,6},{3,7},{4,0},{5,1},{6,2},{7,3},{8,12},{9,13},{10,... | collective-permute-start | bytes 49160 | tf_op jit(solution)/shard_map/ppermute | solution.py:307
  31.4 5.5 %collective-permute-start.10 = (f32[32,128]{1,0:T(8,128)S(1)}, f32[32,128]{1,0:T(8,128)S(1)}, u32[]{:S(2)}, u32[]{:S(2)}) collective-permute-start(f32[32,128]{1,0:T(8,128)S(1)} %get-tuple-element.41), channel_id=1, source_target_pairs={{0,8},{1,9},{2,10},{3,11},{4,12},{5,13},{6,14},{7,15},{8,0},{9,1},... | collective-permute-start | bytes 49160 | tf_op jit(solution)/shard_map/ppermute | solution.py:307
  35.3 5.5 %collective-permute-start.11 = (f32[32,128]{1,0:T(8,128)S(1)}, f32[32,128]{1,0:T(8,128)S(1)}, u32[]{:S(2)}, u32[]{:S(2)}) collective-permute-start(f32[32,128]{1,0:T(8,128)S(1)} %get-tuple-element.42), channel_id=1, source_target_pairs={{0,12},{1,13},{2,14},{3,15},{4,8},{5,9},{6,10},{7,11},{8,4},{9,5},... | collective-permute-start | bytes 49160 | tf_op jit(solution)/shard_map/ppermute | solution.py:307
  40.8 4.4 %collective-permute-start.14 = (f32[4,32,128]{2,1,0:T(8,128)S(1)}, f32[4,32,128]{2,1,0:T(8,128)S(1)}, u32[]{:S(2)}, u32[]{:S(2)}) collective-permute-start(f32[4,32,128]{2,1,0:T(8,128)S(1)} %shard_map.51.refs_0_), channel_id=1, source_target_pairs={{0,3},{1,2},{2,1},{3,0},{4,7},{5,6},{6,5},{7,4},{8,11},{9,10},{10,... | collective-permute-start | bytes 196616 | tf_op jit(solution)/shard_map/ppermute | solution.py:311
  40.8 5.0 %collective-permute-start.13 = (f32[4,32,128]{2,1,0:T(8,128)S(1)}, f32[4,32,128]{2,1,0:T(8,128)S(1)}, u32[]{:S(2)}, u32[]{:S(2)}) collective-permute-start(f32[4,32,128]{2,1,0:T(8,128)S(1)} %shard_map.51.refs_0_), channel_id=1, source_target_pairs={{0,2},{1,3},{2,0},{3,1},{4,6},{5,7},{6,4},{7,5},{8,10},{9,11},{10,... | collective-permute-start | bytes 196616 | tf_op jit(solution)/shard_map/ppermute | solution.py:311
  41.2 4.6 %collective-permute-start.12 = (f32[4,32,128]{2,1,0:T(8,128)S(1)}, f32[4,32,128]{2,1,0:T(8,128)S(1)}, u32[]{:S(2)}, u32[]{:S(2)}) collective-permute-start(f32[4,32,128]{2,1,0:T(8,128)S(1)} %shard_map.51.refs_0_), channel_id=1, source_target_pairs={{0,1},{1,0},{2,3},{3,2},{4,5},{5,4},{6,7},{7,6},{8,9},{9,8},{10,11... | collective-permute-start | bytes 196616 | tf_op jit(solution)/shard_map/ppermute | solution.py:311
  46.3 6.4 %collective-permute-start.15 = (f32[32,128]{1,0:T(8,128)S(1)}, f32[32,128]{1,0:T(8,128)S(1)}, u32[]{:S(2)}, u32[]{:S(2)}) collective-permute-start(f32[32,128]{1,0:T(8,128)S(1)} %get-tuple-element.48), channel_id=1, source_target_pairs={{0,4},{1,5},{2,6},{3,7},{4,0},{5,1},{6,2},{7,3},{8,12},{9,13},{10,... | collective-permute-start | bytes 49160 | tf_op jit(solution)/shard_map/ppermute | solution.py:307
  46.4 6.3 %collective-permute-start.16 = (f32[32,128]{1,0:T(8,128)S(1)}, f32[32,128]{1,0:T(8,128)S(1)}, u32[]{:S(2)}, u32[]{:S(2)}) collective-permute-start(f32[32,128]{1,0:T(8,128)S(1)} %get-tuple-element.49), channel_id=1, source_target_pairs={{0,8},{1,9},{2,10},{3,11},{4,12},{5,13},{6,14},{7,15},{8,0},{9,1},... | collective-permute-start | bytes 49160 | tf_op jit(solution)/shard_map/ppermute | solution.py:307
  47.1 5.6 %collective-permute-start.17 = (f32[32,128]{1,0:T(8,128)S(1)}, f32[32,128]{1,0:T(8,128)S(1)}, u32[]{:S(2)}, u32[]{:S(2)}) collective-permute-start(f32[32,128]{1,0:T(8,128)S(1)} %get-tuple-element.50), channel_id=1, source_target_pairs={{0,12},{1,13},{2,14},{3,15},{4,8},{5,9},{6,10},{7,11},{8,4},{9,5},... | collective-permute-start | bytes 49160 | tf_op jit(solution)/shard_map/ppermute | solution.py:307

commit v9 on v8

--- a/solution.py
+++ b/solution.py
@@ -106,10 +106,12 @@
         copy.wait()
 
 
-def place(tiles, sends):
+def place(tiles, keep, send):
     me = lax.axis_index("rows") // NEAR
-    for k, send in enumerate(sends):
-        send[...] = tiles[me ^ k]
+    half = keep.shape[1]
+    for k in range(half):
+        keep[0, k] = tiles[me ^ k]
+        send[0, k] = tiles[me ^ (half + k)]
 
 
 def column_copies(source, target, sems):
@@ -120,8 +122,8 @@
 
 def sums_kernel(n, pad, *refs):
     far = n // NEAR
-    (probes, lengths_in, ids_in, firms_in), sends = refs[:4], refs[4 : 4 + far]
-    own, own_count, mask_ids, weight, valid, x, acc, lengths, ids, firms, tiles, sems, small = refs[4 + far :]
+    probes, lengths_in, ids_in, firms_in, keep, send, own, own_count, mask_ids, weight = refs[:10]
+    valid, x, acc, lengths, ids, firms, tiles, sems, small = refs[10:]
     copies = column_copies(probes, x, sems)
     first = [
         pltpu.make_async_copy(source, target, small.at[k])
@@ -175,12 +177,27 @@
         for side in range(2):
             packed = jnp.where(eighth // 2 == 2 * owner + side, about[:, owner, side], packed)
     tiles[:, 8 * NEAR :] = packed
-    place(tiles, sends)
-
-
-def join_kernel(*refs):
-    for k, part in enumerate(refs[:-1]):
-        refs[-1][k] = part[...]
+    place(tiles, keep, send)
+
+
+def halve_kernel(kept, received, keep, send):
+    count, half = kept.shape[0], keep.shape[1]
+    for at, part in ((0, kept), (count, received)):
+        keep[at : at + count] = part[:, :half]
+        send[at : at + count] = part[:, half:]
+
+
+def double_kernel(kept, received, keep, send):
+    half, count = keep.shape[0], kept.shape[1]
+    for at, part in ((0, kept), (count, received)):
+        keep[:, at : at + count] = part[:half]
+        send[:, at : at + count] = part[half:]
+
+
+def join_kernel(kept, received, out):
+    count = kept.shape[0]
+    out[:count] = kept[:, 0]
+    out[count:] = received[:, 0]
 
 
 def worker_kernel(pad, lengths, mask_ids, out):
@@ -209,8 +226,8 @@
 
 
 def owner_first_kernel(*refs):
-    parts, sends, (table, scale) = refs[:NEAR], refs[NEAR + 1 : -2], refs[-2:]
-    far = len(sends)
+    parts, (keep, send, table, scale) = refs[:NEAR], refs[NEAR + 1 :]
+    far = 2 * keep.shape[0]
 
     def sides(part, kind):
         about = part[:, 8 * NEAR :].reshape(8 * far, LANES)
@@ -237,35 +254,35 @@
     total = jnp.sum(total, axis=1, keepdims=True)
     scale[...] = jnp.broadcast_to(1.0 / jnp.maximum(total, 1.0), scale.shape)
     means = owner_means([part[:, : 8 * NEAR] for part in parts], table[...], scale[...])
-    for k, send in enumerate(sends):
-        send[...] = means[k]
+    keep[:, 0] = means[: far // 2]
+    send[:, 0] = means[far // 2 :]
 
 
 def owner_second_kernel(*refs):
-    parts, (table, scale), sends = refs[:NEAR], refs[NEAR : NEAR + 2], refs[NEAR + 3 :]
+    parts, (table, scale), (keep, send) = refs[:NEAR], refs[NEAR : NEAR + 2], refs[NEAR + 3 :]
+    far = 2 * keep.shape[0]
     means = owner_means([part[...] for part in parts], table[...], scale[...])
-    for k, send in enumerate(sends):
-        send[...] = means[k]
-
-
-def own_means(parts, tiles):
+    keep[:, 0] = means[: far // 2]
+    send[:, 0] = means[far // 2 :]
+
+
+def own_means(kept, received, tiles):
     me = lax.axis_index("rows") // NEAR
-    for k, part in enumerate(parts):
-        tiles[me ^ k] = part[...]
-    return from_tiles(tiles[...].reshape(len(parts) * NEAR, 8, LANES))
-
-
-def change_kernel(far, *refs):
-    parts, (own, own_count, pairs), sends, (mean, tiles) = (
-        refs[:far], refs[far : far + 3], refs[far + 3 : 2 * far + 3], refs[2 * far + 3 :]
-    )
+    half = kept.shape[1]
+    for k in range(half):
+        tiles[me ^ k] = kept[0, k]
+        tiles[me ^ (half + k)] = received[0, k]
+    return from_tiles(tiles[...].reshape(2 * half * NEAR, 8, LANES))
+
+
+def change_kernel(kept, received, own, own_count, pairs, keep, send, mean, tiles):
     slots = own.shape[0]
-    found = own_means(parts, tiles)
+    found = own_means(kept, received, tiles)
     mean[...] = found
     change = dot(pairs[...], halves(found).astype(BF16))
     new = own[...] - own_count[...] * found + fold(change[:slots] + change[slots:])
-    tiles[...] = to_tiles(new, far * NEAR).reshape(tiles.shape)
-    place(tiles, sends)
+    tiles[...] = to_tiles(new, slots // 16).reshape(tiles.shape)
+    place(tiles, keep, send)
 
 
 def take(parts, ids, slots):
@@ -288,11 +305,10 @@
         y[:, b * BLOCK : (b + 1) * BLOCK] = rest - by_worker(rest, table) * row(weight, start + b, BLOCK)
 
 
-def last_kernel(far, *refs):
-    parts, (before, after, mask_ids, out, tiles, y, sems) = refs[:far], refs[far:]
+def last_kernel(kept, received, before, after, mask_ids, out, tiles, y, sems):
     cut = before.shape[1] // BLOCK
     outs = column_copies(y, out, sems)
-    mean = own_means(parts, tiles)
+    mean = own_means(kept, received, tiles)
     split_mean = halves(mean).T.astype(BF16)
     for b in range(len(outs)):
         spread = take(split_mean, row(mask_ids, b, BLOCK), mean.shape[0])
@@ -300,11 +316,6 @@
         y[:, b * BLOCK : (b + 1) * BLOCK] = source[:, at * BLOCK : (at + 1) * BLOCK] - spread
         outs[b].start()
     wait_all(outs)
-
-
-def exchange(parts, n):
-    steps = [[(i, i ^ (k * NEAR)) for i in range(n)] for k in range(len(parts))]
-    return [parts[0]] + [lax.ppermute(part, "rows", step) for part, step in zip(parts[1:], steps[1:])]
 
 
 def share(part, n):
@@ -349,11 +360,33 @@
     tiles = pltpu.VMEM((far, 8 * NEAR, LANES), F32)
     mine = 16 * NEAR * far
 
-    *sends, own, own_count, mask_ids, weight = call(
+    def swap(part, step):
+        return lax.ppermute(part, "rows", [(i, i ^ (step * NEAR)) for i in range(n)])
+
+    def sort(kernel, kept, received, sources, places):
+        shape = array((sources, places, *kept.shape[2:]), F32)
+        return call(kernel, [shape] * 2, [vmem] * 2, [vmem] * 2, [], 0, shape.size * 16)(kept, received)
+
+    def to_owners(kept, send):
+        places, sources = far // 2, 1
+        while places > 1:
+            kept, send = sort(halve_kernel, kept, swap(send, places), 2 * sources, places // 2)
+            places, sources = places // 2, 2 * sources
+        shape = array((far, *kept.shape[2:]), F32)
+        return call(join_kernel, shape, [vmem] * 2, vmem, [], 0, shape.size * 8)(kept, swap(send, 1))
+
+    def from_owners(kept, send):
+        places = 1
+        while places < far // 2:
+            kept, send = sort(double_kernel, kept, swap(send, places), far // 4 // places, 2 * places)
+            places *= 2
+        return kept, swap(send, places)
+
+    keep, send, own, own_count, mask_ids, weight = call(
         functools.partial(sums_kernel, n, pad),
-        [tile_about] * far + [of_slots, of_slots, array(of_rows, jnp.int32), array(of_rows, F32)],
+        [array((1, far // 2, *tile_about.shape), F32)] * 2 + [of_slots, of_slots, array(of_rows, jnp.int32), array(of_rows, F32)],
         [hbm] * 4,
-        [vmem] * (far + 4),
+        [vmem] * 6,
         [
             pltpu.VMEM(of_rows, F32),
             whole,
@@ -369,11 +402,7 @@
         4 * columns * rows_dev,
     )(in_hbm(probes), in_hbm(lengths), in_hbm(ids), in_hbm(firms))
 
-    def join(parts):
-        shape = array((far, *parts[0].shape), F32)
-        return call(join_kernel, shape, [vmem] * far, vmem, [], 0, shape.size * 8)(*parts)
-
-    received = share(join(exchange(sends, n)), n)
+    received = share(to_owners(keep, send), n)
     pairs = call(
         functools.partial(worker_kernel, pad),
         array((2 * slots, slots), BF16),
@@ -383,26 +412,26 @@
         2 * work,
         4 * slots * slots,
     )(lengths, mask_ids)
-    *sends, table, scale = call(
+    keep, send, table, scale = call(
         owner_first_kernel,
-        [tile] * far + [array((mine, NEAR * mine), BF16), array((mine, LANES), F32)],
+        [array((far // 2, 1, *tile.shape), F32)] * 2 + [array((mine, NEAR * mine), BF16), array((mine, LANES), F32)],
         [vmem] * (NEAR + 1),
-        [vmem] * (far + 2),
+        [vmem] * 4,
         [],
         work // 16,
         slots * slots * 4,
     )(*received, pairs)
-    received = exchange(sends, n)
-    *sends, mean = call(
-        functools.partial(change_kernel, far),
-        [tile] * far + [of_slots],
-        [vmem] * (far + 3),
-        [vmem] * (far + 1),
+    kept, received = from_owners(keep, send)
+    keep, send, mean = call(
+        change_kernel,
+        [array((1, far // 2, *tile.shape), F32)] * 2 + [of_slots],
+        [vmem] * 5,
+        [vmem] * 3,
         [tiles],
         work // 16,
         slots * slots * 4,
-    )(*received, own, own_count, pairs)
-    received = share(join(exchange(sends, n)), n)
+    )(kept, received, own, own_count, pairs)
+    received = share(to_owners(keep, send), n)
 
     def first(start, stop):
         width = (stop - start) * BLOCK
@@ -417,25 +446,25 @@
         )(in_hbm(probes), mean, mask_ids, weight)
 
     before, after = first(0, 5 * blocks // 8), first(5 * blocks // 8, blocks)
-    sends = call(
+    keep, send = call(
         owner_second_kernel,
-        [tile] * far,
+        [array((far // 2, 1, *tile.shape), F32)] * 2,
         [vmem] * (NEAR + 3),
-        [vmem] * far,
+        [vmem] * 2,
         [],
         work // 16,
         slots * slots * 4,
     )(*received, table, scale, before)
-    received = exchange(sends, n)
+    kept, received = from_owners(keep, send)
     return call(
-        functools.partial(last_kernel, far),
+        last_kernel,
         array((columns, rows_dev), F32),
-        [vmem] * (far + 3),
+        [vmem] * 5,
         hbm,
         [tiles, whole, sems],
         work,
         8 * columns * rows_dev,
-    )(*received, before, after, mask_ids)
+    )(kept, received, before, after, mask_ids)
 
 
 def solution(mesh):

time: 54.6 us -> 57.7 us (1.057)
  waiting for transfers between devices: 15.5 us -> 19.8 us
  starting transfers between devices: 22.7 us -> 21.6 us
    ppermute x12 -> x8, waiting for transfers between devices: 12.8 us -> 17.2 us  [swap(): return lax.ppermute(part, 'rows', [(i, i ^ step * NEAR) for i in range(n)])]
    ppermute x12 -> x8, starting transfers between devices: 19 us -> 17.8 us  [swap(): return lax.ppermute(part, 'rows', [(i, i ^ step * NEAR) for i in range(n)])]
    pallas_call x7 -> x11, Pallas kernels: 9.06 us -> 9.07 us  [the longest x1 5.22 us: body(): call(functools.partial(sums_kernel, n, pad), [array((1, far // 2, *tile_a...]
  transfers between devices with their start and end apart: 18 -> 14, of which waited for: 9 -> 10; matrix products, arithmetic and copies ran while one was open for 0% -> 0% of each run, Pallas kernels for 13% -> 12%
where the time goes in v9:
time: 57.7 us; the launch traced here: 57.5 us
  starting transfers between devices  21.6 us (37%)
  waiting for transfers between devices  19.8 us (34%)
  Pallas kernels  16 us (28%)
    ppermute x8, starting transfers between devices, swap(): return lax.ppermute(part, 'rows', [(i, i ^ step * NEAR) for i in range(n)])  17.8 us
    ppermute x8, waiting for transfers between devices, swap(): return lax.ppermute(part, 'rows', [(i, i ^ step * NEAR) for i in range(n)])  17.2 us
    pallas_call x1, Pallas kernels, body(): call(functools.partial(sums_kernel, n, pad), [array((1, far // 2, *tile_a...  5.22 us
    pallas_call x2, Pallas kernels, first(): call(functools.partial(first_kernel, pad, start), array((columns, width),...  4.4 us
    ppermute x6, starting transfers between devices, share(): lax.ppermute(part, 'rows', [(i, i ^ k) for i in range(n)])  3.73 us
    ppermute x6, waiting for transfers between devices, share(): lax.ppermute(part, 'rows', [(i, i ^ k) for i in range(n)])  2.64 us
    pallas_call x1, Pallas kernels, body(): call(functools.partial(worker_kernel, pad), array((2 * slots, slots), BF1...  2.57 us
    pallas_call x1, Pallas kernels, body(): call(last_kernel, array((columns, rows_dev), F32), [vmem] * 5, hbm, [tile...  1.76 us
  transfers between devices with their start and end apart: 14, of which 10 were waited for; matrix products, arithmetic and copies ran while one was open for 0% of the time, Pallas kernels for 12%

profile of v9, /device:TPU:0, one launch (start us, length us, event | category | flops | bytes accessed | tf_op | source)
XLA Modules:
  0.0 57.5 jit_solution(5526604946445500406)
XLA Ops:
  0.0 0.0 copy-start
  0.0 5.2 %shard_map.46 = (f32[1,2,40,128]{3,2,1,0:T(8,128)S(1)}, f32[1,2,40,128]{3,2,1,0:T(8,128)S(1)}, f32[256,128]{1,0:T(8,128)S(1)}, f32[256,128]{1,0:T(8,128)S(1)}, s...) custom-call(f32[64,8192]{1,0:T(8,128)} %probes.3, s32[8,128]{1,0:T(8,128)} %bitcast.3, s32[64,128]{1,0:T(8,128)} %bitcast.5, ...), custom_call_target="tpu_custom_call" | custom-call | flops 1073741824 | bytes 2097152 | tf_op jit(solution)/shard_map/pallas_call | solution.py:385
  5.2 4.1 %collective-permute-start = (f32[1,2,40,128]{3,2,1,0:T(8,128)S(1)}, f32[1,2,40,128]{3,2,1,0:T(8,128)S(1)}, u32[]{:S(2)}, u32[]{:S(2)}) collective-permute-start(f32[1,2,40,128]{3,2,1,0:T(8,128)S(1)} %get-tuple-element.29), channel_id=1, source_target_pairs={{0,8},{1,9},{2,10},{3,11},{4,12},{5,13},{6,14},{7,15},{8,0},{9,1},... | collective-permute-start | bytes 122888 | tf_op jit(solution)/shard_map/ppermute | solution.py:364
  9.3 2.4 %collective-permute-done.received = f32[1,2,40,128]{3,2,1,0:T(8,128)S(1)} collective-permute-done((f32[1,2,40,128]{3,2,1,0:T(8,128)S(1)}, f32[1,2,40,128]{3,2,1,0:T(8,128)S(1)}, u32[]{:S(2)}, u32[]{:S(2)}) %collective-permute-start) | collective-permute-done | bytes 40992 | tf_op jit(solution)/shard_map/ppermute | solution.py:364
  11.8 1.5 %collective-permute-start.1 = (f32[2,1,40,128]{3,2,1,0:T(8,128)S(1)}, f32[2,1,40,128]{3,2,1,0:T(8,128)S(1)}, u32[]{:S(2)}, u32[]{:S(2)}) collective-permute-start(f32[2,1,40,128]{3,2,1,0:T(8,128)S(1)} %get-tuple-element.31), channel_id=1, source_target_pairs={{0,4},{1,5},{2,6},{3,7},{4,0},{5,1},{6,2},{7,3},{8,12},{9,13},{10,... | collective-permute-start | bytes 122888 | tf_op jit(solution)/shard_map/ppermute | solution.py:364
  13.2 2.5 %collective-permute-done.1.received = f32[2,1,40,128]{3,2,1,0:T(8,128)S(1)} collective-permute-done((f32[2,1,40,128]{3,2,1,0:T(8,128)S(1)}, f32[2,1,40,128]{3,2,1,0:T(8,128)S(1)}, u32[]{:S(2)}, u32[]{:S(2)}) %collective-permute-start.1) | collective-permute-done | bytes 40992 | tf_op jit(solution)/shard_map/ppermute | solution.py:364
  15.8 0.0 collective-permute-start.4
  15.8 1.8 %collective-permute-start.3 = (f32[4,40,128]{2,1,0:T(8,128)S(1)}, f32[4,40,128]{2,1,0:T(8,128)S(1)}, u32[]{:S(2)}, u32[]{:S(2)}) collective-permute-start(f32[4,40,128]{2,1,0:T(8,128)S(1)} %shard_map.48.refs_0_), channel_id=1, source_target_pairs={{0,2},{1,3},{2,0},{3,1},{4,6},{5,7},{6,4},{7,5},{8,10},{9,11},{10,... | collective-permute-start | bytes 245768 | tf_op jit(solution)/shard_map/ppermute | solution.py:322
  17.6 0.1 collective-permute-start.2
  17.7 0.0 copy-done
  17.7 2.6 %shard_map.49.refs_4_.pairs = bf16[512,256]{1,0:T(8,128)(2,1)S(1)} custom-call(s32[8,128]{1,0:T(8,128)S(1)} %bitcast.4, s32[64,128]{1,0:T(8,128)S(1)} %get-tuple-element.32.mask_ids), custom_call_target="tpu_custom_call" | custom-call | flops 1073741824 | bytes 262144 | tf_op jit(solution)/shard_map/pallas_call | solution.py:406
  20.2 0.0 collective-permute-done.4.refs_3_
  20.2 2.0 %collective-permute-done.3.refs_2_ = f32[4,40,128]{2,1,0:T(8,128)S(1)} collective-permute-done((f32[4,40,128]{2,1,0:T(8,128)S(1)}, f32[4,40,128]{2,1,0:T(8,128)S(1)}, u32[]{:S(2)}, u32[]{:S(2)}) %collective-permute-start.3) | collective-permute-done | bytes 81952 | tf_op jit(solution)/shard_map/ppermute | solution.py:322
  22.3 0.0 collective-permute-done.2.refs_1_
  22.3 1.2 %shard_map.50 = (f32[2,1,32,128]{3,2,1,0:T(8,128)S(1)}, f32[2,1,32,128]{3,2,1,0:T(8,128)S(1)}, bf16[256,1024]{1,0:T(8,128)(2,1)S(1)}, f32[256,128]{1,0:T(8,128)S(1)}) custom-call(f32[4,40,128]{2,1,0:T(8,128)S(1)} %shard_map.48.refs_0_, f32[4,40,128]{2,1,0:T(8,128)S(1)} %collective-permute-done.2.refs_1_, f32[4,40,128]{2,1,0:T(8,128)S(1)} %collective-permute-done.3.refs_2_, ...), custom_call_target="tpu_custom_call" | custom-call | flops 33554432 | bytes 262144 | tf_op jit(solution)/shard_map/pallas_call | solution.py:415
  23.5 1.5 %collective-permute-start.5 = (f32[2,1,32,128]{3,2,1,0:T(8,128)S(1)}, f32[2,1,32,128]{3,2,1,0:T(8,128)S(1)}, u32[]{:S(2)}, u32[]{:S(2)}) collective-permute-start(f32[2,1,32,128]{3,2,1,0:T(8,128)S(1)} %get-tuple-element.34), channel_id=1, source_target_pairs={{0,4},{1,5},{2,6},{3,7},{4,0},{5,1},{6,2},{7,3},{8,12},{9,13},{10,... | collective-permute-start | bytes 98312 | tf_op jit(solution)/shard_map/ppermute | solution.py:364
  25.0 2.4 %collective-permute-done.5.received = f32[2,1,32,128]{3,2,1,0:T(8,128)S(1)} collective-permute-done((f32[2,1,32,128]{3,2,1,0:T(8,128)S(1)}, f32[2,1,32,128]{3,2,1,0:T(8,128)S(1)}, u32[]{:S(2)}, u32[]{:S(2)}) %collective-permute-start.5) | collective-permute-done | bytes 32800 | tf_op jit(solution)/shard_map/ppermute | solution.py:364
  27.5 2.5 %collective-permute-start.6 = (f32[1,2,32,128]{3,2,1,0:T(8,128)S(1)}, f32[1,2,32,128]{3,2,1,0:T(8,128)S(1)}, u32[]{:S(2)}, u32[]{:S(2)}) collective-permute-start(f32[1,2,32,128]{3,2,1,0:T(8,128)S(1)} %get-tuple-element.36), channel_id=1, source_target_pairs={{0,8},{1,9},{2,10},{3,11},{4,12},{5,13},{6,14},{7,15},{8,0},{9,1},... | collective-permute-start | bytes 98312 | tf_op jit(solution)/shard_map/ppermute | solution.py:364
  30.0 2.3 %collective-permute-done.6.received = f32[1,2,32,128]{3,2,1,0:T(8,128)S(1)} collective-permute-done((f32[1,2,32,128]{3,2,1,0:T(8,128)S(1)}, f32[1,2,32,128]{3,2,1,0:T(8,128)S(1)}, u32[]{:S(2)}, u32[]{:S(2)}) %collective-permute-start.6) | collective-permute-done | bytes 32800 | tf_op jit(solution)/shard_map/ppermute | solution.py:364
  32.3 0.4 shard_map.52
  32.7 2.6 %collective-permute-start.7 = (f32[1,2,32,128]{3,2,1,0:T(8,128)S(1)}, f32[1,2,32,128]{3,2,1,0:T(8,128)S(1)}, u32[]{:S(2)}, u32[]{:S(2)}) collective-permute-start(f32[1,2,32,128]{3,2,1,0:T(8,128)S(1)} %get-tuple-element.40), channel_id=1, source_target_pairs={{0,8},{1,9},{2,10},{3,11},{4,12},{5,13},{6,14},{7,15},{8,0},{9,1},... | collective-permute-start | bytes 98312 | tf_op jit(solution)/shard_map/ppermute | solution.py:364
  35.3 2.3 %collective-permute-done.7.received = f32[1,2,32,128]{3,2,1,0:T(8,128)S(1)} collective-permute-done((f32[1,2,32,128]{3,2,1,0:T(8,128)S(1)}, f32[1,2,32,128]{3,2,1,0:T(8,128)S(1)}, u32[]{:S(2)}, u32[]{:S(2)}) %collective-permute-start.7) | collective-permute-done | bytes 32800 | tf_op jit(solution)/shard_map/ppermute | solution.py:364
  37.6 1.5 %collective-permute-start.8 = (f32[2,1,32,128]{3,2,1,0:T(8,128)S(1)}, f32[2,1,32,128]{3,2,1,0:T(8,128)S(1)}, u32[]{:S(2)}, u32[]{:S(2)}) collective-permute-start(f32[2,1,32,128]{3,2,1,0:T(8,128)S(1)} %get-tuple-element.42), channel_id=1, source_target_pairs={{0,4},{1,5},{2,6},{3,7},{4,0},{5,1},{6,2},{7,3},{8,12},{9,13},{10,... | collective-permute-start | bytes 98312 | tf_op jit(solution)/shard_map/ppermute | solution.py:364
  39.0 2.4 %collective-permute-done.8.received = f32[2,1,32,128]{3,2,1,0:T(8,128)S(1)} collective-permute-done((f32[2,1,32,128]{3,2,1,0:T(8,128)S(1)}, f32[2,1,32,128]{3,2,1,0:T(8,128)S(1)}, u32[]{:S(2)}, u32[]{:S(2)}) %collective-permute-start.8) | collective-permute-done | bytes 32800 | tf_op jit(solution)/shard_map/ppermute | solution.py:364
  41.5 0.0 collective-permute-start.11
  41.5 0.6 %collective-permute-start.10 = (f32[4,32,128]{2,1,0:T(8,128)S(1)}, f32[4,32,128]{2,1,0:T(8,128)S(1)}, u32[]{:S(2)}, u32[]{:S(2)}) collective-permute-start(f32[4,32,128]{2,1,0:T(8,128)S(1)} %shard_map.54.refs_0_), channel_id=1, source_target_pairs={{0,2},{1,3},{2,0},{3,1},{4,6},{5,7},{6,4},{7,5},{8,10},{9,11},{10,... | collective-permute-start | bytes 196616 | tf_op jit(solution)/shard_map/ppermute | solution.py:322
  42.1 1.2 %collective-permute-start.9 = (f32[4,32,128]{2,1,0:T(8,128)S(1)}, f32[4,32,128]{2,1,0:T(8,128)S(1)}, u32[]{:S(2)}, u32[]{:S(2)}) collective-permute-start(f32[4,32,128]{2,1,0:T(8,128)S(1)} %shard_map.54.refs_0_), channel_id=1, source_target_pairs={{0,1},{1,0},{2,3},{3,2},{4,5},{5,4},{6,7},{7,6},{8,9},{9,8},{10,11... | collective-permute-start | bytes 196616 | tf_op jit(solution)/shard_map/ppermute | solution.py:322
  43.4 2.5 %shard_map.55.refs_6_.before = f32[64,5120]{1,0:T(8,128)S(1)} custom-call(f32[64,8192]{1,0:T(8,128)} %probes.3, f32[256,128]{1,0:T(8,128)S(1)} %get-tuple-element.45.mean, s32[64,128]{1,0:T(8,128)S(1)} %get-tuple-element.32.mask_ids, f32[64,128]{1,0:T(8,128)S(1)} %get-tuple-element.46.weight), custom_call_target="tpu_custom_call" | custom-call | flops 671088640 | bytes 2621440 | tf_op jit(solution)/shard_map/pallas_call | solution.py:438
  45.9 0.0 collective-permute-done.11.refs_3_
  45.9 0.6 %collective-permute-done.10.refs_2_ = f32[4,32,128]{2,1,0:T(8,128)S(1)} collective-permute-done((f32[4,32,128]{2,1,0:T(8,128)S(1)}, f32[4,32,128]{2,1,0:T(8,128)S(1)}, u32[]{:S(2)}, u32[]{:S(2)}) %collective-permute-start.10) | collective-permute-done | bytes 65568 | tf_op jit(solution)/shard_map/ppermute | solution.py:322
  46.5 0.0 collective-permute-done.9.refs_1_
  46.5 0.5 shard_map.56
  47.0 1.5 %collective-permute-start.12 = (f32[2,1,32,128]{3,2,1,0:T(8,128)S(1)}, f32[2,1,32,128]{3,2,1,0:T(8,128)S(1)}, u32[]{:S(2)}, u32[]{:S(2)}) collective-permute-start(f32[2,1,32,128]{3,2,1,0:T(8,128)S(1)} %get-tuple-element.48), channel_id=1, source_target_pairs={{0,4},{1,5},{2,6},{3,7},{4,0},{5,1},{6,2},{7,3},{8,12},{9,13},{10,... | collective-permute-start | bytes 98312 | tf_op jit(solution)/shard_map/ppermute | solution.py:364
  48.5 2.4 %collective-permute-done.12.received = f32[2,1,32,128]{3,2,1,0:T(8,128)S(1)} collective-permute-done((f32[2,1,32,128]{3,2,1,0:T(8,128)S(1)}, f32[2,1,32,128]{3,2,1,0:T(8,128)S(1)}, u32[]{:S(2)}, u32[]{:S(2)}) %collective-permute-start.12) | collective-permute-done | bytes 32800 | tf_op jit(solution)/shard_map/ppermute | solution.py:364
  50.9 2.6 %collective-permute-start.13 = (f32[1,2,32,128]{3,2,1,0:T(8,128)S(1)}, f32[1,2,32,128]{3,2,1,0:T(8,128)S(1)}, u32[]{:S(2)}, u32[]{:S(2)}) collective-permute-start(f32[1,2,32,128]{3,2,1,0:T(8,128)S(1)} %get-tuple-element.50), channel_id=1, source_target_pairs={{0,8},{1,9},{2,10},{3,11},{4,12},{5,13},{6,14},{7,15},{8,0},{9,1},... | collective-permute-start | bytes 98312 | tf_op jit(solution)/shard_map/ppermute | solution.py:364
  53.6 1.9 %shard_map.58.after = f32[64,3072]{1,0:T(8,128)S(1)} custom-call(f32[64,8192]{1,0:T(8,128)} %probes.3, f32[256,128]{1,0:T(8,128)S(1)} %get-tuple-element.45.mean, s32[64,128]{1,0:T(8,128)S(1)} %get-tuple-element.32.mask_ids, f32[64,128]{1,0:T(8,128)S(1)} %get-tuple-element.46.weight), custom_call_target="tpu_custom_call" | custom-call | flops 402653184 | bytes 1572864 | tf_op jit(solution)/shard_map/pallas_call | solution.py:438
  55.5 0.3 collective-permute-done.13.received
  55.8 1.8 %shard_map.59 = f32[64,8192]{1,0:T(8,128)} custom-call(f32[1,2,32,128]{3,2,1,0:T(8,128)S(1)} %get-tuple-element.49.kept, f32[1,2,32,128]{3,2,1,0:T(8,128)S(1)} %collective-permute-done.13.received, f32[64,5120]{1,0:T(8,128)S(1)} %shard_map.55.refs_6_.before, f32[64,3072]{1,0:T(8,128)S(1)} %shard_map.58.after, s32[64,128]{1,0:T(8,128)S(1)} %get-tuple-element.32.mask_ids), custom_call_target="tpu_custom_call" | custom-call | flops 536870912 | bytes 4194304 | tf_op jit(solution)/shard_map/pallas_call | solution.py:459
  (6 shorter events, 0.0 us)
Async XLA Ops:
  0.0 17.7 %copy-start = (s32[1024]{0:T(1024)S(1)}, s32[1024]{0:T(1024)}, u32[]{:S(2)}) copy-start(s32[1024]{0:T(1024)} %param.5) | copy-start | bytes 12292
  5.2 6.5 %collective-permute-start = (f32[1,2,40,128]{3,2,1,0:T(8,128)S(1)}, f32[1,2,40,128]{3,2,1,0:T(8,128)S(1)}, u32[]{:S(2)}, u32[]{:S(2)}) collective-permute-start(f32[1,2,40,128]{3,2,1,0:T(8,128)S(1)} %get-tuple-element.29), channel_id=1, source_target_pairs={{0,8},{1,9},{2,10},{3,11},{4,12},{5,13},{6,14},{7,15},{8,0},{9,1},... | collective-permute-start | bytes 122888 | tf_op jit(solution)/shard_map/ppermute | solution.py:364
  11.8 4.0 %collective-permute-start.1 = (f32[2,1,40,128]{3,2,1,0:T(8,128)S(1)}, f32[2,1,40,128]{3,2,1,0:T(8,128)S(1)}, u32[]{:S(2)}, u32[]{:S(2)}) collective-permute-start(f32[2,1,40,128]{3,2,1,0:T(8,128)S(1)} %get-tuple-element.31), channel_id=1, source_target_pairs={{0,4},{1,5},{2,6},{3,7},{4,0},{5,1},{6,2},{7,3},{8,12},{9,13},{10,... | collective-permute-start | bytes 122888 | tf_op jit(solution)/shard_map/ppermute | solution.py:364
  15.8 4.5 %collective-permute-start.4 = (f32[4,40,128]{2,1,0:T(8,128)S(1)}, f32[4,40,128]{2,1,0:T(8,128)S(1)}, u32[]{:S(2)}, u32[]{:S(2)}) collective-permute-start(f32[4,40,128]{2,1,0:T(8,128)S(1)} %shard_map.48.refs_0_), channel_id=1, source_target_pairs={{0,3},{1,2},{2,1},{3,0},{4,7},{5,6},{6,5},{7,4},{8,11},{9,10},{10,... | collective-permute-start | bytes 245768 | tf_op jit(solution)/shard_map/ppermute | solution.py:322
  15.8 6.5 %collective-permute-start.3 = (f32[4,40,128]{2,1,0:T(8,128)S(1)}, f32[4,40,128]{2,1,0:T(8,128)S(1)}, u32[]{:S(2)}, u32[]{:S(2)}) collective-permute-start(f32[4,40,128]{2,1,0:T(8,128)S(1)} %shard_map.48.refs_0_), channel_id=1, source_target_pairs={{0,2},{1,3},{2,0},{3,1},{4,6},{5,7},{6,4},{7,5},{8,10},{9,11},{10,... | collective-permute-start | bytes 245768 | tf_op jit(solution)/shard_map/ppermute | solution.py:322
  17.6 4.7 %collective-permute-start.2 = (f32[4,40,128]{2,1,0:T(8,128)S(1)}, f32[4,40,128]{2,1,0:T(8,128)S(1)}, u32[]{:S(2)}, u32[]{:S(2)}) collective-permute-start(f32[4,40,128]{2,1,0:T(8,128)S(1)} %shard_map.48.refs_0_), channel_id=1, source_target_pairs={{0,1},{1,0},{2,3},{3,2},{4,5},{5,4},{6,7},{7,6},{8,9},{9,8},{10,11... | collective-permute-start | bytes 245768 | tf_op jit(solution)/shard_map/ppermute | solution.py:322
  23.5 4.0 %collective-permute-start.5 = (f32[2,1,32,128]{3,2,1,0:T(8,128)S(1)}, f32[2,1,32,128]{3,2,1,0:T(8,128)S(1)}, u32[]{:S(2)}, u32[]{:S(2)}) collective-permute-start(f32[2,1,32,128]{3,2,1,0:T(8,128)S(1)} %get-tuple-element.34), channel_id=1, source_target_pairs={{0,4},{1,5},{2,6},{3,7},{4,0},{5,1},{6,2},{7,3},{8,12},{9,13},{10,... | collective-permute-start | bytes 98312 | tf_op jit(solution)/shard_map/ppermute | solution.py:364
  27.5 4.8 %collective-permute-start.6 = (f32[1,2,32,128]{3,2,1,0:T(8,128)S(1)}, f32[1,2,32,128]{3,2,1,0:T(8,128)S(1)}, u32[]{:S(2)}, u32[]{:S(2)}) collective-permute-start(f32[1,2,32,128]{3,2,1,0:T(8,128)S(1)} %get-tuple-element.36), channel_id=1, source_target_pairs={{0,8},{1,9},{2,10},{3,11},{4,12},{5,13},{6,14},{7,15},{8,0},{9,1},... | collective-permute-start | bytes 98312 | tf_op jit(solution)/shard_map/ppermute | solution.py:364
  32.7 4.9 %collective-permute-start.7 = (f32[1,2,32,128]{3,2,1,0:T(8,128)S(1)}, f32[1,2,32,128]{3,2,1,0:T(8,128)S(1)}, u32[]{:S(2)}, u32[]{:S(2)}) collective-permute-start(f32[1,2,32,128]{3,2,1,0:T(8,128)S(1)} %get-tuple-element.40), channel_id=1, source_target_pairs={{0,8},{1,9},{2,10},{3,11},{4,12},{5,13},{6,14},{7,15},{8,0},{9,1},... | collective-permute-start | bytes 98312 | tf_op jit(solution)/shard_map/ppermute | solution.py:364
  37.6 3.9 %collective-permute-start.8 = (f32[2,1,32,128]{3,2,1,0:T(8,128)S(1)}, f32[2,1,32,128]{3,2,1,0:T(8,128)S(1)}, u32[]{:S(2)}, u32[]{:S(2)}) collective-permute-start(f32[2,1,32,128]{3,2,1,0:T(8,128)S(1)} %get-tuple-element.42), channel_id=1, source_target_pairs={{0,4},{1,5},{2,6},{3,7},{4,0},{5,1},{6,2},{7,3},{8,12},{9,13},{10,... | collective-permute-start | bytes 98312 | tf_op jit(solution)/shard_map/ppermute | solution.py:364
  41.5 4.4 %collective-permute-start.11 = (f32[4,32,128]{2,1,0:T(8,128)S(1)}, f32[4,32,128]{2,1,0:T(8,128)S(1)}, u32[]{:S(2)}, u32[]{:S(2)}) collective-permute-start(f32[4,32,128]{2,1,0:T(8,128)S(1)} %shard_map.54.refs_0_), channel_id=1, source_target_pairs={{0,3},{1,2},{2,1},{3,0},{4,7},{5,6},{6,5},{7,4},{8,11},{9,10},{10,... | collective-permute-start | bytes 196616 | tf_op jit(solution)/shard_map/ppermute | solution.py:322
  41.5 5.0 %collective-permute-start.10 = (f32[4,32,128]{2,1,0:T(8,128)S(1)}, f32[4,32,128]{2,1,0:T(8,128)S(1)}, u32[]{:S(2)}, u32[]{:S(2)}) collective-permute-start(f32[4,32,128]{2,1,0:T(8,128)S(1)} %shard_map.54.refs_0_), channel_id=1, source_target_pairs={{0,2},{1,3},{2,0},{3,1},{4,6},{5,7},{6,4},{7,5},{8,10},{9,11},{10,... | collective-permute-start | bytes 196616 | tf_op jit(solution)/shard_map/ppermute | solution.py:322
  42.1 4.3 %collective-permute-start.9 = (f32[4,32,128]{2,1,0:T(8,128)S(1)}, f32[4,32,128]{2,1,0:T(8,128)S(1)}, u32[]{:S(2)}, u32[]{:S(2)}) collective-permute-start(f32[4,32,128]{2,1,0:T(8,128)S(1)} %shard_map.54.refs_0_), channel_id=1, source_target_pairs={{0,1},{1,0},{2,3},{3,2},{4,5},{5,4},{6,7},{7,6},{8,9},{9,8},{10,11... | collective-permute-start | bytes 196616 | tf_op jit(solution)/shard_map/ppermute | solution.py:322
  47.0 4.0 %collective-permute-start.12 = (f32[2,1,32,128]{3,2,1,0:T(8,128)S(1)}, f32[2,1,32,128]{3,2,1,0:T(8,128)S(1)}, u32[]{:S(2)}, u32[]{:S(2)}) collective-permute-start(f32[2,1,32,128]{3,2,1,0:T(8,128)S(1)} %get-tuple-element.48), channel_id=1, source_target_pairs={{0,4},{1,5},{2,6},{3,7},{4,0},{5,1},{6,2},{7,3},{8,12},{9,13},{10,... | collective-permute-start | bytes 98312 | tf_op jit(solution)/shard_map/ppermute | solution.py:364
  50.9 4.8 %collective-permute-start.13 = (f32[1,2,32,128]{3,2,1,0:T(8,128)S(1)}, f32[1,2,32,128]{3,2,1,0:T(8,128)S(1)}, u32[]{:S(2)}, u32[]{:S(2)}) collective-permute-start(f32[1,2,32,128]{3,2,1,0:T(8,128)S(1)} %get-tuple-element.50), channel_id=1, source_target_pairs={{0,8},{1,9},{2,10},{3,11},{4,12},{5,13},{6,14},{7,15},{8,0},{9,1},... | collective-permute-start | bytes 98312 | tf_op jit(solution)/shard_map/ppermute | solution.py:364

commit v10 on v8

--- a/solution.py
+++ b/solution.py
@@ -118,10 +118,22 @@
     return [pltpu.make_async_copy(source.at[:, cut], target.at[:, cut], sems.at[b]) for b, cut in enumerate(cuts)]
 
 
+def row_lengths(lengths, pad):
+    total_rows = lengths.shape[0] * pad
+    here = iota((total_rows, LANES), 0)
+    lane = iota((total_rows, LANES), 1)
+    wide = jnp.broadcast_to(lengths.astype(F32)[:, None, :], (lengths.shape[0], pad, LANES)).reshape(total_rows, LANES)
+    per = LANES // pad
+    wide = jnp.where(lane // per == here % pad, wide, 0.0).astype(BF16)
+    spread = (iota((LANES, LANES), 0) % per == iota((LANES, LANES), 1) // pad).astype(F32).astype(BF16)
+    row_len = dot(wide, spread)
+    return row_len, (lane % pad).astype(F32) < row_len
+
+
 def sums_kernel(n, pad, *refs):
     far = n // NEAR
     (probes, lengths_in, ids_in, firms_in), sends = refs[:4], refs[4 : 4 + far]
-    own, own_count, mask_ids, weight, valid, x, acc, lengths, ids, firms, tiles, sems, small = refs[4 + far :]
+    mask_ids, weight, valid, x, acc, lengths, ids, firms, tiles, sems, small = refs[4 + far :]
     copies = column_copies(probes, x, sems)
     first = [
         pltpu.make_async_copy(source, target, small.at[k])
@@ -129,19 +141,9 @@
     ]
     start_all(first)
     start_all(copies)
-    slots = own.shape[0]
-    total_rows = ids.shape[0]
-    here = iota((total_rows, LANES), 0)
-    lane = iota((total_rows, LANES), 1)
+    slots = acc.shape[1]
     wait_all(first)
-    wide = jnp.broadcast_to(
-        lengths[...].astype(F32)[:, None, :], (lengths.shape[0], total_rows // lengths.shape[0], LANES)
-    ).reshape(total_rows, LANES)
-    per = LANES // pad
-    wide = jnp.where(lane // per == here % pad, wide, 0.0).astype(BF16)
-    spread = (iota((LANES, LANES), 0) % per == iota((LANES, LANES), 1) // pad).astype(F32).astype(BF16)
-    row_len = dot(wide, spread)
-    inside = (lane % pad).astype(F32) < row_len
+    row_len, inside = row_lengths(lengths[...], pad)
     valid[...] = jnp.where(inside, 1.0, 0.0)
     weight[...] = jnp.where(inside, 1.0 / row_len, 0.0)
     mask_ids[...] = jnp.where(inside, ids[...], -1)
@@ -163,9 +165,7 @@
     columns = x.shape[0]
     sums = acc[:columns] + acc[columns : 2 * columns]
     both = jnp.concatenate([sums, sums], axis=0).T
-    own[...] = both
     count = jnp.broadcast_to(acc[2 * columns : 2 * columns + 1], (LANES, slots)).T
-    own_count[...] = count
     tiles[:, : 8 * NEAR] = to_tiles(both, n).reshape(far, 8 * NEAR, LANES)
     about = jnp.where(iota((slots, LANES), 1) % 16 < 8, column(firms[...].astype(F32)), count)
     about = about.reshape(far, NEAR, 2, 8, LANES)
@@ -183,21 +183,38 @@
         refs[-1][k] = part[...]
 
 
-def worker_kernel(pad, lengths, mask_ids, out):
-    slots = out.shape[1]
-    workers = lengths.shape[0] * LANES
-    group = 256
-    rows_group = group * pad
-    pick = (iota((rows_group, group), 0) // pad == iota((rows_group, group), 1)).astype(F32).astype(BF16)
-    total = jnp.zeros((2 * slots, slots), F32)
-    for g in range(workers // group):
-        counts = dot(one_hot(row(mask_ids, g, rows_group), slots), pick)
-        inverse = 1.0 / row(lengths, g, group).astype(F32)
-        hi, lo = split(counts * inverse)
-        total += dot(jnp.concatenate([hi, lo], axis=0), counts.astype(BF16), NT)
-    hi, lo = split(total[:slots] + total[slots:])
-    out[:slots] = hi
-    out[slots:] = lo
+def pairs_kernel(pad, far, all_lengths, all_ids, out, counts):
+    me = lax.axis_index("rows") // NEAR
+    own, slots = out.shape[1] // 2, out.shape[2]
+    kind = BF16 if slots <= 256 else F32
+    per = LANES // pad
+    total_rows = all_ids.shape[1]
+    at = iota((LANES, pad * LANES), 1)
+    deal = (iota((LANES, pad * LANES), 0) == at % per * pad + at // LANES).astype(F32).astype(BF16)
+    mine = iota((total_rows, pad * LANES), 1) % LANES // per == iota((total_rows, pad * LANES), 0) % pad
+    slot = iota((slots, LANES), 0).astype(F32).astype(kind)
+    one, zero = jnp.ones((slots, LANES), kind), jnp.zeros((slots, LANES), kind)
+    diagonal = iota((own, slots), 1) == me * own + iota((own, slots), 0)
+    for k in range(far):
+        lengths = all_lengths[me ^ k]
+        _, inside = row_lengths(lengths, pad)
+        ids = jnp.where(inside, all_ids[me ^ k], -1).astype(F32)
+        dealt = dot(jnp.concatenate(split(ids), axis=0), deal)
+        dealt = jnp.where(mine, dealt[:total_rows] + dealt[total_rows:], 0.0)
+        spells = jnp.sum(dealt.reshape(total_rows // pad, pad, pad * LANES), axis=1).astype(kind)
+        for g in range(total_rows // pad):
+            total = zero
+            for j in range(pad):
+                total += jnp.where(slot == spells[g : g + 1, j * LANES : (j + 1) * LANES], one, zero)
+            counts[:, g * LANES : (g + 1) * LANES] = total.astype(BF16)
+        here = counts[pl.ds(pl.multiple_of(me * own, own), own), :].astype(F32)
+        inverse = 1.0 / lengths.astype(F32)
+        inverse = jnp.concatenate([inverse[g : g + 1] for g in range(total_rows // pad)], axis=1)
+        total = dot(jnp.concatenate(split(here * inverse), axis=0), counts[...], NT)
+        total = total[:own] + total[own:] - jnp.where(diagonal, jnp.sum(here, axis=1, keepdims=True), 0.0)
+        hi, lo = split(total)
+        out[k, :own] = hi
+        out[k, own:] = lo
 
 
 def owner_means(parts, table, scale):
@@ -209,8 +226,8 @@
 
 
 def owner_first_kernel(*refs):
-    parts, sends, (table, scale) = refs[:NEAR], refs[NEAR + 1 : -2], refs[-2:]
-    far = len(sends)
+    parts, (send, table, scale) = refs[:NEAR], refs[NEAR:]
+    far = send.shape[0]
 
     def sides(part, kind):
         about = part[:, 8 * NEAR :].reshape(8 * far, LANES)
@@ -236,9 +253,7 @@
         total += jnp.where(hit, count, 0.0)
     total = jnp.sum(total, axis=1, keepdims=True)
     scale[...] = jnp.broadcast_to(1.0 / jnp.maximum(total, 1.0), scale.shape)
-    means = owner_means([part[:, : 8 * NEAR] for part in parts], table[...], scale[...])
-    for k, send in enumerate(sends):
-        send[...] = means[k]
+    send[...] = owner_means([part[:, : 8 * NEAR] for part in parts], table[...], scale[...])
 
 
 def owner_second_kernel(*refs):
@@ -256,16 +271,18 @@
 
 
 def change_kernel(far, *refs):
-    parts, (own, own_count, pairs), sends, (mean, tiles) = (
-        refs[:far], refs[far : far + 3], refs[far + 3 : 2 * far + 3], refs[2 * far + 3 :]
-    )
-    slots = own.shape[0]
-    found = own_means(parts, tiles)
-    mean[...] = found
-    change = dot(pairs[...], halves(found).astype(BF16))
-    new = own[...] - own_count[...] * found + fold(change[:slots] + change[slots:])
-    tiles[...] = to_tiles(new, far * NEAR).reshape(tiles.shape)
-    place(tiles, sends)
+    parts, (sums, pairs, send, mean, tiles) = refs[:far], refs[far:]
+    me = lax.axis_index("rows") // NEAR
+    own = pairs.shape[1] // 2
+    for i in range(far):
+        for k, part in enumerate(parts):
+            tiles[i, me ^ k] = part[k ^ i]
+        found = from_tiles(tiles[i].reshape(far * NEAR, 8, LANES))
+        if i == 0:
+            mean[...] = found
+        change = dot(pairs[i], halves(found).astype(BF16))
+        change = to_tiles(fold(change[:own] + change[own:]), NEAR).reshape(8 * NEAR, LANES)
+        send[i] = sums[i, : 8 * NEAR] + change
 
 
 def take(parts, ids, slots):
@@ -300,6 +317,11 @@
         y[:, b * BLOCK : (b + 1) * BLOCK] = source[:, at * BLOCK : (at + 1) * BLOCK] - spread
         outs[b].start()
     wait_all(outs)
+
+
+def all_far(part, n):
+    steps = [[(i, i ^ (k * NEAR)) for i in range(n)] for k in range(1, part.shape[0])]
+    return [part] + [lax.ppermute(part, "rows", step) for step in steps]
 
 
 def exchange(parts, n):
@@ -349,11 +371,14 @@
     tiles = pltpu.VMEM((far, 8 * NEAR, LANES), F32)
     mine = 16 * NEAR * far
 
-    *sends, own, own_count, mask_ids, weight = call(
+    groups = [list(range(k, n, NEAR)) for k in range(NEAR)]
+    all_ids = lax.all_gather(ids, "rows", axis_index_groups=groups)
+    all_lengths = lax.all_gather(lengths, "rows", axis_index_groups=groups)
+    *sends, mask_ids, weight = call(
         functools.partial(sums_kernel, n, pad),
-        [tile_about] * far + [of_slots, of_slots, array(of_rows, jnp.int32), array(of_rows, F32)],
+        [tile_about] * far + [array(of_rows, jnp.int32), array(of_rows, F32)],
         [hbm] * 4,
-        [vmem] * (far + 4),
+        [vmem] * (far + 2),
         [
             pltpu.VMEM(of_rows, F32),
             whole,
@@ -374,35 +399,35 @@
         return call(join_kernel, shape, [vmem] * far, vmem, [], 0, shape.size * 8)(*parts)
 
     received = share(join(exchange(sends, n)), n)
-    pairs = call(
-        functools.partial(worker_kernel, pad),
-        array((2 * slots, slots), BF16),
-        [vmem, vmem],
-        vmem,
-        [],
-        2 * work,
-        4 * slots * slots,
-    )(lengths, mask_ids)
-    *sends, table, scale = call(
+    means, table, scale = call(
         owner_first_kernel,
-        [tile] * far + [array((mine, NEAR * mine), BF16), array((mine, LANES), F32)],
-        [vmem] * (NEAR + 1),
-        [vmem] * (far + 2),
+        [array((far, *tile.shape), F32), array((mine, NEAR * mine), BF16), array((mine, LANES), F32)],
+        [vmem] * NEAR,
+        [vmem] * 3,
         [],
         work // 16,
         slots * slots * 4,
-    )(*received, pairs)
-    received = exchange(sends, n)
-    *sends, mean = call(
+    )(*received)
+    own = 16 * NEAR
+    pairs = call(
+        functools.partial(pairs_kernel, pad, far),
+        array((far, 2 * own, slots), BF16),
+        [vmem] * 2,
+        vmem,
+        [pltpu.VMEM((slots, workers), BF16)],
+        work,
+        4 * slots * slots,
+    )(all_lengths, all_ids)
+    sums, mean = call(
         functools.partial(change_kernel, far),
-        [tile] * far + [of_slots],
-        [vmem] * (far + 3),
-        [vmem] * (far + 1),
-        [tiles],
+        [array((far, *tile.shape), F32), of_slots],
+        [vmem] * (far + 2),
+        [vmem] * 2,
+        [pltpu.VMEM((far, far, *tile.shape), F32)],
         work // 16,
         slots * slots * 4,
-    )(*received, own, own_count, pairs)
-    received = share(join(exchange(sends, n)), n)
+    )(*all_far(means, n), received[0], pairs)
+    received = share(sums, n)
 
     def first(start, stop):
         width = (stop - start) * BLOCK

time: 54.6 us -> 73.4 us (1.34)
  blocking collectives: 0 us -> 26.6 us
  waiting for transfers between devices: 15.5 us -> 10.8 us
  starting transfers between devices: 22.7 us -> 18.4 us
  Pallas kernels: 16 us -> 17.3 us
    all_gather x0 -> x2, blocking collectives: none -> 26.6 us  [the longest x1 13.5 us: body(): all_ids = lax.all_gather(ids, 'rows', axis_index_groups=groups)]
    ppermute x12 -> x6, starting transfers between devices: 19 us -> 10.1 us  [exchange(): lax.ppermute(part, 'rows', step)]
    ppermute x12 -> x6, waiting for transfers between devices: 12.8 us -> 5.58 us  [exchange(): lax.ppermute(part, 'rows', step)]
    ppermute x0 -> x3, starting transfers between devices: none -> 4.45 us  [all_far(): return [part] + [lax.ppermute(part, 'rows', step) for step in steps]]
    ppermute x6, waiting for transfers between devices: 2.69 us -> 5.25 us  [share(): lax.ppermute(part, 'rows', [(i, i ^ k) for i in range(n)])]
    pallas_call x4, Pallas kernels: 9.4 us -> 10.7 us  [the longest x1 5.36 us: body(): call(functools.partial(sums_kernel, n, pad), [tile_about] * far + [array(...]
  transfers between devices with their start and end apart: 18 -> 15, of which waited for: 9 -> 5; matrix products, arithmetic and copies ran while one was open for 0% -> 0% of each run, Pallas kernels for 13% -> 11%
where the time goes in v10:
time: 73.4 us; the launch traced here: 73.2 us
  blocking collectives  26.6 us (36%)
  starting transfers between devices  18.4 us (25%)
  Pallas kernels  17.3 us (24%)
  waiting for transfers between devices  10.8 us (15%)
    all_gather x1, blocking collectives, body(): all_ids = lax.all_gather(ids, 'rows', axis_index_groups=groups)  13.5 us
    all_gather x1, blocking collectives, body(): all_lengths = lax.all_gather(lengths, 'rows', axis_index_groups=groups)  13.1 us
    ppermute x6, starting transfers between devices, exchange(): lax.ppermute(part, 'rows', step)  10.1 us
    ppermute x6, waiting for transfers between devices, exchange(): lax.ppermute(part, 'rows', step)  5.58 us
    pallas_call x1, Pallas kernels, body(): call(functools.partial(sums_kernel, n, pad), [tile_about] * far + [array(...  5.36 us
    ppermute x6, waiting for transfers between devices, share(): lax.ppermute(part, 'rows', [(i, i ^ k) for i in range(n)])  5.25 us
    ppermute x3, starting transfers between devices, all_far(): return [part] + [lax.ppermute(part, 'rows', step) for step in steps]  4.45 us
    pallas_call x2, Pallas kernels, first(): call(functools.partial(first_kernel, pad, start), array((columns, width),...  4.4 us
  transfers between devices with their start and end apart: 15, of which 5 were waited for; matrix products, arithmetic and copies ran while one was open for 0% of the time, Pallas kernels for 11%

profile of v10, /device:TPU:0, one launch (start us, length us, event | category | flops | bytes accessed | tf_op | source)
XLA Modules:
  0.0 73.2 jit_solution(17730936853156015574)
XLA Ops:
  0.0 0.0 copy-start
  0.0 0.0 copy-start.1
  0.0 5.4 %shard_map.46 = (f32[40,128]{1,0:T(8,128)S(1)}, f32[40,128]{1,0:T(8,128)S(1)}, f32[40,128]{1,0:T(8,128)S(1)}, f32[40,128]{1,0:T(8,128)S(1)}, s32[64,128]{1,0:T(8,128)S(1)}, /*index=5*/f32[64,128]{1,0:T(8,128)S(1)}) custom-call(f32[64,8192]{1,0:T(8,128)} %probes.3, s32[8,128]{1,0:T(8,128)} %bitcast.7, s32[64,128]{1,0:T(8,128)} %bitcast.5, s32[2,128]{1,0:T(2,128)} %bitcast.9), custom_call_target="tpu_custom_call" | custom-call | flops 1073741824 | bytes 2097152 | tf_op jit(solution)/shard_map/pallas_call | solution.py:377
  5.4 3.1 %collective-permute-start = (f32[40,128]{1,0:T(8,128)S(1)}, f32[40,128]{1,0:T(8,128)S(1)}, u32[]{:S(2)}, u32[]{:S(2)}) collective-permute-start(f32[40,128]{1,0:T(8,128)S(1)} %get-tuple-element.21), channel_id=1, source_target_pairs={{0,4},{1,5},{2,6},{3,7},{4,0},{5,1},{6,2},{7,3},{8,12},{9,13},{10,... | collective-permute-start | bytes 61448 | tf_op jit(solution)/shard_map/ppermute | solution.py:329
  8.5 2.6 %collective-permute-start.1 = (f32[40,128]{1,0:T(8,128)S(1)}, f32[40,128]{1,0:T(8,128)S(1)}, u32[]{:S(2)}, u32[]{:S(2)}) collective-permute-start(f32[40,128]{1,0:T(8,128)S(1)} %get-tuple-element.22), channel_id=1, source_target_pairs={{0,8},{1,9},{2,10},{3,11},{4,12},{5,13},{6,14},{7,15},{8,0},{9,1},... | collective-permute-start | bytes 61448 | tf_op jit(solution)/shard_map/ppermute | solution.py:329
  11.1 0.0 collective-permute-start.2
  11.1 0.0 collective-permute-done.refs_1_
  11.1 2.3 %collective-permute-done.1.refs_2_ = f32[40,128]{1,0:T(8,128)S(1)} collective-permute-done((f32[40,128]{1,0:T(8,128)S(1)}, f32[40,128]{1,0:T(8,128)S(1)}, u32[]{:S(2)}, u32[]{:S(2)}) %collective-permute-start.1) | collective-permute-done | bytes 20512 | tf_op jit(solution)/shard_map/ppermute | solution.py:329
  13.4 3.3 %collective-permute-done.2.refs_3_ = f32[40,128]{1,0:T(8,128)S(1)} collective-permute-done((f32[40,128]{1,0:T(8,128)S(1)}, f32[40,128]{1,0:T(8,128)S(1)}, u32[]{:S(2)}, u32[]{:S(2)}) %collective-permute-start.2) | collective-permute-done | bytes 20512 | tf_op jit(solution)/shard_map/ppermute | solution.py:329
  16.6 0.0 collective-permute-start.5
  16.6 1.6 %collective-permute-start.4 = (f32[4,40,128]{2,1,0:T(8,128)S(1)}, f32[4,40,128]{2,1,0:T(8,128)S(1)}, u32[]{:S(2)}, u32[]{:S(2)}) collective-permute-start(f32[4,40,128]{2,1,0:T(8,128)S(1)} %shard_map.47.refs_0_.refs_4_), channel_id=1, source_target_pairs={{0,2},{1,3},{2,0},{3,1},{4,6},{5,7},{6,4},{7,5},{8,10},{9,11},{10,... | collective-permute-start | bytes 245768 | tf_op jit(solution)/shard_map/ppermute | solution.py:333
  18.2 0.3 collective-permute-start.3
  18.5 2.8 %collective-permute-done.5.refs_3_ = f32[4,40,128]{2,1,0:T(8,128)S(1)} collective-permute-done((f32[4,40,128]{2,1,0:T(8,128)S(1)}, f32[4,40,128]{2,1,0:T(8,128)S(1)}, u32[]{:S(2)}, u32[]{:S(2)}) %collective-permute-start.5) | collective-permute-done | bytes 81952 | tf_op jit(solution)/shard_map/ppermute | solution.py:333
  21.3 1.8 %collective-permute-done.4.refs_2_ = f32[4,40,128]{2,1,0:T(8,128)S(1)} collective-permute-done((f32[4,40,128]{2,1,0:T(8,128)S(1)}, f32[4,40,128]{2,1,0:T(8,128)S(1)}, u32[]{:S(2)}, u32[]{:S(2)}) %collective-permute-start.4) | collective-permute-done | bytes 81952 | tf_op jit(solution)/shard_map/ppermute | solution.py:333
  23.1 0.0 collective-permute-done.3.refs_1_
  23.1 1.2 %shard_map.48 = (f32[4,32,128]{2,1,0:T(8,128)S(1)}, bf16[256,1024]{1,0:T(8,128)(2,1)S(1)}, f32[256,128]{1,0:T(8,128)S(1)}) custom-call(f32[4,40,128]{2,1,0:T(8,128)S(1)} %shard_map.47.refs_0_.refs_4_, f32[4,40,128]{2,1,0:T(8,128)S(1)} %collective-permute-done.3.refs_1_, f32[4,40,128]{2,1,0:T(8,128)S(1)} %collective-permute-done.4.refs_2_, ...), custom_call_target="tpu_custom_call" | custom-call | flops 33554432 | bytes 262144 | tf_op jit(solution)/shard_map/pallas_call | solution.py:402
  24.4 0.3 collective-permute-start.8
  24.7 0.0 collective-permute-start.7
  24.7 4.2 %collective-permute-start.6 = (f32[4,32,128]{2,1,0:T(8,128)S(1)}, f32[4,32,128]{2,1,0:T(8,128)S(1)}, u32[]{:S(2)}, u32[]{:S(2)}) collective-permute-start(f32[4,32,128]{2,1,0:T(8,128)S(1)} %get-tuple-element.24.refs_0_), channel_id=1, source_target_pairs={{0,4},{1,5},{2,6},{3,7},{4,0},{5,1},{6,2},{7,3},{8,12},{9,13},{10,... | collective-permute-start | bytes 196616 | tf_op jit(solution)/shard_map/ppermute | solution.py:324
  28.8 0.0 copy-done
  28.8 13.5 %all_gather.7.all_ids = s32[4,64,128]{2,1,0:T(8,128)S(1)} all-gather(s32[1,64,128]{2,1,0:T(8,128)S(1)} %bitcast.6), channel_id=1, replica_groups={{0,4,8,12},{1,5,9,13},{2,6,10,14},{3,7,11,15},{16,20,24,28},{17,21,25,2..., dimensions={0}, use_global_device_ids=true | all-gather | bytes 163840 | tf_op jit(solution)/shard_map/all_gather | solution.py:375
  42.3 0.0 copy-done.1
  42.3 13.1 %all_gather.6.all_lengths = s32[4,8,128]{2,1,0:T(8,128)S(1)} all-gather(s32[1,8,128]{2,1,0:T(8,128)S(1)} %bitcast.8), channel_id=1, replica_groups={{0,4,8,12},{1,5,9,13},{2,6,10,14},{3,7,11,15},{16,20,24,28},{17,21,25,2..., dimensions={0}, use_global_device_ids=true | all-gather | bytes 20480 | tf_op jit(solution)/shard_map/all_gather | solution.py:376
  55.4 3.6 %shard_map.49.refs_5_ = bf16[4,128,256]{2,1,0:T(8,128)(2,1)S(1)} custom-call(s32[4,8,128]{2,1,0:T(8,128)S(1)} %all_gather.6.all_lengths, s32[4,64,128]{2,1,0:T(8,128)S(1)} %all_gather.7.all_ids), custom_call_target="tpu_custom_call" | custom-call | flops 536870912 | bytes 262144 | tf_op jit(solution)/shard_map/pallas_call | solution.py:412
  59.1 0.0 collective-permute-done.8.refs_3_
  59.1 0.0 collective-permute-done.7.refs_2_
  59.1 0.0 collective-permute-done.6.refs_1_
  59.1 0.4 shard_map.50
  59.6 0.1 collective-permute-start.11
  59.6 0.4 collective-permute-start.10
  60.1 1.4 %collective-permute-start.9 = (f32[4,32,128]{2,1,0:T(8,128)S(1)}, f32[4,32,128]{2,1,0:T(8,128)S(1)}, u32[]{:S(2)}, u32[]{:S(2)}) collective-permute-start(f32[4,32,128]{2,1,0:T(8,128)S(1)} %get-tuple-element.25.refs_0_), channel_id=1, source_target_pairs={{0,1},{1,0},{2,3},{3,2},{4,5},{5,4},{6,7},{7,6},{8,9},{9,8},{10,11... | collective-permute-start | bytes 196616 | tf_op jit(solution)/shard_map/ppermute | solution.py:333
  61.5 2.5 %shard_map.51.refs_6_.refs_4_ = f32[64,5120]{1,0:T(8,128)S(1)} custom-call(f32[64,8192]{1,0:T(8,128)} %probes.3, f32[256,128]{1,0:T(8,128)S(1)} %get-tuple-element.28.mean, s32[64,128]{1,0:T(8,128)S(1)} %get-tuple-element.29.mask_ids.refs_6_, f32[64,128]{1,0:T(8,128)S(1)} %get-tuple-element.30.weight), custom_call_target="tpu_custom_call" | custom-call | flops 671088640 | bytes 2621440 | tf_op jit(solution)/shard_map/pallas_call | solution.py:434
  64.0 0.0 collective-permute-done.11.refs_3_
  64.0 0.6 collective-permute-done.10.refs_2_
  64.6 0.0 collective-permute-done.9.refs_1_
  64.6 0.5 shard_map.52
  65.1 0.1 collective-permute-start.12
  65.2 0.7 collective-permute-start.13
  65.9 3.7 %collective-permute-start.14 = (f32[32,128]{1,0:T(8,128)S(1)}, f32[32,128]{1,0:T(8,128)S(1)}, u32[]{:S(2)}, u32[]{:S(2)}) collective-permute-start(f32[32,128]{1,0:T(8,128)S(1)} %get-tuple-element.34), channel_id=1, source_target_pairs={{0,12},{1,13},{2,14},{3,15},{4,8},{5,9},{6,10},{7,11},{8,4},{9,5},... | collective-permute-start | bytes 49160 | tf_op jit(solution)/shard_map/ppermute | solution.py:329
  69.5 1.9 %shard_map.53.refs_5_ = f32[64,3072]{1,0:T(8,128)S(1)} custom-call(f32[64,8192]{1,0:T(8,128)} %probes.3, f32[256,128]{1,0:T(8,128)S(1)} %get-tuple-element.28.mean, s32[64,128]{1,0:T(8,128)S(1)} %get-tuple-element.29.mask_ids.refs_6_, f32[64,128]{1,0:T(8,128)S(1)} %get-tuple-element.30.weight), custom_call_target="tpu_custom_call" | custom-call | flops 402653184 | bytes 1572864 | tf_op jit(solution)/shard_map/pallas_call | solution.py:434
  71.4 0.0 collective-permute-done.12.refs_1_
  71.5 0.0 collective-permute-done.13.refs_2_
  71.5 0.0 collective-permute-done.14.refs_3_
  71.5 1.8 %shard_map.54 = f32[64,8192]{1,0:T(8,128)} custom-call(f32[32,128]{1,0:T(8,128)S(1)} %get-tuple-element.31.refs_0_, f32[32,128]{1,0:T(8,128)S(1)} %collective-permute-done.12.refs_1_, f32[32,128]{1,0:T(8,128)S(1)} %collective-permute-done.13.refs_2_, f32[32,128]{1,0:T(8,128)S(1)} %collective-permute-done.14.refs_3_, ...), custom_call_target="tpu_custom_call" | custom-call | flops 536870912 | bytes 4194304 | tf_op jit(solution)/shard_map/pallas_call | solution.py:455
  (1 shorter events, 0.0 us)
Async XLA Ops:
  0.0 28.8 %copy-start = (s32[8192]{0:T(1024)S(1)}, s32[8192]{0:T(1024)}, u32[]{:S(2)}) copy-start(s32[8192]{0:T(1024)} %param.6) | copy-start | bytes 98308
  0.0 42.3 %copy-start.1 = (s32[1024]{0:T(1024)S(1)}, s32[1024]{0:T(1024)}, u32[]{:S(2)}) copy-start(s32[1024]{0:T(1024)} %param.5) | copy-start | bytes 12292
  5.4 5.7 %collective-permute-start = (f32[40,128]{1,0:T(8,128)S(1)}, f32[40,128]{1,0:T(8,128)S(1)}, u32[]{:S(2)}, u32[]{:S(2)}) collective-permute-start(f32[40,128]{1,0:T(8,128)S(1)} %get-tuple-element.21), channel_id=1, source_target_pairs={{0,4},{1,5},{2,6},{3,7},{4,0},{5,1},{6,2},{7,3},{8,12},{9,13},{10,... | collective-permute-start | bytes 61448 | tf_op jit(solution)/shard_map/ppermute | solution.py:329
  8.5 4.9 %collective-permute-start.1 = (f32[40,128]{1,0:T(8,128)S(1)}, f32[40,128]{1,0:T(8,128)S(1)}, u32[]{:S(2)}, u32[]{:S(2)}) collective-permute-start(f32[40,128]{1,0:T(8,128)S(1)} %get-tuple-element.22), channel_id=1, source_target_pairs={{0,8},{1,9},{2,10},{3,11},{4,12},{5,13},{6,14},{7,15},{8,0},{9,1},... | collective-permute-start | bytes 61448 | tf_op jit(solution)/shard_map/ppermute | solution.py:329
  11.1 5.6 %collective-permute-start.2 = (f32[40,128]{1,0:T(8,128)S(1)}, f32[40,128]{1,0:T(8,128)S(1)}, u32[]{:S(2)}, u32[]{:S(2)}) collective-permute-start(f32[40,128]{1,0:T(8,128)S(1)} %get-tuple-element.23), channel_id=1, source_target_pairs={{0,12},{1,13},{2,14},{3,15},{4,8},{5,9},{6,10},{7,11},{8,4},{9,5},... | collective-permute-start | bytes 61448 | tf_op jit(solution)/shard_map/ppermute | solution.py:329
  16.6 4.7 %collective-permute-start.5 = (f32[4,40,128]{2,1,0:T(8,128)S(1)}, f32[4,40,128]{2,1,0:T(8,128)S(1)}, u32[]{:S(2)}, u32[]{:S(2)}) collective-permute-start(f32[4,40,128]{2,1,0:T(8,128)S(1)} %shard_map.47.refs_0_.refs_4_), channel_id=1, source_target_pairs={{0,3},{1,2},{2,1},{3,0},{4,7},{5,6},{6,5},{7,4},{8,11},{9,10},{10,... | collective-permute-start | bytes 245768 | tf_op jit(solution)/shard_map/ppermute | solution.py:333
  16.6 6.5 %collective-permute-start.4 = (f32[4,40,128]{2,1,0:T(8,128)S(1)}, f32[4,40,128]{2,1,0:T(8,128)S(1)}, u32[]{:S(2)}, u32[]{:S(2)}) collective-permute-start(f32[4,40,128]{2,1,0:T(8,128)S(1)} %shard_map.47.refs_0_.refs_4_), channel_id=1, source_target_pairs={{0,2},{1,3},{2,0},{3,1},{4,6},{5,7},{6,4},{7,5},{8,10},{9,11},{10,... | collective-permute-start | bytes 245768 | tf_op jit(solution)/shard_map/ppermute | solution.py:333
  18.2 4.9 %collective-permute-start.3 = (f32[4,40,128]{2,1,0:T(8,128)S(1)}, f32[4,40,128]{2,1,0:T(8,128)S(1)}, u32[]{:S(2)}, u32[]{:S(2)}) collective-permute-start(f32[4,40,128]{2,1,0:T(8,128)S(1)} %shard_map.47.refs_0_.refs_4_), channel_id=1, source_target_pairs={{0,1},{1,0},{2,3},{3,2},{4,5},{5,4},{6,7},{7,6},{8,9},{9,8},{10,11... | collective-permute-start | bytes 245768 | tf_op jit(solution)/shard_map/ppermute | solution.py:333
  24.4 34.7 %collective-permute-start.8 = (f32[4,32,128]{2,1,0:T(8,128)S(1)}, f32[4,32,128]{2,1,0:T(8,128)S(1)}, u32[]{:S(2)}, u32[]{:S(2)}) collective-permute-start(f32[4,32,128]{2,1,0:T(8,128)S(1)} %get-tuple-element.24.refs_0_), channel_id=1, source_target_pairs={{0,12},{1,13},{2,14},{3,15},{4,8},{5,9},{6,10},{7,11},{8,4},{9,5},... | collective-permute-start | bytes 196616 | tf_op jit(solution)/shard_map/ppermute | solution.py:324
  24.7 34.4 %collective-permute-start.7 = (f32[4,32,128]{2,1,0:T(8,128)S(1)}, f32[4,32,128]{2,1,0:T(8,128)S(1)}, u32[]{:S(2)}, u32[]{:S(2)}) collective-permute-start(f32[4,32,128]{2,1,0:T(8,128)S(1)} %get-tuple-element.24.refs_0_), channel_id=1, source_target_pairs={{0,8},{1,9},{2,10},{3,11},{4,12},{5,13},{6,14},{7,15},{8,0},{9,1},... | collective-permute-start | bytes 196616 | tf_op jit(solution)/shard_map/ppermute | solution.py:324
  24.7 34.5 %collective-permute-start.6 = (f32[4,32,128]{2,1,0:T(8,128)S(1)}, f32[4,32,128]{2,1,0:T(8,128)S(1)}, u32[]{:S(2)}, u32[]{:S(2)}) collective-permute-start(f32[4,32,128]{2,1,0:T(8,128)S(1)} %get-tuple-element.24.refs_0_), channel_id=1, source_target_pairs={{0,4},{1,5},{2,6},{3,7},{4,0},{5,1},{6,2},{7,3},{8,12},{9,13},{10,... | collective-permute-start | bytes 196616 | tf_op jit(solution)/shard_map/ppermute | solution.py:324
  59.6 4.4 %collective-permute-start.11 = (f32[4,32,128]{2,1,0:T(8,128)S(1)}, f32[4,32,128]{2,1,0:T(8,128)S(1)}, u32[]{:S(2)}, u32[]{:S(2)}) collective-permute-start(f32[4,32,128]{2,1,0:T(8,128)S(1)} %get-tuple-element.25.refs_0_), channel_id=1, source_target_pairs={{0,3},{1,2},{2,1},{3,0},{4,7},{5,6},{6,5},{7,4},{8,11},{9,10},{10,... | collective-permute-start | bytes 196616 | tf_op jit(solution)/shard_map/ppermute | solution.py:333
  59.6 5.0 %collective-permute-start.10 = (f32[4,32,128]{2,1,0:T(8,128)S(1)}, f32[4,32,128]{2,1,0:T(8,128)S(1)}, u32[]{:S(2)}, u32[]{:S(2)}) collective-permute-start(f32[4,32,128]{2,1,0:T(8,128)S(1)} %get-tuple-element.25.refs_0_), channel_id=1, source_target_pairs={{0,2},{1,3},{2,0},{3,1},{4,6},{5,7},{6,4},{7,5},{8,10},{9,11},{10,... | collective-permute-start | bytes 196616 | tf_op jit(solution)/shard_map/ppermute | solution.py:333
  60.1 4.5 %collective-permute-start.9 = (f32[4,32,128]{2,1,0:T(8,128)S(1)}, f32[4,32,128]{2,1,0:T(8,128)S(1)}, u32[]{:S(2)}, u32[]{:S(2)}) collective-permute-start(f32[4,32,128]{2,1,0:T(8,128)S(1)} %get-tuple-element.25.refs_0_), channel_id=1, source_target_pairs={{0,1},{1,0},{2,3},{3,2},{4,5},{5,4},{6,7},{7,6},{8,9},{9,8},{10,11... | collective-permute-start | bytes 196616 | tf_op jit(solution)/shard_map/ppermute | solution.py:333
  65.1 6.4 %collective-permute-start.12 = (f32[32,128]{1,0:T(8,128)S(1)}, f32[32,128]{1,0:T(8,128)S(1)}, u32[]{:S(2)}, u32[]{:S(2)}) collective-permute-start(f32[32,128]{1,0:T(8,128)S(1)} %get-tuple-element.32), channel_id=1, source_target_pairs={{0,4},{1,5},{2,6},{3,7},{4,0},{5,1},{6,2},{7,3},{8,12},{9,13},{10,... | collective-permute-start | bytes 49160 | tf_op jit(solution)/shard_map/ppermute | solution.py:329
  65.2 6.3 %collective-permute-start.13 = (f32[32,128]{1,0:T(8,128)S(1)}, f32[32,128]{1,0:T(8,128)S(1)}, u32[]{:S(2)}, u32[]{:S(2)}) collective-permute-start(f32[32,128]{1,0:T(8,128)S(1)} %get-tuple-element.33), channel_id=1, source_target_pairs={{0,8},{1,9},{2,10},{3,11},{4,12},{5,13},{6,14},{7,15},{8,0},{9,1},... | collective-permute-start | bytes 49160 | tf_op jit(solution)/shard_map/ppermute | solution.py:329
  65.9 5.6 %collective-permute-start.14 = (f32[32,128]{1,0:T(8,128)S(1)}, f32[32,128]{1,0:T(8,128)S(1)}, u32[]{:S(2)}, u32[]{:S(2)}) collective-permute-start(f32[32,128]{1,0:T(8,128)S(1)} %get-tuple-element.34), channel_id=1, source_target_pairs={{0,12},{1,13},{2,14},{3,15},{4,8},{5,9},{6,10},{7,11},{8,4},{9,5},... | collective-permute-start | bytes 49160 | tf_op jit(solution)/shard_map/ppermute | solution.py:329

commit v11 on v10

--- a/solution.py
+++ b/solution.py
@@ -109,7 +109,7 @@
 def place(tiles, sends):
     me = lax.axis_index("rows") // NEAR
     for k, send in enumerate(sends):
-        send[...] = tiles[me ^ k]
+        send[: tiles.shape[1]] = tiles[me ^ k]
 
 
 def column_copies(source, target, sems):
@@ -147,6 +147,8 @@
     valid[...] = jnp.where(inside, 1.0, 0.0)
     weight[...] = jnp.where(inside, 1.0 / row_len, 0.0)
     mask_ids[...] = jnp.where(inside, ids[...], -1)
+    for send in sends:
+        send[tiles.shape[1] :] = mask_ids[...].astype(F32)
 
     table = same_worker(pad, 256)
     for b in range(len(copies)):
@@ -180,41 +182,50 @@
 
 def join_kernel(*refs):
     for k, part in enumerate(refs[:-1]):
-        refs[-1][k] = part[...]
-
-
-def pairs_kernel(pad, far, all_lengths, all_ids, out, counts):
+        refs[-1][k] = part[: refs[-1].shape[1]]
+
+
+def pairs_kernel(pad, *refs):
+    parts, (out, ids, counts) = refs[:-3], refs[-3:]
     me = lax.axis_index("rows") // NEAR
-    own, slots = out.shape[1] // 2, out.shape[2]
+    far, own, slots = len(parts), out.shape[1] // 2, out.shape[2]
     kind = BF16 if slots <= 256 else F32
     per = LANES // pad
-    total_rows = all_ids.shape[1]
+    total_rows = ids.shape[1]
+    for k, part in enumerate(parts):
+        ids[k] = part[part.shape[0] - total_rows :]
     at = iota((LANES, pad * LANES), 1)
     deal = (iota((LANES, pad * LANES), 0) == at % per * pad + at // LANES).astype(F32).astype(BF16)
     mine = iota((total_rows, pad * LANES), 1) % LANES // per == iota((total_rows, pad * LANES), 0) % pad
     slot = iota((slots, LANES), 0).astype(F32).astype(kind)
     one, zero = jnp.ones((slots, LANES), kind), jnp.zeros((slots, LANES), kind)
     diagonal = iota((own, slots), 1) == me * own + iota((own, slots), 0)
-    for k in range(far):
-        lengths = all_lengths[me ^ k]
-        _, inside = row_lengths(lengths, pad)
-        ids = jnp.where(inside, all_ids[me ^ k], -1).astype(F32)
-        dealt = dot(jnp.concatenate(split(ids), axis=0), deal)
+
+    def device(k, carry):
+        dealt = dot(jnp.concatenate(split(ids[k]), axis=0), deal)
         dealt = jnp.where(mine, dealt[:total_rows] + dealt[total_rows:], 0.0)
-        spells = jnp.sum(dealt.reshape(total_rows // pad, pad, pad * LANES), axis=1).astype(kind)
+        dealt = jnp.sum(dealt.reshape(total_rows // pad, pad, pad * LANES), axis=1)
+        spells = dealt.astype(kind)
         for g in range(total_rows // pad):
             total = zero
             for j in range(pad):
                 total += jnp.where(slot == spells[g : g + 1, j * LANES : (j + 1) * LANES], one, zero)
             counts[:, g * LANES : (g + 1) * LANES] = total.astype(BF16)
+        valid = jnp.where(dealt >= 0.0, 1.0, 0.0)
+        length = valid[:, :LANES]
+        for j in range(1, pad):
+            length += valid[:, j * LANES : (j + 1) * LANES]
+        inverse = 1.0 / length
+        inverse = jnp.concatenate([inverse[g : g + 1] for g in range(total_rows // pad)], axis=1)
         here = counts[pl.ds(pl.multiple_of(me * own, own), own), :].astype(F32)
-        inverse = 1.0 / lengths.astype(F32)
-        inverse = jnp.concatenate([inverse[g : g + 1] for g in range(total_rows // pad)], axis=1)
         total = dot(jnp.concatenate(split(here * inverse), axis=0), counts[...], NT)
         total = total[:own] + total[own:] - jnp.where(diagonal, jnp.sum(here, axis=1, keepdims=True), 0.0)
         hi, lo = split(total)
         out[k, :own] = hi
         out[k, own:] = lo
+        return carry
+
+    lax.fori_loop(0, far, device, 0, unroll=far if far <= 4 else 1)
 
 
 def owner_means(parts, table, scale):
@@ -371,12 +382,10 @@
     tiles = pltpu.VMEM((far, 8 * NEAR, LANES), F32)
     mine = 16 * NEAR * far
 
-    groups = [list(range(k, n, NEAR)) for k in range(NEAR)]
-    all_ids = lax.all_gather(ids, "rows", axis_index_groups=groups)
-    all_lengths = lax.all_gather(lengths, "rows", axis_index_groups=groups)
     *sends, mask_ids, weight = call(
         functools.partial(sums_kernel, n, pad),
-        [tile_about] * far + [array(of_rows, jnp.int32), array(of_rows, F32)],
+        [array((tile_about.shape[0] + of_rows[0], LANES), F32)] * far
+        + [array(of_rows, jnp.int32), array(of_rows, F32)],
         [hbm] * 4,
         [vmem] * (far + 2),
         [
@@ -395,10 +404,11 @@
     )(in_hbm(probes), in_hbm(lengths), in_hbm(ids), in_hbm(firms))
 
     def join(parts):
-        shape = array((far, *parts[0].shape), F32)
+        shape = array((far, *tile_about.shape), F32)
         return call(join_kernel, shape, [vmem] * far, vmem, [], 0, shape.size * 8)(*parts)
 
-    received = share(join(exchange(sends, n)), n)
+    arrived = exchange(sends, n)
+    received = share(join(arrived), n)
     means, table, scale = call(
         owner_first_kernel,
         [array((far, *tile.shape), F32), array((mine, NEAR * mine), BF16), array((mine, LANES), F32)],
@@ -410,14 +420,14 @@
     )(*received)
     own = 16 * NEAR
     pairs = call(
-        functools.partial(pairs_kernel, pad, far),
+        functools.partial(pairs_kernel, pad),
         array((far, 2 * own, slots), BF16),
-        [vmem] * 2,
+        [vmem] * far,
         vmem,
-        [pltpu.VMEM((slots, workers), BF16)],
+        [pltpu.VMEM((far, *of_rows), F32), pltpu.VMEM((slots, workers), BF16)],
         work,
         4 * slots * slots,
-    )(all_lengths, all_ids)
+    )(*arrived)
     sums, mean = call(
         functools.partial(change_kernel, far),
         [array((far, *tile.shape), F32), of_slots],

time: 73.4 us -> 49.6 us (0.68)
  blocking collectives: 26.6 us -> 0 us
  waiting for transfers between devices: 10.8 us -> 13.8 us
    all_gather x2 -> x0, blocking collectives: 26.6 us -> none  [the longest x1 13.5 us: body(): all_ids = lax.all_gather(ids, 'rows', axis_index_groups=groups)]
    ppermute x6, waiting for transfers between devices: 5.58 us -> 7.25 us  [exchange(): lax.ppermute(part, 'rows', step)]
    ppermute x6, waiting for transfers between devices: 5.25 us -> 6.05 us  [share(): lax.ppermute(part, 'rows', [(i, i ^ k) for i in range(n)])]
  transfers between devices with their start and end apart: 15 -> 15, of which waited for: 5 -> 7; matrix products, arithmetic and copies ran while one was open for 0% -> 0% of each run, Pallas kernels for 11% -> 16%
where the time goes in v11:
time: 49.6 us; the launch traced here: 49.4 us
  starting transfers between devices  18.4 us (37%)
  Pallas kernels  17.1 us (34%)
  waiting for transfers between devices  13.8 us (28%)
    ppermute x6, starting transfers between devices, exchange(): lax.ppermute(part, 'rows', step)  10.1 us
    ppermute x6, waiting for transfers between devices, exchange(): lax.ppermute(part, 'rows', step)  7.25 us
    ppermute x6, waiting for transfers between devices, share(): lax.ppermute(part, 'rows', [(i, i ^ k) for i in range(n)])  6.05 us
    pallas_call x1, Pallas kernels, body(): call(functools.partial(sums_kernel, n, pad), [array((tile_about.shape[0]...  5.22 us
    ppermute x3, starting transfers between devices, all_far(): return [part] + [lax.ppermute(part, 'rows', step) for step in steps]  4.45 us
    pallas_call x2, Pallas kernels, first(): call(functools.partial(first_kernel, pad, start), array((columns, width),...  4.4 us
    ppermute x6, starting transfers between devices, share(): lax.ppermute(part, 'rows', [(i, i ^ k) for i in range(n)])  3.77 us
    pallas_call x1, Pallas kernels, body(): call(functools.partial(pairs_kernel, pad), array((far, 2 * own, slots), B...  3.66 us
  transfers between devices with their start and end apart: 15, of which 7 were waited for; matrix products, arithmetic and copies ran while one was open for 0% of the time, Pallas kernels for 16%

profile of v11, /device:TPU:0, one launch (start us, length us, event | category | flops | bytes accessed | tf_op | source)
XLA Modules:
  0.0 49.4 jit_solution(5719388662477133066)
XLA Ops:
  0.0 5.2 %shard_map.46 = (f32[104,128]{1,0:T(8,128)S(1)}, f32[104,128]{1,0:T(8,128)S(1)}, f32[104,128]{1,0:T(8,128)S(1)}, f32[104,128]{1,0:T(8,128)S(1)}, s32[64,128]{1,0:T(8,128)S(1)}, /*index=5*/f32[64,128]{1,0:T(8,128)S(1)}) custom-call(f32[64,8192]{1,0:T(8,128)} %probes.3, s32[8,128]{1,0:T(8,128)} %bitcast.4, s32[64,128]{1,0:T(8,128)} %bitcast.3, s32[2,128]{1,0:T(2,128)} %bitcast.5), custom_call_target="tpu_custom_call" | custom-call | flops 1073741824 | bytes 2097152 | tf_op jit(solution)/shard_map/pallas_call | solution.py:385
  5.2 3.1 %collective-permute-start = (f32[104,128]{1,0:T(8,128)S(1)}, f32[104,128]{1,0:T(8,128)S(1)}, u32[]{:S(2)}, u32[]{:S(2)}) collective-permute-start(f32[104,128]{1,0:T(8,128)S(1)} %get-tuple-element.21), channel_id=1, source_target_pairs={{0,4},{1,5},{2,6},{3,7},{4,0},{5,1},{6,2},{7,3},{8,12},{9,13},{10,... | collective-permute-start | bytes 159752 | tf_op jit(solution)/shard_map/ppermute | solution.py:340
  8.3 2.6 %collective-permute-start.1 = (f32[104,128]{1,0:T(8,128)S(1)}, f32[104,128]{1,0:T(8,128)S(1)}, u32[]{:S(2)}, u32[]{:S(2)}) collective-permute-start(f32[104,128]{1,0:T(8,128)S(1)} %get-tuple-element.22), channel_id=1, source_target_pairs={{0,8},{1,9},{2,10},{3,11},{4,12},{5,13},{6,14},{7,15},{8,0},{9,1},... | collective-permute-start | bytes 159752 | tf_op jit(solution)/shard_map/ppermute | solution.py:340
  10.9 0.0 collective-permute-start.2
  10.9 0.0 collective-permute-done.refs_1_
  10.9 3.5 %collective-permute-done.1.refs_2_ = f32[104,128]{1,0:T(8,128)S(1)} collective-permute-done((f32[104,128]{1,0:T(8,128)S(1)}, f32[104,128]{1,0:T(8,128)S(1)}, u32[]{:S(2)}, u32[]{:S(2)}) %collective-permute-start.1) | collective-permute-done | bytes 53280 | tf_op jit(solution)/shard_map/ppermute | solution.py:340
  14.4 2.5 %collective-permute-done.2.refs_3_ = f32[104,128]{1,0:T(8,128)S(1)} collective-permute-done((f32[104,128]{1,0:T(8,128)S(1)}, f32[104,128]{1,0:T(8,128)S(1)}, u32[]{:S(2)}, u32[]{:S(2)}) %collective-permute-start.2) | collective-permute-done | bytes 53280 | tf_op jit(solution)/shard_map/ppermute | solution.py:340
  16.9 0.0 collective-permute-start.5
  16.9 1.6 %collective-permute-start.4 = (f32[4,40,128]{2,1,0:T(8,128)S(1)}, f32[4,40,128]{2,1,0:T(8,128)S(1)}, u32[]{:S(2)}, u32[]{:S(2)}) collective-permute-start(f32[4,40,128]{2,1,0:T(8,128)S(1)} %shard_map.47.refs_0_.refs_4_), channel_id=1, source_target_pairs={{0,2},{1,3},{2,0},{3,1},{4,6},{5,7},{6,4},{7,5},{8,10},{9,11},{10,... | collective-permute-start | bytes 245768 | tf_op jit(solution)/shard_map/ppermute | solution.py:344
  18.4 0.3 collective-permute-start.3
  18.7 2.8 %collective-permute-done.5.refs_3_ = f32[4,40,128]{2,1,0:T(8,128)S(1)} collective-permute-done((f32[4,40,128]{2,1,0:T(8,128)S(1)}, f32[4,40,128]{2,1,0:T(8,128)S(1)}, u32[]{:S(2)}, u32[]{:S(2)}) %collective-permute-start.5) | collective-permute-done | bytes 81952 | tf_op jit(solution)/shard_map/ppermute | solution.py:344
  21.5 1.8 %collective-permute-done.4.refs_2_ = f32[4,40,128]{2,1,0:T(8,128)S(1)} collective-permute-done((f32[4,40,128]{2,1,0:T(8,128)S(1)}, f32[4,40,128]{2,1,0:T(8,128)S(1)}, u32[]{:S(2)}, u32[]{:S(2)}) %collective-permute-start.4) | collective-permute-done | bytes 81952 | tf_op jit(solution)/shard_map/ppermute | solution.py:344
  23.4 0.0 collective-permute-done.3.refs_1_
  23.4 1.2 %shard_map.48 = (f32[4,32,128]{2,1,0:T(8,128)S(1)}, bf16[256,1024]{1,0:T(8,128)(2,1)S(1)}, f32[256,128]{1,0:T(8,128)S(1)}) custom-call(f32[4,40,128]{2,1,0:T(8,128)S(1)} %shard_map.47.refs_0_.refs_4_, f32[4,40,128]{2,1,0:T(8,128)S(1)} %collective-permute-done.3.refs_1_, f32[4,40,128]{2,1,0:T(8,128)S(1)} %collective-permute-done.4.refs_2_, ...), custom_call_target="tpu_custom_call" | custom-call | flops 33554432 | bytes 262144 | tf_op jit(solution)/shard_map/pallas_call | solution.py:412
  24.6 1.1 %collective-permute-start.8 = (f32[4,32,128]{2,1,0:T(8,128)S(1)}, f32[4,32,128]{2,1,0:T(8,128)S(1)}, u32[]{:S(2)}, u32[]{:S(2)}) collective-permute-start(f32[4,32,128]{2,1,0:T(8,128)S(1)} %get-tuple-element.24.refs_0_), channel_id=1, source_target_pairs={{0,12},{1,13},{2,14},{3,15},{4,8},{5,9},{6,10},{7,11},{8,4},{9,5},... | collective-permute-start | bytes 196616 | tf_op jit(solution)/shard_map/ppermute | solution.py:335
  25.7 0.0 collective-permute-start.7
  25.7 3.3 %collective-permute-start.6 = (f32[4,32,128]{2,1,0:T(8,128)S(1)}, f32[4,32,128]{2,1,0:T(8,128)S(1)}, u32[]{:S(2)}, u32[]{:S(2)}) collective-permute-start(f32[4,32,128]{2,1,0:T(8,128)S(1)} %get-tuple-element.24.refs_0_), channel_id=1, source_target_pairs={{0,4},{1,5},{2,6},{3,7},{4,0},{5,1},{6,2},{7,3},{8,12},{9,13},{10,... | collective-permute-start | bytes 196616 | tf_op jit(solution)/shard_map/ppermute | solution.py:335
  29.0 3.7 %shard_map.49.refs_5_ = bf16[4,128,256]{2,1,0:T(8,128)(2,1)S(1)} custom-call(f32[104,128]{1,0:T(8,128)S(1)} %get-tuple-element.20.refs_0_, f32[104,128]{1,0:T(8,128)S(1)} %collective-permute-done.refs_1_, f32[104,128]{1,0:T(8,128)S(1)} %collective-permute-done.1.refs_2_, f32[104,128]{1,0:T(8,128)S(1)} %collective-permute-done.2.refs_3_), custom_call_target="tpu_custom_call" | custom-call | flops 536870912 | bytes 262144 | tf_op jit(solution)/shard_map/pallas_call | solution.py:422
  32.7 0.0 collective-permute-done.8.refs_3_
  32.7 0.5 collective-permute-done.7.refs_2_
  33.2 0.0 collective-permute-done.6.refs_1_
  33.2 0.4 shard_map.50
  33.6 0.1 collective-permute-start.11
  33.7 1.5 %collective-permute-start.10 = (f32[4,32,128]{2,1,0:T(8,128)S(1)}, f32[4,32,128]{2,1,0:T(8,128)S(1)}, u32[]{:S(2)}, u32[]{:S(2)}) collective-permute-start(f32[4,32,128]{2,1,0:T(8,128)S(1)} %get-tuple-element.25.refs_0_), channel_id=1, source_target_pairs={{0,2},{1,3},{2,0},{3,1},{4,6},{5,7},{6,4},{7,5},{8,10},{9,11},{10,... | collective-permute-start | bytes 196616 | tf_op jit(solution)/shard_map/ppermute | solution.py:344
  35.2 0.3 collective-permute-start.9
  35.5 2.5 %shard_map.51.refs_6_.refs_4_ = f32[64,5120]{1,0:T(8,128)S(1)} custom-call(f32[64,8192]{1,0:T(8,128)} %probes.3, f32[256,128]{1,0:T(8,128)S(1)} %get-tuple-element.28.mean, s32[64,128]{1,0:T(8,128)S(1)} %get-tuple-element.29.mask_ids.refs_6_, f32[64,128]{1,0:T(8,128)S(1)} %get-tuple-element.30.weight), custom_call_target="tpu_custom_call" | custom-call | flops 671088640 | bytes 2621440 | tf_op jit(solution)/shard_map/pallas_call | solution.py:444
  38.1 0.0 collective-permute-done.11.refs_3_
  38.1 1.4 %collective-permute-done.10.refs_2_ = f32[4,32,128]{2,1,0:T(8,128)S(1)} collective-permute-done((f32[4,32,128]{2,1,0:T(8,128)S(1)}, f32[4,32,128]{2,1,0:T(8,128)S(1)}, u32[]{:S(2)}, u32[]{:S(2)}) %collective-permute-start.10) | collective-permute-done | bytes 65568 | tf_op jit(solution)/shard_map/ppermute | solution.py:344
  39.5 0.0 collective-permute-done.9.refs_1_
  39.5 0.5 shard_map.52
  39.9 0.1 collective-permute-start.12
  40.0 2.1 %collective-permute-start.13 = (f32[32,128]{1,0:T(8,128)S(1)}, f32[32,128]{1,0:T(8,128)S(1)}, u32[]{:S(2)}, u32[]{:S(2)}) collective-permute-start(f32[32,128]{1,0:T(8,128)S(1)} %get-tuple-element.33), channel_id=1, source_target_pairs={{0,8},{1,9},{2,10},{3,11},{4,12},{5,13},{6,14},{7,15},{8,0},{9,1},... | collective-permute-start | bytes 49160 | tf_op jit(solution)/shard_map/ppermute | solution.py:340
  42.1 2.3 %collective-permute-start.14 = (f32[32,128]{1,0:T(8,128)S(1)}, f32[32,128]{1,0:T(8,128)S(1)}, u32[]{:S(2)}, u32[]{:S(2)}) collective-permute-start(f32[32,128]{1,0:T(8,128)S(1)} %get-tuple-element.34), channel_id=1, source_target_pairs={{0,12},{1,13},{2,14},{3,15},{4,8},{5,9},{6,10},{7,11},{8,4},{9,5},... | collective-permute-start | bytes 49160 | tf_op jit(solution)/shard_map/ppermute | solution.py:340
  44.4 1.9 %shard_map.53.refs_5_ = f32[64,3072]{1,0:T(8,128)S(1)} custom-call(f32[64,8192]{1,0:T(8,128)} %probes.3, f32[256,128]{1,0:T(8,128)S(1)} %get-tuple-element.28.mean, s32[64,128]{1,0:T(8,128)S(1)} %get-tuple-element.29.mask_ids.refs_6_, f32[64,128]{1,0:T(8,128)S(1)} %get-tuple-element.30.weight), custom_call_target="tpu_custom_call" | custom-call | flops 402653184 | bytes 1572864 | tf_op jit(solution)/shard_map/pallas_call | solution.py:444
  46.3 0.0 collective-permute-done.12.refs_1_
  46.3 0.0 collective-permute-done.13.refs_2_
  46.3 1.3 %collective-permute-done.14.refs_3_ = f32[32,128]{1,0:T(8,128)S(1)} collective-permute-done((f32[32,128]{1,0:T(8,128)S(1)}, f32[32,128]{1,0:T(8,128)S(1)}, u32[]{:S(2)}, u32[]{:S(2)}) %collective-permute-start.14) | collective-permute-done | bytes 16416 | tf_op jit(solution)/shard_map/ppermute | solution.py:340
  47.6 1.8 %shard_map.54 = f32[64,8192]{1,0:T(8,128)} custom-call(f32[32,128]{1,0:T(8,128)S(1)} %get-tuple-element.31.refs_0_, f32[32,128]{1,0:T(8,128)S(1)} %collective-permute-done.12.refs_1_, f32[32,128]{1,0:T(8,128)S(1)} %collective-permute-done.13.refs_2_, f32[32,128]{1,0:T(8,128)S(1)} %collective-permute-done.14.refs_3_, ...), custom_call_target="tpu_custom_call" | custom-call | flops 536870912 | bytes 4194304 | tf_op jit(solution)/shard_map/pallas_call | solution.py:465
  (1 shorter events, 0.0 us)
Async XLA Ops:
  5.2 5.7 %collective-permute-start = (f32[104,128]{1,0:T(8,128)S(1)}, f32[104,128]{1,0:T(8,128)S(1)}, u32[]{:S(2)}, u32[]{:S(2)}) collective-permute-start(f32[104,128]{1,0:T(8,128)S(1)} %get-tuple-element.21), channel_id=1, source_target_pairs={{0,4},{1,5},{2,6},{3,7},{4,0},{5,1},{6,2},{7,3},{8,12},{9,13},{10,... | collective-permute-start | bytes 159752 | tf_op jit(solution)/shard_map/ppermute | solution.py:340
  8.3 6.1 %collective-permute-start.1 = (f32[104,128]{1,0:T(8,128)S(1)}, f32[104,128]{1,0:T(8,128)S(1)}, u32[]{:S(2)}, u32[]{:S(2)}) collective-permute-start(f32[104,128]{1,0:T(8,128)S(1)} %get-tuple-element.22), channel_id=1, source_target_pairs={{0,8},{1,9},{2,10},{3,11},{4,12},{5,13},{6,14},{7,15},{8,0},{9,1},... | collective-permute-start | bytes 159752 | tf_op jit(solution)/shard_map/ppermute | solution.py:340
  10.9 5.9 %collective-permute-start.2 = (f32[104,128]{1,0:T(8,128)S(1)}, f32[104,128]{1,0:T(8,128)S(1)}, u32[]{:S(2)}, u32[]{:S(2)}) collective-permute-start(f32[104,128]{1,0:T(8,128)S(1)} %get-tuple-element.23), channel_id=1, source_target_pairs={{0,12},{1,13},{2,14},{3,15},{4,8},{5,9},{6,10},{7,11},{8,4},{9,5},... | collective-permute-start | bytes 159752 | tf_op jit(solution)/shard_map/ppermute | solution.py:340
  16.9 4.7 %collective-permute-start.5 = (f32[4,40,128]{2,1,0:T(8,128)S(1)}, f32[4,40,128]{2,1,0:T(8,128)S(1)}, u32[]{:S(2)}, u32[]{:S(2)}) collective-permute-start(f32[4,40,128]{2,1,0:T(8,128)S(1)} %shard_map.47.refs_0_.refs_4_), channel_id=1, source_target_pairs={{0,3},{1,2},{2,1},{3,0},{4,7},{5,6},{6,5},{7,4},{8,11},{9,10},{10,... | collective-permute-start | bytes 245768 | tf_op jit(solution)/shard_map/ppermute | solution.py:344
  16.9 6.5 %collective-permute-start.4 = (f32[4,40,128]{2,1,0:T(8,128)S(1)}, f32[4,40,128]{2,1,0:T(8,128)S(1)}, u32[]{:S(2)}, u32[]{:S(2)}) collective-permute-start(f32[4,40,128]{2,1,0:T(8,128)S(1)} %shard_map.47.refs_0_.refs_4_), channel_id=1, source_target_pairs={{0,2},{1,3},{2,0},{3,1},{4,6},{5,7},{6,4},{7,5},{8,10},{9,11},{10,... | collective-permute-start | bytes 245768 | tf_op jit(solution)/shard_map/ppermute | solution.py:344
  18.4 4.9 %collective-permute-start.3 = (f32[4,40,128]{2,1,0:T(8,128)S(1)}, f32[4,40,128]{2,1,0:T(8,128)S(1)}, u32[]{:S(2)}, u32[]{:S(2)}) collective-permute-start(f32[4,40,128]{2,1,0:T(8,128)S(1)} %shard_map.47.refs_0_.refs_4_), channel_id=1, source_target_pairs={{0,1},{1,0},{2,3},{3,2},{4,5},{5,4},{6,7},{7,6},{8,9},{9,8},{10,11... | collective-permute-start | bytes 245768 | tf_op jit(solution)/shard_map/ppermute | solution.py:344
  24.6 8.1 %collective-permute-start.8 = (f32[4,32,128]{2,1,0:T(8,128)S(1)}, f32[4,32,128]{2,1,0:T(8,128)S(1)}, u32[]{:S(2)}, u32[]{:S(2)}) collective-permute-start(f32[4,32,128]{2,1,0:T(8,128)S(1)} %get-tuple-element.24.refs_0_), channel_id=1, source_target_pairs={{0,12},{1,13},{2,14},{3,15},{4,8},{5,9},{6,10},{7,11},{8,4},{9,5},... | collective-permute-start | bytes 196616 | tf_op jit(solution)/shard_map/ppermute | solution.py:335
  25.7 7.5 %collective-permute-start.7 = (f32[4,32,128]{2,1,0:T(8,128)S(1)}, f32[4,32,128]{2,1,0:T(8,128)S(1)}, u32[]{:S(2)}, u32[]{:S(2)}) collective-permute-start(f32[4,32,128]{2,1,0:T(8,128)S(1)} %get-tuple-element.24.refs_0_), channel_id=1, source_target_pairs={{0,8},{1,9},{2,10},{3,11},{4,12},{5,13},{6,14},{7,15},{8,0},{9,1},... | collective-permute-start | bytes 196616 | tf_op jit(solution)/shard_map/ppermute | solution.py:335
  25.7 7.5 %collective-permute-start.6 = (f32[4,32,128]{2,1,0:T(8,128)S(1)}, f32[4,32,128]{2,1,0:T(8,128)S(1)}, u32[]{:S(2)}, u32[]{:S(2)}) collective-permute-start(f32[4,32,128]{2,1,0:T(8,128)S(1)} %get-tuple-element.24.refs_0_), channel_id=1, source_target_pairs={{0,4},{1,5},{2,6},{3,7},{4,0},{5,1},{6,2},{7,3},{8,12},{9,13},{10,... | collective-permute-start | bytes 196616 | tf_op jit(solution)/shard_map/ppermute | solution.py:335
  33.6 4.4 %collective-permute-start.11 = (f32[4,32,128]{2,1,0:T(8,128)S(1)}, f32[4,32,128]{2,1,0:T(8,128)S(1)}, u32[]{:S(2)}, u32[]{:S(2)}) collective-permute-start(f32[4,32,128]{2,1,0:T(8,128)S(1)} %get-tuple-element.25.refs_0_), channel_id=1, source_target_pairs={{0,3},{1,2},{2,1},{3,0},{4,7},{5,6},{6,5},{7,4},{8,11},{9,10},{10,... | collective-permute-start | bytes 196616 | tf_op jit(solution)/shard_map/ppermute | solution.py:344
  33.7 5.8 %collective-permute-start.10 = (f32[4,32,128]{2,1,0:T(8,128)S(1)}, f32[4,32,128]{2,1,0:T(8,128)S(1)}, u32[]{:S(2)}, u32[]{:S(2)}) collective-permute-start(f32[4,32,128]{2,1,0:T(8,128)S(1)} %get-tuple-element.25.refs_0_), channel_id=1, source_target_pairs={{0,2},{1,3},{2,0},{3,1},{4,6},{5,7},{6,4},{7,5},{8,10},{9,11},{10,... | collective-permute-start | bytes 196616 | tf_op jit(solution)/shard_map/ppermute | solution.py:344
  35.2 4.3 %collective-permute-start.9 = (f32[4,32,128]{2,1,0:T(8,128)S(1)}, f32[4,32,128]{2,1,0:T(8,128)S(1)}, u32[]{:S(2)}, u32[]{:S(2)}) collective-permute-start(f32[4,32,128]{2,1,0:T(8,128)S(1)} %get-tuple-element.25.refs_0_), channel_id=1, source_target_pairs={{0,1},{1,0},{2,3},{3,2},{4,5},{5,4},{6,7},{7,6},{8,9},{9,8},{10,11... | collective-permute-start | bytes 196616 | tf_op jit(solution)/shard_map/ppermute | solution.py:344
  39.9 6.4 %collective-permute-start.12 = (f32[32,128]{1,0:T(8,128)S(1)}, f32[32,128]{1,0:T(8,128)S(1)}, u32[]{:S(2)}, u32[]{:S(2)}) collective-permute-start(f32[32,128]{1,0:T(8,128)S(1)} %get-tuple-element.32), channel_id=1, source_target_pairs={{0,4},{1,5},{2,6},{3,7},{4,0},{5,1},{6,2},{7,3},{8,12},{9,13},{10,... | collective-permute-start | bytes 49160 | tf_op jit(solution)/shard_map/ppermute | solution.py:340
  40.0 6.3 %collective-permute-start.13 = (f32[32,128]{1,0:T(8,128)S(1)}, f32[32,128]{1,0:T(8,128)S(1)}, u32[]{:S(2)}, u32[]{:S(2)}) collective-permute-start(f32[32,128]{1,0:T(8,128)S(1)} %get-tuple-element.33), channel_id=1, source_target_pairs={{0,8},{1,9},{2,10},{3,11},{4,12},{5,13},{6,14},{7,15},{8,0},{9,1},... | collective-permute-start | bytes 49160 | tf_op jit(solution)/shard_map/ppermute | solution.py:340
  42.1 5.5 %collective-permute-start.14 = (f32[32,128]{1,0:T(8,128)S(1)}, f32[32,128]{1,0:T(8,128)S(1)}, u32[]{:S(2)}, u32[]{:S(2)}) collective-permute-start(f32[32,128]{1,0:T(8,128)S(1)} %get-tuple-element.34), channel_id=1, source_target_pairs={{0,12},{1,13},{2,14},{3,15},{4,8},{5,9},{6,10},{7,11},{8,4},{9,5},... | collective-permute-start | bytes 49160 | tf_op jit(solution)/shard_map/ppermute | solution.py:340

commit v12 on v11

v12 whole, which is shorter than its diff:
```python
import functools

import jax
import jax.numpy as jnp
from jax import lax
from jax.experimental import pallas as pl
from jax.experimental.pallas import tpu as pltpu
from jax.sharding import PartitionSpec as P

FIRMS_PER_SHARD = 1024
LANES = 128
BLOCK = 1024
VMEM_BYTES = 32 * 1024 * 1024
NEAR = 4
F32, BF16 = jnp.float32, jnp.bfloat16
NT = (((1,), (1,)), ((), ()))
NN = (((1,), (0,)), ((), ()))


def dot(a, b, dims=NN):
    return lax.dot_general(a, b, dims, preferred_element_type=F32)


def iota(shape, dim):
    return lax.broadcasted_iota(jnp.int32, shape, dim)


def split(x):
    hi = x.astype(BF16)
    return hi, (x - hi.astype(F32)).astype(BF16)


def row(ref, block, size):
    per = size // LANES
    return jnp.concatenate([ref[block * per + k : block * per + k + 1, :] for k in range(per)], axis=1)


def one_hot(ids, slots):
    kind = BF16 if slots <= 256 else F32
    slot = iota((slots, LANES), 0).astype(F32).astype(kind)
    ids = ids.astype(F32).astype(kind)
    one, zero = jnp.ones((slots, LANES), kind), jnp.zeros((slots, LANES), kind)
    parts = [jnp.where(slot == ids[:, k : k + LANES], one, zero) for k in range(0, ids.shape[1], LANES)]
    return jnp.concatenate(parts, axis=1).astype(BF16)


def same_worker(pad, width):
    return (iota((width, width), 0) // pad == iota((width, width), 1) // pad).astype(F32).astype(BF16)


def by_worker(x, table):
    rows, width = x.shape
    hi, lo = split(x)
    both = jnp.concatenate([hi, lo], axis=0)
    step = table.shape[0]
    total = jnp.concatenate([dot(both[:, k : k + step], table) for k in range(0, width, step)], axis=1)
    return total[:rows] + total[rows:]


def start_all(copies):
    for copy in copies:
        copy.start()


def wait_all(copies):
    for copy in copies:
        copy.wait()


def column_copies(source, target, sems):
    width = source.shape[1]
    cuts = [pl.ds(start, BLOCK) for start in range(0, width, BLOCK)]
    return [pltpu.make_async_copy(source.at[:, cut], target.at[:, cut], sems.at[b]) for b, cut in enumerate(cuts)]


def row_lengths(lengths, pad):
    total_rows = lengths.shape[0] * pad
    here = iota((total_rows, LANES), 0)
    lane = iota((total_rows, LANES), 1)
    wide = jnp.broadcast_to(lengths.astype(F32)[:, None, :], (lengths.shape[0], pad, LANES)).reshape(total_rows, LANES)
    per = LANES // pad
    wide = jnp.where(lane // per == here % pad, wide, 0.0).astype(BF16)
    spread = (iota((LANES, LANES), 0) % per == iota((LANES, LANES), 1) // pad).astype(F32).astype(BF16)
    row_len = dot(wide, spread)
    return row_len, (lane % pad).astype(F32) < row_len


def along(ref):
    return jnp.concatenate([ref[k : k + 1, :] for k in range(ref.shape[0])], axis=1)


def sums_kernel(pad, cap, *refs):
    (probes, lengths_in, ids_in, firms_in), sends, refs = refs[:4], refs[4 : 4 + NEAR], refs[4 + NEAR :]
    x1, mask_ids, weight, valid, x, acc, sums, lengths, ids, firms, sems, small = refs
    copies = column_copies(probes, x, sems)
    first = [
        pltpu.make_async_copy(source, target, small.at[k])
        for k, (source, target) in enumerate(((lengths_in, lengths), (ids_in, ids), (firms_in, firms)))
    ]
    start_all(first)
    start_all(copies)
    columns, slots = sums.shape
    part = columns // NEAR
    me = lax.axis_index("rows") % NEAR
    wait_all(first)
    row_len, inside = row_lengths(lengths[...], pad)
    valid[...] = jnp.where(inside, 1.0, 0.0)
    weight[...] = jnp.where(inside, 1.0 / row_len, 0.0)
    masked = jnp.where(inside, ids[...], -1)
    mask_ids[...] = masked
    keys = (iota((1, slots), 1) // cap * FIRMS_PER_SHARD + along(firms)).astype(F32)
    across = slots // LANES
    rows = ids.shape[0] // across
    masked = jnp.concatenate([masked[k * rows : (k + 1) * rows] for k in range(across)], axis=1).astype(F32)
    for send in sends:
        send[part + 8 :] = masked

    table = same_worker(pad, 256)
    for b in range(len(copies)):
        copies[b].wait()
        ok = row(valid, b, BLOCK)
        x0 = x[:, b * BLOCK : (b + 1) * BLOCK] * ok
        rest = x0 - by_worker(x0, table) * row(weight, b, BLOCK)
        x1[:, b * BLOCK : (b + 1) * BLOCK] = rest
        counted = jnp.broadcast_to(ok, (16, BLOCK)).astype(BF16)
        data = jnp.concatenate([*split(rest), counted], axis=0)
        block = dot(data, one_hot(row(mask_ids, b, BLOCK), slots), NT)
        if b == 0:
            acc[...] = block
        else:
            acc[...] += block
    sums[...] = acc[:columns] + acc[columns : 2 * columns]
    about = jnp.where(iota((8, slots), 0) == 0, keys, acc[2 * columns : 2 * columns + 1])
    for k, send in enumerate(sends):
        send[:part] = sums[pl.ds(pl.multiple_of((me ^ k) * part, part), part), :]
        send[part : part + 8] = about


def join_kernel(part, *refs):
    parts, out = refs[:NEAR], refs[-1]
    for k, one in enumerate(parts):
        out[part * k : part * (k + 1)] = one[:part]
        out[part * NEAR + 2 * k : part * NEAR + 2 * k + 2] = one[part : part + 2]


def pairs_kernel(pad, start, *refs):
    parts, (out, ids, counts) = refs[:-3], refs[-3:]
    slots = out.shape[1]
    kind = BF16 if slots <= 256 else F32
    per = LANES // pad
    total_rows = ids.shape[1]
    across = slots // LANES
    rows = total_rows // across
    for k, part in enumerate(parts):
        for at in range(across):
            ids[k, at * rows : (at + 1) * rows] = part[start:, at * LANES : (at + 1) * LANES]
    at = iota((LANES, pad * LANES), 1)
    deal = (iota((LANES, pad * LANES), 0) == at % per * pad + at // LANES).astype(F32).astype(BF16)
    mine = iota((total_rows, pad * LANES), 1) % LANES // per == iota((total_rows, pad * LANES), 0) % pad
    slot = iota((slots, LANES), 0).astype(F32).astype(kind)
    one, zero = jnp.ones((slots, LANES), kind), jnp.zeros((slots, LANES), kind)
    diagonal = iota((slots, slots), 1) == iota((slots, slots), 0)

    def device(k, carry):
        dealt = dot(jnp.concatenate(split(ids[k]), axis=0), deal)
        dealt = jnp.where(mine, dealt[:total_rows] + dealt[total_rows:], 0.0)
        dealt = jnp.sum(dealt.reshape(total_rows // pad, pad, pad * LANES), axis=1)
        spells = dealt.astype(kind)
        for g in range(total_rows // pad):
            total = zero
            for j in range(pad):
                total += jnp.where(slot == spells[g : g + 1, j * LANES : (j + 1) * LANES], one, zero)
            counts[:, g * LANES : (g + 1) * LANES] = total.astype(BF16)
        valid = jnp.where(dealt >= 0.0, 1.0, 0.0)
        length = valid[:, :LANES]
        for j in range(1, pad):
            length += valid[:, j * LANES : (j + 1) * LANES]
        inverse = 1.0 / length
        inverse = jnp.concatenate([inverse[g : g + 1] for g in range(total_rows // pad)], axis=1)
        here = counts[...].astype(F32)
        total = dot(jnp.concatenate(split(here * inverse), axis=0), counts[...], NT)
        total = total[:slots] + total[slots:] - jnp.where(diagonal, jnp.sum(here, axis=1, keepdims=True), 0.0)
        hi, lo = split(total)
        out[k, :, :slots] = hi
        out[k, :, slots:] = lo
        return carry

    lax.fori_loop(0, len(parts), device, 0, unroll=len(parts) if slots <= 256 else 1)


def same_firm(parts, part, at):
    def keys(one, k):
        return one[part * NEAR + 2 * k : part * NEAR + 2 * k + 1, at]

    down = [jnp.broadcast_to(keys(parts[0], k), (LANES, LANES)).T for k in range(NEAR)]
    down = jnp.concatenate(down, axis=0)
    found = [(down == keys(one, k)).astype(F32).astype(BF16) for one in parts for k in range(NEAR)]
    return jnp.concatenate(found, axis=1)


def gathered(parts, part, at):
    data = [one[part * k : part * (k + 1), at] for one in parts for k in range(NEAR)]
    return jnp.concatenate(split(jnp.concatenate(data, axis=1)), axis=0)


def spread_out(means, out, part, at):
    for k in range(NEAR):
        out[part * k : part * (k + 1), at] = means[:, k * LANES : (k + 1) * LANES]


def each_tile(slots, do):
    tiles = slots // LANES
    if tiles <= 2:
        for t in range(tiles):
            do(t, slice(t * LANES, (t + 1) * LANES))
    else:
        lax.fori_loop(0, tiles, lambda t, c: (do(t, pl.ds(pl.multiple_of(t * LANES, LANES), LANES)), c)[1], 0)


def change_kernel(far, part, *refs):
    parts, (own_pairs, pairs, mean, sums, scale), table = refs[:far], refs[far : far + 5], refs[far + 5 :]
    slots = mean.shape[1]

    def tile(t, at):
        same = same_firm(parts, part, at)
        if table:
            table[0][t] = same
        count = [one[part * NEAR + 2 * k + 1 : part * NEAR + 2 * k + 2, at] for one in parts for k in range(NEAR)]
        count = jnp.concatenate(count, axis=1)
        high = count.astype(BF16).astype(F32)
        counts = jnp.where(iota((16, count.shape[1]), 0) < 8, high, count - high).astype(BF16)
        found = dot(jnp.concatenate([gathered(parts, part, at), counts], axis=0), same, NT)
        size = found[2 * part : 2 * part + 1] + found[2 * part + 8 : 2 * part + 9]
        inverse = 1.0 / jnp.maximum(size, 1.0)
        scale[t] = jnp.broadcast_to(inverse, scale.shape[1:])
        spread_out((found[:part] + found[part : 2 * part]) * inverse, mean, part, at)

    each_tile(slots, tile)
    for k in range(NEAR):
        cut = slice(part * k, part * (k + 1))
        both = jnp.concatenate(split(mean[cut]), axis=0)
        change = dot(both, own_pairs[0] if k == 0 else pairs[k - 1])
        change = change[:part] + change[part:]
        sums[cut] = parts[0][cut] + (change[:, :slots] + change[:, slots:])


def means_kernel(far, part, *refs):
    parts, source, (scale, mean), sends, second = refs[:far], refs[far:-7], refs[-7:-5], refs[-5:-1], refs[-1]

    def tile(t, at):
        same = source[0][t] if len(source) == 1 else same_firm(source, part, at)
        found = dot(gathered(parts, part, at), same, NT)
        spread_out((found[:part] + found[part:]) * scale[t][:1], second, part, at)

    each_tile(mean.shape[1], tile)
    for k, send in enumerate(sends):
        cut = slice(part * k, part * (k + 1))
        send[:part] = mean[cut]
        send[part:] = mean[cut] + second[cut]


def last_kernel(pad, part, *refs):
    parts, (x1, mask_ids, weight, out, means, y, sems) = refs[:NEAR], refs[NEAR:]
    outs = column_copies(y, out, sems)
    me = lax.axis_index("rows") % NEAR
    columns, slots = means.shape[1:]
    for k, one in enumerate(parts):
        at = pl.ds(pl.multiple_of((me ^ k) * part, part), part)
        means[0, at, :] = one[:part]
        means[1, at, :] = one[part:]
    both = jnp.concatenate([*split(means[0]), *split(means[1])], axis=0)
    table = same_worker(pad, 256)
    for b in range(len(outs)):
        at = slice(b * BLOCK, (b + 1) * BLOCK)
        found = dot(both, one_hot(row(mask_ids, b, BLOCK), slots))
        first = found[:columns] + found[columns : 2 * columns]
        total = found[2 * columns : 3 * columns] + found[3 * columns :]
        y[:, at] = x1[:, at] - total + by_worker(first, table) * row(weight, b, BLOCK)
        outs[b].start()
    wait_all(outs)


def near_exchange(parts, n):
    steps = [[(i, i ^ k) for i in range(n)] for k in range(1, NEAR)]
    return [parts[0]] + [lax.ppermute(one, "rows", step) for one, step in zip(parts[1:], steps)]


def far_share(one, n):
    steps = [[(i, i ^ (k * NEAR)) for i in range(n)] for k in range(1, n // NEAR)]
    return [one] + [lax.ppermute(one, "rows", step) for step in steps]


def in_hbm(x):
    return pltpu.with_memory_space_constraint(x, pltpu.HBM)


def call(kernel, out_shape, in_specs, out_specs, scratch, flops, moved):
    return pl.pallas_call(
        kernel,
        out_shape=out_shape,
        in_specs=in_specs,
        out_specs=out_specs,
        scratch_shapes=scratch,
        compiler_params=pltpu.CompilerParams(vmem_limit_bytes=VMEM_BYTES),
        cost_estimate=pl.CostEstimate(flops=flops, bytes_accessed=moved, transcendentals=0),
    )


def body(probes, worker_len, spell_to_slot, slot_to_firm, *, n):
    columns, rows_dev = probes.shape
    workers = worker_len.shape[0]
    pad = rows_dev // workers
    slots = slot_to_firm.shape[0]
    tiles = slots // LANES
    part = columns // NEAR
    far = n // NEAR
    keep = tiles * NEAR * n * LANES * LANES * 2 <= 8 * 1024 * 1024
    blocks = rows_dev // BLOCK
    vmem, hbm = pl.BlockSpec(memory_space=pltpu.VMEM), pl.BlockSpec(memory_space=pltpu.HBM)
    lengths = worker_len.reshape(workers // LANES, LANES)
    ids = spell_to_slot.reshape(rows_dev // LANES, LANES)
    firms = slot_to_firm.reshape(tiles, LANES)
    array = jax.ShapeDtypeStruct
    of_rows = (rows_dev // LANES, LANES)
    work = 2 * rows_dev * slots * 2 * columns
    sems = pltpu.SemaphoreType.DMA((blocks,))
    whole = (columns, rows_dev)
    about = part + 8
    message = array((about + rows_dev // slots, slots), F32)
    of_near = array((columns, slots), F32)

    *sends, x1, mask_ids, weight = call(
        functools.partial(sums_kernel, pad, slots // n),
        [message] * NEAR + [array(whole, F32), array(of_rows, jnp.int32), array(of_rows, F32)],
        [hbm] * 4,
        [vmem] * (NEAR + 3),
        [
            pltpu.VMEM(of_rows, F32),
            pltpu.VMEM(whole, F32),
            pltpu.VMEM((2 * columns + 16, slots), F32),
            pltpu.VMEM((columns, slots), F32),
            pltpu.VMEM(lengths.shape, jnp.int32),
            pltpu.VMEM(ids.shape, jnp.int32),
            pltpu.VMEM(firms.shape, jnp.int32),
            sems,
            pltpu.SemaphoreType.DMA((3,)),
        ],
        2 * work,
        4 * columns * rows_dev,
    )(in_hbm(probes), in_hbm(lengths), in_hbm(ids), in_hbm(firms))

    def pair_counts(parts):
        return call(
            functools.partial(pairs_kernel, pad, about),
            array((len(parts), slots, 2 * slots), BF16),
            [vmem] * len(parts),
            vmem,
            [pltpu.VMEM((len(parts), *of_rows), F32), pltpu.VMEM((slots, workers), BF16)],
            work * len(parts) // 4,
            4 * slots * slots,
        )(*parts)

    arrived = near_exchange(sends, n)
    own_pairs = pair_counts(arrived[:1])
    joined = call(
        functools.partial(join_kernel, part),
        array((columns + 2 * NEAR, slots), F32),
        [vmem] * (NEAR + 1),
        vmem,
        [],
        0,
        message.size * 8,
    )(*arrived, own_pairs)
    shared = far_share(joined, n)
    pairs = pair_counts(arrived[1:])
    table = array((tiles, NEAR * LANES, n * LANES), BF16)
    scale = array((tiles, 8, NEAR * LANES), F32)
    mean, sums, scales, *tables = call(
        functools.partial(change_kernel, far, part),
        [of_near, of_near, scale] + [table] * keep,
        [vmem] * (far + 2),
        [vmem] * (3 + keep),
        [],
        work // 4,
        slots * slots * 4,
    )(*shared, own_pairs, pairs)
    again = far_share(sums, n)
    source = tables if keep else shared
    sends = call(
        functools.partial(means_kernel, far, part),
        [array((2 * part, slots), F32)] * NEAR,
        [vmem] * (far + len(source) + 2),
        [vmem] * NEAR,
        [pltpu.VMEM((columns, slots), F32)],
        work // 4,
        slots * slots * 4,
    )(*again, *source, scales, mean)
    arrived = near_exchange(sends, n)
    return call(
        functools.partial(last_kernel, pad, part),
        array(whole, F32),
        [vmem] * (NEAR + 3),
        hbm,
        [pltpu.VMEM((2, columns, slots), F32), pltpu.VMEM(whole, F32), sems],
        work,
        8 * columns * rows_dev,
    )(*arrived, x1, mask_ids, weight)


def solution(mesh):
    placed = (P(None, ("grp", "rows")), P(("grp", "rows")), P(("grp", "rows")), P(("grp", "rows")))
    return jax.shard_map(
        functools.partial(body, n=mesh.shape["rows"]),
        mesh=mesh,
        in_specs=placed,
        out_specs=P(None, ("grp", "rows")),
        check_vma=False,
    )
```

time: 49.6 us -> 42.1 us (0.85)
  starting transfers between devices: 18.4 us -> 13.9 us
  waiting for transfers between devices: 13.8 us -> 11.5 us
  Pallas kernels: 17.1 us -> 16.5 us
    ppermute x15 -> x12, starting transfers between devices: 18.4 us -> 13.9 us  [the longest x6 8.85 us: far_share(): return [one] + [lax.ppermute(one, 'rows', step) for step in steps]]
    ppermute x15 -> x12, waiting for transfers between devices: 13.8 us -> 11.5 us  [the longest x6 6.2 us: far_share(): return [one] + [lax.ppermute(one, 'rows', step) for step in steps]]
    pallas_call x9 -> x7, Pallas kernels: 17.1 us -> 16.5 us  [the longest x2 5.22 us: pair_counts(): call(functools.partial(pairs_kernel, pad, about), array((len(parts), slot...]
  transfers between devices with their start and end apart: 15 -> 12, of which waited for: 7 -> 7; matrix products, arithmetic and copies ran while one was open for 0% -> 0% of each run, Pallas kernels for 16% -> 12%
where the time goes in v12:
time: 42.1 us; the launch traced here: 41.9 us
  Pallas kernels  16.5 us (39%)
  starting transfers between devices  13.9 us (33%)
  waiting for transfers between devices  11.5 us (27%)
    ppermute x6, starting transfers between devices, far_share(): return [one] + [lax.ppermute(one, 'rows', step) for step in steps]  8.85 us
    ppermute x6, waiting for transfers between devices, far_share(): return [one] + [lax.ppermute(one, 'rows', step) for step in steps]  6.2 us
    ppermute x6, waiting for transfers between devices, near_exchange(): lax.ppermute(one, 'rows', step)  5.27 us
    pallas_call x2, Pallas kernels, pair_counts(): call(functools.partial(pairs_kernel, pad, about), array((len(parts), slot...  5.22 us
    pallas_call x1, Pallas kernels, body(): call(functools.partial(sums_kernel, pad, slots // n), [message] * NEAR +...  5.07 us
    ppermute x6, starting transfers between devices, near_exchange(): lax.ppermute(one, 'rows', step)  5.06 us
    pallas_call x1, Pallas kernels, body(): call(functools.partial(last_kernel, pad, part), array(whole, F32), [vmem]...  3.09 us
    pallas_call x1, Pallas kernels, body(): call(functools.partial(change_kernel, far, part), [of_near, of_near, scal...  1.83 us
  transfers between devices with their start and end apart: 12, of which 7 were waited for; matrix products, arithmetic and copies ran while one was open for 0% of the time, Pallas kernels for 12%

profile of v12, /device:TPU:0, one launch (start us, length us, event | category | flops | bytes accessed | tf_op | source)
XLA Modules:
  0.0 41.9 jit_solution(15383185270331002427)
XLA Ops:
  0.0 5.1 %shard_map.46 = (f32[56,256]{1,0:T(8,128)S(1)}, f32[56,256]{1,0:T(8,128)S(1)}, f32[56,256]{1,0:T(8,128)S(1)}, f32[56,256]{1,0:T(8,128)S(1)}, f32[64,8192]{1,0:T(...) custom-call(f32[64,8192]{1,0:T(8,128)} %refs_0_.1, s32[8,128]{1,0:T(8,128)} %bitcast.4, s32[64,128]{1,0:T(8,128)} %bitcast.3, ...), custom_call_target="tpu_custom_call" | custom-call | flops 1073741824 | bytes 2097152 | tf_op jit(solution)/shard_map/pallas_call | solution.py:332
  5.1 0.5 %collective-permute-start = (f32[56,256]{1,0:T(8,128)S(1)}, f32[56,256]{1,0:T(8,128)S(1)}, u32[]{:S(2)}, u32[]{:S(2)}) collective-permute-start(f32[56,256]{1,0:T(8,128)S(1)} %get-tuple-element.21), channel_id=1, source_target_pairs={{0,1},{1,0},{2,3},{3,2},{4,5},{5,4},{6,7},{7,6},{8,9},{9,8},{10,11... | collective-permute-start | bytes 172040 | tf_op jit(solution)/shard_map/ppermute | solution.py:285
  5.6 2.6 %collective-permute-start.1 = (f32[56,256]{1,0:T(8,128)S(1)}, f32[56,256]{1,0:T(8,128)S(1)}, u32[]{:S(2)}, u32[]{:S(2)}) collective-permute-start(f32[56,256]{1,0:T(8,128)S(1)} %get-tuple-element.22), channel_id=1, source_target_pairs={{0,2},{1,3},{2,0},{3,1},{4,6},{5,7},{6,4},{7,5},{8,10},{9,11},{10,... | collective-permute-start | bytes 172040 | tf_op jit(solution)/shard_map/ppermute | solution.py:285
  8.2 0.1 collective-permute-start.2
  8.3 1.3 %shard_map.47.refs_4_ = bf16[1,256,512]{2,1,0:T(8,128)(2,1)S(1)} custom-call(f32[56,256]{1,0:T(8,128)S(1)} %get-tuple-element.20.refs_0_), custom_call_target="tpu_custom_call" | custom-call | flops 134217728 | bytes 262144 | tf_op jit(solution)/shard_map/pallas_call | solution.py:353
  9.6 0.0 collective-permute-done.refs_1_.refs_0_
  9.6 1.1 %collective-permute-done.1.refs_2_.refs_1_ = f32[56,256]{1,0:T(8,128)S(1)} collective-permute-done((f32[56,256]{1,0:T(8,128)S(1)}, f32[56,256]{1,0:T(8,128)S(1)}, u32[]{:S(2)}, u32[]{:S(2)}) %collective-permute-start.1) | collective-permute-done | bytes 57376 | tf_op jit(solution)/shard_map/ppermute | solution.py:285
  10.7 1.4 %collective-permute-done.2.refs_3_.refs_2_ = f32[56,256]{1,0:T(8,128)S(1)} collective-permute-done((f32[56,256]{1,0:T(8,128)S(1)}, f32[56,256]{1,0:T(8,128)S(1)}, u32[]{:S(2)}, u32[]{:S(2)}) %collective-permute-start.2) | collective-permute-done | bytes 57376 | tf_op jit(solution)/shard_map/ppermute | solution.py:285
  12.1 3.7 %collective-permute-start.5 = (f32[72,256]{1,0:T(8,128)S(1)}, f32[72,256]{1,0:T(8,128)S(1)}, u32[]{:S(2)}, u32[]{:S(2)}) collective-permute-start(f32[72,256]{1,0:T(8,128)S(1)} %shard_map.48.refs_0_), channel_id=1, source_target_pairs={{0,12},{1,13},{2,14},{3,15},{4,8},{5,9},{6,10},{7,11},{8,4},{9,5},... | collective-permute-start | bytes 221192 | tf_op jit(solution)/shard_map/ppermute | solution.py:290
  15.7 0.0 collective-permute-start.4
  15.7 0.8 %collective-permute-start.3 = (f32[72,256]{1,0:T(8,128)S(1)}, f32[72,256]{1,0:T(8,128)S(1)}, u32[]{:S(2)}, u32[]{:S(2)}) collective-permute-start(f32[72,256]{1,0:T(8,128)S(1)} %shard_map.48.refs_0_), channel_id=1, source_target_pairs={{0,4},{1,5},{2,6},{3,7},{4,0},{5,1},{6,2},{7,3},{8,12},{9,13},{10,... | collective-permute-start | bytes 221192 | tf_op jit(solution)/shard_map/ppermute | solution.py:290
  16.5 3.9 %shard_map.49.refs_5_ = bf16[3,256,512]{2,1,0:T(8,128)(2,1)S(1)} custom-call(f32[56,256]{1,0:T(8,128)S(1)} %collective-permute-done.refs_1_.refs_0_, f32[56,256]{1,0:T(8,128)S(1)} %collective-permute-done.1.refs_2_.refs_1_, f32[56,256]{1,0:T(8,128)S(1)} %collective-permute-done.2.refs_3_.refs_2_), custom_call_target="tpu_custom_call" | custom-call | flops 402653184 | bytes 262144 | tf_op jit(solution)/shard_map/pallas_call | solution.py:353
  20.4 0.0 collective-permute-done.5.refs_3_
  20.4 1.8 %collective-permute-done.4.refs_2_ = f32[72,256]{1,0:T(8,128)S(1)} collective-permute-done((f32[72,256]{1,0:T(8,128)S(1)}, f32[72,256]{1,0:T(8,128)S(1)}, u32[]{:S(2)}, u32[]{:S(2)}) %collective-permute-start.4) | collective-permute-done | bytes 73760 | tf_op jit(solution)/shard_map/ppermute | solution.py:290
  22.2 0.0 collective-permute-done.3.refs_1_
  22.3 1.8 %shard_map.50 = (f32[64,256]{1,0:T(8,128)S(1)}, f32[64,256]{1,0:T(8,128)S(1)}, f32[2,8,512]{2,1,0:T(8,128)S(1)}, bf16[2,512,2048]{2,1,0:T(8,128)(2,1)S(1)}) custom-call(f32[72,256]{1,0:T(8,128)S(1)} %shard_map.48.refs_0_, f32[72,256]{1,0:T(8,128)S(1)} %collective-permute-done.3.refs_1_, f32[72,256]{1,0:T(8,128)S(1)} %collective-permute-done.4.refs_2_, ...), custom_call_target="tpu_custom_call" | custom-call | flops 134217728 | bytes 262144 | tf_op jit(solution)/shard_map/pallas_call | solution.py:378
  24.1 2.5 %collective-permute-start.8 = (f32[64,256]{1,0:T(8,128)S(1)}, f32[64,256]{1,0:T(8,128)S(1)}, u32[]{:S(2)}, u32[]{:S(2)}) collective-permute-start(f32[64,256]{1,0:T(8,128)S(1)} %get-tuple-element.24.refs_0_), channel_id=1, source_target_pairs={{0,12},{1,13},{2,14},{3,15},{4,8},{5,9},{6,10},{7,11},{8,4},{9,5},... | collective-permute-start | bytes 196616 | tf_op jit(solution)/shard_map/ppermute | solution.py:290
  26.6 0.0 collective-permute-start.7
  26.6 1.9 %collective-permute-start.6 = (f32[64,256]{1,0:T(8,128)S(1)}, f32[64,256]{1,0:T(8,128)S(1)}, u32[]{:S(2)}, u32[]{:S(2)}) collective-permute-start(f32[64,256]{1,0:T(8,128)S(1)} %get-tuple-element.24.refs_0_), channel_id=1, source_target_pairs={{0,4},{1,5},{2,6},{3,7},{4,0},{5,1},{6,2},{7,3},{8,12},{9,13},{10,... | collective-permute-start | bytes 196616 | tf_op jit(solution)/shard_map/ppermute | solution.py:290
  28.5 1.7 %collective-permute-done.8.refs_3_ = f32[64,256]{1,0:T(8,128)S(1)} collective-permute-done((f32[64,256]{1,0:T(8,128)S(1)}, f32[64,256]{1,0:T(8,128)S(1)}, u32[]{:S(2)}, u32[]{:S(2)}) %collective-permute-start.8) | collective-permute-done | bytes 65568 | tf_op jit(solution)/shard_map/ppermute | solution.py:290
  30.2 2.7 %collective-permute-done.7.refs_2_ = f32[64,256]{1,0:T(8,128)S(1)} collective-permute-done((f32[64,256]{1,0:T(8,128)S(1)}, f32[64,256]{1,0:T(8,128)S(1)}, u32[]{:S(2)}, u32[]{:S(2)}) %collective-permute-start.7) | collective-permute-done | bytes 65568 | tf_op jit(solution)/shard_map/ppermute | solution.py:290
  32.9 0.0 collective-permute-done.6.refs_1_
  32.9 1.3 %shard_map.51 = (f32[32,256]{1,0:T(8,128)S(1)}, f32[32,256]{1,0:T(8,128)S(1)}, f32[32,256]{1,0:T(8,128)S(1)}, f32[32,256]{1,0:T(8,128)S(1)}) custom-call(f32[64,256]{1,0:T(8,128)S(1)} %get-tuple-element.24.refs_0_, f32[64,256]{1,0:T(8,128)S(1)} %collective-permute-done.6.refs_1_, f32[64,256]{1,0:T(8,128)S(1)} %collective-permute-done.7.refs_2_, ...), custom_call_target="tpu_custom_call" | custom-call | flops 134217728 | bytes 262144 | tf_op jit(solution)/shard_map/pallas_call | solution.py:389
  34.1 0.0 collective-permute-start.9
  34.2 1.3 %collective-permute-start.10 = (f32[32,256]{1,0:T(8,128)S(1)}, f32[32,256]{1,0:T(8,128)S(1)}, u32[]{:S(2)}, u32[]{:S(2)}) collective-permute-start(f32[32,256]{1,0:T(8,128)S(1)} %get-tuple-element.30), channel_id=1, source_target_pairs={{0,2},{1,3},{2,0},{3,1},{4,6},{5,7},{6,4},{7,5},{8,10},{9,11},{10,... | collective-permute-start | bytes 98312 | tf_op jit(solution)/shard_map/ppermute | solution.py:285
  35.5 0.5 %collective-permute-start.11 = (f32[32,256]{1,0:T(8,128)S(1)}, f32[32,256]{1,0:T(8,128)S(1)}, u32[]{:S(2)}, u32[]{:S(2)}) collective-permute-start(f32[32,256]{1,0:T(8,128)S(1)} %get-tuple-element.31), channel_id=1, source_target_pairs={{0,3},{1,2},{2,1},{3,0},{4,7},{5,6},{6,5},{7,4},{8,11},{9,10},{10,... | collective-permute-start | bytes 98312 | tf_op jit(solution)/shard_map/ppermute | solution.py:285
  36.0 0.0 collective-permute-done.9.refs_1_
  36.0 2.1 %collective-permute-done.10.refs_2_ = f32[32,256]{1,0:T(8,128)S(1)} collective-permute-done((f32[32,256]{1,0:T(8,128)S(1)}, f32[32,256]{1,0:T(8,128)S(1)}, u32[]{:S(2)}, u32[]{:S(2)}) %collective-permute-start.10) | collective-permute-done | bytes 32800 | tf_op jit(solution)/shard_map/ppermute | solution.py:285
  38.1 0.7 %collective-permute-done.11.refs_3_ = f32[32,256]{1,0:T(8,128)S(1)} collective-permute-done((f32[32,256]{1,0:T(8,128)S(1)}, f32[32,256]{1,0:T(8,128)S(1)}, u32[]{:S(2)}, u32[]{:S(2)}) %collective-permute-start.11) | collective-permute-done | bytes 32800 | tf_op jit(solution)/shard_map/ppermute | solution.py:285
  38.8 3.1 %shard_map.52 = f32[64,8192]{1,0:T(8,128)} custom-call(f32[32,256]{1,0:T(8,128)S(1)} %get-tuple-element.28.refs_0_, f32[32,256]{1,0:T(8,128)S(1)} %collective-permute-done.9.refs_1_, f32[32,256]{1,0:T(8,128)S(1)} %collective-permute-done.10.refs_2_, f32[32,256]{1,0:T(8,128)S(1)} %collective-permute-done.11.refs_3_, ...), custom_call_target="tpu_custom_call" | custom-call | flops 536870912 | bytes 4194304 | tf_op jit(solution)/shard_map/pallas_call | solution.py:399
  (1 shorter events, 0.0 us)
Async XLA Ops:
  5.1 4.5 %collective-permute-start = (f32[56,256]{1,0:T(8,128)S(1)}, f32[56,256]{1,0:T(8,128)S(1)}, u32[]{:S(2)}, u32[]{:S(2)}) collective-permute-start(f32[56,256]{1,0:T(8,128)S(1)} %get-tuple-element.21), channel_id=1, source_target_pairs={{0,1},{1,0},{2,3},{3,2},{4,5},{5,4},{6,7},{7,6},{8,9},{9,8},{10,11... | collective-permute-start | bytes 172040 | tf_op jit(solution)/shard_map/ppermute | solution.py:285
  5.6 5.1 %collective-permute-start.1 = (f32[56,256]{1,0:T(8,128)S(1)}, f32[56,256]{1,0:T(8,128)S(1)}, u32[]{:S(2)}, u32[]{:S(2)}) collective-permute-start(f32[56,256]{1,0:T(8,128)S(1)} %get-tuple-element.22), channel_id=1, source_target_pairs={{0,2},{1,3},{2,0},{3,1},{4,6},{5,7},{6,4},{7,5},{8,10},{9,11},{10,... | collective-permute-start | bytes 172040 | tf_op jit(solution)/shard_map/ppermute | solution.py:285
  8.2 3.9 %collective-permute-start.2 = (f32[56,256]{1,0:T(8,128)S(1)}, f32[56,256]{1,0:T(8,128)S(1)}, u32[]{:S(2)}, u32[]{:S(2)}) collective-permute-start(f32[56,256]{1,0:T(8,128)S(1)} %get-tuple-element.23), channel_id=1, source_target_pairs={{0,3},{1,2},{2,1},{3,0},{4,7},{5,6},{6,5},{7,4},{8,11},{9,10},{10,... | collective-permute-start | bytes 172040 | tf_op jit(solution)/shard_map/ppermute | solution.py:285
  12.1 8.4 %collective-permute-start.5 = (f32[72,256]{1,0:T(8,128)S(1)}, f32[72,256]{1,0:T(8,128)S(1)}, u32[]{:S(2)}, u32[]{:S(2)}) collective-permute-start(f32[72,256]{1,0:T(8,128)S(1)} %shard_map.48.refs_0_), channel_id=1, source_target_pairs={{0,12},{1,13},{2,14},{3,15},{4,8},{5,9},{6,10},{7,11},{8,4},{9,5},... | collective-permute-start | bytes 221192 | tf_op jit(solution)/shard_map/ppermute | solution.py:290
  15.7 6.5 %collective-permute-start.4 = (f32[72,256]{1,0:T(8,128)S(1)}, f32[72,256]{1,0:T(8,128)S(1)}, u32[]{:S(2)}, u32[]{:S(2)}) collective-permute-start(f32[72,256]{1,0:T(8,128)S(1)} %shard_map.48.refs_0_), channel_id=1, source_target_pairs={{0,8},{1,9},{2,10},{3,11},{4,12},{5,13},{6,14},{7,15},{8,0},{9,1},... | collective-permute-start | bytes 221192 | tf_op jit(solution)/shard_map/ppermute | solution.py:290
  15.7 6.5 %collective-permute-start.3 = (f32[72,256]{1,0:T(8,128)S(1)}, f32[72,256]{1,0:T(8,128)S(1)}, u32[]{:S(2)}, u32[]{:S(2)}) collective-permute-start(f32[72,256]{1,0:T(8,128)S(1)} %shard_map.48.refs_0_), channel_id=1, source_target_pairs={{0,4},{1,5},{2,6},{3,7},{4,0},{5,1},{6,2},{7,3},{8,12},{9,13},{10,... | collective-permute-start | bytes 221192 | tf_op jit(solution)/shard_map/ppermute | solution.py:290
  24.1 6.1 %collective-permute-start.8 = (f32[64,256]{1,0:T(8,128)S(1)}, f32[64,256]{1,0:T(8,128)S(1)}, u32[]{:S(2)}, u32[]{:S(2)}) collective-permute-start(f32[64,256]{1,0:T(8,128)S(1)} %get-tuple-element.24.refs_0_), channel_id=1, source_target_pairs={{0,12},{1,13},{2,14},{3,15},{4,8},{5,9},{6,10},{7,11},{8,4},{9,5},... | collective-permute-start | bytes 196616 | tf_op jit(solution)/shard_map/ppermute | solution.py:290
  26.6 6.3 %collective-permute-start.7 = (f32[64,256]{1,0:T(8,128)S(1)}, f32[64,256]{1,0:T(8,128)S(1)}, u32[]{:S(2)}, u32[]{:S(2)}) collective-permute-start(f32[64,256]{1,0:T(8,128)S(1)} %get-tuple-element.24.refs_0_), channel_id=1, source_target_pairs={{0,8},{1,9},{2,10},{3,11},{4,12},{5,13},{6,14},{7,15},{8,0},{9,1},... | collective-permute-start | bytes 196616 | tf_op jit(solution)/shard_map/ppermute | solution.py:290
  26.6 6.3 %collective-permute-start.6 = (f32[64,256]{1,0:T(8,128)S(1)}, f32[64,256]{1,0:T(8,128)S(1)}, u32[]{:S(2)}, u32[]{:S(2)}) collective-permute-start(f32[64,256]{1,0:T(8,128)S(1)} %get-tuple-element.24.refs_0_), channel_id=1, source_target_pairs={{0,4},{1,5},{2,6},{3,7},{4,0},{5,1},{6,2},{7,3},{8,12},{9,13},{10,... | collective-permute-start | bytes 196616 | tf_op jit(solution)/shard_map/ppermute | solution.py:290
  34.1 1.9 %collective-permute-start.9 = (f32[32,256]{1,0:T(8,128)S(1)}, f32[32,256]{1,0:T(8,128)S(1)}, u32[]{:S(2)}, u32[]{:S(2)}) collective-permute-start(f32[32,256]{1,0:T(8,128)S(1)} %get-tuple-element.29), channel_id=1, source_target_pairs={{0,1},{1,0},{2,3},{3,2},{4,5},{5,4},{6,7},{7,6},{8,9},{9,8},{10,11... | collective-permute-start | bytes 98312 | tf_op jit(solution)/shard_map/ppermute | solution.py:285
  34.2 4.0 %collective-permute-start.10 = (f32[32,256]{1,0:T(8,128)S(1)}, f32[32,256]{1,0:T(8,128)S(1)}, u32[]{:S(2)}, u32[]{:S(2)}) collective-permute-start(f32[32,256]{1,0:T(8,128)S(1)} %get-tuple-element.30), channel_id=1, source_target_pairs={{0,2},{1,3},{2,0},{3,1},{4,6},{5,7},{6,4},{7,5},{8,10},{9,11},{10,... | collective-permute-start | bytes 98312 | tf_op jit(solution)/shard_map/ppermute | solution.py:285
  35.5 3.3 %collective-permute-start.11 = (f32[32,256]{1,0:T(8,128)S(1)}, f32[32,256]{1,0:T(8,128)S(1)}, u32[]{:S(2)}, u32[]{:S(2)}) collective-permute-start(f32[32,256]{1,0:T(8,128)S(1)} %get-tuple-element.31), channel_id=1, source_target_pairs={{0,3},{1,2},{2,1},{3,0},{4,7},{5,6},{6,5},{7,4},{8,11},{9,10},{10,... | collective-permute-start | bytes 98312 | tf_op jit(solution)/shard_map/ppermute | solution.py:285

commit v13 on v12

--- a/solution.py
+++ b/solution.py
@@ -42,6 +42,17 @@
     one, zero = jnp.ones((slots, LANES), kind), jnp.zeros((slots, LANES), kind)
     parts = [jnp.where(slot == ids[:, k : k + LANES], one, zero) for k in range(0, ids.shape[1], LANES)]
     return jnp.concatenate(parts, axis=1).astype(BF16)
+
+
+def one_hot_down(columns, slots):
+    kind = BF16 if slots <= 256 else F32
+    one, zero = jnp.ones((LANES, LANES), kind), jnp.zeros((LANES, LANES), kind)
+    along_slots = [(iota((LANES, LANES), 1) + at).astype(F32).astype(kind) for at in range(0, slots, LANES)]
+    parts = []
+    for k in range(columns.shape[1]):
+        ids = jnp.broadcast_to(columns[:, k : k + 1], (LANES, LANES)).astype(kind)
+        parts.append(jnp.concatenate([jnp.where(slot == ids, one, zero) for slot in along_slots], axis=1))
+    return jnp.concatenate(parts, axis=0).astype(BF16)
 
 
 def same_worker(pad, width):
@@ -108,6 +119,7 @@
     weight[...] = jnp.where(inside, 1.0 / row_len, 0.0)
     masked = jnp.where(inside, ids[...], -1)
     mask_ids[...] = masked
+    turned = jnp.concatenate([masked.astype(F32)] * (LANES // masked.shape[0]), axis=0).T
     keys = (iota((1, slots), 1) // cap * FIRMS_PER_SHARD + along(firms)).astype(F32)
     across = slots // LANES
     rows = ids.shape[0] // across
@@ -124,7 +136,8 @@
         x1[:, b * BLOCK : (b + 1) * BLOCK] = rest
         counted = jnp.broadcast_to(ok, (16, BLOCK)).astype(BF16)
         data = jnp.concatenate([*split(rest), counted], axis=0)
-        block = dot(data, one_hot(row(mask_ids, b, BLOCK), slots), NT)
+        per = BLOCK // LANES
+        block = dot(data, one_hot_down(turned[:, b * per : (b + 1) * per], slots))
         if b == 0:
             acc[...] = block
         else:
@@ -189,13 +202,11 @@
 
 
 def same_firm(parts, part, at):
-    def keys(one, k):
-        return one[part * NEAR + 2 * k : part * NEAR + 2 * k + 1, at]
-
-    down = [jnp.broadcast_to(keys(parts[0], k), (LANES, LANES)).T for k in range(NEAR)]
-    down = jnp.concatenate(down, axis=0)
-    found = [(down == keys(one, k)).astype(F32).astype(BF16) for one in parts for k in range(NEAR)]
-    return jnp.concatenate(found, axis=1)
+    keys = [one[part * NEAR + 2 * k : part * NEAR + 2 * k + 1, at] for one in parts for k in range(NEAR)]
+    mine = jnp.concatenate(keys[:NEAR], axis=1)
+    down = jnp.concatenate(keys, axis=0).T
+    found = [(down[:, k : k + 1] == mine).astype(F32).astype(BF16) for k in range(len(keys))]
+    return jnp.concatenate(found, axis=0)
 
 
 def gathered(parts, part, at):
@@ -229,7 +240,7 @@
         count = jnp.concatenate(count, axis=1)
         high = count.astype(BF16).astype(F32)
         counts = jnp.where(iota((16, count.shape[1]), 0) < 8, high, count - high).astype(BF16)
-        found = dot(jnp.concatenate([gathered(parts, part, at), counts], axis=0), same, NT)
+        found = dot(jnp.concatenate([gathered(parts, part, at), counts], axis=0), same)
         size = found[2 * part : 2 * part + 1] + found[2 * part + 8 : 2 * part + 9]
         inverse = 1.0 / jnp.maximum(size, 1.0)
         scale[t] = jnp.broadcast_to(inverse, scale.shape[1:])
@@ -249,7 +260,7 @@
 
     def tile(t, at):
         same = source[0][t] if len(source) == 1 else same_firm(source, part, at)
-        found = dot(gathered(parts, part, at), same, NT)
+        found = dot(gathered(parts, part, at), same)
         spread_out((found[:part] + found[part:]) * scale[t][:1], second, part, at)
 
     each_tile(mean.shape[1], tile)
@@ -373,7 +384,7 @@
     )(*arrived, own_pairs)
     shared = far_share(joined, n)
     pairs = pair_counts(arrived[1:])
-    table = array((tiles, NEAR * LANES, n * LANES), BF16)
+    table = array((tiles, n * LANES, NEAR * LANES), BF16)
     scale = array((tiles, 8, NEAR * LANES), F32)
     mean, sums, scales, *tables = call(
         functools.partial(change_kernel, far, part),

time: 42.1 us -> 40.5 us (0.962)
  Pallas kernels: 16.5 us -> 15 us
    pallas_call x1, Pallas kernels: 5.07 us -> 4.41 us  [body(): call(functools.partial(sums_kernel, pad, slots // n), [message] * NEAR +...]
    pallas_call x1, Pallas kernels: 1.28 us -> 0.76 us  [body(): call(functools.partial(means_kernel, far, part), [array((2 * part, slots)...]
  transfers between devices with their start and end apart: 12 -> 12, of which waited for: 7 -> 7; matrix products, arithmetic and copies ran while one was open for 0% -> 0% of each run, Pallas kernels for 12% -> 13%
where the time goes in v13:
time: 40.5 us; the launch traced here: 40.4 us
  Pallas kernels  15 us (37%)
  starting transfers between devices  13.9 us (34%)
  waiting for transfers between devices  11.5 us (28%)
    ppermute x6, starting transfers between devices, far_share(): return [one] + [lax.ppermute(one, 'rows', step) for step in steps]  8.85 us
    ppermute x6, waiting for transfers between devices, far_share(): return [one] + [lax.ppermute(one, 'rows', step) for step in steps]  6.21 us
    ppermute x6, waiting for transfers between devices, near_exchange(): lax.ppermute(one, 'rows', step)  5.25 us
    pallas_call x2, Pallas kernels, pair_counts(): call(functools.partial(pairs_kernel, pad, about), array((len(parts), slot...  5.21 us
    ppermute x6, starting transfers between devices, near_exchange(): lax.ppermute(one, 'rows', step)  5.06 us
    pallas_call x1, Pallas kernels, body(): call(functools.partial(sums_kernel, pad, slots // n), [message] * NEAR +...  4.41 us
    pallas_call x1, Pallas kernels, body(): call(functools.partial(last_kernel, pad, part), array(whole, F32), [vmem]...  3.09 us
    pallas_call x1, Pallas kernels, body(): call(functools.partial(change_kernel, far, part), [of_near, of_near, scal...  1.49 us
  transfers between devices with their start and end apart: 12, of which 7 were waited for; matrix products, arithmetic and copies ran while one was open for 0% of the time, Pallas kernels for 13%

profile of v13, /device:TPU:0, one launch (start us, length us, event | category | flops | bytes accessed | tf_op | source)
XLA Modules:
  0.0 40.4 jit_solution(5896430408891040283)
XLA Ops:
  0.0 4.4 %shard_map.46 = (f32[56,256]{1,0:T(8,128)S(1)}, f32[56,256]{1,0:T(8,128)S(1)}, f32[56,256]{1,0:T(8,128)S(1)}, f32[56,256]{1,0:T(8,128)S(1)}, f32[64,8192]{1,0:T(...) custom-call(f32[64,8192]{1,0:T(8,128)} %refs_0_.1, s32[8,128]{1,0:T(8,128)} %bitcast.4, s32[64,128]{1,0:T(8,128)} %bitcast.3, ...), custom_call_target="tpu_custom_call" | custom-call | flops 1073741824 | bytes 2097152 | tf_op jit(solution)/shard_map/pallas_call | solution.py:343
  4.4 0.5 %collective-permute-start = (f32[56,256]{1,0:T(8,128)S(1)}, f32[56,256]{1,0:T(8,128)S(1)}, u32[]{:S(2)}, u32[]{:S(2)}) collective-permute-start(f32[56,256]{1,0:T(8,128)S(1)} %get-tuple-element.21), channel_id=1, source_target_pairs={{0,1},{1,0},{2,3},{3,2},{4,5},{5,4},{6,7},{7,6},{8,9},{9,8},{10,11... | collective-permute-start | bytes 172040 | tf_op jit(solution)/shard_map/ppermute | solution.py:296
  4.9 2.6 %collective-permute-start.1 = (f32[56,256]{1,0:T(8,128)S(1)}, f32[56,256]{1,0:T(8,128)S(1)}, u32[]{:S(2)}, u32[]{:S(2)}) collective-permute-start(f32[56,256]{1,0:T(8,128)S(1)} %get-tuple-element.22), channel_id=1, source_target_pairs={{0,2},{1,3},{2,0},{3,1},{4,6},{5,7},{6,4},{7,5},{8,10},{9,11},{10,... | collective-permute-start | bytes 172040 | tf_op jit(solution)/shard_map/ppermute | solution.py:296
  7.5 0.1 collective-permute-start.2
  7.6 1.3 %shard_map.47.refs_4_ = bf16[1,256,512]{2,1,0:T(8,128)(2,1)S(1)} custom-call(f32[56,256]{1,0:T(8,128)S(1)} %get-tuple-element.20.refs_0_), custom_call_target="tpu_custom_call" | custom-call | flops 134217728 | bytes 262144 | tf_op jit(solution)/shard_map/pallas_call | solution.py:364
  8.9 0.0 collective-permute-done.refs_1_.refs_0_
  8.9 1.1 %collective-permute-done.1.refs_2_.refs_1_ = f32[56,256]{1,0:T(8,128)S(1)} collective-permute-done((f32[56,256]{1,0:T(8,128)S(1)}, f32[56,256]{1,0:T(8,128)S(1)}, u32[]{:S(2)}, u32[]{:S(2)}) %collective-permute-start.1) | collective-permute-done | bytes 57376 | tf_op jit(solution)/shard_map/ppermute | solution.py:296
  10.0 1.4 %collective-permute-done.2.refs_3_.refs_2_ = f32[56,256]{1,0:T(8,128)S(1)} collective-permute-done((f32[56,256]{1,0:T(8,128)S(1)}, f32[56,256]{1,0:T(8,128)S(1)}, u32[]{:S(2)}, u32[]{:S(2)}) %collective-permute-start.2) | collective-permute-done | bytes 57376 | tf_op jit(solution)/shard_map/ppermute | solution.py:296
  11.4 3.7 %collective-permute-start.5 = (f32[72,256]{1,0:T(8,128)S(1)}, f32[72,256]{1,0:T(8,128)S(1)}, u32[]{:S(2)}, u32[]{:S(2)}) collective-permute-start(f32[72,256]{1,0:T(8,128)S(1)} %shard_map.48.refs_0_), channel_id=1, source_target_pairs={{0,12},{1,13},{2,14},{3,15},{4,8},{5,9},{6,10},{7,11},{8,4},{9,5},... | collective-permute-start | bytes 221192 | tf_op jit(solution)/shard_map/ppermute | solution.py:301
  15.1 0.0 collective-permute-start.4
  15.1 0.8 %collective-permute-start.3 = (f32[72,256]{1,0:T(8,128)S(1)}, f32[72,256]{1,0:T(8,128)S(1)}, u32[]{:S(2)}, u32[]{:S(2)}) collective-permute-start(f32[72,256]{1,0:T(8,128)S(1)} %shard_map.48.refs_0_), channel_id=1, source_target_pairs={{0,4},{1,5},{2,6},{3,7},{4,0},{5,1},{6,2},{7,3},{8,12},{9,13},{10,... | collective-permute-start | bytes 221192 | tf_op jit(solution)/shard_map/ppermute | solution.py:301
  15.9 3.9 %shard_map.49.refs_5_ = bf16[3,256,512]{2,1,0:T(8,128)(2,1)S(1)} custom-call(f32[56,256]{1,0:T(8,128)S(1)} %collective-permute-done.refs_1_.refs_0_, f32[56,256]{1,0:T(8,128)S(1)} %collective-permute-done.1.refs_2_.refs_1_, f32[56,256]{1,0:T(8,128)S(1)} %collective-permute-done.2.refs_3_.refs_2_), custom_call_target="tpu_custom_call" | custom-call | flops 402653184 | bytes 262144 | tf_op jit(solution)/shard_map/pallas_call | solution.py:364
  19.8 0.0 collective-permute-done.5.refs_3_
  19.8 1.8 %collective-permute-done.4.refs_2_ = f32[72,256]{1,0:T(8,128)S(1)} collective-permute-done((f32[72,256]{1,0:T(8,128)S(1)}, f32[72,256]{1,0:T(8,128)S(1)}, u32[]{:S(2)}, u32[]{:S(2)}) %collective-permute-start.4) | collective-permute-done | bytes 73760 | tf_op jit(solution)/shard_map/ppermute | solution.py:301
  21.6 0.0 collective-permute-done.3.refs_1_
  21.6 1.5 %shard_map.50 = (f32[64,256]{1,0:T(8,128)S(1)}, f32[64,256]{1,0:T(8,128)S(1)}, f32[2,8,512]{2,1,0:T(8,128)S(1)}, bf16[2,2048,512]{2,1,0:T(8,128)(2,1)S(1)}) custom-call(f32[72,256]{1,0:T(8,128)S(1)} %shard_map.48.refs_0_, f32[72,256]{1,0:T(8,128)S(1)} %collective-permute-done.3.refs_1_, f32[72,256]{1,0:T(8,128)S(1)} %collective-permute-done.4.refs_2_, ...), custom_call_target="tpu_custom_call" | custom-call | flops 134217728 | bytes 262144 | tf_op jit(solution)/shard_map/pallas_call | solution.py:389
  23.1 2.5 %collective-permute-start.8 = (f32[64,256]{1,0:T(8,128)S(1)}, f32[64,256]{1,0:T(8,128)S(1)}, u32[]{:S(2)}, u32[]{:S(2)}) collective-permute-start(f32[64,256]{1,0:T(8,128)S(1)} %get-tuple-element.24.refs_0_), channel_id=1, source_target_pairs={{0,12},{1,13},{2,14},{3,15},{4,8},{5,9},{6,10},{7,11},{8,4},{9,5},... | collective-permute-start | bytes 196616 | tf_op jit(solution)/shard_map/ppermute | solution.py:301
  25.6 0.0 collective-permute-start.7
  25.6 1.9 %collective-permute-start.6 = (f32[64,256]{1,0:T(8,128)S(1)}, f32[64,256]{1,0:T(8,128)S(1)}, u32[]{:S(2)}, u32[]{:S(2)}) collective-permute-start(f32[64,256]{1,0:T(8,128)S(1)} %get-tuple-element.24.refs_0_), channel_id=1, source_target_pairs={{0,4},{1,5},{2,6},{3,7},{4,0},{5,1},{6,2},{7,3},{8,12},{9,13},{10,... | collective-permute-start | bytes 196616 | tf_op jit(solution)/shard_map/ppermute | solution.py:301
  27.5 1.7 %collective-permute-done.8.refs_3_ = f32[64,256]{1,0:T(8,128)S(1)} collective-permute-done((f32[64,256]{1,0:T(8,128)S(1)}, f32[64,256]{1,0:T(8,128)S(1)}, u32[]{:S(2)}, u32[]{:S(2)}) %collective-permute-start.8) | collective-permute-done | bytes 65568 | tf_op jit(solution)/shard_map/ppermute | solution.py:301
  29.2 2.7 %collective-permute-done.7.refs_2_ = f32[64,256]{1,0:T(8,128)S(1)} collective-permute-done((f32[64,256]{1,0:T(8,128)S(1)}, f32[64,256]{1,0:T(8,128)S(1)}, u32[]{:S(2)}, u32[]{:S(2)}) %collective-permute-start.7) | collective-permute-done | bytes 65568 | tf_op jit(solution)/shard_map/ppermute | solution.py:301
  31.9 0.0 collective-permute-done.6.refs_1_
  31.9 0.8 %shard_map.51 = (f32[32,256]{1,0:T(8,128)S(1)}, f32[32,256]{1,0:T(8,128)S(1)}, f32[32,256]{1,0:T(8,128)S(1)}, f32[32,256]{1,0:T(8,128)S(1)}) custom-call(f32[64,256]{1,0:T(8,128)S(1)} %get-tuple-element.24.refs_0_, f32[64,256]{1,0:T(8,128)S(1)} %collective-permute-done.6.refs_1_, f32[64,256]{1,0:T(8,128)S(1)} %collective-permute-done.7.refs_2_, ...), custom_call_target="tpu_custom_call" | custom-call | flops 134217728 | bytes 262144 | tf_op jit(solution)/shard_map/pallas_call | solution.py:400
  32.6 0.0 collective-permute-start.9
  32.6 1.3 %collective-permute-start.10 = (f32[32,256]{1,0:T(8,128)S(1)}, f32[32,256]{1,0:T(8,128)S(1)}, u32[]{:S(2)}, u32[]{:S(2)}) collective-permute-start(f32[32,256]{1,0:T(8,128)S(1)} %get-tuple-element.30), channel_id=1, source_target_pairs={{0,2},{1,3},{2,0},{3,1},{4,6},{5,7},{6,4},{7,5},{8,10},{9,11},{10,... | collective-permute-start | bytes 98312 | tf_op jit(solution)/shard_map/ppermute | solution.py:296
  34.0 0.5 %collective-permute-start.11 = (f32[32,256]{1,0:T(8,128)S(1)}, f32[32,256]{1,0:T(8,128)S(1)}, u32[]{:S(2)}, u32[]{:S(2)}) collective-permute-start(f32[32,256]{1,0:T(8,128)S(1)} %get-tuple-element.31), channel_id=1, source_target_pairs={{0,3},{1,2},{2,1},{3,0},{4,7},{5,6},{6,5},{7,4},{8,11},{9,10},{10,... | collective-permute-start | bytes 98312 | tf_op jit(solution)/shard_map/ppermute | solution.py:296
  34.5 0.0 collective-permute-done.9.refs_1_
  34.5 2.1 %collective-permute-done.10.refs_2_ = f32[32,256]{1,0:T(8,128)S(1)} collective-permute-done((f32[32,256]{1,0:T(8,128)S(1)}, f32[32,256]{1,0:T(8,128)S(1)}, u32[]{:S(2)}, u32[]{:S(2)}) %collective-permute-start.10) | collective-permute-done | bytes 32800 | tf_op jit(solution)/shard_map/ppermute | solution.py:296
  36.6 0.7 %collective-permute-done.11.refs_3_ = f32[32,256]{1,0:T(8,128)S(1)} collective-permute-done((f32[32,256]{1,0:T(8,128)S(1)}, f32[32,256]{1,0:T(8,128)S(1)}, u32[]{:S(2)}, u32[]{:S(2)}) %collective-permute-start.11) | collective-permute-done | bytes 32800 | tf_op jit(solution)/shard_map/ppermute | solution.py:296
  37.3 3.1 %shard_map.52 = f32[64,8192]{1,0:T(8,128)} custom-call(f32[32,256]{1,0:T(8,128)S(1)} %get-tuple-element.28.refs_0_, f32[32,256]{1,0:T(8,128)S(1)} %collective-permute-done.9.refs_1_, f32[32,256]{1,0:T(8,128)S(1)} %collective-permute-done.10.refs_2_, f32[32,256]{1,0:T(8,128)S(1)} %collective-permute-done.11.refs_3_, ...), custom_call_target="tpu_custom_call" | custom-call | flops 536870912 | bytes 4194304 | tf_op jit(solution)/shard_map/pallas_call | solution.py:410
  (1 shorter events, 0.0 us)
Async XLA Ops:
  4.4 4.5 %collective-permute-start = (f32[56,256]{1,0:T(8,128)S(1)}, f32[56,256]{1,0:T(8,128)S(1)}, u32[]{:S(2)}, u32[]{:S(2)}) collective-permute-start(f32[56,256]{1,0:T(8,128)S(1)} %get-tuple-element.21), channel_id=1, source_target_pairs={{0,1},{1,0},{2,3},{3,2},{4,5},{5,4},{6,7},{7,6},{8,9},{9,8},{10,11... | collective-permute-start | bytes 172040 | tf_op jit(solution)/shard_map/ppermute | solution.py:296
  4.9 5.1 %collective-permute-start.1 = (f32[56,256]{1,0:T(8,128)S(1)}, f32[56,256]{1,0:T(8,128)S(1)}, u32[]{:S(2)}, u32[]{:S(2)}) collective-permute-start(f32[56,256]{1,0:T(8,128)S(1)} %get-tuple-element.22), channel_id=1, source_target_pairs={{0,2},{1,3},{2,0},{3,1},{4,6},{5,7},{6,4},{7,5},{8,10},{9,11},{10,... | collective-permute-start | bytes 172040 | tf_op jit(solution)/shard_map/ppermute | solution.py:296
  7.5 3.9 %collective-permute-start.2 = (f32[56,256]{1,0:T(8,128)S(1)}, f32[56,256]{1,0:T(8,128)S(1)}, u32[]{:S(2)}, u32[]{:S(2)}) collective-permute-start(f32[56,256]{1,0:T(8,128)S(1)} %get-tuple-element.23), channel_id=1, source_target_pairs={{0,3},{1,2},{2,1},{3,0},{4,7},{5,6},{6,5},{7,4},{8,11},{9,10},{10,... | collective-permute-start | bytes 172040 | tf_op jit(solution)/shard_map/ppermute | solution.py:296
  11.4 8.4 %collective-permute-start.5 = (f32[72,256]{1,0:T(8,128)S(1)}, f32[72,256]{1,0:T(8,128)S(1)}, u32[]{:S(2)}, u32[]{:S(2)}) collective-permute-start(f32[72,256]{1,0:T(8,128)S(1)} %shard_map.48.refs_0_), channel_id=1, source_target_pairs={{0,12},{1,13},{2,14},{3,15},{4,8},{5,9},{6,10},{7,11},{8,4},{9,5},... | collective-permute-start | bytes 221192 | tf_op jit(solution)/shard_map/ppermute | solution.py:301
  15.1 6.5 %collective-permute-start.4 = (f32[72,256]{1,0:T(8,128)S(1)}, f32[72,256]{1,0:T(8,128)S(1)}, u32[]{:S(2)}, u32[]{:S(2)}) collective-permute-start(f32[72,256]{1,0:T(8,128)S(1)} %shard_map.48.refs_0_), channel_id=1, source_target_pairs={{0,8},{1,9},{2,10},{3,11},{4,12},{5,13},{6,14},{7,15},{8,0},{9,1},... | collective-permute-start | bytes 221192 | tf_op jit(solution)/shard_map/ppermute | solution.py:301
  15.1 6.5 %collective-permute-start.3 = (f32[72,256]{1,0:T(8,128)S(1)}, f32[72,256]{1,0:T(8,128)S(1)}, u32[]{:S(2)}, u32[]{:S(2)}) collective-permute-start(f32[72,256]{1,0:T(8,128)S(1)} %shard_map.48.refs_0_), channel_id=1, source_target_pairs={{0,4},{1,5},{2,6},{3,7},{4,0},{5,1},{6,2},{7,3},{8,12},{9,13},{10,... | collective-permute-start | bytes 221192 | tf_op jit(solution)/shard_map/ppermute | solution.py:301
  23.1 6.1 %collective-permute-start.8 = (f32[64,256]{1,0:T(8,128)S(1)}, f32[64,256]{1,0:T(8,128)S(1)}, u32[]{:S(2)}, u32[]{:S(2)}) collective-permute-start(f32[64,256]{1,0:T(8,128)S(1)} %get-tuple-element.24.refs_0_), channel_id=1, source_target_pairs={{0,12},{1,13},{2,14},{3,15},{4,8},{5,9},{6,10},{7,11},{8,4},{9,5},... | collective-permute-start | bytes 196616 | tf_op jit(solution)/shard_map/ppermute | solution.py:301
  25.6 6.3 %collective-permute-start.7 = (f32[64,256]{1,0:T(8,128)S(1)}, f32[64,256]{1,0:T(8,128)S(1)}, u32[]{:S(2)}, u32[]{:S(2)}) collective-permute-start(f32[64,256]{1,0:T(8,128)S(1)} %get-tuple-element.24.refs_0_), channel_id=1, source_target_pairs={{0,8},{1,9},{2,10},{3,11},{4,12},{5,13},{6,14},{7,15},{8,0},{9,1},... | collective-permute-start | bytes 196616 | tf_op jit(solution)/shard_map/ppermute | solution.py:301
  25.6 6.3 %collective-permute-start.6 = (f32[64,256]{1,0:T(8,128)S(1)}, f32[64,256]{1,0:T(8,128)S(1)}, u32[]{:S(2)}, u32[]{:S(2)}) collective-permute-start(f32[64,256]{1,0:T(8,128)S(1)} %get-tuple-element.24.refs_0_), channel_id=1, source_target_pairs={{0,4},{1,5},{2,6},{3,7},{4,0},{5,1},{6,2},{7,3},{8,12},{9,13},{10,... | collective-permute-start | bytes 196616 | tf_op jit(solution)/shard_map/ppermute | solution.py:301
  32.6 1.9 %collective-permute-start.9 = (f32[32,256]{1,0:T(8,128)S(1)}, f32[32,256]{1,0:T(8,128)S(1)}, u32[]{:S(2)}, u32[]{:S(2)}) collective-permute-start(f32[32,256]{1,0:T(8,128)S(1)} %get-tuple-element.29), channel_id=1, source_target_pairs={{0,1},{1,0},{2,3},{3,2},{4,5},{5,4},{6,7},{7,6},{8,9},{9,8},{10,11... | collective-permute-start | bytes 98312 | tf_op jit(solution)/shard_map/ppermute | solution.py:296
  32.6 4.0 %collective-permute-start.10 = (f32[32,256]{1,0:T(8,128)S(1)}, f32[32,256]{1,0:T(8,128)S(1)}, u32[]{:S(2)}, u32[]{:S(2)}) collective-permute-start(f32[32,256]{1,0:T(8,128)S(1)} %get-tuple-element.30), channel_id=1, source_target_pairs={{0,2},{1,3},{2,0},{3,1},{4,6},{5,7},{6,4},{7,5},{8,10},{9,11},{10,... | collective-permute-start | bytes 98312 | tf_op jit(solution)/shard_map/ppermute | solution.py:296
  34.0 3.3 %collective-permute-start.11 = (f32[32,256]{1,0:T(8,128)S(1)}, f32[32,256]{1,0:T(8,128)S(1)}, u32[]{:S(2)}, u32[]{:S(2)}) collective-permute-start(f32[32,256]{1,0:T(8,128)S(1)} %get-tuple-element.31), channel_id=1, source_target_pairs={{0,3},{1,2},{2,1},{3,0},{4,7},{5,6},{6,5},{7,4},{8,11},{9,10},{10,... | collective-permute-start | bytes 98312 | tf_op jit(solution)/shard_map/ppermute | solution.py:296

commit v14 on v13

--- a/solution.py
+++ b/solution.py
@@ -55,17 +55,18 @@
     return jnp.concatenate(parts, axis=0).astype(BF16)
 
 
-def same_worker(pad, width):
-    return (iota((width, width), 0) // pad == iota((width, width), 1) // pad).astype(F32).astype(BF16)
-
-
-def by_worker(x, table):
-    rows, width = x.shape
-    hi, lo = split(x)
-    both = jnp.concatenate([hi, lo], axis=0)
-    step = table.shape[0]
-    total = jnp.concatenate([dot(both[:, k : k + step], table) for k in range(0, width, step)], axis=1)
-    return total[:rows] + total[rows:]
+def by_worker(x, pad):
+    parts = []
+    steps = [1 << k for k in range(pad.bit_length() - 1)]
+    for at in range(0, x.shape[1], LANES):
+        part = x[:, at : at + LANES]
+        for step in steps:
+            part += pltpu.roll(part, LANES - step, axis=1)
+        part = jnp.where(iota(part.shape, 1) % pad == 0, part, 0.0)
+        for step in steps:
+            part += pltpu.roll(part, step, axis=1)
+        parts.append(part)
+    return jnp.concatenate(parts, axis=1)
 
 
 def start_all(copies):
@@ -127,12 +128,11 @@
     for send in sends:
         send[part + 8 :] = masked
 
-    table = same_worker(pad, 256)
     for b in range(len(copies)):
         copies[b].wait()
         ok = row(valid, b, BLOCK)
         x0 = x[:, b * BLOCK : (b + 1) * BLOCK] * ok
-        rest = x0 - by_worker(x0, table) * row(weight, b, BLOCK)
+        rest = x0 - by_worker(x0, pad) * row(weight, b, BLOCK)
         x1[:, b * BLOCK : (b + 1) * BLOCK] = rest
         counted = jnp.broadcast_to(ok, (16, BLOCK)).astype(BF16)
         data = jnp.concatenate([*split(rest), counted], axis=0)
@@ -280,13 +280,12 @@
         means[0, at, :] = one[:part]
         means[1, at, :] = one[part:]
     both = jnp.concatenate([*split(means[0]), *split(means[1])], axis=0)
-    table = same_worker(pad, 256)
     for b in range(len(outs)):
         at = slice(b * BLOCK, (b + 1) * BLOCK)
         found = dot(both, one_hot(row(mask_ids, b, BLOCK), slots))
         first = found[:columns] + found[columns : 2 * columns]
         total = found[2 * columns : 3 * columns] + found[3 * columns :]
-        y[:, at] = x1[:, at] - total + by_worker(first, table) * row(weight, b, BLOCK)
+        y[:, at] = x1[:, at] - total + by_worker(first, pad) * row(weight, b, BLOCK)
         outs[b].start()
     wait_all(outs)
 

time: 40.5 us -> 63.9 us (1.58)
  Pallas kernels: 15 us -> 38.2 us
    pallas_call x1, Pallas kernels: 3.09 us -> 18.8 us  [body(): call(functools.partial(last_kernel, pad, part), array(whole, F32), [vmem]...]
    pallas_call x1, Pallas kernels: 4.41 us -> 12 us  [body(): call(functools.partial(sums_kernel, pad, slots // n), [message] * NEAR +...]
  transfers between devices with their start and end apart: 12 -> 12, of which waited for: 7 -> 7; matrix products, arithmetic and copies ran while one was open for 0% -> 0% of each run, Pallas kernels for 13% -> 8%
where the time goes in v14:
time: 63.9 us; the launch traced here: 63.8 us
  Pallas kernels  38.2 us (60%)
  starting transfers between devices  13.9 us (22%)
  waiting for transfers between devices  11.4 us (18%)
    pallas_call x1, Pallas kernels, body(): call(functools.partial(last_kernel, pad, part), array(whole, F32), [vmem]...  18.8 us
    pallas_call x1, Pallas kernels, body(): call(functools.partial(sums_kernel, pad, slots // n), [message] * NEAR +...  12 us
    ppermute x6, starting transfers between devices, far_share(): return [one] + [lax.ppermute(one, 'rows', step) for step in steps]  8.85 us
    ppermute x6, waiting for transfers between devices, far_share(): return [one] + [lax.ppermute(one, 'rows', step) for step in steps]  6.2 us
    ppermute x6, waiting for transfers between devices, near_exchange(): lax.ppermute(one, 'rows', step)  5.25 us
    pallas_call x2, Pallas kernels, pair_counts(): call(functools.partial(pairs_kernel, pad, about), array((len(parts), slot...  5.22 us
    ppermute x6, starting transfers between devices, near_exchange(): lax.ppermute(one, 'rows', step)  5.06 us
    pallas_call x1, Pallas kernels, body(): call(functools.partial(change_kernel, far, part), [of_near, of_near, scal...  1.49 us
  transfers between devices with their start and end apart: 12, of which 7 were waited for; matrix products, arithmetic and copies ran while one was open for 0% of the time, Pallas kernels for 8%

profile of v14, /device:TPU:0, one launch (start us, length us, event | category | flops | bytes accessed | tf_op | source)
XLA Modules:
  0.0 63.8 jit_solution(16194154445014105482)
XLA Ops:
  0.0 12.0 %shard_map.46 = (f32[56,256]{1,0:T(8,128)S(1)}, f32[56,256]{1,0:T(8,128)S(1)}, f32[56,256]{1,0:T(8,128)S(1)}, f32[56,256]{1,0:T(8,128)S(1)}, f32[64,8192]{1,0:T(...) custom-call(f32[64,8192]{1,0:T(8,128)} %refs_0_.1, s32[8,128]{1,0:T(8,128)} %bitcast.4, s32[64,128]{1,0:T(8,128)} %bitcast.3, ...), custom_call_target="tpu_custom_call" | custom-call | flops 1073741824 | bytes 2097152 | tf_op jit(solution)/shard_map/pallas_call | solution.py:342
  12.0 0.5 collective-permute-start
  12.5 2.6 %collective-permute-start.1 = (f32[56,256]{1,0:T(8,128)S(1)}, f32[56,256]{1,0:T(8,128)S(1)}, u32[]{:S(2)}, u32[]{:S(2)}) collective-permute-start(f32[56,256]{1,0:T(8,128)S(1)} %get-tuple-element.22), channel_id=1, source_target_pairs={{0,2},{1,3},{2,0},{3,1},{4,6},{5,7},{6,4},{7,5},{8,10},{9,11},{10,... | collective-permute-start | bytes 172040 | tf_op jit(solution)/shard_map/ppermute | solution.py:295
  15.1 0.1 collective-permute-start.2
  15.2 1.3 %shard_map.47.refs_4_ = bf16[1,256,512]{2,1,0:T(8,128)(2,1)S(1)} custom-call(f32[56,256]{1,0:T(8,128)S(1)} %get-tuple-element.20.refs_0_), custom_call_target="tpu_custom_call" | custom-call | flops 134217728 | bytes 262144 | tf_op jit(solution)/shard_map/pallas_call | solution.py:363
  16.5 0.0 collective-permute-done.refs_1_.refs_0_
  16.5 1.1 %collective-permute-done.1.refs_2_.refs_1_ = f32[56,256]{1,0:T(8,128)S(1)} collective-permute-done((f32[56,256]{1,0:T(8,128)S(1)}, f32[56,256]{1,0:T(8,128)S(1)}, u32[]{:S(2)}, u32[]{:S(2)}) %collective-permute-start.1) | collective-permute-done | bytes 57376 | tf_op jit(solution)/shard_map/ppermute | solution.py:295
  17.6 1.4 %collective-permute-done.2.refs_3_.refs_2_ = f32[56,256]{1,0:T(8,128)S(1)} collective-permute-done((f32[56,256]{1,0:T(8,128)S(1)}, f32[56,256]{1,0:T(8,128)S(1)}, u32[]{:S(2)}, u32[]{:S(2)}) %collective-permute-start.2) | collective-permute-done | bytes 57376 | tf_op jit(solution)/shard_map/ppermute | solution.py:295
  19.0 3.7 %collective-permute-start.5 = (f32[72,256]{1,0:T(8,128)S(1)}, f32[72,256]{1,0:T(8,128)S(1)}, u32[]{:S(2)}, u32[]{:S(2)}) collective-permute-start(f32[72,256]{1,0:T(8,128)S(1)} %shard_map.48.refs_0_), channel_id=1, source_target_pairs={{0,12},{1,13},{2,14},{3,15},{4,8},{5,9},{6,10},{7,11},{8,4},{9,5},... | collective-permute-start | bytes 221192 | tf_op jit(solution)/shard_map/ppermute | solution.py:300
  22.6 0.0 collective-permute-start.4
  22.6 0.8 %collective-permute-start.3 = (f32[72,256]{1,0:T(8,128)S(1)}, f32[72,256]{1,0:T(8,128)S(1)}, u32[]{:S(2)}, u32[]{:S(2)}) collective-permute-start(f32[72,256]{1,0:T(8,128)S(1)} %shard_map.48.refs_0_), channel_id=1, source_target_pairs={{0,4},{1,5},{2,6},{3,7},{4,0},{5,1},{6,2},{7,3},{8,12},{9,13},{10,... | collective-permute-start | bytes 221192 | tf_op jit(solution)/shard_map/ppermute | solution.py:300
  23.4 3.9 %shard_map.49.refs_5_ = bf16[3,256,512]{2,1,0:T(8,128)(2,1)S(1)} custom-call(f32[56,256]{1,0:T(8,128)S(1)} %collective-permute-done.refs_1_.refs_0_, f32[56,256]{1,0:T(8,128)S(1)} %collective-permute-done.1.refs_2_.refs_1_, f32[56,256]{1,0:T(8,128)S(1)} %collective-permute-done.2.refs_3_.refs_2_), custom_call_target="tpu_custom_call" | custom-call | flops 402653184 | bytes 262144 | tf_op jit(solution)/shard_map/pallas_call | solution.py:363
  27.3 0.0 collective-permute-done.5.refs_3_
  27.3 1.8 %collective-permute-done.4.refs_2_ = f32[72,256]{1,0:T(8,128)S(1)} collective-permute-done((f32[72,256]{1,0:T(8,128)S(1)}, f32[72,256]{1,0:T(8,128)S(1)}, u32[]{:S(2)}, u32[]{:S(2)}) %collective-permute-start.4) | collective-permute-done | bytes 73760 | tf_op jit(solution)/shard_map/ppermute | solution.py:300
  29.1 0.0 collective-permute-done.3.refs_1_
  29.1 1.5 %shard_map.50 = (f32[64,256]{1,0:T(8,128)S(1)}, f32[64,256]{1,0:T(8,128)S(1)}, f32[2,8,512]{2,1,0:T(8,128)S(1)}, bf16[2,2048,512]{2,1,0:T(8,128)(2,1)S(1)}) custom-call(f32[72,256]{1,0:T(8,128)S(1)} %shard_map.48.refs_0_, f32[72,256]{1,0:T(8,128)S(1)} %collective-permute-done.3.refs_1_, f32[72,256]{1,0:T(8,128)S(1)} %collective-permute-done.4.refs_2_, ...), custom_call_target="tpu_custom_call" | custom-call | flops 134217728 | bytes 262144 | tf_op jit(solution)/shard_map/pallas_call | solution.py:388
  30.6 2.5 %collective-permute-start.8 = (f32[64,256]{1,0:T(8,128)S(1)}, f32[64,256]{1,0:T(8,128)S(1)}, u32[]{:S(2)}, u32[]{:S(2)}) collective-permute-start(f32[64,256]{1,0:T(8,128)S(1)} %get-tuple-element.24.refs_0_), channel_id=1, source_target_pairs={{0,12},{1,13},{2,14},{3,15},{4,8},{5,9},{6,10},{7,11},{8,4},{9,5},... | collective-permute-start | bytes 196616 | tf_op jit(solution)/shard_map/ppermute | solution.py:300
  33.1 0.0 collective-permute-start.7
  33.1 1.9 %collective-permute-start.6 = (f32[64,256]{1,0:T(8,128)S(1)}, f32[64,256]{1,0:T(8,128)S(1)}, u32[]{:S(2)}, u32[]{:S(2)}) collective-permute-start(f32[64,256]{1,0:T(8,128)S(1)} %get-tuple-element.24.refs_0_), channel_id=1, source_target_pairs={{0,4},{1,5},{2,6},{3,7},{4,0},{5,1},{6,2},{7,3},{8,12},{9,13},{10,... | collective-permute-start | bytes 196616 | tf_op jit(solution)/shard_map/ppermute | solution.py:300
  35.0 1.7 %collective-permute-done.8.refs_3_ = f32[64,256]{1,0:T(8,128)S(1)} collective-permute-done((f32[64,256]{1,0:T(8,128)S(1)}, f32[64,256]{1,0:T(8,128)S(1)}, u32[]{:S(2)}, u32[]{:S(2)}) %collective-permute-start.8) | collective-permute-done | bytes 65568 | tf_op jit(solution)/shard_map/ppermute | solution.py:300
  36.7 2.7 %collective-permute-done.7.refs_2_ = f32[64,256]{1,0:T(8,128)S(1)} collective-permute-done((f32[64,256]{1,0:T(8,128)S(1)}, f32[64,256]{1,0:T(8,128)S(1)}, u32[]{:S(2)}, u32[]{:S(2)}) %collective-permute-start.7) | collective-permute-done | bytes 65568 | tf_op jit(solution)/shard_map/ppermute | solution.py:300
  39.4 0.0 collective-permute-done.6.refs_1_
  39.4 0.8 %shard_map.51 = (f32[32,256]{1,0:T(8,128)S(1)}, f32[32,256]{1,0:T(8,128)S(1)}, f32[32,256]{1,0:T(8,128)S(1)}, f32[32,256]{1,0:T(8,128)S(1)}) custom-call(f32[64,256]{1,0:T(8,128)S(1)} %get-tuple-element.24.refs_0_, f32[64,256]{1,0:T(8,128)S(1)} %collective-permute-done.6.refs_1_, f32[64,256]{1,0:T(8,128)S(1)} %collective-permute-done.7.refs_2_, ...), custom_call_target="tpu_custom_call" | custom-call | flops 134217728 | bytes 262144 | tf_op jit(solution)/shard_map/pallas_call | solution.py:399
  40.2 0.0 collective-permute-start.9
  40.2 1.3 %collective-permute-start.10 = (f32[32,256]{1,0:T(8,128)S(1)}, f32[32,256]{1,0:T(8,128)S(1)}, u32[]{:S(2)}, u32[]{:S(2)}) collective-permute-start(f32[32,256]{1,0:T(8,128)S(1)} %get-tuple-element.30), channel_id=1, source_target_pairs={{0,2},{1,3},{2,0},{3,1},{4,6},{5,7},{6,4},{7,5},{8,10},{9,11},{10,... | collective-permute-start | bytes 98312 | tf_op jit(solution)/shard_map/ppermute | solution.py:295
  41.5 0.6 collective-permute-start.11
  42.1 0.0 collective-permute-done.9.refs_1_
  42.1 2.1 %collective-permute-done.10.refs_2_ = f32[32,256]{1,0:T(8,128)S(1)} collective-permute-done((f32[32,256]{1,0:T(8,128)S(1)}, f32[32,256]{1,0:T(8,128)S(1)}, u32[]{:S(2)}, u32[]{:S(2)}) %collective-permute-start.10) | collective-permute-done | bytes 32800 | tf_op jit(solution)/shard_map/ppermute | solution.py:295
  44.2 0.7 %collective-permute-done.11.refs_3_ = f32[32,256]{1,0:T(8,128)S(1)} collective-permute-done((f32[32,256]{1,0:T(8,128)S(1)}, f32[32,256]{1,0:T(8,128)S(1)}, u32[]{:S(2)}, u32[]{:S(2)}) %collective-permute-start.11) | collective-permute-done | bytes 32800 | tf_op jit(solution)/shard_map/ppermute | solution.py:295
  44.9 18.8 %shard_map.52 = f32[64,8192]{1,0:T(8,128)} custom-call(f32[32,256]{1,0:T(8,128)S(1)} %get-tuple-element.28.refs_0_, f32[32,256]{1,0:T(8,128)S(1)} %collective-permute-done.9.refs_1_, f32[32,256]{1,0:T(8,128)S(1)} %collective-permute-done.10.refs_2_, f32[32,256]{1,0:T(8,128)S(1)} %collective-permute-done.11.refs_3_, ...), custom_call_target="tpu_custom_call" | custom-call | flops 536870912 | bytes 4194304 | tf_op jit(solution)/shard_map/pallas_call | solution.py:409
  (1 shorter events, 0.0 us)
Async XLA Ops:
  12.0 4.5 %collective-permute-start = (f32[56,256]{1,0:T(8,128)S(1)}, f32[56,256]{1,0:T(8,128)S(1)}, u32[]{:S(2)}, u32[]{:S(2)}) collective-permute-start(f32[56,256]{1,0:T(8,128)S(1)} %get-tuple-element.21), channel_id=1, source_target_pairs={{0,1},{1,0},{2,3},{3,2},{4,5},{5,4},{6,7},{7,6},{8,9},{9,8},{10,11... | collective-permute-start | bytes 172040 | tf_op jit(solution)/shard_map/ppermute | solution.py:295
  12.5 5.1 %collective-permute-start.1 = (f32[56,256]{1,0:T(8,128)S(1)}, f32[56,256]{1,0:T(8,128)S(1)}, u32[]{:S(2)}, u32[]{:S(2)}) collective-permute-start(f32[56,256]{1,0:T(8,128)S(1)} %get-tuple-element.22), channel_id=1, source_target_pairs={{0,2},{1,3},{2,0},{3,1},{4,6},{5,7},{6,4},{7,5},{8,10},{9,11},{10,... | collective-permute-start | bytes 172040 | tf_op jit(solution)/shard_map/ppermute | solution.py:295
  15.1 3.9 %collective-permute-start.2 = (f32[56,256]{1,0:T(8,128)S(1)}, f32[56,256]{1,0:T(8,128)S(1)}, u32[]{:S(2)}, u32[]{:S(2)}) collective-permute-start(f32[56,256]{1,0:T(8,128)S(1)} %get-tuple-element.23), channel_id=1, source_target_pairs={{0,3},{1,2},{2,1},{3,0},{4,7},{5,6},{6,5},{7,4},{8,11},{9,10},{10,... | collective-permute-start | bytes 172040 | tf_op jit(solution)/shard_map/ppermute | solution.py:295
  19.0 8.4 %collective-permute-start.5 = (f32[72,256]{1,0:T(8,128)S(1)}, f32[72,256]{1,0:T(8,128)S(1)}, u32[]{:S(2)}, u32[]{:S(2)}) collective-permute-start(f32[72,256]{1,0:T(8,128)S(1)} %shard_map.48.refs_0_), channel_id=1, source_target_pairs={{0,12},{1,13},{2,14},{3,15},{4,8},{5,9},{6,10},{7,11},{8,4},{9,5},... | collective-permute-start | bytes 221192 | tf_op jit(solution)/shard_map/ppermute | solution.py:300
  22.6 6.5 %collective-permute-start.4 = (f32[72,256]{1,0:T(8,128)S(1)}, f32[72,256]{1,0:T(8,128)S(1)}, u32[]{:S(2)}, u32[]{:S(2)}) collective-permute-start(f32[72,256]{1,0:T(8,128)S(1)} %shard_map.48.refs_0_), channel_id=1, source_target_pairs={{0,8},{1,9},{2,10},{3,11},{4,12},{5,13},{6,14},{7,15},{8,0},{9,1},... | collective-permute-start | bytes 221192 | tf_op jit(solution)/shard_map/ppermute | solution.py:300
  22.6 6.5 %collective-permute-start.3 = (f32[72,256]{1,0:T(8,128)S(1)}, f32[72,256]{1,0:T(8,128)S(1)}, u32[]{:S(2)}, u32[]{:S(2)}) collective-permute-start(f32[72,256]{1,0:T(8,128)S(1)} %shard_map.48.refs_0_), channel_id=1, source_target_pairs={{0,4},{1,5},{2,6},{3,7},{4,0},{5,1},{6,2},{7,3},{8,12},{9,13},{10,... | collective-permute-start | bytes 221192 | tf_op jit(solution)/shard_map/ppermute | solution.py:300
  30.6 6.1 %collective-permute-start.8 = (f32[64,256]{1,0:T(8,128)S(1)}, f32[64,256]{1,0:T(8,128)S(1)}, u32[]{:S(2)}, u32[]{:S(2)}) collective-permute-start(f32[64,256]{1,0:T(8,128)S(1)} %get-tuple-element.24.refs_0_), channel_id=1, source_target_pairs={{0,12},{1,13},{2,14},{3,15},{4,8},{5,9},{6,10},{7,11},{8,4},{9,5},... | collective-permute-start | bytes 196616 | tf_op jit(solution)/shard_map/ppermute | solution.py:300
  33.1 6.3 %collective-permute-start.7 = (f32[64,256]{1,0:T(8,128)S(1)}, f32[64,256]{1,0:T(8,128)S(1)}, u32[]{:S(2)}, u32[]{:S(2)}) collective-permute-start(f32[64,256]{1,0:T(8,128)S(1)} %get-tuple-element.24.refs_0_), channel_id=1, source_target_pairs={{0,8},{1,9},{2,10},{3,11},{4,12},{5,13},{6,14},{7,15},{8,0},{9,1},... | collective-permute-start | bytes 196616 | tf_op jit(solution)/shard_map/ppermute | solution.py:300
  33.1 6.3 %collective-permute-start.6 = (f32[64,256]{1,0:T(8,128)S(1)}, f32[64,256]{1,0:T(8,128)S(1)}, u32[]{:S(2)}, u32[]{:S(2)}) collective-permute-start(f32[64,256]{1,0:T(8,128)S(1)} %get-tuple-element.24.refs_0_), channel_id=1, source_target_pairs={{0,4},{1,5},{2,6},{3,7},{4,0},{5,1},{6,2},{7,3},{8,12},{9,13},{10,... | collective-permute-start | bytes 196616 | tf_op jit(solution)/shard_map/ppermute | solution.py:300
  40.2 1.9 %collective-permute-start.9 = (f32[32,256]{1,0:T(8,128)S(1)}, f32[32,256]{1,0:T(8,128)S(1)}, u32[]{:S(2)}, u32[]{:S(2)}) collective-permute-start(f32[32,256]{1,0:T(8,128)S(1)} %get-tuple-element.29), channel_id=1, source_target_pairs={{0,1},{1,0},{2,3},{3,2},{4,5},{5,4},{6,7},{7,6},{8,9},{9,8},{10,11... | collective-permute-start | bytes 98312 | tf_op jit(solution)/shard_map/ppermute | solution.py:295
  40.2 4.0 %collective-permute-start.10 = (f32[32,256]{1,0:T(8,128)S(1)}, f32[32,256]{1,0:T(8,128)S(1)}, u32[]{:S(2)}, u32[]{:S(2)}) collective-permute-start(f32[32,256]{1,0:T(8,128)S(1)} %get-tuple-element.30), channel_id=1, source_target_pairs={{0,2},{1,3},{2,0},{3,1},{4,6},{5,7},{6,4},{7,5},{8,10},{9,11},{10,... | collective-permute-start | bytes 98312 | tf_op jit(solution)/shard_map/ppermute | solution.py:295
  41.5 3.3 %collective-permute-start.11 = (f32[32,256]{1,0:T(8,128)S(1)}, f32[32,256]{1,0:T(8,128)S(1)}, u32[]{:S(2)}, u32[]{:S(2)}) collective-permute-start(f32[32,256]{1,0:T(8,128)S(1)} %get-tuple-element.31), channel_id=1, source_target_pairs={{0,3},{1,2},{2,1},{3,0},{4,7},{5,6},{6,5},{7,4},{8,11},{9,10},{10,... | collective-permute-start | bytes 98312 | tf_op jit(solution)/shard_map/ppermute | solution.py:295

commit v15 on v13

--- a/solution.py
+++ b/solution.py
@@ -256,7 +256,7 @@
 
 
 def means_kernel(far, part, *refs):
-    parts, source, (scale, mean), sends, second = refs[:far], refs[far:-7], refs[-7:-5], refs[-5:-1], refs[-1]
+    parts, source, (scale, mean), sends, second = refs[:far], refs[far:-8], refs[-8:-6], refs[-5:-1], refs[-1]
 
     def tile(t, at):
         same = source[0][t] if len(source) == 1 else same_firm(source, part, at)
@@ -270,8 +270,19 @@
         send[part:] = mean[cut] + second[cut]
 
 
+def tables_kernel(pad, mask_ids, after, spread, workers):
+    slots, width = spread.shape
+    table = same_worker(pad, 256)
+    for b in range(width // BLOCK):
+        found = one_hot(row(mask_ids, b, BLOCK), slots)
+        spread[:, b * BLOCK : (b + 1) * BLOCK] = found
+        for at in range(0, BLOCK, 256):
+            count = dot(found[:, at : at + 256], table)
+            workers[:, b * BLOCK + at : b * BLOCK + at + 256] = count.astype(BF16)
+
+
 def last_kernel(pad, part, *refs):
-    parts, (x1, mask_ids, weight, out, means, y, sems) = refs[:NEAR], refs[NEAR:]
+    parts, (x1, mask_ids, weight), tables, (out, means, y, sems) = refs[:NEAR], refs[NEAR : NEAR + 3], refs[NEAR + 3 : -4], refs[-4:]
     outs = column_copies(y, out, sems)
     me = lax.axis_index("rows") % NEAR
     columns, slots = means.shape[1:]
@@ -279,14 +290,19 @@
         at = pl.ds(pl.multiple_of((me ^ k) * part, part), part)
         means[0, at, :] = one[:part]
         means[1, at, :] = one[part:]
-    both = jnp.concatenate([*split(means[0]), *split(means[1])], axis=0)
+    first, total = (jnp.concatenate(split(means[k]), axis=0) for k in range(2))
     table = same_worker(pad, 256)
     for b in range(len(outs)):
         at = slice(b * BLOCK, (b + 1) * BLOCK)
-        found = dot(both, one_hot(row(mask_ids, b, BLOCK), slots))
-        first = found[:columns] + found[columns : 2 * columns]
-        total = found[2 * columns : 3 * columns] + found[3 * columns :]
-        y[:, at] = x1[:, at] - total + by_worker(first, table) * row(weight, b, BLOCK)
+        if tables:
+            spread = dot(total, tables[0][:, at])
+            worker = dot(first, tables[1][:, at])
+            worker = worker[:columns] + worker[columns:]
+        else:
+            found = one_hot(row(mask_ids, b, BLOCK), slots)
+            spread, worker = dot(total, found), dot(first, found)
+            worker = by_worker(worker[:columns] + worker[columns:], table)
+        y[:, at] = x1[:, at] - (spread[:columns] + spread[columns:]) + worker * row(weight, b, BLOCK)
         outs[b].start()
     wait_all(outs)
 
@@ -397,25 +413,36 @@
     )(*shared, own_pairs, pairs)
     again = far_share(sums, n)
     source = tables if keep else shared
+    spreads = []
+    if keep:
+        spreads = call(
+            functools.partial(tables_kernel, pad),
+            [array((slots, rows_dev), BF16)] * 2,
+            [vmem] * 2,
+            [vmem] * 2,
+            [],
+            work,
+            4 * slots * rows_dev,
+        )(mask_ids, scales)
     sends = call(
         functools.partial(means_kernel, far, part),
         [array((2 * part, slots), F32)] * NEAR,
-        [vmem] * (far + len(source) + 2),
+        [vmem] * (far + len(source) + 3),
         [vmem] * NEAR,
         [pltpu.VMEM((columns, slots), F32)],
         work // 4,
         slots * slots * 4,
-    )(*again, *source, scales, mean)
+    )(*again, *source, scales, mean, spreads[1] if keep else mean)
     arrived = near_exchange(sends, n)
     return call(
         functools.partial(last_kernel, pad, part),
         array(whole, F32),
-        [vmem] * (NEAR + 3),
+        [vmem] * (NEAR + 3 + len(spreads)),
         hbm,
         [pltpu.VMEM((2, columns, slots), F32), pltpu.VMEM(whole, F32), sems],
         work,
         8 * columns * rows_dev,
-    )(*arrived, x1, mask_ids, weight)
+    )(*arrived, x1, mask_ids, weight, *spreads)
 
 
 def solution(mesh):

time: 40.5 us -> 39.5 us (0.975)
  waiting for transfers between devices: 11.5 us -> 10.2 us
    ppermute x6, waiting for transfers between devices: 6.21 us -> 4.92 us  [far_share(): return [one] + [lax.ppermute(one, 'rows', step) for step in steps]]
    pallas_call x0 -> x1, Pallas kernels: none -> 1.28 us  [body(): call(functools.partial(tables_kernel, pad), [array((slots, rows_dev), BF1...]
    pallas_call x1, Pallas kernels: 3.09 us -> 2.09 us  [body(): call(functools.partial(last_kernel, pad, part), array(whole, F32), [vmem]...]
  transfers between devices with their start and end apart: 12 -> 12, of which waited for: 7 -> 7; matrix products, arithmetic and copies ran while one was open for 0% -> 0% of each run, Pallas kernels for 13% -> 16%
where the time goes in v15:
time: 39.5 us; the launch traced here: 39.4 us
  Pallas kernels  15.3 us (39%)
  starting transfers between devices  13.9 us (35%)
  waiting for transfers between devices  10.2 us (26%)
    ppermute x6, starting transfers between devices, far_share(): return [one] + [lax.ppermute(one, 'rows', step) for step in steps]  8.85 us
    ppermute x6, waiting for transfers between devices, near_exchange(): lax.ppermute(one, 'rows', step)  5.26 us
    pallas_call x2, Pallas kernels, pair_counts(): call(functools.partial(pairs_kernel, pad, about), array((len(parts), slot...  5.22 us
    ppermute x6, starting transfers between devices, near_exchange(): lax.ppermute(one, 'rows', step)  5.06 us
    ppermute x6, waiting for transfers between devices, far_share(): return [one] + [lax.ppermute(one, 'rows', step) for step in steps]  4.92 us
    pallas_call x1, Pallas kernels, body(): call(functools.partial(sums_kernel, pad, slots // n), [message] * NEAR +...  4.42 us
    pallas_call x1, Pallas kernels, body(): call(functools.partial(last_kernel, pad, part), array(whole, F32), [vmem]...  2.09 us
    pallas_call x1, Pallas kernels, body(): call(functools.partial(change_kernel, far, part), [of_near, of_near, scal...  1.49 us
  transfers between devices with their start and end apart: 12, of which 7 were waited for; matrix products, arithmetic and copies ran while one was open for 0% of the time, Pallas kernels for 16%

profile of v15, /device:TPU:0, one launch (start us, length us, event | category | flops | bytes accessed | tf_op | source)
XLA Modules:
  0.0 39.4 jit_solution(2469775099321431535)
XLA Ops:
  0.0 4.4 %shard_map.46 = (f32[56,256]{1,0:T(8,128)S(1)}, f32[56,256]{1,0:T(8,128)S(1)}, f32[56,256]{1,0:T(8,128)S(1)}, f32[56,256]{1,0:T(8,128)S(1)}, f32[64,8192]{1,0:T(...) custom-call(f32[64,8192]{1,0:T(8,128)} %refs_0_.1, s32[8,128]{1,0:T(8,128)} %bitcast.4, s32[64,128]{1,0:T(8,128)} %bitcast.3, ...), custom_call_target="tpu_custom_call" | custom-call | flops 1073741824 | bytes 2097152 | tf_op jit(solution)/shard_map/pallas_call | solution.py:359
  4.4 0.5 %collective-permute-start = (f32[56,256]{1,0:T(8,128)S(1)}, f32[56,256]{1,0:T(8,128)S(1)}, u32[]{:S(2)}, u32[]{:S(2)}) collective-permute-start(f32[56,256]{1,0:T(8,128)S(1)} %get-tuple-element.23), channel_id=1, source_target_pairs={{0,1},{1,0},{2,3},{3,2},{4,5},{5,4},{6,7},{7,6},{8,9},{9,8},{10,11... | collective-permute-start | bytes 172040 | tf_op jit(solution)/shard_map/ppermute | solution.py:312
  4.9 2.6 %collective-permute-start.1 = (f32[56,256]{1,0:T(8,128)S(1)}, f32[56,256]{1,0:T(8,128)S(1)}, u32[]{:S(2)}, u32[]{:S(2)}) collective-permute-start(f32[56,256]{1,0:T(8,128)S(1)} %get-tuple-element.24), channel_id=1, source_target_pairs={{0,2},{1,3},{2,0},{3,1},{4,6},{5,7},{6,4},{7,5},{8,10},{9,11},{10,... | collective-permute-start | bytes 172040 | tf_op jit(solution)/shard_map/ppermute | solution.py:312
  7.5 0.1 collective-permute-start.2
  7.6 1.3 %shard_map.47.refs_4_ = bf16[1,256,512]{2,1,0:T(8,128)(2,1)S(1)} custom-call(f32[56,256]{1,0:T(8,128)S(1)} %get-tuple-element.22.refs_0_), custom_call_target="tpu_custom_call" | custom-call | flops 134217728 | bytes 262144 | tf_op jit(solution)/shard_map/pallas_call | solution.py:380
  8.9 0.0 collective-permute-done.refs_1_.refs_0_
  8.9 1.1 %collective-permute-done.1.refs_2_.refs_1_ = f32[56,256]{1,0:T(8,128)S(1)} collective-permute-done((f32[56,256]{1,0:T(8,128)S(1)}, f32[56,256]{1,0:T(8,128)S(1)}, u32[]{:S(2)}, u32[]{:S(2)}) %collective-permute-start.1) | collective-permute-done | bytes 57376 | tf_op jit(solution)/shard_map/ppermute | solution.py:312
  10.0 1.4 %collective-permute-done.2.refs_3_.refs_2_ = f32[56,256]{1,0:T(8,128)S(1)} collective-permute-done((f32[56,256]{1,0:T(8,128)S(1)}, f32[56,256]{1,0:T(8,128)S(1)}, u32[]{:S(2)}, u32[]{:S(2)}) %collective-permute-start.2) | collective-permute-done | bytes 57376 | tf_op jit(solution)/shard_map/ppermute | solution.py:312
  11.4 3.7 %collective-permute-start.5 = (f32[72,256]{1,0:T(8,128)S(1)}, f32[72,256]{1,0:T(8,128)S(1)}, u32[]{:S(2)}, u32[]{:S(2)}) collective-permute-start(f32[72,256]{1,0:T(8,128)S(1)} %shard_map.48.refs_0_), channel_id=1, source_target_pairs={{0,12},{1,13},{2,14},{3,15},{4,8},{5,9},{6,10},{7,11},{8,4},{9,5},... | collective-permute-start | bytes 221192 | tf_op jit(solution)/shard_map/ppermute | solution.py:317
  15.1 0.0 collective-permute-start.4
  15.1 0.8 %collective-permute-start.3 = (f32[72,256]{1,0:T(8,128)S(1)}, f32[72,256]{1,0:T(8,128)S(1)}, u32[]{:S(2)}, u32[]{:S(2)}) collective-permute-start(f32[72,256]{1,0:T(8,128)S(1)} %shard_map.48.refs_0_), channel_id=1, source_target_pairs={{0,4},{1,5},{2,6},{3,7},{4,0},{5,1},{6,2},{7,3},{8,12},{9,13},{10,... | collective-permute-start | bytes 221192 | tf_op jit(solution)/shard_map/ppermute | solution.py:317
  15.9 3.9 %shard_map.49.refs_5_ = bf16[3,256,512]{2,1,0:T(8,128)(2,1)S(1)} custom-call(f32[56,256]{1,0:T(8,128)S(1)} %collective-permute-done.refs_1_.refs_0_, f32[56,256]{1,0:T(8,128)S(1)} %collective-permute-done.1.refs_2_.refs_1_, f32[56,256]{1,0:T(8,128)S(1)} %collective-permute-done.2.refs_3_.refs_2_), custom_call_target="tpu_custom_call" | custom-call | flops 402653184 | bytes 262144 | tf_op jit(solution)/shard_map/pallas_call | solution.py:380
  19.8 0.0 collective-permute-done.5.refs_3_
  19.8 1.8 %collective-permute-done.4.refs_2_ = f32[72,256]{1,0:T(8,128)S(1)} collective-permute-done((f32[72,256]{1,0:T(8,128)S(1)}, f32[72,256]{1,0:T(8,128)S(1)}, u32[]{:S(2)}, u32[]{:S(2)}) %collective-permute-start.4) | collective-permute-done | bytes 73760 | tf_op jit(solution)/shard_map/ppermute | solution.py:317
  21.6 0.0 collective-permute-done.3.refs_1_
  21.6 1.5 %shard_map.50 = (f32[64,256]{1,0:T(8,128)S(1)}, f32[64,256]{1,0:T(8,128)S(1)}, f32[2,8,512]{2,1,0:T(8,128)S(1)}, bf16[2,2048,512]{2,1,0:T(8,128)(2,1)S(1)}) custom-call(f32[72,256]{1,0:T(8,128)S(1)} %shard_map.48.refs_0_, f32[72,256]{1,0:T(8,128)S(1)} %collective-permute-done.3.refs_1_, f32[72,256]{1,0:T(8,128)S(1)} %collective-permute-done.4.refs_2_, ...), custom_call_target="tpu_custom_call" | custom-call | flops 134217728 | bytes 262144 | tf_op jit(solution)/shard_map/pallas_call | solution.py:405
  23.1 2.5 %collective-permute-start.8 = (f32[64,256]{1,0:T(8,128)S(1)}, f32[64,256]{1,0:T(8,128)S(1)}, u32[]{:S(2)}, u32[]{:S(2)}) collective-permute-start(f32[64,256]{1,0:T(8,128)S(1)} %get-tuple-element.26.refs_0_), channel_id=1, source_target_pairs={{0,12},{1,13},{2,14},{3,15},{4,8},{5,9},{6,10},{7,11},{8,4},{9,5},... | collective-permute-start | bytes 196616 | tf_op jit(solution)/shard_map/ppermute | solution.py:317
  25.6 0.0 collective-permute-start.7
  25.6 1.9 %collective-permute-start.6 = (f32[64,256]{1,0:T(8,128)S(1)}, f32[64,256]{1,0:T(8,128)S(1)}, u32[]{:S(2)}, u32[]{:S(2)}) collective-permute-start(f32[64,256]{1,0:T(8,128)S(1)} %get-tuple-element.26.refs_0_), channel_id=1, source_target_pairs={{0,4},{1,5},{2,6},{3,7},{4,0},{5,1},{6,2},{7,3},{8,12},{9,13},{10,... | collective-permute-start | bytes 196616 | tf_op jit(solution)/shard_map/ppermute | solution.py:317
  27.5 1.3 %shard_map.51 = (bf16[256,8192]{1,0:T(8,128)(2,1)S(1)}, bf16[256,8192]{1,0:T(8,128)(2,1)S(1)}) custom-call(s32[64,128]{1,0:T(8,128)S(1)} %get-tuple-element.30.mask_ids.refs_5_, f32[2,8,512]{2,1,0:T(8,128)S(1)} %get-tuple-element.28.after.refs_5_), custom_call_target="tpu_custom_call" | custom-call | flops 536870912 | bytes 8388608 | tf_op jit(solution)/shard_map/pallas_call | solution.py:418
  28.8 0.4 collective-permute-done.8.refs_3_
  29.2 2.7 %collective-permute-done.7.refs_2_ = f32[64,256]{1,0:T(8,128)S(1)} collective-permute-done((f32[64,256]{1,0:T(8,128)S(1)}, f32[64,256]{1,0:T(8,128)S(1)}, u32[]{:S(2)}, u32[]{:S(2)}) %collective-permute-start.7) | collective-permute-done | bytes 65568 | tf_op jit(solution)/shard_map/ppermute | solution.py:317
  31.9 0.0 collective-permute-done.6.refs_1_
  31.9 0.8 %shard_map.52 = (f32[32,256]{1,0:T(8,128)S(1)}, f32[32,256]{1,0:T(8,128)S(1)}, f32[32,256]{1,0:T(8,128)S(1)}, f32[32,256]{1,0:T(8,128)S(1)}) custom-call(f32[64,256]{1,0:T(8,128)S(1)} %get-tuple-element.26.refs_0_, f32[64,256]{1,0:T(8,128)S(1)} %collective-permute-done.6.refs_1_, f32[64,256]{1,0:T(8,128)S(1)} %collective-permute-done.7.refs_2_, ...), custom_call_target="tpu_custom_call" | custom-call | flops 134217728 | bytes 262144 | tf_op jit(solution)/shard_map/pallas_call | solution.py:427
  32.6 0.0 collective-permute-start.9
  32.6 1.3 %collective-permute-start.10 = (f32[32,256]{1,0:T(8,128)S(1)}, f32[32,256]{1,0:T(8,128)S(1)}, u32[]{:S(2)}, u32[]{:S(2)}) collective-permute-start(f32[32,256]{1,0:T(8,128)S(1)} %get-tuple-element.34), channel_id=1, source_target_pairs={{0,2},{1,3},{2,0},{3,1},{4,6},{5,7},{6,4},{7,5},{8,10},{9,11},{10,... | collective-permute-start | bytes 98312 | tf_op jit(solution)/shard_map/ppermute | solution.py:312
  34.0 0.5 %collective-permute-start.11 = (f32[32,256]{1,0:T(8,128)S(1)}, f32[32,256]{1,0:T(8,128)S(1)}, u32[]{:S(2)}, u32[]{:S(2)}) collective-permute-start(f32[32,256]{1,0:T(8,128)S(1)} %get-tuple-element.35), channel_id=1, source_target_pairs={{0,3},{1,2},{2,1},{3,0},{4,7},{5,6},{6,5},{7,4},{8,11},{9,10},{10,... | collective-permute-start | bytes 98312 | tf_op jit(solution)/shard_map/ppermute | solution.py:312
  34.5 0.0 collective-permute-done.9.refs_1_
  34.5 2.1 %collective-permute-done.10.refs_2_ = f32[32,256]{1,0:T(8,128)S(1)} collective-permute-done((f32[32,256]{1,0:T(8,128)S(1)}, f32[32,256]{1,0:T(8,128)S(1)}, u32[]{:S(2)}, u32[]{:S(2)}) %collective-permute-start.10) | collective-permute-done | bytes 32800 | tf_op jit(solution)/shard_map/ppermute | solution.py:312
  36.6 0.7 %collective-permute-done.11.refs_3_ = f32[32,256]{1,0:T(8,128)S(1)} collective-permute-done((f32[32,256]{1,0:T(8,128)S(1)}, f32[32,256]{1,0:T(8,128)S(1)}, u32[]{:S(2)}, u32[]{:S(2)}) %collective-permute-start.11) | collective-permute-done | bytes 32800 | tf_op jit(solution)/shard_map/ppermute | solution.py:312
  37.3 2.1 %shard_map.53 = f32[64,8192]{1,0:T(8,128)} custom-call(f32[32,256]{1,0:T(8,128)S(1)} %get-tuple-element.32.refs_0_, f32[32,256]{1,0:T(8,128)S(1)} %collective-permute-done.9.refs_1_, f32[32,256]{1,0:T(8,128)S(1)} %collective-permute-done.10.refs_2_, f32[32,256]{1,0:T(8,128)S(1)} %collective-permute-done.11.refs_3_, ...), custom_call_target="tpu_custom_call" | custom-call | flops 536870912 | bytes 4194304 | tf_op jit(solution)/shard_map/pallas_call | solution.py:437
  (1 shorter events, 0.0 us)
Async XLA Ops:
  4.4 4.5 %collective-permute-start = (f32[56,256]{1,0:T(8,128)S(1)}, f32[56,256]{1,0:T(8,128)S(1)}, u32[]{:S(2)}, u32[]{:S(2)}) collective-permute-start(f32[56,256]{1,0:T(8,128)S(1)} %get-tuple-element.23), channel_id=1, source_target_pairs={{0,1},{1,0},{2,3},{3,2},{4,5},{5,4},{6,7},{7,6},{8,9},{9,8},{10,11... | collective-permute-start | bytes 172040 | tf_op jit(solution)/shard_map/ppermute | solution.py:312
  4.9 5.1 %collective-permute-start.1 = (f32[56,256]{1,0:T(8,128)S(1)}, f32[56,256]{1,0:T(8,128)S(1)}, u32[]{:S(2)}, u32[]{:S(2)}) collective-permute-start(f32[56,256]{1,0:T(8,128)S(1)} %get-tuple-element.24), channel_id=1, source_target_pairs={{0,2},{1,3},{2,0},{3,1},{4,6},{5,7},{6,4},{7,5},{8,10},{9,11},{10,... | collective-permute-start | bytes 172040 | tf_op jit(solution)/shard_map/ppermute | solution.py:312
  7.5 3.9 %collective-permute-start.2 = (f32[56,256]{1,0:T(8,128)S(1)}, f32[56,256]{1,0:T(8,128)S(1)}, u32[]{:S(2)}, u32[]{:S(2)}) collective-permute-start(f32[56,256]{1,0:T(8,128)S(1)} %get-tuple-element.25), channel_id=1, source_target_pairs={{0,3},{1,2},{2,1},{3,0},{4,7},{5,6},{6,5},{7,4},{8,11},{9,10},{10,... | collective-permute-start | bytes 172040 | tf_op jit(solution)/shard_map/ppermute | solution.py:312
  11.4 8.4 %collective-permute-start.5 = (f32[72,256]{1,0:T(8,128)S(1)}, f32[72,256]{1,0:T(8,128)S(1)}, u32[]{:S(2)}, u32[]{:S(2)}) collective-permute-start(f32[72,256]{1,0:T(8,128)S(1)} %shard_map.48.refs_0_), channel_id=1, source_target_pairs={{0,12},{1,13},{2,14},{3,15},{4,8},{5,9},{6,10},{7,11},{8,4},{9,5},... | collective-permute-start | bytes 221192 | tf_op jit(solution)/shard_map/ppermute | solution.py:317
  15.1 6.5 %collective-permute-start.4 = (f32[72,256]{1,0:T(8,128)S(1)}, f32[72,256]{1,0:T(8,128)S(1)}, u32[]{:S(2)}, u32[]{:S(2)}) collective-permute-start(f32[72,256]{1,0:T(8,128)S(1)} %shard_map.48.refs_0_), channel_id=1, source_target_pairs={{0,8},{1,9},{2,10},{3,11},{4,12},{5,13},{6,14},{7,15},{8,0},{9,1},... | collective-permute-start | bytes 221192 | tf_op jit(solution)/shard_map/ppermute | solution.py:317
  15.1 6.5 %collective-permute-start.3 = (f32[72,256]{1,0:T(8,128)S(1)}, f32[72,256]{1,0:T(8,128)S(1)}, u32[]{:S(2)}, u32[]{:S(2)}) collective-permute-start(f32[72,256]{1,0:T(8,128)S(1)} %shard_map.48.refs_0_), channel_id=1, source_target_pairs={{0,4},{1,5},{2,6},{3,7},{4,0},{5,1},{6,2},{7,3},{8,12},{9,13},{10,... | collective-permute-start | bytes 221192 | tf_op jit(solution)/shard_map/ppermute | solution.py:317
  23.1 6.1 %collective-permute-start.8 = (f32[64,256]{1,0:T(8,128)S(1)}, f32[64,256]{1,0:T(8,128)S(1)}, u32[]{:S(2)}, u32[]{:S(2)}) collective-permute-start(f32[64,256]{1,0:T(8,128)S(1)} %get-tuple-element.26.refs_0_), channel_id=1, source_target_pairs={{0,12},{1,13},{2,14},{3,15},{4,8},{5,9},{6,10},{7,11},{8,4},{9,5},... | collective-permute-start | bytes 196616 | tf_op jit(solution)/shard_map/ppermute | solution.py:317
  25.6 6.3 %collective-permute-start.7 = (f32[64,256]{1,0:T(8,128)S(1)}, f32[64,256]{1,0:T(8,128)S(1)}, u32[]{:S(2)}, u32[]{:S(2)}) collective-permute-start(f32[64,256]{1,0:T(8,128)S(1)} %get-tuple-element.26.refs_0_), channel_id=1, source_target_pairs={{0,8},{1,9},{2,10},{3,11},{4,12},{5,13},{6,14},{7,15},{8,0},{9,1},... | collective-permute-start | bytes 196616 | tf_op jit(solution)/shard_map/ppermute | solution.py:317
  25.6 6.3 %collective-permute-start.6 = (f32[64,256]{1,0:T(8,128)S(1)}, f32[64,256]{1,0:T(8,128)S(1)}, u32[]{:S(2)}, u32[]{:S(2)}) collective-permute-start(f32[64,256]{1,0:T(8,128)S(1)} %get-tuple-element.26.refs_0_), channel_id=1, source_target_pairs={{0,4},{1,5},{2,6},{3,7},{4,0},{5,1},{6,2},{7,3},{8,12},{9,13},{10,... | collective-permute-start | bytes 196616 | tf_op jit(solution)/shard_map/ppermute | solution.py:317
  32.6 1.9 %collective-permute-start.9 = (f32[32,256]{1,0:T(8,128)S(1)}, f32[32,256]{1,0:T(8,128)S(1)}, u32[]{:S(2)}, u32[]{:S(2)}) collective-permute-start(f32[32,256]{1,0:T(8,128)S(1)} %get-tuple-element.33), channel_id=1, source_target_pairs={{0,1},{1,0},{2,3},{3,2},{4,5},{5,4},{6,7},{7,6},{8,9},{9,8},{10,11... | collective-permute-start | bytes 98312 | tf_op jit(solution)/shard_map/ppermute | solution.py:312
  32.6 4.0 %collective-permute-start.10 = (f32[32,256]{1,0:T(8,128)S(1)}, f32[32,256]{1,0:T(8,128)S(1)}, u32[]{:S(2)}, u32[]{:S(2)}) collective-permute-start(f32[32,256]{1,0:T(8,128)S(1)} %get-tuple-element.34), channel_id=1, source_target_pairs={{0,2},{1,3},{2,0},{3,1},{4,6},{5,7},{6,4},{7,5},{8,10},{9,11},{10,... | collective-permute-start | bytes 98312 | tf_op jit(solution)/shard_map/ppermute | solution.py:312
  34.0 3.3 %collective-permute-start.11 = (f32[32,256]{1,0:T(8,128)S(1)}, f32[32,256]{1,0:T(8,128)S(1)}, u32[]{:S(2)}, u32[]{:S(2)}) collective-permute-start(f32[32,256]{1,0:T(8,128)S(1)} %get-tuple-element.35), channel_id=1, source_target_pairs={{0,3},{1,2},{2,1},{3,0},{4,7},{5,6},{6,5},{7,4},{8,11},{9,10},{10,... | collective-permute-start | bytes 98312 | tf_op jit(solution)/shard_map/ppermute | solution.py:312

commit v16 on v15

--- a/solution.py
+++ b/solution.py
@@ -78,9 +78,9 @@
         copy.wait()
 
 
-def column_copies(source, target, sems):
+def column_copies(source, target, sems, size=BLOCK):
     width = source.shape[1]
-    cuts = [pl.ds(start, BLOCK) for start in range(0, width, BLOCK)]
+    cuts = [pl.ds(start, size) for start in range(0, width, size)]
     return [pltpu.make_async_copy(source.at[:, cut], target.at[:, cut], sems.at[b]) for b, cut in enumerate(cuts)]
 
 
@@ -102,7 +102,7 @@
 
 def sums_kernel(pad, cap, *refs):
     (probes, lengths_in, ids_in, firms_in), sends, refs = refs[:4], refs[4 : 4 + NEAR], refs[4 + NEAR :]
-    x1, mask_ids, weight, valid, x, acc, sums, lengths, ids, firms, sems, small = refs
+    x1, mask_ids, weight, valid, x, sums, lengths, ids, firms, sems, small = refs
     copies = column_copies(probes, x, sems)
     first = [
         pltpu.make_async_copy(source, target, small.at[k])
@@ -128,8 +128,9 @@
         send[part + 8 :] = masked
 
     table = same_worker(pad, 256)
+    wait_all(copies)
+    total = None
     for b in range(len(copies)):
-        copies[b].wait()
         ok = row(valid, b, BLOCK)
         x0 = x[:, b * BLOCK : (b + 1) * BLOCK] * ok
         rest = x0 - by_worker(x0, table) * row(weight, b, BLOCK)
@@ -138,12 +139,9 @@
         data = jnp.concatenate([*split(rest), counted], axis=0)
         per = BLOCK // LANES
         block = dot(data, one_hot_down(turned[:, b * per : (b + 1) * per], slots))
-        if b == 0:
-            acc[...] = block
-        else:
-            acc[...] += block
-    sums[...] = acc[:columns] + acc[columns : 2 * columns]
-    about = jnp.where(iota((8, slots), 0) == 0, keys, acc[2 * columns : 2 * columns + 1])
+        total = block if total is None else total + block
+    sums[...] = total[:columns] + total[columns : 2 * columns]
+    about = jnp.where(iota((8, slots), 0) == 0, keys, total[2 * columns : 2 * columns + 1])
     for k, send in enumerate(sends):
         send[:part] = sums[pl.ds(pl.multiple_of((me ^ k) * part, part), part), :]
         send[part : part + 8] = about
@@ -201,22 +199,12 @@
     lax.fori_loop(0, len(parts), device, 0, unroll=len(parts) if slots <= 256 else 1)
 
 
-def same_firm(parts, part, at):
-    keys = [one[part * NEAR + 2 * k : part * NEAR + 2 * k + 1, at] for one in parts for k in range(NEAR)]
-    mine = jnp.concatenate(keys[:NEAR], axis=1)
-    down = jnp.concatenate(keys, axis=0).T
-    found = [(down[:, k : k + 1] == mine).astype(F32).astype(BF16) for k in range(len(keys))]
+def same_firm(own, one, part, at):
+    mine, keys = ([ref[part * NEAR + 2 * k : part * NEAR + 2 * k + 1, at] for k in range(NEAR)] for ref in (own, one))
+    mine = jnp.concatenate(mine, axis=1)
+    down = jnp.concatenate([jnp.broadcast_to(key, (8, LANES)) for key in keys], axis=0).T
+    found = [(down[:, 8 * k : 8 * k + 1] == mine).astype(F32).astype(BF16) for k in range(NEAR)]
     return jnp.concatenate(found, axis=0)
-
-
-def gathered(parts, part, at):
-    data = [one[part * k : part * (k + 1), at] for one in parts for k in range(NEAR)]
-    return jnp.concatenate(split(jnp.concatenate(data, axis=1)), axis=0)
-
-
-def spread_out(means, out, part, at):
-    for k in range(NEAR):
-        out[part * k : part * (k + 1), at] = means[:, k * LANES : (k + 1) * LANES]
 
 
 def each_tile(slots, do):
@@ -228,14 +216,27 @@
         lax.fori_loop(0, tiles, lambda t, c: (do(t, pl.ds(pl.multiple_of(t * LANES, LANES), LANES)), c)[1], 0)
 
 
+def firms_kernel(part, own, one, out):
+    each_tile(own.shape[1], lambda t, at: out.__setitem__(t, same_firm(own, one, part, at)))
+
+
+def gathered(parts, part, at):
+    data = [one[part * k : part * (k + 1), at] for one in parts for k in range(NEAR)]
+    return jnp.concatenate(split(jnp.concatenate(data, axis=1)), axis=0)
+
+
+def spread_out(means, out, part, at):
+    for k in range(NEAR):
+        out[part * k : part * (k + 1), at] = means[:, k * LANES : (k + 1) * LANES]
+
+
 def change_kernel(far, part, *refs):
-    parts, (own_pairs, pairs, mean, sums, scale), table = refs[:far], refs[far : far + 5], refs[far + 5 :]
+    parts, tables, (own_pairs, pairs, mean, sums, scale) = refs[:far], refs[far:-5], refs[-5:]
     slots = mean.shape[1]
 
     def tile(t, at):
-        same = same_firm(parts, part, at)
-        if table:
-            table[0][t] = same
+        same = [table[t] for table in tables] or [same_firm(parts[0], one, part, at) for one in parts]
+        same = jnp.concatenate(same, axis=0)
         count = [one[part * NEAR + 2 * k + 1 : part * NEAR + 2 * k + 2, at] for one in parts for k in range(NEAR)]
         count = jnp.concatenate(count, axis=1)
         high = count.astype(BF16).astype(F32)
@@ -255,11 +256,12 @@
         sums[cut] = parts[0][cut] + (change[:, :slots] + change[:, slots:])
 
 
-def means_kernel(far, part, *refs):
+def means_kernel(far, part, kept, *refs):
     parts, source, (scale, mean), sends, second = refs[:far], refs[far:-8], refs[-8:-6], refs[-5:-1], refs[-1]
 
     def tile(t, at):
-        same = source[0][t] if len(source) == 1 else same_firm(source, part, at)
+        same = [table[t] if kept else same_firm(source[0], table, part, at) for table in source]
+        same = jnp.concatenate(same, axis=0)
         found = dot(gathered(parts, part, at), same)
         spread_out((found[:part] + found[part:]) * scale[t][:1], second, part, at)
 
@@ -283,7 +285,7 @@
 
 def last_kernel(pad, part, *refs):
     parts, (x1, mask_ids, weight), tables, (out, means, y, sems) = refs[:NEAR], refs[NEAR : NEAR + 3], refs[NEAR + 3 : -4], refs[-4:]
-    outs = column_copies(y, out, sems)
+    outs = column_copies(y, out, sems, 2 * BLOCK)
     me = lax.axis_index("rows") % NEAR
     columns, slots = means.shape[1:]
     for k, one in enumerate(parts):
@@ -292,7 +294,7 @@
         means[1, at, :] = one[part:]
     first, total = (jnp.concatenate(split(means[k]), axis=0) for k in range(2))
     table = same_worker(pad, 256)
-    for b in range(len(outs)):
+    for b in range(2 * len(outs)):
         at = slice(b * BLOCK, (b + 1) * BLOCK)
         if tables:
             spread = dot(total, tables[0][:, at])
@@ -303,7 +305,8 @@
             spread, worker = dot(total, found), dot(first, found)
             worker = by_worker(worker[:columns] + worker[columns:], table)
         y[:, at] = x1[:, at] - (spread[:columns] + spread[columns:]) + worker * row(weight, b, BLOCK)
-        outs[b].start()
+        if b % 2:
+            outs[b // 2].start()
     wait_all(outs)
 
 
@@ -364,7 +367,6 @@
         [
             pltpu.VMEM(of_rows, F32),
             pltpu.VMEM(whole, F32),
-            pltpu.VMEM((2 * columns + 16, slots), F32),
             pltpu.VMEM((columns, slots), F32),
             pltpu.VMEM(lengths.shape, jnp.int32),
             pltpu.VMEM(ids.shape, jnp.int32),
@@ -400,17 +402,30 @@
     )(*arrived, own_pairs)
     shared = far_share(joined, n)
     pairs = pair_counts(arrived[1:])
-    table = array((tiles, n * LANES, NEAR * LANES), BF16)
+    tables = []
+    if keep:
+        tables = [
+            call(
+                functools.partial(firms_kernel, part),
+                array((tiles, NEAR * LANES, NEAR * LANES), BF16),
+                [vmem] * 2,
+                vmem,
+                [],
+                work // 64,
+                tiles * (NEAR * LANES) ** 2 * 2,
+            )(joined, one)
+            for one in shared
+        ]
     scale = array((tiles, 8, NEAR * LANES), F32)
-    mean, sums, scales, *tables = call(
+    mean, sums, scales = call(
         functools.partial(change_kernel, far, part),
-        [of_near, of_near, scale] + [table] * keep,
-        [vmem] * (far + 2),
-        [vmem] * (3 + keep),
+        [of_near, of_near, scale],
+        [vmem] * (far + len(tables) + 2),
+        [vmem] * 3,
         [],
         work // 4,
         slots * slots * 4,
-    )(*shared, own_pairs, pairs)
+    )(*shared, *tables, own_pairs, pairs)
     again = far_share(sums, n)
     source = tables if keep else shared
     spreads = []
@@ -425,7 +440,7 @@
             4 * slots * rows_dev,
         )(mask_ids, scales)
     sends = call(
-        functools.partial(means_kernel, far, part),
+        functools.partial(means_kernel, far, part, keep),
         [array((2 * part, slots), F32)] * NEAR,
         [vmem] * (far + len(source) + 3),
         [vmem] * NEAR,

time: 39.5 us -> 38.7 us (0.980)
  waiting for transfers between devices: 10.2 us -> 9.47 us
    pallas_call x1 -> x5, Pallas kernels: 0.76 us -> 1.99 us  [the longest x4 1.23 us: body(): call(functools.partial(firms_kernel, part), array((tiles, NEAR * LANES, N...]
    pallas_call x1, Pallas kernels: 4.42 us -> 3.34 us  [body(): call(functools.partial(sums_kernel, pad, slots // n), [message] * NEAR +...]
    ppermute x6, waiting for transfers between devices: 4.92 us -> 4.1 us  [far_share(): return [one] + [lax.ppermute(one, 'rows', step) for step in steps]]
    pallas_call x1, Pallas kernels: 1.49 us -> 1.04 us  [body(): call(functools.partial(change_kernel, far, part), [of_near, of_near, scal...]
  transfers between devices with their start and end apart: 12 -> 12, of which waited for: 7 -> 7; matrix products, arithmetic and copies ran while one was open for 0% -> 0% of each run, Pallas kernels for 16% -> 19%
where the time goes in v16:
time: 38.7 us; the launch traced here: 38.5 us
  Pallas kernels  15 us (39%)
  starting transfers between devices  13.9 us (36%)
  waiting for transfers between devices  9.47 us (24%)
    ppermute x6, starting transfers between devices, far_share(): return [one] + [lax.ppermute(one, 'rows', step) for step in steps]  8.85 us
    ppermute x6, waiting for transfers between devices, near_exchange(): lax.ppermute(one, 'rows', step)  5.37 us
    pallas_call x2, Pallas kernels, pair_counts(): call(functools.partial(pairs_kernel, pad, about), array((len(parts), slot...  5.21 us
    ppermute x6, starting transfers between devices, near_exchange(): lax.ppermute(one, 'rows', step)  5.06 us
    ppermute x6, waiting for transfers between devices, far_share(): return [one] + [lax.ppermute(one, 'rows', step) for step in steps]  4.1 us
    pallas_call x1, Pallas kernels, body(): call(functools.partial(sums_kernel, pad, slots // n), [message] * NEAR +...  3.34 us
    pallas_call x1, Pallas kernels, body(): call(functools.partial(last_kernel, pad, part), array(whole, F32), [vmem]...  2.18 us
    pallas_call x1, Pallas kernels, body(): call(functools.partial(tables_kernel, pad), [array((slots, rows_dev), BF1...  1.27 us
  transfers between devices with their start and end apart: 12, of which 7 were waited for; matrix products, arithmetic and copies ran while one was open for 0% of the time, Pallas kernels for 19%

profile of v16, /device:TPU:0, one launch (start us, length us, event | category | flops | bytes accessed | tf_op | source)
XLA Modules:
  0.0 38.5 jit_solution(12670222032822276429)
XLA Ops:
  0.0 3.3 %shard_map.46 = (f32[56,256]{1,0:T(8,128)S(1)}, f32[56,256]{1,0:T(8,128)S(1)}, f32[56,256]{1,0:T(8,128)S(1)}, f32[56,256]{1,0:T(8,128)S(1)}, f32[64,8192]{1,0:T(...) custom-call(f32[64,8192]{1,0:T(8,128)} %refs_0_.1, s32[8,128]{1,0:T(8,128)} %bitcast.4, s32[64,128]{1,0:T(8,128)} %bitcast.3, ...), custom_call_target="tpu_custom_call" | custom-call | flops 1073741824 | bytes 2097152 | tf_op jit(solution)/shard_map/pallas_call | solution.py:362
  3.3 0.5 %collective-permute-start = (f32[56,256]{1,0:T(8,128)S(1)}, f32[56,256]{1,0:T(8,128)S(1)}, u32[]{:S(2)}, u32[]{:S(2)}) collective-permute-start(f32[56,256]{1,0:T(8,128)S(1)} %get-tuple-element.22), channel_id=1, source_target_pairs={{0,1},{1,0},{2,3},{3,2},{4,5},{5,4},{6,7},{7,6},{8,9},{9,8},{10,11... | collective-permute-start | bytes 172040 | tf_op jit(solution)/shard_map/ppermute | solution.py:315
  3.9 2.6 %collective-permute-start.1 = (f32[56,256]{1,0:T(8,128)S(1)}, f32[56,256]{1,0:T(8,128)S(1)}, u32[]{:S(2)}, u32[]{:S(2)}) collective-permute-start(f32[56,256]{1,0:T(8,128)S(1)} %get-tuple-element.23), channel_id=1, source_target_pairs={{0,2},{1,3},{2,0},{3,1},{4,6},{5,7},{6,4},{7,5},{8,10},{9,11},{10,... | collective-permute-start | bytes 172040 | tf_op jit(solution)/shard_map/ppermute | solution.py:315
  6.5 0.1 collective-permute-start.2
  6.5 1.3 %shard_map.47.refs_4_.refs_8_ = bf16[1,256,512]{2,1,0:T(8,128)(2,1)S(1)} custom-call(f32[56,256]{1,0:T(8,128)S(1)} %get-tuple-element.21.refs_0_), custom_call_target="tpu_custom_call" | custom-call | flops 134217728 | bytes 262144 | tf_op jit(solution)/shard_map/pallas_call | solution.py:382
  7.9 0.0 collective-permute-done.refs_1_.refs_0_
  7.9 1.1 %collective-permute-done.1.refs_2_.refs_1_ = f32[56,256]{1,0:T(8,128)S(1)} collective-permute-done((f32[56,256]{1,0:T(8,128)S(1)}, f32[56,256]{1,0:T(8,128)S(1)}, u32[]{:S(2)}, u32[]{:S(2)}) %collective-permute-start.1) | collective-permute-done | bytes 57376 | tf_op jit(solution)/shard_map/ppermute | solution.py:315
  9.0 1.4 %collective-permute-done.2.refs_3_.refs_2_ = f32[56,256]{1,0:T(8,128)S(1)} collective-permute-done((f32[56,256]{1,0:T(8,128)S(1)}, f32[56,256]{1,0:T(8,128)S(1)}, u32[]{:S(2)}, u32[]{:S(2)}) %collective-permute-start.2) | collective-permute-done | bytes 57376 | tf_op jit(solution)/shard_map/ppermute | solution.py:315
  10.3 1.6 %collective-permute-start.3 = (f32[72,256]{1,0:T(8,128)S(1)}, f32[72,256]{1,0:T(8,128)S(1)}, u32[]{:S(2)}, u32[]{:S(2)}) collective-permute-start(f32[72,256]{1,0:T(8,128)S(1)} %shard_map.48.own.one.refs_0_), channel_id=1, source_target_pairs={{0,4},{1,5},{2,6},{3,7},{4,0},{5,1},{6,2},{7,3},{8,12},{9,13},{10,... | collective-permute-start | bytes 221192 | tf_op jit(solution)/shard_map/ppermute | solution.py:320
  12.0 2.6 %collective-permute-start.4 = (f32[72,256]{1,0:T(8,128)S(1)}, f32[72,256]{1,0:T(8,128)S(1)}, u32[]{:S(2)}, u32[]{:S(2)}) collective-permute-start(f32[72,256]{1,0:T(8,128)S(1)} %shard_map.48.own.one.refs_0_), channel_id=1, source_target_pairs={{0,8},{1,9},{2,10},{3,11},{4,12},{5,13},{6,14},{7,15},{8,0},{9,1},... | collective-permute-start | bytes 221192 | tf_op jit(solution)/shard_map/ppermute | solution.py:320
  14.6 0.2 collective-permute-start.5
  14.8 0.3 shard_map.49.refs_4_
  15.1 3.9 %shard_map.53.refs_9_ = bf16[3,256,512]{2,1,0:T(8,128)(2,1)S(1)} custom-call(f32[56,256]{1,0:T(8,128)S(1)} %collective-permute-done.refs_1_.refs_0_, f32[56,256]{1,0:T(8,128)S(1)} %collective-permute-done.1.refs_2_.refs_1_, f32[56,256]{1,0:T(8,128)S(1)} %collective-permute-done.2.refs_3_.refs_2_), custom_call_target="tpu_custom_call" | custom-call | flops 402653184 | bytes 262144 | tf_op jit(solution)/shard_map/pallas_call | solution.py:382
  19.0 0.0 collective-permute-done.3.one.refs_1_
  19.0 0.3 shard_map.50.refs_5_
  19.3 1.5 %collective-permute-done.4.one.refs_2_ = f32[72,256]{1,0:T(8,128)S(1)} collective-permute-done((f32[72,256]{1,0:T(8,128)S(1)}, f32[72,256]{1,0:T(8,128)S(1)}, u32[]{:S(2)}, u32[]{:S(2)}) %collective-permute-start.4) | collective-permute-done | bytes 73760 | tf_op jit(solution)/shard_map/ppermute | solution.py:320
  20.9 0.3 shard_map.51.refs_6_
  21.2 0.0 collective-permute-done.5.one.refs_3_
  21.2 0.3 shard_map.52.refs_7_
  21.5 1.0 %shard_map.54 = (f32[64,256]{1,0:T(8,128)S(1)}, f32[64,256]{1,0:T(8,128)S(1)}, f32[2,8,512]{2,1,0:T(8,128)S(1)}) custom-call(f32[72,256]{1,0:T(8,128)S(1)} %shard_map.48.own.one.refs_0_, f32[72,256]{1,0:T(8,128)S(1)} %collective-permute-done.3.one.refs_1_, f32[72,256]{1,0:T(8,128)S(1)} %collective-permute-done.4.one.refs_2_, ...), custom_call_target="tpu_custom_call" | custom-call | flops 134217728 | bytes 262144 | tf_op jit(solution)/shard_map/pallas_call | solution.py:420
  22.5 2.5 %collective-permute-start.8 = (f32[64,256]{1,0:T(8,128)S(1)}, f32[64,256]{1,0:T(8,128)S(1)}, u32[]{:S(2)}, u32[]{:S(2)}) collective-permute-start(f32[64,256]{1,0:T(8,128)S(1)} %get-tuple-element.25.refs_0_), channel_id=1, source_target_pairs={{0,12},{1,13},{2,14},{3,15},{4,8},{5,9},{6,10},{7,11},{8,4},{9,5},... | collective-permute-start | bytes 196616 | tf_op jit(solution)/shard_map/ppermute | solution.py:320
  25.1 0.1 collective-permute-start.7
  25.1 1.8 %collective-permute-start.6 = (f32[64,256]{1,0:T(8,128)S(1)}, f32[64,256]{1,0:T(8,128)S(1)}, u32[]{:S(2)}, u32[]{:S(2)}) collective-permute-start(f32[64,256]{1,0:T(8,128)S(1)} %get-tuple-element.25.refs_0_), channel_id=1, source_target_pairs={{0,4},{1,5},{2,6},{3,7},{4,0},{5,1},{6,2},{7,3},{8,12},{9,13},{10,... | collective-permute-start | bytes 196616 | tf_op jit(solution)/shard_map/ppermute | solution.py:320
  26.9 1.3 %shard_map.55 = (bf16[256,8192]{1,0:T(8,128)(2,1)S(1)}, bf16[256,8192]{1,0:T(8,128)(2,1)S(1)}) custom-call(s32[64,128]{1,0:T(8,128)S(1)} %get-tuple-element.28.mask_ids.refs_5_, f32[2,8,512]{2,1,0:T(8,128)S(1)} %get-tuple-element.26.after.refs_8_), custom_call_target="tpu_custom_call" | custom-call | flops 536870912 | bytes 8388608 | tf_op jit(solution)/shard_map/pallas_call | solution.py:433
  28.2 0.8 %collective-permute-done.8.refs_3_ = f32[64,256]{1,0:T(8,128)S(1)} collective-permute-done((f32[64,256]{1,0:T(8,128)S(1)}, f32[64,256]{1,0:T(8,128)S(1)}, u32[]{:S(2)}, u32[]{:S(2)}) %collective-permute-start.8) | collective-permute-done | bytes 65568 | tf_op jit(solution)/shard_map/ppermute | solution.py:320
  29.0 1.8 %collective-permute-done.7.refs_2_ = f32[64,256]{1,0:T(8,128)S(1)} collective-permute-done((f32[64,256]{1,0:T(8,128)S(1)}, f32[64,256]{1,0:T(8,128)S(1)}, u32[]{:S(2)}, u32[]{:S(2)}) %collective-permute-start.7) | collective-permute-done | bytes 65568 | tf_op jit(solution)/shard_map/ppermute | solution.py:320
  30.8 0.0 collective-permute-done.6.refs_1_
  30.8 0.8 %shard_map.56 = (f32[32,256]{1,0:T(8,128)S(1)}, f32[32,256]{1,0:T(8,128)S(1)}, f32[32,256]{1,0:T(8,128)S(1)}, f32[32,256]{1,0:T(8,128)S(1)}) custom-call(f32[64,256]{1,0:T(8,128)S(1)} %get-tuple-element.25.refs_0_, f32[64,256]{1,0:T(8,128)S(1)} %collective-permute-done.6.refs_1_, f32[64,256]{1,0:T(8,128)S(1)} %collective-permute-done.7.refs_2_, ...), custom_call_target="tpu_custom_call" | custom-call | flops 134217728 | bytes 262144 | tf_op jit(solution)/shard_map/pallas_call | solution.py:442
  31.5 0.0 collective-permute-start.9
  31.6 1.4 %collective-permute-start.10 = (f32[32,256]{1,0:T(8,128)S(1)}, f32[32,256]{1,0:T(8,128)S(1)}, u32[]{:S(2)}, u32[]{:S(2)}) collective-permute-start(f32[32,256]{1,0:T(8,128)S(1)} %get-tuple-element.32), channel_id=1, source_target_pairs={{0,2},{1,3},{2,0},{3,1},{4,6},{5,7},{6,4},{7,5},{8,10},{9,11},{10,... | collective-permute-start | bytes 98312 | tf_op jit(solution)/shard_map/ppermute | solution.py:315
  33.0 0.4 %collective-permute-start.11 = (f32[32,256]{1,0:T(8,128)S(1)}, f32[32,256]{1,0:T(8,128)S(1)}, u32[]{:S(2)}, u32[]{:S(2)}) collective-permute-start(f32[32,256]{1,0:T(8,128)S(1)} %get-tuple-element.33), channel_id=1, source_target_pairs={{0,3},{1,2},{2,1},{3,0},{4,7},{5,6},{6,5},{7,4},{8,11},{9,10},{10,... | collective-permute-start | bytes 98312 | tf_op jit(solution)/shard_map/ppermute | solution.py:315
  33.4 0.0 collective-permute-done.9.refs_1_
  33.4 2.1 %collective-permute-done.10.refs_2_ = f32[32,256]{1,0:T(8,128)S(1)} collective-permute-done((f32[32,256]{1,0:T(8,128)S(1)}, f32[32,256]{1,0:T(8,128)S(1)}, u32[]{:S(2)}, u32[]{:S(2)}) %collective-permute-start.10) | collective-permute-done | bytes 32800 | tf_op jit(solution)/shard_map/ppermute | solution.py:315
  35.5 0.8 %collective-permute-done.11.refs_3_ = f32[32,256]{1,0:T(8,128)S(1)} collective-permute-done((f32[32,256]{1,0:T(8,128)S(1)}, f32[32,256]{1,0:T(8,128)S(1)}, u32[]{:S(2)}, u32[]{:S(2)}) %collective-permute-start.11) | collective-permute-done | bytes 32800 | tf_op jit(solution)/shard_map/ppermute | solution.py:315
  36.3 2.2 %shard_map.57 = f32[64,8192]{1,0:T(8,128)} custom-call(f32[32,256]{1,0:T(8,128)S(1)} %get-tuple-element.30.refs_0_, f32[32,256]{1,0:T(8,128)S(1)} %collective-permute-done.9.refs_1_, f32[32,256]{1,0:T(8,128)S(1)} %collective-permute-done.10.refs_2_, f32[32,256]{1,0:T(8,128)S(1)} %collective-permute-done.11.refs_3_, ...), custom_call_target="tpu_custom_call" | custom-call | flops 536870912 | bytes 4194304 | tf_op jit(solution)/shard_map/pallas_call | solution.py:452
  (1 shorter events, 0.0 us)
Async XLA Ops:
  3.3 4.5 %collective-permute-start = (f32[56,256]{1,0:T(8,128)S(1)}, f32[56,256]{1,0:T(8,128)S(1)}, u32[]{:S(2)}, u32[]{:S(2)}) collective-permute-start(f32[56,256]{1,0:T(8,128)S(1)} %get-tuple-element.22), channel_id=1, source_target_pairs={{0,1},{1,0},{2,3},{3,2},{4,5},{5,4},{6,7},{7,6},{8,9},{9,8},{10,11... | collective-permute-start | bytes 172040 | tf_op jit(solution)/shard_map/ppermute | solution.py:315
  3.9 5.1 %collective-permute-start.1 = (f32[56,256]{1,0:T(8,128)S(1)}, f32[56,256]{1,0:T(8,128)S(1)}, u32[]{:S(2)}, u32[]{:S(2)}) collective-permute-start(f32[56,256]{1,0:T(8,128)S(1)} %get-tuple-element.23), channel_id=1, source_target_pairs={{0,2},{1,3},{2,0},{3,1},{4,6},{5,7},{6,4},{7,5},{8,10},{9,11},{10,... | collective-permute-start | bytes 172040 | tf_op jit(solution)/shard_map/ppermute | solution.py:315
  6.5 3.9 %collective-permute-start.2 = (f32[56,256]{1,0:T(8,128)S(1)}, f32[56,256]{1,0:T(8,128)S(1)}, u32[]{:S(2)}, u32[]{:S(2)}) collective-permute-start(f32[56,256]{1,0:T(8,128)S(1)} %get-tuple-element.24), channel_id=1, source_target_pairs={{0,3},{1,2},{2,1},{3,0},{4,7},{5,6},{6,5},{7,4},{8,11},{9,10},{10,... | collective-permute-start | bytes 172040 | tf_op jit(solution)/shard_map/ppermute | solution.py:315
  10.3 8.7 %collective-permute-start.3 = (f32[72,256]{1,0:T(8,128)S(1)}, f32[72,256]{1,0:T(8,128)S(1)}, u32[]{:S(2)}, u32[]{:S(2)}) collective-permute-start(f32[72,256]{1,0:T(8,128)S(1)} %shard_map.48.own.one.refs_0_), channel_id=1, source_target_pairs={{0,4},{1,5},{2,6},{3,7},{4,0},{5,1},{6,2},{7,3},{8,12},{9,13},{10,... | collective-permute-start | bytes 221192 | tf_op jit(solution)/shard_map/ppermute | solution.py:320
  12.0 8.9 %collective-permute-start.4 = (f32[72,256]{1,0:T(8,128)S(1)}, f32[72,256]{1,0:T(8,128)S(1)}, u32[]{:S(2)}, u32[]{:S(2)}) collective-permute-start(f32[72,256]{1,0:T(8,128)S(1)} %shard_map.48.own.one.refs_0_), channel_id=1, source_target_pairs={{0,8},{1,9},{2,10},{3,11},{4,12},{5,13},{6,14},{7,15},{8,0},{9,1},... | collective-permute-start | bytes 221192 | tf_op jit(solution)/shard_map/ppermute | solution.py:320
  14.6 6.6 %collective-permute-start.5 = (f32[72,256]{1,0:T(8,128)S(1)}, f32[72,256]{1,0:T(8,128)S(1)}, u32[]{:S(2)}, u32[]{:S(2)}) collective-permute-start(f32[72,256]{1,0:T(8,128)S(1)} %shard_map.48.own.one.refs_0_), channel_id=1, source_target_pairs={{0,12},{1,13},{2,14},{3,15},{4,8},{5,9},{6,10},{7,11},{8,4},{9,5},... | collective-permute-start | bytes 221192 | tf_op jit(solution)/shard_map/ppermute | solution.py:320
  22.5 6.5 %collective-permute-start.8 = (f32[64,256]{1,0:T(8,128)S(1)}, f32[64,256]{1,0:T(8,128)S(1)}, u32[]{:S(2)}, u32[]{:S(2)}) collective-permute-start(f32[64,256]{1,0:T(8,128)S(1)} %get-tuple-element.25.refs_0_), channel_id=1, source_target_pairs={{0,12},{1,13},{2,14},{3,15},{4,8},{5,9},{6,10},{7,11},{8,4},{9,5},... | collective-permute-start | bytes 196616 | tf_op jit(solution)/shard_map/ppermute | solution.py:320
  25.1 5.7 %collective-permute-start.7 = (f32[64,256]{1,0:T(8,128)S(1)}, f32[64,256]{1,0:T(8,128)S(1)}, u32[]{:S(2)}, u32[]{:S(2)}) collective-permute-start(f32[64,256]{1,0:T(8,128)S(1)} %get-tuple-element.25.refs_0_), channel_id=1, source_target_pairs={{0,8},{1,9},{2,10},{3,11},{4,12},{5,13},{6,14},{7,15},{8,0},{9,1},... | collective-permute-start | bytes 196616 | tf_op jit(solution)/shard_map/ppermute | solution.py:320
  25.1 5.6 %collective-permute-start.6 = (f32[64,256]{1,0:T(8,128)S(1)}, f32[64,256]{1,0:T(8,128)S(1)}, u32[]{:S(2)}, u32[]{:S(2)}) collective-permute-start(f32[64,256]{1,0:T(8,128)S(1)} %get-tuple-element.25.refs_0_), channel_id=1, source_target_pairs={{0,4},{1,5},{2,6},{3,7},{4,0},{5,1},{6,2},{7,3},{8,12},{9,13},{10,... | collective-permute-start | bytes 196616 | tf_op jit(solution)/shard_map/ppermute | solution.py:320
  31.5 1.9 %collective-permute-start.9 = (f32[32,256]{1,0:T(8,128)S(1)}, f32[32,256]{1,0:T(8,128)S(1)}, u32[]{:S(2)}, u32[]{:S(2)}) collective-permute-start(f32[32,256]{1,0:T(8,128)S(1)} %get-tuple-element.31), channel_id=1, source_target_pairs={{0,1},{1,0},{2,3},{3,2},{4,5},{5,4},{6,7},{7,6},{8,9},{9,8},{10,11... | collective-permute-start | bytes 98312 | tf_op jit(solution)/shard_map/ppermute | solution.py:315
  31.6 4.0 %collective-permute-start.10 = (f32[32,256]{1,0:T(8,128)S(1)}, f32[32,256]{1,0:T(8,128)S(1)}, u32[]{:S(2)}, u32[]{:S(2)}) collective-permute-start(f32[32,256]{1,0:T(8,128)S(1)} %get-tuple-element.32), channel_id=1, source_target_pairs={{0,2},{1,3},{2,0},{3,1},{4,6},{5,7},{6,4},{7,5},{8,10},{9,11},{10,... | collective-permute-start | bytes 98312 | tf_op jit(solution)/shard_map/ppermute | solution.py:315
  33.0 3.3 %collective-permute-start.11 = (f32[32,256]{1,0:T(8,128)S(1)}, f32[32,256]{1,0:T(8,128)S(1)}, u32[]{:S(2)}, u32[]{:S(2)}) collective-permute-start(f32[32,256]{1,0:T(8,128)S(1)} %get-tuple-element.33), channel_id=1, source_target_pairs={{0,3},{1,2},{2,1},{3,0},{4,7},{5,6},{6,5},{7,4},{8,11},{9,10},{10,... | collective-permute-start | bytes 98312 | tf_op jit(solution)/shard_map/ppermute | solution.py:315

commit v17 on v16

--- a/solution.py
+++ b/solution.py
@@ -155,7 +155,7 @@
 
 
 def pairs_kernel(pad, start, *refs):
-    parts, (out, ids, counts) = refs[:-3], refs[-3:]
+    parts, (out, ids, size, counts) = refs[:-4], refs[-4:]
     slots = out.shape[1]
     kind = BF16 if slots <= 256 else F32
     per = LANES // pad
@@ -163,6 +163,7 @@
     across = slots // LANES
     rows = total_rows // across
     for k, part in enumerate(parts):
+        size[k] = jnp.broadcast_to(part[start - 7 : start - 6], (8, slots))
         for at in range(across):
             ids[k, at * rows : (at + 1) * rows] = part[start:, at * LANES : (at + 1) * LANES]
     at = iota((LANES, pad * LANES), 1)
@@ -181,16 +182,16 @@
             total = zero
             for j in range(pad):
                 total += jnp.where(slot == spells[g : g + 1, j * LANES : (j + 1) * LANES], one, zero)
-            counts[:, g * LANES : (g + 1) * LANES] = total.astype(BF16)
+            counts[k, :, g * LANES : (g + 1) * LANES] = total.astype(BF16)
         valid = jnp.where(dealt >= 0.0, 1.0, 0.0)
         length = valid[:, :LANES]
         for j in range(1, pad):
             length += valid[:, j * LANES : (j + 1) * LANES]
         inverse = 1.0 / length
         inverse = jnp.concatenate([inverse[g : g + 1] for g in range(total_rows // pad)], axis=1)
-        here = counts[...].astype(F32)
-        total = dot(jnp.concatenate(split(here * inverse), axis=0), counts[...], NT)
-        total = total[:slots] + total[slots:] - jnp.where(diagonal, jnp.sum(here, axis=1, keepdims=True), 0.0)
+        here = counts[k]
+        total = dot(jnp.concatenate(split(here.astype(F32) * inverse), axis=0), here, NT)
+        total = total[:slots] + total[slots:] - jnp.where(diagonal, size[k, :1], 0.0)
         hi, lo = split(total)
         out[k, :, :slots] = hi
         out[k, :, slots:] = lo
@@ -384,7 +385,11 @@
             array((len(parts), slots, 2 * slots), BF16),
             [vmem] * len(parts),
             vmem,
-            [pltpu.VMEM((len(parts), *of_rows), F32), pltpu.VMEM((slots, workers), BF16)],
+            [
+                pltpu.VMEM((len(parts), *of_rows), F32),
+                pltpu.VMEM((len(parts), 8, slots), F32),
+                pltpu.VMEM((len(parts), slots, workers), BF16),
+            ],
             work * len(parts) // 4,
             4 * slots * slots,
         )(*parts)

time: 38.7 us -> 38.6 us (level)
  Pallas kernels: 15 us -> 14.3 us
  waiting for transfers between devices: 9.47 us -> 10.1 us
    pallas_call x2, Pallas kernels: 5.21 us -> 4.52 us  [pair_counts(): call(functools.partial(pairs_kernel, pad, about), array((len(parts), slot...]
    ppermute x6, waiting for transfers between devices: 4.1 us -> 4.69 us  [far_share(): return [one] + [lax.ppermute(one, 'rows', step) for step in steps]]
  transfers between devices with their start and end apart: 12 -> 12, of which waited for: 7 -> 7; matrix products, arithmetic and copies ran while one was open for 0% -> 0% of each run, Pallas kernels for 19% -> 17%
where the time goes in v17:
time: 38.6 us; the launch traced here: 38.4 us
  Pallas kernels  14.3 us (37%)
  starting transfers between devices  13.9 us (36%)
  waiting for transfers between devices  10.1 us (26%)
    ppermute x6, starting transfers between devices, far_share(): return [one] + [lax.ppermute(one, 'rows', step) for step in steps]  8.85 us
    ppermute x6, waiting for transfers between devices, near_exchange(): lax.ppermute(one, 'rows', step)  5.37 us
    ppermute x6, starting transfers between devices, near_exchange(): lax.ppermute(one, 'rows', step)  5.06 us
    ppermute x6, waiting for transfers between devices, far_share(): return [one] + [lax.ppermute(one, 'rows', step) for step in steps]  4.69 us
    pallas_call x2, Pallas kernels, pair_counts(): call(functools.partial(pairs_kernel, pad, about), array((len(parts), slot...  4.52 us
    pallas_call x1, Pallas kernels, body(): call(functools.partial(sums_kernel, pad, slots // n), [message] * NEAR +...  3.34 us
    pallas_call x1, Pallas kernels, body(): call(functools.partial(last_kernel, pad, part), array(whole, F32), [vmem]...  2.18 us
    pallas_call x1, Pallas kernels, body(): call(functools.partial(tables_kernel, pad), [array((slots, rows_dev), BF1...  1.27 us
  transfers between devices with their start and end apart: 12, of which 7 were waited for; matrix products, arithmetic and copies ran while one was open for 0% of the time, Pallas kernels for 17%

profile of v17, /device:TPU:0, one launch (start us, length us, event | category | flops | bytes accessed | tf_op | source)
XLA Modules:
  0.0 38.4 jit_solution(17159502418381801900)
XLA Ops:
  0.0 3.3 %shard_map.46 = (f32[56,256]{1,0:T(8,128)S(1)}, f32[56,256]{1,0:T(8,128)S(1)}, f32[56,256]{1,0:T(8,128)S(1)}, f32[56,256]{1,0:T(8,128)S(1)}, f32[64,8192]{1,0:T(...) custom-call(f32[64,8192]{1,0:T(8,128)} %refs_0_.1, s32[8,128]{1,0:T(8,128)} %bitcast.4, s32[64,128]{1,0:T(8,128)} %bitcast.3, ...), custom_call_target="tpu_custom_call" | custom-call | flops 1073741824 | bytes 2097152 | tf_op jit(solution)/shard_map/pallas_call | solution.py:363
  3.3 0.5 %collective-permute-start = (f32[56,256]{1,0:T(8,128)S(1)}, f32[56,256]{1,0:T(8,128)S(1)}, u32[]{:S(2)}, u32[]{:S(2)}) collective-permute-start(f32[56,256]{1,0:T(8,128)S(1)} %get-tuple-element.22), channel_id=1, source_target_pairs={{0,1},{1,0},{2,3},{3,2},{4,5},{5,4},{6,7},{7,6},{8,9},{9,8},{10,11... | collective-permute-start | bytes 172040 | tf_op jit(solution)/shard_map/ppermute | solution.py:316
  3.9 2.6 %collective-permute-start.1 = (f32[56,256]{1,0:T(8,128)S(1)}, f32[56,256]{1,0:T(8,128)S(1)}, u32[]{:S(2)}, u32[]{:S(2)}) collective-permute-start(f32[56,256]{1,0:T(8,128)S(1)} %get-tuple-element.23), channel_id=1, source_target_pairs={{0,2},{1,3},{2,0},{3,1},{4,6},{5,7},{6,4},{7,5},{8,10},{9,11},{10,... | collective-permute-start | bytes 172040 | tf_op jit(solution)/shard_map/ppermute | solution.py:316
  6.5 0.1 collective-permute-start.2
  6.5 1.2 %shard_map.47.refs_4_.refs_8_ = bf16[1,256,512]{2,1,0:T(8,128)(2,1)S(1)} custom-call(f32[56,256]{1,0:T(8,128)S(1)} %get-tuple-element.21.refs_0_), custom_call_target="tpu_custom_call" | custom-call | flops 134217728 | bytes 262144 | tf_op jit(solution)/shard_map/pallas_call | solution.py:383
  7.8 0.0 collective-permute-done.refs_1_.refs_0_
  7.8 1.2 %collective-permute-done.1.refs_2_.refs_1_ = f32[56,256]{1,0:T(8,128)S(1)} collective-permute-done((f32[56,256]{1,0:T(8,128)S(1)}, f32[56,256]{1,0:T(8,128)S(1)}, u32[]{:S(2)}, u32[]{:S(2)}) %collective-permute-start.1) | collective-permute-done | bytes 57376 | tf_op jit(solution)/shard_map/ppermute | solution.py:316
  9.0 1.4 %collective-permute-done.2.refs_3_.refs_2_ = f32[56,256]{1,0:T(8,128)S(1)} collective-permute-done((f32[56,256]{1,0:T(8,128)S(1)}, f32[56,256]{1,0:T(8,128)S(1)}, u32[]{:S(2)}, u32[]{:S(2)}) %collective-permute-start.2) | collective-permute-done | bytes 57376 | tf_op jit(solution)/shard_map/ppermute | solution.py:316
  10.3 1.6 %collective-permute-start.3 = (f32[72,256]{1,0:T(8,128)S(1)}, f32[72,256]{1,0:T(8,128)S(1)}, u32[]{:S(2)}, u32[]{:S(2)}) collective-permute-start(f32[72,256]{1,0:T(8,128)S(1)} %shard_map.48.own.one.refs_0_), channel_id=1, source_target_pairs={{0,4},{1,5},{2,6},{3,7},{4,0},{5,1},{6,2},{7,3},{8,12},{9,13},{10,... | collective-permute-start | bytes 221192 | tf_op jit(solution)/shard_map/ppermute | solution.py:321
  12.0 2.6 %collective-permute-start.4 = (f32[72,256]{1,0:T(8,128)S(1)}, f32[72,256]{1,0:T(8,128)S(1)}, u32[]{:S(2)}, u32[]{:S(2)}) collective-permute-start(f32[72,256]{1,0:T(8,128)S(1)} %shard_map.48.own.one.refs_0_), channel_id=1, source_target_pairs={{0,8},{1,9},{2,10},{3,11},{4,12},{5,13},{6,14},{7,15},{8,0},{9,1},... | collective-permute-start | bytes 221192 | tf_op jit(solution)/shard_map/ppermute | solution.py:321
  14.6 0.2 collective-permute-start.5
  14.8 0.3 shard_map.49.refs_4_
  15.1 3.3 %shard_map.53.refs_9_ = bf16[3,256,512]{2,1,0:T(8,128)(2,1)S(1)} custom-call(f32[56,256]{1,0:T(8,128)S(1)} %collective-permute-done.refs_1_.refs_0_, f32[56,256]{1,0:T(8,128)S(1)} %collective-permute-done.1.refs_2_.refs_1_, f32[56,256]{1,0:T(8,128)S(1)} %collective-permute-done.2.refs_3_.refs_2_), custom_call_target="tpu_custom_call" | custom-call | flops 402653184 | bytes 262144 | tf_op jit(solution)/shard_map/pallas_call | solution.py:383
  18.4 0.0 collective-permute-done.3.one.refs_1_
  18.4 0.3 shard_map.50.refs_5_
  18.7 2.1 %collective-permute-done.4.one.refs_2_ = f32[72,256]{1,0:T(8,128)S(1)} collective-permute-done((f32[72,256]{1,0:T(8,128)S(1)}, f32[72,256]{1,0:T(8,128)S(1)}, u32[]{:S(2)}, u32[]{:S(2)}) %collective-permute-start.4) | collective-permute-done | bytes 73760 | tf_op jit(solution)/shard_map/ppermute | solution.py:321
  20.9 0.3 shard_map.51.refs_6_
  21.2 0.0 collective-permute-done.5.one.refs_3_
  21.2 0.3 shard_map.52.refs_7_
  21.5 1.0 %shard_map.54 = (f32[64,256]{1,0:T(8,128)S(1)}, f32[64,256]{1,0:T(8,128)S(1)}, f32[2,8,512]{2,1,0:T(8,128)S(1)}) custom-call(f32[72,256]{1,0:T(8,128)S(1)} %shard_map.48.own.one.refs_0_, f32[72,256]{1,0:T(8,128)S(1)} %collective-permute-done.3.one.refs_1_, f32[72,256]{1,0:T(8,128)S(1)} %collective-permute-done.4.one.refs_2_, ...), custom_call_target="tpu_custom_call" | custom-call | flops 134217728 | bytes 262144 | tf_op jit(solution)/shard_map/pallas_call | solution.py:425
  22.5 2.5 %collective-permute-start.8 = (f32[64,256]{1,0:T(8,128)S(1)}, f32[64,256]{1,0:T(8,128)S(1)}, u32[]{:S(2)}, u32[]{:S(2)}) collective-permute-start(f32[64,256]{1,0:T(8,128)S(1)} %get-tuple-element.25.refs_0_), channel_id=1, source_target_pairs={{0,12},{1,13},{2,14},{3,15},{4,8},{5,9},{6,10},{7,11},{8,4},{9,5},... | collective-permute-start | bytes 196616 | tf_op jit(solution)/shard_map/ppermute | solution.py:321
  25.1 0.1 collective-permute-start.7
  25.1 1.8 %collective-permute-start.6 = (f32[64,256]{1,0:T(8,128)S(1)}, f32[64,256]{1,0:T(8,128)S(1)}, u32[]{:S(2)}, u32[]{:S(2)}) collective-permute-start(f32[64,256]{1,0:T(8,128)S(1)} %get-tuple-element.25.refs_0_), channel_id=1, source_target_pairs={{0,4},{1,5},{2,6},{3,7},{4,0},{5,1},{6,2},{7,3},{8,12},{9,13},{10,... | collective-permute-start | bytes 196616 | tf_op jit(solution)/shard_map/ppermute | solution.py:321
  26.9 1.3 %shard_map.55 = (bf16[256,8192]{1,0:T(8,128)(2,1)S(1)}, bf16[256,8192]{1,0:T(8,128)(2,1)S(1)}) custom-call(s32[64,128]{1,0:T(8,128)S(1)} %get-tuple-element.28.mask_ids.refs_5_, f32[2,8,512]{2,1,0:T(8,128)S(1)} %get-tuple-element.26.after.refs_8_), custom_call_target="tpu_custom_call" | custom-call | flops 536870912 | bytes 8388608 | tf_op jit(solution)/shard_map/pallas_call | solution.py:438
  28.2 1.1 %collective-permute-done.8.refs_3_ = f32[64,256]{1,0:T(8,128)S(1)} collective-permute-done((f32[64,256]{1,0:T(8,128)S(1)}, f32[64,256]{1,0:T(8,128)S(1)}, u32[]{:S(2)}, u32[]{:S(2)}) %collective-permute-start.8) | collective-permute-done | bytes 65568 | tf_op jit(solution)/shard_map/ppermute | solution.py:321
  29.3 1.5 %collective-permute-done.7.refs_2_ = f32[64,256]{1,0:T(8,128)S(1)} collective-permute-done((f32[64,256]{1,0:T(8,128)S(1)}, f32[64,256]{1,0:T(8,128)S(1)}, u32[]{:S(2)}, u32[]{:S(2)}) %collective-permute-start.7) | collective-permute-done | bytes 65568 | tf_op jit(solution)/shard_map/ppermute | solution.py:321
  30.8 0.0 collective-permute-done.6.refs_1_
  30.8 0.8 %shard_map.56 = (f32[32,256]{1,0:T(8,128)S(1)}, f32[32,256]{1,0:T(8,128)S(1)}, f32[32,256]{1,0:T(8,128)S(1)}, f32[32,256]{1,0:T(8,128)S(1)}) custom-call(f32[64,256]{1,0:T(8,128)S(1)} %get-tuple-element.25.refs_0_, f32[64,256]{1,0:T(8,128)S(1)} %collective-permute-done.6.refs_1_, f32[64,256]{1,0:T(8,128)S(1)} %collective-permute-done.7.refs_2_, ...), custom_call_target="tpu_custom_call" | custom-call | flops 134217728 | bytes 262144 | tf_op jit(solution)/shard_map/pallas_call | solution.py:447
  31.5 0.0 collective-permute-start.9
  31.6 1.3 %collective-permute-start.10 = (f32[32,256]{1,0:T(8,128)S(1)}, f32[32,256]{1,0:T(8,128)S(1)}, u32[]{:S(2)}, u32[]{:S(2)}) collective-permute-start(f32[32,256]{1,0:T(8,128)S(1)} %get-tuple-element.32), channel_id=1, source_target_pairs={{0,2},{1,3},{2,0},{3,1},{4,6},{5,7},{6,4},{7,5},{8,10},{9,11},{10,... | collective-permute-start | bytes 98312 | tf_op jit(solution)/shard_map/ppermute | solution.py:316
  32.9 0.5 %collective-permute-start.11 = (f32[32,256]{1,0:T(8,128)S(1)}, f32[32,256]{1,0:T(8,128)S(1)}, u32[]{:S(2)}, u32[]{:S(2)}) collective-permute-start(f32[32,256]{1,0:T(8,128)S(1)} %get-tuple-element.33), channel_id=1, source_target_pairs={{0,3},{1,2},{2,1},{3,0},{4,7},{5,6},{6,5},{7,4},{8,11},{9,10},{10,... | collective-permute-start | bytes 98312 | tf_op jit(solution)/shard_map/ppermute | solution.py:316
  33.4 0.0 collective-permute-done.9.refs_1_
  33.4 2.1 %collective-permute-done.10.refs_2_ = f32[32,256]{1,0:T(8,128)S(1)} collective-permute-done((f32[32,256]{1,0:T(8,128)S(1)}, f32[32,256]{1,0:T(8,128)S(1)}, u32[]{:S(2)}, u32[]{:S(2)}) %collective-permute-start.10) | collective-permute-done | bytes 32800 | tf_op jit(solution)/shard_map/ppermute | solution.py:316
  35.5 0.7 %collective-permute-done.11.refs_3_ = f32[32,256]{1,0:T(8,128)S(1)} collective-permute-done((f32[32,256]{1,0:T(8,128)S(1)}, f32[32,256]{1,0:T(8,128)S(1)}, u32[]{:S(2)}, u32[]{:S(2)}) %collective-permute-start.11) | collective-permute-done | bytes 32800 | tf_op jit(solution)/shard_map/ppermute | solution.py:316
  36.2 2.2 %shard_map.57 = f32[64,8192]{1,0:T(8,128)} custom-call(f32[32,256]{1,0:T(8,128)S(1)} %get-tuple-element.30.refs_0_, f32[32,256]{1,0:T(8,128)S(1)} %collective-permute-done.9.refs_1_, f32[32,256]{1,0:T(8,128)S(1)} %collective-permute-done.10.refs_2_, f32[32,256]{1,0:T(8,128)S(1)} %collective-permute-done.11.refs_3_, ...), custom_call_target="tpu_custom_call" | custom-call | flops 536870912 | bytes 4194304 | tf_op jit(solution)/shard_map/pallas_call | solution.py:457
  (1 shorter events, 0.0 us)
Async XLA Ops:
  3.3 4.4 %collective-permute-start = (f32[56,256]{1,0:T(8,128)S(1)}, f32[56,256]{1,0:T(8,128)S(1)}, u32[]{:S(2)}, u32[]{:S(2)}) collective-permute-start(f32[56,256]{1,0:T(8,128)S(1)} %get-tuple-element.22), channel_id=1, source_target_pairs={{0,1},{1,0},{2,3},{3,2},{4,5},{5,4},{6,7},{7,6},{8,9},{9,8},{10,11... | collective-permute-start | bytes 172040 | tf_op jit(solution)/shard_map/ppermute | solution.py:316
  3.9 5.1 %collective-permute-start.1 = (f32[56,256]{1,0:T(8,128)S(1)}, f32[56,256]{1,0:T(8,128)S(1)}, u32[]{:S(2)}, u32[]{:S(2)}) collective-permute-start(f32[56,256]{1,0:T(8,128)S(1)} %get-tuple-element.23), channel_id=1, source_target_pairs={{0,2},{1,3},{2,0},{3,1},{4,6},{5,7},{6,4},{7,5},{8,10},{9,11},{10,... | collective-permute-start | bytes 172040 | tf_op jit(solution)/shard_map/ppermute | solution.py:316
  6.5 3.9 %collective-permute-start.2 = (f32[56,256]{1,0:T(8,128)S(1)}, f32[56,256]{1,0:T(8,128)S(1)}, u32[]{:S(2)}, u32[]{:S(2)}) collective-permute-start(f32[56,256]{1,0:T(8,128)S(1)} %get-tuple-element.24), channel_id=1, source_target_pairs={{0,3},{1,2},{2,1},{3,0},{4,7},{5,6},{6,5},{7,4},{8,11},{9,10},{10,... | collective-permute-start | bytes 172040 | tf_op jit(solution)/shard_map/ppermute | solution.py:316
  10.3 8.1 %collective-permute-start.3 = (f32[72,256]{1,0:T(8,128)S(1)}, f32[72,256]{1,0:T(8,128)S(1)}, u32[]{:S(2)}, u32[]{:S(2)}) collective-permute-start(f32[72,256]{1,0:T(8,128)S(1)} %shard_map.48.own.one.refs_0_), channel_id=1, source_target_pairs={{0,4},{1,5},{2,6},{3,7},{4,0},{5,1},{6,2},{7,3},{8,12},{9,13},{10,... | collective-permute-start | bytes 221192 | tf_op jit(solution)/shard_map/ppermute | solution.py:321
  12.0 8.9 %collective-permute-start.4 = (f32[72,256]{1,0:T(8,128)S(1)}, f32[72,256]{1,0:T(8,128)S(1)}, u32[]{:S(2)}, u32[]{:S(2)}) collective-permute-start(f32[72,256]{1,0:T(8,128)S(1)} %shard_map.48.own.one.refs_0_), channel_id=1, source_target_pairs={{0,8},{1,9},{2,10},{3,11},{4,12},{5,13},{6,14},{7,15},{8,0},{9,1},... | collective-permute-start | bytes 221192 | tf_op jit(solution)/shard_map/ppermute | solution.py:321
  14.6 6.6 %collective-permute-start.5 = (f32[72,256]{1,0:T(8,128)S(1)}, f32[72,256]{1,0:T(8,128)S(1)}, u32[]{:S(2)}, u32[]{:S(2)}) collective-permute-start(f32[72,256]{1,0:T(8,128)S(1)} %shard_map.48.own.one.refs_0_), channel_id=1, source_target_pairs={{0,12},{1,13},{2,14},{3,15},{4,8},{5,9},{6,10},{7,11},{8,4},{9,5},... | collective-permute-start | bytes 221192 | tf_op jit(solution)/shard_map/ppermute | solution.py:321
  22.5 6.7 %collective-permute-start.8 = (f32[64,256]{1,0:T(8,128)S(1)}, f32[64,256]{1,0:T(8,128)S(1)}, u32[]{:S(2)}, u32[]{:S(2)}) collective-permute-start(f32[64,256]{1,0:T(8,128)S(1)} %get-tuple-element.25.refs_0_), channel_id=1, source_target_pairs={{0,12},{1,13},{2,14},{3,15},{4,8},{5,9},{6,10},{7,11},{8,4},{9,5},... | collective-permute-start | bytes 196616 | tf_op jit(solution)/shard_map/ppermute | solution.py:321
  25.1 5.7 %collective-permute-start.7 = (f32[64,256]{1,0:T(8,128)S(1)}, f32[64,256]{1,0:T(8,128)S(1)}, u32[]{:S(2)}, u32[]{:S(2)}) collective-permute-start(f32[64,256]{1,0:T(8,128)S(1)} %get-tuple-element.25.refs_0_), channel_id=1, source_target_pairs={{0,8},{1,9},{2,10},{3,11},{4,12},{5,13},{6,14},{7,15},{8,0},{9,1},... | collective-permute-start | bytes 196616 | tf_op jit(solution)/shard_map/ppermute | solution.py:321
  25.1 5.6 %collective-permute-start.6 = (f32[64,256]{1,0:T(8,128)S(1)}, f32[64,256]{1,0:T(8,128)S(1)}, u32[]{:S(2)}, u32[]{:S(2)}) collective-permute-start(f32[64,256]{1,0:T(8,128)S(1)} %get-tuple-element.25.refs_0_), channel_id=1, source_target_pairs={{0,4},{1,5},{2,6},{3,7},{4,0},{5,1},{6,2},{7,3},{8,12},{9,13},{10,... | collective-permute-start | bytes 196616 | tf_op jit(solution)/shard_map/ppermute | solution.py:321
  31.5 1.9 %collective-permute-start.9 = (f32[32,256]{1,0:T(8,128)S(1)}, f32[32,256]{1,0:T(8,128)S(1)}, u32[]{:S(2)}, u32[]{:S(2)}) collective-permute-start(f32[32,256]{1,0:T(8,128)S(1)} %get-tuple-element.31), channel_id=1, source_target_pairs={{0,1},{1,0},{2,3},{3,2},{4,5},{5,4},{6,7},{7,6},{8,9},{9,8},{10,11... | collective-permute-start | bytes 98312 | tf_op jit(solution)/shard_map/ppermute | solution.py:316
  31.6 4.0 %collective-permute-start.10 = (f32[32,256]{1,0:T(8,128)S(1)}, f32[32,256]{1,0:T(8,128)S(1)}, u32[]{:S(2)}, u32[]{:S(2)}) collective-permute-start(f32[32,256]{1,0:T(8,128)S(1)} %get-tuple-element.32), channel_id=1, source_target_pairs={{0,2},{1,3},{2,0},{3,1},{4,6},{5,7},{6,4},{7,5},{8,10},{9,11},{10,... | collective-permute-start | bytes 98312 | tf_op jit(solution)/shard_map/ppermute | solution.py:316
  32.9 3.3 %collective-permute-start.11 = (f32[32,256]{1,0:T(8,128)S(1)}, f32[32,256]{1,0:T(8,128)S(1)}, u32[]{:S(2)}, u32[]{:S(2)}) collective-permute-start(f32[32,256]{1,0:T(8,128)S(1)} %get-tuple-element.33), channel_id=1, source_target_pairs={{0,3},{1,2},{2,1},{3,0},{4,7},{5,6},{6,5},{7,4},{8,11},{9,10},{10,... | collective-permute-start | bytes 98312 | tf_op jit(solution)/shard_map/ppermute | solution.py:316

commit v18 on v17

--- a/solution.py
+++ b/solution.py
@@ -12,6 +12,7 @@
 BLOCK = 1024
 VMEM_BYTES = 32 * 1024 * 1024
 NEAR = 4
+NEAR_STEPS = (0, 2, 3, 1)
 F32, BF16 = jnp.float32, jnp.bfloat16
 NT = (((1,), (1,)), ((), ()))
 NN = (((1,), (0,)), ((), ()))
@@ -142,8 +143,8 @@
         total = block if total is None else total + block
     sums[...] = total[:columns] + total[columns : 2 * columns]
     about = jnp.where(iota((8, slots), 0) == 0, keys, total[2 * columns : 2 * columns + 1])
-    for k, send in enumerate(sends):
-        send[:part] = sums[pl.ds(pl.multiple_of((me ^ k) * part, part), part), :]
+    for step, send in zip(NEAR_STEPS, sends):
+        send[:part] = sums[pl.ds(pl.multiple_of((me ^ step) * part, part), part), :]
         send[part : part + 8] = about
 
 
@@ -217,7 +218,7 @@
         lax.fori_loop(0, tiles, lambda t, c: (do(t, pl.ds(pl.multiple_of(t * LANES, LANES), LANES)), c)[1], 0)
 
 
-def firms_kernel(part, own, one, out):
+def firms_kernel(part, own, one, after, out):
     each_tile(own.shape[1], lambda t, at: out.__setitem__(t, same_firm(own, one, part, at)))
 
 
@@ -289,8 +290,8 @@
     outs = column_copies(y, out, sems, 2 * BLOCK)
     me = lax.axis_index("rows") % NEAR
     columns, slots = means.shape[1:]
-    for k, one in enumerate(parts):
-        at = pl.ds(pl.multiple_of((me ^ k) * part, part), part)
+    for step, one in zip(NEAR_STEPS, parts):
+        at = pl.ds(pl.multiple_of((me ^ step) * part, part), part)
         means[0, at, :] = one[:part]
         means[1, at, :] = one[part:]
     first, total = (jnp.concatenate(split(means[k]), axis=0) for k in range(2))
@@ -312,7 +313,7 @@
 
 
 def near_exchange(parts, n):
-    steps = [[(i, i ^ k) for i in range(n)] for k in range(1, NEAR)]
+    steps = [[(i, i ^ step) for i in range(n)] for step in NEAR_STEPS[1:]]
     return [parts[0]] + [lax.ppermute(one, "rows", step) for one, step in zip(parts[1:], steps)]
 
 
@@ -409,18 +410,19 @@
     pairs = pair_counts(arrived[1:])
     tables = []
     if keep:
-        tables = [
-            call(
+        after = joined
+        for one in [shared[0]] + shared[:0:-1]:
+            after = call(
                 functools.partial(firms_kernel, part),
                 array((tiles, NEAR * LANES, NEAR * LANES), BF16),
-                [vmem] * 2,
+                [vmem] * 3,
                 vmem,
                 [],
                 work // 64,
                 tiles * (NEAR * LANES) ** 2 * 2,
-            )(joined, one)
-            for one in shared
-        ]
+            )(joined, one, after)
+            tables.append(after)
+        tables = tables[:1] + tables[:0:-1]
     scale = array((tiles, 8, NEAR * LANES), F32)
     mean, sums, scales = call(
         functools.partial(change_kernel, far, part),

time: 38.6 us -> 38.5 us (level)
  waiting for transfers between devices: 10.1 us -> 9.67 us
  transfers between devices with their start and end apart: 12 -> 12, of which waited for: 7 -> 7; matrix products, arithmetic and copies ran while one was open for 0% -> 0% of each run, Pallas kernels for 17% -> 18%
where the time goes in v18:
time: 38.5 us; the launch traced here: 38.3 us
  Pallas kernels  14.4 us (37%)
  starting transfers between devices  14.2 us (37%)
  waiting for transfers between devices  9.67 us (25%)
    ppermute x6, starting transfers between devices, far_share(): return [one] + [lax.ppermute(one, 'rows', step) for step in steps]  8.85 us
    ppermute x6, starting transfers between devices, near_exchange(): lax.ppermute(one, 'rows', step)  5.38 us
    ppermute x6, waiting for transfers between devices, near_exchange(): lax.ppermute(one, 'rows', step)  5.25 us
    pallas_call x2, Pallas kernels, pair_counts(): call(functools.partial(pairs_kernel, pad, about), array((len(parts), slot...  4.52 us
    ppermute x6, waiting for transfers between devices, far_share(): return [one] + [lax.ppermute(one, 'rows', step) for step in steps]  4.41 us
    pallas_call x1, Pallas kernels, body(): call(functools.partial(sums_kernel, pad, slots // n), [message] * NEAR +...  3.34 us
    pallas_call x1, Pallas kernels, body(): call(functools.partial(last_kernel, pad, part), array(whole, F32), [vmem]...  2.18 us
    pallas_call x1, Pallas kernels, body(): call(functools.partial(tables_kernel, pad), [array((slots, rows_dev), BF1...  1.28 us
  transfers between devices with their start and end apart: 12, of which 7 were waited for; matrix products, arithmetic and copies ran while one was open for 0% of the time, Pallas kernels for 18%

profile of v18, /device:TPU:0, one launch (start us, length us, event | category | flops | bytes accessed | tf_op | source)
XLA Modules:
  0.0 38.3 jit_solution(6667257771158127349)
XLA Ops:
  0.0 3.3 %shard_map.46 = (f32[56,256]{1,0:T(8,128)S(1)}, f32[56,256]{1,0:T(8,128)S(1)}, f32[56,256]{1,0:T(8,128)S(1)}, f32[56,256]{1,0:T(8,128)S(1)}, f32[64,8192]{1,0:T(...) custom-call(f32[64,8192]{1,0:T(8,128)} %refs_0_.1, s32[8,128]{1,0:T(8,128)} %bitcast.4, s32[64,128]{1,0:T(8,128)} %bitcast.3, ...), custom_call_target="tpu_custom_call" | custom-call | flops 1073741824 | bytes 2097152 | tf_op jit(solution)/shard_map/pallas_call | solution.py:364
  3.3 3.0 %collective-permute-start = (f32[56,256]{1,0:T(8,128)S(1)}, f32[56,256]{1,0:T(8,128)S(1)}, u32[]{:S(2)}, u32[]{:S(2)}) collective-permute-start(f32[56,256]{1,0:T(8,128)S(1)} %get-tuple-element.22), channel_id=1, source_target_pairs={{0,2},{1,3},{2,0},{3,1},{4,6},{5,7},{6,4},{7,5},{8,10},{9,11},{10,... | collective-permute-start | bytes 172040 | tf_op jit(solution)/shard_map/ppermute | solution.py:317
  6.4 0.0 collective-permute-start.1
  6.4 0.2 collective-permute-start.2
  6.6 1.2 %shard_map.47.refs_4_.refs_8_ = bf16[1,256,512]{2,1,0:T(8,128)(2,1)S(1)} custom-call(f32[56,256]{1,0:T(8,128)S(1)} %get-tuple-element.21.refs_0_), custom_call_target="tpu_custom_call" | custom-call | flops 134217728 | bytes 262144 | tf_op jit(solution)/shard_map/pallas_call | solution.py:384
  7.8 0.7 %collective-permute-done.refs_1_.refs_0_ = f32[56,256]{1,0:T(8,128)S(1)} collective-permute-done((f32[56,256]{1,0:T(8,128)S(1)}, f32[56,256]{1,0:T(8,128)S(1)}, u32[]{:S(2)}, u32[]{:S(2)}) %collective-permute-start) | collective-permute-done | bytes 57376 | tf_op jit(solution)/shard_map/ppermute | solution.py:317
  8.5 1.8 %collective-permute-done.1.refs_2_.refs_1_ = f32[56,256]{1,0:T(8,128)S(1)} collective-permute-done((f32[56,256]{1,0:T(8,128)S(1)}, f32[56,256]{1,0:T(8,128)S(1)}, u32[]{:S(2)}, u32[]{:S(2)}) %collective-permute-start.1) | collective-permute-done | bytes 57376 | tf_op jit(solution)/shard_map/ppermute | solution.py:317
  10.3 0.0 collective-permute-done.2.refs_3_.refs_2_
  10.3 3.7 %collective-permute-start.5 = (f32[72,256]{1,0:T(8,128)S(1)}, f32[72,256]{1,0:T(8,128)S(1)}, u32[]{:S(2)}, u32[]{:S(2)}) collective-permute-start(f32[72,256]{1,0:T(8,128)S(1)} %shard_map.48.own.one.after.refs_0_), channel_id=1, source_target_pairs={{0,12},{1,13},{2,14},{3,15},{4,8},{5,9},{6,10},{7,11},{8,4},{9,5},... | collective-permute-start | bytes 221192 | tf_op jit(solution)/shard_map/ppermute | solution.py:322
  14.0 0.0 collective-permute-start.4
  14.0 0.8 %collective-permute-start.3 = (f32[72,256]{1,0:T(8,128)S(1)}, f32[72,256]{1,0:T(8,128)S(1)}, u32[]{:S(2)}, u32[]{:S(2)}) collective-permute-start(f32[72,256]{1,0:T(8,128)S(1)} %shard_map.48.own.one.after.refs_0_), channel_id=1, source_target_pairs={{0,4},{1,5},{2,6},{3,7},{4,0},{5,1},{6,2},{7,3},{8,12},{9,13},{10,... | collective-permute-start | bytes 221192 | tf_op jit(solution)/shard_map/ppermute | solution.py:322
  14.8 0.3 shard_map.49.after.refs_4_
  15.1 3.3 %shard_map.53.refs_9_ = bf16[3,256,512]{2,1,0:T(8,128)(2,1)S(1)} custom-call(f32[56,256]{1,0:T(8,128)S(1)} %collective-permute-done.refs_1_.refs_0_, f32[56,256]{1,0:T(8,128)S(1)} %collective-permute-done.1.refs_2_.refs_1_, f32[56,256]{1,0:T(8,128)S(1)} %collective-permute-done.2.refs_3_.refs_2_), custom_call_target="tpu_custom_call" | custom-call | flops 402653184 | bytes 262144 | tf_op jit(solution)/shard_map/pallas_call | solution.py:384
  18.4 0.0 collective-permute-done.5.one.refs_3_
  18.4 0.3 shard_map.50.after.refs_7_
  18.7 1.5 %collective-permute-done.4.one.refs_2_ = f32[72,256]{1,0:T(8,128)S(1)} collective-permute-done((f32[72,256]{1,0:T(8,128)S(1)}, f32[72,256]{1,0:T(8,128)S(1)}, u32[]{:S(2)}, u32[]{:S(2)}) %collective-permute-start.4) | collective-permute-done | bytes 73760 | tf_op jit(solution)/shard_map/ppermute | solution.py:322
  20.2 0.3 shard_map.51.after.refs_6_
  20.6 0.0 collective-permute-done.3.one.refs_1_
  20.6 0.3 shard_map.52.refs_5_
  20.9 1.0 %shard_map.54 = (f32[64,256]{1,0:T(8,128)S(1)}, f32[64,256]{1,0:T(8,128)S(1)}, f32[2,8,512]{2,1,0:T(8,128)S(1)}) custom-call(f32[72,256]{1,0:T(8,128)S(1)} %shard_map.48.own.one.after.refs_0_, f32[72,256]{1,0:T(8,128)S(1)} %collective-permute-done.3.one.refs_1_, f32[72,256]{1,0:T(8,128)S(1)} %collective-permute-done.4.one.refs_2_, ...), custom_call_target="tpu_custom_call" | custom-call | flops 134217728 | bytes 262144 | tf_op jit(solution)/shard_map/pallas_call | solution.py:427
  21.9 2.7 %collective-permute-start.8 = (f32[64,256]{1,0:T(8,128)S(1)}, f32[64,256]{1,0:T(8,128)S(1)}, u32[]{:S(2)}, u32[]{:S(2)}) collective-permute-start(f32[64,256]{1,0:T(8,128)S(1)} %get-tuple-element.25.refs_0_), channel_id=1, source_target_pairs={{0,12},{1,13},{2,14},{3,15},{4,8},{5,9},{6,10},{7,11},{8,4},{9,5},... | collective-permute-start | bytes 196616 | tf_op jit(solution)/shard_map/ppermute | solution.py:322
  24.7 0.0 collective-permute-start.7
  24.7 1.7 %collective-permute-start.6 = (f32[64,256]{1,0:T(8,128)S(1)}, f32[64,256]{1,0:T(8,128)S(1)}, u32[]{:S(2)}, u32[]{:S(2)}) collective-permute-start(f32[64,256]{1,0:T(8,128)S(1)} %get-tuple-element.25.refs_0_), channel_id=1, source_target_pairs={{0,4},{1,5},{2,6},{3,7},{4,0},{5,1},{6,2},{7,3},{8,12},{9,13},{10,... | collective-permute-start | bytes 196616 | tf_op jit(solution)/shard_map/ppermute | solution.py:322
  26.3 1.3 %shard_map.55 = (bf16[256,8192]{1,0:T(8,128)(2,1)S(1)}, bf16[256,8192]{1,0:T(8,128)(2,1)S(1)}) custom-call(s32[64,128]{1,0:T(8,128)S(1)} %get-tuple-element.28.mask_ids.refs_5_, f32[2,8,512]{2,1,0:T(8,128)S(1)} %get-tuple-element.26.after.refs_8_), custom_call_target="tpu_custom_call" | custom-call | flops 536870912 | bytes 8388608 | tf_op jit(solution)/shard_map/pallas_call | solution.py:440
  27.6 1.0 %collective-permute-done.8.refs_3_ = f32[64,256]{1,0:T(8,128)S(1)} collective-permute-done((f32[64,256]{1,0:T(8,128)S(1)}, f32[64,256]{1,0:T(8,128)S(1)}, u32[]{:S(2)}, u32[]{:S(2)}) %collective-permute-start.8) | collective-permute-done | bytes 65568 | tf_op jit(solution)/shard_map/ppermute | solution.py:322
  28.6 1.9 %collective-permute-done.7.refs_2_ = f32[64,256]{1,0:T(8,128)S(1)} collective-permute-done((f32[64,256]{1,0:T(8,128)S(1)}, f32[64,256]{1,0:T(8,128)S(1)}, u32[]{:S(2)}, u32[]{:S(2)}) %collective-permute-start.7) | collective-permute-done | bytes 65568 | tf_op jit(solution)/shard_map/ppermute | solution.py:322
  30.5 0.0 collective-permute-done.6.refs_1_
  30.5 0.8 %shard_map.56 = (f32[32,256]{1,0:T(8,128)S(1)}, f32[32,256]{1,0:T(8,128)S(1)}, f32[32,256]{1,0:T(8,128)S(1)}, f32[32,256]{1,0:T(8,128)S(1)}) custom-call(f32[64,256]{1,0:T(8,128)S(1)} %get-tuple-element.25.refs_0_, f32[64,256]{1,0:T(8,128)S(1)} %collective-permute-done.6.refs_1_, f32[64,256]{1,0:T(8,128)S(1)} %collective-permute-done.7.refs_2_, ...), custom_call_target="tpu_custom_call" | custom-call | flops 134217728 | bytes 262144 | tf_op jit(solution)/shard_map/pallas_call | solution.py:449
  31.3 1.4 %collective-permute-start.9 = (f32[32,256]{1,0:T(8,128)S(1)}, f32[32,256]{1,0:T(8,128)S(1)}, u32[]{:S(2)}, u32[]{:S(2)}) collective-permute-start(f32[32,256]{1,0:T(8,128)S(1)} %get-tuple-element.31), channel_id=1, source_target_pairs={{0,2},{1,3},{2,0},{3,1},{4,6},{5,7},{6,4},{7,5},{8,10},{9,11},{10,... | collective-permute-start | bytes 98312 | tf_op jit(solution)/shard_map/ppermute | solution.py:317
  32.7 0.0 collective-permute-start.10
  32.7 0.8 %collective-permute-start.11 = (f32[32,256]{1,0:T(8,128)S(1)}, f32[32,256]{1,0:T(8,128)S(1)}, u32[]{:S(2)}, u32[]{:S(2)}) collective-permute-start(f32[32,256]{1,0:T(8,128)S(1)} %get-tuple-element.33), channel_id=1, source_target_pairs={{0,1},{1,0},{2,3},{3,2},{4,5},{5,4},{6,7},{7,6},{8,9},{9,8},{10,11... | collective-permute-start | bytes 98312 | tf_op jit(solution)/shard_map/ppermute | solution.py:317
  33.4 1.8 %collective-permute-done.9.refs_1_ = f32[32,256]{1,0:T(8,128)S(1)} collective-permute-done((f32[32,256]{1,0:T(8,128)S(1)}, f32[32,256]{1,0:T(8,128)S(1)}, u32[]{:S(2)}, u32[]{:S(2)}) %collective-permute-start.9) | collective-permute-done | bytes 32800 | tf_op jit(solution)/shard_map/ppermute | solution.py:317
  35.2 0.9 %collective-permute-done.10.refs_2_ = f32[32,256]{1,0:T(8,128)S(1)} collective-permute-done((f32[32,256]{1,0:T(8,128)S(1)}, f32[32,256]{1,0:T(8,128)S(1)}, u32[]{:S(2)}, u32[]{:S(2)}) %collective-permute-start.10) | collective-permute-done | bytes 32800 | tf_op jit(solution)/shard_map/ppermute | solution.py:317
  36.2 0.0 collective-permute-done.11.refs_3_
  36.2 2.2 %shard_map.57 = f32[64,8192]{1,0:T(8,128)} custom-call(f32[32,256]{1,0:T(8,128)S(1)} %get-tuple-element.30.refs_0_, f32[32,256]{1,0:T(8,128)S(1)} %collective-permute-done.9.refs_1_, f32[32,256]{1,0:T(8,128)S(1)} %collective-permute-done.10.refs_2_, f32[32,256]{1,0:T(8,128)S(1)} %collective-permute-done.11.refs_3_, ...), custom_call_target="tpu_custom_call" | custom-call | flops 536870912 | bytes 4194304 | tf_op jit(solution)/shard_map/pallas_call | solution.py:459
  (1 shorter events, 0.0 us)
Async XLA Ops:
  3.3 5.2 %collective-permute-start = (f32[56,256]{1,0:T(8,128)S(1)}, f32[56,256]{1,0:T(8,128)S(1)}, u32[]{:S(2)}, u32[]{:S(2)}) collective-permute-start(f32[56,256]{1,0:T(8,128)S(1)} %get-tuple-element.22), channel_id=1, source_target_pairs={{0,2},{1,3},{2,0},{3,1},{4,6},{5,7},{6,4},{7,5},{8,10},{9,11},{10,... | collective-permute-start | bytes 172040 | tf_op jit(solution)/shard_map/ppermute | solution.py:317
  6.4 4.0 %collective-permute-start.1 = (f32[56,256]{1,0:T(8,128)S(1)}, f32[56,256]{1,0:T(8,128)S(1)}, u32[]{:S(2)}, u32[]{:S(2)}) collective-permute-start(f32[56,256]{1,0:T(8,128)S(1)} %get-tuple-element.23), channel_id=1, source_target_pairs={{0,3},{1,2},{2,1},{3,0},{4,7},{5,6},{6,5},{7,4},{8,11},{9,10},{10,... | collective-permute-start | bytes 172040 | tf_op jit(solution)/shard_map/ppermute | solution.py:317
  6.4 4.0 %collective-permute-start.2 = (f32[56,256]{1,0:T(8,128)S(1)}, f32[56,256]{1,0:T(8,128)S(1)}, u32[]{:S(2)}, u32[]{:S(2)}) collective-permute-start(f32[56,256]{1,0:T(8,128)S(1)} %get-tuple-element.24), channel_id=1, source_target_pairs={{0,1},{1,0},{2,3},{3,2},{4,5},{5,4},{6,7},{7,6},{8,9},{9,8},{10,11... | collective-permute-start | bytes 172040 | tf_op jit(solution)/shard_map/ppermute | solution.py:317
  10.3 8.1 %collective-permute-start.5 = (f32[72,256]{1,0:T(8,128)S(1)}, f32[72,256]{1,0:T(8,128)S(1)}, u32[]{:S(2)}, u32[]{:S(2)}) collective-permute-start(f32[72,256]{1,0:T(8,128)S(1)} %shard_map.48.own.one.after.refs_0_), channel_id=1, source_target_pairs={{0,12},{1,13},{2,14},{3,15},{4,8},{5,9},{6,10},{7,11},{8,4},{9,5},... | collective-permute-start | bytes 221192 | tf_op jit(solution)/shard_map/ppermute | solution.py:322
  14.0 6.2 %collective-permute-start.4 = (f32[72,256]{1,0:T(8,128)S(1)}, f32[72,256]{1,0:T(8,128)S(1)}, u32[]{:S(2)}, u32[]{:S(2)}) collective-permute-start(f32[72,256]{1,0:T(8,128)S(1)} %shard_map.48.own.one.after.refs_0_), channel_id=1, source_target_pairs={{0,8},{1,9},{2,10},{3,11},{4,12},{5,13},{6,14},{7,15},{8,0},{9,1},... | collective-permute-start | bytes 221192 | tf_op jit(solution)/shard_map/ppermute | solution.py:322
  14.0 6.5 %collective-permute-start.3 = (f32[72,256]{1,0:T(8,128)S(1)}, f32[72,256]{1,0:T(8,128)S(1)}, u32[]{:S(2)}, u32[]{:S(2)}) collective-permute-start(f32[72,256]{1,0:T(8,128)S(1)} %shard_map.48.own.one.after.refs_0_), channel_id=1, source_target_pairs={{0,4},{1,5},{2,6},{3,7},{4,0},{5,1},{6,2},{7,3},{8,12},{9,13},{10,... | collective-permute-start | bytes 221192 | tf_op jit(solution)/shard_map/ppermute | solution.py:322
  21.9 6.7 %collective-permute-start.8 = (f32[64,256]{1,0:T(8,128)S(1)}, f32[64,256]{1,0:T(8,128)S(1)}, u32[]{:S(2)}, u32[]{:S(2)}) collective-permute-start(f32[64,256]{1,0:T(8,128)S(1)} %get-tuple-element.25.refs_0_), channel_id=1, source_target_pairs={{0,12},{1,13},{2,14},{3,15},{4,8},{5,9},{6,10},{7,11},{8,4},{9,5},... | collective-permute-start | bytes 196616 | tf_op jit(solution)/shard_map/ppermute | solution.py:322
  24.7 5.9 %collective-permute-start.7 = (f32[64,256]{1,0:T(8,128)S(1)}, f32[64,256]{1,0:T(8,128)S(1)}, u32[]{:S(2)}, u32[]{:S(2)}) collective-permute-start(f32[64,256]{1,0:T(8,128)S(1)} %get-tuple-element.25.refs_0_), channel_id=1, source_target_pairs={{0,8},{1,9},{2,10},{3,11},{4,12},{5,13},{6,14},{7,15},{8,0},{9,1},... | collective-permute-start | bytes 196616 | tf_op jit(solution)/shard_map/ppermute | solution.py:322
  24.7 5.9 %collective-permute-start.6 = (f32[64,256]{1,0:T(8,128)S(1)}, f32[64,256]{1,0:T(8,128)S(1)}, u32[]{:S(2)}, u32[]{:S(2)}) collective-permute-start(f32[64,256]{1,0:T(8,128)S(1)} %get-tuple-element.25.refs_0_), channel_id=1, source_target_pairs={{0,4},{1,5},{2,6},{3,7},{4,0},{5,1},{6,2},{7,3},{8,12},{9,13},{10,... | collective-permute-start | bytes 196616 | tf_op jit(solution)/shard_map/ppermute | solution.py:322
  31.3 3.9 %collective-permute-start.9 = (f32[32,256]{1,0:T(8,128)S(1)}, f32[32,256]{1,0:T(8,128)S(1)}, u32[]{:S(2)}, u32[]{:S(2)}) collective-permute-start(f32[32,256]{1,0:T(8,128)S(1)} %get-tuple-element.31), channel_id=1, source_target_pairs={{0,2},{1,3},{2,0},{3,1},{4,6},{5,7},{6,4},{7,5},{8,10},{9,11},{10,... | collective-permute-start | bytes 98312 | tf_op jit(solution)/shard_map/ppermute | solution.py:317
  32.7 3.5 %collective-permute-start.10 = (f32[32,256]{1,0:T(8,128)S(1)}, f32[32,256]{1,0:T(8,128)S(1)}, u32[]{:S(2)}, u32[]{:S(2)}) collective-permute-start(f32[32,256]{1,0:T(8,128)S(1)} %get-tuple-element.32), channel_id=1, source_target_pairs={{0,3},{1,2},{2,1},{3,0},{4,7},{5,6},{6,5},{7,4},{8,11},{9,10},{10,... | collective-permute-start | bytes 98312 | tf_op jit(solution)/shard_map/ppermute | solution.py:317
  32.7 3.5 %collective-permute-start.11 = (f32[32,256]{1,0:T(8,128)S(1)}, f32[32,256]{1,0:T(8,128)S(1)}, u32[]{:S(2)}, u32[]{:S(2)}) collective-permute-start(f32[32,256]{1,0:T(8,128)S(1)} %get-tuple-element.33), channel_id=1, source_target_pairs={{0,1},{1,0},{2,3},{3,2},{4,5},{5,4},{6,7},{7,6},{8,9},{9,8},{10,11... | collective-permute-start | bytes 98312 | tf_op jit(solution)/shard_map/ppermute | solution.py:317

commit v19 on v18

--- a/solution.py
+++ b/solution.py
@@ -12,7 +12,7 @@
 BLOCK = 1024
 VMEM_BYTES = 32 * 1024 * 1024
 NEAR = 4
-NEAR_STEPS = (0, 2, 3, 1)
+NEAR_STEPS = (0, 1, 2, 3)
 F32, BF16 = jnp.float32, jnp.bfloat16
 NT = (((1,), (1,)), ((), ()))
 NN = (((1,), (0,)), ((), ()))
@@ -233,7 +233,8 @@
 
 
 def change_kernel(far, part, *refs):
-    parts, tables, (own_pairs, pairs, mean, sums, scale) = refs[:far], refs[far:-5], refs[-5:]
+    parts, tables, pairs, (mean, sums, scale) = refs[:far], refs[far:-6], refs[-6:-3], refs[-3:]
+    pairs = [(group, k) for group in pairs for k in range(group.shape[0])]
     slots = mean.shape[1]
 
     def tile(t, at):
@@ -253,7 +254,7 @@
     for k in range(NEAR):
         cut = slice(part * k, part * (k + 1))
         both = jnp.concatenate(split(mean[cut]), axis=0)
-        change = dot(both, own_pairs[0] if k == 0 else pairs[k - 1])
+        change = dot(both, pairs[k][0][pairs[k][1]])
         change = change[:part] + change[part:]
         sums[cut] = parts[0][cut] + (change[:, :slots] + change[:, slots:])
 
@@ -396,18 +397,18 @@
         )(*parts)
 
     arrived = near_exchange(sends, n)
-    own_pairs = pair_counts(arrived[:1])
+    pairs = [pair_counts(arrived[:1]), pair_counts(arrived[1:2])]
     joined = call(
         functools.partial(join_kernel, part),
         array((columns + 2 * NEAR, slots), F32),
-        [vmem] * (NEAR + 1),
+        [vmem] * (NEAR + 2),
         vmem,
         [],
         0,
         message.size * 8,
-    )(*arrived, own_pairs)
+    )(*arrived, *pairs)
     shared = far_share(joined, n)
-    pairs = pair_counts(arrived[1:])
+    pairs.append(pair_counts(arrived[2:]))
     tables = []
     if keep:
         after = joined
@@ -427,12 +428,12 @@
     mean, sums, scales = call(
         functools.partial(change_kernel, far, part),
         [of_near, of_near, scale],
-        [vmem] * (far + len(tables) + 2),
+        [vmem] * (far + len(tables) + len(pairs)),
         [vmem] * 3,
         [],
         work // 4,
         slots * slots * 4,
-    )(*shared, *tables, own_pairs, pairs)
+    )(*shared, *tables, *pairs)
     again = far_share(sums, n)
     source = tables if keep else shared
     spreads = []

time: 38.5 us -> 38.6 us (level)
  waiting for transfers between devices: 9.67 us -> 10.1 us
    ppermute x6, waiting for transfers between devices: 4.41 us -> 5.94 us  [far_share(): return [one] + [lax.ppermute(one, 'rows', step) for step in steps]]
    ppermute x6, waiting for transfers between devices: 5.25 us -> 4.11 us  [near_exchange(): lax.ppermute(one, 'rows', step)]
    pallas_call x2 -> x3, Pallas kernels: 4.52 us -> 4.55 us  [pair_counts(): call(functools.partial(pairs_kernel, pad, about), array((len(parts), slot...]
  transfers between devices with their start and end apart: 12 -> 12, of which waited for: 7 -> 6; matrix products, arithmetic and copies ran while one was open for 0% -> 0% of each run, Pallas kernels for 18% -> 18%
where the time goes in v19:
time: 38.6 us; the launch traced here: 38.5 us
  Pallas kernels  14.4 us (37%)
  starting transfers between devices  13.9 us (36%)
  waiting for transfers between devices  10.1 us (26%)
    ppermute x6, starting transfers between devices, far_share(): return [one] + [lax.ppermute(one, 'rows', step) for step in steps]  8.85 us
    ppermute x6, waiting for transfers between devices, far_share(): return [one] + [lax.ppermute(one, 'rows', step) for step in steps]  5.94 us
    ppermute x6, starting transfers between devices, near_exchange(): lax.ppermute(one, 'rows', step)  5.06 us
    pallas_call x3, Pallas kernels, pair_counts(): call(functools.partial(pairs_kernel, pad, about), array((len(parts), slot...  4.55 us
    ppermute x6, waiting for transfers between devices, near_exchange(): lax.ppermute(one, 'rows', step)  4.11 us
    pallas_call x1, Pallas kernels, body(): call(functools.partial(sums_kernel, pad, slots // n), [message] * NEAR +...  3.34 us
    pallas_call x1, Pallas kernels, body(): call(functools.partial(last_kernel, pad, part), array(whole, F32), [vmem]...  2.18 us
    pallas_call x1, Pallas kernels, body(): call(functools.partial(tables_kernel, pad), [array((slots, rows_dev), BF1...  1.27 us
  transfers between devices with their start and end apart: 12, of which 6 were waited for; matrix products, arithmetic and copies ran while one was open for 0% of the time, Pallas kernels for 18%

profile of v19, /device:TPU:0, one launch (start us, length us, event | category | flops | bytes accessed | tf_op | source)
XLA Modules:
  0.0 38.5 jit_solution(10256622827567797241)
XLA Ops:
  0.0 3.3 %shard_map.46 = (f32[56,256]{1,0:T(8,128)S(1)}, f32[56,256]{1,0:T(8,128)S(1)}, f32[56,256]{1,0:T(8,128)S(1)}, f32[56,256]{1,0:T(8,128)S(1)}, f32[64,8192]{1,0:T(...) custom-call(f32[64,8192]{1,0:T(8,128)} %refs_0_.1, s32[8,128]{1,0:T(8,128)} %bitcast.4, s32[64,128]{1,0:T(8,128)} %bitcast.3, ...), custom_call_target="tpu_custom_call" | custom-call | flops 1073741824 | bytes 2097152 | tf_op jit(solution)/shard_map/pallas_call | solution.py:365
  3.3 0.5 %collective-permute-start = (f32[56,256]{1,0:T(8,128)S(1)}, f32[56,256]{1,0:T(8,128)S(1)}, u32[]{:S(2)}, u32[]{:S(2)}) collective-permute-start(f32[56,256]{1,0:T(8,128)S(1)} %get-tuple-element.22), channel_id=1, source_target_pairs={{0,1},{1,0},{2,3},{3,2},{4,5},{5,4},{6,7},{7,6},{8,9},{9,8},{10,11... | collective-permute-start | bytes 172040 | tf_op jit(solution)/shard_map/ppermute | solution.py:318
  3.9 2.6 %collective-permute-start.1 = (f32[56,256]{1,0:T(8,128)S(1)}, f32[56,256]{1,0:T(8,128)S(1)}, u32[]{:S(2)}, u32[]{:S(2)}) collective-permute-start(f32[56,256]{1,0:T(8,128)S(1)} %get-tuple-element.23), channel_id=1, source_target_pairs={{0,2},{1,3},{2,0},{3,1},{4,6},{5,7},{6,4},{7,5},{8,10},{9,11},{10,... | collective-permute-start | bytes 172040 | tf_op jit(solution)/shard_map/ppermute | solution.py:318
  6.5 0.1 collective-permute-start.2
  6.5 1.2 %shard_map.47.refs_4_.refs_8_ = bf16[1,256,512]{2,1,0:T(8,128)(2,1)S(1)} custom-call(f32[56,256]{1,0:T(8,128)S(1)} %get-tuple-element.21.refs_0_), custom_call_target="tpu_custom_call" | custom-call | flops 134217728 | bytes 262144 | tf_op jit(solution)/shard_map/pallas_call | solution.py:385
  7.8 0.0 collective-permute-done.refs_0_.refs_1_
  7.8 1.2 %shard_map.48.refs_5_.refs_9_ = bf16[1,256,512]{2,1,0:T(8,128)(2,1)S(1)} custom-call(f32[56,256]{1,0:T(8,128)S(1)} %collective-permute-done.refs_0_.refs_1_), custom_call_target="tpu_custom_call" | custom-call | flops 134217728 | bytes 262144 | tf_op jit(solution)/shard_map/pallas_call | solution.py:385
  9.0 0.0 collective-permute-done.1.refs_2_.refs_0_
  9.0 1.3 %collective-permute-done.2.refs_3_.refs_1_ = f32[56,256]{1,0:T(8,128)S(1)} collective-permute-done((f32[56,256]{1,0:T(8,128)S(1)}, f32[56,256]{1,0:T(8,128)S(1)}, u32[]{:S(2)}, u32[]{:S(2)}) %collective-permute-start.2) | collective-permute-done | bytes 57376 | tf_op jit(solution)/shard_map/ppermute | solution.py:318
  10.3 3.7 %collective-permute-start.5 = (f32[72,256]{1,0:T(8,128)S(1)}, f32[72,256]{1,0:T(8,128)S(1)}, u32[]{:S(2)}, u32[]{:S(2)}) collective-permute-start(f32[72,256]{1,0:T(8,128)S(1)} %shard_map.49.own.one.after.refs_0_), channel_id=1, source_target_pairs={{0,12},{1,13},{2,14},{3,15},{4,8},{5,9},{6,10},{7,11},{8,4},{9,5},... | collective-permute-start | bytes 221192 | tf_op jit(solution)/shard_map/ppermute | solution.py:323
  14.0 0.0 collective-permute-start.4
  14.0 0.8 %collective-permute-start.3 = (f32[72,256]{1,0:T(8,128)S(1)}, f32[72,256]{1,0:T(8,128)S(1)}, u32[]{:S(2)}, u32[]{:S(2)}) collective-permute-start(f32[72,256]{1,0:T(8,128)S(1)} %shard_map.49.own.one.after.refs_0_), channel_id=1, source_target_pairs={{0,4},{1,5},{2,6},{3,7},{4,0},{5,1},{6,2},{7,3},{8,12},{9,13},{10,... | collective-permute-start | bytes 221192 | tf_op jit(solution)/shard_map/ppermute | solution.py:323
  14.8 0.3 shard_map.50.after.refs_4_
  15.1 2.1 %shard_map.54.refs_10_ = bf16[2,256,512]{2,1,0:T(8,128)(2,1)S(1)} custom-call(f32[56,256]{1,0:T(8,128)S(1)} %collective-permute-done.1.refs_2_.refs_0_, f32[56,256]{1,0:T(8,128)S(1)} %collective-permute-done.2.refs_3_.refs_1_), custom_call_target="tpu_custom_call" | custom-call | flops 268435456 | bytes 262144 | tf_op jit(solution)/shard_map/pallas_call | solution.py:385
  17.2 0.0 collective-permute-done.5.one.refs_3_
  17.2 0.3 shard_map.51.after.refs_7_
  17.5 3.0 %collective-permute-done.4.one.refs_2_ = f32[72,256]{1,0:T(8,128)S(1)} collective-permute-done((f32[72,256]{1,0:T(8,128)S(1)}, f32[72,256]{1,0:T(8,128)S(1)}, u32[]{:S(2)}, u32[]{:S(2)}) %collective-permute-start.4) | collective-permute-done | bytes 73760 | tf_op jit(solution)/shard_map/ppermute | solution.py:323
  20.5 0.3 shard_map.52.after.refs_6_
  20.8 0.0 collective-permute-done.3.one.refs_1_
  20.8 0.3 shard_map.53.refs_5_
  21.2 1.0 %shard_map.55 = (f32[64,256]{1,0:T(8,128)S(1)}, f32[64,256]{1,0:T(8,128)S(1)}, f32[2,8,512]{2,1,0:T(8,128)S(1)}) custom-call(f32[72,256]{1,0:T(8,128)S(1)} %shard_map.49.own.one.after.refs_0_, f32[72,256]{1,0:T(8,128)S(1)} %collective-permute-done.3.one.refs_1_, f32[72,256]{1,0:T(8,128)S(1)} %collective-permute-done.4.one.refs_2_, ...), custom_call_target="tpu_custom_call" | custom-call | flops 134217728 | bytes 262144 | tf_op jit(solution)/shard_map/pallas_call | solution.py:428
  22.2 2.5 %collective-permute-start.8 = (f32[64,256]{1,0:T(8,128)S(1)}, f32[64,256]{1,0:T(8,128)S(1)}, u32[]{:S(2)}, u32[]{:S(2)}) collective-permute-start(f32[64,256]{1,0:T(8,128)S(1)} %get-tuple-element.25.refs_0_), channel_id=1, source_target_pairs={{0,12},{1,13},{2,14},{3,15},{4,8},{5,9},{6,10},{7,11},{8,4},{9,5},... | collective-permute-start | bytes 196616 | tf_op jit(solution)/shard_map/ppermute | solution.py:323
  24.7 0.0 collective-permute-start.7
  24.7 1.9 %collective-permute-start.6 = (f32[64,256]{1,0:T(8,128)S(1)}, f32[64,256]{1,0:T(8,128)S(1)}, u32[]{:S(2)}, u32[]{:S(2)}) collective-permute-start(f32[64,256]{1,0:T(8,128)S(1)} %get-tuple-element.25.refs_0_), channel_id=1, source_target_pairs={{0,4},{1,5},{2,6},{3,7},{4,0},{5,1},{6,2},{7,3},{8,12},{9,13},{10,... | collective-permute-start | bytes 196616 | tf_op jit(solution)/shard_map/ppermute | solution.py:323
  26.6 1.3 %shard_map.56 = (bf16[256,8192]{1,0:T(8,128)(2,1)S(1)}, bf16[256,8192]{1,0:T(8,128)(2,1)S(1)}) custom-call(s32[64,128]{1,0:T(8,128)S(1)} %get-tuple-element.28.mask_ids.refs_5_, f32[2,8,512]{2,1,0:T(8,128)S(1)} %get-tuple-element.26.after.refs_8_), custom_call_target="tpu_custom_call" | custom-call | flops 536870912 | bytes 8388608 | tf_op jit(solution)/shard_map/pallas_call | solution.py:441
  27.9 0.4 %collective-permute-done.8.refs_3_ = f32[64,256]{1,0:T(8,128)S(1)} collective-permute-done((f32[64,256]{1,0:T(8,128)S(1)}, f32[64,256]{1,0:T(8,128)S(1)}, u32[]{:S(2)}, u32[]{:S(2)}) %collective-permute-start.8) | collective-permute-done | bytes 65568 | tf_op jit(solution)/shard_map/ppermute | solution.py:323
  28.3 2.6 %collective-permute-done.7.refs_2_ = f32[64,256]{1,0:T(8,128)S(1)} collective-permute-done((f32[64,256]{1,0:T(8,128)S(1)}, f32[64,256]{1,0:T(8,128)S(1)}, u32[]{:S(2)}, u32[]{:S(2)}) %collective-permute-start.7) | collective-permute-done | bytes 65568 | tf_op jit(solution)/shard_map/ppermute | solution.py:323
  30.8 0.0 collective-permute-done.6.refs_1_
  30.8 0.8 %shard_map.57 = (f32[32,256]{1,0:T(8,128)S(1)}, f32[32,256]{1,0:T(8,128)S(1)}, f32[32,256]{1,0:T(8,128)S(1)}, f32[32,256]{1,0:T(8,128)S(1)}) custom-call(f32[64,256]{1,0:T(8,128)S(1)} %get-tuple-element.25.refs_0_, f32[64,256]{1,0:T(8,128)S(1)} %collective-permute-done.6.refs_1_, f32[64,256]{1,0:T(8,128)S(1)} %collective-permute-done.7.refs_2_, ...), custom_call_target="tpu_custom_call" | custom-call | flops 134217728 | bytes 262144 | tf_op jit(solution)/shard_map/pallas_call | solution.py:450
  31.6 0.0 collective-permute-start.9
  31.6 1.3 %collective-permute-start.10 = (f32[32,256]{1,0:T(8,128)S(1)}, f32[32,256]{1,0:T(8,128)S(1)}, u32[]{:S(2)}, u32[]{:S(2)}) collective-permute-start(f32[32,256]{1,0:T(8,128)S(1)} %get-tuple-element.32), channel_id=1, source_target_pairs={{0,2},{1,3},{2,0},{3,1},{4,6},{5,7},{6,4},{7,5},{8,10},{9,11},{10,... | collective-permute-start | bytes 98312 | tf_op jit(solution)/shard_map/ppermute | solution.py:318
  32.9 0.5 %collective-permute-start.11 = (f32[32,256]{1,0:T(8,128)S(1)}, f32[32,256]{1,0:T(8,128)S(1)}, u32[]{:S(2)}, u32[]{:S(2)}) collective-permute-start(f32[32,256]{1,0:T(8,128)S(1)} %get-tuple-element.33), channel_id=1, source_target_pairs={{0,3},{1,2},{2,1},{3,0},{4,7},{5,6},{6,5},{7,4},{8,11},{9,10},{10,... | collective-permute-start | bytes 98312 | tf_op jit(solution)/shard_map/ppermute | solution.py:318
  33.5 0.0 collective-permute-done.9.refs_1_
  33.5 2.1 %collective-permute-done.10.refs_2_ = f32[32,256]{1,0:T(8,128)S(1)} collective-permute-done((f32[32,256]{1,0:T(8,128)S(1)}, f32[32,256]{1,0:T(8,128)S(1)}, u32[]{:S(2)}, u32[]{:S(2)}) %collective-permute-start.10) | collective-permute-done | bytes 32800 | tf_op jit(solution)/shard_map/ppermute | solution.py:318
  35.6 0.7 %collective-permute-done.11.refs_3_ = f32[32,256]{1,0:T(8,128)S(1)} collective-permute-done((f32[32,256]{1,0:T(8,128)S(1)}, f32[32,256]{1,0:T(8,128)S(1)}, u32[]{:S(2)}, u32[]{:S(2)}) %collective-permute-start.11) | collective-permute-done | bytes 32800 | tf_op jit(solution)/shard_map/ppermute | solution.py:318
  36.3 2.2 %shard_map.58 = f32[64,8192]{1,0:T(8,128)} custom-call(f32[32,256]{1,0:T(8,128)S(1)} %get-tuple-element.30.refs_0_, f32[32,256]{1,0:T(8,128)S(1)} %collective-permute-done.9.refs_1_, f32[32,256]{1,0:T(8,128)S(1)} %collective-permute-done.10.refs_2_, f32[32,256]{1,0:T(8,128)S(1)} %collective-permute-done.11.refs_3_, ...), custom_call_target="tpu_custom_call" | custom-call | flops 536870912 | bytes 4194304 | tf_op jit(solution)/shard_map/pallas_call | solution.py:460
  (1 shorter events, 0.0 us)
Async XLA Ops:
  3.3 4.4 %collective-permute-start = (f32[56,256]{1,0:T(8,128)S(1)}, f32[56,256]{1,0:T(8,128)S(1)}, u32[]{:S(2)}, u32[]{:S(2)}) collective-permute-start(f32[56,256]{1,0:T(8,128)S(1)} %get-tuple-element.22), channel_id=1, source_target_pairs={{0,1},{1,0},{2,3},{3,2},{4,5},{5,4},{6,7},{7,6},{8,9},{9,8},{10,11... | collective-permute-start | bytes 172040 | tf_op jit(solution)/shard_map/ppermute | solution.py:318
  3.9 5.1 %collective-permute-start.1 = (f32[56,256]{1,0:T(8,128)S(1)}, f32[56,256]{1,0:T(8,128)S(1)}, u32[]{:S(2)}, u32[]{:S(2)}) collective-permute-start(f32[56,256]{1,0:T(8,128)S(1)} %get-tuple-element.23), channel_id=1, source_target_pairs={{0,2},{1,3},{2,0},{3,1},{4,6},{5,7},{6,4},{7,5},{8,10},{9,11},{10,... | collective-permute-start | bytes 172040 | tf_op jit(solution)/shard_map/ppermute | solution.py:318
  6.5 3.9 %collective-permute-start.2 = (f32[56,256]{1,0:T(8,128)S(1)}, f32[56,256]{1,0:T(8,128)S(1)}, u32[]{:S(2)}, u32[]{:S(2)}) collective-permute-start(f32[56,256]{1,0:T(8,128)S(1)} %get-tuple-element.24), channel_id=1, source_target_pairs={{0,3},{1,2},{2,1},{3,0},{4,7},{5,6},{6,5},{7,4},{8,11},{9,10},{10,... | collective-permute-start | bytes 172040 | tf_op jit(solution)/shard_map/ppermute | solution.py:318
  10.3 6.9 %collective-permute-start.5 = (f32[72,256]{1,0:T(8,128)S(1)}, f32[72,256]{1,0:T(8,128)S(1)}, u32[]{:S(2)}, u32[]{:S(2)}) collective-permute-start(f32[72,256]{1,0:T(8,128)S(1)} %shard_map.49.own.one.after.refs_0_), channel_id=1, source_target_pairs={{0,12},{1,13},{2,14},{3,15},{4,8},{5,9},{6,10},{7,11},{8,4},{9,5},... | collective-permute-start | bytes 221192 | tf_op jit(solution)/shard_map/ppermute | solution.py:323
  14.0 6.5 %collective-permute-start.4 = (f32[72,256]{1,0:T(8,128)S(1)}, f32[72,256]{1,0:T(8,128)S(1)}, u32[]{:S(2)}, u32[]{:S(2)}) collective-permute-start(f32[72,256]{1,0:T(8,128)S(1)} %shard_map.49.own.one.after.refs_0_), channel_id=1, source_target_pairs={{0,8},{1,9},{2,10},{3,11},{4,12},{5,13},{6,14},{7,15},{8,0},{9,1},... | collective-permute-start | bytes 221192 | tf_op jit(solution)/shard_map/ppermute | solution.py:323
  14.0 6.8 %collective-permute-start.3 = (f32[72,256]{1,0:T(8,128)S(1)}, f32[72,256]{1,0:T(8,128)S(1)}, u32[]{:S(2)}, u32[]{:S(2)}) collective-permute-start(f32[72,256]{1,0:T(8,128)S(1)} %shard_map.49.own.one.after.refs_0_), channel_id=1, source_target_pairs={{0,4},{1,5},{2,6},{3,7},{4,0},{5,1},{6,2},{7,3},{8,12},{9,13},{10,... | collective-permute-start | bytes 221192 | tf_op jit(solution)/shard_map/ppermute | solution.py:323
  22.2 6.1 %collective-permute-start.8 = (f32[64,256]{1,0:T(8,128)S(1)}, f32[64,256]{1,0:T(8,128)S(1)}, u32[]{:S(2)}, u32[]{:S(2)}) collective-permute-start(f32[64,256]{1,0:T(8,128)S(1)} %get-tuple-element.25.refs_0_), channel_id=1, source_target_pairs={{0,12},{1,13},{2,14},{3,15},{4,8},{5,9},{6,10},{7,11},{8,4},{9,5},... | collective-permute-start | bytes 196616 | tf_op jit(solution)/shard_map/ppermute | solution.py:323
  24.7 6.2 %collective-permute-start.7 = (f32[64,256]{1,0:T(8,128)S(1)}, f32[64,256]{1,0:T(8,128)S(1)}, u32[]{:S(2)}, u32[]{:S(2)}) collective-permute-start(f32[64,256]{1,0:T(8,128)S(1)} %get-tuple-element.25.refs_0_), channel_id=1, source_target_pairs={{0,8},{1,9},{2,10},{3,11},{4,12},{5,13},{6,14},{7,15},{8,0},{9,1},... | collective-permute-start | bytes 196616 | tf_op jit(solution)/shard_map/ppermute | solution.py:323
  24.7 6.2 %collective-permute-start.6 = (f32[64,256]{1,0:T(8,128)S(1)}, f32[64,256]{1,0:T(8,128)S(1)}, u32[]{:S(2)}, u32[]{:S(2)}) collective-permute-start(f32[64,256]{1,0:T(8,128)S(1)} %get-tuple-element.25.refs_0_), channel_id=1, source_target_pairs={{0,4},{1,5},{2,6},{3,7},{4,0},{5,1},{6,2},{7,3},{8,12},{9,13},{10,... | collective-permute-start | bytes 196616 | tf_op jit(solution)/shard_map/ppermute | solution.py:323
  31.6 1.9 %collective-permute-start.9 = (f32[32,256]{1,0:T(8,128)S(1)}, f32[32,256]{1,0:T(8,128)S(1)}, u32[]{:S(2)}, u32[]{:S(2)}) collective-permute-start(f32[32,256]{1,0:T(8,128)S(1)} %get-tuple-element.31), channel_id=1, source_target_pairs={{0,1},{1,0},{2,3},{3,2},{4,5},{5,4},{6,7},{7,6},{8,9},{9,8},{10,11... | collective-permute-start | bytes 98312 | tf_op jit(solution)/shard_map/ppermute | solution.py:318
  31.6 4.0 %collective-permute-start.10 = (f32[32,256]{1,0:T(8,128)S(1)}, f32[32,256]{1,0:T(8,128)S(1)}, u32[]{:S(2)}, u32[]{:S(2)}) collective-permute-start(f32[32,256]{1,0:T(8,128)S(1)} %get-tuple-element.32), channel_id=1, source_target_pairs={{0,2},{1,3},{2,0},{3,1},{4,6},{5,7},{6,4},{7,5},{8,10},{9,11},{10,... | collective-permute-start | bytes 98312 | tf_op jit(solution)/shard_map/ppermute | solution.py:318
  32.9 3.3 %collective-permute-start.11 = (f32[32,256]{1,0:T(8,128)S(1)}, f32[32,256]{1,0:T(8,128)S(1)}, u32[]{:S(2)}, u32[]{:S(2)}) collective-permute-start(f32[32,256]{1,0:T(8,128)S(1)} %get-tuple-element.33), channel_id=1, source_target_pairs={{0,3},{1,2},{2,1},{3,0},{4,7},{5,6},{6,5},{7,4},{8,11},{9,10},{10,... | collective-permute-start | bytes 98312 | tf_op jit(solution)/shard_map/ppermute | solution.py:318

commit v20 on v19

--- a/solution.py
+++ b/solution.py
@@ -259,23 +259,10 @@
         sums[cut] = parts[0][cut] + (change[:, :slots] + change[:, slots:])
 
 
-def means_kernel(far, part, kept, *refs):
-    parts, source, (scale, mean), sends, second = refs[:far], refs[far:-8], refs[-8:-6], refs[-5:-1], refs[-1]
-
-    def tile(t, at):
-        same = [table[t] if kept else same_firm(source[0], table, part, at) for table in source]
-        same = jnp.concatenate(same, axis=0)
-        found = dot(gathered(parts, part, at), same)
-        spread_out((found[:part] + found[part:]) * scale[t][:1], second, part, at)
-
-    each_tile(mean.shape[1], tile)
+def tables_kernel(pad, mask_ids, mean, spread, workers, *sends):
+    part = mean.shape[0] // NEAR
     for k, send in enumerate(sends):
-        cut = slice(part * k, part * (k + 1))
-        send[:part] = mean[cut]
-        send[part:] = mean[cut] + second[cut]
-
-
-def tables_kernel(pad, mask_ids, after, spread, workers):
+        send[...] = mean[part * k : part * (k + 1)]
     slots, width = spread.shape
     table = same_worker(pad, 256)
     for b in range(width // BLOCK):
@@ -286,28 +273,56 @@
             workers[:, b * BLOCK + at : b * BLOCK + at + 256] = count.astype(BF16)
 
 
-def last_kernel(pad, part, *refs):
-    parts, (x1, mask_ids, weight), tables, (out, means, y, sems) = refs[:NEAR], refs[NEAR : NEAR + 3], refs[NEAR + 3 : -4], refs[-4:]
-    outs = column_copies(y, out, sems, 2 * BLOCK)
+def means_kernel(far, part, kept, *refs):
+    parts, source, scale, sends, mean = refs[:far], refs[far:-7], refs[-7], refs[-5:-1], refs[-1]
+
+    def tile(t, at):
+        same = [table[t] if kept else same_firm(source[0], table, part, at) for table in source]
+        same = jnp.concatenate(same, axis=0)
+        found = dot(gathered(parts, part, at), same)
+        spread_out((found[:part] + found[part:]) * scale[t][:1], mean, part, at)
+
+    each_tile(mean.shape[1], tile)
+    for k, send in enumerate(sends):
+        send[...] = mean[part * k : part * (k + 1)]
+
+
+def own_means(parts, means):
     me = lax.axis_index("rows") % NEAR
-    columns, slots = means.shape[1:]
+    part = parts[0].shape[0]
     for step, one in zip(NEAR_STEPS, parts):
-        at = pl.ds(pl.multiple_of((me ^ step) * part, part), part)
-        means[0, at, :] = one[:part]
-        means[1, at, :] = one[part:]
-    first, total = (jnp.concatenate(split(means[k]), axis=0) for k in range(2))
+        means[pl.ds(pl.multiple_of((me ^ step) * part, part), part), :] = one[...]
+    return jnp.concatenate(split(means[...]), axis=0)
+
+
+def first_kernel(pad, *refs):
+    parts, (x1, mask_ids, weight), tables, (y, means) = refs[:NEAR], refs[NEAR : NEAR + 3], refs[NEAR + 3 : -2], refs[-2:]
+    columns, slots = means.shape
+    first = own_means(parts, means)
     table = same_worker(pad, 256)
-    for b in range(2 * len(outs)):
+    for b in range(y.shape[1] // BLOCK):
         at = slice(b * BLOCK, (b + 1) * BLOCK)
+        found = tables[0][:, at] if tables else one_hot(row(mask_ids, b, BLOCK), slots)
+        spread = dot(first, found)
+        spread = spread[:columns] + spread[columns:]
         if tables:
-            spread = dot(total, tables[0][:, at])
             worker = dot(first, tables[1][:, at])
             worker = worker[:columns] + worker[columns:]
         else:
-            found = one_hot(row(mask_ids, b, BLOCK), slots)
-            spread, worker = dot(total, found), dot(first, found)
-            worker = by_worker(worker[:columns] + worker[columns:], table)
-        y[:, at] = x1[:, at] - (spread[:columns] + spread[columns:]) + worker * row(weight, b, BLOCK)
+            worker = by_worker(spread, table)
+        y[:, at] = x1[:, at] - spread + worker * row(weight, b, BLOCK)
+
+
+def last_kernel(*refs):
+    parts, (before, mask_ids), tables, (out, means, y, sems) = refs[:NEAR], refs[NEAR : NEAR + 2], refs[NEAR + 2 : -4], refs[-4:]
+    outs = column_copies(y, out, sems, 2 * BLOCK)
+    columns, slots = means.shape
+    second = own_means(parts, means)
+    for b in range(2 * len(outs)):
+        at = slice(b * BLOCK, (b + 1) * BLOCK)
+        found = tables[0][:, at] if tables else one_hot(row(mask_ids, b, BLOCK), slots)
+        spread = dot(second, found)
+        y[:, at] = before[:, at] - (spread[:columns] + spread[columns:])
         if b % 2:
             outs[b // 2].start()
     wait_all(outs)
@@ -437,35 +452,47 @@
     again = far_share(sums, n)
     source = tables if keep else shared
     spreads = []
+    sends = [mean[part * k : part * (k + 1)] for k in range(NEAR)]
     if keep:
-        spreads = call(
+        *spreads, a, b, c, d = call(
             functools.partial(tables_kernel, pad),
-            [array((slots, rows_dev), BF16)] * 2,
+            [array((slots, rows_dev), BF16)] * 2 + [array((part, slots), F32)] * NEAR,
             [vmem] * 2,
-            [vmem] * 2,
+            [vmem] * (2 + NEAR),
             [],
             work,
             4 * slots * rows_dev,
-        )(mask_ids, scales)
+        )(mask_ids, mean)
+        sends = [a, b, c, d]
+    first = near_exchange(sends, n)
     sends = call(
         functools.partial(means_kernel, far, part, keep),
-        [array((2 * part, slots), F32)] * NEAR,
-        [vmem] * (far + len(source) + 3),
+        [array((part, slots), F32)] * NEAR,
+        [vmem] * (far + len(source) + 2),
         [vmem] * NEAR,
         [pltpu.VMEM((columns, slots), F32)],
         work // 4,
         slots * slots * 4,
-    )(*again, *source, scales, mean, spreads[1] if keep else mean)
+    )(*again, *source, scales, spreads[1] if keep else scales)
     arrived = near_exchange(sends, n)
-    return call(
-        functools.partial(last_kernel, pad, part),
+    before = call(
+        functools.partial(first_kernel, pad),
         array(whole, F32),
         [vmem] * (NEAR + 3 + len(spreads)),
-        hbm,
-        [pltpu.VMEM((2, columns, slots), F32), pltpu.VMEM(whole, F32), sems],
+        vmem,
+        [pltpu.VMEM((columns, slots), F32)],
         work,
         8 * columns * rows_dev,
-    )(*arrived, x1, mask_ids, weight, *spreads)
+    )(*first, x1, mask_ids, weight, *spreads)
+    return call(
+        last_kernel,
+        array(whole, F32),
+        [vmem] * (NEAR + 2 + len(spreads[:1])),
+        hbm,
+        [pltpu.VMEM((columns, slots), F32), pltpu.VMEM(whole, F32), sems],
+        work,
+        8 * columns * rows_dev,
+    )(*arrived, before, mask_ids, *spreads[:1])
 
 
 def solution(mesh):

time: 38.6 us -> 37.9 us (0.982)
  waiting for transfers between devices: 10.1 us -> 6.57 us
  starting transfers between devices: 13.9 us -> 15.8 us
  Pallas kernels: 14.4 us -> 15.2 us
    ppermute x6, waiting for transfers between devices: 5.94 us -> 3.99 us  [far_share(): return [one] + [lax.ppermute(one, 'rows', step) for step in steps]]
    ppermute x6 -> x9, starting transfers between devices: 5.06 us -> 6.99 us  [near_exchange(): lax.ppermute(one, 'rows', step)]
    ppermute x6 -> x9, waiting for transfers between devices: 4.11 us -> 2.58 us  [near_exchange(): lax.ppermute(one, 'rows', step)]
    pallas_call x2 -> x3, Pallas kernels: 2.94 us -> 3.78 us  [the longest x1 1.7 us: body(): call(last_kernel, array(whole, F32), [vmem] * (NEAR + 2 + len(spreads[:1]...]
  transfers between devices with their start and end apart: 12 -> 15, of which waited for: 6 -> 5; matrix products, arithmetic and copies ran while one was open for 0% -> 0% of each run, Pallas kernels for 18% -> 23%
where the time goes in v20:
time: 37.9 us; the launch traced here: 37.8 us
  starting transfers between devices  15.8 us (42%)
  Pallas kernels  15.2 us (40%)
  waiting for transfers between devices  6.57 us (17%)
    ppermute x6, starting transfers between devices, far_share(): return [one] + [lax.ppermute(one, 'rows', step) for step in steps]  8.85 us
    ppermute x9, starting transfers between devices, near_exchange(): lax.ppermute(one, 'rows', step)  6.99 us
    pallas_call x3, Pallas kernels, pair_counts(): call(functools.partial(pairs_kernel, pad, about), array((len(parts), slot...  4.55 us
    ppermute x6, waiting for transfers between devices, far_share(): return [one] + [lax.ppermute(one, 'rows', step) for step in steps]  3.99 us
    pallas_call x1, Pallas kernels, body(): call(functools.partial(sums_kernel, pad, slots // n), [message] * NEAR +...  3.34 us
    ppermute x9, waiting for transfers between devices, near_exchange(): lax.ppermute(one, 'rows', step)  2.58 us
    pallas_call x1, Pallas kernels, body(): call(last_kernel, array(whole, F32), [vmem] * (NEAR + 2 + len(spreads[:1]...  1.7 us
    pallas_call x1, Pallas kernels, body(): call(functools.partial(first_kernel, pad), array(whole, F32), [vmem] * (N...  1.32 us
  transfers between devices with their start and end apart: 15, of which 5 were waited for; matrix products, arithmetic and copies ran while one was open for 0% of the time, Pallas kernels for 23%

profile of v20, /device:TPU:0, one launch (start us, length us, event | category | flops | bytes accessed | tf_op | source)
XLA Modules:
  0.0 37.8 jit_solution(2417716036197483328)
XLA Ops:
  0.0 3.3 %shard_map.46 = (f32[56,256]{1,0:T(8,128)S(1)}, f32[56,256]{1,0:T(8,128)S(1)}, f32[56,256]{1,0:T(8,128)S(1)}, f32[56,256]{1,0:T(8,128)S(1)}, f32[64,8192]{1,0:T(...) custom-call(f32[64,8192]{1,0:T(8,128)} %refs_0_.1, s32[8,128]{1,0:T(8,128)} %bitcast.4, s32[64,128]{1,0:T(8,128)} %bitcast.3, ...), custom_call_target="tpu_custom_call" | custom-call | flops 1073741824 | bytes 2097152 | tf_op jit(solution)/shard_map/pallas_call | solution.py:380
  3.3 0.5 %collective-permute-start = (f32[56,256]{1,0:T(8,128)S(1)}, f32[56,256]{1,0:T(8,128)S(1)}, u32[]{:S(2)}, u32[]{:S(2)}) collective-permute-start(f32[56,256]{1,0:T(8,128)S(1)} %get-tuple-element.26), channel_id=1, source_target_pairs={{0,1},{1,0},{2,3},{3,2},{4,5},{5,4},{6,7},{7,6},{8,9},{9,8},{10,11... | collective-permute-start | bytes 172040 | tf_op jit(solution)/shard_map/ppermute | solution.py:333
  3.9 2.6 %collective-permute-start.1 = (f32[56,256]{1,0:T(8,128)S(1)}, f32[56,256]{1,0:T(8,128)S(1)}, u32[]{:S(2)}, u32[]{:S(2)}) collective-permute-start(f32[56,256]{1,0:T(8,128)S(1)} %get-tuple-element.27), channel_id=1, source_target_pairs={{0,2},{1,3},{2,0},{3,1},{4,6},{5,7},{6,4},{7,5},{8,10},{9,11},{10,... | collective-permute-start | bytes 172040 | tf_op jit(solution)/shard_map/ppermute | solution.py:333
  6.5 0.1 collective-permute-start.2
  6.5 1.2 %shard_map.47.refs_4_.refs_8_ = bf16[1,256,512]{2,1,0:T(8,128)(2,1)S(1)} custom-call(f32[56,256]{1,0:T(8,128)S(1)} %get-tuple-element.25.refs_0_), custom_call_target="tpu_custom_call" | custom-call | flops 134217728 | bytes 262144 | tf_op jit(solution)/shard_map/pallas_call | solution.py:400
  7.8 0.0 collective-permute-done.refs_0_.refs_1_
  7.8 1.2 %shard_map.48.refs_5_.refs_9_ = bf16[1,256,512]{2,1,0:T(8,128)(2,1)S(1)} custom-call(f32[56,256]{1,0:T(8,128)S(1)} %collective-permute-done.refs_0_.refs_1_), custom_call_target="tpu_custom_call" | custom-call | flops 134217728 | bytes 262144 | tf_op jit(solution)/shard_map/pallas_call | solution.py:400
  9.0 0.0 collective-permute-done.1.refs_2_.refs_0_
  9.0 1.3 %collective-permute-done.2.refs_3_.refs_1_ = f32[56,256]{1,0:T(8,128)S(1)} collective-permute-done((f32[56,256]{1,0:T(8,128)S(1)}, f32[56,256]{1,0:T(8,128)S(1)}, u32[]{:S(2)}, u32[]{:S(2)}) %collective-permute-start.2) | collective-permute-done | bytes 57376 | tf_op jit(solution)/shard_map/ppermute | solution.py:333
  10.3 3.7 %collective-permute-start.5 = (f32[72,256]{1,0:T(8,128)S(1)}, f32[72,256]{1,0:T(8,128)S(1)}, u32[]{:S(2)}, u32[]{:S(2)}) collective-permute-start(f32[72,256]{1,0:T(8,128)S(1)} %shard_map.49.own.one.after.refs_0_), channel_id=1, source_target_pairs={{0,12},{1,13},{2,14},{3,15},{4,8},{5,9},{6,10},{7,11},{8,4},{9,5},... | collective-permute-start | bytes 221192 | tf_op jit(solution)/shard_map/ppermute | solution.py:338
  14.0 0.0 collective-permute-start.4
  14.0 0.8 %collective-permute-start.3 = (f32[72,256]{1,0:T(8,128)S(1)}, f32[72,256]{1,0:T(8,128)S(1)}, u32[]{:S(2)}, u32[]{:S(2)}) collective-permute-start(f32[72,256]{1,0:T(8,128)S(1)} %shard_map.49.own.one.after.refs_0_), channel_id=1, source_target_pairs={{0,4},{1,5},{2,6},{3,7},{4,0},{5,1},{6,2},{7,3},{8,12},{9,13},{10,... | collective-permute-start | bytes 221192 | tf_op jit(solution)/shard_map/ppermute | solution.py:338
  14.8 0.3 shard_map.50.after.refs_4_
  15.1 2.1 %shard_map.54.refs_10_ = bf16[2,256,512]{2,1,0:T(8,128)(2,1)S(1)} custom-call(f32[56,256]{1,0:T(8,128)S(1)} %collective-permute-done.1.refs_2_.refs_0_, f32[56,256]{1,0:T(8,128)S(1)} %collective-permute-done.2.refs_3_.refs_1_), custom_call_target="tpu_custom_call" | custom-call | flops 268435456 | bytes 262144 | tf_op jit(solution)/shard_map/pallas_call | solution.py:400
  17.2 0.0 collective-permute-done.5.one.refs_3_
  17.2 0.3 shard_map.51.after.refs_7_
  17.5 3.0 %collective-permute-done.4.one.refs_2_ = f32[72,256]{1,0:T(8,128)S(1)} collective-permute-done((f32[72,256]{1,0:T(8,128)S(1)}, f32[72,256]{1,0:T(8,128)S(1)}, u32[]{:S(2)}, u32[]{:S(2)}) %collective-permute-start.4) | collective-permute-done | bytes 73760 | tf_op jit(solution)/shard_map/ppermute | solution.py:338
  20.5 0.3 shard_map.52.after.refs_6_
  20.8 0.0 collective-permute-done.3.one.refs_1_
  20.8 0.3 shard_map.53.refs_5_
  21.2 1.0 %shard_map.55 = (f32[64,256]{1,0:T(8,128)S(1)}, f32[64,256]{1,0:T(8,128)S(1)}, f32[2,8,512]{2,1,0:T(8,128)S(1)}) custom-call(f32[72,256]{1,0:T(8,128)S(1)} %shard_map.49.own.one.after.refs_0_, f32[72,256]{1,0:T(8,128)S(1)} %collective-permute-done.3.one.refs_1_, f32[72,256]{1,0:T(8,128)S(1)} %collective-permute-done.4.one.refs_2_, ...), custom_call_target="tpu_custom_call" | custom-call | flops 134217728 | bytes 262144 | tf_op jit(solution)/shard_map/pallas_call | solution.py:443
  22.2 2.5 %collective-permute-start.8 = (f32[64,256]{1,0:T(8,128)S(1)}, f32[64,256]{1,0:T(8,128)S(1)}, u32[]{:S(2)}, u32[]{:S(2)}) collective-permute-start(f32[64,256]{1,0:T(8,128)S(1)} %get-tuple-element.29.refs_0_), channel_id=1, source_target_pairs={{0,12},{1,13},{2,14},{3,15},{4,8},{5,9},{6,10},{7,11},{8,4},{9,5},... | collective-permute-start | bytes 196616 | tf_op jit(solution)/shard_map/ppermute | solution.py:338
  24.7 0.0 collective-permute-start.7
  24.7 1.9 %collective-permute-start.6 = (f32[64,256]{1,0:T(8,128)S(1)}, f32[64,256]{1,0:T(8,128)S(1)}, u32[]{:S(2)}, u32[]{:S(2)}) collective-permute-start(f32[64,256]{1,0:T(8,128)S(1)} %get-tuple-element.29.refs_0_), channel_id=1, source_target_pairs={{0,4},{1,5},{2,6},{3,7},{4,0},{5,1},{6,2},{7,3},{8,12},{9,13},{10,... | collective-permute-start | bytes 196616 | tf_op jit(solution)/shard_map/ppermute | solution.py:338
  26.6 1.3 %shard_map.56 = (bf16[256,8192]{1,0:T(8,128)(2,1)S(1)}, bf16[256,8192]{1,0:T(8,128)(2,1)S(1)}, f32[16,256]{1,0:T(8,128)S(1)}, f32[16,256]{1,0:T(8,128)S(1)}, f32...) custom-call(s32[64,128]{1,0:T(8,128)S(1)} %get-tuple-element.31.mask_ids.refs_5_, f32[64,256]{1,0:T(8,128)S(1)} %get-tuple-element.32.mean), custom_call_target="tpu_custom_call" | custom-call | flops 536870912 | bytes 8388608 | tf_op jit(solution)/shard_map/pallas_call | solution.py:457
  27.9 0.1 collective-permute-start.12
  28.0 1.3 %collective-permute-start.13 = (f32[16,256]{1,0:T(8,128)S(1)}, f32[16,256]{1,0:T(8,128)S(1)}, u32[]{:S(2)}, u32[]{:S(2)}) collective-permute-start(f32[16,256]{1,0:T(8,128)S(1)} %get-tuple-element.40), channel_id=1, source_target_pairs={{0,2},{1,3},{2,0},{3,1},{4,6},{5,7},{6,4},{7,5},{8,10},{9,11},{10,... | collective-permute-start | bytes 49160 | tf_op jit(solution)/shard_map/ppermute | solution.py:333
  29.3 0.0 collective-permute-done.8.refs_3_
  29.3 0.5 %collective-permute-start.14 = (f32[16,256]{1,0:T(8,128)S(1)}, f32[16,256]{1,0:T(8,128)S(1)}, u32[]{:S(2)}, u32[]{:S(2)}) collective-permute-start(f32[16,256]{1,0:T(8,128)S(1)} %get-tuple-element.41), channel_id=1, source_target_pairs={{0,3},{1,2},{2,1},{3,0},{4,7},{5,6},{6,5},{7,4},{8,11},{9,10},{10,... | collective-permute-start | bytes 49160 | tf_op jit(solution)/shard_map/ppermute | solution.py:333
  29.8 1.0 %collective-permute-done.7.refs_2_ = f32[64,256]{1,0:T(8,128)S(1)} collective-permute-done((f32[64,256]{1,0:T(8,128)S(1)}, f32[64,256]{1,0:T(8,128)S(1)}, u32[]{:S(2)}, u32[]{:S(2)}) %collective-permute-start.7) | collective-permute-done | bytes 65568 | tf_op jit(solution)/shard_map/ppermute | solution.py:338
  30.8 0.0 collective-permute-done.6.refs_1_
  30.8 0.8 %shard_map.57 = (f32[16,256]{1,0:T(8,128)S(1)}, f32[16,256]{1,0:T(8,128)S(1)}, f32[16,256]{1,0:T(8,128)S(1)}, f32[16,256]{1,0:T(8,128)S(1)}) custom-call(f32[64,256]{1,0:T(8,128)S(1)} %get-tuple-element.29.refs_0_, f32[64,256]{1,0:T(8,128)S(1)} %collective-permute-done.6.refs_1_, f32[64,256]{1,0:T(8,128)S(1)} %collective-permute-done.7.refs_2_, ...), custom_call_target="tpu_custom_call" | custom-call | flops 134217728 | bytes 262144 | tf_op jit(solution)/shard_map/pallas_call | solution.py:468
  31.6 0.0 collective-permute-start.9
  31.6 1.3 %collective-permute-start.10 = (f32[16,256]{1,0:T(8,128)S(1)}, f32[16,256]{1,0:T(8,128)S(1)}, u32[]{:S(2)}, u32[]{:S(2)}) collective-permute-start(f32[16,256]{1,0:T(8,128)S(1)} %get-tuple-element.36), channel_id=1, source_target_pairs={{0,2},{1,3},{2,0},{3,1},{4,6},{5,7},{6,4},{7,5},{8,10},{9,11},{10,... | collective-permute-start | bytes 49160 | tf_op jit(solution)/shard_map/ppermute | solution.py:333
  32.9 0.0 collective-permute-done.12.refs_1_
  32.9 0.6 %collective-permute-start.11 = (f32[16,256]{1,0:T(8,128)S(1)}, f32[16,256]{1,0:T(8,128)S(1)}, u32[]{:S(2)}, u32[]{:S(2)}) collective-permute-start(f32[16,256]{1,0:T(8,128)S(1)} %get-tuple-element.37), channel_id=1, source_target_pairs={{0,3},{1,2},{2,1},{3,0},{4,7},{5,6},{6,5},{7,4},{8,11},{9,10},{10,... | collective-permute-start | bytes 49160 | tf_op jit(solution)/shard_map/ppermute | solution.py:333
  33.5 0.0 collective-permute-done.13.refs_2_
  33.5 0.0 collective-permute-done.14.refs_3_
  33.5 1.3 %shard_map.58.refs_4_ = f32[64,8192]{1,0:T(8,128)S(1)} custom-call(f32[16,256]{1,0:T(8,128)S(1)} %get-tuple-element.38.refs_0_, f32[16,256]{1,0:T(8,128)S(1)} %collective-permute-done.12.refs_1_, f32[16,256]{1,0:T(8,128)S(1)} %collective-permute-done.13.refs_2_, f32[16,256]{1,0:T(8,128)S(1)} %collective-permute-done.14.refs_3_, ...), custom_call_target="tpu_custom_call" | custom-call | flops 536870912 | bytes 4194304 | tf_op jit(solution)/shard_map/pallas_call | solution.py:478
  34.8 0.0 collective-permute-done.9.refs_1_
  34.8 0.5 %collective-permute-done.10.refs_2_ = f32[16,256]{1,0:T(8,128)S(1)} collective-permute-done((f32[16,256]{1,0:T(8,128)S(1)}, f32[16,256]{1,0:T(8,128)S(1)}, u32[]{:S(2)}, u32[]{:S(2)}) %collective-permute-start.10) | collective-permute-done | bytes 16416 | tf_op jit(solution)/shard_map/ppermute | solution.py:333
  35.4 0.7 %collective-permute-done.11.refs_3_ = f32[16,256]{1,0:T(8,128)S(1)} collective-permute-done((f32[16,256]{1,0:T(8,128)S(1)}, f32[16,256]{1,0:T(8,128)S(1)}, u32[]{:S(2)}, u32[]{:S(2)}) %collective-permute-start.11) | collective-permute-done | bytes 16416 | tf_op jit(solution)/shard_map/ppermute | solution.py:333
  36.1 1.7 %shard_map.59 = f32[64,8192]{1,0:T(8,128)} custom-call(f32[16,256]{1,0:T(8,128)S(1)} %get-tuple-element.34.refs_0_, f32[16,256]{1,0:T(8,128)S(1)} %collective-permute-done.9.refs_1_, f32[16,256]{1,0:T(8,128)S(1)} %collective-permute-done.10.refs_2_, f32[16,256]{1,0:T(8,128)S(1)} %collective-permute-done.11.refs_3_, f32[64,8192]{1,0:T(8,128)S(1)} %shard_map.58.refs_4_, ...), custom_call_target="tpu_custom_call" | custom-call | flops 536870912 | bytes 4194304 | tf_op jit(solution)/shard_map/pallas_call | solution.py:487
  (1 shorter events, 0.0 us)
Async XLA Ops:
  3.3 4.4 %collective-permute-start = (f32[56,256]{1,0:T(8,128)S(1)}, f32[56,256]{1,0:T(8,128)S(1)}, u32[]{:S(2)}, u32[]{:S(2)}) collective-permute-start(f32[56,256]{1,0:T(8,128)S(1)} %get-tuple-element.26), channel_id=1, source_target_pairs={{0,1},{1,0},{2,3},{3,2},{4,5},{5,4},{6,7},{7,6},{8,9},{9,8},{10,11... | collective-permute-start | bytes 172040 | tf_op jit(solution)/shard_map/ppermute | solution.py:333
  3.9 5.1 %collective-permute-start.1 = (f32[56,256]{1,0:T(8,128)S(1)}, f32[56,256]{1,0:T(8,128)S(1)}, u32[]{:S(2)}, u32[]{:S(2)}) collective-permute-start(f32[56,256]{1,0:T(8,128)S(1)} %get-tuple-element.27), channel_id=1, source_target_pairs={{0,2},{1,3},{2,0},{3,1},{4,6},{5,7},{6,4},{7,5},{8,10},{9,11},{10,... | collective-permute-start | bytes 172040 | tf_op jit(solution)/shard_map/ppermute | solution.py:333
  6.5 3.9 %collective-permute-start.2 = (f32[56,256]{1,0:T(8,128)S(1)}, f32[56,256]{1,0:T(8,128)S(1)}, u32[]{:S(2)}, u32[]{:S(2)}) collective-permute-start(f32[56,256]{1,0:T(8,128)S(1)} %get-tuple-element.28), channel_id=1, source_target_pairs={{0,3},{1,2},{2,1},{3,0},{4,7},{5,6},{6,5},{7,4},{8,11},{9,10},{10,... | collective-permute-start | bytes 172040 | tf_op jit(solution)/shard_map/ppermute | solution.py:333
  10.3 6.9 %collective-permute-start.5 = (f32[72,256]{1,0:T(8,128)S(1)}, f32[72,256]{1,0:T(8,128)S(1)}, u32[]{:S(2)}, u32[]{:S(2)}) collective-permute-start(f32[72,256]{1,0:T(8,128)S(1)} %shard_map.49.own.one.after.refs_0_), channel_id=1, source_target_pairs={{0,12},{1,13},{2,14},{3,15},{4,8},{5,9},{6,10},{7,11},{8,4},{9,5},... | collective-permute-start | bytes 221192 | tf_op jit(solution)/shard_map/ppermute | solution.py:338
  14.0 6.5 %collective-permute-start.4 = (f32[72,256]{1,0:T(8,128)S(1)}, f32[72,256]{1,0:T(8,128)S(1)}, u32[]{:S(2)}, u32[]{:S(2)}) collective-permute-start(f32[72,256]{1,0:T(8,128)S(1)} %shard_map.49.own.one.after.refs_0_), channel_id=1, source_target_pairs={{0,8},{1,9},{2,10},{3,11},{4,12},{5,13},{6,14},{7,15},{8,0},{9,1},... | collective-permute-start | bytes 221192 | tf_op jit(solution)/shard_map/ppermute | solution.py:338
  14.0 6.8 %collective-permute-start.3 = (f32[72,256]{1,0:T(8,128)S(1)}, f32[72,256]{1,0:T(8,128)S(1)}, u32[]{:S(2)}, u32[]{:S(2)}) collective-permute-start(f32[72,256]{1,0:T(8,128)S(1)} %shard_map.49.own.one.after.refs_0_), channel_id=1, source_target_pairs={{0,4},{1,5},{2,6},{3,7},{4,0},{5,1},{6,2},{7,3},{8,12},{9,13},{10,... | collective-permute-start | bytes 221192 | tf_op jit(solution)/shard_map/ppermute | solution.py:338
  22.2 7.1 %collective-permute-start.8 = (f32[64,256]{1,0:T(8,128)S(1)}, f32[64,256]{1,0:T(8,128)S(1)}, u32[]{:S(2)}, u32[]{:S(2)}) collective-permute-start(f32[64,256]{1,0:T(8,128)S(1)} %get-tuple-element.29.refs_0_), channel_id=1, source_target_pairs={{0,12},{1,13},{2,14},{3,15},{4,8},{5,9},{6,10},{7,11},{8,4},{9,5},... | collective-permute-start | bytes 196616 | tf_op jit(solution)/shard_map/ppermute | solution.py:338
  24.7 6.2 %collective-permute-start.7 = (f32[64,256]{1,0:T(8,128)S(1)}, f32[64,256]{1,0:T(8,128)S(1)}, u32[]{:S(2)}, u32[]{:S(2)}) collective-permute-start(f32[64,256]{1,0:T(8,128)S(1)} %get-tuple-element.29.refs_0_), channel_id=1, source_target_pairs={{0,8},{1,9},{2,10},{3,11},{4,12},{5,13},{6,14},{7,15},{8,0},{9,1},... | collective-permute-start | bytes 196616 | tf_op jit(solution)/shard_map/ppermute | solution.py:338
  24.7 6.2 %collective-permute-start.6 = (f32[64,256]{1,0:T(8,128)S(1)}, f32[64,256]{1,0:T(8,128)S(1)}, u32[]{:S(2)}, u32[]{:S(2)}) collective-permute-start(f32[64,256]{1,0:T(8,128)S(1)} %get-tuple-element.29.refs_0_), channel_id=1, source_target_pairs={{0,4},{1,5},{2,6},{3,7},{4,0},{5,1},{6,2},{7,3},{8,12},{9,13},{10,... | collective-permute-start | bytes 196616 | tf_op jit(solution)/shard_map/ppermute | solution.py:338
  27.9 5.0 %collective-permute-start.12 = (f32[16,256]{1,0:T(8,128)S(1)}, f32[16,256]{1,0:T(8,128)S(1)}, u32[]{:S(2)}, u32[]{:S(2)}) collective-permute-start(f32[16,256]{1,0:T(8,128)S(1)} %get-tuple-element.39), channel_id=1, source_target_pairs={{0,1},{1,0},{2,3},{3,2},{4,5},{5,4},{6,7},{7,6},{8,9},{9,8},{10,11... | collective-permute-start | bytes 49160 | tf_op jit(solution)/shard_map/ppermute | solution.py:333
  28.0 5.5 %collective-permute-start.13 = (f32[16,256]{1,0:T(8,128)S(1)}, f32[16,256]{1,0:T(8,128)S(1)}, u32[]{:S(2)}, u32[]{:S(2)}) collective-permute-start(f32[16,256]{1,0:T(8,128)S(1)} %get-tuple-element.40), channel_id=1, source_target_pairs={{0,2},{1,3},{2,0},{3,1},{4,6},{5,7},{6,4},{7,5},{8,10},{9,11},{10,... | collective-permute-start | bytes 49160 | tf_op jit(solution)/shard_map/ppermute | solution.py:333
  29.3 4.2 %collective-permute-start.14 = (f32[16,256]{1,0:T(8,128)S(1)}, f32[16,256]{1,0:T(8,128)S(1)}, u32[]{:S(2)}, u32[]{:S(2)}) collective-permute-start(f32[16,256]{1,0:T(8,128)S(1)} %get-tuple-element.41), channel_id=1, source_target_pairs={{0,3},{1,2},{2,1},{3,0},{4,7},{5,6},{6,5},{7,4},{8,11},{9,10},{10,... | collective-permute-start | bytes 49160 | tf_op jit(solution)/shard_map/ppermute | solution.py:333
  31.6 3.2 %collective-permute-start.9 = (f32[16,256]{1,0:T(8,128)S(1)}, f32[16,256]{1,0:T(8,128)S(1)}, u32[]{:S(2)}, u32[]{:S(2)}) collective-permute-start(f32[16,256]{1,0:T(8,128)S(1)} %get-tuple-element.35), channel_id=1, source_target_pairs={{0,1},{1,0},{2,3},{3,2},{4,5},{5,4},{6,7},{7,6},{8,9},{9,8},{10,11... | collective-permute-start | bytes 49160 | tf_op jit(solution)/shard_map/ppermute | solution.py:333
  31.6 3.8 %collective-permute-start.10 = (f32[16,256]{1,0:T(8,128)S(1)}, f32[16,256]{1,0:T(8,128)S(1)}, u32[]{:S(2)}, u32[]{:S(2)}) collective-permute-start(f32[16,256]{1,0:T(8,128)S(1)} %get-tuple-element.36), channel_id=1, source_target_pairs={{0,2},{1,3},{2,0},{3,1},{4,6},{5,7},{6,4},{7,5},{8,10},{9,11},{10,... | collective-permute-start | bytes 49160 | tf_op jit(solution)/shard_map/ppermute | solution.py:333
  32.9 3.2 %collective-permute-start.11 = (f32[16,256]{1,0:T(8,128)S(1)}, f32[16,256]{1,0:T(8,128)S(1)}, u32[]{:S(2)}, u32[]{:S(2)}) collective-permute-start(f32[16,256]{1,0:T(8,128)S(1)} %get-tuple-element.37), channel_id=1, source_target_pairs={{0,3},{1,2},{2,1},{3,0},{4,7},{5,6},{6,5},{7,4},{8,11},{9,10},{10,... | collective-permute-start | bytes 49160 | tf_op jit(solution)/shard_map/ppermute | solution.py:333

commit v21 on v20

--- a/solution.py
+++ b/solution.py
@@ -125,13 +125,14 @@
     across = slots // LANES
     rows = ids.shape[0] // across
     masked = jnp.concatenate([masked[k * rows : (k + 1) * rows] for k in range(across)], axis=1).astype(F32)
-    for send in sends:
+    for send in sends[:3]:
         send[part + 8 :] = masked
 
     table = same_worker(pad, 256)
-    wait_all(copies)
     total = None
     for b in range(len(copies)):
+        if b % 4 == 0:
+            wait_all(copies[b : b + 4])
         ok = row(valid, b, BLOCK)
         x0 = x[:, b * BLOCK : (b + 1) * BLOCK] * ok
         rest = x0 - by_worker(x0, table) * row(weight, b, BLOCK)
@@ -218,7 +219,9 @@
         lax.fori_loop(0, tiles, lambda t, c: (do(t, pl.ds(pl.multiple_of(t * LANES, LANES), LANES)), c)[1], 0)
 
 
-def firms_kernel(part, own, one, after, out):
+def firms_kernel(part, own, one, passed, out, *copy):
+    for ref in copy:
+        ref[...] = passed[...]
     each_tile(own.shape[1], lambda t, at: out.__setitem__(t, same_firm(own, one, part, at)))
 
 
@@ -232,13 +235,19 @@
         out[part * k : part * (k + 1), at] = means[:, k * LANES : (k + 1) * LANES]
 
 
-def change_kernel(far, part, *refs):
-    parts, tables, pairs, (mean, sums, scale) = refs[:far], refs[far:-6], refs[-6:-3], refs[-3:]
-    pairs = [(group, k) for group in pairs for k in range(group.shape[0])]
+def change_kernel(far, part, ready, *refs):
+    tables, pairs, refs = refs[far : far + ready], refs[far + ready : far + ready + NEAR], refs
+    parts, (mean, sums, scale), made = refs[:far], refs[far + ready + NEAR :][:3], refs[far + ready + NEAR + 3 :]
     slots = mean.shape[1]
 
     def tile(t, at):
-        same = [table[t] for table in tables] or [same_firm(parts[0], one, part, at) for one in parts]
+        if tables:
+            between = [same_firm(parts[0], one, part, at) for one in parts[1:-1]]
+            for ref, one in zip(made, between):
+                ref[t] = one
+            same = [tables[0][t], *between, tables[1][t]]
+        else:
+            same = [same_firm(parts[0], one, part, at) for one in parts]
         same = jnp.concatenate(same, axis=0)
         count = [one[part * NEAR + 2 * k + 1 : part * NEAR + 2 * k + 2, at] for one in parts for k in range(NEAR)]
         count = jnp.concatenate(count, axis=1)
@@ -254,7 +263,7 @@
     for k in range(NEAR):
         cut = slice(part * k, part * (k + 1))
         both = jnp.concatenate(split(mean[cut]), axis=0)
-        change = dot(both, pairs[k][0][pairs[k][1]])
+        change = dot(both, pairs[k][0])
         change = change[:part] + change[part:]
         sums[cut] = parts[0][cut] + (change[:, :slots] + change[:, slots:])
 
@@ -379,7 +388,7 @@
 
     *sends, x1, mask_ids, weight = call(
         functools.partial(sums_kernel, pad, slots // n),
-        [message] * NEAR + [array(whole, F32), array(of_rows, jnp.int32), array(of_rows, F32)],
+        [message] * 3 + [array((about, slots), F32), array(whole, F32), array(of_rows, jnp.int32), array(of_rows, F32)],
         [hbm] * 4,
         [vmem] * (NEAR + 3),
         [
@@ -423,34 +432,38 @@
         message.size * 8,
     )(*arrived, *pairs)
     shared = far_share(joined, n)
-    pairs.append(pair_counts(arrived[2:]))
-    tables = []
+    tables, passed = [], arrived[2]
+    table = array((tiles, NEAR * LANES, NEAR * LANES), BF16)
+
+    def firm_table(one, passed, out):
+        return call(
+            functools.partial(firms_kernel, part),
+            out,
+            [vmem] * 3,
+            [vmem] * len(out),
+            [],
+            work // 64,
+            tiles * (NEAR * LANES) ** 2 * 2,
+        )(joined, one, passed)
+
     if keep:
-        after = joined
-        for one in [shared[0]] + shared[:0:-1]:
-            after = call(
-                functools.partial(firms_kernel, part),
-                array((tiles, NEAR * LANES, NEAR * LANES), BF16),
-                [vmem] * 3,
-                vmem,
-                [],
-                work // 64,
-                tiles * (NEAR * LANES) ** 2 * 2,
-            )(joined, one, after)
-            tables.append(after)
-        tables = tables[:1] + tables[:0:-1]
+        first_table, passed = firm_table(joined, passed, [table, message])
+        tables = [first_table, *firm_table(shared[-1], first_table, [table])]
+    passed = lax.ppermute(passed, "rows", [(i, i ^ 1) for i in range(n)])
+    pairs += [pair_counts(arrived[2:3]), pair_counts([passed])]
     scale = array((tiles, 8, NEAR * LANES), F32)
-    mean, sums, scales = call(
-        functools.partial(change_kernel, far, part),
-        [of_near, of_near, scale],
+    made = [table] * (far - 2) * keep
+    mean, sums, scales, *made = call(
+        functools.partial(change_kernel, far, part, len(tables)),
+        [of_near, of_near, scale, *made],
         [vmem] * (far + len(tables) + len(pairs)),
-        [vmem] * 3,
+        [vmem] * (3 + len(made)),
         [],
         work // 4,
         slots * slots * 4,
     )(*shared, *tables, *pairs)
     again = far_share(sums, n)
-    source = tables if keep else shared
+    source = [tables[0], *made, tables[1]] if keep else shared
     spreads = []
     sends = [mean[part * k : part * (k + 1)] for k in range(NEAR)]
     if keep:

time: 37.9 us -> 37.3 us (0.984)
  waiting for transfers between devices: 6.57 us -> 5.61 us
    ppermute x9, waiting for transfers between devices: 2.58 us -> 1.93 us  [near_exchange(): lax.ppermute(one, 'rows', step)]
    pallas_call x3 -> x4, Pallas kernels: 4.55 us -> 4.91 us  [pair_counts(): call(functools.partial(pairs_kernel, pad, about), array((len(parts), slot...]
    pallas_call x6 -> x4, Pallas kernels: 5.61 us -> 5.48 us  [the longest x1 3.5 us: body(): call(functools.partial(sums_kernel, pad, slots // n), [message] * 3 + [ar...]
  transfers between devices with their start and end apart: 15 -> 16, of which waited for: 5 -> 5; matrix products, arithmetic and copies ran while one was open for 0% -> 0% of each run, Pallas kernels for 23% -> 24%
where the time goes in v21:
time: 37.3 us; the launch traced here: 37.1 us
  starting transfers between devices  15.9 us (43%)
  Pallas kernels  15.5 us (42%)
  waiting for transfers between devices  5.61 us (15%)
    ppermute x6, starting transfers between devices, far_share(): return [one] + [lax.ppermute(one, 'rows', step) for step in steps]  8.85 us
    ppermute x9, starting transfers between devices, near_exchange(): lax.ppermute(one, 'rows', step)  6.99 us
    pallas_call x4, Pallas kernels, pair_counts(): call(functools.partial(pairs_kernel, pad, about), array((len(parts), slot...  4.91 us
    ppermute x6, waiting for transfers between devices, far_share(): return [one] + [lax.ppermute(one, 'rows', step) for step in steps]  3.67 us
    pallas_call x1, Pallas kernels, body(): call(functools.partial(sums_kernel, pad, slots // n), [message] * 3 + [ar...  3.5 us
    ppermute x9, waiting for transfers between devices, near_exchange(): lax.ppermute(one, 'rows', step)  1.93 us
    pallas_call x1, Pallas kernels, body(): call(last_kernel, array(whole, F32), [vmem] * (NEAR + 2 + len(spreads[:1]...  1.69 us
    pallas_call x1, Pallas kernels, body(): call(functools.partial(change_kernel, far, part, len(tables)), [of_near,...  1.37 us
  transfers between devices with their start and end apart: 16, of which 5 were waited for; matrix products, arithmetic and copies ran while one was open for 0% of the time, Pallas kernels for 24%

profile of v21, /device:TPU:0, one launch (start us, length us, event | category | flops | bytes accessed | tf_op | source)
XLA Modules:
  0.0 37.1 jit_solution(15742349086793618248)
XLA Ops:
  0.0 3.5 %shard_map.46 = (f32[56,256]{1,0:T(8,128)S(1)}, f32[56,256]{1,0:T(8,128)S(1)}, f32[56,256]{1,0:T(8,128)S(1)}, f32[24,256]{1,0:T(8,128)S(1)}, f32[64,8192]{1,0:T(...) custom-call(f32[64,8192]{1,0:T(8,128)} %refs_0_.1, s32[8,128]{1,0:T(8,128)} %bitcast.4, s32[64,128]{1,0:T(8,128)} %bitcast.3, ...), custom_call_target="tpu_custom_call" | custom-call | flops 1073741824 | bytes 2097152 | tf_op jit(solution)/shard_map/pallas_call | solution.py:389
  3.5 0.5 %collective-permute-start = (f32[56,256]{1,0:T(8,128)S(1)}, f32[56,256]{1,0:T(8,128)S(1)}, u32[]{:S(2)}, u32[]{:S(2)}) collective-permute-start(f32[56,256]{1,0:T(8,128)S(1)} %get-tuple-element.30), channel_id=1, source_target_pairs={{0,1},{1,0},{2,3},{3,2},{4,5},{5,4},{6,7},{7,6},{8,9},{9,8},{10,11... | collective-permute-start | bytes 172040 | tf_op jit(solution)/shard_map/ppermute | solution.py:342
  4.0 2.6 %collective-permute-start.1 = (f32[56,256]{1,0:T(8,128)S(1)}, f32[56,256]{1,0:T(8,128)S(1)}, u32[]{:S(2)}, u32[]{:S(2)}) collective-permute-start(f32[56,256]{1,0:T(8,128)S(1)} %get-tuple-element.31), channel_id=1, source_target_pairs={{0,2},{1,3},{2,0},{3,1},{4,6},{5,7},{6,4},{7,5},{8,10},{9,11},{10,... | collective-permute-start | bytes 172040 | tf_op jit(solution)/shard_map/ppermute | solution.py:342
  6.6 0.1 collective-permute-start.2
  6.7 1.2 %shard_map.47.refs_4_.refs_6_ = bf16[1,256,512]{2,1,0:T(8,128)(2,1)S(1)} custom-call(f32[56,256]{1,0:T(8,128)S(1)} %get-tuple-element.29.refs_0_), custom_call_target="tpu_custom_call" | custom-call | flops 134217728 | bytes 262144 | tf_op jit(solution)/shard_map/pallas_call | solution.py:409
  7.9 0.0 collective-permute-done.refs_0_.refs_1_
  7.9 1.2 %shard_map.48.refs_5_.refs_7_ = bf16[1,256,512]{2,1,0:T(8,128)(2,1)S(1)} custom-call(f32[56,256]{1,0:T(8,128)S(1)} %collective-permute-done.refs_0_.refs_1_), custom_call_target="tpu_custom_call" | custom-call | flops 134217728 | bytes 262144 | tf_op jit(solution)/shard_map/pallas_call | solution.py:409
  9.2 0.7 %collective-permute-done.2.refs_3_ = f32[24,256]{1,0:T(8,128)S(1)} collective-permute-done((f32[24,256]{1,0:T(8,128)S(1)}, f32[24,256]{1,0:T(8,128)S(1)}, u32[]{:S(2)}, u32[]{:S(2)}) %collective-permute-start.2) | collective-permute-done | bytes 24608 | tf_op jit(solution)/shard_map/ppermute | solution.py:342
  9.9 0.0 collective-permute-done.1.refs_2_.passed.refs_0_
  9.9 3.7 %collective-permute-start.5 = (f32[72,256]{1,0:T(8,128)S(1)}, f32[72,256]{1,0:T(8,128)S(1)}, u32[]{:S(2)}, u32[]{:S(2)}) collective-permute-start(f32[72,256]{1,0:T(8,128)S(1)} %shard_map.49.own.one.refs_0_), channel_id=1, source_target_pairs={{0,12},{1,13},{2,14},{3,15},{4,8},{5,9},{6,10},{7,11},{8,4},{9,5},... | collective-permute-start | bytes 221192 | tf_op jit(solution)/shard_map/ppermute | solution.py:347
  13.6 0.0 collective-permute-start.4
  13.6 0.8 %collective-permute-start.3 = (f32[72,256]{1,0:T(8,128)S(1)}, f32[72,256]{1,0:T(8,128)S(1)}, u32[]{:S(2)}, u32[]{:S(2)}) collective-permute-start(f32[72,256]{1,0:T(8,128)S(1)} %shard_map.49.own.one.refs_0_), channel_id=1, source_target_pairs={{0,4},{1,5},{2,6},{3,7},{4,0},{5,1},{6,2},{7,3},{8,12},{9,13},{10,... | collective-permute-start | bytes 221192 | tf_op jit(solution)/shard_map/ppermute | solution.py:347
  14.3 0.3 shard_map.50
  14.7 0.1 collective-permute-start.6
  14.7 1.2 %shard_map.52.refs_8_ = bf16[1,256,512]{2,1,0:T(8,128)(2,1)S(1)} custom-call(f32[56,256]{1,0:T(8,128)S(1)} %collective-permute-done.1.refs_2_.passed.refs_0_), custom_call_target="tpu_custom_call" | custom-call | flops 134217728 | bytes 262144 | tf_op jit(solution)/shard_map/pallas_call | solution.py:409
  16.0 0.0 collective-permute-done.6.refs_0_
  16.0 1.2 %shard_map.53.refs_9_ = bf16[1,256,512]{2,1,0:T(8,128)(2,1)S(1)} custom-call(f32[56,256]{1,0:T(8,128)S(1)} %collective-permute-done.6.refs_0_), custom_call_target="tpu_custom_call" | custom-call | flops 134217728 | bytes 262144 | tf_op jit(solution)/shard_map/pallas_call | solution.py:409
  17.2 0.0 collective-permute-done.5.one.refs_3_
  17.2 0.3 shard_map.51.refs_5_.refs_7_
  17.5 2.5 %collective-permute-done.4.refs_2_ = f32[72,256]{1,0:T(8,128)S(1)} collective-permute-done((f32[72,256]{1,0:T(8,128)S(1)}, f32[72,256]{1,0:T(8,128)S(1)}, u32[]{:S(2)}, u32[]{:S(2)}) %collective-permute-start.4) | collective-permute-done | bytes 73760 | tf_op jit(solution)/shard_map/ppermute | solution.py:347
  20.1 0.0 collective-permute-done.3.refs_1_
  20.1 1.4 %shard_map.54 = (f32[64,256]{1,0:T(8,128)S(1)}, f32[64,256]{1,0:T(8,128)S(1)}, f32[2,8,512]{2,1,0:T(8,128)S(1)}, bf16[2,512,512]{2,1,0:T(8,128)(2,1)S(1)}, bf16[2,512,512]{2,1,0:T(8,128)(2,1)S(1)}) custom-call(f32[72,256]{1,0:T(8,128)S(1)} %shard_map.49.own.one.refs_0_, f32[72,256]{1,0:T(8,128)S(1)} %collective-permute-done.3.refs_1_, ...), custom_call_target="tpu_custom_call" | custom-call | flops 134217728 | bytes 262144 | tf_op jit(solution)/shard_map/pallas_call | solution.py:456
  21.4 2.5 %collective-permute-start.9 = (f32[64,256]{1,0:T(8,128)S(1)}, f32[64,256]{1,0:T(8,128)S(1)}, u32[]{:S(2)}, u32[]{:S(2)}) collective-permute-start(f32[64,256]{1,0:T(8,128)S(1)} %get-tuple-element.35.refs_0_), channel_id=1, source_target_pairs={{0,12},{1,13},{2,14},{3,15},{4,8},{5,9},{6,10},{7,11},{8,4},{9,5},... | collective-permute-start | bytes 196616 | tf_op jit(solution)/shard_map/ppermute | solution.py:347
  23.9 0.0 collective-permute-start.8
  23.9 1.9 %collective-permute-start.7 = (f32[64,256]{1,0:T(8,128)S(1)}, f32[64,256]{1,0:T(8,128)S(1)}, u32[]{:S(2)}, u32[]{:S(2)}) collective-permute-start(f32[64,256]{1,0:T(8,128)S(1)} %get-tuple-element.35.refs_0_), channel_id=1, source_target_pairs={{0,4},{1,5},{2,6},{3,7},{4,0},{5,1},{6,2},{7,3},{8,12},{9,13},{10,... | collective-permute-start | bytes 196616 | tf_op jit(solution)/shard_map/ppermute | solution.py:347
  25.8 1.3 %shard_map.55 = (bf16[256,8192]{1,0:T(8,128)(2,1)S(1)}, bf16[256,8192]{1,0:T(8,128)(2,1)S(1)}, f32[16,256]{1,0:T(8,128)S(1)}, f32[16,256]{1,0:T(8,128)S(1)}, f32...) custom-call(s32[64,128]{1,0:T(8,128)S(1)} %get-tuple-element.39.mask_ids.refs_5_, f32[64,256]{1,0:T(8,128)S(1)} %get-tuple-element.40.mean), custom_call_target="tpu_custom_call" | custom-call | flops 536870912 | bytes 8388608 | tf_op jit(solution)/shard_map/pallas_call | solution.py:470
  27.1 0.1 collective-permute-start.13
  27.2 1.3 %collective-permute-start.14 = (f32[16,256]{1,0:T(8,128)S(1)}, f32[16,256]{1,0:T(8,128)S(1)}, u32[]{:S(2)}, u32[]{:S(2)}) collective-permute-start(f32[16,256]{1,0:T(8,128)S(1)} %get-tuple-element.48), channel_id=1, source_target_pairs={{0,2},{1,3},{2,0},{3,1},{4,6},{5,7},{6,4},{7,5},{8,10},{9,11},{10,... | collective-permute-start | bytes 49160 | tf_op jit(solution)/shard_map/ppermute | solution.py:342
  28.5 0.0 collective-permute-done.9.refs_3_
  28.5 0.5 %collective-permute-start.15 = (f32[16,256]{1,0:T(8,128)S(1)}, f32[16,256]{1,0:T(8,128)S(1)}, u32[]{:S(2)}, u32[]{:S(2)}) collective-permute-start(f32[16,256]{1,0:T(8,128)S(1)} %get-tuple-element.49), channel_id=1, source_target_pairs={{0,3},{1,2},{2,1},{3,0},{4,7},{5,6},{6,5},{7,4},{8,11},{9,10},{10,... | collective-permute-start | bytes 49160 | tf_op jit(solution)/shard_map/ppermute | solution.py:342
  29.1 1.1 %collective-permute-done.8.refs_2_ = f32[64,256]{1,0:T(8,128)S(1)} collective-permute-done((f32[64,256]{1,0:T(8,128)S(1)}, f32[64,256]{1,0:T(8,128)S(1)}, u32[]{:S(2)}, u32[]{:S(2)}) %collective-permute-start.8) | collective-permute-done | bytes 65568 | tf_op jit(solution)/shard_map/ppermute | solution.py:347
  30.2 0.0 collective-permute-done.7.refs_1_
  30.2 0.8 %shard_map.56 = (f32[16,256]{1,0:T(8,128)S(1)}, f32[16,256]{1,0:T(8,128)S(1)}, f32[16,256]{1,0:T(8,128)S(1)}, f32[16,256]{1,0:T(8,128)S(1)}) custom-call(f32[64,256]{1,0:T(8,128)S(1)} %get-tuple-element.35.refs_0_, f32[64,256]{1,0:T(8,128)S(1)} %collective-permute-done.7.refs_1_, f32[64,256]{1,0:T(8,128)S(1)} %collective-permute-done.8.refs_2_, ...), custom_call_target="tpu_custom_call" | custom-call | flops 134217728 | bytes 262144 | tf_op jit(solution)/shard_map/pallas_call | solution.py:481
  31.0 0.0 collective-permute-start.10
  31.0 1.3 %collective-permute-start.11 = (f32[16,256]{1,0:T(8,128)S(1)}, f32[16,256]{1,0:T(8,128)S(1)}, u32[]{:S(2)}, u32[]{:S(2)}) collective-permute-start(f32[16,256]{1,0:T(8,128)S(1)} %get-tuple-element.44), channel_id=1, source_target_pairs={{0,2},{1,3},{2,0},{3,1},{4,6},{5,7},{6,4},{7,5},{8,10},{9,11},{10,... | collective-permute-start | bytes 49160 | tf_op jit(solution)/shard_map/ppermute | solution.py:342
  32.2 0.0 collective-permute-done.13.refs_1_
  32.3 0.6 %collective-permute-start.12 = (f32[16,256]{1,0:T(8,128)S(1)}, f32[16,256]{1,0:T(8,128)S(1)}, u32[]{:S(2)}, u32[]{:S(2)}) collective-permute-start(f32[16,256]{1,0:T(8,128)S(1)} %get-tuple-element.45), channel_id=1, source_target_pairs={{0,3},{1,2},{2,1},{3,0},{4,7},{5,6},{6,5},{7,4},{8,11},{9,10},{10,... | collective-permute-start | bytes 49160 | tf_op jit(solution)/shard_map/ppermute | solution.py:342
  32.9 0.0 collective-permute-done.14.refs_2_
  32.9 0.0 collective-permute-done.15.refs_3_
  32.9 1.3 %shard_map.57.refs_4_ = f32[64,8192]{1,0:T(8,128)S(1)} custom-call(f32[16,256]{1,0:T(8,128)S(1)} %get-tuple-element.46.refs_0_, f32[16,256]{1,0:T(8,128)S(1)} %collective-permute-done.13.refs_1_, f32[16,256]{1,0:T(8,128)S(1)} %collective-permute-done.14.refs_2_, f32[16,256]{1,0:T(8,128)S(1)} %collective-permute-done.15.refs_3_, ...), custom_call_target="tpu_custom_call" | custom-call | flops 536870912 | bytes 4194304 | tf_op jit(solution)/shard_map/pallas_call | solution.py:491
  34.2 0.0 collective-permute-done.10.refs_1_
  34.2 0.6 %collective-permute-done.11.refs_2_ = f32[16,256]{1,0:T(8,128)S(1)} collective-permute-done((f32[16,256]{1,0:T(8,128)S(1)}, f32[16,256]{1,0:T(8,128)S(1)}, u32[]{:S(2)}, u32[]{:S(2)}) %collective-permute-start.11) | collective-permute-done | bytes 16416 | tf_op jit(solution)/shard_map/ppermute | solution.py:342
  34.8 0.7 %collective-permute-done.12.refs_3_ = f32[16,256]{1,0:T(8,128)S(1)} collective-permute-done((f32[16,256]{1,0:T(8,128)S(1)}, f32[16,256]{1,0:T(8,128)S(1)}, u32[]{:S(2)}, u32[]{:S(2)}) %collective-permute-start.12) | collective-permute-done | bytes 16416 | tf_op jit(solution)/shard_map/ppermute | solution.py:342
  35.4 1.7 %shard_map.58 = f32[64,8192]{1,0:T(8,128)} custom-call(f32[16,256]{1,0:T(8,128)S(1)} %get-tuple-element.42.refs_0_, f32[16,256]{1,0:T(8,128)S(1)} %collective-permute-done.10.refs_1_, f32[16,256]{1,0:T(8,128)S(1)} %collective-permute-done.11.refs_2_, f32[16,256]{1,0:T(8,128)S(1)} %collective-permute-done.12.refs_3_, f32[64,8192]{1,0:T(8,128)S(1)} %shard_map.57.refs_4_, ...), custom_call_target="tpu_custom_call" | custom-call | flops 536870912 | bytes 4194304 | tf_op jit(solution)/shard_map/pallas_call | solution.py:500
  (1 shorter events, 0.0 us)
Async XLA Ops:
  3.5 4.4 %collective-permute-start = (f32[56,256]{1,0:T(8,128)S(1)}, f32[56,256]{1,0:T(8,128)S(1)}, u32[]{:S(2)}, u32[]{:S(2)}) collective-permute-start(f32[56,256]{1,0:T(8,128)S(1)} %get-tuple-element.30), channel_id=1, source_target_pairs={{0,1},{1,0},{2,3},{3,2},{4,5},{5,4},{6,7},{7,6},{8,9},{9,8},{10,11... | collective-permute-start | bytes 172040 | tf_op jit(solution)/shard_map/ppermute | solution.py:342
  4.0 5.8 %collective-permute-start.1 = (f32[56,256]{1,0:T(8,128)S(1)}, f32[56,256]{1,0:T(8,128)S(1)}, u32[]{:S(2)}, u32[]{:S(2)}) collective-permute-start(f32[56,256]{1,0:T(8,128)S(1)} %get-tuple-element.31), channel_id=1, source_target_pairs={{0,2},{1,3},{2,0},{3,1},{4,6},{5,7},{6,4},{7,5},{8,10},{9,11},{10,... | collective-permute-start | bytes 172040 | tf_op jit(solution)/shard_map/ppermute | solution.py:342
  6.6 3.3 %collective-permute-start.2 = (f32[24,256]{1,0:T(8,128)S(1)}, f32[24,256]{1,0:T(8,128)S(1)}, u32[]{:S(2)}, u32[]{:S(2)}) collective-permute-start(f32[24,256]{1,0:T(8,128)S(1)} %get-tuple-element.32), channel_id=1, source_target_pairs={{0,3},{1,2},{2,1},{3,0},{4,7},{5,6},{6,5},{7,4},{8,11},{9,10},{10,... | collective-permute-start | bytes 73736 | tf_op jit(solution)/shard_map/ppermute | solution.py:342
  9.9 7.3 %collective-permute-start.5 = (f32[72,256]{1,0:T(8,128)S(1)}, f32[72,256]{1,0:T(8,128)S(1)}, u32[]{:S(2)}, u32[]{:S(2)}) collective-permute-start(f32[72,256]{1,0:T(8,128)S(1)} %shard_map.49.own.one.refs_0_), channel_id=1, source_target_pairs={{0,12},{1,13},{2,14},{3,15},{4,8},{5,9},{6,10},{7,11},{8,4},{9,5},... | collective-permute-start | bytes 221192 | tf_op jit(solution)/shard_map/ppermute | solution.py:347
  13.6 6.5 %collective-permute-start.4 = (f32[72,256]{1,0:T(8,128)S(1)}, f32[72,256]{1,0:T(8,128)S(1)}, u32[]{:S(2)}, u32[]{:S(2)}) collective-permute-start(f32[72,256]{1,0:T(8,128)S(1)} %shard_map.49.own.one.refs_0_), channel_id=1, source_target_pairs={{0,8},{1,9},{2,10},{3,11},{4,12},{5,13},{6,14},{7,15},{8,0},{9,1},... | collective-permute-start | bytes 221192 | tf_op jit(solution)/shard_map/ppermute | solution.py:347
  13.6 6.5 %collective-permute-start.3 = (f32[72,256]{1,0:T(8,128)S(1)}, f32[72,256]{1,0:T(8,128)S(1)}, u32[]{:S(2)}, u32[]{:S(2)}) collective-permute-start(f32[72,256]{1,0:T(8,128)S(1)} %shard_map.49.own.one.refs_0_), channel_id=1, source_target_pairs={{0,4},{1,5},{2,6},{3,7},{4,0},{5,1},{6,2},{7,3},{8,12},{9,13},{10,... | collective-permute-start | bytes 221192 | tf_op jit(solution)/shard_map/ppermute | solution.py:347
  14.7 1.3 %collective-permute-start.6 = (f32[56,256]{1,0:T(8,128)S(1)}, f32[56,256]{1,0:T(8,128)S(1)}, u32[]{:S(2)}, u32[]{:S(2)}) collective-permute-start(f32[56,256]{1,0:T(8,128)S(1)} %get-tuple-element.34), channel_id=1, source_target_pairs={{0,1},{1,0},{2,3},{3,2},{4,5},{5,4},{6,7},{7,6},{8,9},{9,8},{10,11... | collective-permute-start | bytes 172040 | tf_op jit(solution)/shard_map/ppermute | solution.py:452
  21.4 7.1 %collective-permute-start.9 = (f32[64,256]{1,0:T(8,128)S(1)}, f32[64,256]{1,0:T(8,128)S(1)}, u32[]{:S(2)}, u32[]{:S(2)}) collective-permute-start(f32[64,256]{1,0:T(8,128)S(1)} %get-tuple-element.35.refs_0_), channel_id=1, source_target_pairs={{0,12},{1,13},{2,14},{3,15},{4,8},{5,9},{6,10},{7,11},{8,4},{9,5},... | collective-permute-start | bytes 196616 | tf_op jit(solution)/shard_map/ppermute | solution.py:347
  23.9 6.3 %collective-permute-start.8 = (f32[64,256]{1,0:T(8,128)S(1)}, f32[64,256]{1,0:T(8,128)S(1)}, u32[]{:S(2)}, u32[]{:S(2)}) collective-permute-start(f32[64,256]{1,0:T(8,128)S(1)} %get-tuple-element.35.refs_0_), channel_id=1, source_target_pairs={{0,8},{1,9},{2,10},{3,11},{4,12},{5,13},{6,14},{7,15},{8,0},{9,1},... | collective-permute-start | bytes 196616 | tf_op jit(solution)/shard_map/ppermute | solution.py:347
  23.9 6.3 %collective-permute-start.7 = (f32[64,256]{1,0:T(8,128)S(1)}, f32[64,256]{1,0:T(8,128)S(1)}, u32[]{:S(2)}, u32[]{:S(2)}) collective-permute-start(f32[64,256]{1,0:T(8,128)S(1)} %get-tuple-element.35.refs_0_), channel_id=1, source_target_pairs={{0,4},{1,5},{2,6},{3,7},{4,0},{5,1},{6,2},{7,3},{8,12},{9,13},{10,... | collective-permute-start | bytes 196616 | tf_op jit(solution)/shard_map/ppermute | solution.py:347
  27.1 5.1 %collective-permute-start.13 = (f32[16,256]{1,0:T(8,128)S(1)}, f32[16,256]{1,0:T(8,128)S(1)}, u32[]{:S(2)}, u32[]{:S(2)}) collective-permute-start(f32[16,256]{1,0:T(8,128)S(1)} %get-tuple-element.47), channel_id=1, source_target_pairs={{0,1},{1,0},{2,3},{3,2},{4,5},{5,4},{6,7},{7,6},{8,9},{9,8},{10,11... | collective-permute-start | bytes 49160 | tf_op jit(solution)/shard_map/ppermute | solution.py:342
  27.2 5.7 %collective-permute-start.14 = (f32[16,256]{1,0:T(8,128)S(1)}, f32[16,256]{1,0:T(8,128)S(1)}, u32[]{:S(2)}, u32[]{:S(2)}) collective-permute-start(f32[16,256]{1,0:T(8,128)S(1)} %get-tuple-element.48), channel_id=1, source_target_pairs={{0,2},{1,3},{2,0},{3,1},{4,6},{5,7},{6,4},{7,5},{8,10},{9,11},{10,... | collective-permute-start | bytes 49160 | tf_op jit(solution)/shard_map/ppermute | solution.py:342
  28.5 4.3 %collective-permute-start.15 = (f32[16,256]{1,0:T(8,128)S(1)}, f32[16,256]{1,0:T(8,128)S(1)}, u32[]{:S(2)}, u32[]{:S(2)}) collective-permute-start(f32[16,256]{1,0:T(8,128)S(1)} %get-tuple-element.49), channel_id=1, source_target_pairs={{0,3},{1,2},{2,1},{3,0},{4,7},{5,6},{6,5},{7,4},{8,11},{9,10},{10,... | collective-permute-start | bytes 49160 | tf_op jit(solution)/shard_map/ppermute | solution.py:342
  31.0 3.2 %collective-permute-start.10 = (f32[16,256]{1,0:T(8,128)S(1)}, f32[16,256]{1,0:T(8,128)S(1)}, u32[]{:S(2)}, u32[]{:S(2)}) collective-permute-start(f32[16,256]{1,0:T(8,128)S(1)} %get-tuple-element.43), channel_id=1, source_target_pairs={{0,1},{1,0},{2,3},{3,2},{4,5},{5,4},{6,7},{7,6},{8,9},{9,8},{10,11... | collective-permute-start | bytes 49160 | tf_op jit(solution)/shard_map/ppermute | solution.py:342
  31.0 3.8 %collective-permute-start.11 = (f32[16,256]{1,0:T(8,128)S(1)}, f32[16,256]{1,0:T(8,128)S(1)}, u32[]{:S(2)}, u32[]{:S(2)}) collective-permute-start(f32[16,256]{1,0:T(8,128)S(1)} %get-tuple-element.44), channel_id=1, source_target_pairs={{0,2},{1,3},{2,0},{3,1},{4,6},{5,7},{6,4},{7,5},{8,10},{9,11},{10,... | collective-permute-start | bytes 49160 | tf_op jit(solution)/shard_map/ppermute | solution.py:342
  32.3 3.2 %collective-permute-start.12 = (f32[16,256]{1,0:T(8,128)S(1)}, f32[16,256]{1,0:T(8,128)S(1)}, u32[]{:S(2)}, u32[]{:S(2)}) collective-permute-start(f32[16,256]{1,0:T(8,128)S(1)} %get-tuple-element.45), channel_id=1, source_target_pairs={{0,3},{1,2},{2,1},{3,0},{4,7},{5,6},{6,5},{7,4},{8,11},{9,10},{10,... | collective-permute-start | bytes 49160 | tf_op jit(solution)/shard_map/ppermute | solution.py:342

commit v22 on v21

--- a/solution.py
+++ b/solution.py
@@ -62,11 +62,12 @@
 
 def by_worker(x, table):
     rows, width = x.shape
-    hi, lo = split(x)
-    both = jnp.concatenate([hi, lo], axis=0)
-    step = table.shape[0]
-    total = jnp.concatenate([dot(both[:, k : k + step], table) for k in range(0, width, step)], axis=1)
-    return total[:rows] + total[rows:]
+    step = table.shape[1]
+    both = [
+        jnp.concatenate([one[:, k : k + step] for k in range(0, width, step)], axis=0) for one in split(x)
+    ]
+    total = dot(jnp.concatenate(both, axis=1), table)
+    return jnp.concatenate([total[k : k + rows] for k in range(0, total.shape[0], rows)], axis=1)
 
 
 def start_all(copies):
@@ -128,11 +129,10 @@
     for send in sends[:3]:
         send[part + 8 :] = masked
 
-    table = same_worker(pad, 256)
+    table = jnp.concatenate([same_worker(pad, 256)] * 2, axis=0)
+    wait_all(copies)
     total = None
     for b in range(len(copies)):
-        if b % 4 == 0:
-            wait_all(copies[b : b + 4])
         ok = row(valid, b, BLOCK)
         x0 = x[:, b * BLOCK : (b + 1) * BLOCK] * ok
         rest = x0 - by_worker(x0, table) * row(weight, b, BLOCK)
@@ -273,12 +273,12 @@
     for k, send in enumerate(sends):
         send[...] = mean[part * k : part * (k + 1)]
     slots, width = spread.shape
-    table = same_worker(pad, 256)
+    table = jnp.concatenate([same_worker(pad, 256)] * 2, axis=0)
     for b in range(width // BLOCK):
         found = one_hot(row(mask_ids, b, BLOCK), slots)
         spread[:, b * BLOCK : (b + 1) * BLOCK] = found
         for at in range(0, BLOCK, 256):
-            count = dot(found[:, at : at + 256], table)
+            count = dot(found[:, at : at + 256], table[:256])
             workers[:, b * BLOCK + at : b * BLOCK + at + 256] = count.astype(BF16)
 
 
@@ -308,7 +308,7 @@
     parts, (x1, mask_ids, weight), tables, (y, means) = refs[:NEAR], refs[NEAR : NEAR + 3], refs[NEAR + 3 : -2], refs[-2:]
     columns, slots = means.shape
     first = own_means(parts, means)
-    table = same_worker(pad, 256)
+    table = jnp.concatenate([same_worker(pad, 256)] * 2, axis=0)
     for b in range(y.shape[1] // BLOCK):
         at = slice(b * BLOCK, (b + 1) * BLOCK)
         found = tables[0][:, at] if tables else one_hot(row(mask_ids, b, BLOCK), slots)

time: 37.3 us -> 37.1 us (level)
  no operation moved by 1% of the time
where the time goes in v22:
time: 37.1 us; the launch traced here: 37 us
  starting transfers between devices  15.9 us (43%)
  Pallas kernels  15.3 us (41%)
  waiting for transfers between devices  5.61 us (15%)
    ppermute x6, starting transfers between devices, far_share(): return [one] + [lax.ppermute(one, 'rows', step) for step in steps]  8.85 us
    ppermute x9, starting transfers between devices, near_exchange(): lax.ppermute(one, 'rows', step)  6.99 us
    pallas_call x4, Pallas kernels, pair_counts(): call(functools.partial(pairs_kernel, pad, about), array((len(parts), slot...  4.92 us
    ppermute x6, waiting for transfers between devices, far_share(): return [one] + [lax.ppermute(one, 'rows', step) for step in steps]  3.68 us
    pallas_call x1, Pallas kernels, body(): call(functools.partial(sums_kernel, pad, slots // n), [message] * 3 + [ar...  3.35 us
    ppermute x9, waiting for transfers between devices, near_exchange(): lax.ppermute(one, 'rows', step)  1.93 us
    pallas_call x1, Pallas kernels, body(): call(last_kernel, array(whole, F32), [vmem] * (NEAR + 2 + len(spreads[:1]...  1.7 us
    pallas_call x1, Pallas kernels, body(): call(functools.partial(change_kernel, far, part, len(tables)), [of_near,...  1.37 us
  transfers between devices with their start and end apart: 16, of which 5 were waited for; matrix products, arithmetic and copies ran while one was open for 0% of the time, Pallas kernels for 24%

profile of v22, /device:TPU:0, one launch (start us, length us, event | category | flops | bytes accessed | tf_op | source)
XLA Modules:
  0.0 37.0 jit_solution(15432394235339352144)
XLA Ops:
  0.0 3.3 %shard_map.46 = (f32[56,256]{1,0:T(8,128)S(1)}, f32[56,256]{1,0:T(8,128)S(1)}, f32[56,256]{1,0:T(8,128)S(1)}, f32[24,256]{1,0:T(8,128)S(1)}, f32[64,8192]{1,0:T(...) custom-call(f32[64,8192]{1,0:T(8,128)} %refs_0_.1, s32[8,128]{1,0:T(8,128)} %bitcast.4, s32[64,128]{1,0:T(8,128)} %bitcast.3, ...), custom_call_target="tpu_custom_call" | custom-call | flops 1073741824 | bytes 2097152 | tf_op jit(solution)/shard_map/pallas_call | solution.py:389
  3.4 0.5 %collective-permute-start = (f32[56,256]{1,0:T(8,128)S(1)}, f32[56,256]{1,0:T(8,128)S(1)}, u32[]{:S(2)}, u32[]{:S(2)}) collective-permute-start(f32[56,256]{1,0:T(8,128)S(1)} %get-tuple-element.30), channel_id=1, source_target_pairs={{0,1},{1,0},{2,3},{3,2},{4,5},{5,4},{6,7},{7,6},{8,9},{9,8},{10,11... | collective-permute-start | bytes 172040 | tf_op jit(solution)/shard_map/ppermute | solution.py:342
  3.9 2.6 %collective-permute-start.1 = (f32[56,256]{1,0:T(8,128)S(1)}, f32[56,256]{1,0:T(8,128)S(1)}, u32[]{:S(2)}, u32[]{:S(2)}) collective-permute-start(f32[56,256]{1,0:T(8,128)S(1)} %get-tuple-element.31), channel_id=1, source_target_pairs={{0,2},{1,3},{2,0},{3,1},{4,6},{5,7},{6,4},{7,5},{8,10},{9,11},{10,... | collective-permute-start | bytes 172040 | tf_op jit(solution)/shard_map/ppermute | solution.py:342
  6.5 0.1 collective-permute-start.2
  6.5 1.2 %shard_map.47.refs_4_.refs_6_ = bf16[1,256,512]{2,1,0:T(8,128)(2,1)S(1)} custom-call(f32[56,256]{1,0:T(8,128)S(1)} %get-tuple-element.29.refs_0_), custom_call_target="tpu_custom_call" | custom-call | flops 134217728 | bytes 262144 | tf_op jit(solution)/shard_map/pallas_call | solution.py:409
  7.8 0.0 collective-permute-done.refs_0_.refs_1_
  7.8 1.2 %shard_map.48.refs_5_.refs_7_ = bf16[1,256,512]{2,1,0:T(8,128)(2,1)S(1)} custom-call(f32[56,256]{1,0:T(8,128)S(1)} %collective-permute-done.refs_0_.refs_1_), custom_call_target="tpu_custom_call" | custom-call | flops 134217728 | bytes 262144 | tf_op jit(solution)/shard_map/pallas_call | solution.py:409
  9.0 0.7 %collective-permute-done.2.refs_3_ = f32[24,256]{1,0:T(8,128)S(1)} collective-permute-done((f32[24,256]{1,0:T(8,128)S(1)}, f32[24,256]{1,0:T(8,128)S(1)}, u32[]{:S(2)}, u32[]{:S(2)}) %collective-permute-start.2) | collective-permute-done | bytes 24608 | tf_op jit(solution)/shard_map/ppermute | solution.py:342
  9.7 0.0 collective-permute-done.1.refs_2_.passed.refs_0_
  9.7 3.7 %collective-permute-start.5 = (f32[72,256]{1,0:T(8,128)S(1)}, f32[72,256]{1,0:T(8,128)S(1)}, u32[]{:S(2)}, u32[]{:S(2)}) collective-permute-start(f32[72,256]{1,0:T(8,128)S(1)} %shard_map.49.own.one.refs_0_), channel_id=1, source_target_pairs={{0,12},{1,13},{2,14},{3,15},{4,8},{5,9},{6,10},{7,11},{8,4},{9,5},... | collective-permute-start | bytes 221192 | tf_op jit(solution)/shard_map/ppermute | solution.py:347
  13.4 0.0 collective-permute-start.4
  13.4 0.8 %collective-permute-start.3 = (f32[72,256]{1,0:T(8,128)S(1)}, f32[72,256]{1,0:T(8,128)S(1)}, u32[]{:S(2)}, u32[]{:S(2)}) collective-permute-start(f32[72,256]{1,0:T(8,128)S(1)} %shard_map.49.own.one.refs_0_), channel_id=1, source_target_pairs={{0,4},{1,5},{2,6},{3,7},{4,0},{5,1},{6,2},{7,3},{8,12},{9,13},{10,... | collective-permute-start | bytes 221192 | tf_op jit(solution)/shard_map/ppermute | solution.py:347
  14.2 0.3 shard_map.50
  14.5 0.1 collective-permute-start.6
  14.6 1.2 %shard_map.52.refs_8_ = bf16[1,256,512]{2,1,0:T(8,128)(2,1)S(1)} custom-call(f32[56,256]{1,0:T(8,128)S(1)} %collective-permute-done.1.refs_2_.passed.refs_0_), custom_call_target="tpu_custom_call" | custom-call | flops 134217728 | bytes 262144 | tf_op jit(solution)/shard_map/pallas_call | solution.py:409
  15.8 0.0 collective-permute-done.6.refs_0_
  15.8 1.2 %shard_map.53.refs_9_ = bf16[1,256,512]{2,1,0:T(8,128)(2,1)S(1)} custom-call(f32[56,256]{1,0:T(8,128)S(1)} %collective-permute-done.6.refs_0_), custom_call_target="tpu_custom_call" | custom-call | flops 134217728 | bytes 262144 | tf_op jit(solution)/shard_map/pallas_call | solution.py:409
  17.1 0.0 collective-permute-done.5.one.refs_3_
  17.1 0.3 shard_map.51.refs_5_.refs_7_
  17.4 2.5 %collective-permute-done.4.refs_2_ = f32[72,256]{1,0:T(8,128)S(1)} collective-permute-done((f32[72,256]{1,0:T(8,128)S(1)}, f32[72,256]{1,0:T(8,128)S(1)}, u32[]{:S(2)}, u32[]{:S(2)}) %collective-permute-start.4) | collective-permute-done | bytes 73760 | tf_op jit(solution)/shard_map/ppermute | solution.py:347
  19.9 0.0 collective-permute-done.3.refs_1_
  19.9 1.4 %shard_map.54 = (f32[64,256]{1,0:T(8,128)S(1)}, f32[64,256]{1,0:T(8,128)S(1)}, f32[2,8,512]{2,1,0:T(8,128)S(1)}, bf16[2,512,512]{2,1,0:T(8,128)(2,1)S(1)}, bf16[2,512,512]{2,1,0:T(8,128)(2,1)S(1)}) custom-call(f32[72,256]{1,0:T(8,128)S(1)} %shard_map.49.own.one.refs_0_, f32[72,256]{1,0:T(8,128)S(1)} %collective-permute-done.3.refs_1_, ...), custom_call_target="tpu_custom_call" | custom-call | flops 134217728 | bytes 262144 | tf_op jit(solution)/shard_map/pallas_call | solution.py:456
  21.3 2.5 %collective-permute-start.9 = (f32[64,256]{1,0:T(8,128)S(1)}, f32[64,256]{1,0:T(8,128)S(1)}, u32[]{:S(2)}, u32[]{:S(2)}) collective-permute-start(f32[64,256]{1,0:T(8,128)S(1)} %get-tuple-element.35.refs_0_), channel_id=1, source_target_pairs={{0,12},{1,13},{2,14},{3,15},{4,8},{5,9},{6,10},{7,11},{8,4},{9,5},... | collective-permute-start | bytes 196616 | tf_op jit(solution)/shard_map/ppermute | solution.py:347
  23.8 0.0 collective-permute-start.8
  23.8 1.9 %collective-permute-start.7 = (f32[64,256]{1,0:T(8,128)S(1)}, f32[64,256]{1,0:T(8,128)S(1)}, u32[]{:S(2)}, u32[]{:S(2)}) collective-permute-start(f32[64,256]{1,0:T(8,128)S(1)} %get-tuple-element.35.refs_0_), channel_id=1, source_target_pairs={{0,4},{1,5},{2,6},{3,7},{4,0},{5,1},{6,2},{7,3},{8,12},{9,13},{10,... | collective-permute-start | bytes 196616 | tf_op jit(solution)/shard_map/ppermute | solution.py:347
  25.7 1.3 %shard_map.55 = (bf16[256,8192]{1,0:T(8,128)(2,1)S(1)}, bf16[256,8192]{1,0:T(8,128)(2,1)S(1)}, f32[16,256]{1,0:T(8,128)S(1)}, f32[16,256]{1,0:T(8,128)S(1)}, f32...) custom-call(s32[64,128]{1,0:T(8,128)S(1)} %get-tuple-element.39.mask_ids.refs_5_, f32[64,256]{1,0:T(8,128)S(1)} %get-tuple-element.40.mean), custom_call_target="tpu_custom_call" | custom-call | flops 536870912 | bytes 8388608 | tf_op jit(solution)/shard_map/pallas_call | solution.py:470
  27.0 0.1 collective-permute-start.13
  27.0 1.3 %collective-permute-start.14 = (f32[16,256]{1,0:T(8,128)S(1)}, f32[16,256]{1,0:T(8,128)S(1)}, u32[]{:S(2)}, u32[]{:S(2)}) collective-permute-start(f32[16,256]{1,0:T(8,128)S(1)} %get-tuple-element.48), channel_id=1, source_target_pairs={{0,2},{1,3},{2,0},{3,1},{4,6},{5,7},{6,4},{7,5},{8,10},{9,11},{10,... | collective-permute-start | bytes 49160 | tf_op jit(solution)/shard_map/ppermute | solution.py:342
  28.4 0.0 collective-permute-done.9.refs_3_
  28.4 0.5 %collective-permute-start.15 = (f32[16,256]{1,0:T(8,128)S(1)}, f32[16,256]{1,0:T(8,128)S(1)}, u32[]{:S(2)}, u32[]{:S(2)}) collective-permute-start(f32[16,256]{1,0:T(8,128)S(1)} %get-tuple-element.49), channel_id=1, source_target_pairs={{0,3},{1,2},{2,1},{3,0},{4,7},{5,6},{6,5},{7,4},{8,11},{9,10},{10,... | collective-permute-start | bytes 49160 | tf_op jit(solution)/shard_map/ppermute | solution.py:342
  28.9 1.1 %collective-permute-done.8.refs_2_ = f32[64,256]{1,0:T(8,128)S(1)} collective-permute-done((f32[64,256]{1,0:T(8,128)S(1)}, f32[64,256]{1,0:T(8,128)S(1)}, u32[]{:S(2)}, u32[]{:S(2)}) %collective-permute-start.8) | collective-permute-done | bytes 65568 | tf_op jit(solution)/shard_map/ppermute | solution.py:347
  30.1 0.0 collective-permute-done.7.refs_1_
  30.1 0.8 %shard_map.56 = (f32[16,256]{1,0:T(8,128)S(1)}, f32[16,256]{1,0:T(8,128)S(1)}, f32[16,256]{1,0:T(8,128)S(1)}, f32[16,256]{1,0:T(8,128)S(1)}) custom-call(f32[64,256]{1,0:T(8,128)S(1)} %get-tuple-element.35.refs_0_, f32[64,256]{1,0:T(8,128)S(1)} %collective-permute-done.7.refs_1_, f32[64,256]{1,0:T(8,128)S(1)} %collective-permute-done.8.refs_2_, ...), custom_call_target="tpu_custom_call" | custom-call | flops 134217728 | bytes 262144 | tf_op jit(solution)/shard_map/pallas_call | solution.py:481
  30.8 0.0 collective-permute-start.10
  30.8 1.3 %collective-permute-start.11 = (f32[16,256]{1,0:T(8,128)S(1)}, f32[16,256]{1,0:T(8,128)S(1)}, u32[]{:S(2)}, u32[]{:S(2)}) collective-permute-start(f32[16,256]{1,0:T(8,128)S(1)} %get-tuple-element.44), channel_id=1, source_target_pairs={{0,2},{1,3},{2,0},{3,1},{4,6},{5,7},{6,4},{7,5},{8,10},{9,11},{10,... | collective-permute-start | bytes 49160 | tf_op jit(solution)/shard_map/ppermute | solution.py:342
  32.1 0.0 collective-permute-done.13.refs_1_
  32.1 0.6 %collective-permute-start.12 = (f32[16,256]{1,0:T(8,128)S(1)}, f32[16,256]{1,0:T(8,128)S(1)}, u32[]{:S(2)}, u32[]{:S(2)}) collective-permute-start(f32[16,256]{1,0:T(8,128)S(1)} %get-tuple-element.45), channel_id=1, source_target_pairs={{0,3},{1,2},{2,1},{3,0},{4,7},{5,6},{6,5},{7,4},{8,11},{9,10},{10,... | collective-permute-start | bytes 49160 | tf_op jit(solution)/shard_map/ppermute | solution.py:342
  32.7 0.0 collective-permute-done.14.refs_2_
  32.7 0.0 collective-permute-done.15.refs_3_
  32.7 1.3 %shard_map.57.refs_4_ = f32[64,8192]{1,0:T(8,128)S(1)} custom-call(f32[16,256]{1,0:T(8,128)S(1)} %get-tuple-element.46.refs_0_, f32[16,256]{1,0:T(8,128)S(1)} %collective-permute-done.13.refs_1_, f32[16,256]{1,0:T(8,128)S(1)} %collective-permute-done.14.refs_2_, f32[16,256]{1,0:T(8,128)S(1)} %collective-permute-done.15.refs_3_, ...), custom_call_target="tpu_custom_call" | custom-call | flops 536870912 | bytes 4194304 | tf_op jit(solution)/shard_map/pallas_call | solution.py:491
  34.0 0.0 collective-permute-done.10.refs_1_
  34.0 0.6 %collective-permute-done.11.refs_2_ = f32[16,256]{1,0:T(8,128)S(1)} collective-permute-done((f32[16,256]{1,0:T(8,128)S(1)}, f32[16,256]{1,0:T(8,128)S(1)}, u32[]{:S(2)}, u32[]{:S(2)}) %collective-permute-start.11) | collective-permute-done | bytes 16416 | tf_op jit(solution)/shard_map/ppermute | solution.py:342
  34.6 0.7 %collective-permute-done.12.refs_3_ = f32[16,256]{1,0:T(8,128)S(1)} collective-permute-done((f32[16,256]{1,0:T(8,128)S(1)}, f32[16,256]{1,0:T(8,128)S(1)}, u32[]{:S(2)}, u32[]{:S(2)}) %collective-permute-start.12) | collective-permute-done | bytes 16416 | tf_op jit(solution)/shard_map/ppermute | solution.py:342
  35.3 1.7 %shard_map.58 = f32[64,8192]{1,0:T(8,128)} custom-call(f32[16,256]{1,0:T(8,128)S(1)} %get-tuple-element.42.refs_0_, f32[16,256]{1,0:T(8,128)S(1)} %collective-permute-done.10.refs_1_, f32[16,256]{1,0:T(8,128)S(1)} %collective-permute-done.11.refs_2_, f32[16,256]{1,0:T(8,128)S(1)} %collective-permute-done.12.refs_3_, f32[64,8192]{1,0:T(8,128)S(1)} %shard_map.57.refs_4_, ...), custom_call_target="tpu_custom_call" | custom-call | flops 536870912 | bytes 4194304 | tf_op jit(solution)/shard_map/pallas_call | solution.py:500
  (1 shorter events, 0.0 us)
Async XLA Ops:
  3.4 4.4 %collective-permute-start = (f32[56,256]{1,0:T(8,128)S(1)}, f32[56,256]{1,0:T(8,128)S(1)}, u32[]{:S(2)}, u32[]{:S(2)}) collective-permute-start(f32[56,256]{1,0:T(8,128)S(1)} %get-tuple-element.30), channel_id=1, source_target_pairs={{0,1},{1,0},{2,3},{3,2},{4,5},{5,4},{6,7},{7,6},{8,9},{9,8},{10,11... | collective-permute-start | bytes 172040 | tf_op jit(solution)/shard_map/ppermute | solution.py:342
  3.9 5.8 %collective-permute-start.1 = (f32[56,256]{1,0:T(8,128)S(1)}, f32[56,256]{1,0:T(8,128)S(1)}, u32[]{:S(2)}, u32[]{:S(2)}) collective-permute-start(f32[56,256]{1,0:T(8,128)S(1)} %get-tuple-element.31), channel_id=1, source_target_pairs={{0,2},{1,3},{2,0},{3,1},{4,6},{5,7},{6,4},{7,5},{8,10},{9,11},{10,... | collective-permute-start | bytes 172040 | tf_op jit(solution)/shard_map/ppermute | solution.py:342
  6.5 3.3 %collective-permute-start.2 = (f32[24,256]{1,0:T(8,128)S(1)}, f32[24,256]{1,0:T(8,128)S(1)}, u32[]{:S(2)}, u32[]{:S(2)}) collective-permute-start(f32[24,256]{1,0:T(8,128)S(1)} %get-tuple-element.32), channel_id=1, source_target_pairs={{0,3},{1,2},{2,1},{3,0},{4,7},{5,6},{6,5},{7,4},{8,11},{9,10},{10,... | collective-permute-start | bytes 73736 | tf_op jit(solution)/shard_map/ppermute | solution.py:342
  9.7 7.3 %collective-permute-start.5 = (f32[72,256]{1,0:T(8,128)S(1)}, f32[72,256]{1,0:T(8,128)S(1)}, u32[]{:S(2)}, u32[]{:S(2)}) collective-permute-start(f32[72,256]{1,0:T(8,128)S(1)} %shard_map.49.own.one.refs_0_), channel_id=1, source_target_pairs={{0,12},{1,13},{2,14},{3,15},{4,8},{5,9},{6,10},{7,11},{8,4},{9,5},... | collective-permute-start | bytes 221192 | tf_op jit(solution)/shard_map/ppermute | solution.py:347
  13.4 6.5 %collective-permute-start.4 = (f32[72,256]{1,0:T(8,128)S(1)}, f32[72,256]{1,0:T(8,128)S(1)}, u32[]{:S(2)}, u32[]{:S(2)}) collective-permute-start(f32[72,256]{1,0:T(8,128)S(1)} %shard_map.49.own.one.refs_0_), channel_id=1, source_target_pairs={{0,8},{1,9},{2,10},{3,11},{4,12},{5,13},{6,14},{7,15},{8,0},{9,1},... | collective-permute-start | bytes 221192 | tf_op jit(solution)/shard_map/ppermute | solution.py:347
  13.4 6.5 %collective-permute-start.3 = (f32[72,256]{1,0:T(8,128)S(1)}, f32[72,256]{1,0:T(8,128)S(1)}, u32[]{:S(2)}, u32[]{:S(2)}) collective-permute-start(f32[72,256]{1,0:T(8,128)S(1)} %shard_map.49.own.one.refs_0_), channel_id=1, source_target_pairs={{0,4},{1,5},{2,6},{3,7},{4,0},{5,1},{6,2},{7,3},{8,12},{9,13},{10,... | collective-permute-start | bytes 221192 | tf_op jit(solution)/shard_map/ppermute | solution.py:347
  14.5 1.3 %collective-permute-start.6 = (f32[56,256]{1,0:T(8,128)S(1)}, f32[56,256]{1,0:T(8,128)S(1)}, u32[]{:S(2)}, u32[]{:S(2)}) collective-permute-start(f32[56,256]{1,0:T(8,128)S(1)} %get-tuple-element.34), channel_id=1, source_target_pairs={{0,1},{1,0},{2,3},{3,2},{4,5},{5,4},{6,7},{7,6},{8,9},{9,8},{10,11... | collective-permute-start | bytes 172040 | tf_op jit(solution)/shard_map/ppermute | solution.py:452
  21.3 7.1 %collective-permute-start.9 = (f32[64,256]{1,0:T(8,128)S(1)}, f32[64,256]{1,0:T(8,128)S(1)}, u32[]{:S(2)}, u32[]{:S(2)}) collective-permute-start(f32[64,256]{1,0:T(8,128)S(1)} %get-tuple-element.35.refs_0_), channel_id=1, source_target_pairs={{0,12},{1,13},{2,14},{3,15},{4,8},{5,9},{6,10},{7,11},{8,4},{9,5},... | collective-permute-start | bytes 196616 | tf_op jit(solution)/shard_map/ppermute | solution.py:347
  23.8 6.3 %collective-permute-start.8 = (f32[64,256]{1,0:T(8,128)S(1)}, f32[64,256]{1,0:T(8,128)S(1)}, u32[]{:S(2)}, u32[]{:S(2)}) collective-permute-start(f32[64,256]{1,0:T(8,128)S(1)} %get-tuple-element.35.refs_0_), channel_id=1, source_target_pairs={{0,8},{1,9},{2,10},{3,11},{4,12},{5,13},{6,14},{7,15},{8,0},{9,1},... | collective-permute-start | bytes 196616 | tf_op jit(solution)/shard_map/ppermute | solution.py:347
  23.8 6.3 %collective-permute-start.7 = (f32[64,256]{1,0:T(8,128)S(1)}, f32[64,256]{1,0:T(8,128)S(1)}, u32[]{:S(2)}, u32[]{:S(2)}) collective-permute-start(f32[64,256]{1,0:T(8,128)S(1)} %get-tuple-element.35.refs_0_), channel_id=1, source_target_pairs={{0,4},{1,5},{2,6},{3,7},{4,0},{5,1},{6,2},{7,3},{8,12},{9,13},{10,... | collective-permute-start | bytes 196616 | tf_op jit(solution)/shard_map/ppermute | solution.py:347
  27.0 5.1 %collective-permute-start.13 = (f32[16,256]{1,0:T(8,128)S(1)}, f32[16,256]{1,0:T(8,128)S(1)}, u32[]{:S(2)}, u32[]{:S(2)}) collective-permute-start(f32[16,256]{1,0:T(8,128)S(1)} %get-tuple-element.47), channel_id=1, source_target_pairs={{0,1},{1,0},{2,3},{3,2},{4,5},{5,4},{6,7},{7,6},{8,9},{9,8},{10,11... | collective-permute-start | bytes 49160 | tf_op jit(solution)/shard_map/ppermute | solution.py:342
  27.0 5.7 %collective-permute-start.14 = (f32[16,256]{1,0:T(8,128)S(1)}, f32[16,256]{1,0:T(8,128)S(1)}, u32[]{:S(2)}, u32[]{:S(2)}) collective-permute-start(f32[16,256]{1,0:T(8,128)S(1)} %get-tuple-element.48), channel_id=1, source_target_pairs={{0,2},{1,3},{2,0},{3,1},{4,6},{5,7},{6,4},{7,5},{8,10},{9,11},{10,... | collective-permute-start | bytes 49160 | tf_op jit(solution)/shard_map/ppermute | solution.py:342
  28.4 4.3 %collective-permute-start.15 = (f32[16,256]{1,0:T(8,128)S(1)}, f32[16,256]{1,0:T(8,128)S(1)}, u32[]{:S(2)}, u32[]{:S(2)}) collective-permute-start(f32[16,256]{1,0:T(8,128)S(1)} %get-tuple-element.49), channel_id=1, source_target_pairs={{0,3},{1,2},{2,1},{3,0},{4,7},{5,6},{6,5},{7,4},{8,11},{9,10},{10,... | collective-permute-start | bytes 49160 | tf_op jit(solution)/shard_map/ppermute | solution.py:342
  30.8 3.2 %collective-permute-start.10 = (f32[16,256]{1,0:T(8,128)S(1)}, f32[16,256]{1,0:T(8,128)S(1)}, u32[]{:S(2)}, u32[]{:S(2)}) collective-permute-start(f32[16,256]{1,0:T(8,128)S(1)} %get-tuple-element.43), channel_id=1, source_target_pairs={{0,1},{1,0},{2,3},{3,2},{4,5},{5,4},{6,7},{7,6},{8,9},{9,8},{10,11... | collective-permute-start | bytes 49160 | tf_op jit(solution)/shard_map/ppermute | solution.py:342
  30.8 3.8 %collective-permute-start.11 = (f32[16,256]{1,0:T(8,128)S(1)}, f32[16,256]{1,0:T(8,128)S(1)}, u32[]{:S(2)}, u32[]{:S(2)}) collective-permute-start(f32[16,256]{1,0:T(8,128)S(1)} %get-tuple-element.44), channel_id=1, source_target_pairs={{0,2},{1,3},{2,0},{3,1},{4,6},{5,7},{6,4},{7,5},{8,10},{9,11},{10,... | collective-permute-start | bytes 49160 | tf_op jit(solution)/shard_map/ppermute | solution.py:342
  32.1 3.2 %collective-permute-start.12 = (f32[16,256]{1,0:T(8,128)S(1)}, f32[16,256]{1,0:T(8,128)S(1)}, u32[]{:S(2)}, u32[]{:S(2)}) collective-permute-start(f32[16,256]{1,0:T(8,128)S(1)} %get-tuple-element.45), channel_id=1, source_target_pairs={{0,3},{1,2},{2,1},{3,0},{4,7},{5,6},{6,5},{7,4},{8,11},{9,10},{10,... | collective-permute-start | bytes 49160 | tf_op jit(solution)/shard_map/ppermute | solution.py:342

commit v23 on v22

--- a/solution.py
+++ b/solution.py
@@ -49,9 +49,9 @@
     kind = BF16 if slots <= 256 else F32
     one, zero = jnp.ones((LANES, LANES), kind), jnp.zeros((LANES, LANES), kind)
     along_slots = [(iota((LANES, LANES), 1) + at).astype(F32).astype(kind) for at in range(0, slots, LANES)]
-    parts = []
+    parts, columns = [], columns.astype(kind)
     for k in range(columns.shape[1]):
-        ids = jnp.broadcast_to(columns[:, k : k + 1], (LANES, LANES)).astype(kind)
+        ids = jnp.broadcast_to(columns[:, k : k + 1], (LANES, LANES))
         parts.append(jnp.concatenate([jnp.where(slot == ids, one, zero) for slot in along_slots], axis=1))
     return jnp.concatenate(parts, axis=0).astype(BF16)
 
@@ -324,16 +324,15 @@
 
 def last_kernel(*refs):
     parts, (before, mask_ids), tables, (out, means, y, sems) = refs[:NEAR], refs[NEAR : NEAR + 2], refs[NEAR + 2 : -4], refs[-4:]
-    outs = column_copies(y, out, sems, 2 * BLOCK)
+    outs = column_copies(y, out, sems)
     columns, slots = means.shape
     second = own_means(parts, means)
-    for b in range(2 * len(outs)):
+    for b in range(len(outs)):
         at = slice(b * BLOCK, (b + 1) * BLOCK)
         found = tables[0][:, at] if tables else one_hot(row(mask_ids, b, BLOCK), slots)
         spread = dot(second, found)
         y[:, at] = before[:, at] - (spread[:columns] + spread[columns:])
-        if b % 2:
-            outs[b // 2].start()
+        outs[b].start()
     wait_all(outs)
 
 

time: 37.1 us -> 37 us (level)
  no operation moved by 1% of the time
where the time goes in v23:
time: 37 us; the launch traced here: 36.9 us
  starting transfers between devices  15.9 us (43%)
  Pallas kernels  15.3 us (41%)
  waiting for transfers between devices  5.59 us (15%)
    ppermute x6, starting transfers between devices, far_share(): return [one] + [lax.ppermute(one, 'rows', step) for step in steps]  8.85 us
    ppermute x9, starting transfers between devices, near_exchange(): lax.ppermute(one, 'rows', step)  6.99 us
    pallas_call x4, Pallas kernels, pair_counts(): call(functools.partial(pairs_kernel, pad, about), array((len(parts), slot...  4.92 us
    ppermute x6, waiting for transfers between devices, far_share(): return [one] + [lax.ppermute(one, 'rows', step) for step in steps]  3.66 us
    pallas_call x1, Pallas kernels, body(): call(functools.partial(sums_kernel, pad, slots // n), [message] * 3 + [ar...  3.37 us
    ppermute x9, waiting for transfers between devices, near_exchange(): lax.ppermute(one, 'rows', step)  1.92 us
    pallas_call x1, Pallas kernels, body(): call(last_kernel, array(whole, F32), [vmem] * (NEAR + 2 + len(spreads[:1]...  1.62 us
    pallas_call x1, Pallas kernels, body(): call(functools.partial(change_kernel, far, part, len(tables)), [of_near,...  1.37 us
  transfers between devices with their start and end apart: 16, of which 5 were waited for; matrix products, arithmetic and copies ran while one was open for 0% of the time, Pallas kernels for 24%

profile of v23, /device:TPU:0, one launch (start us, length us, event | category | flops | bytes accessed | tf_op | source)
XLA Modules:
  0.0 36.9 jit_solution(18416689453299018954)
XLA Ops:
  0.0 3.4 %shard_map.46 = (f32[56,256]{1,0:T(8,128)S(1)}, f32[56,256]{1,0:T(8,128)S(1)}, f32[56,256]{1,0:T(8,128)S(1)}, f32[24,256]{1,0:T(8,128)S(1)}, f32[64,8192]{1,0:T(...) custom-call(f32[64,8192]{1,0:T(8,128)} %refs_0_.1, s32[8,128]{1,0:T(8,128)} %bitcast.4, s32[64,128]{1,0:T(8,128)} %bitcast.3, ...), custom_call_target="tpu_custom_call" | custom-call | flops 1073741824 | bytes 2097152 | tf_op jit(solution)/shard_map/pallas_call | solution.py:388
  3.4 0.5 %collective-permute-start = (f32[56,256]{1,0:T(8,128)S(1)}, f32[56,256]{1,0:T(8,128)S(1)}, u32[]{:S(2)}, u32[]{:S(2)}) collective-permute-start(f32[56,256]{1,0:T(8,128)S(1)} %get-tuple-element.30), channel_id=1, source_target_pairs={{0,1},{1,0},{2,3},{3,2},{4,5},{5,4},{6,7},{7,6},{8,9},{9,8},{10,11... | collective-permute-start | bytes 172040 | tf_op jit(solution)/shard_map/ppermute | solution.py:341
  3.9 2.6 %collective-permute-start.1 = (f32[56,256]{1,0:T(8,128)S(1)}, f32[56,256]{1,0:T(8,128)S(1)}, u32[]{:S(2)}, u32[]{:S(2)}) collective-permute-start(f32[56,256]{1,0:T(8,128)S(1)} %get-tuple-element.31), channel_id=1, source_target_pairs={{0,2},{1,3},{2,0},{3,1},{4,6},{5,7},{6,4},{7,5},{8,10},{9,11},{10,... | collective-permute-start | bytes 172040 | tf_op jit(solution)/shard_map/ppermute | solution.py:341
  6.5 0.1 collective-permute-start.2
  6.6 1.2 %shard_map.47.refs_4_.refs_6_ = bf16[1,256,512]{2,1,0:T(8,128)(2,1)S(1)} custom-call(f32[56,256]{1,0:T(8,128)S(1)} %get-tuple-element.29.refs_0_), custom_call_target="tpu_custom_call" | custom-call | flops 134217728 | bytes 262144 | tf_op jit(solution)/shard_map/pallas_call | solution.py:408
  7.8 0.0 collective-permute-done.refs_0_.refs_1_
  7.8 1.2 %shard_map.48.refs_5_.refs_7_ = bf16[1,256,512]{2,1,0:T(8,128)(2,1)S(1)} custom-call(f32[56,256]{1,0:T(8,128)S(1)} %collective-permute-done.refs_0_.refs_1_), custom_call_target="tpu_custom_call" | custom-call | flops 134217728 | bytes 262144 | tf_op jit(solution)/shard_map/pallas_call | solution.py:408
  9.0 0.7 %collective-permute-done.2.refs_3_ = f32[24,256]{1,0:T(8,128)S(1)} collective-permute-done((f32[24,256]{1,0:T(8,128)S(1)}, f32[24,256]{1,0:T(8,128)S(1)}, u32[]{:S(2)}, u32[]{:S(2)}) %collective-permute-start.2) | collective-permute-done | bytes 24608 | tf_op jit(solution)/shard_map/ppermute | solution.py:341
  9.7 0.0 collective-permute-done.1.refs_2_.passed.refs_0_
  9.8 3.7 %collective-permute-start.5 = (f32[72,256]{1,0:T(8,128)S(1)}, f32[72,256]{1,0:T(8,128)S(1)}, u32[]{:S(2)}, u32[]{:S(2)}) collective-permute-start(f32[72,256]{1,0:T(8,128)S(1)} %shard_map.49.own.one.refs_0_), channel_id=1, source_target_pairs={{0,12},{1,13},{2,14},{3,15},{4,8},{5,9},{6,10},{7,11},{8,4},{9,5},... | collective-permute-start | bytes 221192 | tf_op jit(solution)/shard_map/ppermute | solution.py:346
  13.4 0.0 collective-permute-start.4
  13.4 0.8 %collective-permute-start.3 = (f32[72,256]{1,0:T(8,128)S(1)}, f32[72,256]{1,0:T(8,128)S(1)}, u32[]{:S(2)}, u32[]{:S(2)}) collective-permute-start(f32[72,256]{1,0:T(8,128)S(1)} %shard_map.49.own.one.refs_0_), channel_id=1, source_target_pairs={{0,4},{1,5},{2,6},{3,7},{4,0},{5,1},{6,2},{7,3},{8,12},{9,13},{10,... | collective-permute-start | bytes 221192 | tf_op jit(solution)/shard_map/ppermute | solution.py:346
  14.2 0.3 shard_map.50
  14.5 0.1 collective-permute-start.6
  14.6 1.2 %shard_map.52.refs_8_ = bf16[1,256,512]{2,1,0:T(8,128)(2,1)S(1)} custom-call(f32[56,256]{1,0:T(8,128)S(1)} %collective-permute-done.1.refs_2_.passed.refs_0_), custom_call_target="tpu_custom_call" | custom-call | flops 134217728 | bytes 262144 | tf_op jit(solution)/shard_map/pallas_call | solution.py:408
  15.8 0.0 collective-permute-done.6.refs_0_
  15.8 1.2 %shard_map.53.refs_9_ = bf16[1,256,512]{2,1,0:T(8,128)(2,1)S(1)} custom-call(f32[56,256]{1,0:T(8,128)S(1)} %collective-permute-done.6.refs_0_), custom_call_target="tpu_custom_call" | custom-call | flops 134217728 | bytes 262144 | tf_op jit(solution)/shard_map/pallas_call | solution.py:408
  17.1 0.0 collective-permute-done.5.one.refs_3_
  17.1 0.3 shard_map.51.refs_5_.refs_7_
  17.4 2.5 %collective-permute-done.4.refs_2_ = f32[72,256]{1,0:T(8,128)S(1)} collective-permute-done((f32[72,256]{1,0:T(8,128)S(1)}, f32[72,256]{1,0:T(8,128)S(1)}, u32[]{:S(2)}, u32[]{:S(2)}) %collective-permute-start.4) | collective-permute-done | bytes 73760 | tf_op jit(solution)/shard_map/ppermute | solution.py:346
  19.9 0.0 collective-permute-done.3.refs_1_
  19.9 1.4 %shard_map.54 = (f32[64,256]{1,0:T(8,128)S(1)}, f32[64,256]{1,0:T(8,128)S(1)}, f32[2,8,512]{2,1,0:T(8,128)S(1)}, bf16[2,512,512]{2,1,0:T(8,128)(2,1)S(1)}, bf16[2,512,512]{2,1,0:T(8,128)(2,1)S(1)}) custom-call(f32[72,256]{1,0:T(8,128)S(1)} %shard_map.49.own.one.refs_0_, f32[72,256]{1,0:T(8,128)S(1)} %collective-permute-done.3.refs_1_, ...), custom_call_target="tpu_custom_call" | custom-call | flops 134217728 | bytes 262144 | tf_op jit(solution)/shard_map/pallas_call | solution.py:455
  21.3 2.5 %collective-permute-start.9 = (f32[64,256]{1,0:T(8,128)S(1)}, f32[64,256]{1,0:T(8,128)S(1)}, u32[]{:S(2)}, u32[]{:S(2)}) collective-permute-start(f32[64,256]{1,0:T(8,128)S(1)} %get-tuple-element.35.refs_0_), channel_id=1, source_target_pairs={{0,12},{1,13},{2,14},{3,15},{4,8},{5,9},{6,10},{7,11},{8,4},{9,5},... | collective-permute-start | bytes 196616 | tf_op jit(solution)/shard_map/ppermute | solution.py:346
  23.8 0.0 collective-permute-start.8
  23.8 1.9 %collective-permute-start.7 = (f32[64,256]{1,0:T(8,128)S(1)}, f32[64,256]{1,0:T(8,128)S(1)}, u32[]{:S(2)}, u32[]{:S(2)}) collective-permute-start(f32[64,256]{1,0:T(8,128)S(1)} %get-tuple-element.35.refs_0_), channel_id=1, source_target_pairs={{0,4},{1,5},{2,6},{3,7},{4,0},{5,1},{6,2},{7,3},{8,12},{9,13},{10,... | collective-permute-start | bytes 196616 | tf_op jit(solution)/shard_map/ppermute | solution.py:346
  25.7 1.3 %shard_map.55 = (bf16[256,8192]{1,0:T(8,128)(2,1)S(1)}, bf16[256,8192]{1,0:T(8,128)(2,1)S(1)}, f32[16,256]{1,0:T(8,128)S(1)}, f32[16,256]{1,0:T(8,128)S(1)}, f32...) custom-call(s32[64,128]{1,0:T(8,128)S(1)} %get-tuple-element.39.mask_ids.refs_5_, f32[64,256]{1,0:T(8,128)S(1)} %get-tuple-element.40.mean), custom_call_target="tpu_custom_call" | custom-call | flops 536870912 | bytes 8388608 | tf_op jit(solution)/shard_map/pallas_call | solution.py:469
  27.0 0.1 collective-permute-start.13
  27.1 1.3 %collective-permute-start.14 = (f32[16,256]{1,0:T(8,128)S(1)}, f32[16,256]{1,0:T(8,128)S(1)}, u32[]{:S(2)}, u32[]{:S(2)}) collective-permute-start(f32[16,256]{1,0:T(8,128)S(1)} %get-tuple-element.48), channel_id=1, source_target_pairs={{0,2},{1,3},{2,0},{3,1},{4,6},{5,7},{6,4},{7,5},{8,10},{9,11},{10,... | collective-permute-start | bytes 49160 | tf_op jit(solution)/shard_map/ppermute | solution.py:341
  28.4 0.0 collective-permute-done.9.refs_3_
  28.4 0.5 %collective-permute-start.15 = (f32[16,256]{1,0:T(8,128)S(1)}, f32[16,256]{1,0:T(8,128)S(1)}, u32[]{:S(2)}, u32[]{:S(2)}) collective-permute-start(f32[16,256]{1,0:T(8,128)S(1)} %get-tuple-element.49), channel_id=1, source_target_pairs={{0,3},{1,2},{2,1},{3,0},{4,7},{5,6},{6,5},{7,4},{8,11},{9,10},{10,... | collective-permute-start | bytes 49160 | tf_op jit(solution)/shard_map/ppermute | solution.py:341
  28.9 1.1 %collective-permute-done.8.refs_2_ = f32[64,256]{1,0:T(8,128)S(1)} collective-permute-done((f32[64,256]{1,0:T(8,128)S(1)}, f32[64,256]{1,0:T(8,128)S(1)}, u32[]{:S(2)}, u32[]{:S(2)}) %collective-permute-start.8) | collective-permute-done | bytes 65568 | tf_op jit(solution)/shard_map/ppermute | solution.py:346
  30.1 0.0 collective-permute-done.7.refs_1_
  30.1 0.8 %shard_map.56 = (f32[16,256]{1,0:T(8,128)S(1)}, f32[16,256]{1,0:T(8,128)S(1)}, f32[16,256]{1,0:T(8,128)S(1)}, f32[16,256]{1,0:T(8,128)S(1)}) custom-call(f32[64,256]{1,0:T(8,128)S(1)} %get-tuple-element.35.refs_0_, f32[64,256]{1,0:T(8,128)S(1)} %collective-permute-done.7.refs_1_, f32[64,256]{1,0:T(8,128)S(1)} %collective-permute-done.8.refs_2_, ...), custom_call_target="tpu_custom_call" | custom-call | flops 134217728 | bytes 262144 | tf_op jit(solution)/shard_map/pallas_call | solution.py:480
  30.8 0.0 collective-permute-start.10
  30.8 1.3 %collective-permute-start.11 = (f32[16,256]{1,0:T(8,128)S(1)}, f32[16,256]{1,0:T(8,128)S(1)}, u32[]{:S(2)}, u32[]{:S(2)}) collective-permute-start(f32[16,256]{1,0:T(8,128)S(1)} %get-tuple-element.44), channel_id=1, source_target_pairs={{0,2},{1,3},{2,0},{3,1},{4,6},{5,7},{6,4},{7,5},{8,10},{9,11},{10,... | collective-permute-start | bytes 49160 | tf_op jit(solution)/shard_map/ppermute | solution.py:341
  32.1 0.0 collective-permute-done.13.refs_1_
  32.1 0.6 %collective-permute-start.12 = (f32[16,256]{1,0:T(8,128)S(1)}, f32[16,256]{1,0:T(8,128)S(1)}, u32[]{:S(2)}, u32[]{:S(2)}) collective-permute-start(f32[16,256]{1,0:T(8,128)S(1)} %get-tuple-element.45), channel_id=1, source_target_pairs={{0,3},{1,2},{2,1},{3,0},{4,7},{5,6},{6,5},{7,4},{8,11},{9,10},{10,... | collective-permute-start | bytes 49160 | tf_op jit(solution)/shard_map/ppermute | solution.py:341
  32.7 0.0 collective-permute-done.14.refs_2_
  32.7 0.0 collective-permute-done.15.refs_3_
  32.7 1.3 %shard_map.57.refs_4_ = f32[64,8192]{1,0:T(8,128)S(1)} custom-call(f32[16,256]{1,0:T(8,128)S(1)} %get-tuple-element.46.refs_0_, f32[16,256]{1,0:T(8,128)S(1)} %collective-permute-done.13.refs_1_, f32[16,256]{1,0:T(8,128)S(1)} %collective-permute-done.14.refs_2_, f32[16,256]{1,0:T(8,128)S(1)} %collective-permute-done.15.refs_3_, ...), custom_call_target="tpu_custom_call" | custom-call | flops 536870912 | bytes 4194304 | tf_op jit(solution)/shard_map/pallas_call | solution.py:490
  34.1 0.0 collective-permute-done.10.refs_1_
  34.1 0.5 %collective-permute-done.11.refs_2_ = f32[16,256]{1,0:T(8,128)S(1)} collective-permute-done((f32[16,256]{1,0:T(8,128)S(1)}, f32[16,256]{1,0:T(8,128)S(1)}, u32[]{:S(2)}, u32[]{:S(2)}) %collective-permute-start.11) | collective-permute-done | bytes 16416 | tf_op jit(solution)/shard_map/ppermute | solution.py:341
  34.6 0.7 %collective-permute-done.12.refs_3_ = f32[16,256]{1,0:T(8,128)S(1)} collective-permute-done((f32[16,256]{1,0:T(8,128)S(1)}, f32[16,256]{1,0:T(8,128)S(1)}, u32[]{:S(2)}, u32[]{:S(2)}) %collective-permute-start.12) | collective-permute-done | bytes 16416 | tf_op jit(solution)/shard_map/ppermute | solution.py:341
  35.3 1.6 %shard_map.58 = f32[64,8192]{1,0:T(8,128)} custom-call(f32[16,256]{1,0:T(8,128)S(1)} %get-tuple-element.42.refs_0_, f32[16,256]{1,0:T(8,128)S(1)} %collective-permute-done.10.refs_1_, f32[16,256]{1,0:T(8,128)S(1)} %collective-permute-done.11.refs_2_, f32[16,256]{1,0:T(8,128)S(1)} %collective-permute-done.12.refs_3_, f32[64,8192]{1,0:T(8,128)S(1)} %shard_map.57.refs_4_, ...), custom_call_target="tpu_custom_call" | custom-call | flops 536870912 | bytes 4194304 | tf_op jit(solution)/shard_map/pallas_call | solution.py:499
  (1 shorter events, 0.0 us)
Async XLA Ops:
  3.4 4.4 %collective-permute-start = (f32[56,256]{1,0:T(8,128)S(1)}, f32[56,256]{1,0:T(8,128)S(1)}, u32[]{:S(2)}, u32[]{:S(2)}) collective-permute-start(f32[56,256]{1,0:T(8,128)S(1)} %get-tuple-element.30), channel_id=1, source_target_pairs={{0,1},{1,0},{2,3},{3,2},{4,5},{5,4},{6,7},{7,6},{8,9},{9,8},{10,11... | collective-permute-start | bytes 172040 | tf_op jit(solution)/shard_map/ppermute | solution.py:341
  3.9 5.8 %collective-permute-start.1 = (f32[56,256]{1,0:T(8,128)S(1)}, f32[56,256]{1,0:T(8,128)S(1)}, u32[]{:S(2)}, u32[]{:S(2)}) collective-permute-start(f32[56,256]{1,0:T(8,128)S(1)} %get-tuple-element.31), channel_id=1, source_target_pairs={{0,2},{1,3},{2,0},{3,1},{4,6},{5,7},{6,4},{7,5},{8,10},{9,11},{10,... | collective-permute-start | bytes 172040 | tf_op jit(solution)/shard_map/ppermute | solution.py:341
  6.5 3.3 %collective-permute-start.2 = (f32[24,256]{1,0:T(8,128)S(1)}, f32[24,256]{1,0:T(8,128)S(1)}, u32[]{:S(2)}, u32[]{:S(2)}) collective-permute-start(f32[24,256]{1,0:T(8,128)S(1)} %get-tuple-element.32), channel_id=1, source_target_pairs={{0,3},{1,2},{2,1},{3,0},{4,7},{5,6},{6,5},{7,4},{8,11},{9,10},{10,... | collective-permute-start | bytes 73736 | tf_op jit(solution)/shard_map/ppermute | solution.py:341
  9.8 7.3 %collective-permute-start.5 = (f32[72,256]{1,0:T(8,128)S(1)}, f32[72,256]{1,0:T(8,128)S(1)}, u32[]{:S(2)}, u32[]{:S(2)}) collective-permute-start(f32[72,256]{1,0:T(8,128)S(1)} %shard_map.49.own.one.refs_0_), channel_id=1, source_target_pairs={{0,12},{1,13},{2,14},{3,15},{4,8},{5,9},{6,10},{7,11},{8,4},{9,5},... | collective-permute-start | bytes 221192 | tf_op jit(solution)/shard_map/ppermute | solution.py:346
  13.4 6.5 %collective-permute-start.4 = (f32[72,256]{1,0:T(8,128)S(1)}, f32[72,256]{1,0:T(8,128)S(1)}, u32[]{:S(2)}, u32[]{:S(2)}) collective-permute-start(f32[72,256]{1,0:T(8,128)S(1)} %shard_map.49.own.one.refs_0_), channel_id=1, source_target_pairs={{0,8},{1,9},{2,10},{3,11},{4,12},{5,13},{6,14},{7,15},{8,0},{9,1},... | collective-permute-start | bytes 221192 | tf_op jit(solution)/shard_map/ppermute | solution.py:346
  13.4 6.5 %collective-permute-start.3 = (f32[72,256]{1,0:T(8,128)S(1)}, f32[72,256]{1,0:T(8,128)S(1)}, u32[]{:S(2)}, u32[]{:S(2)}) collective-permute-start(f32[72,256]{1,0:T(8,128)S(1)} %shard_map.49.own.one.refs_0_), channel_id=1, source_target_pairs={{0,4},{1,5},{2,6},{3,7},{4,0},{5,1},{6,2},{7,3},{8,12},{9,13},{10,... | collective-permute-start | bytes 221192 | tf_op jit(solution)/shard_map/ppermute | solution.py:346
  14.5 1.3 %collective-permute-start.6 = (f32[56,256]{1,0:T(8,128)S(1)}, f32[56,256]{1,0:T(8,128)S(1)}, u32[]{:S(2)}, u32[]{:S(2)}) collective-permute-start(f32[56,256]{1,0:T(8,128)S(1)} %get-tuple-element.34), channel_id=1, source_target_pairs={{0,1},{1,0},{2,3},{3,2},{4,5},{5,4},{6,7},{7,6},{8,9},{9,8},{10,11... | collective-permute-start | bytes 172040 | tf_op jit(solution)/shard_map/ppermute | solution.py:451
  21.3 7.1 %collective-permute-start.9 = (f32[64,256]{1,0:T(8,128)S(1)}, f32[64,256]{1,0:T(8,128)S(1)}, u32[]{:S(2)}, u32[]{:S(2)}) collective-permute-start(f32[64,256]{1,0:T(8,128)S(1)} %get-tuple-element.35.refs_0_), channel_id=1, source_target_pairs={{0,12},{1,13},{2,14},{3,15},{4,8},{5,9},{6,10},{7,11},{8,4},{9,5},... | collective-permute-start | bytes 196616 | tf_op jit(solution)/shard_map/ppermute | solution.py:346
  23.8 6.3 %collective-permute-start.8 = (f32[64,256]{1,0:T(8,128)S(1)}, f32[64,256]{1,0:T(8,128)S(1)}, u32[]{:S(2)}, u32[]{:S(2)}) collective-permute-start(f32[64,256]{1,0:T(8,128)S(1)} %get-tuple-element.35.refs_0_), channel_id=1, source_target_pairs={{0,8},{1,9},{2,10},{3,11},{4,12},{5,13},{6,14},{7,15},{8,0},{9,1},... | collective-permute-start | bytes 196616 | tf_op jit(solution)/shard_map/ppermute | solution.py:346
  23.8 6.3 %collective-permute-start.7 = (f32[64,256]{1,0:T(8,128)S(1)}, f32[64,256]{1,0:T(8,128)S(1)}, u32[]{:S(2)}, u32[]{:S(2)}) collective-permute-start(f32[64,256]{1,0:T(8,128)S(1)} %get-tuple-element.35.refs_0_), channel_id=1, source_target_pairs={{0,4},{1,5},{2,6},{3,7},{4,0},{5,1},{6,2},{7,3},{8,12},{9,13},{10,... | collective-permute-start | bytes 196616 | tf_op jit(solution)/shard_map/ppermute | solution.py:346
  27.0 5.1 %collective-permute-start.13 = (f32[16,256]{1,0:T(8,128)S(1)}, f32[16,256]{1,0:T(8,128)S(1)}, u32[]{:S(2)}, u32[]{:S(2)}) collective-permute-start(f32[16,256]{1,0:T(8,128)S(1)} %get-tuple-element.47), channel_id=1, source_target_pairs={{0,1},{1,0},{2,3},{3,2},{4,5},{5,4},{6,7},{7,6},{8,9},{9,8},{10,11... | collective-permute-start | bytes 49160 | tf_op jit(solution)/shard_map/ppermute | solution.py:341
  27.1 5.7 %collective-permute-start.14 = (f32[16,256]{1,0:T(8,128)S(1)}, f32[16,256]{1,0:T(8,128)S(1)}, u32[]{:S(2)}, u32[]{:S(2)}) collective-permute-start(f32[16,256]{1,0:T(8,128)S(1)} %get-tuple-element.48), channel_id=1, source_target_pairs={{0,2},{1,3},{2,0},{3,1},{4,6},{5,7},{6,4},{7,5},{8,10},{9,11},{10,... | collective-permute-start | bytes 49160 | tf_op jit(solution)/shard_map/ppermute | solution.py:341
  28.4 4.3 %collective-permute-start.15 = (f32[16,256]{1,0:T(8,128)S(1)}, f32[16,256]{1,0:T(8,128)S(1)}, u32[]{:S(2)}, u32[]{:S(2)}) collective-permute-start(f32[16,256]{1,0:T(8,128)S(1)} %get-tuple-element.49), channel_id=1, source_target_pairs={{0,3},{1,2},{2,1},{3,0},{4,7},{5,6},{6,5},{7,4},{8,11},{9,10},{10,... | collective-permute-start | bytes 49160 | tf_op jit(solution)/shard_map/ppermute | solution.py:341
  30.8 3.2 %collective-permute-start.10 = (f32[16,256]{1,0:T(8,128)S(1)}, f32[16,256]{1,0:T(8,128)S(1)}, u32[]{:S(2)}, u32[]{:S(2)}) collective-permute-start(f32[16,256]{1,0:T(8,128)S(1)} %get-tuple-element.43), channel_id=1, source_target_pairs={{0,1},{1,0},{2,3},{3,2},{4,5},{5,4},{6,7},{7,6},{8,9},{9,8},{10,11... | collective-permute-start | bytes 49160 | tf_op jit(solution)/shard_map/ppermute | solution.py:341
  30.8 3.8 %collective-permute-start.11 = (f32[16,256]{1,0:T(8,128)S(1)}, f32[16,256]{1,0:T(8,128)S(1)}, u32[]{:S(2)}, u32[]{:S(2)}) collective-permute-start(f32[16,256]{1,0:T(8,128)S(1)} %get-tuple-element.44), channel_id=1, source_target_pairs={{0,2},{1,3},{2,0},{3,1},{4,6},{5,7},{6,4},{7,5},{8,10},{9,11},{10,... | collective-permute-start | bytes 49160 | tf_op jit(solution)/shard_map/ppermute | solution.py:341
  32.1 3.2 %collective-permute-start.12 = (f32[16,256]{1,0:T(8,128)S(1)}, f32[16,256]{1,0:T(8,128)S(1)}, u32[]{:S(2)}, u32[]{:S(2)}) collective-permute-start(f32[16,256]{1,0:T(8,128)S(1)} %get-tuple-element.45), channel_id=1, source_target_pairs={{0,3},{1,2},{2,1},{3,0},{4,7},{5,6},{6,5},{7,4},{8,11},{9,10},{10,... | collective-permute-start | bytes 49160 | tf_op jit(solution)/shard_map/ppermute | solution.py:341

commit v24 on v23

--- a/solution.py
+++ b/solution.py
@@ -10,6 +10,7 @@
 FIRMS_PER_SHARD = 1024
 LANES = 128
 BLOCK = 1024
+PIECE = 512
 VMEM_BYTES = 32 * 1024 * 1024
 NEAR = 4
 NEAR_STEPS = (0, 1, 2, 3)
@@ -132,14 +133,14 @@
     table = jnp.concatenate([same_worker(pad, 256)] * 2, axis=0)
     wait_all(copies)
     total = None
-    for b in range(len(copies)):
-        ok = row(valid, b, BLOCK)
-        x0 = x[:, b * BLOCK : (b + 1) * BLOCK] * ok
-        rest = x0 - by_worker(x0, table) * row(weight, b, BLOCK)
-        x1[:, b * BLOCK : (b + 1) * BLOCK] = rest
-        counted = jnp.broadcast_to(ok, (16, BLOCK)).astype(BF16)
+    for b in range(x.shape[1] // PIECE):
+        ok = row(valid, b, PIECE)
+        x0 = x[:, b * PIECE : (b + 1) * PIECE] * ok
+        rest = x0 - by_worker(x0, table) * row(weight, b, PIECE)
+        x1[:, b * PIECE : (b + 1) * PIECE] = rest
+        counted = jnp.broadcast_to(ok, (16, PIECE)).astype(BF16)
         data = jnp.concatenate([*split(rest), counted], axis=0)
-        per = BLOCK // LANES
+        per = PIECE // LANES
         block = dot(data, one_hot_down(turned[:, b * per : (b + 1) * per], slots))
         total = block if total is None else total + block
     sums[...] = total[:columns] + total[columns : 2 * columns]
@@ -327,12 +328,13 @@
     outs = column_copies(y, out, sems)
     columns, slots = means.shape
     second = own_means(parts, means)
-    for b in range(len(outs)):
-        at = slice(b * BLOCK, (b + 1) * BLOCK)
-        found = tables[0][:, at] if tables else one_hot(row(mask_ids, b, BLOCK), slots)
+    for b in range(y.shape[1] // PIECE):
+        at = slice(b * PIECE, (b + 1) * PIECE)
+        found = tables[0][:, at] if tables else one_hot(row(mask_ids, b, PIECE), slots)
         spread = dot(second, found)
         y[:, at] = before[:, at] - (spread[:columns] + spread[columns:])
-        outs[b].start()
+        if (b + 1) * PIECE % BLOCK == 0:
+            outs[b * PIECE // BLOCK].start()
     wait_all(outs)
 
 

time: 37 us -> 37.1 us (level)
  no operation moved by 1% of the time
where the time goes in v24:
time: 37.1 us; the launch traced here: 36.9 us
  starting transfers between devices  15.9 us (43%)
  Pallas kernels  15.3 us (41%)
  waiting for transfers between devices  5.61 us (15%)
    ppermute x6, starting transfers between devices, far_share(): return [one] + [lax.ppermute(one, 'rows', step) for step in steps]  8.85 us
    ppermute x9, starting transfers between devices, near_exchange(): lax.ppermute(one, 'rows', step)  6.99 us
    pallas_call x4, Pallas kernels, pair_counts(): call(functools.partial(pairs_kernel, pad, about), array((len(parts), slot...  4.91 us
    ppermute x6, waiting for transfers between devices, far_share(): return [one] + [lax.ppermute(one, 'rows', step) for step in steps]  3.68 us
    pallas_call x1, Pallas kernels, body(): call(functools.partial(sums_kernel, pad, slots // n), [message] * 3 + [ar...  3.38 us
    ppermute x9, waiting for transfers between devices, near_exchange(): lax.ppermute(one, 'rows', step)  1.93 us
    pallas_call x1, Pallas kernels, body(): call(last_kernel, array(whole, F32), [vmem] * (NEAR + 2 + len(spreads[:1]...  1.62 us
    pallas_call x1, Pallas kernels, body(): call(functools.partial(change_kernel, far, part, len(tables)), [of_near,...  1.37 us
  transfers between devices with their start and end apart: 16, of which 5 were waited for; matrix products, arithmetic and copies ran while one was open for 0% of the time, Pallas kernels for 24%

profile of v24, /device:TPU:0, one launch (start us, length us, event | category | flops | bytes accessed | tf_op | source)
XLA Modules:
  0.0 36.9 jit_solution(4568347912935992315)
XLA Ops:
  0.0 3.4 %shard_map.46 = (f32[56,256]{1,0:T(8,128)S(1)}, f32[56,256]{1,0:T(8,128)S(1)}, f32[56,256]{1,0:T(8,128)S(1)}, f32[24,256]{1,0:T(8,128)S(1)}, f32[64,8192]{1,0:T(...) custom-call(f32[64,8192]{1,0:T(8,128)} %refs_0_.1, s32[8,128]{1,0:T(8,128)} %bitcast.4, s32[64,128]{1,0:T(8,128)} %bitcast.3, ...), custom_call_target="tpu_custom_call" | custom-call | flops 1073741824 | bytes 2097152 | tf_op jit(solution)/shard_map/pallas_call | solution.py:390
  3.4 0.5 %collective-permute-start = (f32[56,256]{1,0:T(8,128)S(1)}, f32[56,256]{1,0:T(8,128)S(1)}, u32[]{:S(2)}, u32[]{:S(2)}) collective-permute-start(f32[56,256]{1,0:T(8,128)S(1)} %get-tuple-element.30), channel_id=1, source_target_pairs={{0,1},{1,0},{2,3},{3,2},{4,5},{5,4},{6,7},{7,6},{8,9},{9,8},{10,11... | collective-permute-start | bytes 172040 | tf_op jit(solution)/shard_map/ppermute | solution.py:343
  3.9 2.6 %collective-permute-start.1 = (f32[56,256]{1,0:T(8,128)S(1)}, f32[56,256]{1,0:T(8,128)S(1)}, u32[]{:S(2)}, u32[]{:S(2)}) collective-permute-start(f32[56,256]{1,0:T(8,128)S(1)} %get-tuple-element.31), channel_id=1, source_target_pairs={{0,2},{1,3},{2,0},{3,1},{4,6},{5,7},{6,4},{7,5},{8,10},{9,11},{10,... | collective-permute-start | bytes 172040 | tf_op jit(solution)/shard_map/ppermute | solution.py:343
  6.5 0.1 collective-permute-start.2
  6.6 1.2 %shard_map.47.refs_4_.refs_6_ = bf16[1,256,512]{2,1,0:T(8,128)(2,1)S(1)} custom-call(f32[56,256]{1,0:T(8,128)S(1)} %get-tuple-element.29.refs_0_), custom_call_target="tpu_custom_call" | custom-call | flops 134217728 | bytes 262144 | tf_op jit(solution)/shard_map/pallas_call | solution.py:410
  7.8 0.0 collective-permute-done.refs_0_.refs_1_
  7.8 1.2 %shard_map.48.refs_5_.refs_7_ = bf16[1,256,512]{2,1,0:T(8,128)(2,1)S(1)} custom-call(f32[56,256]{1,0:T(8,128)S(1)} %collective-permute-done.refs_0_.refs_1_), custom_call_target="tpu_custom_call" | custom-call | flops 134217728 | bytes 262144 | tf_op jit(solution)/shard_map/pallas_call | solution.py:410
  9.1 0.7 %collective-permute-done.2.refs_3_ = f32[24,256]{1,0:T(8,128)S(1)} collective-permute-done((f32[24,256]{1,0:T(8,128)S(1)}, f32[24,256]{1,0:T(8,128)S(1)}, u32[]{:S(2)}, u32[]{:S(2)}) %collective-permute-start.2) | collective-permute-done | bytes 24608 | tf_op jit(solution)/shard_map/ppermute | solution.py:343
  9.8 0.0 collective-permute-done.1.refs_2_.passed.refs_0_
  9.8 3.7 %collective-permute-start.5 = (f32[72,256]{1,0:T(8,128)S(1)}, f32[72,256]{1,0:T(8,128)S(1)}, u32[]{:S(2)}, u32[]{:S(2)}) collective-permute-start(f32[72,256]{1,0:T(8,128)S(1)} %shard_map.49.own.one.refs_0_), channel_id=1, source_target_pairs={{0,12},{1,13},{2,14},{3,15},{4,8},{5,9},{6,10},{7,11},{8,4},{9,5},... | collective-permute-start | bytes 221192 | tf_op jit(solution)/shard_map/ppermute | solution.py:348
  13.4 0.0 collective-permute-start.4
  13.4 0.8 %collective-permute-start.3 = (f32[72,256]{1,0:T(8,128)S(1)}, f32[72,256]{1,0:T(8,128)S(1)}, u32[]{:S(2)}, u32[]{:S(2)}) collective-permute-start(f32[72,256]{1,0:T(8,128)S(1)} %shard_map.49.own.one.refs_0_), channel_id=1, source_target_pairs={{0,4},{1,5},{2,6},{3,7},{4,0},{5,1},{6,2},{7,3},{8,12},{9,13},{10,... | collective-permute-start | bytes 221192 | tf_op jit(solution)/shard_map/ppermute | solution.py:348
  14.2 0.3 shard_map.50
  14.5 0.1 collective-permute-start.6
  14.6 1.2 %shard_map.52.refs_8_ = bf16[1,256,512]{2,1,0:T(8,128)(2,1)S(1)} custom-call(f32[56,256]{1,0:T(8,128)S(1)} %collective-permute-done.1.refs_2_.passed.refs_0_), custom_call_target="tpu_custom_call" | custom-call | flops 134217728 | bytes 262144 | tf_op jit(solution)/shard_map/pallas_call | solution.py:410
  15.8 0.0 collective-permute-done.6.refs_0_
  15.9 1.2 %shard_map.53.refs_9_ = bf16[1,256,512]{2,1,0:T(8,128)(2,1)S(1)} custom-call(f32[56,256]{1,0:T(8,128)S(1)} %collective-permute-done.6.refs_0_), custom_call_target="tpu_custom_call" | custom-call | flops 134217728 | bytes 262144 | tf_op jit(solution)/shard_map/pallas_call | solution.py:410
  17.1 0.0 collective-permute-done.5.one.refs_3_
  17.1 0.3 shard_map.51.refs_5_.refs_7_
  17.4 2.5 %collective-permute-done.4.refs_2_ = f32[72,256]{1,0:T(8,128)S(1)} collective-permute-done((f32[72,256]{1,0:T(8,128)S(1)}, f32[72,256]{1,0:T(8,128)S(1)}, u32[]{:S(2)}, u32[]{:S(2)}) %collective-permute-start.4) | collective-permute-done | bytes 73760 | tf_op jit(solution)/shard_map/ppermute | solution.py:348
  19.9 0.0 collective-permute-done.3.refs_1_
  19.9 1.4 %shard_map.54 = (f32[64,256]{1,0:T(8,128)S(1)}, f32[64,256]{1,0:T(8,128)S(1)}, f32[2,8,512]{2,1,0:T(8,128)S(1)}, bf16[2,512,512]{2,1,0:T(8,128)(2,1)S(1)}, bf16[2,512,512]{2,1,0:T(8,128)(2,1)S(1)}) custom-call(f32[72,256]{1,0:T(8,128)S(1)} %shard_map.49.own.one.refs_0_, f32[72,256]{1,0:T(8,128)S(1)} %collective-permute-done.3.refs_1_, ...), custom_call_target="tpu_custom_call" | custom-call | flops 134217728 | bytes 262144 | tf_op jit(solution)/shard_map/pallas_call | solution.py:457
  21.3 2.5 %collective-permute-start.9 = (f32[64,256]{1,0:T(8,128)S(1)}, f32[64,256]{1,0:T(8,128)S(1)}, u32[]{:S(2)}, u32[]{:S(2)}) collective-permute-start(f32[64,256]{1,0:T(8,128)S(1)} %get-tuple-element.35.refs_0_), channel_id=1, source_target_pairs={{0,12},{1,13},{2,14},{3,15},{4,8},{5,9},{6,10},{7,11},{8,4},{9,5},... | collective-permute-start | bytes 196616 | tf_op jit(solution)/shard_map/ppermute | solution.py:348
  23.8 0.0 collective-permute-start.8
  23.8 1.9 %collective-permute-start.7 = (f32[64,256]{1,0:T(8,128)S(1)}, f32[64,256]{1,0:T(8,128)S(1)}, u32[]{:S(2)}, u32[]{:S(2)}) collective-permute-start(f32[64,256]{1,0:T(8,128)S(1)} %get-tuple-element.35.refs_0_), channel_id=1, source_target_pairs={{0,4},{1,5},{2,6},{3,7},{4,0},{5,1},{6,2},{7,3},{8,12},{9,13},{10,... | collective-permute-start | bytes 196616 | tf_op jit(solution)/shard_map/ppermute | solution.py:348
  25.7 1.3 %shard_map.55 = (bf16[256,8192]{1,0:T(8,128)(2,1)S(1)}, bf16[256,8192]{1,0:T(8,128)(2,1)S(1)}, f32[16,256]{1,0:T(8,128)S(1)}, f32[16,256]{1,0:T(8,128)S(1)}, f32...) custom-call(s32[64,128]{1,0:T(8,128)S(1)} %get-tuple-element.39.mask_ids.refs_5_, f32[64,256]{1,0:T(8,128)S(1)} %get-tuple-element.40.mean), custom_call_target="tpu_custom_call" | custom-call | flops 536870912 | bytes 8388608 | tf_op jit(solution)/shard_map/pallas_call | solution.py:471
  27.0 0.1 collective-permute-start.13
  27.1 1.3 %collective-permute-start.14 = (f32[16,256]{1,0:T(8,128)S(1)}, f32[16,256]{1,0:T(8,128)S(1)}, u32[]{:S(2)}, u32[]{:S(2)}) collective-permute-start(f32[16,256]{1,0:T(8,128)S(1)} %get-tuple-element.48), channel_id=1, source_target_pairs={{0,2},{1,3},{2,0},{3,1},{4,6},{5,7},{6,4},{7,5},{8,10},{9,11},{10,... | collective-permute-start | bytes 49160 | tf_op jit(solution)/shard_map/ppermute | solution.py:343
  28.4 0.0 collective-permute-done.9.refs_3_
  28.4 0.5 %collective-permute-start.15 = (f32[16,256]{1,0:T(8,128)S(1)}, f32[16,256]{1,0:T(8,128)S(1)}, u32[]{:S(2)}, u32[]{:S(2)}) collective-permute-start(f32[16,256]{1,0:T(8,128)S(1)} %get-tuple-element.49), channel_id=1, source_target_pairs={{0,3},{1,2},{2,1},{3,0},{4,7},{5,6},{6,5},{7,4},{8,11},{9,10},{10,... | collective-permute-start | bytes 49160 | tf_op jit(solution)/shard_map/ppermute | solution.py:343
  28.9 1.1 %collective-permute-done.8.refs_2_ = f32[64,256]{1,0:T(8,128)S(1)} collective-permute-done((f32[64,256]{1,0:T(8,128)S(1)}, f32[64,256]{1,0:T(8,128)S(1)}, u32[]{:S(2)}, u32[]{:S(2)}) %collective-permute-start.8) | collective-permute-done | bytes 65568 | tf_op jit(solution)/shard_map/ppermute | solution.py:348
  30.1 0.0 collective-permute-done.7.refs_1_
  30.1 0.8 %shard_map.56 = (f32[16,256]{1,0:T(8,128)S(1)}, f32[16,256]{1,0:T(8,128)S(1)}, f32[16,256]{1,0:T(8,128)S(1)}, f32[16,256]{1,0:T(8,128)S(1)}) custom-call(f32[64,256]{1,0:T(8,128)S(1)} %get-tuple-element.35.refs_0_, f32[64,256]{1,0:T(8,128)S(1)} %collective-permute-done.7.refs_1_, f32[64,256]{1,0:T(8,128)S(1)} %collective-permute-done.8.refs_2_, ...), custom_call_target="tpu_custom_call" | custom-call | flops 134217728 | bytes 262144 | tf_op jit(solution)/shard_map/pallas_call | solution.py:482
  30.9 0.0 collective-permute-start.10
  30.9 1.3 %collective-permute-start.11 = (f32[16,256]{1,0:T(8,128)S(1)}, f32[16,256]{1,0:T(8,128)S(1)}, u32[]{:S(2)}, u32[]{:S(2)}) collective-permute-start(f32[16,256]{1,0:T(8,128)S(1)} %get-tuple-element.44), channel_id=1, source_target_pairs={{0,2},{1,3},{2,0},{3,1},{4,6},{5,7},{6,4},{7,5},{8,10},{9,11},{10,... | collective-permute-start | bytes 49160 | tf_op jit(solution)/shard_map/ppermute | solution.py:343
  32.1 0.0 collective-permute-done.13.refs_1_
  32.1 0.6 %collective-permute-start.12 = (f32[16,256]{1,0:T(8,128)S(1)}, f32[16,256]{1,0:T(8,128)S(1)}, u32[]{:S(2)}, u32[]{:S(2)}) collective-permute-start(f32[16,256]{1,0:T(8,128)S(1)} %get-tuple-element.45), channel_id=1, source_target_pairs={{0,3},{1,2},{2,1},{3,0},{4,7},{5,6},{6,5},{7,4},{8,11},{9,10},{10,... | collective-permute-start | bytes 49160 | tf_op jit(solution)/shard_map/ppermute | solution.py:343
  32.7 0.0 collective-permute-done.14.refs_2_
  32.7 0.0 collective-permute-done.15.refs_3_
  32.7 1.3 %shard_map.57.refs_4_ = f32[64,8192]{1,0:T(8,128)S(1)} custom-call(f32[16,256]{1,0:T(8,128)S(1)} %get-tuple-element.46.refs_0_, f32[16,256]{1,0:T(8,128)S(1)} %collective-permute-done.13.refs_1_, f32[16,256]{1,0:T(8,128)S(1)} %collective-permute-done.14.refs_2_, f32[16,256]{1,0:T(8,128)S(1)} %collective-permute-done.15.refs_3_, ...), custom_call_target="tpu_custom_call" | custom-call | flops 536870912 | bytes 4194304 | tf_op jit(solution)/shard_map/pallas_call | solution.py:492
  34.1 0.0 collective-permute-done.10.refs_1_
  34.1 0.6 %collective-permute-done.11.refs_2_ = f32[16,256]{1,0:T(8,128)S(1)} collective-permute-done((f32[16,256]{1,0:T(8,128)S(1)}, f32[16,256]{1,0:T(8,128)S(1)}, u32[]{:S(2)}, u32[]{:S(2)}) %collective-permute-start.11) | collective-permute-done | bytes 16416 | tf_op jit(solution)/shard_map/ppermute | solution.py:343
  34.6 0.7 %collective-permute-done.12.refs_3_ = f32[16,256]{1,0:T(8,128)S(1)} collective-permute-done((f32[16,256]{1,0:T(8,128)S(1)}, f32[16,256]{1,0:T(8,128)S(1)}, u32[]{:S(2)}, u32[]{:S(2)}) %collective-permute-start.12) | collective-permute-done | bytes 16416 | tf_op jit(solution)/shard_map/ppermute | solution.py:343
  35.3 1.6 %shard_map.58 = f32[64,8192]{1,0:T(8,128)} custom-call(f32[16,256]{1,0:T(8,128)S(1)} %get-tuple-element.42.refs_0_, f32[16,256]{1,0:T(8,128)S(1)} %collective-permute-done.10.refs_1_, f32[16,256]{1,0:T(8,128)S(1)} %collective-permute-done.11.refs_2_, f32[16,256]{1,0:T(8,128)S(1)} %collective-permute-done.12.refs_3_, f32[64,8192]{1,0:T(8,128)S(1)} %shard_map.57.refs_4_, ...), custom_call_target="tpu_custom_call" | custom-call | flops 536870912 | bytes 4194304 | tf_op jit(solution)/shard_map/pallas_call | solution.py:501
  (1 shorter events, 0.0 us)
Async XLA Ops:
  3.4 4.4 %collective-permute-start = (f32[56,256]{1,0:T(8,128)S(1)}, f32[56,256]{1,0:T(8,128)S(1)}, u32[]{:S(2)}, u32[]{:S(2)}) collective-permute-start(f32[56,256]{1,0:T(8,128)S(1)} %get-tuple-element.30), channel_id=1, source_target_pairs={{0,1},{1,0},{2,3},{3,2},{4,5},{5,4},{6,7},{7,6},{8,9},{9,8},{10,11... | collective-permute-start | bytes 172040 | tf_op jit(solution)/shard_map/ppermute | solution.py:343
  3.9 5.8 %collective-permute-start.1 = (f32[56,256]{1,0:T(8,128)S(1)}, f32[56,256]{1,0:T(8,128)S(1)}, u32[]{:S(2)}, u32[]{:S(2)}) collective-permute-start(f32[56,256]{1,0:T(8,128)S(1)} %get-tuple-element.31), channel_id=1, source_target_pairs={{0,2},{1,3},{2,0},{3,1},{4,6},{5,7},{6,4},{7,5},{8,10},{9,11},{10,... | collective-permute-start | bytes 172040 | tf_op jit(solution)/shard_map/ppermute | solution.py:343
  6.5 3.3 %collective-permute-start.2 = (f32[24,256]{1,0:T(8,128)S(1)}, f32[24,256]{1,0:T(8,128)S(1)}, u32[]{:S(2)}, u32[]{:S(2)}) collective-permute-start(f32[24,256]{1,0:T(8,128)S(1)} %get-tuple-element.32), channel_id=1, source_target_pairs={{0,3},{1,2},{2,1},{3,0},{4,7},{5,6},{6,5},{7,4},{8,11},{9,10},{10,... | collective-permute-start | bytes 73736 | tf_op jit(solution)/shard_map/ppermute | solution.py:343
  9.8 7.3 %collective-permute-start.5 = (f32[72,256]{1,0:T(8,128)S(1)}, f32[72,256]{1,0:T(8,128)S(1)}, u32[]{:S(2)}, u32[]{:S(2)}) collective-permute-start(f32[72,256]{1,0:T(8,128)S(1)} %shard_map.49.own.one.refs_0_), channel_id=1, source_target_pairs={{0,12},{1,13},{2,14},{3,15},{4,8},{5,9},{6,10},{7,11},{8,4},{9,5},... | collective-permute-start | bytes 221192 | tf_op jit(solution)/shard_map/ppermute | solution.py:348
  13.4 6.5 %collective-permute-start.4 = (f32[72,256]{1,0:T(8,128)S(1)}, f32[72,256]{1,0:T(8,128)S(1)}, u32[]{:S(2)}, u32[]{:S(2)}) collective-permute-start(f32[72,256]{1,0:T(8,128)S(1)} %shard_map.49.own.one.refs_0_), channel_id=1, source_target_pairs={{0,8},{1,9},{2,10},{3,11},{4,12},{5,13},{6,14},{7,15},{8,0},{9,1},... | collective-permute-start | bytes 221192 | tf_op jit(solution)/shard_map/ppermute | solution.py:348
  13.4 6.5 %collective-permute-start.3 = (f32[72,256]{1,0:T(8,128)S(1)}, f32[72,256]{1,0:T(8,128)S(1)}, u32[]{:S(2)}, u32[]{:S(2)}) collective-permute-start(f32[72,256]{1,0:T(8,128)S(1)} %shard_map.49.own.one.refs_0_), channel_id=1, source_target_pairs={{0,4},{1,5},{2,6},{3,7},{4,0},{5,1},{6,2},{7,3},{8,12},{9,13},{10,... | collective-permute-start | bytes 221192 | tf_op jit(solution)/shard_map/ppermute | solution.py:348
  14.5 1.3 %collective-permute-start.6 = (f32[56,256]{1,0:T(8,128)S(1)}, f32[56,256]{1,0:T(8,128)S(1)}, u32[]{:S(2)}, u32[]{:S(2)}) collective-permute-start(f32[56,256]{1,0:T(8,128)S(1)} %get-tuple-element.34), channel_id=1, source_target_pairs={{0,1},{1,0},{2,3},{3,2},{4,5},{5,4},{6,7},{7,6},{8,9},{9,8},{10,11... | collective-permute-start | bytes 172040 | tf_op jit(solution)/shard_map/ppermute | solution.py:453
  21.3 7.1 %collective-permute-start.9 = (f32[64,256]{1,0:T(8,128)S(1)}, f32[64,256]{1,0:T(8,128)S(1)}, u32[]{:S(2)}, u32[]{:S(2)}) collective-permute-start(f32[64,256]{1,0:T(8,128)S(1)} %get-tuple-element.35.refs_0_), channel_id=1, source_target_pairs={{0,12},{1,13},{2,14},{3,15},{4,8},{5,9},{6,10},{7,11},{8,4},{9,5},... | collective-permute-start | bytes 196616 | tf_op jit(solution)/shard_map/ppermute | solution.py:348
  23.8 6.3 %collective-permute-start.8 = (f32[64,256]{1,0:T(8,128)S(1)}, f32[64,256]{1,0:T(8,128)S(1)}, u32[]{:S(2)}, u32[]{:S(2)}) collective-permute-start(f32[64,256]{1,0:T(8,128)S(1)} %get-tuple-element.35.refs_0_), channel_id=1, source_target_pairs={{0,8},{1,9},{2,10},{3,11},{4,12},{5,13},{6,14},{7,15},{8,0},{9,1},... | collective-permute-start | bytes 196616 | tf_op jit(solution)/shard_map/ppermute | solution.py:348
  23.8 6.3 %collective-permute-start.7 = (f32[64,256]{1,0:T(8,128)S(1)}, f32[64,256]{1,0:T(8,128)S(1)}, u32[]{:S(2)}, u32[]{:S(2)}) collective-permute-start(f32[64,256]{1,0:T(8,128)S(1)} %get-tuple-element.35.refs_0_), channel_id=1, source_target_pairs={{0,4},{1,5},{2,6},{3,7},{4,0},{5,1},{6,2},{7,3},{8,12},{9,13},{10,... | collective-permute-start | bytes 196616 | tf_op jit(solution)/shard_map/ppermute | solution.py:348
  27.0 5.1 %collective-permute-start.13 = (f32[16,256]{1,0:T(8,128)S(1)}, f32[16,256]{1,0:T(8,128)S(1)}, u32[]{:S(2)}, u32[]{:S(2)}) collective-permute-start(f32[16,256]{1,0:T(8,128)S(1)} %get-tuple-element.47), channel_id=1, source_target_pairs={{0,1},{1,0},{2,3},{3,2},{4,5},{5,4},{6,7},{7,6},{8,9},{9,8},{10,11... | collective-permute-start | bytes 49160 | tf_op jit(solution)/shard_map/ppermute | solution.py:343
  27.1 5.7 %collective-permute-start.14 = (f32[16,256]{1,0:T(8,128)S(1)}, f32[16,256]{1,0:T(8,128)S(1)}, u32[]{:S(2)}, u32[]{:S(2)}) collective-permute-start(f32[16,256]{1,0:T(8,128)S(1)} %get-tuple-element.48), channel_id=1, source_target_pairs={{0,2},{1,3},{2,0},{3,1},{4,6},{5,7},{6,4},{7,5},{8,10},{9,11},{10,... | collective-permute-start | bytes 49160 | tf_op jit(solution)/shard_map/ppermute | solution.py:343
  28.4 4.3 %collective-permute-start.15 = (f32[16,256]{1,0:T(8,128)S(1)}, f32[16,256]{1,0:T(8,128)S(1)}, u32[]{:S(2)}, u32[]{:S(2)}) collective-permute-start(f32[16,256]{1,0:T(8,128)S(1)} %get-tuple-element.49), channel_id=1, source_target_pairs={{0,3},{1,2},{2,1},{3,0},{4,7},{5,6},{6,5},{7,4},{8,11},{9,10},{10,... | collective-permute-start | bytes 49160 | tf_op jit(solution)/shard_map/ppermute | solution.py:343
  30.9 3.2 %collective-permute-start.10 = (f32[16,256]{1,0:T(8,128)S(1)}, f32[16,256]{1,0:T(8,128)S(1)}, u32[]{:S(2)}, u32[]{:S(2)}) collective-permute-start(f32[16,256]{1,0:T(8,128)S(1)} %get-tuple-element.43), channel_id=1, source_target_pairs={{0,1},{1,0},{2,3},{3,2},{4,5},{5,4},{6,7},{7,6},{8,9},{9,8},{10,11... | collective-permute-start | bytes 49160 | tf_op jit(solution)/shard_map/ppermute | solution.py:343
  30.9 3.8 %collective-permute-start.11 = (f32[16,256]{1,0:T(8,128)S(1)}, f32[16,256]{1,0:T(8,128)S(1)}, u32[]{:S(2)}, u32[]{:S(2)}) collective-permute-start(f32[16,256]{1,0:T(8,128)S(1)} %get-tuple-element.44), channel_id=1, source_target_pairs={{0,2},{1,3},{2,0},{3,1},{4,6},{5,7},{6,4},{7,5},{8,10},{9,11},{10,... | collective-permute-start | bytes 49160 | tf_op jit(solution)/shard_map/ppermute | solution.py:343
  32.1 3.2 %collective-permute-start.12 = (f32[16,256]{1,0:T(8,128)S(1)}, f32[16,256]{1,0:T(8,128)S(1)}, u32[]{:S(2)}, u32[]{:S(2)}) collective-permute-start(f32[16,256]{1,0:T(8,128)S(1)} %get-tuple-element.45), channel_id=1, source_target_pairs={{0,3},{1,2},{2,1},{3,0},{4,7},{5,6},{6,5},{7,4},{8,11},{9,10},{10,... | collective-permute-start | bytes 49160 | tf_op jit(solution)/shard_map/ppermute | solution.py:343

commit v25 on v23

--- a/solution.py
+++ b/solution.py
@@ -342,7 +342,8 @@
 
 
 def far_share(one, n):
-    steps = [[(i, i ^ (k * NEAR)) for i in range(n)] for k in range(1, n // NEAR)]
+    order = sorted(range(1, n // NEAR), key=lambda k: k == 2)
+    steps = [[(i, i ^ (k * NEAR)) for i in range(n)] for k in order]
     return [one] + [lax.ppermute(one, "rows", step) for step in steps]
 
 

time: 37 us -> 37.1 us (level)
  waiting for transfers between devices: 5.59 us -> 6.55 us
  starting transfers between devices: 15.9 us -> 15 us
    ppermute x6, waiting for transfers between devices: 3.66 us -> 4.62 us  [far_share(): return [one] + [lax.ppermute(one, 'rows', step) for step in steps]]
    ppermute x6, starting transfers between devices: 8.85 us -> 8.12 us  [far_share(): return [one] + [lax.ppermute(one, 'rows', step) for step in steps]]
  transfers between devices with their start and end apart: 16 -> 16, of which waited for: 5 -> 8; matrix products, arithmetic and copies ran while one was open for 0% -> 0% of each run, Pallas kernels for 24% -> 24%
where the time goes in v25:
time: 37.1 us; the launch traced here: 36.9 us
  Pallas kernels  15.2 us (41%)
  starting transfers between devices  15 us (40%)
  waiting for transfers between devices  6.55 us (18%)
    ppermute x6, starting transfers between devices, far_share(): return [one] + [lax.ppermute(one, 'rows', step) for step in steps]  8.12 us
    ppermute x9, starting transfers between devices, near_exchange(): lax.ppermute(one, 'rows', step)  6.83 us
    pallas_call x4, Pallas kernels, pair_counts(): call(functools.partial(pairs_kernel, pad, about), array((len(parts), slot...  4.92 us
    ppermute x6, waiting for transfers between devices, far_share(): return [one] + [lax.ppermute(one, 'rows', step) for step in steps]  4.62 us
    pallas_call x1, Pallas kernels, body(): call(functools.partial(sums_kernel, pad, slots // n), [message] * 3 + [ar...  3.37 us
    ppermute x9, waiting for transfers between devices, near_exchange(): lax.ppermute(one, 'rows', step)  1.93 us
    pallas_call x1, Pallas kernels, body(): call(last_kernel, array(whole, F32), [vmem] * (NEAR + 2 + len(spreads[:1]...  1.61 us
    pallas_call x1, Pallas kernels, body(): call(functools.partial(change_kernel, far, part, len(tables)), [of_near,...  1.36 us
  transfers between devices with their start and end apart: 16, of which 8 were waited for; matrix products, arithmetic and copies ran while one was open for 0% of the time, Pallas kernels for 24%

profile of v25, /device:TPU:0, one launch (start us, length us, event | category | flops | bytes accessed | tf_op | source)
XLA Modules:
  0.0 36.9 jit_solution(14224648723733176456)
XLA Ops:
  0.0 3.4 %shard_map.46 = (f32[56,256]{1,0:T(8,128)S(1)}, f32[56,256]{1,0:T(8,128)S(1)}, f32[56,256]{1,0:T(8,128)S(1)}, f32[24,256]{1,0:T(8,128)S(1)}, f32[64,8192]{1,0:T(...) custom-call(f32[64,8192]{1,0:T(8,128)} %refs_0_.1, s32[8,128]{1,0:T(8,128)} %bitcast.4, s32[64,128]{1,0:T(8,128)} %bitcast.3, ...), custom_call_target="tpu_custom_call" | custom-call | flops 1073741824 | bytes 2097152 | tf_op jit(solution)/shard_map/pallas_call | solution.py:389
  3.4 0.5 %collective-permute-start = (f32[56,256]{1,0:T(8,128)S(1)}, f32[56,256]{1,0:T(8,128)S(1)}, u32[]{:S(2)}, u32[]{:S(2)}) collective-permute-start(f32[56,256]{1,0:T(8,128)S(1)} %get-tuple-element.30), channel_id=1, source_target_pairs={{0,1},{1,0},{2,3},{3,2},{4,5},{5,4},{6,7},{7,6},{8,9},{9,8},{10,11... | collective-permute-start | bytes 172040 | tf_op jit(solution)/shard_map/ppermute | solution.py:341
  3.9 2.6 %collective-permute-start.1 = (f32[56,256]{1,0:T(8,128)S(1)}, f32[56,256]{1,0:T(8,128)S(1)}, u32[]{:S(2)}, u32[]{:S(2)}) collective-permute-start(f32[56,256]{1,0:T(8,128)S(1)} %get-tuple-element.31), channel_id=1, source_target_pairs={{0,2},{1,3},{2,0},{3,1},{4,6},{5,7},{6,4},{7,5},{8,10},{9,11},{10,... | collective-permute-start | bytes 172040 | tf_op jit(solution)/shard_map/ppermute | solution.py:341
  6.5 0.1 collective-permute-start.2
  6.6 1.2 %shard_map.47.refs_4_.refs_6_ = bf16[1,256,512]{2,1,0:T(8,128)(2,1)S(1)} custom-call(f32[56,256]{1,0:T(8,128)S(1)} %get-tuple-element.29.refs_0_), custom_call_target="tpu_custom_call" | custom-call | flops 134217728 | bytes 262144 | tf_op jit(solution)/shard_map/pallas_call | solution.py:409
  7.8 0.0 collective-permute-done.refs_0_.refs_1_
  7.8 1.2 %shard_map.48.refs_5_.refs_7_ = bf16[1,256,512]{2,1,0:T(8,128)(2,1)S(1)} custom-call(f32[56,256]{1,0:T(8,128)S(1)} %collective-permute-done.refs_0_.refs_1_), custom_call_target="tpu_custom_call" | custom-call | flops 134217728 | bytes 262144 | tf_op jit(solution)/shard_map/pallas_call | solution.py:409
  9.0 0.7 %collective-permute-done.2.refs_3_ = f32[24,256]{1,0:T(8,128)S(1)} collective-permute-done((f32[24,256]{1,0:T(8,128)S(1)}, f32[24,256]{1,0:T(8,128)S(1)}, u32[]{:S(2)}, u32[]{:S(2)}) %collective-permute-start.2) | collective-permute-done | bytes 24608 | tf_op jit(solution)/shard_map/ppermute | solution.py:341
  9.7 0.0 collective-permute-done.1.refs_2_.passed.refs_0_
  9.8 2.7 %collective-permute-start.5 = (f32[72,256]{1,0:T(8,128)S(1)}, f32[72,256]{1,0:T(8,128)S(1)}, u32[]{:S(2)}, u32[]{:S(2)}) collective-permute-start(f32[72,256]{1,0:T(8,128)S(1)} %shard_map.49.own.one.refs_0_), channel_id=1, source_target_pairs={{0,8},{1,9},{2,10},{3,11},{4,12},{5,13},{6,14},{7,15},{8,0},{9,1},... | collective-permute-start | bytes 221192 | tf_op jit(solution)/shard_map/ppermute | solution.py:347
  12.4 1.3 %collective-permute-start.4 = (f32[72,256]{1,0:T(8,128)S(1)}, f32[72,256]{1,0:T(8,128)S(1)}, u32[]{:S(2)}, u32[]{:S(2)}) collective-permute-start(f32[72,256]{1,0:T(8,128)S(1)} %shard_map.49.own.one.refs_0_), channel_id=1, source_target_pairs={{0,12},{1,13},{2,14},{3,15},{4,8},{5,9},{6,10},{7,11},{8,4},{9,5},... | collective-permute-start | bytes 221192 | tf_op jit(solution)/shard_map/ppermute | solution.py:347
  13.8 0.2 collective-permute-start.3
  14.0 0.3 shard_map.50
  14.3 0.1 collective-permute-start.6
  14.4 1.2 %shard_map.52.refs_8_ = bf16[1,256,512]{2,1,0:T(8,128)(2,1)S(1)} custom-call(f32[56,256]{1,0:T(8,128)S(1)} %collective-permute-done.1.refs_2_.passed.refs_0_), custom_call_target="tpu_custom_call" | custom-call | flops 134217728 | bytes 262144 | tf_op jit(solution)/shard_map/pallas_call | solution.py:409
  15.6 0.0 collective-permute-done.6.refs_0_
  15.6 1.2 %shard_map.53.refs_9_ = bf16[1,256,512]{2,1,0:T(8,128)(2,1)S(1)} custom-call(f32[56,256]{1,0:T(8,128)S(1)} %collective-permute-done.6.refs_0_), custom_call_target="tpu_custom_call" | custom-call | flops 134217728 | bytes 262144 | tf_op jit(solution)/shard_map/pallas_call | solution.py:409
  16.9 1.2 %collective-permute-done.5.one.refs_3_ = f32[72,256]{1,0:T(8,128)S(1)} collective-permute-done((f32[72,256]{1,0:T(8,128)S(1)}, f32[72,256]{1,0:T(8,128)S(1)}, u32[]{:S(2)}, u32[]{:S(2)}) %collective-permute-start.5) | collective-permute-done | bytes 73760 | tf_op jit(solution)/shard_map/ppermute | solution.py:347
  18.1 0.3 shard_map.51.refs_5_.refs_7_
  18.4 0.7 %collective-permute-done.4.refs_2_ = f32[72,256]{1,0:T(8,128)S(1)} collective-permute-done((f32[72,256]{1,0:T(8,128)S(1)}, f32[72,256]{1,0:T(8,128)S(1)}, u32[]{:S(2)}, u32[]{:S(2)}) %collective-permute-start.4) | collective-permute-done | bytes 73760 | tf_op jit(solution)/shard_map/ppermute | solution.py:347
  19.1 0.5 %collective-permute-done.3.refs_1_ = f32[72,256]{1,0:T(8,128)S(1)} collective-permute-done((f32[72,256]{1,0:T(8,128)S(1)}, f32[72,256]{1,0:T(8,128)S(1)}, u32[]{:S(2)}, u32[]{:S(2)}) %collective-permute-start.3) | collective-permute-done | bytes 73760 | tf_op jit(solution)/shard_map/ppermute | solution.py:347
  19.6 1.4 %shard_map.54 = (f32[64,256]{1,0:T(8,128)S(1)}, f32[64,256]{1,0:T(8,128)S(1)}, f32[2,8,512]{2,1,0:T(8,128)S(1)}, bf16[2,512,512]{2,1,0:T(8,128)(2,1)S(1)}, bf16[2,512,512]{2,1,0:T(8,128)(2,1)S(1)}) custom-call(f32[72,256]{1,0:T(8,128)S(1)} %shard_map.49.own.one.refs_0_, f32[72,256]{1,0:T(8,128)S(1)} %collective-permute-done.3.refs_1_, ...), custom_call_target="tpu_custom_call" | custom-call | flops 134217728 | bytes 262144 | tf_op jit(solution)/shard_map/pallas_call | solution.py:456
  21.0 2.8 %collective-permute-start.9 = (f32[64,256]{1,0:T(8,128)S(1)}, f32[64,256]{1,0:T(8,128)S(1)}, u32[]{:S(2)}, u32[]{:S(2)}) collective-permute-start(f32[64,256]{1,0:T(8,128)S(1)} %get-tuple-element.35.refs_0_), channel_id=1, source_target_pairs={{0,8},{1,9},{2,10},{3,11},{4,12},{5,13},{6,14},{7,15},{8,0},{9,1},... | collective-permute-start | bytes 196616 | tf_op jit(solution)/shard_map/ppermute | solution.py:347
  23.8 0.6 %collective-permute-start.8 = (f32[64,256]{1,0:T(8,128)S(1)}, f32[64,256]{1,0:T(8,128)S(1)}, u32[]{:S(2)}, u32[]{:S(2)}) collective-permute-start(f32[64,256]{1,0:T(8,128)S(1)} %get-tuple-element.35.refs_0_), channel_id=1, source_target_pairs={{0,12},{1,13},{2,14},{3,15},{4,8},{5,9},{6,10},{7,11},{8,4},{9,5},... | collective-permute-start | bytes 196616 | tf_op jit(solution)/shard_map/ppermute | solution.py:347
  24.4 0.5 %collective-permute-start.7 = (f32[64,256]{1,0:T(8,128)S(1)}, f32[64,256]{1,0:T(8,128)S(1)}, u32[]{:S(2)}, u32[]{:S(2)}) collective-permute-start(f32[64,256]{1,0:T(8,128)S(1)} %get-tuple-element.35.refs_0_), channel_id=1, source_target_pairs={{0,4},{1,5},{2,6},{3,7},{4,0},{5,1},{6,2},{7,3},{8,12},{9,13},{10,... | collective-permute-start | bytes 196616 | tf_op jit(solution)/shard_map/ppermute | solution.py:347
  24.9 1.3 %shard_map.55 = (bf16[256,8192]{1,0:T(8,128)(2,1)S(1)}, bf16[256,8192]{1,0:T(8,128)(2,1)S(1)}, f32[16,256]{1,0:T(8,128)S(1)}, f32[16,256]{1,0:T(8,128)S(1)}, f32...) custom-call(s32[64,128]{1,0:T(8,128)S(1)} %get-tuple-element.39.mask_ids.refs_5_, f32[64,256]{1,0:T(8,128)S(1)} %get-tuple-element.40.mean), custom_call_target="tpu_custom_call" | custom-call | flops 536870912 | bytes 8388608 | tf_op jit(solution)/shard_map/pallas_call | solution.py:470
  26.2 0.1 collective-permute-start.13
  26.2 1.3 %collective-permute-start.14 = (f32[16,256]{1,0:T(8,128)S(1)}, f32[16,256]{1,0:T(8,128)S(1)}, u32[]{:S(2)}, u32[]{:S(2)}) collective-permute-start(f32[16,256]{1,0:T(8,128)S(1)} %get-tuple-element.48), channel_id=1, source_target_pairs={{0,2},{1,3},{2,0},{3,1},{4,6},{5,7},{6,4},{7,5},{8,10},{9,11},{10,... | collective-permute-start | bytes 49160 | tf_op jit(solution)/shard_map/ppermute | solution.py:341
  27.5 0.3 collective-permute-done.9.refs_3_
  27.8 0.4 %collective-permute-start.15 = (f32[16,256]{1,0:T(8,128)S(1)}, f32[16,256]{1,0:T(8,128)S(1)}, u32[]{:S(2)}, u32[]{:S(2)}) collective-permute-start(f32[16,256]{1,0:T(8,128)S(1)} %get-tuple-element.49), channel_id=1, source_target_pairs={{0,3},{1,2},{2,1},{3,0},{4,7},{5,6},{6,5},{7,4},{8,11},{9,10},{10,... | collective-permute-start | bytes 49160 | tf_op jit(solution)/shard_map/ppermute | solution.py:341
  28.2 1.9 %collective-permute-done.8.refs_2_ = f32[64,256]{1,0:T(8,128)S(1)} collective-permute-done((f32[64,256]{1,0:T(8,128)S(1)}, f32[64,256]{1,0:T(8,128)S(1)}, u32[]{:S(2)}, u32[]{:S(2)}) %collective-permute-start.8) | collective-permute-done | bytes 65568 | tf_op jit(solution)/shard_map/ppermute | solution.py:347
  30.1 0.0 collective-permute-done.7.refs_1_
  30.1 0.8 %shard_map.56 = (f32[16,256]{1,0:T(8,128)S(1)}, f32[16,256]{1,0:T(8,128)S(1)}, f32[16,256]{1,0:T(8,128)S(1)}, f32[16,256]{1,0:T(8,128)S(1)}) custom-call(f32[64,256]{1,0:T(8,128)S(1)} %get-tuple-element.35.refs_0_, f32[64,256]{1,0:T(8,128)S(1)} %collective-permute-done.7.refs_1_, f32[64,256]{1,0:T(8,128)S(1)} %collective-permute-done.8.refs_2_, ...), custom_call_target="tpu_custom_call" | custom-call | flops 134217728 | bytes 262144 | tf_op jit(solution)/shard_map/pallas_call | solution.py:481
  30.9 0.0 collective-permute-start.10
  30.9 1.3 %collective-permute-start.11 = (f32[16,256]{1,0:T(8,128)S(1)}, f32[16,256]{1,0:T(8,128)S(1)}, u32[]{:S(2)}, u32[]{:S(2)}) collective-permute-start(f32[16,256]{1,0:T(8,128)S(1)} %get-tuple-element.44), channel_id=1, source_target_pairs={{0,2},{1,3},{2,0},{3,1},{4,6},{5,7},{6,4},{7,5},{8,10},{9,11},{10,... | collective-permute-start | bytes 49160 | tf_op jit(solution)/shard_map/ppermute | solution.py:341
  32.2 0.0 collective-permute-done.13.refs_1_
  32.2 0.6 %collective-permute-start.12 = (f32[16,256]{1,0:T(8,128)S(1)}, f32[16,256]{1,0:T(8,128)S(1)}, u32[]{:S(2)}, u32[]{:S(2)}) collective-permute-start(f32[16,256]{1,0:T(8,128)S(1)} %get-tuple-element.45), channel_id=1, source_target_pairs={{0,3},{1,2},{2,1},{3,0},{4,7},{5,6},{6,5},{7,4},{8,11},{9,10},{10,... | collective-permute-start | bytes 49160 | tf_op jit(solution)/shard_map/ppermute | solution.py:341
  32.8 0.0 collective-permute-done.14.refs_2_
  32.8 0.0 collective-permute-done.15.refs_3_
  32.8 1.3 %shard_map.57.refs_4_ = f32[64,8192]{1,0:T(8,128)S(1)} custom-call(f32[16,256]{1,0:T(8,128)S(1)} %get-tuple-element.46.refs_0_, f32[16,256]{1,0:T(8,128)S(1)} %collective-permute-done.13.refs_1_, f32[16,256]{1,0:T(8,128)S(1)} %collective-permute-done.14.refs_2_, f32[16,256]{1,0:T(8,128)S(1)} %collective-permute-done.15.refs_3_, ...), custom_call_target="tpu_custom_call" | custom-call | flops 536870912 | bytes 4194304 | tf_op jit(solution)/shard_map/pallas_call | solution.py:491
  34.1 0.0 collective-permute-done.10.refs_1_
  34.1 0.6 %collective-permute-done.11.refs_2_ = f32[16,256]{1,0:T(8,128)S(1)} collective-permute-done((f32[16,256]{1,0:T(8,128)S(1)}, f32[16,256]{1,0:T(8,128)S(1)}, u32[]{:S(2)}, u32[]{:S(2)}) %collective-permute-start.11) | collective-permute-done | bytes 16416 | tf_op jit(solution)/shard_map/ppermute | solution.py:341
  34.7 0.7 %collective-permute-done.12.refs_3_ = f32[16,256]{1,0:T(8,128)S(1)} collective-permute-done((f32[16,256]{1,0:T(8,128)S(1)}, f32[16,256]{1,0:T(8,128)S(1)}, u32[]{:S(2)}, u32[]{:S(2)}) %collective-permute-start.12) | collective-permute-done | bytes 16416 | tf_op jit(solution)/shard_map/ppermute | solution.py:341
  35.3 1.6 %shard_map.58 = f32[64,8192]{1,0:T(8,128)} custom-call(f32[16,256]{1,0:T(8,128)S(1)} %get-tuple-element.42.refs_0_, f32[16,256]{1,0:T(8,128)S(1)} %collective-permute-done.10.refs_1_, f32[16,256]{1,0:T(8,128)S(1)} %collective-permute-done.11.refs_2_, f32[16,256]{1,0:T(8,128)S(1)} %collective-permute-done.12.refs_3_, f32[64,8192]{1,0:T(8,128)S(1)} %shard_map.57.refs_4_, ...), custom_call_target="tpu_custom_call" | custom-call | flops 536870912 | bytes 4194304 | tf_op jit(solution)/shard_map/pallas_call | solution.py:500
  (1 shorter events, 0.0 us)
Async XLA Ops:
  3.4 4.4 %collective-permute-start = (f32[56,256]{1,0:T(8,128)S(1)}, f32[56,256]{1,0:T(8,128)S(1)}, u32[]{:S(2)}, u32[]{:S(2)}) collective-permute-start(f32[56,256]{1,0:T(8,128)S(1)} %get-tuple-element.30), channel_id=1, source_target_pairs={{0,1},{1,0},{2,3},{3,2},{4,5},{5,4},{6,7},{7,6},{8,9},{9,8},{10,11... | collective-permute-start | bytes 172040 | tf_op jit(solution)/shard_map/ppermute | solution.py:341
  3.9 5.8 %collective-permute-start.1 = (f32[56,256]{1,0:T(8,128)S(1)}, f32[56,256]{1,0:T(8,128)S(1)}, u32[]{:S(2)}, u32[]{:S(2)}) collective-permute-start(f32[56,256]{1,0:T(8,128)S(1)} %get-tuple-element.31), channel_id=1, source_target_pairs={{0,2},{1,3},{2,0},{3,1},{4,6},{5,7},{6,4},{7,5},{8,10},{9,11},{10,... | collective-permute-start | bytes 172040 | tf_op jit(solution)/shard_map/ppermute | solution.py:341
  6.5 3.3 %collective-permute-start.2 = (f32[24,256]{1,0:T(8,128)S(1)}, f32[24,256]{1,0:T(8,128)S(1)}, u32[]{:S(2)}, u32[]{:S(2)}) collective-permute-start(f32[24,256]{1,0:T(8,128)S(1)} %get-tuple-element.32), channel_id=1, source_target_pairs={{0,3},{1,2},{2,1},{3,0},{4,7},{5,6},{6,5},{7,4},{8,11},{9,10},{10,... | collective-permute-start | bytes 73736 | tf_op jit(solution)/shard_map/ppermute | solution.py:341
  9.8 8.3 %collective-permute-start.5 = (f32[72,256]{1,0:T(8,128)S(1)}, f32[72,256]{1,0:T(8,128)S(1)}, u32[]{:S(2)}, u32[]{:S(2)}) collective-permute-start(f32[72,256]{1,0:T(8,128)S(1)} %shard_map.49.own.one.refs_0_), channel_id=1, source_target_pairs={{0,8},{1,9},{2,10},{3,11},{4,12},{5,13},{6,14},{7,15},{8,0},{9,1},... | collective-permute-start | bytes 221192 | tf_op jit(solution)/shard_map/ppermute | solution.py:347
  12.4 6.7 %collective-permute-start.4 = (f32[72,256]{1,0:T(8,128)S(1)}, f32[72,256]{1,0:T(8,128)S(1)}, u32[]{:S(2)}, u32[]{:S(2)}) collective-permute-start(f32[72,256]{1,0:T(8,128)S(1)} %shard_map.49.own.one.refs_0_), channel_id=1, source_target_pairs={{0,12},{1,13},{2,14},{3,15},{4,8},{5,9},{6,10},{7,11},{8,4},{9,5},... | collective-permute-start | bytes 221192 | tf_op jit(solution)/shard_map/ppermute | solution.py:347
  13.8 5.9 %collective-permute-start.3 = (f32[72,256]{1,0:T(8,128)S(1)}, f32[72,256]{1,0:T(8,128)S(1)}, u32[]{:S(2)}, u32[]{:S(2)}) collective-permute-start(f32[72,256]{1,0:T(8,128)S(1)} %shard_map.49.own.one.refs_0_), channel_id=1, source_target_pairs={{0,4},{1,5},{2,6},{3,7},{4,0},{5,1},{6,2},{7,3},{8,12},{9,13},{10,... | collective-permute-start | bytes 221192 | tf_op jit(solution)/shard_map/ppermute | solution.py:347
  14.3 1.3 %collective-permute-start.6 = (f32[56,256]{1,0:T(8,128)S(1)}, f32[56,256]{1,0:T(8,128)S(1)}, u32[]{:S(2)}, u32[]{:S(2)}) collective-permute-start(f32[56,256]{1,0:T(8,128)S(1)} %get-tuple-element.34), channel_id=1, source_target_pairs={{0,1},{1,0},{2,3},{3,2},{4,5},{5,4},{6,7},{7,6},{8,9},{9,8},{10,11... | collective-permute-start | bytes 172040 | tf_op jit(solution)/shard_map/ppermute | solution.py:452
  21.0 6.8 %collective-permute-start.9 = (f32[64,256]{1,0:T(8,128)S(1)}, f32[64,256]{1,0:T(8,128)S(1)}, u32[]{:S(2)}, u32[]{:S(2)}) collective-permute-start(f32[64,256]{1,0:T(8,128)S(1)} %get-tuple-element.35.refs_0_), channel_id=1, source_target_pairs={{0,8},{1,9},{2,10},{3,11},{4,12},{5,13},{6,14},{7,15},{8,0},{9,1},... | collective-permute-start | bytes 196616 | tf_op jit(solution)/shard_map/ppermute | solution.py:347
  23.8 6.3 %collective-permute-start.8 = (f32[64,256]{1,0:T(8,128)S(1)}, f32[64,256]{1,0:T(8,128)S(1)}, u32[]{:S(2)}, u32[]{:S(2)}) collective-permute-start(f32[64,256]{1,0:T(8,128)S(1)} %get-tuple-element.35.refs_0_), channel_id=1, source_target_pairs={{0,12},{1,13},{2,14},{3,15},{4,8},{5,9},{6,10},{7,11},{8,4},{9,5},... | collective-permute-start | bytes 196616 | tf_op jit(solution)/shard_map/ppermute | solution.py:347
  24.4 5.8 %collective-permute-start.7 = (f32[64,256]{1,0:T(8,128)S(1)}, f32[64,256]{1,0:T(8,128)S(1)}, u32[]{:S(2)}, u32[]{:S(2)}) collective-permute-start(f32[64,256]{1,0:T(8,128)S(1)} %get-tuple-element.35.refs_0_), channel_id=1, source_target_pairs={{0,4},{1,5},{2,6},{3,7},{4,0},{5,1},{6,2},{7,3},{8,12},{9,13},{10,... | collective-permute-start | bytes 196616 | tf_op jit(solution)/shard_map/ppermute | solution.py:347
  26.2 6.0 %collective-permute-start.13 = (f32[16,256]{1,0:T(8,128)S(1)}, f32[16,256]{1,0:T(8,128)S(1)}, u32[]{:S(2)}, u32[]{:S(2)}) collective-permute-start(f32[16,256]{1,0:T(8,128)S(1)} %get-tuple-element.47), channel_id=1, source_target_pairs={{0,1},{1,0},{2,3},{3,2},{4,5},{5,4},{6,7},{7,6},{8,9},{9,8},{10,11... | collective-permute-start | bytes 49160 | tf_op jit(solution)/shard_map/ppermute | solution.py:341
  26.2 6.5 %collective-permute-start.14 = (f32[16,256]{1,0:T(8,128)S(1)}, f32[16,256]{1,0:T(8,128)S(1)}, u32[]{:S(2)}, u32[]{:S(2)}) collective-permute-start(f32[16,256]{1,0:T(8,128)S(1)} %get-tuple-element.48), channel_id=1, source_target_pairs={{0,2},{1,3},{2,0},{3,1},{4,6},{5,7},{6,4},{7,5},{8,10},{9,11},{10,... | collective-permute-start | bytes 49160 | tf_op jit(solution)/shard_map/ppermute | solution.py:341
  27.8 5.0 %collective-permute-start.15 = (f32[16,256]{1,0:T(8,128)S(1)}, f32[16,256]{1,0:T(8,128)S(1)}, u32[]{:S(2)}, u32[]{:S(2)}) collective-permute-start(f32[16,256]{1,0:T(8,128)S(1)} %get-tuple-element.49), channel_id=1, source_target_pairs={{0,3},{1,2},{2,1},{3,0},{4,7},{5,6},{6,5},{7,4},{8,11},{9,10},{10,... | collective-permute-start | bytes 49160 | tf_op jit(solution)/shard_map/ppermute | solution.py:341
  30.9 3.2 %collective-permute-start.10 = (f32[16,256]{1,0:T(8,128)S(1)}, f32[16,256]{1,0:T(8,128)S(1)}, u32[]{:S(2)}, u32[]{:S(2)}) collective-permute-start(f32[16,256]{1,0:T(8,128)S(1)} %get-tuple-element.43), channel_id=1, source_target_pairs={{0,1},{1,0},{2,3},{3,2},{4,5},{5,4},{6,7},{7,6},{8,9},{9,8},{10,11... | collective-permute-start | bytes 49160 | tf_op jit(solution)/shard_map/ppermute | solution.py:341
  30.9 3.8 %collective-permute-start.11 = (f32[16,256]{1,0:T(8,128)S(1)}, f32[16,256]{1,0:T(8,128)S(1)}, u32[]{:S(2)}, u32[]{:S(2)}) collective-permute-start(f32[16,256]{1,0:T(8,128)S(1)} %get-tuple-element.44), channel_id=1, source_target_pairs={{0,2},{1,3},{2,0},{3,1},{4,6},{5,7},{6,4},{7,5},{8,10},{9,11},{10,... | collective-permute-start | bytes 49160 | tf_op jit(solution)/shard_map/ppermute | solution.py:341
  32.2 3.2 %collective-permute-start.12 = (f32[16,256]{1,0:T(8,128)S(1)}, f32[16,256]{1,0:T(8,128)S(1)}, u32[]{:S(2)}, u32[]{:S(2)}) collective-permute-start(f32[16,256]{1,0:T(8,128)S(1)} %get-tuple-element.45), channel_id=1, source_target_pairs={{0,3},{1,2},{2,1},{3,0},{4,7},{5,6},{6,5},{7,4},{8,11},{9,10},{10,... | collective-permute-start | bytes 49160 | tf_op jit(solution)/shard_map/ppermute | solution.py:341

commit v26 on v23

--- a/solution.py
+++ b/solution.py
@@ -12,7 +12,6 @@
 BLOCK = 1024
 VMEM_BYTES = 32 * 1024 * 1024
 NEAR = 4
-NEAR_STEPS = (0, 1, 2, 3)
 F32, BF16 = jnp.float32, jnp.bfloat16
 NT = (((1,), (1,)), ((), ()))
 NN = (((1,), (0,)), ((), ()))
@@ -98,11 +97,16 @@
     return row_len, (lane % pad).astype(F32) < row_len
 
 
+def near_index(n):
+    me = lax.axis_index("rows")
+    return me % 2 + 2 * (me // (n // 2))
+
+
 def along(ref):
     return jnp.concatenate([ref[k : k + 1, :] for k in range(ref.shape[0])], axis=1)
 
 
-def sums_kernel(pad, cap, *refs):
+def sums_kernel(pad, n, *refs):
     (probes, lengths_in, ids_in, firms_in), sends, refs = refs[:4], refs[4 : 4 + NEAR], refs[4 + NEAR :]
     x1, mask_ids, weight, valid, x, sums, lengths, ids, firms, sems, small = refs
     copies = column_copies(probes, x, sems)
@@ -114,7 +118,7 @@
     start_all(copies)
     columns, slots = sums.shape
     part = columns // NEAR
-    me = lax.axis_index("rows") % NEAR
+    me = near_index(n)
     wait_all(first)
     row_len, inside = row_lengths(lengths[...], pad)
     valid[...] = jnp.where(inside, 1.0, 0.0)
@@ -122,7 +126,7 @@
     masked = jnp.where(inside, ids[...], -1)
     mask_ids[...] = masked
     turned = jnp.concatenate([masked.astype(F32)] * (LANES // masked.shape[0]), axis=0).T
-    keys = (iota((1, slots), 1) // cap * FIRMS_PER_SHARD + along(firms)).astype(F32)
+    keys = (iota((1, slots), 1) // (slots // n) * FIRMS_PER_SHARD + along(firms)).astype(F32)
     across = slots // LANES
     rows = ids.shape[0] // across
     masked = jnp.concatenate([masked[k * rows : (k + 1) * rows] for k in range(across)], axis=1).astype(F32)
@@ -144,7 +148,7 @@
         total = block if total is None else total + block
     sums[...] = total[:columns] + total[columns : 2 * columns]
     about = jnp.where(iota((8, slots), 0) == 0, keys, total[2 * columns : 2 * columns + 1])
-    for step, send in zip(NEAR_STEPS, sends):
+    for step, send in enumerate(sends):
         send[:part] = sums[pl.ds(pl.multiple_of((me ^ step) * part, part), part), :]
         send[part : part + 8] = about
 
@@ -296,18 +300,18 @@
         send[...] = mean[part * k : part * (k + 1)]
 
 
-def own_means(parts, means):
-    me = lax.axis_index("rows") % NEAR
+def own_means(n, parts, means):
+    me = near_index(n)
     part = parts[0].shape[0]
-    for step, one in zip(NEAR_STEPS, parts):
+    for step, one in enumerate(parts):
         means[pl.ds(pl.multiple_of((me ^ step) * part, part), part), :] = one[...]
     return jnp.concatenate(split(means[...]), axis=0)
 
 
-def first_kernel(pad, *refs):
+def first_kernel(pad, n, *refs):
     parts, (x1, mask_ids, weight), tables, (y, means) = refs[:NEAR], refs[NEAR : NEAR + 3], refs[NEAR + 3 : -2], refs[-2:]
     columns, slots = means.shape
-    first = own_means(parts, means)
+    first = own_means(n, parts, means)
     table = jnp.concatenate([same_worker(pad, 256)] * 2, axis=0)
     for b in range(y.shape[1] // BLOCK):
         at = slice(b * BLOCK, (b + 1) * BLOCK)
@@ -322,11 +326,11 @@
         y[:, at] = x1[:, at] - spread + worker * row(weight, b, BLOCK)
 
 
-def last_kernel(*refs):
+def last_kernel(n, *refs):
     parts, (before, mask_ids), tables, (out, means, y, sems) = refs[:NEAR], refs[NEAR : NEAR + 2], refs[NEAR + 2 : -4], refs[-4:]
     outs = column_copies(y, out, sems)
     columns, slots = means.shape
-    second = own_means(parts, means)
+    second = own_means(n, parts, means)
     for b in range(len(outs)):
         at = slice(b * BLOCK, (b + 1) * BLOCK)
         found = tables[0][:, at] if tables else one_hot(row(mask_ids, b, BLOCK), slots)
@@ -337,12 +341,12 @@
 
 
 def near_exchange(parts, n):
-    steps = [[(i, i ^ step) for i in range(n)] for step in NEAR_STEPS[1:]]
+    steps = [[(i, i ^ step) for i in range(n)] for step in (1, n // 2, n // 2 + 1)]
     return [parts[0]] + [lax.ppermute(one, "rows", step) for one, step in zip(parts[1:], steps)]
 
 
 def far_share(one, n):
-    steps = [[(i, i ^ (k * NEAR)) for i in range(n)] for k in range(1, n // NEAR)]
+    steps = [[(i, i ^ (2 * k)) for i in range(n)] for k in range(1, n // NEAR)]
     return [one] + [lax.ppermute(one, "rows", step) for step in steps]
 
 
@@ -386,7 +390,7 @@
     of_near = array((columns, slots), F32)
 
     *sends, x1, mask_ids, weight = call(
-        functools.partial(sums_kernel, pad, slots // n),
+        functools.partial(sums_kernel, pad, n),
         [message] * 3 + [array((about, slots), F32), array(whole, F32), array(of_rows, jnp.int32), array(of_rows, F32)],
         [hbm] * 4,
         [vmem] * (NEAR + 3),
@@ -488,7 +492,7 @@
     )(*again, *source, scales, spreads[1] if keep else scales)
     arrived = near_exchange(sends, n)
     before = call(
-        functools.partial(first_kernel, pad),
+        functools.partial(first_kernel, pad, n),
         array(whole, F32),
         [vmem] * (NEAR + 3 + len(spreads)),
         vmem,
@@ -497,7 +501,7 @@
         8 * columns * rows_dev,
     )(*first, x1, mask_ids, weight, *spreads)
     return call(
-        last_kernel,
+        functools.partial(last_kernel, n),
         array(whole, F32),
         [vmem] * (NEAR + 2 + len(spreads[:1])),
         hbm,

time: 37 us -> 37.9 us (1.024)
  starting transfers between devices: 15.9 us -> 17.3 us
  waiting for transfers between devices: 5.59 us -> 5.08 us
    ppermute x9, starting transfers between devices: 6.99 us -> 10.1 us  [near_exchange(): lax.ppermute(one, 'rows', step)]
    ppermute x6, waiting for transfers between devices: 3.66 us -> 0.64 us  [far_share(): return [one] + [lax.ppermute(one, 'rows', step) for step in steps]]
    ppermute x9, waiting for transfers between devices: 1.92 us -> 4.44 us  [near_exchange(): lax.ppermute(one, 'rows', step)]
    ppermute x6, starting transfers between devices: 8.85 us -> 7.05 us  [far_share(): return [one] + [lax.ppermute(one, 'rows', step) for step in steps]]
  transfers between devices with their start and end apart: 16 -> 16, of which waited for: 5 -> 6; matrix products, arithmetic and copies ran while one was open for 0% -> 0% of each run, Pallas kernels for 24% -> 24%
where the time goes in v26:
time: 37.9 us; the launch traced here: 37.7 us
  starting transfers between devices  17.3 us (46%)
  Pallas kernels  15.3 us (40%)
  waiting for transfers between devices  5.08 us (13%)
    ppermute x9, starting transfers between devices, near_exchange(): lax.ppermute(one, 'rows', step)  10.1 us
    ppermute x6, starting transfers between devices, far_share(): return [one] + [lax.ppermute(one, 'rows', step) for step in steps]  7.05 us
    pallas_call x4, Pallas kernels, pair_counts(): call(functools.partial(pairs_kernel, pad, about), array((len(parts), slot...  4.93 us
    ppermute x9, waiting for transfers between devices, near_exchange(): lax.ppermute(one, 'rows', step)  4.44 us
    pallas_call x1, Pallas kernels, body(): call(functools.partial(sums_kernel, pad, n), [message] * 3 + [array((abou...  3.37 us
    pallas_call x1, Pallas kernels, body(): call(functools.partial(last_kernel, n), array(whole, F32), [vmem] * (NEAR...  1.62 us
    pallas_call x1, Pallas kernels, body(): call(functools.partial(change_kernel, far, part, len(tables)), [of_near,...  1.36 us
    pallas_call x1, Pallas kernels, body(): call(functools.partial(first_kernel, pad, n), array(whole, F32), [vmem] *...  1.32 us
  transfers between devices with their start and end apart: 16, of which 6 were waited for; matrix products, arithmetic and copies ran while one was open for 0% of the time, Pallas kernels for 24%

profile of v26, /device:TPU:0, one launch (start us, length us, event | category | flops | bytes accessed | tf_op | source)
XLA Modules:
  0.0 37.7 jit_solution(10791771865816286109)
XLA Ops:
  0.0 3.4 %shard_map.46 = (f32[56,256]{1,0:T(8,128)S(1)}, f32[56,256]{1,0:T(8,128)S(1)}, f32[56,256]{1,0:T(8,128)S(1)}, f32[24,256]{1,0:T(8,128)S(1)}, f32[64,8192]{1,0:T(...) custom-call(f32[64,8192]{1,0:T(8,128)} %refs_0_.1, s32[8,128]{1,0:T(8,128)} %bitcast.4, s32[64,128]{1,0:T(8,128)} %bitcast.3, ...), custom_call_target="tpu_custom_call" | custom-call | flops 1073741824 | bytes 2097152 | tf_op jit(solution)/shard_map/pallas_call | solution.py:392
  3.4 0.5 %collective-permute-start = (f32[56,256]{1,0:T(8,128)S(1)}, f32[56,256]{1,0:T(8,128)S(1)}, u32[]{:S(2)}, u32[]{:S(2)}) collective-permute-start(f32[56,256]{1,0:T(8,128)S(1)} %get-tuple-element.30), channel_id=1, source_target_pairs={{0,1},{1,0},{2,3},{3,2},{4,5},{5,4},{6,7},{7,6},{8,9},{9,8},{10,11... | collective-permute-start | bytes 172040 | tf_op jit(solution)/shard_map/ppermute | solution.py:345
  3.9 3.7 %collective-permute-start.1 = (f32[56,256]{1,0:T(8,128)S(1)}, f32[56,256]{1,0:T(8,128)S(1)}, u32[]{:S(2)}, u32[]{:S(2)}) collective-permute-start(f32[56,256]{1,0:T(8,128)S(1)} %get-tuple-element.31), channel_id=1, source_target_pairs={{0,8},{1,9},{2,10},{3,11},{4,12},{5,13},{6,14},{7,15},{8,0},{9,1},... | collective-permute-start | bytes 172040 | tf_op jit(solution)/shard_map/ppermute | solution.py:345
  7.6 0.1 collective-permute-start.2
  7.6 1.2 %shard_map.47.refs_4_.refs_6_ = bf16[1,256,512]{2,1,0:T(8,128)(2,1)S(1)} custom-call(f32[56,256]{1,0:T(8,128)S(1)} %get-tuple-element.29.refs_0_), custom_call_target="tpu_custom_call" | custom-call | flops 134217728 | bytes 262144 | tf_op jit(solution)/shard_map/pallas_call | solution.py:412
  8.9 0.0 collective-permute-done.refs_0_.refs_1_
  8.9 1.2 %shard_map.48.refs_5_.refs_7_ = bf16[1,256,512]{2,1,0:T(8,128)(2,1)S(1)} custom-call(f32[56,256]{1,0:T(8,128)S(1)} %collective-permute-done.refs_0_.refs_1_), custom_call_target="tpu_custom_call" | custom-call | flops 134217728 | bytes 262144 | tf_op jit(solution)/shard_map/pallas_call | solution.py:412
  10.1 1.6 %collective-permute-done.2.refs_3_ = f32[24,256]{1,0:T(8,128)S(1)} collective-permute-done((f32[24,256]{1,0:T(8,128)S(1)}, f32[24,256]{1,0:T(8,128)S(1)}, u32[]{:S(2)}, u32[]{:S(2)}) %collective-permute-start.2) | collective-permute-done | bytes 24608 | tf_op jit(solution)/shard_map/ppermute | solution.py:345
  11.7 0.0 collective-permute-done.1.refs_2_.passed.refs_0_
  11.7 2.6 %collective-permute-start.5 = (f32[72,256]{1,0:T(8,128)S(1)}, f32[72,256]{1,0:T(8,128)S(1)}, u32[]{:S(2)}, u32[]{:S(2)}) collective-permute-start(f32[72,256]{1,0:T(8,128)S(1)} %shard_map.49.own.one.refs_0_), channel_id=1, source_target_pairs={{0,6},{1,7},{2,4},{3,5},{4,2},{5,3},{6,0},{7,1},{8,14},{9,15},{10,... | collective-permute-start | bytes 221192 | tf_op jit(solution)/shard_map/ppermute | solution.py:350
  14.3 0.4 %collective-permute-start.4 = (f32[72,256]{1,0:T(8,128)S(1)}, f32[72,256]{1,0:T(8,128)S(1)}, u32[]{:S(2)}, u32[]{:S(2)}) collective-permute-start(f32[72,256]{1,0:T(8,128)S(1)} %shard_map.49.own.one.refs_0_), channel_id=1, source_target_pairs={{0,4},{1,5},{2,6},{3,7},{4,0},{5,1},{6,2},{7,3},{8,12},{9,13},{10,... | collective-permute-start | bytes 221192 | tf_op jit(solution)/shard_map/ppermute | solution.py:350
  14.8 0.5 %collective-permute-start.3 = (f32[72,256]{1,0:T(8,128)S(1)}, f32[72,256]{1,0:T(8,128)S(1)}, u32[]{:S(2)}, u32[]{:S(2)}) collective-permute-start(f32[72,256]{1,0:T(8,128)S(1)} %shard_map.49.own.one.refs_0_), channel_id=1, source_target_pairs={{0,2},{1,3},{2,0},{3,1},{4,6},{5,7},{6,4},{7,5},{8,10},{9,11},{10,... | collective-permute-start | bytes 221192 | tf_op jit(solution)/shard_map/ppermute | solution.py:350
  15.3 0.3 shard_map.50
  15.6 0.1 collective-permute-start.6
  15.7 1.2 %shard_map.52.refs_8_ = bf16[1,256,512]{2,1,0:T(8,128)(2,1)S(1)} custom-call(f32[56,256]{1,0:T(8,128)S(1)} %collective-permute-done.1.refs_2_.passed.refs_0_), custom_call_target="tpu_custom_call" | custom-call | flops 134217728 | bytes 262144 | tf_op jit(solution)/shard_map/pallas_call | solution.py:412
  16.9 0.0 collective-permute-done.6.refs_0_
  16.9 1.2 %shard_map.53.refs_9_ = bf16[1,256,512]{2,1,0:T(8,128)(2,1)S(1)} custom-call(f32[56,256]{1,0:T(8,128)S(1)} %collective-permute-done.6.refs_0_), custom_call_target="tpu_custom_call" | custom-call | flops 134217728 | bytes 262144 | tf_op jit(solution)/shard_map/pallas_call | solution.py:412
  18.2 0.0 collective-permute-done.5.one.refs_3_
  18.2 0.3 shard_map.51.refs_5_.refs_7_
  18.5 0.2 collective-permute-done.4.refs_2_
  18.7 0.4 %collective-permute-done.3.refs_1_ = f32[72,256]{1,0:T(8,128)S(1)} collective-permute-done((f32[72,256]{1,0:T(8,128)S(1)}, f32[72,256]{1,0:T(8,128)S(1)}, u32[]{:S(2)}, u32[]{:S(2)}) %collective-permute-start.3) | collective-permute-done | bytes 73760 | tf_op jit(solution)/shard_map/ppermute | solution.py:350
  19.1 1.4 %shard_map.54 = (f32[64,256]{1,0:T(8,128)S(1)}, f32[64,256]{1,0:T(8,128)S(1)}, f32[2,8,512]{2,1,0:T(8,128)S(1)}, bf16[2,512,512]{2,1,0:T(8,128)(2,1)S(1)}, bf16[2,512,512]{2,1,0:T(8,128)(2,1)S(1)}) custom-call(f32[72,256]{1,0:T(8,128)S(1)} %shard_map.49.own.one.refs_0_, f32[72,256]{1,0:T(8,128)S(1)} %collective-permute-done.3.refs_1_, ...), custom_call_target="tpu_custom_call" | custom-call | flops 134217728 | bytes 262144 | tf_op jit(solution)/shard_map/pallas_call | solution.py:459
  20.5 2.1 %collective-permute-start.9 = (f32[64,256]{1,0:T(8,128)S(1)}, f32[64,256]{1,0:T(8,128)S(1)}, u32[]{:S(2)}, u32[]{:S(2)}) collective-permute-start(f32[64,256]{1,0:T(8,128)S(1)} %get-tuple-element.35.refs_0_), channel_id=1, source_target_pairs={{0,6},{1,7},{2,4},{3,5},{4,2},{5,3},{6,0},{7,1},{8,14},{9,15},{10,... | collective-permute-start | bytes 196616 | tf_op jit(solution)/shard_map/ppermute | solution.py:350
  22.5 0.4 %collective-permute-start.8 = (f32[64,256]{1,0:T(8,128)S(1)}, f32[64,256]{1,0:T(8,128)S(1)}, u32[]{:S(2)}, u32[]{:S(2)}) collective-permute-start(f32[64,256]{1,0:T(8,128)S(1)} %get-tuple-element.35.refs_0_), channel_id=1, source_target_pairs={{0,4},{1,5},{2,6},{3,7},{4,0},{5,1},{6,2},{7,3},{8,12},{9,13},{10,... | collective-permute-start | bytes 196616 | tf_op jit(solution)/shard_map/ppermute | solution.py:350
  23.0 1.0 %collective-permute-start.7 = (f32[64,256]{1,0:T(8,128)S(1)}, f32[64,256]{1,0:T(8,128)S(1)}, u32[]{:S(2)}, u32[]{:S(2)}) collective-permute-start(f32[64,256]{1,0:T(8,128)S(1)} %get-tuple-element.35.refs_0_), channel_id=1, source_target_pairs={{0,2},{1,3},{2,0},{3,1},{4,6},{5,7},{6,4},{7,5},{8,10},{9,11},{10,... | collective-permute-start | bytes 196616 | tf_op jit(solution)/shard_map/ppermute | solution.py:350
  24.0 1.3 %shard_map.55 = (bf16[256,8192]{1,0:T(8,128)(2,1)S(1)}, bf16[256,8192]{1,0:T(8,128)(2,1)S(1)}, f32[16,256]{1,0:T(8,128)S(1)}, f32[16,256]{1,0:T(8,128)S(1)}, f32...) custom-call(s32[64,128]{1,0:T(8,128)S(1)} %get-tuple-element.39.mask_ids.refs_5_, f32[64,256]{1,0:T(8,128)S(1)} %get-tuple-element.40.mean), custom_call_target="tpu_custom_call" | custom-call | flops 536870912 | bytes 8388608 | tf_op jit(solution)/shard_map/pallas_call | solution.py:473
  25.3 0.1 collective-permute-start.13
  25.4 2.8 %collective-permute-start.14 = (f32[16,256]{1,0:T(8,128)S(1)}, f32[16,256]{1,0:T(8,128)S(1)}, u32[]{:S(2)}, u32[]{:S(2)}) collective-permute-start(f32[16,256]{1,0:T(8,128)S(1)} %get-tuple-element.48), channel_id=1, source_target_pairs={{0,8},{1,9},{2,10},{3,11},{4,12},{5,13},{6,14},{7,15},{8,0},{9,1},... | collective-permute-start | bytes 49160 | tf_op jit(solution)/shard_map/ppermute | solution.py:345
  28.1 0.0 collective-permute-done.9.refs_3_
  28.1 0.1 collective-permute-start.15
  28.2 0.0 collective-permute-done.8.refs_2_
  28.2 0.0 collective-permute-done.7.refs_1_
  28.2 0.8 %shard_map.56 = (f32[16,256]{1,0:T(8,128)S(1)}, f32[16,256]{1,0:T(8,128)S(1)}, f32[16,256]{1,0:T(8,128)S(1)}, f32[16,256]{1,0:T(8,128)S(1)}) custom-call(f32[64,256]{1,0:T(8,128)S(1)} %get-tuple-element.35.refs_0_, f32[64,256]{1,0:T(8,128)S(1)} %collective-permute-done.7.refs_1_, f32[64,256]{1,0:T(8,128)S(1)} %collective-permute-done.8.refs_2_, ...), custom_call_target="tpu_custom_call" | custom-call | flops 134217728 | bytes 262144 | tf_op jit(solution)/shard_map/pallas_call | solution.py:484
  28.9 0.4 %collective-permute-start.10 = (f32[16,256]{1,0:T(8,128)S(1)}, f32[16,256]{1,0:T(8,128)S(1)}, u32[]{:S(2)}, u32[]{:S(2)}) collective-permute-start(f32[16,256]{1,0:T(8,128)S(1)} %get-tuple-element.43), channel_id=1, source_target_pairs={{0,1},{1,0},{2,3},{3,2},{4,5},{5,4},{6,7},{7,6},{8,9},{9,8},{10,11... | collective-permute-start | bytes 49160 | tf_op jit(solution)/shard_map/ppermute | solution.py:345
  29.4 2.6 %collective-permute-start.11 = (f32[16,256]{1,0:T(8,128)S(1)}, f32[16,256]{1,0:T(8,128)S(1)}, u32[]{:S(2)}, u32[]{:S(2)}) collective-permute-start(f32[16,256]{1,0:T(8,128)S(1)} %get-tuple-element.44), channel_id=1, source_target_pairs={{0,8},{1,9},{2,10},{3,11},{4,12},{5,13},{6,14},{7,15},{8,0},{9,1},... | collective-permute-start | bytes 49160 | tf_op jit(solution)/shard_map/ppermute | solution.py:345
  31.9 0.0 collective-permute-done.13.refs_1_
  31.9 0.0 collective-permute-start.12
  31.9 0.0 collective-permute-done.14.refs_2_
  32.0 0.2 collective-permute-done.15.refs_3_
  32.2 1.3 %shard_map.57.refs_4_ = f32[64,8192]{1,0:T(8,128)S(1)} custom-call(f32[16,256]{1,0:T(8,128)S(1)} %get-tuple-element.46.refs_0_, f32[16,256]{1,0:T(8,128)S(1)} %collective-permute-done.13.refs_1_, f32[16,256]{1,0:T(8,128)S(1)} %collective-permute-done.14.refs_2_, f32[16,256]{1,0:T(8,128)S(1)} %collective-permute-done.15.refs_3_, ...), custom_call_target="tpu_custom_call" | custom-call | flops 536870912 | bytes 4194304 | tf_op jit(solution)/shard_map/pallas_call | solution.py:494
  33.5 0.0 collective-permute-done.10.refs_1_
  33.5 0.6 %collective-permute-done.11.refs_2_ = f32[16,256]{1,0:T(8,128)S(1)} collective-permute-done((f32[16,256]{1,0:T(8,128)S(1)}, f32[16,256]{1,0:T(8,128)S(1)}, u32[]{:S(2)}, u32[]{:S(2)}) %collective-permute-start.11) | collective-permute-done | bytes 16416 | tf_op jit(solution)/shard_map/ppermute | solution.py:345
  34.2 2.0 %collective-permute-done.12.refs_3_ = f32[16,256]{1,0:T(8,128)S(1)} collective-permute-done((f32[16,256]{1,0:T(8,128)S(1)}, f32[16,256]{1,0:T(8,128)S(1)}, u32[]{:S(2)}, u32[]{:S(2)}) %collective-permute-start.12) | collective-permute-done | bytes 16416 | tf_op jit(solution)/shard_map/ppermute | solution.py:345
  36.1 1.6 %shard_map.58 = f32[64,8192]{1,0:T(8,128)} custom-call(f32[16,256]{1,0:T(8,128)S(1)} %get-tuple-element.42.refs_0_, f32[16,256]{1,0:T(8,128)S(1)} %collective-permute-done.10.refs_1_, f32[16,256]{1,0:T(8,128)S(1)} %collective-permute-done.11.refs_2_, f32[16,256]{1,0:T(8,128)S(1)} %collective-permute-done.12.refs_3_, f32[64,8192]{1,0:T(8,128)S(1)} %shard_map.57.refs_4_, ...), custom_call_target="tpu_custom_call" | custom-call | flops 536870912 | bytes 4194304 | tf_op jit(solution)/shard_map/pallas_call | solution.py:503
  (1 shorter events, 0.0 us)
Async XLA Ops:
  3.4 5.5 %collective-permute-start = (f32[56,256]{1,0:T(8,128)S(1)}, f32[56,256]{1,0:T(8,128)S(1)}, u32[]{:S(2)}, u32[]{:S(2)}) collective-permute-start(f32[56,256]{1,0:T(8,128)S(1)} %get-tuple-element.30), channel_id=1, source_target_pairs={{0,1},{1,0},{2,3},{3,2},{4,5},{5,4},{6,7},{7,6},{8,9},{9,8},{10,11... | collective-permute-start | bytes 172040 | tf_op jit(solution)/shard_map/ppermute | solution.py:345
  3.9 7.8 %collective-permute-start.1 = (f32[56,256]{1,0:T(8,128)S(1)}, f32[56,256]{1,0:T(8,128)S(1)}, u32[]{:S(2)}, u32[]{:S(2)}) collective-permute-start(f32[56,256]{1,0:T(8,128)S(1)} %get-tuple-element.31), channel_id=1, source_target_pairs={{0,8},{1,9},{2,10},{3,11},{4,12},{5,13},{6,14},{7,15},{8,0},{9,1},... | collective-permute-start | bytes 172040 | tf_op jit(solution)/shard_map/ppermute | solution.py:345
  7.6 4.2 %collective-permute-start.2 = (f32[24,256]{1,0:T(8,128)S(1)}, f32[24,256]{1,0:T(8,128)S(1)}, u32[]{:S(2)}, u32[]{:S(2)}) collective-permute-start(f32[24,256]{1,0:T(8,128)S(1)} %get-tuple-element.32), channel_id=1, source_target_pairs={{0,9},{1,8},{2,11},{3,10},{4,13},{5,12},{6,15},{7,14},{8,1},{9,0},... | collective-permute-start | bytes 73736 | tf_op jit(solution)/shard_map/ppermute | solution.py:345
  11.7 6.4 %collective-permute-start.5 = (f32[72,256]{1,0:T(8,128)S(1)}, f32[72,256]{1,0:T(8,128)S(1)}, u32[]{:S(2)}, u32[]{:S(2)}) collective-permute-start(f32[72,256]{1,0:T(8,128)S(1)} %shard_map.49.own.one.refs_0_), channel_id=1, source_target_pairs={{0,6},{1,7},{2,4},{3,5},{4,2},{5,3},{6,0},{7,1},{8,14},{9,15},{10,... | collective-permute-start | bytes 221192 | tf_op jit(solution)/shard_map/ppermute | solution.py:350
  14.3 4.4 %collective-permute-start.4 = (f32[72,256]{1,0:T(8,128)S(1)}, f32[72,256]{1,0:T(8,128)S(1)}, u32[]{:S(2)}, u32[]{:S(2)}) collective-permute-start(f32[72,256]{1,0:T(8,128)S(1)} %shard_map.49.own.one.refs_0_), channel_id=1, source_target_pairs={{0,4},{1,5},{2,6},{3,7},{4,0},{5,1},{6,2},{7,3},{8,12},{9,13},{10,... | collective-permute-start | bytes 221192 | tf_op jit(solution)/shard_map/ppermute | solution.py:350
  14.8 4.4 %collective-permute-start.3 = (f32[72,256]{1,0:T(8,128)S(1)}, f32[72,256]{1,0:T(8,128)S(1)}, u32[]{:S(2)}, u32[]{:S(2)}) collective-permute-start(f32[72,256]{1,0:T(8,128)S(1)} %shard_map.49.own.one.refs_0_), channel_id=1, source_target_pairs={{0,2},{1,3},{2,0},{3,1},{4,6},{5,7},{6,4},{7,5},{8,10},{9,11},{10,... | collective-permute-start | bytes 221192 | tf_op jit(solution)/shard_map/ppermute | solution.py:350
  15.6 1.3 %collective-permute-start.6 = (f32[56,256]{1,0:T(8,128)S(1)}, f32[56,256]{1,0:T(8,128)S(1)}, u32[]{:S(2)}, u32[]{:S(2)}) collective-permute-start(f32[56,256]{1,0:T(8,128)S(1)} %get-tuple-element.34), channel_id=1, source_target_pairs={{0,1},{1,0},{2,3},{3,2},{4,5},{5,4},{6,7},{7,6},{8,9},{9,8},{10,11... | collective-permute-start | bytes 172040 | tf_op jit(solution)/shard_map/ppermute | solution.py:455
  20.5 7.6 %collective-permute-start.9 = (f32[64,256]{1,0:T(8,128)S(1)}, f32[64,256]{1,0:T(8,128)S(1)}, u32[]{:S(2)}, u32[]{:S(2)}) collective-permute-start(f32[64,256]{1,0:T(8,128)S(1)} %get-tuple-element.35.refs_0_), channel_id=1, source_target_pairs={{0,6},{1,7},{2,4},{3,5},{4,2},{5,3},{6,0},{7,1},{8,14},{9,15},{10,... | collective-permute-start | bytes 196616 | tf_op jit(solution)/shard_map/ppermute | solution.py:350
  22.5 5.6 %collective-permute-start.8 = (f32[64,256]{1,0:T(8,128)S(1)}, f32[64,256]{1,0:T(8,128)S(1)}, u32[]{:S(2)}, u32[]{:S(2)}) collective-permute-start(f32[64,256]{1,0:T(8,128)S(1)} %get-tuple-element.35.refs_0_), channel_id=1, source_target_pairs={{0,4},{1,5},{2,6},{3,7},{4,0},{5,1},{6,2},{7,3},{8,12},{9,13},{10,... | collective-permute-start | bytes 196616 | tf_op jit(solution)/shard_map/ppermute | solution.py:350
  23.0 5.2 %collective-permute-start.7 = (f32[64,256]{1,0:T(8,128)S(1)}, f32[64,256]{1,0:T(8,128)S(1)}, u32[]{:S(2)}, u32[]{:S(2)}) collective-permute-start(f32[64,256]{1,0:T(8,128)S(1)} %get-tuple-element.35.refs_0_), channel_id=1, source_target_pairs={{0,2},{1,3},{2,0},{3,1},{4,6},{5,7},{6,4},{7,5},{8,10},{9,11},{10,... | collective-permute-start | bytes 196616 | tf_op jit(solution)/shard_map/ppermute | solution.py:350
  25.3 6.7 %collective-permute-start.13 = (f32[16,256]{1,0:T(8,128)S(1)}, f32[16,256]{1,0:T(8,128)S(1)}, u32[]{:S(2)}, u32[]{:S(2)}) collective-permute-start(f32[16,256]{1,0:T(8,128)S(1)} %get-tuple-element.47), channel_id=1, source_target_pairs={{0,1},{1,0},{2,3},{3,2},{4,5},{5,4},{6,7},{7,6},{8,9},{9,8},{10,11... | collective-permute-start | bytes 49160 | tf_op jit(solution)/shard_map/ppermute | solution.py:345
  25.4 6.6 %collective-permute-start.14 = (f32[16,256]{1,0:T(8,128)S(1)}, f32[16,256]{1,0:T(8,128)S(1)}, u32[]{:S(2)}, u32[]{:S(2)}) collective-permute-start(f32[16,256]{1,0:T(8,128)S(1)} %get-tuple-element.48), channel_id=1, source_target_pairs={{0,8},{1,9},{2,10},{3,11},{4,12},{5,13},{6,14},{7,15},{8,0},{9,1},... | collective-permute-start | bytes 49160 | tf_op jit(solution)/shard_map/ppermute | solution.py:345
  28.1 4.1 %collective-permute-start.15 = (f32[16,256]{1,0:T(8,128)S(1)}, f32[16,256]{1,0:T(8,128)S(1)}, u32[]{:S(2)}, u32[]{:S(2)}) collective-permute-start(f32[16,256]{1,0:T(8,128)S(1)} %get-tuple-element.49), channel_id=1, source_target_pairs={{0,9},{1,8},{2,11},{3,10},{4,13},{5,12},{6,15},{7,14},{8,1},{9,0},... | collective-permute-start | bytes 49160 | tf_op jit(solution)/shard_map/ppermute | solution.py:345
  28.9 4.6 %collective-permute-start.10 = (f32[16,256]{1,0:T(8,128)S(1)}, f32[16,256]{1,0:T(8,128)S(1)}, u32[]{:S(2)}, u32[]{:S(2)}) collective-permute-start(f32[16,256]{1,0:T(8,128)S(1)} %get-tuple-element.43), channel_id=1, source_target_pairs={{0,1},{1,0},{2,3},{3,2},{4,5},{5,4},{6,7},{7,6},{8,9},{9,8},{10,11... | collective-permute-start | bytes 49160 | tf_op jit(solution)/shard_map/ppermute | solution.py:345
  29.4 4.8 %collective-permute-start.11 = (f32[16,256]{1,0:T(8,128)S(1)}, f32[16,256]{1,0:T(8,128)S(1)}, u32[]{:S(2)}, u32[]{:S(2)}) collective-permute-start(f32[16,256]{1,0:T(8,128)S(1)} %get-tuple-element.44), channel_id=1, source_target_pairs={{0,8},{1,9},{2,10},{3,11},{4,12},{5,13},{6,14},{7,15},{8,0},{9,1},... | collective-permute-start | bytes 49160 | tf_op jit(solution)/shard_map/ppermute | solution.py:345
  31.9 4.2 %collective-permute-start.12 = (f32[16,256]{1,0:T(8,128)S(1)}, f32[16,256]{1,0:T(8,128)S(1)}, u32[]{:S(2)}, u32[]{:S(2)}) collective-permute-start(f32[16,256]{1,0:T(8,128)S(1)} %get-tuple-element.45), channel_id=1, source_target_pairs={{0,9},{1,8},{2,11},{3,10},{4,13},{5,12},{6,15},{7,14},{8,1},{9,0},... | collective-permute-start | bytes 49160 | tf_op jit(solution)/shard_map/ppermute | solution.py:345

commit v27 on v23

--- a/solution.py
+++ b/solution.py
@@ -104,8 +104,9 @@
 
 def sums_kernel(pad, cap, *refs):
     (probes, lengths_in, ids_in, firms_in), sends, refs = refs[:4], refs[4 : 4 + NEAR], refs[4 + NEAR :]
-    x1, mask_ids, weight, valid, x, sums, lengths, ids, firms, sems, small = refs
-    copies = column_copies(probes, x, sems)
+    x1, mask_ids, weight, valid, x, sums, lengths, ids, firms, bands_sem, small = refs
+    bands = [pl.ds(at, 8) for at in range(0, x.shape[0], 8)]
+    copies = [pltpu.make_async_copy(probes.at[at], x.at[at], bands_sem.at[b]) for b, at in enumerate(bands)]
     first = [
         pltpu.make_async_copy(source, target, small.at[k])
         for k, (source, target) in enumerate(((lengths_in, lengths), (ids_in, ids), (firms_in, firms)))
@@ -132,7 +133,7 @@
     table = jnp.concatenate([same_worker(pad, 256)] * 2, axis=0)
     wait_all(copies)
     total = None
-    for b in range(len(copies)):
+    for b in range(x.shape[1] // BLOCK):
         ok = row(valid, b, BLOCK)
         x0 = x[:, b * BLOCK : (b + 1) * BLOCK] * ok
         rest = x0 - by_worker(x0, table) * row(weight, b, BLOCK)
@@ -397,7 +398,7 @@
             pltpu.VMEM(lengths.shape, jnp.int32),
             pltpu.VMEM(ids.shape, jnp.int32),
             pltpu.VMEM(firms.shape, jnp.int32),
-            sems,
+            pltpu.SemaphoreType.DMA((columns // 8,)),
             pltpu.SemaphoreType.DMA((3,)),
         ],
         2 * work,

time: 37 us -> 37 us (level)
  no operation moved by 1% of the time
where the time goes in v27:
time: 37 us; the launch traced here: 36.9 us
  starting transfers between devices  15.9 us (43%)
  Pallas kernels  15.3 us (41%)
  waiting for transfers between devices  5.59 us (15%)
    ppermute x6, starting transfers between devices, far_share(): return [one] + [lax.ppermute(one, 'rows', step) for step in steps]  8.85 us
    ppermute x9, starting transfers between devices, near_exchange(): lax.ppermute(one, 'rows', step)  6.99 us
    pallas_call x4, Pallas kernels, pair_counts(): call(functools.partial(pairs_kernel, pad, about), array((len(parts), slot...  4.92 us
    ppermute x6, waiting for transfers between devices, far_share(): return [one] + [lax.ppermute(one, 'rows', step) for step in steps]  3.66 us
    pallas_call x1, Pallas kernels, body(): call(functools.partial(sums_kernel, pad, slots // n), [message] * 3 + [ar...  3.37 us
    ppermute x9, waiting for transfers between devices, near_exchange(): lax.ppermute(one, 'rows', step)  1.92 us
    pallas_call x1, Pallas kernels, body(): call(last_kernel, array(whole, F32), [vmem] * (NEAR + 2 + len(spreads[:1]...  1.62 us
    pallas_call x1, Pallas kernels, body(): call(functools.partial(change_kernel, far, part, len(tables)), [of_near,...  1.37 us
  transfers between devices with their start and end apart: 16, of which 5 were waited for; matrix products, arithmetic and copies ran while one was open for 0% of the time, Pallas kernels for 24%

profile of v27, /device:TPU:0, one launch (start us, length us, event | category | flops | bytes accessed | tf_op | source)
XLA Modules:
  0.0 36.9 jit_solution(3675415554714102930)
XLA Ops:
  0.0 3.4 %shard_map.46 = (f32[56,256]{1,0:T(8,128)S(1)}, f32[56,256]{1,0:T(8,128)S(1)}, f32[56,256]{1,0:T(8,128)S(1)}, f32[24,256]{1,0:T(8,128)S(1)}, f32[64,8192]{1,0:T(...) custom-call(f32[64,8192]{1,0:T(8,128)} %refs_0_.1, s32[8,128]{1,0:T(8,128)} %bitcast.4, s32[64,128]{1,0:T(8,128)} %bitcast.3, ...), custom_call_target="tpu_custom_call" | custom-call | flops 1073741824 | bytes 2097152 | tf_op jit(solution)/shard_map/pallas_call | solution.py:389
  3.4 0.5 %collective-permute-start = (f32[56,256]{1,0:T(8,128)S(1)}, f32[56,256]{1,0:T(8,128)S(1)}, u32[]{:S(2)}, u32[]{:S(2)}) collective-permute-start(f32[56,256]{1,0:T(8,128)S(1)} %get-tuple-element.30), channel_id=1, source_target_pairs={{0,1},{1,0},{2,3},{3,2},{4,5},{5,4},{6,7},{7,6},{8,9},{9,8},{10,11... | collective-permute-start | bytes 172040 | tf_op jit(solution)/shard_map/ppermute | solution.py:342
  3.9 2.6 %collective-permute-start.1 = (f32[56,256]{1,0:T(8,128)S(1)}, f32[56,256]{1,0:T(8,128)S(1)}, u32[]{:S(2)}, u32[]{:S(2)}) collective-permute-start(f32[56,256]{1,0:T(8,128)S(1)} %get-tuple-element.31), channel_id=1, source_target_pairs={{0,2},{1,3},{2,0},{3,1},{4,6},{5,7},{6,4},{7,5},{8,10},{9,11},{10,... | collective-permute-start | bytes 172040 | tf_op jit(solution)/shard_map/ppermute | solution.py:342
  6.5 0.1 collective-permute-start.2
  6.6 1.2 %shard_map.47.refs_4_.refs_6_ = bf16[1,256,512]{2,1,0:T(8,128)(2,1)S(1)} custom-call(f32[56,256]{1,0:T(8,128)S(1)} %get-tuple-element.29.refs_0_), custom_call_target="tpu_custom_call" | custom-call | flops 134217728 | bytes 262144 | tf_op jit(solution)/shard_map/pallas_call | solution.py:409
  7.8 0.0 collective-permute-done.refs_0_.refs_1_
  7.8 1.2 %shard_map.48.refs_5_.refs_7_ = bf16[1,256,512]{2,1,0:T(8,128)(2,1)S(1)} custom-call(f32[56,256]{1,0:T(8,128)S(1)} %collective-permute-done.refs_0_.refs_1_), custom_call_target="tpu_custom_call" | custom-call | flops 134217728 | bytes 262144 | tf_op jit(solution)/shard_map/pallas_call | solution.py:409
  9.0 0.7 %collective-permute-done.2.refs_3_ = f32[24,256]{1,0:T(8,128)S(1)} collective-permute-done((f32[24,256]{1,0:T(8,128)S(1)}, f32[24,256]{1,0:T(8,128)S(1)}, u32[]{:S(2)}, u32[]{:S(2)}) %collective-permute-start.2) | collective-permute-done | bytes 24608 | tf_op jit(solution)/shard_map/ppermute | solution.py:342
  9.7 0.0 collective-permute-done.1.refs_2_.passed.refs_0_
  9.8 3.7 %collective-permute-start.5 = (f32[72,256]{1,0:T(8,128)S(1)}, f32[72,256]{1,0:T(8,128)S(1)}, u32[]{:S(2)}, u32[]{:S(2)}) collective-permute-start(f32[72,256]{1,0:T(8,128)S(1)} %shard_map.49.own.one.refs_0_), channel_id=1, source_target_pairs={{0,12},{1,13},{2,14},{3,15},{4,8},{5,9},{6,10},{7,11},{8,4},{9,5},... | collective-permute-start | bytes 221192 | tf_op jit(solution)/shard_map/ppermute | solution.py:347
  13.4 0.0 collective-permute-start.4
  13.4 0.8 %collective-permute-start.3 = (f32[72,256]{1,0:T(8,128)S(1)}, f32[72,256]{1,0:T(8,128)S(1)}, u32[]{:S(2)}, u32[]{:S(2)}) collective-permute-start(f32[72,256]{1,0:T(8,128)S(1)} %shard_map.49.own.one.refs_0_), channel_id=1, source_target_pairs={{0,4},{1,5},{2,6},{3,7},{4,0},{5,1},{6,2},{7,3},{8,12},{9,13},{10,... | collective-permute-start | bytes 221192 | tf_op jit(solution)/shard_map/ppermute | solution.py:347
  14.2 0.3 shard_map.50
  14.5 0.1 collective-permute-start.6
  14.6 1.2 %shard_map.52.refs_8_ = bf16[1,256,512]{2,1,0:T(8,128)(2,1)S(1)} custom-call(f32[56,256]{1,0:T(8,128)S(1)} %collective-permute-done.1.refs_2_.passed.refs_0_), custom_call_target="tpu_custom_call" | custom-call | flops 134217728 | bytes 262144 | tf_op jit(solution)/shard_map/pallas_call | solution.py:409
  15.8 0.0 collective-permute-done.6.refs_0_
  15.8 1.2 %shard_map.53.refs_9_ = bf16[1,256,512]{2,1,0:T(8,128)(2,1)S(1)} custom-call(f32[56,256]{1,0:T(8,128)S(1)} %collective-permute-done.6.refs_0_), custom_call_target="tpu_custom_call" | custom-call | flops 134217728 | bytes 262144 | tf_op jit(solution)/shard_map/pallas_call | solution.py:409
  17.1 0.0 collective-permute-done.5.one.refs_3_
  17.1 0.3 shard_map.51.refs_5_.refs_7_
  17.4 2.5 %collective-permute-done.4.refs_2_ = f32[72,256]{1,0:T(8,128)S(1)} collective-permute-done((f32[72,256]{1,0:T(8,128)S(1)}, f32[72,256]{1,0:T(8,128)S(1)}, u32[]{:S(2)}, u32[]{:S(2)}) %collective-permute-start.4) | collective-permute-done | bytes 73760 | tf_op jit(solution)/shard_map/ppermute | solution.py:347
  19.9 0.0 collective-permute-done.3.refs_1_
  19.9 1.4 %shard_map.54 = (f32[64,256]{1,0:T(8,128)S(1)}, f32[64,256]{1,0:T(8,128)S(1)}, f32[2,8,512]{2,1,0:T(8,128)S(1)}, bf16[2,512,512]{2,1,0:T(8,128)(2,1)S(1)}, bf16[2,512,512]{2,1,0:T(8,128)(2,1)S(1)}) custom-call(f32[72,256]{1,0:T(8,128)S(1)} %shard_map.49.own.one.refs_0_, f32[72,256]{1,0:T(8,128)S(1)} %collective-permute-done.3.refs_1_, ...), custom_call_target="tpu_custom_call" | custom-call | flops 134217728 | bytes 262144 | tf_op jit(solution)/shard_map/pallas_call | solution.py:456
  21.3 2.5 %collective-permute-start.9 = (f32[64,256]{1,0:T(8,128)S(1)}, f32[64,256]{1,0:T(8,128)S(1)}, u32[]{:S(2)}, u32[]{:S(2)}) collective-permute-start(f32[64,256]{1,0:T(8,128)S(1)} %get-tuple-element.35.refs_0_), channel_id=1, source_target_pairs={{0,12},{1,13},{2,14},{3,15},{4,8},{5,9},{6,10},{7,11},{8,4},{9,5},... | collective-permute-start | bytes 196616 | tf_op jit(solution)/shard_map/ppermute | solution.py:347
  23.8 0.0 collective-permute-start.8
  23.8 1.9 %collective-permute-start.7 = (f32[64,256]{1,0:T(8,128)S(1)}, f32[64,256]{1,0:T(8,128)S(1)}, u32[]{:S(2)}, u32[]{:S(2)}) collective-permute-start(f32[64,256]{1,0:T(8,128)S(1)} %get-tuple-element.35.refs_0_), channel_id=1, source_target_pairs={{0,4},{1,5},{2,6},{3,7},{4,0},{5,1},{6,2},{7,3},{8,12},{9,13},{10,... | collective-permute-start | bytes 196616 | tf_op jit(solution)/shard_map/ppermute | solution.py:347
  25.7 1.3 %shard_map.55 = (bf16[256,8192]{1,0:T(8,128)(2,1)S(1)}, bf16[256,8192]{1,0:T(8,128)(2,1)S(1)}, f32[16,256]{1,0:T(8,128)S(1)}, f32[16,256]{1,0:T(8,128)S(1)}, f32...) custom-call(s32[64,128]{1,0:T(8,128)S(1)} %get-tuple-element.39.mask_ids.refs_5_, f32[64,256]{1,0:T(8,128)S(1)} %get-tuple-element.40.mean), custom_call_target="tpu_custom_call" | custom-call | flops 536870912 | bytes 8388608 | tf_op jit(solution)/shard_map/pallas_call | solution.py:470
  27.0 0.1 collective-permute-start.13
  27.1 1.3 %collective-permute-start.14 = (f32[16,256]{1,0:T(8,128)S(1)}, f32[16,256]{1,0:T(8,128)S(1)}, u32[]{:S(2)}, u32[]{:S(2)}) collective-permute-start(f32[16,256]{1,0:T(8,128)S(1)} %get-tuple-element.48), channel_id=1, source_target_pairs={{0,2},{1,3},{2,0},{3,1},{4,6},{5,7},{6,4},{7,5},{8,10},{9,11},{10,... | collective-permute-start | bytes 49160 | tf_op jit(solution)/shard_map/ppermute | solution.py:342
  28.4 0.0 collective-permute-done.9.refs_3_
  28.4 0.5 %collective-permute-start.15 = (f32[16,256]{1,0:T(8,128)S(1)}, f32[16,256]{1,0:T(8,128)S(1)}, u32[]{:S(2)}, u32[]{:S(2)}) collective-permute-start(f32[16,256]{1,0:T(8,128)S(1)} %get-tuple-element.49), channel_id=1, source_target_pairs={{0,3},{1,2},{2,1},{3,0},{4,7},{5,6},{6,5},{7,4},{8,11},{9,10},{10,... | collective-permute-start | bytes 49160 | tf_op jit(solution)/shard_map/ppermute | solution.py:342
  28.9 1.1 %collective-permute-done.8.refs_2_ = f32[64,256]{1,0:T(8,128)S(1)} collective-permute-done((f32[64,256]{1,0:T(8,128)S(1)}, f32[64,256]{1,0:T(8,128)S(1)}, u32[]{:S(2)}, u32[]{:S(2)}) %collective-permute-start.8) | collective-permute-done | bytes 65568 | tf_op jit(solution)/shard_map/ppermute | solution.py:347
  30.1 0.0 collective-permute-done.7.refs_1_
  30.1 0.8 %shard_map.56 = (f32[16,256]{1,0:T(8,128)S(1)}, f32[16,256]{1,0:T(8,128)S(1)}, f32[16,256]{1,0:T(8,128)S(1)}, f32[16,256]{1,0:T(8,128)S(1)}) custom-call(f32[64,256]{1,0:T(8,128)S(1)} %get-tuple-element.35.refs_0_, f32[64,256]{1,0:T(8,128)S(1)} %collective-permute-done.7.refs_1_, f32[64,256]{1,0:T(8,128)S(1)} %collective-permute-done.8.refs_2_, ...), custom_call_target="tpu_custom_call" | custom-call | flops 134217728 | bytes 262144 | tf_op jit(solution)/shard_map/pallas_call | solution.py:481
  30.8 0.0 collective-permute-start.10
  30.8 1.3 %collective-permute-start.11 = (f32[16,256]{1,0:T(8,128)S(1)}, f32[16,256]{1,0:T(8,128)S(1)}, u32[]{:S(2)}, u32[]{:S(2)}) collective-permute-start(f32[16,256]{1,0:T(8,128)S(1)} %get-tuple-element.44), channel_id=1, source_target_pairs={{0,2},{1,3},{2,0},{3,1},{4,6},{5,7},{6,4},{7,5},{8,10},{9,11},{10,... | collective-permute-start | bytes 49160 | tf_op jit(solution)/shard_map/ppermute | solution.py:342
  32.1 0.0 collective-permute-done.13.refs_1_
  32.1 0.6 %collective-permute-start.12 = (f32[16,256]{1,0:T(8,128)S(1)}, f32[16,256]{1,0:T(8,128)S(1)}, u32[]{:S(2)}, u32[]{:S(2)}) collective-permute-start(f32[16,256]{1,0:T(8,128)S(1)} %get-tuple-element.45), channel_id=1, source_target_pairs={{0,3},{1,2},{2,1},{3,0},{4,7},{5,6},{6,5},{7,4},{8,11},{9,10},{10,... | collective-permute-start | bytes 49160 | tf_op jit(solution)/shard_map/ppermute | solution.py:342
  32.7 0.0 collective-permute-done.14.refs_2_
  32.7 0.0 collective-permute-done.15.refs_3_
  32.7 1.3 %shard_map.57.refs_4_ = f32[64,8192]{1,0:T(8,128)S(1)} custom-call(f32[16,256]{1,0:T(8,128)S(1)} %get-tuple-element.46.refs_0_, f32[16,256]{1,0:T(8,128)S(1)} %collective-permute-done.13.refs_1_, f32[16,256]{1,0:T(8,128)S(1)} %collective-permute-done.14.refs_2_, f32[16,256]{1,0:T(8,128)S(1)} %collective-permute-done.15.refs_3_, ...), custom_call_target="tpu_custom_call" | custom-call | flops 536870912 | bytes 4194304 | tf_op jit(solution)/shard_map/pallas_call | solution.py:491
  34.1 0.0 collective-permute-done.10.refs_1_
  34.1 0.5 %collective-permute-done.11.refs_2_ = f32[16,256]{1,0:T(8,128)S(1)} collective-permute-done((f32[16,256]{1,0:T(8,128)S(1)}, f32[16,256]{1,0:T(8,128)S(1)}, u32[]{:S(2)}, u32[]{:S(2)}) %collective-permute-start.11) | collective-permute-done | bytes 16416 | tf_op jit(solution)/shard_map/ppermute | solution.py:342
  34.6 0.7 %collective-permute-done.12.refs_3_ = f32[16,256]{1,0:T(8,128)S(1)} collective-permute-done((f32[16,256]{1,0:T(8,128)S(1)}, f32[16,256]{1,0:T(8,128)S(1)}, u32[]{:S(2)}, u32[]{:S(2)}) %collective-permute-start.12) | collective-permute-done | bytes 16416 | tf_op jit(solution)/shard_map/ppermute | solution.py:342
  35.3 1.6 %shard_map.58 = f32[64,8192]{1,0:T(8,128)} custom-call(f32[16,256]{1,0:T(8,128)S(1)} %get-tuple-element.42.refs_0_, f32[16,256]{1,0:T(8,128)S(1)} %collective-permute-done.10.refs_1_, f32[16,256]{1,0:T(8,128)S(1)} %collective-permute-done.11.refs_2_, f32[16,256]{1,0:T(8,128)S(1)} %collective-permute-done.12.refs_3_, f32[64,8192]{1,0:T(8,128)S(1)} %shard_map.57.refs_4_, ...), custom_call_target="tpu_custom_call" | custom-call | flops 536870912 | bytes 4194304 | tf_op jit(solution)/shard_map/pallas_call | solution.py:500
  (1 shorter events, 0.0 us)
Async XLA Ops:
  3.4 4.4 %collective-permute-start = (f32[56,256]{1,0:T(8,128)S(1)}, f32[56,256]{1,0:T(8,128)S(1)}, u32[]{:S(2)}, u32[]{:S(2)}) collective-permute-start(f32[56,256]{1,0:T(8,128)S(1)} %get-tuple-element.30), channel_id=1, source_target_pairs={{0,1},{1,0},{2,3},{3,2},{4,5},{5,4},{6,7},{7,6},{8,9},{9,8},{10,11... | collective-permute-start | bytes 172040 | tf_op jit(solution)/shard_map/ppermute | solution.py:342
  3.9 5.8 %collective-permute-start.1 = (f32[56,256]{1,0:T(8,128)S(1)}, f32[56,256]{1,0:T(8,128)S(1)}, u32[]{:S(2)}, u32[]{:S(2)}) collective-permute-start(f32[56,256]{1,0:T(8,128)S(1)} %get-tuple-element.31), channel_id=1, source_target_pairs={{0,2},{1,3},{2,0},{3,1},{4,6},{5,7},{6,4},{7,5},{8,10},{9,11},{10,... | collective-permute-start | bytes 172040 | tf_op jit(solution)/shard_map/ppermute | solution.py:342
  6.5 3.3 %collective-permute-start.2 = (f32[24,256]{1,0:T(8,128)S(1)}, f32[24,256]{1,0:T(8,128)S(1)}, u32[]{:S(2)}, u32[]{:S(2)}) collective-permute-start(f32[24,256]{1,0:T(8,128)S(1)} %get-tuple-element.32), channel_id=1, source_target_pairs={{0,3},{1,2},{2,1},{3,0},{4,7},{5,6},{6,5},{7,4},{8,11},{9,10},{10,... | collective-permute-start | bytes 73736 | tf_op jit(solution)/shard_map/ppermute | solution.py:342
  9.8 7.3 %collective-permute-start.5 = (f32[72,256]{1,0:T(8,128)S(1)}, f32[72,256]{1,0:T(8,128)S(1)}, u32[]{:S(2)}, u32[]{:S(2)}) collective-permute-start(f32[72,256]{1,0:T(8,128)S(1)} %shard_map.49.own.one.refs_0_), channel_id=1, source_target_pairs={{0,12},{1,13},{2,14},{3,15},{4,8},{5,9},{6,10},{7,11},{8,4},{9,5},... | collective-permute-start | bytes 221192 | tf_op jit(solution)/shard_map/ppermute | solution.py:347
  13.4 6.5 %collective-permute-start.4 = (f32[72,256]{1,0:T(8,128)S(1)}, f32[72,256]{1,0:T(8,128)S(1)}, u32[]{:S(2)}, u32[]{:S(2)}) collective-permute-start(f32[72,256]{1,0:T(8,128)S(1)} %shard_map.49.own.one.refs_0_), channel_id=1, source_target_pairs={{0,8},{1,9},{2,10},{3,11},{4,12},{5,13},{6,14},{7,15},{8,0},{9,1},... | collective-permute-start | bytes 221192 | tf_op jit(solution)/shard_map/ppermute | solution.py:347
  13.4 6.5 %collective-permute-start.3 = (f32[72,256]{1,0:T(8,128)S(1)}, f32[72,256]{1,0:T(8,128)S(1)}, u32[]{:S(2)}, u32[]{:S(2)}) collective-permute-start(f32[72,256]{1,0:T(8,128)S(1)} %shard_map.49.own.one.refs_0_), channel_id=1, source_target_pairs={{0,4},{1,5},{2,6},{3,7},{4,0},{5,1},{6,2},{7,3},{8,12},{9,13},{10,... | collective-permute-start | bytes 221192 | tf_op jit(solution)/shard_map/ppermute | solution.py:347
  14.5 1.3 %collective-permute-start.6 = (f32[56,256]{1,0:T(8,128)S(1)}, f32[56,256]{1,0:T(8,128)S(1)}, u32[]{:S(2)}, u32[]{:S(2)}) collective-permute-start(f32[56,256]{1,0:T(8,128)S(1)} %get-tuple-element.34), channel_id=1, source_target_pairs={{0,1},{1,0},{2,3},{3,2},{4,5},{5,4},{6,7},{7,6},{8,9},{9,8},{10,11... | collective-permute-start | bytes 172040 | tf_op jit(solution)/shard_map/ppermute | solution.py:452
  21.3 7.1 %collective-permute-start.9 = (f32[64,256]{1,0:T(8,128)S(1)}, f32[64,256]{1,0:T(8,128)S(1)}, u32[]{:S(2)}, u32[]{:S(2)}) collective-permute-start(f32[64,256]{1,0:T(8,128)S(1)} %get-tuple-element.35.refs_0_), channel_id=1, source_target_pairs={{0,12},{1,13},{2,14},{3,15},{4,8},{5,9},{6,10},{7,11},{8,4},{9,5},... | collective-permute-start | bytes 196616 | tf_op jit(solution)/shard_map/ppermute | solution.py:347
  23.8 6.3 %collective-permute-start.8 = (f32[64,256]{1,0:T(8,128)S(1)}, f32[64,256]{1,0:T(8,128)S(1)}, u32[]{:S(2)}, u32[]{:S(2)}) collective-permute-start(f32[64,256]{1,0:T(8,128)S(1)} %get-tuple-element.35.refs_0_), channel_id=1, source_target_pairs={{0,8},{1,9},{2,10},{3,11},{4,12},{5,13},{6,14},{7,15},{8,0},{9,1},... | collective-permute-start | bytes 196616 | tf_op jit(solution)/shard_map/ppermute | solution.py:347
  23.8 6.3 %collective-permute-start.7 = (f32[64,256]{1,0:T(8,128)S(1)}, f32[64,256]{1,0:T(8,128)S(1)}, u32[]{:S(2)}, u32[]{:S(2)}) collective-permute-start(f32[64,256]{1,0:T(8,128)S(1)} %get-tuple-element.35.refs_0_), channel_id=1, source_target_pairs={{0,4},{1,5},{2,6},{3,7},{4,0},{5,1},{6,2},{7,3},{8,12},{9,13},{10,... | collective-permute-start | bytes 196616 | tf_op jit(solution)/shard_map/ppermute | solution.py:347
  27.0 5.1 %collective-permute-start.13 = (f32[16,256]{1,0:T(8,128)S(1)}, f32[16,256]{1,0:T(8,128)S(1)}, u32[]{:S(2)}, u32[]{:S(2)}) collective-permute-start(f32[16,256]{1,0:T(8,128)S(1)} %get-tuple-element.47), channel_id=1, source_target_pairs={{0,1},{1,0},{2,3},{3,2},{4,5},{5,4},{6,7},{7,6},{8,9},{9,8},{10,11... | collective-permute-start | bytes 49160 | tf_op jit(solution)/shard_map/ppermute | solution.py:342
  27.1 5.7 %collective-permute-start.14 = (f32[16,256]{1,0:T(8,128)S(1)}, f32[16,256]{1,0:T(8,128)S(1)}, u32[]{:S(2)}, u32[]{:S(2)}) collective-permute-start(f32[16,256]{1,0:T(8,128)S(1)} %get-tuple-element.48), channel_id=1, source_target_pairs={{0,2},{1,3},{2,0},{3,1},{4,6},{5,7},{6,4},{7,5},{8,10},{9,11},{10,... | collective-permute-start | bytes 49160 | tf_op jit(solution)/shard_map/ppermute | solution.py:342
  28.4 4.3 %collective-permute-start.15 = (f32[16,256]{1,0:T(8,128)S(1)}, f32[16,256]{1,0:T(8,128)S(1)}, u32[]{:S(2)}, u32[]{:S(2)}) collective-permute-start(f32[16,256]{1,0:T(8,128)S(1)} %get-tuple-element.49), channel_id=1, source_target_pairs={{0,3},{1,2},{2,1},{3,0},{4,7},{5,6},{6,5},{7,4},{8,11},{9,10},{10,... | collective-permute-start | bytes 49160 | tf_op jit(solution)/shard_map/ppermute | solution.py:342
  30.8 3.2 %collective-permute-start.10 = (f32[16,256]{1,0:T(8,128)S(1)}, f32[16,256]{1,0:T(8,128)S(1)}, u32[]{:S(2)}, u32[]{:S(2)}) collective-permute-start(f32[16,256]{1,0:T(8,128)S(1)} %get-tuple-element.43), channel_id=1, source_target_pairs={{0,1},{1,0},{2,3},{3,2},{4,5},{5,4},{6,7},{7,6},{8,9},{9,8},{10,11... | collective-permute-start | bytes 49160 | tf_op jit(solution)/shard_map/ppermute | solution.py:342
  30.8 3.8 %collective-permute-start.11 = (f32[16,256]{1,0:T(8,128)S(1)}, f32[16,256]{1,0:T(8,128)S(1)}, u32[]{:S(2)}, u32[]{:S(2)}) collective-permute-start(f32[16,256]{1,0:T(8,128)S(1)} %get-tuple-element.44), channel_id=1, source_target_pairs={{0,2},{1,3},{2,0},{3,1},{4,6},{5,7},{6,4},{7,5},{8,10},{9,11},{10,... | collective-permute-start | bytes 49160 | tf_op jit(solution)/shard_map/ppermute | solution.py:342
  32.1 3.2 %collective-permute-start.12 = (f32[16,256]{1,0:T(8,128)S(1)}, f32[16,256]{1,0:T(8,128)S(1)}, u32[]{:S(2)}, u32[]{:S(2)}) collective-permute-start(f32[16,256]{1,0:T(8,128)S(1)} %get-tuple-element.45), channel_id=1, source_target_pairs={{0,3},{1,2},{2,1},{3,0},{4,7},{5,6},{6,5},{7,4},{8,11},{9,10},{10,... | collective-permute-start | bytes 49160 | tf_op jit(solution)/shard_map/ppermute | solution.py:342

commit v28 on v27

--- a/solution.py
+++ b/solution.py
@@ -103,7 +103,8 @@
 
 
 def sums_kernel(pad, cap, *refs):
-    (probes, lengths_in, ids_in, firms_in), sends, refs = refs[:4], refs[4 : 4 + NEAR], refs[4 + NEAR :]
+    (probes, lengths_in, ids_in, firms_in), sends, slots_out = refs[:4], refs[4 : 4 + NEAR], refs[4 + NEAR]
+    refs = refs[5 + NEAR :]
     x1, mask_ids, weight, valid, x, sums, lengths, ids, firms, bands_sem, small = refs
     bands = [pl.ds(at, 8) for at in range(0, x.shape[0], 8)]
     copies = [pltpu.make_async_copy(probes.at[at], x.at[at], bands_sem.at[b]) for b, at in enumerate(bands)]
@@ -127,8 +128,8 @@
     across = slots // LANES
     rows = ids.shape[0] // across
     masked = jnp.concatenate([masked[k * rows : (k + 1) * rows] for k in range(across)], axis=1).astype(F32)
-    for send in sends[:3]:
-        send[part + 8 :] = masked
+    sends[1][part + 8 :] = masked
+    slots_out[8:] = masked
 
     table = jnp.concatenate([same_worker(pad, 256)] * 2, axis=0)
     wait_all(copies)
@@ -148,6 +149,7 @@
     for step, send in zip(NEAR_STEPS, sends):
         send[:part] = sums[pl.ds(pl.multiple_of((me ^ step) * part, part), part), :]
         send[part : part + 8] = about
+    slots_out[:8] = about
 
 
 def join_kernel(part, *refs):
@@ -157,8 +159,10 @@
         out[part * NEAR + 2 * k : part * NEAR + 2 * k + 2] = one[part : part + 2]
 
 
-def pairs_kernel(pad, start, *refs):
-    parts, (out, ids, size, counts) = refs[:-4], refs[-4:]
+def pairs_kernel(pad, start, several, *refs):
+    parts, (out, *copy, ids, size, counts) = refs[:several], refs[several:]
+    for ref in copy:
+        ref[...] = parts[0][...]
     slots = out.shape[1]
     kind = BF16 if slots <= 256 else F32
     per = LANES // pad
@@ -384,13 +388,15 @@
     whole = (columns, rows_dev)
     about = part + 8
     message = array((about + rows_dev // slots, slots), F32)
+    short = array((about, slots), F32)
+    slots_message = array((message.shape[0] - part, slots), F32)
     of_near = array((columns, slots), F32)
 
-    *sends, x1, mask_ids, weight = call(
+    *sends, own_slots, x1, mask_ids, weight = call(
         functools.partial(sums_kernel, pad, slots // n),
-        [message] * 3 + [array((about, slots), F32), array(whole, F32), array(of_rows, jnp.int32), array(of_rows, F32)],
+        [short, message, short, short, slots_message, array(whole, F32), array(of_rows, jnp.int32), array(of_rows, F32)],
         [hbm] * 4,
-        [vmem] * (NEAR + 3),
+        [vmem] * (NEAR + 4),
         [
             pltpu.VMEM(of_rows, F32),
             pltpu.VMEM(whole, F32),
@@ -405,34 +411,39 @@
         4 * columns * rows_dev,
     )(in_hbm(probes), in_hbm(lengths), in_hbm(ids), in_hbm(firms))
 
-    def pair_counts(parts):
+    def pair_counts(one, start, copy=()):
         return call(
-            functools.partial(pairs_kernel, pad, about),
-            array((len(parts), slots, 2 * slots), BF16),
-            [vmem] * len(parts),
-            vmem,
+            functools.partial(pairs_kernel, pad, start, 1),
+            [array((1, slots, 2 * slots), BF16), *copy],
+            [vmem],
+            [vmem] * (1 + len(copy)),
             [
-                pltpu.VMEM((len(parts), *of_rows), F32),
-                pltpu.VMEM((len(parts), 8, slots), F32),
-                pltpu.VMEM((len(parts), slots, workers), BF16),
+                pltpu.VMEM((1, *of_rows), F32),
+                pltpu.VMEM((1, 8, slots), F32),
+                pltpu.VMEM((1, slots, workers), BF16),
             ],
-            work * len(parts) // 4,
+            work // 4,
             4 * slots * slots,
-        )(*parts)
+        )(one)
+
+    def near_step(one, step):
+        return lax.ppermute(one, "rows", [(i, i ^ step) for i in range(n)])
 
     arrived = near_exchange(sends, n)
-    pairs = [pair_counts(arrived[:1]), pair_counts(arrived[1:2])]
+    own_pairs, own_slots = pair_counts(own_slots, 8, [slots_message])
+    passed = near_step(own_slots, 2)
+    pairs = [own_pairs]
     joined = call(
         functools.partial(join_kernel, part),
         array((columns + 2 * NEAR, slots), F32),
-        [vmem] * (NEAR + 2),
+        [vmem] * (NEAR + 1),
         vmem,
         [],
         0,
         message.size * 8,
     )(*arrived, *pairs)
     shared = far_share(joined, n)
-    tables, passed = [], arrived[2]
+    tables, beside = [], passed
     table = array((tiles, NEAR * LANES, NEAR * LANES), BF16)
 
     def firm_table(one, passed, out):
@@ -447,10 +458,9 @@
         )(joined, one, passed)
 
     if keep:
-        first_table, passed = firm_table(joined, passed, [table, message])
+        first_table, beside = firm_table(joined, passed, [table, slots_message])
         tables = [first_table, *firm_table(shared[-1], first_table, [table])]
-    passed = lax.ppermute(passed, "rows", [(i, i ^ 1) for i in range(n)])
-    pairs += [pair_counts(arrived[2:3]), pair_counts([passed])]
+    pairs += pair_counts(arrived[1], about) + pair_counts(passed, 8) + pair_counts(near_step(beside, 1), 8)
     scale = array((tiles, 8, NEAR * LANES), F32)
     made = [table] * (far - 2) * keep
     mean, sums, scales, *made = call(

time: 37 us -> 36.6 us (0.989)
  waiting for transfers between devices: 5.59 us -> 3.32 us
  starting transfers between devices: 15.9 us -> 17.7 us
    ppermute x1 -> x2, starting transfers between devices: 0.07 us -> 1.87 us  [near_step(): return lax.ppermute(one, 'rows', [(i, i ^ step) for i in range(n)])]
    ppermute x6, waiting for transfers between devices: 3.66 us -> 2.42 us  [far_share(): return [one] + [lax.ppermute(one, 'rows', step) for step in steps]]
    ppermute x9, waiting for transfers between devices: 1.92 us -> 0.9 us  [near_exchange(): lax.ppermute(one, 'rows', step)]
  transfers between devices with their start and end apart: 16 -> 17, of which waited for: 5 -> 5; matrix products, arithmetic and copies ran while one was open for 0% -> 0% of each run, Pallas kernels for 24% -> 24%
where the time goes in v28:
time: 36.6 us; the launch traced here: 36.4 us
  starting transfers between devices  17.7 us (48%)
  Pallas kernels  15.3 us (42%)
  waiting for transfers between devices  3.32 us (9%)
    ppermute x6, starting transfers between devices, far_share(): return [one] + [lax.ppermute(one, 'rows', step) for step in steps]  8.85 us
    ppermute x9, starting transfers between devices, near_exchange(): lax.ppermute(one, 'rows', step)  6.99 us
    pallas_call x4, Pallas kernels, pair_counts(): call(functools.partial(pairs_kernel, pad, start, 1), [array((1, slots, 2...  4.92 us
    pallas_call x1, Pallas kernels, body(): call(functools.partial(sums_kernel, pad, slots // n), [short, message, sh...  3.37 us
    ppermute x6, waiting for transfers between devices, far_share(): return [one] + [lax.ppermute(one, 'rows', step) for step in steps]  2.42 us
    ppermute x2, starting transfers between devices, near_step(): return lax.ppermute(one, 'rows', [(i, i ^ step) for i in range(n)])  1.87 us
    pallas_call x1, Pallas kernels, body(): call(last_kernel, array(whole, F32), [vmem] * (NEAR + 2 + len(spreads[:1]...  1.61 us
    pallas_call x1, Pallas kernels, body(): call(functools.partial(change_kernel, far, part, len(tables)), [of_near,...  1.37 us
  transfers between devices with their start and end apart: 17, of which 5 were waited for; matrix products, arithmetic and copies ran while one was open for 0% of the time, Pallas kernels for 24%

profile of v28, /device:TPU:0, one launch (start us, length us, event | category | flops | bytes accessed | tf_op | source)
XLA Modules:
  0.0 36.4 jit_solution(14718171338923136378)
XLA Ops:
  0.0 3.4 %shard_map.46 = (f32[24,256]{1,0:T(8,128)S(1)}, f32[56,256]{1,0:T(8,128)S(1)}, f32[24,256]{1,0:T(8,128)S(1)}, f32[24,256]{1,0:T(8,128)S(1)}, f32[40,256]{1,0:T(8...) custom-call(f32[64,8192]{1,0:T(8,128)} %refs_0_.1, s32[8,128]{1,0:T(8,128)} %bitcast.4, ...), custom_call_target="tpu_custom_call" | custom-call | flops 1073741824 | bytes 2097152 | tf_op jit(solution)/shard_map/pallas_call | solution.py:395
  3.4 0.5 %collective-permute-start = (f32[56,256]{1,0:T(8,128)S(1)}, f32[56,256]{1,0:T(8,128)S(1)}, u32[]{:S(2)}, u32[]{:S(2)}) collective-permute-start(f32[56,256]{1,0:T(8,128)S(1)} %get-tuple-element.33), channel_id=1, source_target_pairs={{0,1},{1,0},{2,3},{3,2},{4,5},{5,4},{6,7},{7,6},{8,9},{9,8},{10,11... | collective-permute-start | bytes 172040 | tf_op jit(solution)/shard_map/ppermute | solution.py:346
  3.9 2.6 %collective-permute-start.1 = (f32[24,256]{1,0:T(8,128)S(1)}, f32[24,256]{1,0:T(8,128)S(1)}, u32[]{:S(2)}, u32[]{:S(2)}) collective-permute-start(f32[24,256]{1,0:T(8,128)S(1)} %get-tuple-element.34), channel_id=1, source_target_pairs={{0,2},{1,3},{2,0},{3,1},{4,6},{5,7},{6,4},{7,5},{8,10},{9,11},{10,... | collective-permute-start | bytes 73736 | tf_op jit(solution)/shard_map/ppermute | solution.py:346
  6.5 0.1 collective-permute-start.2
  6.6 1.2 %shard_map.47 = (bf16[1,256,512]{2,1,0:T(8,128)(2,1)S(1)}, f32[40,256]{1,0:T(8,128)S(1)}) custom-call(f32[40,256]{1,0:T(8,128)S(1)} %get-tuple-element.36.refs_0_), custom_call_target="tpu_custom_call" | custom-call | flops 134217728 | bytes 262144 | tf_op jit(solution)/shard_map/pallas_call | solution.py:415
  7.8 1.8 %collective-permute-start.6 = (f32[40,256]{1,0:T(8,128)S(1)}, f32[40,256]{1,0:T(8,128)S(1)}, u32[]{:S(2)}, u32[]{:S(2)}) collective-permute-start(f32[40,256]{1,0:T(8,128)S(1)} %get-tuple-element.38), channel_id=1, source_target_pairs={{0,2},{1,3},{2,0},{3,1},{4,6},{5,7},{6,4},{7,5},{8,10},{9,11},{10,... | collective-permute-start | bytes 122888 | tf_op jit(solution)/shard_map/ppermute | solution.py:430
  9.6 0.0 collective-permute-done.1.refs_2_
  9.6 0.2 collective-permute-done.2.refs_3_
  9.7 0.0 collective-permute-done.refs_1_.refs_0_
  9.8 3.7 %collective-permute-start.5 = (f32[72,256]{1,0:T(8,128)S(1)}, f32[72,256]{1,0:T(8,128)S(1)}, u32[]{:S(2)}, u32[]{:S(2)}) collective-permute-start(f32[72,256]{1,0:T(8,128)S(1)} %shard_map.48.own.one.refs_0_), channel_id=1, source_target_pairs={{0,12},{1,13},{2,14},{3,15},{4,8},{5,9},{6,10},{7,11},{8,4},{9,5},... | collective-permute-start | bytes 221192 | tf_op jit(solution)/shard_map/ppermute | solution.py:351
  13.4 0.0 collective-permute-start.4
  13.4 0.8 %collective-permute-start.3 = (f32[72,256]{1,0:T(8,128)S(1)}, f32[72,256]{1,0:T(8,128)S(1)}, u32[]{:S(2)}, u32[]{:S(2)}) collective-permute-start(f32[72,256]{1,0:T(8,128)S(1)} %shard_map.48.own.one.refs_0_), channel_id=1, source_target_pairs={{0,4},{1,5},{2,6},{3,7},{4,0},{5,1},{6,2},{7,3},{8,12},{9,13},{10,... | collective-permute-start | bytes 221192 | tf_op jit(solution)/shard_map/ppermute | solution.py:351
  14.2 0.0 collective-permute-done.6.passed.refs_0_
  14.2 0.3 shard_map.49
  14.5 0.1 collective-permute-start.7
  14.6 1.2 %shard_map.52.refs_8_ = bf16[1,256,512]{2,1,0:T(8,128)(2,1)S(1)} custom-call(f32[40,256]{1,0:T(8,128)S(1)} %collective-permute-done.6.passed.refs_0_), custom_call_target="tpu_custom_call" | custom-call | flops 134217728 | bytes 262144 | tf_op jit(solution)/shard_map/pallas_call | solution.py:415
  15.8 1.2 %shard_map.51.refs_7_ = bf16[1,256,512]{2,1,0:T(8,128)(2,1)S(1)} custom-call(f32[56,256]{1,0:T(8,128)S(1)} %collective-permute-done.refs_1_.refs_0_), custom_call_target="tpu_custom_call" | custom-call | flops 134217728 | bytes 262144 | tf_op jit(solution)/shard_map/pallas_call | solution.py:415
  17.1 0.0 collective-permute-done.7.refs_0_
  17.1 1.2 %shard_map.53.refs_9_ = bf16[1,256,512]{2,1,0:T(8,128)(2,1)S(1)} custom-call(f32[40,256]{1,0:T(8,128)S(1)} %collective-permute-done.7.refs_0_), custom_call_target="tpu_custom_call" | custom-call | flops 134217728 | bytes 262144 | tf_op jit(solution)/shard_map/pallas_call | solution.py:415
  18.3 0.0 collective-permute-done.5.one.refs_3_
  18.3 0.3 shard_map.50.refs_5_.refs_7_
  18.7 1.3 %collective-permute-done.4.refs_2_ = f32[72,256]{1,0:T(8,128)S(1)} collective-permute-done((f32[72,256]{1,0:T(8,128)S(1)}, f32[72,256]{1,0:T(8,128)S(1)}, u32[]{:S(2)}, u32[]{:S(2)}) %collective-permute-start.4) | collective-permute-done | bytes 73760 | tf_op jit(solution)/shard_map/ppermute | solution.py:351
  19.9 0.0 collective-permute-done.3.refs_1_
  19.9 1.4 %shard_map.54 = (f32[64,256]{1,0:T(8,128)S(1)}, f32[64,256]{1,0:T(8,128)S(1)}, f32[2,8,512]{2,1,0:T(8,128)S(1)}, bf16[2,512,512]{2,1,0:T(8,128)(2,1)S(1)}, bf16[2,512,512]{2,1,0:T(8,128)(2,1)S(1)}) custom-call(f32[72,256]{1,0:T(8,128)S(1)} %shard_map.48.own.one.refs_0_, f32[72,256]{1,0:T(8,128)S(1)} %collective-permute-done.3.refs_1_, ...), custom_call_target="tpu_custom_call" | custom-call | flops 134217728 | bytes 262144 | tf_op jit(solution)/shard_map/pallas_call | solution.py:466
  21.3 2.5 %collective-permute-start.10 = (f32[64,256]{1,0:T(8,128)S(1)}, f32[64,256]{1,0:T(8,128)S(1)}, u32[]{:S(2)}, u32[]{:S(2)}) collective-permute-start(f32[64,256]{1,0:T(8,128)S(1)} %get-tuple-element.41.refs_0_), channel_id=1, source_target_pairs={{0,12},{1,13},{2,14},{3,15},{4,8},{5,9},{6,10},{7,11},{8,4},{9,5},... | collective-permute-start | bytes 196616 | tf_op jit(solution)/shard_map/ppermute | solution.py:351
  23.8 0.0 collective-permute-start.9
  23.8 1.9 %collective-permute-start.8 = (f32[64,256]{1,0:T(8,128)S(1)}, f32[64,256]{1,0:T(8,128)S(1)}, u32[]{:S(2)}, u32[]{:S(2)}) collective-permute-start(f32[64,256]{1,0:T(8,128)S(1)} %get-tuple-element.41.refs_0_), channel_id=1, source_target_pairs={{0,4},{1,5},{2,6},{3,7},{4,0},{5,1},{6,2},{7,3},{8,12},{9,13},{10,... | collective-permute-start | bytes 196616 | tf_op jit(solution)/shard_map/ppermute | solution.py:351
  25.7 1.3 %shard_map.55 = (bf16[256,8192]{1,0:T(8,128)(2,1)S(1)}, bf16[256,8192]{1,0:T(8,128)(2,1)S(1)}, f32[16,256]{1,0:T(8,128)S(1)}, f32[16,256]{1,0:T(8,128)S(1)}, f32...) custom-call(s32[64,128]{1,0:T(8,128)S(1)} %get-tuple-element.45.mask_ids.refs_5_, f32[64,256]{1,0:T(8,128)S(1)} %get-tuple-element.46.mean), custom_call_target="tpu_custom_call" | custom-call | flops 536870912 | bytes 8388608 | tf_op jit(solution)/shard_map/pallas_call | solution.py:480
  27.0 0.1 collective-permute-start.14
  27.1 0.8 %collective-permute-start.15 = (f32[16,256]{1,0:T(8,128)S(1)}, f32[16,256]{1,0:T(8,128)S(1)}, u32[]{:S(2)}, u32[]{:S(2)}) collective-permute-start(f32[16,256]{1,0:T(8,128)S(1)} %get-tuple-element.54), channel_id=1, source_target_pairs={{0,2},{1,3},{2,0},{3,1},{4,6},{5,7},{6,4},{7,5},{8,10},{9,11},{10,... | collective-permute-start | bytes 49160 | tf_op jit(solution)/shard_map/ppermute | solution.py:346
  27.9 0.0 collective-permute-done.10.refs_3_
  27.9 1.0 %collective-permute-start.16 = (f32[16,256]{1,0:T(8,128)S(1)}, f32[16,256]{1,0:T(8,128)S(1)}, u32[]{:S(2)}, u32[]{:S(2)}) collective-permute-start(f32[16,256]{1,0:T(8,128)S(1)} %get-tuple-element.55), channel_id=1, source_target_pairs={{0,3},{1,2},{2,1},{3,0},{4,7},{5,6},{6,5},{7,4},{8,11},{9,10},{10,... | collective-permute-start | bytes 49160 | tf_op jit(solution)/shard_map/ppermute | solution.py:346
  28.9 1.1 %collective-permute-done.9.refs_2_ = f32[64,256]{1,0:T(8,128)S(1)} collective-permute-done((f32[64,256]{1,0:T(8,128)S(1)}, f32[64,256]{1,0:T(8,128)S(1)}, u32[]{:S(2)}, u32[]{:S(2)}) %collective-permute-start.9) | collective-permute-done | bytes 65568 | tf_op jit(solution)/shard_map/ppermute | solution.py:351
  30.1 0.0 collective-permute-done.8.refs_1_
  30.1 0.8 %shard_map.56 = (f32[16,256]{1,0:T(8,128)S(1)}, f32[16,256]{1,0:T(8,128)S(1)}, f32[16,256]{1,0:T(8,128)S(1)}, f32[16,256]{1,0:T(8,128)S(1)}) custom-call(f32[64,256]{1,0:T(8,128)S(1)} %get-tuple-element.41.refs_0_, f32[64,256]{1,0:T(8,128)S(1)} %collective-permute-done.8.refs_1_, f32[64,256]{1,0:T(8,128)S(1)} %collective-permute-done.9.refs_2_, ...), custom_call_target="tpu_custom_call" | custom-call | flops 134217728 | bytes 262144 | tf_op jit(solution)/shard_map/pallas_call | solution.py:491
  30.8 0.0 collective-permute-start.11
  30.8 0.8 %collective-permute-start.12 = (f32[16,256]{1,0:T(8,128)S(1)}, f32[16,256]{1,0:T(8,128)S(1)}, u32[]{:S(2)}, u32[]{:S(2)}) collective-permute-start(f32[16,256]{1,0:T(8,128)S(1)} %get-tuple-element.50), channel_id=1, source_target_pairs={{0,2},{1,3},{2,0},{3,1},{4,6},{5,7},{6,4},{7,5},{8,10},{9,11},{10,... | collective-permute-start | bytes 49160 | tf_op jit(solution)/shard_map/ppermute | solution.py:346
  31.6 0.0 collective-permute-done.14.refs_1_
  31.6 1.1 %collective-permute-start.13 = (f32[16,256]{1,0:T(8,128)S(1)}, f32[16,256]{1,0:T(8,128)S(1)}, u32[]{:S(2)}, u32[]{:S(2)}) collective-permute-start(f32[16,256]{1,0:T(8,128)S(1)} %get-tuple-element.51), channel_id=1, source_target_pairs={{0,3},{1,2},{2,1},{3,0},{4,7},{5,6},{6,5},{7,4},{8,11},{9,10},{10,... | collective-permute-start | bytes 49160 | tf_op jit(solution)/shard_map/ppermute | solution.py:346
  32.7 0.0 collective-permute-done.15.refs_2_
  32.7 0.0 collective-permute-done.16.refs_3_
  32.7 1.3 %shard_map.57.refs_4_ = f32[64,8192]{1,0:T(8,128)S(1)} custom-call(f32[16,256]{1,0:T(8,128)S(1)} %get-tuple-element.52.refs_0_, f32[16,256]{1,0:T(8,128)S(1)} %collective-permute-done.14.refs_1_, f32[16,256]{1,0:T(8,128)S(1)} %collective-permute-done.15.refs_2_, f32[16,256]{1,0:T(8,128)S(1)} %collective-permute-done.16.refs_3_, ...), custom_call_target="tpu_custom_call" | custom-call | flops 536870912 | bytes 4194304 | tf_op jit(solution)/shard_map/pallas_call | solution.py:501
  34.1 0.0 collective-permute-done.11.refs_1_
  34.1 0.6 %collective-permute-done.12.refs_2_ = f32[16,256]{1,0:T(8,128)S(1)} collective-permute-done((f32[16,256]{1,0:T(8,128)S(1)}, f32[16,256]{1,0:T(8,128)S(1)}, u32[]{:S(2)}, u32[]{:S(2)}) %collective-permute-start.12) | collective-permute-done | bytes 16416 | tf_op jit(solution)/shard_map/ppermute | solution.py:346
  34.6 0.1 collective-permute-done.13.refs_3_
  34.8 1.6 %shard_map.58 = f32[64,8192]{1,0:T(8,128)} custom-call(f32[16,256]{1,0:T(8,128)S(1)} %get-tuple-element.48.refs_0_, f32[16,256]{1,0:T(8,128)S(1)} %collective-permute-done.11.refs_1_, f32[16,256]{1,0:T(8,128)S(1)} %collective-permute-done.12.refs_2_, f32[16,256]{1,0:T(8,128)S(1)} %collective-permute-done.13.refs_3_, f32[64,8192]{1,0:T(8,128)S(1)} %shard_map.57.refs_4_, ...), custom_call_target="tpu_custom_call" | custom-call | flops 536870912 | bytes 4194304 | tf_op jit(solution)/shard_map/pallas_call | solution.py:510
  (1 shorter events, 0.0 us)
Async XLA Ops:
  3.4 6.4 %collective-permute-start = (f32[56,256]{1,0:T(8,128)S(1)}, f32[56,256]{1,0:T(8,128)S(1)}, u32[]{:S(2)}, u32[]{:S(2)}) collective-permute-start(f32[56,256]{1,0:T(8,128)S(1)} %get-tuple-element.33), channel_id=1, source_target_pairs={{0,1},{1,0},{2,3},{3,2},{4,5},{5,4},{6,7},{7,6},{8,9},{9,8},{10,11... | collective-permute-start | bytes 172040 | tf_op jit(solution)/shard_map/ppermute | solution.py:346
  3.9 5.7 %collective-permute-start.1 = (f32[24,256]{1,0:T(8,128)S(1)}, f32[24,256]{1,0:T(8,128)S(1)}, u32[]{:S(2)}, u32[]{:S(2)}) collective-permute-start(f32[24,256]{1,0:T(8,128)S(1)} %get-tuple-element.34), channel_id=1, source_target_pairs={{0,2},{1,3},{2,0},{3,1},{4,6},{5,7},{6,4},{7,5},{8,10},{9,11},{10,... | collective-permute-start | bytes 73736 | tf_op jit(solution)/shard_map/ppermute | solution.py:346
  6.5 3.3 %collective-permute-start.2 = (f32[24,256]{1,0:T(8,128)S(1)}, f32[24,256]{1,0:T(8,128)S(1)}, u32[]{:S(2)}, u32[]{:S(2)}) collective-permute-start(f32[24,256]{1,0:T(8,128)S(1)} %get-tuple-element.35), channel_id=1, source_target_pairs={{0,3},{1,2},{2,1},{3,0},{4,7},{5,6},{6,5},{7,4},{8,11},{9,10},{10,... | collective-permute-start | bytes 73736 | tf_op jit(solution)/shard_map/ppermute | solution.py:346
  7.8 6.4 %collective-permute-start.6 = (f32[40,256]{1,0:T(8,128)S(1)}, f32[40,256]{1,0:T(8,128)S(1)}, u32[]{:S(2)}, u32[]{:S(2)}) collective-permute-start(f32[40,256]{1,0:T(8,128)S(1)} %get-tuple-element.38), channel_id=1, source_target_pairs={{0,2},{1,3},{2,0},{3,1},{4,6},{5,7},{6,4},{7,5},{8,10},{9,11},{10,... | collective-permute-start | bytes 122888 | tf_op jit(solution)/shard_map/ppermute | solution.py:430
  9.8 8.6 %collective-permute-start.5 = (f32[72,256]{1,0:T(8,128)S(1)}, f32[72,256]{1,0:T(8,128)S(1)}, u32[]{:S(2)}, u32[]{:S(2)}) collective-permute-start(f32[72,256]{1,0:T(8,128)S(1)} %shard_map.48.own.one.refs_0_), channel_id=1, source_target_pairs={{0,12},{1,13},{2,14},{3,15},{4,8},{5,9},{6,10},{7,11},{8,4},{9,5},... | collective-permute-start | bytes 221192 | tf_op jit(solution)/shard_map/ppermute | solution.py:351
  13.4 6.5 %collective-permute-start.4 = (f32[72,256]{1,0:T(8,128)S(1)}, f32[72,256]{1,0:T(8,128)S(1)}, u32[]{:S(2)}, u32[]{:S(2)}) collective-permute-start(f32[72,256]{1,0:T(8,128)S(1)} %shard_map.48.own.one.refs_0_), channel_id=1, source_target_pairs={{0,8},{1,9},{2,10},{3,11},{4,12},{5,13},{6,14},{7,15},{8,0},{9,1},... | collective-permute-start | bytes 221192 | tf_op jit(solution)/shard_map/ppermute | solution.py:351
  13.4 6.5 %collective-permute-start.3 = (f32[72,256]{1,0:T(8,128)S(1)}, f32[72,256]{1,0:T(8,128)S(1)}, u32[]{:S(2)}, u32[]{:S(2)}) collective-permute-start(f32[72,256]{1,0:T(8,128)S(1)} %shard_map.48.own.one.refs_0_), channel_id=1, source_target_pairs={{0,4},{1,5},{2,6},{3,7},{4,0},{5,1},{6,2},{7,3},{8,12},{9,13},{10,... | collective-permute-start | bytes 221192 | tf_op jit(solution)/shard_map/ppermute | solution.py:351
  14.5 2.6 %collective-permute-start.7 = (f32[40,256]{1,0:T(8,128)S(1)}, f32[40,256]{1,0:T(8,128)S(1)}, u32[]{:S(2)}, u32[]{:S(2)}) collective-permute-start(f32[40,256]{1,0:T(8,128)S(1)} %get-tuple-element.40), channel_id=1, source_target_pairs={{0,1},{1,0},{2,3},{3,2},{4,5},{5,4},{6,7},{7,6},{8,9},{9,8},{10,11... | collective-permute-start | bytes 122888 | tf_op jit(solution)/shard_map/ppermute | solution.py:430
  21.3 6.6 %collective-permute-start.10 = (f32[64,256]{1,0:T(8,128)S(1)}, f32[64,256]{1,0:T(8,128)S(1)}, u32[]{:S(2)}, u32[]{:S(2)}) collective-permute-start(f32[64,256]{1,0:T(8,128)S(1)} %get-tuple-element.41.refs_0_), channel_id=1, source_target_pairs={{0,12},{1,13},{2,14},{3,15},{4,8},{5,9},{6,10},{7,11},{8,4},{9,5},... | collective-permute-start | bytes 196616 | tf_op jit(solution)/shard_map/ppermute | solution.py:351
  23.8 6.3 %collective-permute-start.9 = (f32[64,256]{1,0:T(8,128)S(1)}, f32[64,256]{1,0:T(8,128)S(1)}, u32[]{:S(2)}, u32[]{:S(2)}) collective-permute-start(f32[64,256]{1,0:T(8,128)S(1)} %get-tuple-element.41.refs_0_), channel_id=1, source_target_pairs={{0,8},{1,9},{2,10},{3,11},{4,12},{5,13},{6,14},{7,15},{8,0},{9,1},... | collective-permute-start | bytes 196616 | tf_op jit(solution)/shard_map/ppermute | solution.py:351
  23.8 6.3 %collective-permute-start.8 = (f32[64,256]{1,0:T(8,128)S(1)}, f32[64,256]{1,0:T(8,128)S(1)}, u32[]{:S(2)}, u32[]{:S(2)}) collective-permute-start(f32[64,256]{1,0:T(8,128)S(1)} %get-tuple-element.41.refs_0_), channel_id=1, source_target_pairs={{0,4},{1,5},{2,6},{3,7},{4,0},{5,1},{6,2},{7,3},{8,12},{9,13},{10,... | collective-permute-start | bytes 196616 | tf_op jit(solution)/shard_map/ppermute | solution.py:351
  27.0 4.6 %collective-permute-start.14 = (f32[16,256]{1,0:T(8,128)S(1)}, f32[16,256]{1,0:T(8,128)S(1)}, u32[]{:S(2)}, u32[]{:S(2)}) collective-permute-start(f32[16,256]{1,0:T(8,128)S(1)} %get-tuple-element.53), channel_id=1, source_target_pairs={{0,1},{1,0},{2,3},{3,2},{4,5},{5,4},{6,7},{7,6},{8,9},{9,8},{10,11... | collective-permute-start | bytes 49160 | tf_op jit(solution)/shard_map/ppermute | solution.py:346
  27.1 5.7 %collective-permute-start.15 = (f32[16,256]{1,0:T(8,128)S(1)}, f32[16,256]{1,0:T(8,128)S(1)}, u32[]{:S(2)}, u32[]{:S(2)}) collective-permute-start(f32[16,256]{1,0:T(8,128)S(1)} %get-tuple-element.54), channel_id=1, source_target_pairs={{0,2},{1,3},{2,0},{3,1},{4,6},{5,7},{6,4},{7,5},{8,10},{9,11},{10,... | collective-permute-start | bytes 49160 | tf_op jit(solution)/shard_map/ppermute | solution.py:346
  27.9 4.8 %collective-permute-start.16 = (f32[16,256]{1,0:T(8,128)S(1)}, f32[16,256]{1,0:T(8,128)S(1)}, u32[]{:S(2)}, u32[]{:S(2)}) collective-permute-start(f32[16,256]{1,0:T(8,128)S(1)} %get-tuple-element.55), channel_id=1, source_target_pairs={{0,3},{1,2},{2,1},{3,0},{4,7},{5,6},{6,5},{7,4},{8,11},{9,10},{10,... | collective-permute-start | bytes 49160 | tf_op jit(solution)/shard_map/ppermute | solution.py:346
  30.8 3.2 %collective-permute-start.11 = (f32[16,256]{1,0:T(8,128)S(1)}, f32[16,256]{1,0:T(8,128)S(1)}, u32[]{:S(2)}, u32[]{:S(2)}) collective-permute-start(f32[16,256]{1,0:T(8,128)S(1)} %get-tuple-element.49), channel_id=1, source_target_pairs={{0,1},{1,0},{2,3},{3,2},{4,5},{5,4},{6,7},{7,6},{8,9},{9,8},{10,11... | collective-permute-start | bytes 49160 | tf_op jit(solution)/shard_map/ppermute | solution.py:346
  30.8 3.8 %collective-permute-start.12 = (f32[16,256]{1,0:T(8,128)S(1)}, f32[16,256]{1,0:T(8,128)S(1)}, u32[]{:S(2)}, u32[]{:S(2)}) collective-permute-start(f32[16,256]{1,0:T(8,128)S(1)} %get-tuple-element.50), channel_id=1, source_target_pairs={{0,2},{1,3},{2,0},{3,1},{4,6},{5,7},{6,4},{7,5},{8,10},{9,11},{10,... | collective-permute-start | bytes 49160 | tf_op jit(solution)/shard_map/ppermute | solution.py:346
  31.6 3.2 %collective-permute-start.13 = (f32[16,256]{1,0:T(8,128)S(1)}, f32[16,256]{1,0:T(8,128)S(1)}, u32[]{:S(2)}, u32[]{:S(2)}) collective-permute-start(f32[16,256]{1,0:T(8,128)S(1)} %get-tuple-element.51), channel_id=1, source_target_pairs={{0,3},{1,2},{2,1},{3,0},{4,7},{5,6},{6,5},{7,4},{8,11},{9,10},{10,... | collective-permute-start | bytes 49160 | tf_op jit(solution)/shard_map/ppermute | solution.py:346

commit v29 on v28

--- a/solution.py
+++ b/solution.py
@@ -159,7 +159,7 @@
         out[part * NEAR + 2 * k : part * NEAR + 2 * k + 2] = one[part : part + 2]
 
 
-def pairs_kernel(pad, start, several, *refs):
+def pairs_kernel(pad, several, *refs):
     parts, (out, *copy, ids, size, counts) = refs[:several], refs[several:]
     for ref in copy:
         ref[...] = parts[0][...]
@@ -170,6 +170,7 @@
     across = slots // LANES
     rows = total_rows // across
     for k, part in enumerate(parts):
+        start = part.shape[0] - rows
         size[k] = jnp.broadcast_to(part[start - 7 : start - 6], (8, slots))
         for at in range(across):
             ids[k, at * rows : (at + 1) * rows] = part[start:, at * LANES : (at + 1) * LANES]
@@ -241,8 +242,9 @@
 
 
 def change_kernel(far, part, ready, *refs):
-    tables, pairs, refs = refs[far : far + ready], refs[far + ready : far + ready + NEAR], refs
-    parts, (mean, sums, scale), made = refs[:far], refs[far + ready + NEAR :][:3], refs[far + ready + NEAR + 3 :]
+    parts, tables, refs = refs[:far], refs[far : far + ready], refs[far + ready :]
+    pairs = [(group, k) for group in refs[:3] for k in range(group.shape[0])]
+    (mean, sums, scale), made = refs[3:6], refs[6:]
     slots = mean.shape[1]
 
     def tile(t, at):
@@ -268,7 +270,7 @@
     for k in range(NEAR):
         cut = slice(part * k, part * (k + 1))
         both = jnp.concatenate(split(mean[cut]), axis=0)
-        change = dot(both, pairs[k][0])
+        change = dot(both, pairs[k][0][pairs[k][1]])
         change = change[:part] + change[part:]
         sums[cut] = parts[0][cut] + (change[:, :slots] + change[:, slots:])
 
@@ -411,26 +413,27 @@
         4 * columns * rows_dev,
     )(in_hbm(probes), in_hbm(lengths), in_hbm(ids), in_hbm(firms))
 
-    def pair_counts(one, start, copy=()):
+    def pair_counts(parts, copy=()):
+        count = len(parts)
         return call(
-            functools.partial(pairs_kernel, pad, start, 1),
-            [array((1, slots, 2 * slots), BF16), *copy],
-            [vmem],
+            functools.partial(pairs_kernel, pad, count),
+            [array((count, slots, 2 * slots), BF16), *copy],
+            [vmem] * count,
             [vmem] * (1 + len(copy)),
             [
-                pltpu.VMEM((1, *of_rows), F32),
-                pltpu.VMEM((1, 8, slots), F32),
-                pltpu.VMEM((1, slots, workers), BF16),
+                pltpu.VMEM((count, *of_rows), F32),
+                pltpu.VMEM((count, 8, slots), F32),
+                pltpu.VMEM((count, slots, workers), BF16),
             ],
-            work // 4,
+            work * count // 4,
             4 * slots * slots,
-        )(one)
+        )(*parts)
 
     def near_step(one, step):
         return lax.ppermute(one, "rows", [(i, i ^ step) for i in range(n)])
 
     arrived = near_exchange(sends, n)
-    own_pairs, own_slots = pair_counts(own_slots, 8, [slots_message])
+    own_pairs, own_slots = pair_counts([own_slots], [slots_message])
     passed = near_step(own_slots, 2)
     pairs = [own_pairs]
     joined = call(
@@ -460,7 +463,7 @@
     if keep:
         first_table, beside = firm_table(joined, passed, [table, slots_message])
         tables = [first_table, *firm_table(shared[-1], first_table, [table])]
-    pairs += pair_counts(arrived[1], about) + pair_counts(passed, 8) + pair_counts(near_step(beside, 1), 8)
+    pairs += pair_counts([arrived[1], passed]) + pair_counts([near_step(beside, 1)])
     scale = array((tiles, 8, NEAR * LANES), F32)
     made = [table] * (far - 2) * keep
     mean, sums, scales, *made = call(

time: 36.6 us -> 36.6 us (level)
  Pallas kernels: 15.3 us -> 14.9 us
  waiting for transfers between devices: 3.32 us -> 3.7 us
    ppermute x6, waiting for transfers between devices: 2.42 us -> 2.8 us  [far_share(): return [one] + [lax.ppermute(one, 'rows', step) for step in steps]]
    pallas_call x4 -> x3, Pallas kernels: 4.92 us -> 4.55 us  [pair_counts(): call(functools.partial(pairs_kernel, pad, count), [array((count, slots, 2...]
  transfers between devices with their start and end apart: 17 -> 17, of which waited for: 5 -> 5; matrix products, arithmetic and copies ran while one was open for 0% -> 0% of each run, Pallas kernels for 24% -> 23%
where the time goes in v29:
time: 36.6 us; the launch traced here: 36.4 us
  starting transfers between devices  17.7 us (48%)
  Pallas kernels  14.9 us (41%)
  waiting for transfers between devices  3.7 us (10%)
    ppermute x6, starting transfers between devices, far_share(): return [one] + [lax.ppermute(one, 'rows', step) for step in steps]  8.85 us
    ppermute x9, starting transfers between devices, near_exchange(): lax.ppermute(one, 'rows', step)  6.99 us
    pallas_call x3, Pallas kernels, pair_counts(): call(functools.partial(pairs_kernel, pad, count), [array((count, slots, 2...  4.55 us
    pallas_call x1, Pallas kernels, body(): call(functools.partial(sums_kernel, pad, slots // n), [short, message, sh...  3.37 us
    ppermute x6, waiting for transfers between devices, far_share(): return [one] + [lax.ppermute(one, 'rows', step) for step in steps]  2.8 us
    ppermute x2, starting transfers between devices, near_step(): return lax.ppermute(one, 'rows', [(i, i ^ step) for i in range(n)])  1.87 us
    pallas_call x1, Pallas kernels, body(): call(last_kernel, array(whole, F32), [vmem] * (NEAR + 2 + len(spreads[:1]...  1.61 us
    pallas_call x1, Pallas kernels, body(): call(functools.partial(change_kernel, far, part, len(tables)), [of_near,...  1.37 us
  transfers between devices with their start and end apart: 17, of which 5 were waited for; matrix products, arithmetic and copies ran while one was open for 0% of the time, Pallas kernels for 23%

profile of v29, /device:TPU:0, one launch (start us, length us, event | category | flops | bytes accessed | tf_op | source)
XLA Modules:
  0.0 36.4 jit_solution(8547000362660562669)
XLA Ops:
  0.0 3.4 %shard_map.46 = (f32[24,256]{1,0:T(8,128)S(1)}, f32[56,256]{1,0:T(8,128)S(1)}, f32[24,256]{1,0:T(8,128)S(1)}, f32[24,256]{1,0:T(8,128)S(1)}, f32[40,256]{1,0:T(8...) custom-call(f32[64,8192]{1,0:T(8,128)} %refs_0_.1, s32[8,128]{1,0:T(8,128)} %bitcast.4, ...), custom_call_target="tpu_custom_call" | custom-call | flops 1073741824 | bytes 2097152 | tf_op jit(solution)/shard_map/pallas_call | solution.py:397
  3.4 0.5 %collective-permute-start = (f32[56,256]{1,0:T(8,128)S(1)}, f32[56,256]{1,0:T(8,128)S(1)}, u32[]{:S(2)}, u32[]{:S(2)}) collective-permute-start(f32[56,256]{1,0:T(8,128)S(1)} %get-tuple-element.33), channel_id=1, source_target_pairs={{0,1},{1,0},{2,3},{3,2},{4,5},{5,4},{6,7},{7,6},{8,9},{9,8},{10,11... | collective-permute-start | bytes 172040 | tf_op jit(solution)/shard_map/ppermute | solution.py:348
  3.9 2.6 %collective-permute-start.1 = (f32[24,256]{1,0:T(8,128)S(1)}, f32[24,256]{1,0:T(8,128)S(1)}, u32[]{:S(2)}, u32[]{:S(2)}) collective-permute-start(f32[24,256]{1,0:T(8,128)S(1)} %get-tuple-element.34), channel_id=1, source_target_pairs={{0,2},{1,3},{2,0},{3,1},{4,6},{5,7},{6,4},{7,5},{8,10},{9,11},{10,... | collective-permute-start | bytes 73736 | tf_op jit(solution)/shard_map/ppermute | solution.py:348
  6.5 0.1 collective-permute-start.2
  6.6 1.2 %shard_map.47 = (bf16[1,256,512]{2,1,0:T(8,128)(2,1)S(1)}, f32[40,256]{1,0:T(8,128)S(1)}) custom-call(f32[40,256]{1,0:T(8,128)S(1)} %get-tuple-element.36.refs_0_), custom_call_target="tpu_custom_call" | custom-call | flops 134217728 | bytes 262144 | tf_op jit(solution)/shard_map/pallas_call | solution.py:418
  7.8 1.8 %collective-permute-start.6 = (f32[40,256]{1,0:T(8,128)S(1)}, f32[40,256]{1,0:T(8,128)S(1)}, u32[]{:S(2)}, u32[]{:S(2)}) collective-permute-start(f32[40,256]{1,0:T(8,128)S(1)} %get-tuple-element.38), channel_id=1, source_target_pairs={{0,2},{1,3},{2,0},{3,1},{4,6},{5,7},{6,4},{7,5},{8,10},{9,11},{10,... | collective-permute-start | bytes 122888 | tf_op jit(solution)/shard_map/ppermute | solution.py:433
  9.6 0.0 collective-permute-done.1.refs_2_
  9.6 0.2 collective-permute-done.2.refs_3_
  9.7 0.0 collective-permute-done.refs_1_.refs_0_
  9.8 3.7 %collective-permute-start.5 = (f32[72,256]{1,0:T(8,128)S(1)}, f32[72,256]{1,0:T(8,128)S(1)}, u32[]{:S(2)}, u32[]{:S(2)}) collective-permute-start(f32[72,256]{1,0:T(8,128)S(1)} %shard_map.48.own.one.refs_0_), channel_id=1, source_target_pairs={{0,12},{1,13},{2,14},{3,15},{4,8},{5,9},{6,10},{7,11},{8,4},{9,5},... | collective-permute-start | bytes 221192 | tf_op jit(solution)/shard_map/ppermute | solution.py:353
  13.4 0.0 collective-permute-start.4
  13.4 0.8 %collective-permute-start.3 = (f32[72,256]{1,0:T(8,128)S(1)}, f32[72,256]{1,0:T(8,128)S(1)}, u32[]{:S(2)}, u32[]{:S(2)}) collective-permute-start(f32[72,256]{1,0:T(8,128)S(1)} %shard_map.48.own.one.refs_0_), channel_id=1, source_target_pairs={{0,4},{1,5},{2,6},{3,7},{4,0},{5,1},{6,2},{7,3},{8,12},{9,13},{10,... | collective-permute-start | bytes 221192 | tf_op jit(solution)/shard_map/ppermute | solution.py:353
  14.2 0.0 collective-permute-done.6.passed.refs_1_
  14.2 0.3 shard_map.49
  14.5 0.1 collective-permute-start.7
  14.6 2.1 %shard_map.51.refs_7_ = bf16[2,256,512]{2,1,0:T(8,128)(2,1)S(1)} custom-call(f32[56,256]{1,0:T(8,128)S(1)} %collective-permute-done.refs_1_.refs_0_, f32[40,256]{1,0:T(8,128)S(1)} %collective-permute-done.6.passed.refs_1_), custom_call_target="tpu_custom_call" | custom-call | flops 268435456 | bytes 262144 | tf_op jit(solution)/shard_map/pallas_call | solution.py:418
  16.7 0.0 collective-permute-done.7.refs_0_
  16.7 1.2 %shard_map.52.refs_8_ = bf16[1,256,512]{2,1,0:T(8,128)(2,1)S(1)} custom-call(f32[40,256]{1,0:T(8,128)S(1)} %collective-permute-done.7.refs_0_), custom_call_target="tpu_custom_call" | custom-call | flops 134217728 | bytes 262144 | tf_op jit(solution)/shard_map/pallas_call | solution.py:418
  18.0 0.0 collective-permute-done.5.one.refs_3_
  18.0 0.3 shard_map.50.refs_5_.refs_7_
  18.3 1.6 %collective-permute-done.4.refs_2_ = f32[72,256]{1,0:T(8,128)S(1)} collective-permute-done((f32[72,256]{1,0:T(8,128)S(1)}, f32[72,256]{1,0:T(8,128)S(1)}, u32[]{:S(2)}, u32[]{:S(2)}) %collective-permute-start.4) | collective-permute-done | bytes 73760 | tf_op jit(solution)/shard_map/ppermute | solution.py:353
  19.9 0.0 collective-permute-done.3.refs_1_
  19.9 1.4 %shard_map.53 = (f32[64,256]{1,0:T(8,128)S(1)}, f32[64,256]{1,0:T(8,128)S(1)}, f32[2,8,512]{2,1,0:T(8,128)S(1)}, bf16[2,512,512]{2,1,0:T(8,128)(2,1)S(1)}, bf16[2,512,512]{2,1,0:T(8,128)(2,1)S(1)}) custom-call(f32[72,256]{1,0:T(8,128)S(1)} %shard_map.48.own.one.refs_0_, f32[72,256]{1,0:T(8,128)S(1)} %collective-permute-done.3.refs_1_, ...), custom_call_target="tpu_custom_call" | custom-call | flops 134217728 | bytes 262144 | tf_op jit(solution)/shard_map/pallas_call | solution.py:469
  21.3 2.5 %collective-permute-start.10 = (f32[64,256]{1,0:T(8,128)S(1)}, f32[64,256]{1,0:T(8,128)S(1)}, u32[]{:S(2)}, u32[]{:S(2)}) collective-permute-start(f32[64,256]{1,0:T(8,128)S(1)} %get-tuple-element.41.refs_0_), channel_id=1, source_target_pairs={{0,12},{1,13},{2,14},{3,15},{4,8},{5,9},{6,10},{7,11},{8,4},{9,5},... | collective-permute-start | bytes 196616 | tf_op jit(solution)/shard_map/ppermute | solution.py:353
  23.8 0.0 collective-permute-start.9
  23.8 1.9 %collective-permute-start.8 = (f32[64,256]{1,0:T(8,128)S(1)}, f32[64,256]{1,0:T(8,128)S(1)}, u32[]{:S(2)}, u32[]{:S(2)}) collective-permute-start(f32[64,256]{1,0:T(8,128)S(1)} %get-tuple-element.41.refs_0_), channel_id=1, source_target_pairs={{0,4},{1,5},{2,6},{3,7},{4,0},{5,1},{6,2},{7,3},{8,12},{9,13},{10,... | collective-permute-start | bytes 196616 | tf_op jit(solution)/shard_map/ppermute | solution.py:353
  25.7 1.3 %shard_map.54 = (bf16[256,8192]{1,0:T(8,128)(2,1)S(1)}, bf16[256,8192]{1,0:T(8,128)(2,1)S(1)}, f32[16,256]{1,0:T(8,128)S(1)}, f32[16,256]{1,0:T(8,128)S(1)}, f32...) custom-call(s32[64,128]{1,0:T(8,128)S(1)} %get-tuple-element.45.mask_ids.refs_5_, f32[64,256]{1,0:T(8,128)S(1)} %get-tuple-element.46.mean), custom_call_target="tpu_custom_call" | custom-call | flops 536870912 | bytes 8388608 | tf_op jit(solution)/shard_map/pallas_call | solution.py:483
  27.0 0.1 collective-permute-start.14
  27.1 0.8 %collective-permute-start.15 = (f32[16,256]{1,0:T(8,128)S(1)}, f32[16,256]{1,0:T(8,128)S(1)}, u32[]{:S(2)}, u32[]{:S(2)}) collective-permute-start(f32[16,256]{1,0:T(8,128)S(1)} %get-tuple-element.54), channel_id=1, source_target_pairs={{0,2},{1,3},{2,0},{3,1},{4,6},{5,7},{6,4},{7,5},{8,10},{9,11},{10,... | collective-permute-start | bytes 49160 | tf_op jit(solution)/shard_map/ppermute | solution.py:348
  27.9 0.0 collective-permute-done.10.refs_3_
  27.9 1.0 %collective-permute-start.16 = (f32[16,256]{1,0:T(8,128)S(1)}, f32[16,256]{1,0:T(8,128)S(1)}, u32[]{:S(2)}, u32[]{:S(2)}) collective-permute-start(f32[16,256]{1,0:T(8,128)S(1)} %get-tuple-element.55), channel_id=1, source_target_pairs={{0,3},{1,2},{2,1},{3,0},{4,7},{5,6},{6,5},{7,4},{8,11},{9,10},{10,... | collective-permute-start | bytes 49160 | tf_op jit(solution)/shard_map/ppermute | solution.py:348
  28.9 1.1 %collective-permute-done.9.refs_2_ = f32[64,256]{1,0:T(8,128)S(1)} collective-permute-done((f32[64,256]{1,0:T(8,128)S(1)}, f32[64,256]{1,0:T(8,128)S(1)}, u32[]{:S(2)}, u32[]{:S(2)}) %collective-permute-start.9) | collective-permute-done | bytes 65568 | tf_op jit(solution)/shard_map/ppermute | solution.py:353
  30.1 0.0 collective-permute-done.8.refs_1_
  30.1 0.8 %shard_map.55 = (f32[16,256]{1,0:T(8,128)S(1)}, f32[16,256]{1,0:T(8,128)S(1)}, f32[16,256]{1,0:T(8,128)S(1)}, f32[16,256]{1,0:T(8,128)S(1)}) custom-call(f32[64,256]{1,0:T(8,128)S(1)} %get-tuple-element.41.refs_0_, f32[64,256]{1,0:T(8,128)S(1)} %collective-permute-done.8.refs_1_, f32[64,256]{1,0:T(8,128)S(1)} %collective-permute-done.9.refs_2_, ...), custom_call_target="tpu_custom_call" | custom-call | flops 134217728 | bytes 262144 | tf_op jit(solution)/shard_map/pallas_call | solution.py:494
  30.8 0.0 collective-permute-start.11
  30.8 0.8 %collective-permute-start.12 = (f32[16,256]{1,0:T(8,128)S(1)}, f32[16,256]{1,0:T(8,128)S(1)}, u32[]{:S(2)}, u32[]{:S(2)}) collective-permute-start(f32[16,256]{1,0:T(8,128)S(1)} %get-tuple-element.50), channel_id=1, source_target_pairs={{0,2},{1,3},{2,0},{3,1},{4,6},{5,7},{6,4},{7,5},{8,10},{9,11},{10,... | collective-permute-start | bytes 49160 | tf_op jit(solution)/shard_map/ppermute | solution.py:348
  31.6 0.0 collective-permute-done.14.refs_1_
  31.6 1.1 %collective-permute-start.13 = (f32[16,256]{1,0:T(8,128)S(1)}, f32[16,256]{1,0:T(8,128)S(1)}, u32[]{:S(2)}, u32[]{:S(2)}) collective-permute-start(f32[16,256]{1,0:T(8,128)S(1)} %get-tuple-element.51), channel_id=1, source_target_pairs={{0,3},{1,2},{2,1},{3,0},{4,7},{5,6},{6,5},{7,4},{8,11},{9,10},{10,... | collective-permute-start | bytes 49160 | tf_op jit(solution)/shard_map/ppermute | solution.py:348
  32.7 0.0 collective-permute-done.15.refs_2_
  32.7 0.0 collective-permute-done.16.refs_3_
  32.7 1.3 %shard_map.56.refs_4_ = f32[64,8192]{1,0:T(8,128)S(1)} custom-call(f32[16,256]{1,0:T(8,128)S(1)} %get-tuple-element.52.refs_0_, f32[16,256]{1,0:T(8,128)S(1)} %collective-permute-done.14.refs_1_, f32[16,256]{1,0:T(8,128)S(1)} %collective-permute-done.15.refs_2_, f32[16,256]{1,0:T(8,128)S(1)} %collective-permute-done.16.refs_3_, ...), custom_call_target="tpu_custom_call" | custom-call | flops 536870912 | bytes 4194304 | tf_op jit(solution)/shard_map/pallas_call | solution.py:504
  34.1 0.0 collective-permute-done.11.refs_1_
  34.1 0.6 %collective-permute-done.12.refs_2_ = f32[16,256]{1,0:T(8,128)S(1)} collective-permute-done((f32[16,256]{1,0:T(8,128)S(1)}, f32[16,256]{1,0:T(8,128)S(1)}, u32[]{:S(2)}, u32[]{:S(2)}) %collective-permute-start.12) | collective-permute-done | bytes 16416 | tf_op jit(solution)/shard_map/ppermute | solution.py:348
  34.6 0.1 collective-permute-done.13.refs_3_
  34.8 1.6 %shard_map.57 = f32[64,8192]{1,0:T(8,128)} custom-call(f32[16,256]{1,0:T(8,128)S(1)} %get-tuple-element.48.refs_0_, f32[16,256]{1,0:T(8,128)S(1)} %collective-permute-done.11.refs_1_, f32[16,256]{1,0:T(8,128)S(1)} %collective-permute-done.12.refs_2_, f32[16,256]{1,0:T(8,128)S(1)} %collective-permute-done.13.refs_3_, f32[64,8192]{1,0:T(8,128)S(1)} %shard_map.56.refs_4_, ...), custom_call_target="tpu_custom_call" | custom-call | flops 536870912 | bytes 4194304 | tf_op jit(solution)/shard_map/pallas_call | solution.py:513
  (1 shorter events, 0.0 us)
Async XLA Ops:
  3.4 6.4 %collective-permute-start = (f32[56,256]{1,0:T(8,128)S(1)}, f32[56,256]{1,0:T(8,128)S(1)}, u32[]{:S(2)}, u32[]{:S(2)}) collective-permute-start(f32[56,256]{1,0:T(8,128)S(1)} %get-tuple-element.33), channel_id=1, source_target_pairs={{0,1},{1,0},{2,3},{3,2},{4,5},{5,4},{6,7},{7,6},{8,9},{9,8},{10,11... | collective-permute-start | bytes 172040 | tf_op jit(solution)/shard_map/ppermute | solution.py:348
  3.9 5.7 %collective-permute-start.1 = (f32[24,256]{1,0:T(8,128)S(1)}, f32[24,256]{1,0:T(8,128)S(1)}, u32[]{:S(2)}, u32[]{:S(2)}) collective-permute-start(f32[24,256]{1,0:T(8,128)S(1)} %get-tuple-element.34), channel_id=1, source_target_pairs={{0,2},{1,3},{2,0},{3,1},{4,6},{5,7},{6,4},{7,5},{8,10},{9,11},{10,... | collective-permute-start | bytes 73736 | tf_op jit(solution)/shard_map/ppermute | solution.py:348
  6.5 3.3 %collective-permute-start.2 = (f32[24,256]{1,0:T(8,128)S(1)}, f32[24,256]{1,0:T(8,128)S(1)}, u32[]{:S(2)}, u32[]{:S(2)}) collective-permute-start(f32[24,256]{1,0:T(8,128)S(1)} %get-tuple-element.35), channel_id=1, source_target_pairs={{0,3},{1,2},{2,1},{3,0},{4,7},{5,6},{6,5},{7,4},{8,11},{9,10},{10,... | collective-permute-start | bytes 73736 | tf_op jit(solution)/shard_map/ppermute | solution.py:348
  7.8 6.4 %collective-permute-start.6 = (f32[40,256]{1,0:T(8,128)S(1)}, f32[40,256]{1,0:T(8,128)S(1)}, u32[]{:S(2)}, u32[]{:S(2)}) collective-permute-start(f32[40,256]{1,0:T(8,128)S(1)} %get-tuple-element.38), channel_id=1, source_target_pairs={{0,2},{1,3},{2,0},{3,1},{4,6},{5,7},{6,4},{7,5},{8,10},{9,11},{10,... | collective-permute-start | bytes 122888 | tf_op jit(solution)/shard_map/ppermute | solution.py:433
  9.8 8.2 %collective-permute-start.5 = (f32[72,256]{1,0:T(8,128)S(1)}, f32[72,256]{1,0:T(8,128)S(1)}, u32[]{:S(2)}, u32[]{:S(2)}) collective-permute-start(f32[72,256]{1,0:T(8,128)S(1)} %shard_map.48.own.one.refs_0_), channel_id=1, source_target_pairs={{0,12},{1,13},{2,14},{3,15},{4,8},{5,9},{6,10},{7,11},{8,4},{9,5},... | collective-permute-start | bytes 221192 | tf_op jit(solution)/shard_map/ppermute | solution.py:353
  13.4 6.5 %collective-permute-start.4 = (f32[72,256]{1,0:T(8,128)S(1)}, f32[72,256]{1,0:T(8,128)S(1)}, u32[]{:S(2)}, u32[]{:S(2)}) collective-permute-start(f32[72,256]{1,0:T(8,128)S(1)} %shard_map.48.own.one.refs_0_), channel_id=1, source_target_pairs={{0,8},{1,9},{2,10},{3,11},{4,12},{5,13},{6,14},{7,15},{8,0},{9,1},... | collective-permute-start | bytes 221192 | tf_op jit(solution)/shard_map/ppermute | solution.py:353
  13.4 6.5 %collective-permute-start.3 = (f32[72,256]{1,0:T(8,128)S(1)}, f32[72,256]{1,0:T(8,128)S(1)}, u32[]{:S(2)}, u32[]{:S(2)}) collective-permute-start(f32[72,256]{1,0:T(8,128)S(1)} %shard_map.48.own.one.refs_0_), channel_id=1, source_target_pairs={{0,4},{1,5},{2,6},{3,7},{4,0},{5,1},{6,2},{7,3},{8,12},{9,13},{10,... | collective-permute-start | bytes 221192 | tf_op jit(solution)/shard_map/ppermute | solution.py:353
  14.5 2.2 %collective-permute-start.7 = (f32[40,256]{1,0:T(8,128)S(1)}, f32[40,256]{1,0:T(8,128)S(1)}, u32[]{:S(2)}, u32[]{:S(2)}) collective-permute-start(f32[40,256]{1,0:T(8,128)S(1)} %get-tuple-element.40), channel_id=1, source_target_pairs={{0,1},{1,0},{2,3},{3,2},{4,5},{5,4},{6,7},{7,6},{8,9},{9,8},{10,11... | collective-permute-start | bytes 122888 | tf_op jit(solution)/shard_map/ppermute | solution.py:433
  21.3 6.6 %collective-permute-start.10 = (f32[64,256]{1,0:T(8,128)S(1)}, f32[64,256]{1,0:T(8,128)S(1)}, u32[]{:S(2)}, u32[]{:S(2)}) collective-permute-start(f32[64,256]{1,0:T(8,128)S(1)} %get-tuple-element.41.refs_0_), channel_id=1, source_target_pairs={{0,12},{1,13},{2,14},{3,15},{4,8},{5,9},{6,10},{7,11},{8,4},{9,5},... | collective-permute-start | bytes 196616 | tf_op jit(solution)/shard_map/ppermute | solution.py:353
  23.8 6.3 %collective-permute-start.9 = (f32[64,256]{1,0:T(8,128)S(1)}, f32[64,256]{1,0:T(8,128)S(1)}, u32[]{:S(2)}, u32[]{:S(2)}) collective-permute-start(f32[64,256]{1,0:T(8,128)S(1)} %get-tuple-element.41.refs_0_), channel_id=1, source_target_pairs={{0,8},{1,9},{2,10},{3,11},{4,12},{5,13},{6,14},{7,15},{8,0},{9,1},... | collective-permute-start | bytes 196616 | tf_op jit(solution)/shard_map/ppermute | solution.py:353
  23.8 6.3 %collective-permute-start.8 = (f32[64,256]{1,0:T(8,128)S(1)}, f32[64,256]{1,0:T(8,128)S(1)}, u32[]{:S(2)}, u32[]{:S(2)}) collective-permute-start(f32[64,256]{1,0:T(8,128)S(1)} %get-tuple-element.41.refs_0_), channel_id=1, source_target_pairs={{0,4},{1,5},{2,6},{3,7},{4,0},{5,1},{6,2},{7,3},{8,12},{9,13},{10,... | collective-permute-start | bytes 196616 | tf_op jit(solution)/shard_map/ppermute | solution.py:353
  27.0 4.6 %collective-permute-start.14 = (f32[16,256]{1,0:T(8,128)S(1)}, f32[16,256]{1,0:T(8,128)S(1)}, u32[]{:S(2)}, u32[]{:S(2)}) collective-permute-start(f32[16,256]{1,0:T(8,128)S(1)} %get-tuple-element.53), channel_id=1, source_target_pairs={{0,1},{1,0},{2,3},{3,2},{4,5},{5,4},{6,7},{7,6},{8,9},{9,8},{10,11... | collective-permute-start | bytes 49160 | tf_op jit(solution)/shard_map/ppermute | solution.py:348
  27.1 5.7 %collective-permute-start.15 = (f32[16,256]{1,0:T(8,128)S(1)}, f32[16,256]{1,0:T(8,128)S(1)}, u32[]{:S(2)}, u32[]{:S(2)}) collective-permute-start(f32[16,256]{1,0:T(8,128)S(1)} %get-tuple-element.54), channel_id=1, source_target_pairs={{0,2},{1,3},{2,0},{3,1},{4,6},{5,7},{6,4},{7,5},{8,10},{9,11},{10,... | collective-permute-start | bytes 49160 | tf_op jit(solution)/shard_map/ppermute | solution.py:348
  27.9 4.8 %collective-permute-start.16 = (f32[16,256]{1,0:T(8,128)S(1)}, f32[16,256]{1,0:T(8,128)S(1)}, u32[]{:S(2)}, u32[]{:S(2)}) collective-permute-start(f32[16,256]{1,0:T(8,128)S(1)} %get-tuple-element.55), channel_id=1, source_target_pairs={{0,3},{1,2},{2,1},{3,0},{4,7},{5,6},{6,5},{7,4},{8,11},{9,10},{10,... | collective-permute-start | bytes 49160 | tf_op jit(solution)/shard_map/ppermute | solution.py:348
  30.8 3.2 %collective-permute-start.11 = (f32[16,256]{1,0:T(8,128)S(1)}, f32[16,256]{1,0:T(8,128)S(1)}, u32[]{:S(2)}, u32[]{:S(2)}) collective-permute-start(f32[16,256]{1,0:T(8,128)S(1)} %get-tuple-element.49), channel_id=1, source_target_pairs={{0,1},{1,0},{2,3},{3,2},{4,5},{5,4},{6,7},{7,6},{8,9},{9,8},{10,11... | collective-permute-start | bytes 49160 | tf_op jit(solution)/shard_map/ppermute | solution.py:348
  30.8 3.8 %collective-permute-start.12 = (f32[16,256]{1,0:T(8,128)S(1)}, f32[16,256]{1,0:T(8,128)S(1)}, u32[]{:S(2)}, u32[]{:S(2)}) collective-permute-start(f32[16,256]{1,0:T(8,128)S(1)} %get-tuple-element.50), channel_id=1, source_target_pairs={{0,2},{1,3},{2,0},{3,1},{4,6},{5,7},{6,4},{7,5},{8,10},{9,11},{10,... | collective-permute-start | bytes 49160 | tf_op jit(solution)/shard_map/ppermute | solution.py:348
  31.6 3.2 %collective-permute-start.13 = (f32[16,256]{1,0:T(8,128)S(1)}, f32[16,256]{1,0:T(8,128)S(1)}, u32[]{:S(2)}, u32[]{:S(2)}) collective-permute-start(f32[16,256]{1,0:T(8,128)S(1)} %get-tuple-element.51), channel_id=1, source_target_pairs={{0,3},{1,2},{2,1},{3,0},{4,7},{5,6},{6,5},{7,4},{8,11},{9,10},{10,... | collective-permute-start | bytes 49160 | tf_op jit(solution)/shard_map/ppermute | solution.py:348

commit v30 on v29

--- a/solution.py
+++ b/solution.py
@@ -331,15 +331,15 @@
 
 def last_kernel(*refs):
     parts, (before, mask_ids), tables, (out, means, y, sems) = refs[:NEAR], refs[NEAR : NEAR + 2], refs[NEAR + 2 : -4], refs[-4:]
-    outs = column_copies(y, out, sems)
+    outs = column_copies(y, out, sems, BLOCK // 2)
     columns, slots = means.shape
     second = own_means(parts, means)
-    for b in range(len(outs)):
-        at = slice(b * BLOCK, (b + 1) * BLOCK)
-        found = tables[0][:, at] if tables else one_hot(row(mask_ids, b, BLOCK), slots)
+    for b, copy in enumerate(outs):
+        at = slice(b * BLOCK // 2, (b + 1) * BLOCK // 2)
+        found = tables[0][:, at] if tables else one_hot(row(mask_ids, b, BLOCK // 2), slots)
         spread = dot(second, found)
         y[:, at] = before[:, at] - (spread[:columns] + spread[columns:])
-        outs[b].start()
+        copy.start()
     wait_all(outs)
 
 
@@ -515,7 +515,7 @@
         array(whole, F32),
         [vmem] * (NEAR + 2 + len(spreads[:1])),
         hbm,
-        [pltpu.VMEM((columns, slots), F32), pltpu.VMEM(whole, F32), sems],
+        [pltpu.VMEM((columns, slots), F32), pltpu.VMEM(whole, F32), pltpu.SemaphoreType.DMA((2 * blocks,))],
         work,
         8 * columns * rows_dev,
     )(*arrived, before, mask_ids, *spreads[:1])

time: 36.6 us -> 36.6 us (level)
  no operation moved by 1% of the time
where the time goes in v30:
time: 36.6 us; the launch traced here: 36.4 us
  starting transfers between devices  17.7 us (48%)
  Pallas kernels  14.9 us (41%)
  waiting for transfers between devices  3.7 us (10%)
    ppermute x6, starting transfers between devices, far_share(): return [one] + [lax.ppermute(one, 'rows', step) for step in steps]  8.85 us
    ppermute x9, starting transfers between devices, near_exchange(): lax.ppermute(one, 'rows', step)  6.99 us
    pallas_call x3, Pallas kernels, pair_counts(): call(functools.partial(pairs_kernel, pad, count), [array((count, slots, 2...  4.55 us
    pallas_call x1, Pallas kernels, body(): call(functools.partial(sums_kernel, pad, slots // n), [short, message, sh...  3.37 us
    ppermute x6, waiting for transfers between devices, far_share(): return [one] + [lax.ppermute(one, 'rows', step) for step in steps]  2.8 us
    ppermute x2, starting transfers between devices, near_step(): return lax.ppermute(one, 'rows', [(i, i ^ step) for i in range(n)])  1.87 us
    pallas_call x1, Pallas kernels, body(): call(last_kernel, array(whole, F32), [vmem] * (NEAR + 2 + len(spreads[:1]...  1.64 us
    pallas_call x1, Pallas kernels, body(): call(functools.partial(change_kernel, far, part, len(tables)), [of_near,...  1.37 us
  transfers between devices with their start and end apart: 17, of which 5 were waited for; matrix products, arithmetic and copies ran while one was open for 0% of the time, Pallas kernels for 23%

profile of v30, /device:TPU:0, one launch (start us, length us, event | category | flops | bytes accessed | tf_op | source)
XLA Modules:
  0.0 36.4 jit_solution(12735462979590730545)
XLA Ops:
  0.0 3.4 %shard_map.46 = (f32[24,256]{1,0:T(8,128)S(1)}, f32[56,256]{1,0:T(8,128)S(1)}, f32[24,256]{1,0:T(8,128)S(1)}, f32[24,256]{1,0:T(8,128)S(1)}, f32[40,256]{1,0:T(8...) custom-call(f32[64,8192]{1,0:T(8,128)} %refs_0_.1, s32[8,128]{1,0:T(8,128)} %bitcast.4, ...), custom_call_target="tpu_custom_call" | custom-call | flops 1073741824 | bytes 2097152 | tf_op jit(solution)/shard_map/pallas_call | solution.py:397
  3.4 0.5 %collective-permute-start = (f32[56,256]{1,0:T(8,128)S(1)}, f32[56,256]{1,0:T(8,128)S(1)}, u32[]{:S(2)}, u32[]{:S(2)}) collective-permute-start(f32[56,256]{1,0:T(8,128)S(1)} %get-tuple-element.33), channel_id=1, source_target_pairs={{0,1},{1,0},{2,3},{3,2},{4,5},{5,4},{6,7},{7,6},{8,9},{9,8},{10,11... | collective-permute-start | bytes 172040 | tf_op jit(solution)/shard_map/ppermute | solution.py:348
  3.9 2.6 %collective-permute-start.1 = (f32[24,256]{1,0:T(8,128)S(1)}, f32[24,256]{1,0:T(8,128)S(1)}, u32[]{:S(2)}, u32[]{:S(2)}) collective-permute-start(f32[24,256]{1,0:T(8,128)S(1)} %get-tuple-element.34), channel_id=1, source_target_pairs={{0,2},{1,3},{2,0},{3,1},{4,6},{5,7},{6,4},{7,5},{8,10},{9,11},{10,... | collective-permute-start | bytes 73736 | tf_op jit(solution)/shard_map/ppermute | solution.py:348
  6.5 0.1 collective-permute-start.2
  6.6 1.2 %shard_map.47 = (bf16[1,256,512]{2,1,0:T(8,128)(2,1)S(1)}, f32[40,256]{1,0:T(8,128)S(1)}) custom-call(f32[40,256]{1,0:T(8,128)S(1)} %get-tuple-element.36.refs_0_), custom_call_target="tpu_custom_call" | custom-call | flops 134217728 | bytes 262144 | tf_op jit(solution)/shard_map/pallas_call | solution.py:418
  7.8 1.8 %collective-permute-start.6 = (f32[40,256]{1,0:T(8,128)S(1)}, f32[40,256]{1,0:T(8,128)S(1)}, u32[]{:S(2)}, u32[]{:S(2)}) collective-permute-start(f32[40,256]{1,0:T(8,128)S(1)} %get-tuple-element.38), channel_id=1, source_target_pairs={{0,2},{1,3},{2,0},{3,1},{4,6},{5,7},{6,4},{7,5},{8,10},{9,11},{10,... | collective-permute-start | bytes 122888 | tf_op jit(solution)/shard_map/ppermute | solution.py:433
  9.6 0.0 collective-permute-done.1.refs_2_
  9.6 0.2 collective-permute-done.2.refs_3_
  9.7 0.0 collective-permute-done.refs_1_.refs_0_
  9.8 3.7 %collective-permute-start.5 = (f32[72,256]{1,0:T(8,128)S(1)}, f32[72,256]{1,0:T(8,128)S(1)}, u32[]{:S(2)}, u32[]{:S(2)}) collective-permute-start(f32[72,256]{1,0:T(8,128)S(1)} %shard_map.48.own.one.refs_0_), channel_id=1, source_target_pairs={{0,12},{1,13},{2,14},{3,15},{4,8},{5,9},{6,10},{7,11},{8,4},{9,5},... | collective-permute-start | bytes 221192 | tf_op jit(solution)/shard_map/ppermute | solution.py:353
  13.4 0.0 collective-permute-start.4
  13.4 0.8 %collective-permute-start.3 = (f32[72,256]{1,0:T(8,128)S(1)}, f32[72,256]{1,0:T(8,128)S(1)}, u32[]{:S(2)}, u32[]{:S(2)}) collective-permute-start(f32[72,256]{1,0:T(8,128)S(1)} %shard_map.48.own.one.refs_0_), channel_id=1, source_target_pairs={{0,4},{1,5},{2,6},{3,7},{4,0},{5,1},{6,2},{7,3},{8,12},{9,13},{10,... | collective-permute-start | bytes 221192 | tf_op jit(solution)/shard_map/ppermute | solution.py:353
  14.2 0.0 collective-permute-done.6.passed.refs_1_
  14.2 0.3 shard_map.49
  14.5 0.1 collective-permute-start.7
  14.6 2.1 %shard_map.51.refs_7_ = bf16[2,256,512]{2,1,0:T(8,128)(2,1)S(1)} custom-call(f32[56,256]{1,0:T(8,128)S(1)} %collective-permute-done.refs_1_.refs_0_, f32[40,256]{1,0:T(8,128)S(1)} %collective-permute-done.6.passed.refs_1_), custom_call_target="tpu_custom_call" | custom-call | flops 268435456 | bytes 262144 | tf_op jit(solution)/shard_map/pallas_call | solution.py:418
  16.7 0.0 collective-permute-done.7.refs_0_
  16.7 1.2 %shard_map.52.refs_8_ = bf16[1,256,512]{2,1,0:T(8,128)(2,1)S(1)} custom-call(f32[40,256]{1,0:T(8,128)S(1)} %collective-permute-done.7.refs_0_), custom_call_target="tpu_custom_call" | custom-call | flops 134217728 | bytes 262144 | tf_op jit(solution)/shard_map/pallas_call | solution.py:418
  18.0 0.0 collective-permute-done.5.one.refs_3_
  18.0 0.3 shard_map.50.refs_5_.refs_7_
  18.3 1.6 %collective-permute-done.4.refs_2_ = f32[72,256]{1,0:T(8,128)S(1)} collective-permute-done((f32[72,256]{1,0:T(8,128)S(1)}, f32[72,256]{1,0:T(8,128)S(1)}, u32[]{:S(2)}, u32[]{:S(2)}) %collective-permute-start.4) | collective-permute-done | bytes 73760 | tf_op jit(solution)/shard_map/ppermute | solution.py:353
  19.9 0.0 collective-permute-done.3.refs_1_
  19.9 1.4 %shard_map.53 = (f32[64,256]{1,0:T(8,128)S(1)}, f32[64,256]{1,0:T(8,128)S(1)}, f32[2,8,512]{2,1,0:T(8,128)S(1)}, bf16[2,512,512]{2,1,0:T(8,128)(2,1)S(1)}, bf16[2,512,512]{2,1,0:T(8,128)(2,1)S(1)}) custom-call(f32[72,256]{1,0:T(8,128)S(1)} %shard_map.48.own.one.refs_0_, f32[72,256]{1,0:T(8,128)S(1)} %collective-permute-done.3.refs_1_, ...), custom_call_target="tpu_custom_call" | custom-call | flops 134217728 | bytes 262144 | tf_op jit(solution)/shard_map/pallas_call | solution.py:469
  21.3 2.5 %collective-permute-start.10 = (f32[64,256]{1,0:T(8,128)S(1)}, f32[64,256]{1,0:T(8,128)S(1)}, u32[]{:S(2)}, u32[]{:S(2)}) collective-permute-start(f32[64,256]{1,0:T(8,128)S(1)} %get-tuple-element.41.refs_0_), channel_id=1, source_target_pairs={{0,12},{1,13},{2,14},{3,15},{4,8},{5,9},{6,10},{7,11},{8,4},{9,5},... | collective-permute-start | bytes 196616 | tf_op jit(solution)/shard_map/ppermute | solution.py:353
  23.8 0.0 collective-permute-start.9
  23.8 1.9 %collective-permute-start.8 = (f32[64,256]{1,0:T(8,128)S(1)}, f32[64,256]{1,0:T(8,128)S(1)}, u32[]{:S(2)}, u32[]{:S(2)}) collective-permute-start(f32[64,256]{1,0:T(8,128)S(1)} %get-tuple-element.41.refs_0_), channel_id=1, source_target_pairs={{0,4},{1,5},{2,6},{3,7},{4,0},{5,1},{6,2},{7,3},{8,12},{9,13},{10,... | collective-permute-start | bytes 196616 | tf_op jit(solution)/shard_map/ppermute | solution.py:353
  25.7 1.3 %shard_map.54 = (bf16[256,8192]{1,0:T(8,128)(2,1)S(1)}, bf16[256,8192]{1,0:T(8,128)(2,1)S(1)}, f32[16,256]{1,0:T(8,128)S(1)}, f32[16,256]{1,0:T(8,128)S(1)}, f32...) custom-call(s32[64,128]{1,0:T(8,128)S(1)} %get-tuple-element.45.mask_ids.refs_5_, f32[64,256]{1,0:T(8,128)S(1)} %get-tuple-element.46.mean), custom_call_target="tpu_custom_call" | custom-call | flops 536870912 | bytes 8388608 | tf_op jit(solution)/shard_map/pallas_call | solution.py:483
  27.0 0.1 collective-permute-start.14
  27.1 0.8 %collective-permute-start.15 = (f32[16,256]{1,0:T(8,128)S(1)}, f32[16,256]{1,0:T(8,128)S(1)}, u32[]{:S(2)}, u32[]{:S(2)}) collective-permute-start(f32[16,256]{1,0:T(8,128)S(1)} %get-tuple-element.54), channel_id=1, source_target_pairs={{0,2},{1,3},{2,0},{3,1},{4,6},{5,7},{6,4},{7,5},{8,10},{9,11},{10,... | collective-permute-start | bytes 49160 | tf_op jit(solution)/shard_map/ppermute | solution.py:348
  27.9 0.0 collective-permute-done.10.refs_3_
  27.9 1.0 %collective-permute-start.16 = (f32[16,256]{1,0:T(8,128)S(1)}, f32[16,256]{1,0:T(8,128)S(1)}, u32[]{:S(2)}, u32[]{:S(2)}) collective-permute-start(f32[16,256]{1,0:T(8,128)S(1)} %get-tuple-element.55), channel_id=1, source_target_pairs={{0,3},{1,2},{2,1},{3,0},{4,7},{5,6},{6,5},{7,4},{8,11},{9,10},{10,... | collective-permute-start | bytes 49160 | tf_op jit(solution)/shard_map/ppermute | solution.py:348
  28.9 1.1 %collective-permute-done.9.refs_2_ = f32[64,256]{1,0:T(8,128)S(1)} collective-permute-done((f32[64,256]{1,0:T(8,128)S(1)}, f32[64,256]{1,0:T(8,128)S(1)}, u32[]{:S(2)}, u32[]{:S(2)}) %collective-permute-start.9) | collective-permute-done | bytes 65568 | tf_op jit(solution)/shard_map/ppermute | solution.py:353
  30.1 0.0 collective-permute-done.8.refs_1_
  30.1 0.8 %shard_map.55 = (f32[16,256]{1,0:T(8,128)S(1)}, f32[16,256]{1,0:T(8,128)S(1)}, f32[16,256]{1,0:T(8,128)S(1)}, f32[16,256]{1,0:T(8,128)S(1)}) custom-call(f32[64,256]{1,0:T(8,128)S(1)} %get-tuple-element.41.refs_0_, f32[64,256]{1,0:T(8,128)S(1)} %collective-permute-done.8.refs_1_, f32[64,256]{1,0:T(8,128)S(1)} %collective-permute-done.9.refs_2_, ...), custom_call_target="tpu_custom_call" | custom-call | flops 134217728 | bytes 262144 | tf_op jit(solution)/shard_map/pallas_call | solution.py:494
  30.8 0.0 collective-permute-start.11
  30.8 0.8 %collective-permute-start.12 = (f32[16,256]{1,0:T(8,128)S(1)}, f32[16,256]{1,0:T(8,128)S(1)}, u32[]{:S(2)}, u32[]{:S(2)}) collective-permute-start(f32[16,256]{1,0:T(8,128)S(1)} %get-tuple-element.50), channel_id=1, source_target_pairs={{0,2},{1,3},{2,0},{3,1},{4,6},{5,7},{6,4},{7,5},{8,10},{9,11},{10,... | collective-permute-start | bytes 49160 | tf_op jit(solution)/shard_map/ppermute | solution.py:348
  31.6 0.0 collective-permute-done.14.refs_1_
  31.6 1.1 %collective-permute-start.13 = (f32[16,256]{1,0:T(8,128)S(1)}, f32[16,256]{1,0:T(8,128)S(1)}, u32[]{:S(2)}, u32[]{:S(2)}) collective-permute-start(f32[16,256]{1,0:T(8,128)S(1)} %get-tuple-element.51), channel_id=1, source_target_pairs={{0,3},{1,2},{2,1},{3,0},{4,7},{5,6},{6,5},{7,4},{8,11},{9,10},{10,... | collective-permute-start | bytes 49160 | tf_op jit(solution)/shard_map/ppermute | solution.py:348
  32.7 0.0 collective-permute-done.15.refs_2_
  32.7 0.0 collective-permute-done.16.refs_3_
  32.7 1.3 %shard_map.56.refs_4_ = f32[64,8192]{1,0:T(8,128)S(1)} custom-call(f32[16,256]{1,0:T(8,128)S(1)} %get-tuple-element.52.refs_0_, f32[16,256]{1,0:T(8,128)S(1)} %collective-permute-done.14.refs_1_, f32[16,256]{1,0:T(8,128)S(1)} %collective-permute-done.15.refs_2_, f32[16,256]{1,0:T(8,128)S(1)} %collective-permute-done.16.refs_3_, ...), custom_call_target="tpu_custom_call" | custom-call | flops 536870912 | bytes 4194304 | tf_op jit(solution)/shard_map/pallas_call | solution.py:504
  34.1 0.0 collective-permute-done.11.refs_1_
  34.1 0.6 %collective-permute-done.12.refs_2_ = f32[16,256]{1,0:T(8,128)S(1)} collective-permute-done((f32[16,256]{1,0:T(8,128)S(1)}, f32[16,256]{1,0:T(8,128)S(1)}, u32[]{:S(2)}, u32[]{:S(2)}) %collective-permute-start.12) | collective-permute-done | bytes 16416 | tf_op jit(solution)/shard_map/ppermute | solution.py:348
  34.6 0.1 collective-permute-done.13.refs_3_
  34.8 1.6 %shard_map.57 = f32[64,8192]{1,0:T(8,128)} custom-call(f32[16,256]{1,0:T(8,128)S(1)} %get-tuple-element.48.refs_0_, f32[16,256]{1,0:T(8,128)S(1)} %collective-permute-done.11.refs_1_, f32[16,256]{1,0:T(8,128)S(1)} %collective-permute-done.12.refs_2_, f32[16,256]{1,0:T(8,128)S(1)} %collective-permute-done.13.refs_3_, f32[64,8192]{1,0:T(8,128)S(1)} %shard_map.56.refs_4_, ...), custom_call_target="tpu_custom_call" | custom-call | flops 536870912 | bytes 4194304 | tf_op jit(solution)/shard_map/pallas_call | solution.py:513
  (1 shorter events, 0.0 us)
Async XLA Ops:
  3.4 6.4 %collective-permute-start = (f32[56,256]{1,0:T(8,128)S(1)}, f32[56,256]{1,0:T(8,128)S(1)}, u32[]{:S(2)}, u32[]{:S(2)}) collective-permute-start(f32[56,256]{1,0:T(8,128)S(1)} %get-tuple-element.33), channel_id=1, source_target_pairs={{0,1},{1,0},{2,3},{3,2},{4,5},{5,4},{6,7},{7,6},{8,9},{9,8},{10,11... | collective-permute-start | bytes 172040 | tf_op jit(solution)/shard_map/ppermute | solution.py:348
  3.9 5.7 %collective-permute-start.1 = (f32[24,256]{1,0:T(8,128)S(1)}, f32[24,256]{1,0:T(8,128)S(1)}, u32[]{:S(2)}, u32[]{:S(2)}) collective-permute-start(f32[24,256]{1,0:T(8,128)S(1)} %get-tuple-element.34), channel_id=1, source_target_pairs={{0,2},{1,3},{2,0},{3,1},{4,6},{5,7},{6,4},{7,5},{8,10},{9,11},{10,... | collective-permute-start | bytes 73736 | tf_op jit(solution)/shard_map/ppermute | solution.py:348
  6.5 3.3 %collective-permute-start.2 = (f32[24,256]{1,0:T(8,128)S(1)}, f32[24,256]{1,0:T(8,128)S(1)}, u32[]{:S(2)}, u32[]{:S(2)}) collective-permute-start(f32[24,256]{1,0:T(8,128)S(1)} %get-tuple-element.35), channel_id=1, source_target_pairs={{0,3},{1,2},{2,1},{3,0},{4,7},{5,6},{6,5},{7,4},{8,11},{9,10},{10,... | collective-permute-start | bytes 73736 | tf_op jit(solution)/shard_map/ppermute | solution.py:348
  7.8 6.4 %collective-permute-start.6 = (f32[40,256]{1,0:T(8,128)S(1)}, f32[40,256]{1,0:T(8,128)S(1)}, u32[]{:S(2)}, u32[]{:S(2)}) collective-permute-start(f32[40,256]{1,0:T(8,128)S(1)} %get-tuple-element.38), channel_id=1, source_target_pairs={{0,2},{1,3},{2,0},{3,1},{4,6},{5,7},{6,4},{7,5},{8,10},{9,11},{10,... | collective-permute-start | bytes 122888 | tf_op jit(solution)/shard_map/ppermute | solution.py:433
  9.8 8.2 %collective-permute-start.5 = (f32[72,256]{1,0:T(8,128)S(1)}, f32[72,256]{1,0:T(8,128)S(1)}, u32[]{:S(2)}, u32[]{:S(2)}) collective-permute-start(f32[72,256]{1,0:T(8,128)S(1)} %shard_map.48.own.one.refs_0_), channel_id=1, source_target_pairs={{0,12},{1,13},{2,14},{3,15},{4,8},{5,9},{6,10},{7,11},{8,4},{9,5},... | collective-permute-start | bytes 221192 | tf_op jit(solution)/shard_map/ppermute | solution.py:353
  13.4 6.5 %collective-permute-start.4 = (f32[72,256]{1,0:T(8,128)S(1)}, f32[72,256]{1,0:T(8,128)S(1)}, u32[]{:S(2)}, u32[]{:S(2)}) collective-permute-start(f32[72,256]{1,0:T(8,128)S(1)} %shard_map.48.own.one.refs_0_), channel_id=1, source_target_pairs={{0,8},{1,9},{2,10},{3,11},{4,12},{5,13},{6,14},{7,15},{8,0},{9,1},... | collective-permute-start | bytes 221192 | tf_op jit(solution)/shard_map/ppermute | solution.py:353
  13.4 6.5 %collective-permute-start.3 = (f32[72,256]{1,0:T(8,128)S(1)}, f32[72,256]{1,0:T(8,128)S(1)}, u32[]{:S(2)}, u32[]{:S(2)}) collective-permute-start(f32[72,256]{1,0:T(8,128)S(1)} %shard_map.48.own.one.refs_0_), channel_id=1, source_target_pairs={{0,4},{1,5},{2,6},{3,7},{4,0},{5,1},{6,2},{7,3},{8,12},{9,13},{10,... | collective-permute-start | bytes 221192 | tf_op jit(solution)/shard_map/ppermute | solution.py:353
  14.5 2.2 %collective-permute-start.7 = (f32[40,256]{1,0:T(8,128)S(1)}, f32[40,256]{1,0:T(8,128)S(1)}, u32[]{:S(2)}, u32[]{:S(2)}) collective-permute-start(f32[40,256]{1,0:T(8,128)S(1)} %get-tuple-element.40), channel_id=1, source_target_pairs={{0,1},{1,0},{2,3},{3,2},{4,5},{5,4},{6,7},{7,6},{8,9},{9,8},{10,11... | collective-permute-start | bytes 122888 | tf_op jit(solution)/shard_map/ppermute | solution.py:433
  21.3 6.6 %collective-permute-start.10 = (f32[64,256]{1,0:T(8,128)S(1)}, f32[64,256]{1,0:T(8,128)S(1)}, u32[]{:S(2)}, u32[]{:S(2)}) collective-permute-start(f32[64,256]{1,0:T(8,128)S(1)} %get-tuple-element.41.refs_0_), channel_id=1, source_target_pairs={{0,12},{1,13},{2,14},{3,15},{4,8},{5,9},{6,10},{7,11},{8,4},{9,5},... | collective-permute-start | bytes 196616 | tf_op jit(solution)/shard_map/ppermute | solution.py:353
  23.8 6.3 %collective-permute-start.9 = (f32[64,256]{1,0:T(8,128)S(1)}, f32[64,256]{1,0:T(8,128)S(1)}, u32[]{:S(2)}, u32[]{:S(2)}) collective-permute-start(f32[64,256]{1,0:T(8,128)S(1)} %get-tuple-element.41.refs_0_), channel_id=1, source_target_pairs={{0,8},{1,9},{2,10},{3,11},{4,12},{5,13},{6,14},{7,15},{8,0},{9,1},... | collective-permute-start | bytes 196616 | tf_op jit(solution)/shard_map/ppermute | solution.py:353
  23.8 6.3 %collective-permute-start.8 = (f32[64,256]{1,0:T(8,128)S(1)}, f32[64,256]{1,0:T(8,128)S(1)}, u32[]{:S(2)}, u32[]{:S(2)}) collective-permute-start(f32[64,256]{1,0:T(8,128)S(1)} %get-tuple-element.41.refs_0_), channel_id=1, source_target_pairs={{0,4},{1,5},{2,6},{3,7},{4,0},{5,1},{6,2},{7,3},{8,12},{9,13},{10,... | collective-permute-start | bytes 196616 | tf_op jit(solution)/shard_map/ppermute | solution.py:353
  27.0 4.6 %collective-permute-start.14 = (f32[16,256]{1,0:T(8,128)S(1)}, f32[16,256]{1,0:T(8,128)S(1)}, u32[]{:S(2)}, u32[]{:S(2)}) collective-permute-start(f32[16,256]{1,0:T(8,128)S(1)} %get-tuple-element.53), channel_id=1, source_target_pairs={{0,1},{1,0},{2,3},{3,2},{4,5},{5,4},{6,7},{7,6},{8,9},{9,8},{10,11... | collective-permute-start | bytes 49160 | tf_op jit(solution)/shard_map/ppermute | solution.py:348
  27.1 5.7 %collective-permute-start.15 = (f32[16,256]{1,0:T(8,128)S(1)}, f32[16,256]{1,0:T(8,128)S(1)}, u32[]{:S(2)}, u32[]{:S(2)}) collective-permute-start(f32[16,256]{1,0:T(8,128)S(1)} %get-tuple-element.54), channel_id=1, source_target_pairs={{0,2},{1,3},{2,0},{3,1},{4,6},{5,7},{6,4},{7,5},{8,10},{9,11},{10,... | collective-permute-start | bytes 49160 | tf_op jit(solution)/shard_map/ppermute | solution.py:348
  27.9 4.8 %collective-permute-start.16 = (f32[16,256]{1,0:T(8,128)S(1)}, f32[16,256]{1,0:T(8,128)S(1)}, u32[]{:S(2)}, u32[]{:S(2)}) collective-permute-start(f32[16,256]{1,0:T(8,128)S(1)} %get-tuple-element.55), channel_id=1, source_target_pairs={{0,3},{1,2},{2,1},{3,0},{4,7},{5,6},{6,5},{7,4},{8,11},{9,10},{10,... | collective-permute-start | bytes 49160 | tf_op jit(solution)/shard_map/ppermute | solution.py:348
  30.8 3.2 %collective-permute-start.11 = (f32[16,256]{1,0:T(8,128)S(1)}, f32[16,256]{1,0:T(8,128)S(1)}, u32[]{:S(2)}, u32[]{:S(2)}) collective-permute-start(f32[16,256]{1,0:T(8,128)S(1)} %get-tuple-element.49), channel_id=1, source_target_pairs={{0,1},{1,0},{2,3},{3,2},{4,5},{5,4},{6,7},{7,6},{8,9},{9,8},{10,11... | collective-permute-start | bytes 49160 | tf_op jit(solution)/shard_map/ppermute | solution.py:348
  30.8 3.8 %collective-permute-start.12 = (f32[16,256]{1,0:T(8,128)S(1)}, f32[16,256]{1,0:T(8,128)S(1)}, u32[]{:S(2)}, u32[]{:S(2)}) collective-permute-start(f32[16,256]{1,0:T(8,128)S(1)} %get-tuple-element.50), channel_id=1, source_target_pairs={{0,2},{1,3},{2,0},{3,1},{4,6},{5,7},{6,4},{7,5},{8,10},{9,11},{10,... | collective-permute-start | bytes 49160 | tf_op jit(solution)/shard_map/ppermute | solution.py:348
  31.6 3.2 %collective-permute-start.13 = (f32[16,256]{1,0:T(8,128)S(1)}, f32[16,256]{1,0:T(8,128)S(1)}, u32[]{:S(2)}, u32[]{:S(2)}) collective-permute-start(f32[16,256]{1,0:T(8,128)S(1)} %get-tuple-element.51), channel_id=1, source_target_pairs={{0,3},{1,2},{2,1},{3,0},{4,7},{5,6},{6,5},{7,4},{8,11},{9,10},{10,... | collective-permute-start | bytes 49160 | tf_op jit(solution)/shard_map/ppermute | solution.py:348

commit v31 on v28

--- a/solution.py
+++ b/solution.py
@@ -10,6 +10,7 @@
 FIRMS_PER_SHARD = 1024
 LANES = 128
 BLOCK = 1024
+WIDE = 2048
 VMEM_BYTES = 32 * 1024 * 1024
 NEAR = 4
 NEAR_STEPS = (0, 1, 2, 3)
@@ -134,14 +135,14 @@
     table = jnp.concatenate([same_worker(pad, 256)] * 2, axis=0)
     wait_all(copies)
     total = None
-    for b in range(x.shape[1] // BLOCK):
-        ok = row(valid, b, BLOCK)
-        x0 = x[:, b * BLOCK : (b + 1) * BLOCK] * ok
-        rest = x0 - by_worker(x0, table) * row(weight, b, BLOCK)
-        x1[:, b * BLOCK : (b + 1) * BLOCK] = rest
-        counted = jnp.broadcast_to(ok, (16, BLOCK)).astype(BF16)
+    for b in range(x.shape[1] // WIDE):
+        ok = row(valid, b, WIDE)
+        x0 = x[:, b * WIDE : (b + 1) * WIDE] * ok
+        rest = x0 - by_worker(x0, table) * row(weight, b, WIDE)
+        x1[:, b * WIDE : (b + 1) * WIDE] = rest
+        counted = jnp.broadcast_to(ok, (16, WIDE)).astype(BF16)
         data = jnp.concatenate([*split(rest), counted], axis=0)
-        per = BLOCK // LANES
+        per = WIDE // LANES
         block = dot(data, one_hot_down(turned[:, b * per : (b + 1) * per], slots))
         total = block if total is None else total + block
     sums[...] = total[:columns] + total[columns : 2 * columns]

time: 36.6 us -> 36.8 us (level)
  no operation moved by 1% of the time
where the time goes in v31:
time: 36.8 us; the launch traced here: 36.6 us
  starting transfers between devices  17.7 us (48%)
  Pallas kernels  15.5 us (42%)
  waiting for transfers between devices  3.32 us (9%)
    ppermute x6, starting transfers between devices, far_share(): return [one] + [lax.ppermute(one, 'rows', step) for step in steps]  8.85 us
    ppermute x9, starting transfers between devices, near_exchange(): lax.ppermute(one, 'rows', step)  6.99 us
    pallas_call x4, Pallas kernels, pair_counts(): call(functools.partial(pairs_kernel, pad, start, 1), [array((1, slots, 2...  4.92 us
    pallas_call x1, Pallas kernels, body(): call(functools.partial(sums_kernel, pad, slots // n), [short, message, sh...  3.56 us
    ppermute x6, waiting for transfers between devices, far_share(): return [one] + [lax.ppermute(one, 'rows', step) for step in steps]  2.43 us
    ppermute x2, starting transfers between devices, near_step(): return lax.ppermute(one, 'rows', [(i, i ^ step) for i in range(n)])  1.87 us
    pallas_call x1, Pallas kernels, body(): call(last_kernel, array(whole, F32), [vmem] * (NEAR + 2 + len(spreads[:1]...  1.62 us
    pallas_call x1, Pallas kernels, body(): call(functools.partial(change_kernel, far, part, len(tables)), [of_near,...  1.36 us
  transfers between devices with their start and end apart: 17, of which 5 were waited for; matrix products, arithmetic and copies ran while one was open for 0% of the time, Pallas kernels for 24%

profile of v31, /device:TPU:0, one launch (start us, length us, event | category | flops | bytes accessed | tf_op | source)
XLA Modules:
  0.0 36.6 jit_solution(15809017623418795061)
XLA Ops:
  0.0 3.6 %shard_map.46 = (f32[24,256]{1,0:T(8,128)S(1)}, f32[56,256]{1,0:T(8,128)S(1)}, f32[24,256]{1,0:T(8,128)S(1)}, f32[24,256]{1,0:T(8,128)S(1)}, f32[40,256]{1,0:T(8...) custom-call(f32[64,8192]{1,0:T(8,128)} %refs_0_.1, s32[8,128]{1,0:T(8,128)} %bitcast.4, ...), custom_call_target="tpu_custom_call" | custom-call | flops 1073741824 | bytes 2097152 | tf_op jit(solution)/shard_map/pallas_call | solution.py:396
  3.6 0.5 %collective-permute-start = (f32[56,256]{1,0:T(8,128)S(1)}, f32[56,256]{1,0:T(8,128)S(1)}, u32[]{:S(2)}, u32[]{:S(2)}) collective-permute-start(f32[56,256]{1,0:T(8,128)S(1)} %get-tuple-element.33), channel_id=1, source_target_pairs={{0,1},{1,0},{2,3},{3,2},{4,5},{5,4},{6,7},{7,6},{8,9},{9,8},{10,11... | collective-permute-start | bytes 172040 | tf_op jit(solution)/shard_map/ppermute | solution.py:347
  4.1 2.6 %collective-permute-start.1 = (f32[24,256]{1,0:T(8,128)S(1)}, f32[24,256]{1,0:T(8,128)S(1)}, u32[]{:S(2)}, u32[]{:S(2)}) collective-permute-start(f32[24,256]{1,0:T(8,128)S(1)} %get-tuple-element.34), channel_id=1, source_target_pairs={{0,2},{1,3},{2,0},{3,1},{4,6},{5,7},{6,4},{7,5},{8,10},{9,11},{10,... | collective-permute-start | bytes 73736 | tf_op jit(solution)/shard_map/ppermute | solution.py:347
  6.7 0.1 collective-permute-start.2
  6.7 1.2 %shard_map.47 = (bf16[1,256,512]{2,1,0:T(8,128)(2,1)S(1)}, f32[40,256]{1,0:T(8,128)S(1)}) custom-call(f32[40,256]{1,0:T(8,128)S(1)} %get-tuple-element.36.refs_0_), custom_call_target="tpu_custom_call" | custom-call | flops 134217728 | bytes 262144 | tf_op jit(solution)/shard_map/pallas_call | solution.py:416
  8.0 1.8 %collective-permute-start.6 = (f32[40,256]{1,0:T(8,128)S(1)}, f32[40,256]{1,0:T(8,128)S(1)}, u32[]{:S(2)}, u32[]{:S(2)}) collective-permute-start(f32[40,256]{1,0:T(8,128)S(1)} %get-tuple-element.38), channel_id=1, source_target_pairs={{0,2},{1,3},{2,0},{3,1},{4,6},{5,7},{6,4},{7,5},{8,10},{9,11},{10,... | collective-permute-start | bytes 122888 | tf_op jit(solution)/shard_map/ppermute | solution.py:431
  9.8 0.0 collective-permute-done.1.refs_2_
  9.8 0.1 collective-permute-done.2.refs_3_
  9.9 0.0 collective-permute-done.refs_1_.refs_0_
  9.9 3.7 %collective-permute-start.5 = (f32[72,256]{1,0:T(8,128)S(1)}, f32[72,256]{1,0:T(8,128)S(1)}, u32[]{:S(2)}, u32[]{:S(2)}) collective-permute-start(f32[72,256]{1,0:T(8,128)S(1)} %shard_map.48.own.one.refs_0_), channel_id=1, source_target_pairs={{0,12},{1,13},{2,14},{3,15},{4,8},{5,9},{6,10},{7,11},{8,4},{9,5},... | collective-permute-start | bytes 221192 | tf_op jit(solution)/shard_map/ppermute | solution.py:352
  13.6 0.0 collective-permute-start.4
  13.6 0.8 %collective-permute-start.3 = (f32[72,256]{1,0:T(8,128)S(1)}, f32[72,256]{1,0:T(8,128)S(1)}, u32[]{:S(2)}, u32[]{:S(2)}) collective-permute-start(f32[72,256]{1,0:T(8,128)S(1)} %shard_map.48.own.one.refs_0_), channel_id=1, source_target_pairs={{0,4},{1,5},{2,6},{3,7},{4,0},{5,1},{6,2},{7,3},{8,12},{9,13},{10,... | collective-permute-start | bytes 221192 | tf_op jit(solution)/shard_map/ppermute | solution.py:352
  14.4 0.0 collective-permute-done.6.passed.refs_0_
  14.4 0.3 shard_map.49
  14.7 0.1 collective-permute-start.7
  14.8 1.2 %shard_map.52.refs_8_ = bf16[1,256,512]{2,1,0:T(8,128)(2,1)S(1)} custom-call(f32[40,256]{1,0:T(8,128)S(1)} %collective-permute-done.6.passed.refs_0_), custom_call_target="tpu_custom_call" | custom-call | flops 134217728 | bytes 262144 | tf_op jit(solution)/shard_map/pallas_call | solution.py:416
  16.0 1.2 %shard_map.51.refs_7_ = bf16[1,256,512]{2,1,0:T(8,128)(2,1)S(1)} custom-call(f32[56,256]{1,0:T(8,128)S(1)} %collective-permute-done.refs_1_.refs_0_), custom_call_target="tpu_custom_call" | custom-call | flops 134217728 | bytes 262144 | tf_op jit(solution)/shard_map/pallas_call | solution.py:416
  17.3 0.0 collective-permute-done.7.refs_0_
  17.3 1.2 %shard_map.53.refs_9_ = bf16[1,256,512]{2,1,0:T(8,128)(2,1)S(1)} custom-call(f32[40,256]{1,0:T(8,128)S(1)} %collective-permute-done.7.refs_0_), custom_call_target="tpu_custom_call" | custom-call | flops 134217728 | bytes 262144 | tf_op jit(solution)/shard_map/pallas_call | solution.py:416
  18.5 0.0 collective-permute-done.5.one.refs_3_
  18.5 0.3 shard_map.50.refs_5_.refs_7_
  18.8 1.3 %collective-permute-done.4.refs_2_ = f32[72,256]{1,0:T(8,128)S(1)} collective-permute-done((f32[72,256]{1,0:T(8,128)S(1)}, f32[72,256]{1,0:T(8,128)S(1)}, u32[]{:S(2)}, u32[]{:S(2)}) %collective-permute-start.4) | collective-permute-done | bytes 73760 | tf_op jit(solution)/shard_map/ppermute | solution.py:352
  20.1 0.0 collective-permute-done.3.refs_1_
  20.1 1.4 %shard_map.54 = (f32[64,256]{1,0:T(8,128)S(1)}, f32[64,256]{1,0:T(8,128)S(1)}, f32[2,8,512]{2,1,0:T(8,128)S(1)}, bf16[2,512,512]{2,1,0:T(8,128)(2,1)S(1)}, bf16[2,512,512]{2,1,0:T(8,128)(2,1)S(1)}) custom-call(f32[72,256]{1,0:T(8,128)S(1)} %shard_map.48.own.one.refs_0_, f32[72,256]{1,0:T(8,128)S(1)} %collective-permute-done.3.refs_1_, ...), custom_call_target="tpu_custom_call" | custom-call | flops 134217728 | bytes 262144 | tf_op jit(solution)/shard_map/pallas_call | solution.py:467
  21.5 2.5 %collective-permute-start.10 = (f32[64,256]{1,0:T(8,128)S(1)}, f32[64,256]{1,0:T(8,128)S(1)}, u32[]{:S(2)}, u32[]{:S(2)}) collective-permute-start(f32[64,256]{1,0:T(8,128)S(1)} %get-tuple-element.41.refs_0_), channel_id=1, source_target_pairs={{0,12},{1,13},{2,14},{3,15},{4,8},{5,9},{6,10},{7,11},{8,4},{9,5},... | collective-permute-start | bytes 196616 | tf_op jit(solution)/shard_map/ppermute | solution.py:352
  24.0 0.0 collective-permute-start.9
  24.0 1.9 %collective-permute-start.8 = (f32[64,256]{1,0:T(8,128)S(1)}, f32[64,256]{1,0:T(8,128)S(1)}, u32[]{:S(2)}, u32[]{:S(2)}) collective-permute-start(f32[64,256]{1,0:T(8,128)S(1)} %get-tuple-element.41.refs_0_), channel_id=1, source_target_pairs={{0,4},{1,5},{2,6},{3,7},{4,0},{5,1},{6,2},{7,3},{8,12},{9,13},{10,... | collective-permute-start | bytes 196616 | tf_op jit(solution)/shard_map/ppermute | solution.py:352
  25.9 1.3 %shard_map.55 = (bf16[256,8192]{1,0:T(8,128)(2,1)S(1)}, bf16[256,8192]{1,0:T(8,128)(2,1)S(1)}, f32[16,256]{1,0:T(8,128)S(1)}, f32[16,256]{1,0:T(8,128)S(1)}, f32...) custom-call(s32[64,128]{1,0:T(8,128)S(1)} %get-tuple-element.45.mask_ids.refs_5_, f32[64,256]{1,0:T(8,128)S(1)} %get-tuple-element.46.mean), custom_call_target="tpu_custom_call" | custom-call | flops 536870912 | bytes 8388608 | tf_op jit(solution)/shard_map/pallas_call | solution.py:481
  27.2 0.1 collective-permute-start.14
  27.3 0.8 %collective-permute-start.15 = (f32[16,256]{1,0:T(8,128)S(1)}, f32[16,256]{1,0:T(8,128)S(1)}, u32[]{:S(2)}, u32[]{:S(2)}) collective-permute-start(f32[16,256]{1,0:T(8,128)S(1)} %get-tuple-element.54), channel_id=1, source_target_pairs={{0,2},{1,3},{2,0},{3,1},{4,6},{5,7},{6,4},{7,5},{8,10},{9,11},{10,... | collective-permute-start | bytes 49160 | tf_op jit(solution)/shard_map/ppermute | solution.py:347
  28.1 0.0 collective-permute-done.10.refs_3_
  28.1 1.0 %collective-permute-start.16 = (f32[16,256]{1,0:T(8,128)S(1)}, f32[16,256]{1,0:T(8,128)S(1)}, u32[]{:S(2)}, u32[]{:S(2)}) collective-permute-start(f32[16,256]{1,0:T(8,128)S(1)} %get-tuple-element.55), channel_id=1, source_target_pairs={{0,3},{1,2},{2,1},{3,0},{4,7},{5,6},{6,5},{7,4},{8,11},{9,10},{10,... | collective-permute-start | bytes 49160 | tf_op jit(solution)/shard_map/ppermute | solution.py:347
  29.1 1.1 %collective-permute-done.9.refs_2_ = f32[64,256]{1,0:T(8,128)S(1)} collective-permute-done((f32[64,256]{1,0:T(8,128)S(1)}, f32[64,256]{1,0:T(8,128)S(1)}, u32[]{:S(2)}, u32[]{:S(2)}) %collective-permute-start.9) | collective-permute-done | bytes 65568 | tf_op jit(solution)/shard_map/ppermute | solution.py:352
  30.3 0.0 collective-permute-done.8.refs_1_
  30.3 0.8 %shard_map.56 = (f32[16,256]{1,0:T(8,128)S(1)}, f32[16,256]{1,0:T(8,128)S(1)}, f32[16,256]{1,0:T(8,128)S(1)}, f32[16,256]{1,0:T(8,128)S(1)}) custom-call(f32[64,256]{1,0:T(8,128)S(1)} %get-tuple-element.41.refs_0_, f32[64,256]{1,0:T(8,128)S(1)} %collective-permute-done.8.refs_1_, f32[64,256]{1,0:T(8,128)S(1)} %collective-permute-done.9.refs_2_, ...), custom_call_target="tpu_custom_call" | custom-call | flops 134217728 | bytes 262144 | tf_op jit(solution)/shard_map/pallas_call | solution.py:492
  31.0 0.0 collective-permute-start.11
  31.0 0.8 %collective-permute-start.12 = (f32[16,256]{1,0:T(8,128)S(1)}, f32[16,256]{1,0:T(8,128)S(1)}, u32[]{:S(2)}, u32[]{:S(2)}) collective-permute-start(f32[16,256]{1,0:T(8,128)S(1)} %get-tuple-element.50), channel_id=1, source_target_pairs={{0,2},{1,3},{2,0},{3,1},{4,6},{5,7},{6,4},{7,5},{8,10},{9,11},{10,... | collective-permute-start | bytes 49160 | tf_op jit(solution)/shard_map/ppermute | solution.py:347
  31.8 0.0 collective-permute-done.14.refs_1_
  31.8 1.1 %collective-permute-start.13 = (f32[16,256]{1,0:T(8,128)S(1)}, f32[16,256]{1,0:T(8,128)S(1)}, u32[]{:S(2)}, u32[]{:S(2)}) collective-permute-start(f32[16,256]{1,0:T(8,128)S(1)} %get-tuple-element.51), channel_id=1, source_target_pairs={{0,3},{1,2},{2,1},{3,0},{4,7},{5,6},{6,5},{7,4},{8,11},{9,10},{10,... | collective-permute-start | bytes 49160 | tf_op jit(solution)/shard_map/ppermute | solution.py:347
  32.9 0.0 collective-permute-done.15.refs_2_
  32.9 0.0 collective-permute-done.16.refs_3_
  32.9 1.3 %shard_map.57.refs_4_ = f32[64,8192]{1,0:T(8,128)S(1)} custom-call(f32[16,256]{1,0:T(8,128)S(1)} %get-tuple-element.52.refs_0_, f32[16,256]{1,0:T(8,128)S(1)} %collective-permute-done.14.refs_1_, f32[16,256]{1,0:T(8,128)S(1)} %collective-permute-done.15.refs_2_, f32[16,256]{1,0:T(8,128)S(1)} %collective-permute-done.16.refs_3_, ...), custom_call_target="tpu_custom_call" | custom-call | flops 536870912 | bytes 4194304 | tf_op jit(solution)/shard_map/pallas_call | solution.py:502
  34.3 0.0 collective-permute-done.11.refs_1_
  34.3 0.6 %collective-permute-done.12.refs_2_ = f32[16,256]{1,0:T(8,128)S(1)} collective-permute-done((f32[16,256]{1,0:T(8,128)S(1)}, f32[16,256]{1,0:T(8,128)S(1)}, u32[]{:S(2)}, u32[]{:S(2)}) %collective-permute-start.12) | collective-permute-done | bytes 16416 | tf_op jit(solution)/shard_map/ppermute | solution.py:347
  34.8 0.1 collective-permute-done.13.refs_3_
  35.0 1.6 %shard_map.58 = f32[64,8192]{1,0:T(8,128)} custom-call(f32[16,256]{1,0:T(8,128)S(1)} %get-tuple-element.48.refs_0_, f32[16,256]{1,0:T(8,128)S(1)} %collective-permute-done.11.refs_1_, f32[16,256]{1,0:T(8,128)S(1)} %collective-permute-done.12.refs_2_, f32[16,256]{1,0:T(8,128)S(1)} %collective-permute-done.13.refs_3_, f32[64,8192]{1,0:T(8,128)S(1)} %shard_map.57.refs_4_, ...), custom_call_target="tpu_custom_call" | custom-call | flops 536870912 | bytes 4194304 | tf_op jit(solution)/shard_map/pallas_call | solution.py:511
  (1 shorter events, 0.0 us)
Async XLA Ops:
  3.6 6.4 %collective-permute-start = (f32[56,256]{1,0:T(8,128)S(1)}, f32[56,256]{1,0:T(8,128)S(1)}, u32[]{:S(2)}, u32[]{:S(2)}) collective-permute-start(f32[56,256]{1,0:T(8,128)S(1)} %get-tuple-element.33), channel_id=1, source_target_pairs={{0,1},{1,0},{2,3},{3,2},{4,5},{5,4},{6,7},{7,6},{8,9},{9,8},{10,11... | collective-permute-start | bytes 172040 | tf_op jit(solution)/shard_map/ppermute | solution.py:347
  4.1 5.7 %collective-permute-start.1 = (f32[24,256]{1,0:T(8,128)S(1)}, f32[24,256]{1,0:T(8,128)S(1)}, u32[]{:S(2)}, u32[]{:S(2)}) collective-permute-start(f32[24,256]{1,0:T(8,128)S(1)} %get-tuple-element.34), channel_id=1, source_target_pairs={{0,2},{1,3},{2,0},{3,1},{4,6},{5,7},{6,4},{7,5},{8,10},{9,11},{10,... | collective-permute-start | bytes 73736 | tf_op jit(solution)/shard_map/ppermute | solution.py:347
  6.7 3.3 %collective-permute-start.2 = (f32[24,256]{1,0:T(8,128)S(1)}, f32[24,256]{1,0:T(8,128)S(1)}, u32[]{:S(2)}, u32[]{:S(2)}) collective-permute-start(f32[24,256]{1,0:T(8,128)S(1)} %get-tuple-element.35), channel_id=1, source_target_pairs={{0,3},{1,2},{2,1},{3,0},{4,7},{5,6},{6,5},{7,4},{8,11},{9,10},{10,... | collective-permute-start | bytes 73736 | tf_op jit(solution)/shard_map/ppermute | solution.py:347
  8.0 6.4 %collective-permute-start.6 = (f32[40,256]{1,0:T(8,128)S(1)}, f32[40,256]{1,0:T(8,128)S(1)}, u32[]{:S(2)}, u32[]{:S(2)}) collective-permute-start(f32[40,256]{1,0:T(8,128)S(1)} %get-tuple-element.38), channel_id=1, source_target_pairs={{0,2},{1,3},{2,0},{3,1},{4,6},{5,7},{6,4},{7,5},{8,10},{9,11},{10,... | collective-permute-start | bytes 122888 | tf_op jit(solution)/shard_map/ppermute | solution.py:431
  9.9 8.6 %collective-permute-start.5 = (f32[72,256]{1,0:T(8,128)S(1)}, f32[72,256]{1,0:T(8,128)S(1)}, u32[]{:S(2)}, u32[]{:S(2)}) collective-permute-start(f32[72,256]{1,0:T(8,128)S(1)} %shard_map.48.own.one.refs_0_), channel_id=1, source_target_pairs={{0,12},{1,13},{2,14},{3,15},{4,8},{5,9},{6,10},{7,11},{8,4},{9,5},... | collective-permute-start | bytes 221192 | tf_op jit(solution)/shard_map/ppermute | solution.py:352
  13.6 6.5 %collective-permute-start.4 = (f32[72,256]{1,0:T(8,128)S(1)}, f32[72,256]{1,0:T(8,128)S(1)}, u32[]{:S(2)}, u32[]{:S(2)}) collective-permute-start(f32[72,256]{1,0:T(8,128)S(1)} %shard_map.48.own.one.refs_0_), channel_id=1, source_target_pairs={{0,8},{1,9},{2,10},{3,11},{4,12},{5,13},{6,14},{7,15},{8,0},{9,1},... | collective-permute-start | bytes 221192 | tf_op jit(solution)/shard_map/ppermute | solution.py:352
  13.6 6.5 %collective-permute-start.3 = (f32[72,256]{1,0:T(8,128)S(1)}, f32[72,256]{1,0:T(8,128)S(1)}, u32[]{:S(2)}, u32[]{:S(2)}) collective-permute-start(f32[72,256]{1,0:T(8,128)S(1)} %shard_map.48.own.one.refs_0_), channel_id=1, source_target_pairs={{0,4},{1,5},{2,6},{3,7},{4,0},{5,1},{6,2},{7,3},{8,12},{9,13},{10,... | collective-permute-start | bytes 221192 | tf_op jit(solution)/shard_map/ppermute | solution.py:352
  14.7 2.6 %collective-permute-start.7 = (f32[40,256]{1,0:T(8,128)S(1)}, f32[40,256]{1,0:T(8,128)S(1)}, u32[]{:S(2)}, u32[]{:S(2)}) collective-permute-start(f32[40,256]{1,0:T(8,128)S(1)} %get-tuple-element.40), channel_id=1, source_target_pairs={{0,1},{1,0},{2,3},{3,2},{4,5},{5,4},{6,7},{7,6},{8,9},{9,8},{10,11... | collective-permute-start | bytes 122888 | tf_op jit(solution)/shard_map/ppermute | solution.py:431
  21.5 6.6 %collective-permute-start.10 = (f32[64,256]{1,0:T(8,128)S(1)}, f32[64,256]{1,0:T(8,128)S(1)}, u32[]{:S(2)}, u32[]{:S(2)}) collective-permute-start(f32[64,256]{1,0:T(8,128)S(1)} %get-tuple-element.41.refs_0_), channel_id=1, source_target_pairs={{0,12},{1,13},{2,14},{3,15},{4,8},{5,9},{6,10},{7,11},{8,4},{9,5},... | collective-permute-start | bytes 196616 | tf_op jit(solution)/shard_map/ppermute | solution.py:352
  24.0 6.3 %collective-permute-start.9 = (f32[64,256]{1,0:T(8,128)S(1)}, f32[64,256]{1,0:T(8,128)S(1)}, u32[]{:S(2)}, u32[]{:S(2)}) collective-permute-start(f32[64,256]{1,0:T(8,128)S(1)} %get-tuple-element.41.refs_0_), channel_id=1, source_target_pairs={{0,8},{1,9},{2,10},{3,11},{4,12},{5,13},{6,14},{7,15},{8,0},{9,1},... | collective-permute-start | bytes 196616 | tf_op jit(solution)/shard_map/ppermute | solution.py:352
  24.0 6.3 %collective-permute-start.8 = (f32[64,256]{1,0:T(8,128)S(1)}, f32[64,256]{1,0:T(8,128)S(1)}, u32[]{:S(2)}, u32[]{:S(2)}) collective-permute-start(f32[64,256]{1,0:T(8,128)S(1)} %get-tuple-element.41.refs_0_), channel_id=1, source_target_pairs={{0,4},{1,5},{2,6},{3,7},{4,0},{5,1},{6,2},{7,3},{8,12},{9,13},{10,... | collective-permute-start | bytes 196616 | tf_op jit(solution)/shard_map/ppermute | solution.py:352
  27.2 4.6 %collective-permute-start.14 = (f32[16,256]{1,0:T(8,128)S(1)}, f32[16,256]{1,0:T(8,128)S(1)}, u32[]{:S(2)}, u32[]{:S(2)}) collective-permute-start(f32[16,256]{1,0:T(8,128)S(1)} %get-tuple-element.53), channel_id=1, source_target_pairs={{0,1},{1,0},{2,3},{3,2},{4,5},{5,4},{6,7},{7,6},{8,9},{9,8},{10,11... | collective-permute-start | bytes 49160 | tf_op jit(solution)/shard_map/ppermute | solution.py:347
  27.3 5.7 %collective-permute-start.15 = (f32[16,256]{1,0:T(8,128)S(1)}, f32[16,256]{1,0:T(8,128)S(1)}, u32[]{:S(2)}, u32[]{:S(2)}) collective-permute-start(f32[16,256]{1,0:T(8,128)S(1)} %get-tuple-element.54), channel_id=1, source_target_pairs={{0,2},{1,3},{2,0},{3,1},{4,6},{5,7},{6,4},{7,5},{8,10},{9,11},{10,... | collective-permute-start | bytes 49160 | tf_op jit(solution)/shard_map/ppermute | solution.py:347
  28.1 4.8 %collective-permute-start.16 = (f32[16,256]{1,0:T(8,128)S(1)}, f32[16,256]{1,0:T(8,128)S(1)}, u32[]{:S(2)}, u32[]{:S(2)}) collective-permute-start(f32[16,256]{1,0:T(8,128)S(1)} %get-tuple-element.55), channel_id=1, source_target_pairs={{0,3},{1,2},{2,1},{3,0},{4,7},{5,6},{6,5},{7,4},{8,11},{9,10},{10,... | collective-permute-start | bytes 49160 | tf_op jit(solution)/shard_map/ppermute | solution.py:347
  31.0 3.2 %collective-permute-start.11 = (f32[16,256]{1,0:T(8,128)S(1)}, f32[16,256]{1,0:T(8,128)S(1)}, u32[]{:S(2)}, u32[]{:S(2)}) collective-permute-start(f32[16,256]{1,0:T(8,128)S(1)} %get-tuple-element.49), channel_id=1, source_target_pairs={{0,1},{1,0},{2,3},{3,2},{4,5},{5,4},{6,7},{7,6},{8,9},{9,8},{10,11... | collective-permute-start | bytes 49160 | tf_op jit(solution)/shard_map/ppermute | solution.py:347
  31.0 3.8 %collective-permute-start.12 = (f32[16,256]{1,0:T(8,128)S(1)}, f32[16,256]{1,0:T(8,128)S(1)}, u32[]{:S(2)}, u32[]{:S(2)}) collective-permute-start(f32[16,256]{1,0:T(8,128)S(1)} %get-tuple-element.50), channel_id=1, source_target_pairs={{0,2},{1,3},{2,0},{3,1},{4,6},{5,7},{6,4},{7,5},{8,10},{9,11},{10,... | collective-permute-start | bytes 49160 | tf_op jit(solution)/shard_map/ppermute | solution.py:347
  31.8 3.2 %collective-permute-start.13 = (f32[16,256]{1,0:T(8,128)S(1)}, f32[16,256]{1,0:T(8,128)S(1)}, u32[]{:S(2)}, u32[]{:S(2)}) collective-permute-start(f32[16,256]{1,0:T(8,128)S(1)} %get-tuple-element.51), channel_id=1, source_target_pairs={{0,3},{1,2},{2,1},{3,0},{4,7},{5,6},{6,5},{7,4},{8,11},{9,10},{10,... | collective-permute-start | bytes 49160 | tf_op jit(solution)/shard_map/ppermute | solution.py:347

commit v32 on v29

--- a/solution.py
+++ b/solution.py
@@ -152,6 +152,10 @@
     slots_out[:8] = about
 
 
+def join_copy(one, out):
+    out[...] = one[...]
+
+
 def join_kernel(part, *refs):
     parts, out = refs[:NEAR], refs[-1]
     for k, one in enumerate(parts):
@@ -243,8 +247,8 @@
 
 def change_kernel(far, part, ready, *refs):
     parts, tables, refs = refs[:far], refs[far : far + ready], refs[far + ready :]
-    pairs = [(group, k) for group in refs[:3] for k in range(group.shape[0])]
-    (mean, sums, scale), made = refs[3:6], refs[6:]
+    pairs = [(group, k) for group in refs[:2] for k in range(group.shape[0])]
+    (mean, sums, scale), made = refs[2:5], refs[5:]
     slots = mean.shape[1]
 
     def tile(t, at):
@@ -433,18 +437,17 @@
         return lax.ppermute(one, "rows", [(i, i ^ step) for i in range(n)])
 
     arrived = near_exchange(sends, n)
-    own_pairs, own_slots = pair_counts([own_slots], [slots_message])
-    passed = near_step(own_slots, 2)
-    pairs = [own_pairs]
+    ready = call(join_copy, slots_message, [vmem], vmem, [], 0, slots_message.size * 8)(own_slots)
+    passed = near_step(ready, 2)
     joined = call(
         functools.partial(join_kernel, part),
         array((columns + 2 * NEAR, slots), F32),
-        [vmem] * (NEAR + 1),
+        [vmem] * NEAR,
         vmem,
         [],
         0,
         message.size * 8,
-    )(*arrived, *pairs)
+    )(*arrived)
     shared = far_share(joined, n)
     tables, beside = [], passed
     table = array((tiles, NEAR * LANES, NEAR * LANES), BF16)
@@ -463,7 +466,7 @@
     if keep:
         first_table, beside = firm_table(joined, passed, [table, slots_message])
         tables = [first_table, *firm_table(shared[-1], first_table, [table])]
-    pairs += pair_counts([arrived[1], passed]) + pair_counts([near_step(beside, 1)])
+    pairs = pair_counts([own_slots, arrived[1], passed]) + pair_counts([near_step(beside, 1)])
     scale = array((tiles, 8, NEAR * LANES), F32)
     made = [table] * (far - 2) * keep
     mean, sums, scales, *made = call(

time: 36.6 us -> 37.1 us (1.014)
  waiting for transfers between devices: 3.7 us -> 4.75 us
  starting transfers between devices: 17.7 us -> 17.2 us
    ppermute x9, waiting for transfers between devices: 0.9 us -> 2.19 us  [near_exchange(): lax.ppermute(one, 'rows', step)]
    ppermute x9, starting transfers between devices: 6.99 us -> 6.6 us  [near_exchange(): lax.ppermute(one, 'rows', step)]
    pallas_call x3 -> x2, Pallas kernels: 4.55 us -> 4.53 us  [pair_counts(): call(functools.partial(pairs_kernel, pad, count), [array((count, slots, 2...]
where the time goes in v32:
time: 37.1 us; the launch traced here: 37 us
  starting transfers between devices  17.2 us (46%)
  Pallas kernels  14.9 us (40%)
  waiting for transfers between devices  4.75 us (13%)
    ppermute x6, starting transfers between devices, far_share(): return [one] + [lax.ppermute(one, 'rows', step) for step in steps]  8.85 us
    ppermute x9, starting transfers between devices, near_exchange(): lax.ppermute(one, 'rows', step)  6.6 us
    pallas_call x2, Pallas kernels, pair_counts(): call(functools.partial(pairs_kernel, pad, count), [array((count, slots, 2...  4.53 us
    pallas_call x1, Pallas kernels, body(): call(functools.partial(sums_kernel, pad, slots // n), [short, message, sh...  3.37 us
    ppermute x6, waiting for transfers between devices, far_share(): return [one] + [lax.ppermute(one, 'rows', step) for step in steps]  2.56 us
    ppermute x9, waiting for transfers between devices, near_exchange(): lax.ppermute(one, 'rows', step)  2.19 us
    ppermute x2, starting transfers between devices, near_step(): return lax.ppermute(one, 'rows', [(i, i ^ step) for i in range(n)])  1.8 us
    pallas_call x1, Pallas kernels, body(): call(last_kernel, array(whole, F32), [vmem] * (NEAR + 2 + len(spreads[:1]...  1.61 us
  transfers between devices with their start and end apart: 17, of which 5 were waited for; matrix products, arithmetic and copies ran while one was open for 0% of the time, Pallas kernels for 23%

profile of v32, /device:TPU:0, one launch (start us, length us, event | category | flops | bytes accessed | tf_op | source)
XLA Modules:
  0.0 37.0 jit_solution(10898091962214232843)
XLA Ops:
  0.0 3.4 %shard_map.46 = (f32[24,256]{1,0:T(8,128)S(1)}, f32[56,256]{1,0:T(8,128)S(1)}, f32[24,256]{1,0:T(8,128)S(1)}, f32[24,256]{1,0:T(8,128)S(1)}, f32[40,256]{1,0:T(8...) custom-call(f32[64,8192]{1,0:T(8,128)} %refs_0_.1, s32[8,128]{1,0:T(8,128)} %bitcast.4, ...), custom_call_target="tpu_custom_call" | custom-call | flops 1073741824 | bytes 2097152 | tf_op jit(solution)/shard_map/pallas_call | solution.py:401
  3.4 0.5 %collective-permute-start = (f32[56,256]{1,0:T(8,128)S(1)}, f32[56,256]{1,0:T(8,128)S(1)}, u32[]{:S(2)}, u32[]{:S(2)}) collective-permute-start(f32[56,256]{1,0:T(8,128)S(1)} %get-tuple-element.31), channel_id=1, source_target_pairs={{0,1},{1,0},{2,3},{3,2},{4,5},{5,4},{6,7},{7,6},{8,9},{9,8},{10,11... | collective-permute-start | bytes 172040 | tf_op jit(solution)/shard_map/ppermute | solution.py:352
  3.9 2.6 %collective-permute-start.1 = (f32[24,256]{1,0:T(8,128)S(1)}, f32[24,256]{1,0:T(8,128)S(1)}, u32[]{:S(2)}, u32[]{:S(2)}) collective-permute-start(f32[24,256]{1,0:T(8,128)S(1)} %get-tuple-element.32), channel_id=1, source_target_pairs={{0,2},{1,3},{2,0},{3,1},{4,6},{5,7},{6,4},{7,5},{8,10},{9,11},{10,... | collective-permute-start | bytes 73736 | tf_op jit(solution)/shard_map/ppermute | solution.py:352
  6.5 0.1 collective-permute-start.2
  6.6 1.7 %collective-permute-start.6 = (f32[40,256]{1,0:T(8,128)S(1)}, f32[40,256]{1,0:T(8,128)S(1)}, u32[]{:S(2)}, u32[]{:S(2)}) collective-permute-start(f32[40,256]{1,0:T(8,128)S(1)} %shard_map.48), channel_id=1, source_target_pairs={{0,2},{1,3},{2,0},{3,1},{4,6},{5,7},{6,4},{7,5},{8,10},{9,11},{10,... | collective-permute-start | bytes 122888 | tf_op jit(solution)/shard_map/ppermute | solution.py:437
  8.3 0.0 collective-permute-done.1.refs_2_
  8.3 1.4 %collective-permute-done.2.refs_3_ = f32[24,256]{1,0:T(8,128)S(1)} collective-permute-done((f32[24,256]{1,0:T(8,128)S(1)}, f32[24,256]{1,0:T(8,128)S(1)}, u32[]{:S(2)}, u32[]{:S(2)}) %collective-permute-start.2) | collective-permute-done | bytes 24608 | tf_op jit(solution)/shard_map/ppermute | solution.py:352
  9.7 0.0 collective-permute-done.refs_1_
  9.8 3.7 %collective-permute-start.5 = (f32[72,256]{1,0:T(8,128)S(1)}, f32[72,256]{1,0:T(8,128)S(1)}, u32[]{:S(2)}, u32[]{:S(2)}) collective-permute-start(f32[72,256]{1,0:T(8,128)S(1)} %shard_map.47.own.one.refs_0_), channel_id=1, source_target_pairs={{0,12},{1,13},{2,14},{3,15},{4,8},{5,9},{6,10},{7,11},{8,4},{9,5},... | collective-permute-start | bytes 221192 | tf_op jit(solution)/shard_map/ppermute | solution.py:357
  13.4 0.0 collective-permute-start.4
  13.4 0.8 %collective-permute-start.3 = (f32[72,256]{1,0:T(8,128)S(1)}, f32[72,256]{1,0:T(8,128)S(1)}, u32[]{:S(2)}, u32[]{:S(2)}) collective-permute-start(f32[72,256]{1,0:T(8,128)S(1)} %shard_map.47.own.one.refs_0_), channel_id=1, source_target_pairs={{0,4},{1,5},{2,6},{3,7},{4,0},{5,1},{6,2},{7,3},{8,12},{9,13},{10,... | collective-permute-start | bytes 221192 | tf_op jit(solution)/shard_map/ppermute | solution.py:357
  14.2 0.0 collective-permute-done.6.passed.refs_2_
  14.2 0.3 shard_map.49
  14.5 0.1 collective-permute-start.7
  14.6 3.3 %shard_map.51.refs_6_ = bf16[3,256,512]{2,1,0:T(8,128)(2,1)S(1)} custom-call(f32[40,256]{1,0:T(8,128)S(1)} %get-tuple-element.34.one.refs_0_, f32[56,256]{1,0:T(8,128)S(1)} %collective-permute-done.refs_1_, f32[40,256]{1,0:T(8,128)S(1)} %collective-permute-done.6.passed.refs_2_), custom_call_target="tpu_custom_call" | custom-call | flops 402653184 | bytes 262144 | tf_op jit(solution)/shard_map/pallas_call | solution.py:422
  17.9 0.0 collective-permute-done.7.refs_0_
  17.9 1.2 %shard_map.52.refs_7_ = bf16[1,256,512]{2,1,0:T(8,128)(2,1)S(1)} custom-call(f32[40,256]{1,0:T(8,128)S(1)} %collective-permute-done.7.refs_0_), custom_call_target="tpu_custom_call" | custom-call | flops 134217728 | bytes 262144 | tf_op jit(solution)/shard_map/pallas_call | solution.py:422
  19.2 0.0 collective-permute-done.5.one.refs_3_
  19.2 0.3 shard_map.50.refs_5_.refs_7_
  19.5 0.7 %collective-permute-done.4.refs_2_ = f32[72,256]{1,0:T(8,128)S(1)} collective-permute-done((f32[72,256]{1,0:T(8,128)S(1)}, f32[72,256]{1,0:T(8,128)S(1)}, u32[]{:S(2)}, u32[]{:S(2)}) %collective-permute-start.4) | collective-permute-done | bytes 73760 | tf_op jit(solution)/shard_map/ppermute | solution.py:357
  20.2 0.0 collective-permute-done.3.refs_1_
  20.2 1.4 %shard_map.53 = (f32[64,256]{1,0:T(8,128)S(1)}, f32[64,256]{1,0:T(8,128)S(1)}, f32[2,8,512]{2,1,0:T(8,128)S(1)}, bf16[2,512,512]{2,1,0:T(8,128)(2,1)S(1)}, bf16[2,512,512]{2,1,0:T(8,128)(2,1)S(1)}) custom-call(f32[72,256]{1,0:T(8,128)S(1)} %shard_map.47.own.one.refs_0_, f32[72,256]{1,0:T(8,128)S(1)} %collective-permute-done.3.refs_1_, ...), custom_call_target="tpu_custom_call" | custom-call | flops 134217728 | bytes 262144 | tf_op jit(solution)/shard_map/pallas_call | solution.py:472
  21.6 2.9 %collective-permute-start.10 = (f32[64,256]{1,0:T(8,128)S(1)}, f32[64,256]{1,0:T(8,128)S(1)}, u32[]{:S(2)}, u32[]{:S(2)}) collective-permute-start(f32[64,256]{1,0:T(8,128)S(1)} %get-tuple-element.37.refs_0_), channel_id=1, source_target_pairs={{0,12},{1,13},{2,14},{3,15},{4,8},{5,9},{6,10},{7,11},{8,4},{9,5},... | collective-permute-start | bytes 196616 | tf_op jit(solution)/shard_map/ppermute | solution.py:357
  24.5 0.0 collective-permute-start.9
  24.5 1.5 %collective-permute-start.8 = (f32[64,256]{1,0:T(8,128)S(1)}, f32[64,256]{1,0:T(8,128)S(1)}, u32[]{:S(2)}, u32[]{:S(2)}) collective-permute-start(f32[64,256]{1,0:T(8,128)S(1)} %get-tuple-element.37.refs_0_), channel_id=1, source_target_pairs={{0,4},{1,5},{2,6},{3,7},{4,0},{5,1},{6,2},{7,3},{8,12},{9,13},{10,... | collective-permute-start | bytes 196616 | tf_op jit(solution)/shard_map/ppermute | solution.py:357
  26.0 1.3 %shard_map.54 = (bf16[256,8192]{1,0:T(8,128)(2,1)S(1)}, bf16[256,8192]{1,0:T(8,128)(2,1)S(1)}, f32[16,256]{1,0:T(8,128)S(1)}, f32[16,256]{1,0:T(8,128)S(1)}, f32...) custom-call(s32[64,128]{1,0:T(8,128)S(1)} %get-tuple-element.41.mask_ids.refs_5_, f32[64,256]{1,0:T(8,128)S(1)} %get-tuple-element.42.mean), custom_call_target="tpu_custom_call" | custom-call | flops 536870912 | bytes 8388608 | tf_op jit(solution)/shard_map/pallas_call | solution.py:486
  27.2 0.1 collective-permute-start.14
  27.3 0.6 %collective-permute-start.15 = (f32[16,256]{1,0:T(8,128)S(1)}, f32[16,256]{1,0:T(8,128)S(1)}, u32[]{:S(2)}, u32[]{:S(2)}) collective-permute-start(f32[16,256]{1,0:T(8,128)S(1)} %get-tuple-element.50), channel_id=1, source_target_pairs={{0,2},{1,3},{2,0},{3,1},{4,6},{5,7},{6,4},{7,5},{8,10},{9,11},{10,... | collective-permute-start | bytes 49160 | tf_op jit(solution)/shard_map/ppermute | solution.py:352
  27.9 0.4 %collective-permute-done.10.refs_3_ = f32[64,256]{1,0:T(8,128)S(1)} collective-permute-done((f32[64,256]{1,0:T(8,128)S(1)}, f32[64,256]{1,0:T(8,128)S(1)}, u32[]{:S(2)}, u32[]{:S(2)}) %collective-permute-start.10) | collective-permute-done | bytes 65568 | tf_op jit(solution)/shard_map/ppermute | solution.py:357
  28.3 0.9 %collective-permute-start.16 = (f32[16,256]{1,0:T(8,128)S(1)}, f32[16,256]{1,0:T(8,128)S(1)}, u32[]{:S(2)}, u32[]{:S(2)}) collective-permute-start(f32[16,256]{1,0:T(8,128)S(1)} %get-tuple-element.51), channel_id=1, source_target_pairs={{0,3},{1,2},{2,1},{3,0},{4,7},{5,6},{6,5},{7,4},{8,11},{9,10},{10,... | collective-permute-start | bytes 49160 | tf_op jit(solution)/shard_map/ppermute | solution.py:352
  29.2 1.4 %collective-permute-done.9.refs_2_ = f32[64,256]{1,0:T(8,128)S(1)} collective-permute-done((f32[64,256]{1,0:T(8,128)S(1)}, f32[64,256]{1,0:T(8,128)S(1)}, u32[]{:S(2)}, u32[]{:S(2)}) %collective-permute-start.9) | collective-permute-done | bytes 65568 | tf_op jit(solution)/shard_map/ppermute | solution.py:357
  30.6 0.0 collective-permute-done.8.refs_1_
  30.6 0.8 %shard_map.55 = (f32[16,256]{1,0:T(8,128)S(1)}, f32[16,256]{1,0:T(8,128)S(1)}, f32[16,256]{1,0:T(8,128)S(1)}, f32[16,256]{1,0:T(8,128)S(1)}) custom-call(f32[64,256]{1,0:T(8,128)S(1)} %get-tuple-element.37.refs_0_, f32[64,256]{1,0:T(8,128)S(1)} %collective-permute-done.8.refs_1_, f32[64,256]{1,0:T(8,128)S(1)} %collective-permute-done.9.refs_2_, ...), custom_call_target="tpu_custom_call" | custom-call | flops 134217728 | bytes 262144 | tf_op jit(solution)/shard_map/pallas_call | solution.py:497
  31.4 0.0 collective-permute-start.11
  31.4 0.6 %collective-permute-start.12 = (f32[16,256]{1,0:T(8,128)S(1)}, f32[16,256]{1,0:T(8,128)S(1)}, u32[]{:S(2)}, u32[]{:S(2)}) collective-permute-start(f32[16,256]{1,0:T(8,128)S(1)} %get-tuple-element.46), channel_id=1, source_target_pairs={{0,2},{1,3},{2,0},{3,1},{4,6},{5,7},{6,4},{7,5},{8,10},{9,11},{10,... | collective-permute-start | bytes 49160 | tf_op jit(solution)/shard_map/ppermute | solution.py:352
  32.1 0.0 collective-permute-done.14.refs_1_
  32.1 1.2 %collective-permute-start.13 = (f32[16,256]{1,0:T(8,128)S(1)}, f32[16,256]{1,0:T(8,128)S(1)}, u32[]{:S(2)}, u32[]{:S(2)}) collective-permute-start(f32[16,256]{1,0:T(8,128)S(1)} %get-tuple-element.47), channel_id=1, source_target_pairs={{0,3},{1,2},{2,1},{3,0},{4,7},{5,6},{6,5},{7,4},{8,11},{9,10},{10,... | collective-permute-start | bytes 49160 | tf_op jit(solution)/shard_map/ppermute | solution.py:352
  33.3 0.0 collective-permute-done.15.refs_2_
  33.3 0.0 collective-permute-done.16.refs_3_
  33.3 1.3 %shard_map.56.refs_4_ = f32[64,8192]{1,0:T(8,128)S(1)} custom-call(f32[16,256]{1,0:T(8,128)S(1)} %get-tuple-element.48.refs_0_, f32[16,256]{1,0:T(8,128)S(1)} %collective-permute-done.14.refs_1_, f32[16,256]{1,0:T(8,128)S(1)} %collective-permute-done.15.refs_2_, f32[16,256]{1,0:T(8,128)S(1)} %collective-permute-done.16.refs_3_, ...), custom_call_target="tpu_custom_call" | custom-call | flops 536870912 | bytes 4194304 | tf_op jit(solution)/shard_map/pallas_call | solution.py:507
  34.6 0.0 collective-permute-done.11.refs_1_
  34.6 0.7 %collective-permute-done.12.refs_2_ = f32[16,256]{1,0:T(8,128)S(1)} collective-permute-done((f32[16,256]{1,0:T(8,128)S(1)}, f32[16,256]{1,0:T(8,128)S(1)}, u32[]{:S(2)}, u32[]{:S(2)}) %collective-permute-start.12) | collective-permute-done | bytes 16416 | tf_op jit(solution)/shard_map/ppermute | solution.py:352
  35.3 0.0 collective-permute-done.13.refs_3_
  35.4 1.6 %shard_map.57 = f32[64,8192]{1,0:T(8,128)} custom-call(f32[16,256]{1,0:T(8,128)S(1)} %get-tuple-element.44.refs_0_, f32[16,256]{1,0:T(8,128)S(1)} %collective-permute-done.11.refs_1_, f32[16,256]{1,0:T(8,128)S(1)} %collective-permute-done.12.refs_2_, f32[16,256]{1,0:T(8,128)S(1)} %collective-permute-done.13.refs_3_, f32[64,8192]{1,0:T(8,128)S(1)} %shard_map.56.refs_4_, ...), custom_call_target="tpu_custom_call" | custom-call | flops 536870912 | bytes 4194304 | tf_op jit(solution)/shard_map/pallas_call | solution.py:516
  (2 shorter events, 0.0 us)
Async XLA Ops:
  3.4 6.4 %collective-permute-start = (f32[56,256]{1,0:T(8,128)S(1)}, f32[56,256]{1,0:T(8,128)S(1)}, u32[]{:S(2)}, u32[]{:S(2)}) collective-permute-start(f32[56,256]{1,0:T(8,128)S(1)} %get-tuple-element.31), channel_id=1, source_target_pairs={{0,1},{1,0},{2,3},{3,2},{4,5},{5,4},{6,7},{7,6},{8,9},{9,8},{10,11... | collective-permute-start | bytes 172040 | tf_op jit(solution)/shard_map/ppermute | solution.py:352
  3.9 4.4 %collective-permute-start.1 = (f32[24,256]{1,0:T(8,128)S(1)}, f32[24,256]{1,0:T(8,128)S(1)}, u32[]{:S(2)}, u32[]{:S(2)}) collective-permute-start(f32[24,256]{1,0:T(8,128)S(1)} %get-tuple-element.32), channel_id=1, source_target_pairs={{0,2},{1,3},{2,0},{3,1},{4,6},{5,7},{6,4},{7,5},{8,10},{9,11},{10,... | collective-permute-start | bytes 73736 | tf_op jit(solution)/shard_map/ppermute | solution.py:352
  6.5 3.3 %collective-permute-start.2 = (f32[24,256]{1,0:T(8,128)S(1)}, f32[24,256]{1,0:T(8,128)S(1)}, u32[]{:S(2)}, u32[]{:S(2)}) collective-permute-start(f32[24,256]{1,0:T(8,128)S(1)} %get-tuple-element.33), channel_id=1, source_target_pairs={{0,3},{1,2},{2,1},{3,0},{4,7},{5,6},{6,5},{7,4},{8,11},{9,10},{10,... | collective-permute-start | bytes 73736 | tf_op jit(solution)/shard_map/ppermute | solution.py:352
  6.6 7.7 %collective-permute-start.6 = (f32[40,256]{1,0:T(8,128)S(1)}, f32[40,256]{1,0:T(8,128)S(1)}, u32[]{:S(2)}, u32[]{:S(2)}) collective-permute-start(f32[40,256]{1,0:T(8,128)S(1)} %shard_map.48), channel_id=1, source_target_pairs={{0,2},{1,3},{2,0},{3,1},{4,6},{5,7},{6,4},{7,5},{8,10},{9,11},{10,... | collective-permute-start | bytes 122888 | tf_op jit(solution)/shard_map/ppermute | solution.py:437
  9.8 9.4 %collective-permute-start.5 = (f32[72,256]{1,0:T(8,128)S(1)}, f32[72,256]{1,0:T(8,128)S(1)}, u32[]{:S(2)}, u32[]{:S(2)}) collective-permute-start(f32[72,256]{1,0:T(8,128)S(1)} %shard_map.47.own.one.refs_0_), channel_id=1, source_target_pairs={{0,12},{1,13},{2,14},{3,15},{4,8},{5,9},{6,10},{7,11},{8,4},{9,5},... | collective-permute-start | bytes 221192 | tf_op jit(solution)/shard_map/ppermute | solution.py:357
  13.4 6.8 %collective-permute-start.4 = (f32[72,256]{1,0:T(8,128)S(1)}, f32[72,256]{1,0:T(8,128)S(1)}, u32[]{:S(2)}, u32[]{:S(2)}) collective-permute-start(f32[72,256]{1,0:T(8,128)S(1)} %shard_map.47.own.one.refs_0_), channel_id=1, source_target_pairs={{0,8},{1,9},{2,10},{3,11},{4,12},{5,13},{6,14},{7,15},{8,0},{9,1},... | collective-permute-start | bytes 221192 | tf_op jit(solution)/shard_map/ppermute | solution.py:357
  13.4 6.8 %collective-permute-start.3 = (f32[72,256]{1,0:T(8,128)S(1)}, f32[72,256]{1,0:T(8,128)S(1)}, u32[]{:S(2)}, u32[]{:S(2)}) collective-permute-start(f32[72,256]{1,0:T(8,128)S(1)} %shard_map.47.own.one.refs_0_), channel_id=1, source_target_pairs={{0,4},{1,5},{2,6},{3,7},{4,0},{5,1},{6,2},{7,3},{8,12},{9,13},{10,... | collective-permute-start | bytes 221192 | tf_op jit(solution)/shard_map/ppermute | solution.py:357
  14.5 3.4 %collective-permute-start.7 = (f32[40,256]{1,0:T(8,128)S(1)}, f32[40,256]{1,0:T(8,128)S(1)}, u32[]{:S(2)}, u32[]{:S(2)}) collective-permute-start(f32[40,256]{1,0:T(8,128)S(1)} %get-tuple-element.36), channel_id=1, source_target_pairs={{0,1},{1,0},{2,3},{3,2},{4,5},{5,4},{6,7},{7,6},{8,9},{9,8},{10,11... | collective-permute-start | bytes 122888 | tf_op jit(solution)/shard_map/ppermute | solution.py:437
  21.6 6.7 %collective-permute-start.10 = (f32[64,256]{1,0:T(8,128)S(1)}, f32[64,256]{1,0:T(8,128)S(1)}, u32[]{:S(2)}, u32[]{:S(2)}) collective-permute-start(f32[64,256]{1,0:T(8,128)S(1)} %get-tuple-element.37.refs_0_), channel_id=1, source_target_pairs={{0,12},{1,13},{2,14},{3,15},{4,8},{5,9},{6,10},{7,11},{8,4},{9,5},... | collective-permute-start | bytes 196616 | tf_op jit(solution)/shard_map/ppermute | solution.py:357
  24.5 6.1 %collective-permute-start.9 = (f32[64,256]{1,0:T(8,128)S(1)}, f32[64,256]{1,0:T(8,128)S(1)}, u32[]{:S(2)}, u32[]{:S(2)}) collective-permute-start(f32[64,256]{1,0:T(8,128)S(1)} %get-tuple-element.37.refs_0_), channel_id=1, source_target_pairs={{0,8},{1,9},{2,10},{3,11},{4,12},{5,13},{6,14},{7,15},{8,0},{9,1},... | collective-permute-start | bytes 196616 | tf_op jit(solution)/shard_map/ppermute | solution.py:357
  24.5 6.2 %collective-permute-start.8 = (f32[64,256]{1,0:T(8,128)S(1)}, f32[64,256]{1,0:T(8,128)S(1)}, u32[]{:S(2)}, u32[]{:S(2)}) collective-permute-start(f32[64,256]{1,0:T(8,128)S(1)} %get-tuple-element.37.refs_0_), channel_id=1, source_target_pairs={{0,4},{1,5},{2,6},{3,7},{4,0},{5,1},{6,2},{7,3},{8,12},{9,13},{10,... | collective-permute-start | bytes 196616 | tf_op jit(solution)/shard_map/ppermute | solution.py:357
  27.2 4.8 %collective-permute-start.14 = (f32[16,256]{1,0:T(8,128)S(1)}, f32[16,256]{1,0:T(8,128)S(1)}, u32[]{:S(2)}, u32[]{:S(2)}) collective-permute-start(f32[16,256]{1,0:T(8,128)S(1)} %get-tuple-element.49), channel_id=1, source_target_pairs={{0,1},{1,0},{2,3},{3,2},{4,5},{5,4},{6,7},{7,6},{8,9},{9,8},{10,11... | collective-permute-start | bytes 49160 | tf_op jit(solution)/shard_map/ppermute | solution.py:352
  27.3 6.0 %collective-permute-start.15 = (f32[16,256]{1,0:T(8,128)S(1)}, f32[16,256]{1,0:T(8,128)S(1)}, u32[]{:S(2)}, u32[]{:S(2)}) collective-permute-start(f32[16,256]{1,0:T(8,128)S(1)} %get-tuple-element.50), channel_id=1, source_target_pairs={{0,2},{1,3},{2,0},{3,1},{4,6},{5,7},{6,4},{7,5},{8,10},{9,11},{10,... | collective-permute-start | bytes 49160 | tf_op jit(solution)/shard_map/ppermute | solution.py:352
  28.3 5.0 %collective-permute-start.16 = (f32[16,256]{1,0:T(8,128)S(1)}, f32[16,256]{1,0:T(8,128)S(1)}, u32[]{:S(2)}, u32[]{:S(2)}) collective-permute-start(f32[16,256]{1,0:T(8,128)S(1)} %get-tuple-element.51), channel_id=1, source_target_pairs={{0,3},{1,2},{2,1},{3,0},{4,7},{5,6},{6,5},{7,4},{8,11},{9,10},{10,... | collective-permute-start | bytes 49160 | tf_op jit(solution)/shard_map/ppermute | solution.py:352
  31.4 3.2 %collective-permute-start.11 = (f32[16,256]{1,0:T(8,128)S(1)}, f32[16,256]{1,0:T(8,128)S(1)}, u32[]{:S(2)}, u32[]{:S(2)}) collective-permute-start(f32[16,256]{1,0:T(8,128)S(1)} %get-tuple-element.45), channel_id=1, source_target_pairs={{0,1},{1,0},{2,3},{3,2},{4,5},{5,4},{6,7},{7,6},{8,9},{9,8},{10,11... | collective-permute-start | bytes 49160 | tf_op jit(solution)/shard_map/ppermute | solution.py:352
  31.4 3.9 %collective-permute-start.12 = (f32[16,256]{1,0:T(8,128)S(1)}, f32[16,256]{1,0:T(8,128)S(1)}, u32[]{:S(2)}, u32[]{:S(2)}) collective-permute-start(f32[16,256]{1,0:T(8,128)S(1)} %get-tuple-element.46), channel_id=1, source_target_pairs={{0,2},{1,3},{2,0},{3,1},{4,6},{5,7},{6,4},{7,5},{8,10},{9,11},{10,... | collective-permute-start | bytes 49160 | tf_op jit(solution)/shard_map/ppermute | solution.py:352
  32.1 3.3 %collective-permute-start.13 = (f32[16,256]{1,0:T(8,128)S(1)}, f32[16,256]{1,0:T(8,128)S(1)}, u32[]{:S(2)}, u32[]{:S(2)}) collective-permute-start(f32[16,256]{1,0:T(8,128)S(1)} %get-tuple-element.47), channel_id=1, source_target_pairs={{0,3},{1,2},{2,1},{3,0},{4,7},{5,6},{6,5},{7,4},{8,11},{9,10},{10,... | collective-permute-start | bytes 49160 | tf_op jit(solution)/shard_map/ppermute | solution.py:352

commit v33 on v28

--- a/solution.py
+++ b/solution.py
@@ -331,7 +331,7 @@
     parts, (before, mask_ids), tables, (out, means, y, sems) = refs[:NEAR], refs[NEAR : NEAR + 2], refs[NEAR + 2 : -4], refs[-4:]
     outs = column_copies(y, out, sems)
     columns, slots = means.shape
-    second = own_means(parts, means)
+    second = own_means([*parts[:2], parts[3], parts[2]], means)
     for b in range(len(outs)):
         at = slice(b * BLOCK, (b + 1) * BLOCK)
         found = tables[0][:, at] if tables else one_hot(row(mask_ids, b, BLOCK), slots)
@@ -515,7 +515,7 @@
         [pltpu.VMEM((columns, slots), F32), pltpu.VMEM(whole, F32), sems],
         work,
         8 * columns * rows_dev,
-    )(*arrived, before, mask_ids, *spreads[:1])
+    )(*arrived[:2], arrived[3], arrived[2], before, mask_ids, *spreads[:1])
 
 
 def solution(mesh):

time: 36.6 us -> 37.2 us (1.016)
  transfers between devices with their start and end apart: 17 -> 17, of which waited for: 5 -> 4; matrix products, arithmetic and copies ran while one was open for 0% -> 0% of each run, Pallas kernels for 24% -> 24%
where the time goes in v33:
time: 37.2 us; the launch traced here: 37.1 us
  starting transfers between devices  18 us (48%)
  Pallas kernels  15.3 us (41%)
  waiting for transfers between devices  3.67 us (10%)
    ppermute x6, starting transfers between devices, far_share(): return [one] + [lax.ppermute(one, 'rows', step) for step in steps]  8.85 us
    ppermute x9, starting transfers between devices, near_exchange(): lax.ppermute(one, 'rows', step)  7.27 us
    pallas_call x4, Pallas kernels, pair_counts(): call(functools.partial(pairs_kernel, pad, start, 1), [array((1, slots, 2...  4.92 us
    pallas_call x1, Pallas kernels, body(): call(functools.partial(sums_kernel, pad, slots // n), [short, message, sh...  3.37 us
    ppermute x6, waiting for transfers between devices, far_share(): return [one] + [lax.ppermute(one, 'rows', step) for step in steps]  2.42 us
    ppermute x2, starting transfers between devices, near_step(): return lax.ppermute(one, 'rows', [(i, i ^ step) for i in range(n)])  1.87 us
    pallas_call x1, Pallas kernels, body(): call(last_kernel, array(whole, F32), [vmem] * (NEAR + 2 + len(spreads[:1]...  1.62 us
    pallas_call x1, Pallas kernels, body(): call(functools.partial(change_kernel, far, part, len(tables)), [of_near,...  1.37 us
  transfers between devices with their start and end apart: 17, of which 4 were waited for; matrix products, arithmetic and copies ran while one was open for 0% of the time, Pallas kernels for 24%

profile of v33, /device:TPU:0, one launch (start us, length us, event | category | flops | bytes accessed | tf_op | source)
XLA Modules:
  0.0 37.1 jit_solution(18116948723695254373)
XLA Ops:
  0.0 3.4 %shard_map.46 = (f32[24,256]{1,0:T(8,128)S(1)}, f32[56,256]{1,0:T(8,128)S(1)}, f32[24,256]{1,0:T(8,128)S(1)}, f32[24,256]{1,0:T(8,128)S(1)}, f32[40,256]{1,0:T(8...) custom-call(f32[64,8192]{1,0:T(8,128)} %refs_0_.1, s32[8,128]{1,0:T(8,128)} %bitcast.4, ...), custom_call_target="tpu_custom_call" | custom-call | flops 1073741824 | bytes 2097152 | tf_op jit(solution)/shard_map/pallas_call | solution.py:395
  3.4 0.5 %collective-permute-start = (f32[56,256]{1,0:T(8,128)S(1)}, f32[56,256]{1,0:T(8,128)S(1)}, u32[]{:S(2)}, u32[]{:S(2)}) collective-permute-start(f32[56,256]{1,0:T(8,128)S(1)} %get-tuple-element.33), channel_id=1, source_target_pairs={{0,1},{1,0},{2,3},{3,2},{4,5},{5,4},{6,7},{7,6},{8,9},{9,8},{10,11... | collective-permute-start | bytes 172040 | tf_op jit(solution)/shard_map/ppermute | solution.py:346
  3.9 2.6 %collective-permute-start.1 = (f32[24,256]{1,0:T(8,128)S(1)}, f32[24,256]{1,0:T(8,128)S(1)}, u32[]{:S(2)}, u32[]{:S(2)}) collective-permute-start(f32[24,256]{1,0:T(8,128)S(1)} %get-tuple-element.34), channel_id=1, source_target_pairs={{0,2},{1,3},{2,0},{3,1},{4,6},{5,7},{6,4},{7,5},{8,10},{9,11},{10,... | collective-permute-start | bytes 73736 | tf_op jit(solution)/shard_map/ppermute | solution.py:346
  6.5 0.1 collective-permute-start.2
  6.6 1.2 %shard_map.47 = (bf16[1,256,512]{2,1,0:T(8,128)(2,1)S(1)}, f32[40,256]{1,0:T(8,128)S(1)}) custom-call(f32[40,256]{1,0:T(8,128)S(1)} %get-tuple-element.36.refs_0_), custom_call_target="tpu_custom_call" | custom-call | flops 134217728 | bytes 262144 | tf_op jit(solution)/shard_map/pallas_call | solution.py:415
  7.8 1.8 %collective-permute-start.6 = (f32[40,256]{1,0:T(8,128)S(1)}, f32[40,256]{1,0:T(8,128)S(1)}, u32[]{:S(2)}, u32[]{:S(2)}) collective-permute-start(f32[40,256]{1,0:T(8,128)S(1)} %get-tuple-element.38), channel_id=1, source_target_pairs={{0,2},{1,3},{2,0},{3,1},{4,6},{5,7},{6,4},{7,5},{8,10},{9,11},{10,... | collective-permute-start | bytes 122888 | tf_op jit(solution)/shard_map/ppermute | solution.py:430
  9.6 0.0 collective-permute-done.1.refs_2_
  9.6 0.2 collective-permute-done.2.refs_3_
  9.7 0.0 collective-permute-done.refs_1_.refs_0_
  9.8 3.7 %collective-permute-start.5 = (f32[72,256]{1,0:T(8,128)S(1)}, f32[72,256]{1,0:T(8,128)S(1)}, u32[]{:S(2)}, u32[]{:S(2)}) collective-permute-start(f32[72,256]{1,0:T(8,128)S(1)} %shard_map.48.own.one.refs_0_), channel_id=1, source_target_pairs={{0,12},{1,13},{2,14},{3,15},{4,8},{5,9},{6,10},{7,11},{8,4},{9,5},... | collective-permute-start | bytes 221192 | tf_op jit(solution)/shard_map/ppermute | solution.py:351
  13.4 0.0 collective-permute-start.4
  13.4 0.8 %collective-permute-start.3 = (f32[72,256]{1,0:T(8,128)S(1)}, f32[72,256]{1,0:T(8,128)S(1)}, u32[]{:S(2)}, u32[]{:S(2)}) collective-permute-start(f32[72,256]{1,0:T(8,128)S(1)} %shard_map.48.own.one.refs_0_), channel_id=1, source_target_pairs={{0,4},{1,5},{2,6},{3,7},{4,0},{5,1},{6,2},{7,3},{8,12},{9,13},{10,... | collective-permute-start | bytes 221192 | tf_op jit(solution)/shard_map/ppermute | solution.py:351
  14.2 0.0 collective-permute-done.6.passed.refs_0_
  14.2 0.3 shard_map.49
  14.5 0.1 collective-permute-start.7
  14.6 1.2 %shard_map.52.refs_8_ = bf16[1,256,512]{2,1,0:T(8,128)(2,1)S(1)} custom-call(f32[40,256]{1,0:T(8,128)S(1)} %collective-permute-done.6.passed.refs_0_), custom_call_target="tpu_custom_call" | custom-call | flops 134217728 | bytes 262144 | tf_op jit(solution)/shard_map/pallas_call | solution.py:415
  15.8 1.2 %shard_map.51.refs_7_ = bf16[1,256,512]{2,1,0:T(8,128)(2,1)S(1)} custom-call(f32[56,256]{1,0:T(8,128)S(1)} %collective-permute-done.refs_1_.refs_0_), custom_call_target="tpu_custom_call" | custom-call | flops 134217728 | bytes 262144 | tf_op jit(solution)/shard_map/pallas_call | solution.py:415
  17.1 0.0 collective-permute-done.7.refs_0_
  17.1 1.2 %shard_map.53.refs_9_ = bf16[1,256,512]{2,1,0:T(8,128)(2,1)S(1)} custom-call(f32[40,256]{1,0:T(8,128)S(1)} %collective-permute-done.7.refs_0_), custom_call_target="tpu_custom_call" | custom-call | flops 134217728 | bytes 262144 | tf_op jit(solution)/shard_map/pallas_call | solution.py:415
  18.3 0.0 collective-permute-done.5.one.refs_3_
  18.3 0.3 shard_map.50.refs_5_.refs_7_
  18.7 1.3 %collective-permute-done.4.refs_2_ = f32[72,256]{1,0:T(8,128)S(1)} collective-permute-done((f32[72,256]{1,0:T(8,128)S(1)}, f32[72,256]{1,0:T(8,128)S(1)}, u32[]{:S(2)}, u32[]{:S(2)}) %collective-permute-start.4) | collective-permute-done | bytes 73760 | tf_op jit(solution)/shard_map/ppermute | solution.py:351
  19.9 0.0 collective-permute-done.3.refs_1_
  19.9 1.4 %shard_map.54 = (f32[64,256]{1,0:T(8,128)S(1)}, f32[64,256]{1,0:T(8,128)S(1)}, f32[2,8,512]{2,1,0:T(8,128)S(1)}, bf16[2,512,512]{2,1,0:T(8,128)(2,1)S(1)}, bf16[2,512,512]{2,1,0:T(8,128)(2,1)S(1)}) custom-call(f32[72,256]{1,0:T(8,128)S(1)} %shard_map.48.own.one.refs_0_, f32[72,256]{1,0:T(8,128)S(1)} %collective-permute-done.3.refs_1_, ...), custom_call_target="tpu_custom_call" | custom-call | flops 134217728 | bytes 262144 | tf_op jit(solution)/shard_map/pallas_call | solution.py:466
  21.3 2.5 %collective-permute-start.10 = (f32[64,256]{1,0:T(8,128)S(1)}, f32[64,256]{1,0:T(8,128)S(1)}, u32[]{:S(2)}, u32[]{:S(2)}) collective-permute-start(f32[64,256]{1,0:T(8,128)S(1)} %get-tuple-element.41.refs_0_), channel_id=1, source_target_pairs={{0,12},{1,13},{2,14},{3,15},{4,8},{5,9},{6,10},{7,11},{8,4},{9,5},... | collective-permute-start | bytes 196616 | tf_op jit(solution)/shard_map/ppermute | solution.py:351
  23.8 0.0 collective-permute-start.9
  23.8 1.9 %collective-permute-start.8 = (f32[64,256]{1,0:T(8,128)S(1)}, f32[64,256]{1,0:T(8,128)S(1)}, u32[]{:S(2)}, u32[]{:S(2)}) collective-permute-start(f32[64,256]{1,0:T(8,128)S(1)} %get-tuple-element.41.refs_0_), channel_id=1, source_target_pairs={{0,4},{1,5},{2,6},{3,7},{4,0},{5,1},{6,2},{7,3},{8,12},{9,13},{10,... | collective-permute-start | bytes 196616 | tf_op jit(solution)/shard_map/ppermute | solution.py:351
  25.7 1.3 %shard_map.55 = (bf16[256,8192]{1,0:T(8,128)(2,1)S(1)}, bf16[256,8192]{1,0:T(8,128)(2,1)S(1)}, f32[16,256]{1,0:T(8,128)S(1)}, f32[16,256]{1,0:T(8,128)S(1)}, f32...) custom-call(s32[64,128]{1,0:T(8,128)S(1)} %get-tuple-element.45.mask_ids.refs_5_, f32[64,256]{1,0:T(8,128)S(1)} %get-tuple-element.46.mean), custom_call_target="tpu_custom_call" | custom-call | flops 536870912 | bytes 8388608 | tf_op jit(solution)/shard_map/pallas_call | solution.py:480
  27.0 0.1 collective-permute-start.14
  27.1 0.8 %collective-permute-start.15 = (f32[16,256]{1,0:T(8,128)S(1)}, f32[16,256]{1,0:T(8,128)S(1)}, u32[]{:S(2)}, u32[]{:S(2)}) collective-permute-start(f32[16,256]{1,0:T(8,128)S(1)} %get-tuple-element.54), channel_id=1, source_target_pairs={{0,2},{1,3},{2,0},{3,1},{4,6},{5,7},{6,4},{7,5},{8,10},{9,11},{10,... | collective-permute-start | bytes 49160 | tf_op jit(solution)/shard_map/ppermute | solution.py:346
  27.9 0.0 collective-permute-done.10.refs_3_
  27.9 1.0 %collective-permute-start.16 = (f32[16,256]{1,0:T(8,128)S(1)}, f32[16,256]{1,0:T(8,128)S(1)}, u32[]{:S(2)}, u32[]{:S(2)}) collective-permute-start(f32[16,256]{1,0:T(8,128)S(1)} %get-tuple-element.55), channel_id=1, source_target_pairs={{0,3},{1,2},{2,1},{3,0},{4,7},{5,6},{6,5},{7,4},{8,11},{9,10},{10,... | collective-permute-start | bytes 49160 | tf_op jit(solution)/shard_map/ppermute | solution.py:346
  28.9 1.1 %collective-permute-done.9.refs_2_ = f32[64,256]{1,0:T(8,128)S(1)} collective-permute-done((f32[64,256]{1,0:T(8,128)S(1)}, f32[64,256]{1,0:T(8,128)S(1)}, u32[]{:S(2)}, u32[]{:S(2)}) %collective-permute-start.9) | collective-permute-done | bytes 65568 | tf_op jit(solution)/shard_map/ppermute | solution.py:351
  30.1 0.0 collective-permute-done.8.refs_1_
  30.1 0.8 %shard_map.56 = (f32[16,256]{1,0:T(8,128)S(1)}, f32[16,256]{1,0:T(8,128)S(1)}, f32[16,256]{1,0:T(8,128)S(1)}, f32[16,256]{1,0:T(8,128)S(1)}) custom-call(f32[64,256]{1,0:T(8,128)S(1)} %get-tuple-element.41.refs_0_, f32[64,256]{1,0:T(8,128)S(1)} %collective-permute-done.8.refs_1_, f32[64,256]{1,0:T(8,128)S(1)} %collective-permute-done.9.refs_2_, ...), custom_call_target="tpu_custom_call" | custom-call | flops 134217728 | bytes 262144 | tf_op jit(solution)/shard_map/pallas_call | solution.py:491
  30.8 0.0 collective-permute-start.11
  30.8 0.8 %collective-permute-start.12 = (f32[16,256]{1,0:T(8,128)S(1)}, f32[16,256]{1,0:T(8,128)S(1)}, u32[]{:S(2)}, u32[]{:S(2)}) collective-permute-start(f32[16,256]{1,0:T(8,128)S(1)} %get-tuple-element.50), channel_id=1, source_target_pairs={{0,3},{1,2},{2,1},{3,0},{4,7},{5,6},{6,5},{7,4},{8,11},{9,10},{10,... | collective-permute-start | bytes 49160 | tf_op jit(solution)/shard_map/ppermute | solution.py:346
  31.7 0.0 collective-permute-done.14.refs_1_
  31.7 1.3 %collective-permute-start.13 = (f32[16,256]{1,0:T(8,128)S(1)}, f32[16,256]{1,0:T(8,128)S(1)}, u32[]{:S(2)}, u32[]{:S(2)}) collective-permute-start(f32[16,256]{1,0:T(8,128)S(1)} %get-tuple-element.51), channel_id=1, source_target_pairs={{0,2},{1,3},{2,0},{3,1},{4,6},{5,7},{6,4},{7,5},{8,10},{9,11},{10,... | collective-permute-start | bytes 49160 | tf_op jit(solution)/shard_map/ppermute | solution.py:346
  33.0 0.0 collective-permute-done.15.refs_2_
  33.0 0.0 collective-permute-done.16.refs_3_
  33.0 1.3 %shard_map.57.refs_4_ = f32[64,8192]{1,0:T(8,128)S(1)} custom-call(f32[16,256]{1,0:T(8,128)S(1)} %get-tuple-element.52.refs_0_, f32[16,256]{1,0:T(8,128)S(1)} %collective-permute-done.14.refs_1_, f32[16,256]{1,0:T(8,128)S(1)} %collective-permute-done.15.refs_2_, f32[16,256]{1,0:T(8,128)S(1)} %collective-permute-done.16.refs_3_, ...), custom_call_target="tpu_custom_call" | custom-call | flops 536870912 | bytes 4194304 | tf_op jit(solution)/shard_map/pallas_call | solution.py:501
  34.3 0.0 collective-permute-done.11.refs_1_
  34.3 0.0 collective-permute-done.12.refs_2_
  34.4 1.1 %collective-permute-done.13.refs_3_ = f32[16,256]{1,0:T(8,128)S(1)} collective-permute-done((f32[16,256]{1,0:T(8,128)S(1)}, f32[16,256]{1,0:T(8,128)S(1)}, u32[]{:S(2)}, u32[]{:S(2)}) %collective-permute-start.13) | collective-permute-done | bytes 16416 | tf_op jit(solution)/shard_map/ppermute | solution.py:346
  35.4 1.6 %shard_map.58 = f32[64,8192]{1,0:T(8,128)} custom-call(f32[16,256]{1,0:T(8,128)S(1)} %get-tuple-element.48.refs_0_, f32[16,256]{1,0:T(8,128)S(1)} %collective-permute-done.11.refs_1_, f32[16,256]{1,0:T(8,128)S(1)} %collective-permute-done.12.refs_2_, f32[16,256]{1,0:T(8,128)S(1)} %collective-permute-done.13.refs_3_, f32[64,8192]{1,0:T(8,128)S(1)} %shard_map.57.refs_4_, ...), custom_call_target="tpu_custom_call" | custom-call | flops 536870912 | bytes 4194304 | tf_op jit(solution)/shard_map/pallas_call | solution.py:510
  (1 shorter events, 0.0 us)
Async XLA Ops:
  3.4 6.4 %collective-permute-start = (f32[56,256]{1,0:T(8,128)S(1)}, f32[56,256]{1,0:T(8,128)S(1)}, u32[]{:S(2)}, u32[]{:S(2)}) collective-permute-start(f32[56,256]{1,0:T(8,128)S(1)} %get-tuple-element.33), channel_id=1, source_target_pairs={{0,1},{1,0},{2,3},{3,2},{4,5},{5,4},{6,7},{7,6},{8,9},{9,8},{10,11... | collective-permute-start | bytes 172040 | tf_op jit(solution)/shard_map/ppermute | solution.py:346
  3.9 5.7 %collective-permute-start.1 = (f32[24,256]{1,0:T(8,128)S(1)}, f32[24,256]{1,0:T(8,128)S(1)}, u32[]{:S(2)}, u32[]{:S(2)}) collective-permute-start(f32[24,256]{1,0:T(8,128)S(1)} %get-tuple-element.34), channel_id=1, source_target_pairs={{0,2},{1,3},{2,0},{3,1},{4,6},{5,7},{6,4},{7,5},{8,10},{9,11},{10,... | collective-permute-start | bytes 73736 | tf_op jit(solution)/shard_map/ppermute | solution.py:346
  6.5 3.3 %collective-permute-start.2 = (f32[24,256]{1,0:T(8,128)S(1)}, f32[24,256]{1,0:T(8,128)S(1)}, u32[]{:S(2)}, u32[]{:S(2)}) collective-permute-start(f32[24,256]{1,0:T(8,128)S(1)} %get-tuple-element.35), channel_id=1, source_target_pairs={{0,3},{1,2},{2,1},{3,0},{4,7},{5,6},{6,5},{7,4},{8,11},{9,10},{10,... | collective-permute-start | bytes 73736 | tf_op jit(solution)/shard_map/ppermute | solution.py:346
  7.8 6.4 %collective-permute-start.6 = (f32[40,256]{1,0:T(8,128)S(1)}, f32[40,256]{1,0:T(8,128)S(1)}, u32[]{:S(2)}, u32[]{:S(2)}) collective-permute-start(f32[40,256]{1,0:T(8,128)S(1)} %get-tuple-element.38), channel_id=1, source_target_pairs={{0,2},{1,3},{2,0},{3,1},{4,6},{5,7},{6,4},{7,5},{8,10},{9,11},{10,... | collective-permute-start | bytes 122888 | tf_op jit(solution)/shard_map/ppermute | solution.py:430
  9.8 8.6 %collective-permute-start.5 = (f32[72,256]{1,0:T(8,128)S(1)}, f32[72,256]{1,0:T(8,128)S(1)}, u32[]{:S(2)}, u32[]{:S(2)}) collective-permute-start(f32[72,256]{1,0:T(8,128)S(1)} %shard_map.48.own.one.refs_0_), channel_id=1, source_target_pairs={{0,12},{1,13},{2,14},{3,15},{4,8},{5,9},{6,10},{7,11},{8,4},{9,5},... | collective-permute-start | bytes 221192 | tf_op jit(solution)/shard_map/ppermute | solution.py:351
  13.4 6.5 %collective-permute-start.4 = (f32[72,256]{1,0:T(8,128)S(1)}, f32[72,256]{1,0:T(8,128)S(1)}, u32[]{:S(2)}, u32[]{:S(2)}) collective-permute-start(f32[72,256]{1,0:T(8,128)S(1)} %shard_map.48.own.one.refs_0_), channel_id=1, source_target_pairs={{0,8},{1,9},{2,10},{3,11},{4,12},{5,13},{6,14},{7,15},{8,0},{9,1},... | collective-permute-start | bytes 221192 | tf_op jit(solution)/shard_map/ppermute | solution.py:351
  13.4 6.5 %collective-permute-start.3 = (f32[72,256]{1,0:T(8,128)S(1)}, f32[72,256]{1,0:T(8,128)S(1)}, u32[]{:S(2)}, u32[]{:S(2)}) collective-permute-start(f32[72,256]{1,0:T(8,128)S(1)} %shard_map.48.own.one.refs_0_), channel_id=1, source_target_pairs={{0,4},{1,5},{2,6},{3,7},{4,0},{5,1},{6,2},{7,3},{8,12},{9,13},{10,... | collective-permute-start | bytes 221192 | tf_op jit(solution)/shard_map/ppermute | solution.py:351
  14.5 2.6 %collective-permute-start.7 = (f32[40,256]{1,0:T(8,128)S(1)}, f32[40,256]{1,0:T(8,128)S(1)}, u32[]{:S(2)}, u32[]{:S(2)}) collective-permute-start(f32[40,256]{1,0:T(8,128)S(1)} %get-tuple-element.40), channel_id=1, source_target_pairs={{0,1},{1,0},{2,3},{3,2},{4,5},{5,4},{6,7},{7,6},{8,9},{9,8},{10,11... | collective-permute-start | bytes 122888 | tf_op jit(solution)/shard_map/ppermute | solution.py:430
  21.3 6.6 %collective-permute-start.10 = (f32[64,256]{1,0:T(8,128)S(1)}, f32[64,256]{1,0:T(8,128)S(1)}, u32[]{:S(2)}, u32[]{:S(2)}) collective-permute-start(f32[64,256]{1,0:T(8,128)S(1)} %get-tuple-element.41.refs_0_), channel_id=1, source_target_pairs={{0,12},{1,13},{2,14},{3,15},{4,8},{5,9},{6,10},{7,11},{8,4},{9,5},... | collective-permute-start | bytes 196616 | tf_op jit(solution)/shard_map/ppermute | solution.py:351
  23.8 6.3 %collective-permute-start.9 = (f32[64,256]{1,0:T(8,128)S(1)}, f32[64,256]{1,0:T(8,128)S(1)}, u32[]{:S(2)}, u32[]{:S(2)}) collective-permute-start(f32[64,256]{1,0:T(8,128)S(1)} %get-tuple-element.41.refs_0_), channel_id=1, source_target_pairs={{0,8},{1,9},{2,10},{3,11},{4,12},{5,13},{6,14},{7,15},{8,0},{9,1},... | collective-permute-start | bytes 196616 | tf_op jit(solution)/shard_map/ppermute | solution.py:351
  23.8 6.3 %collective-permute-start.8 = (f32[64,256]{1,0:T(8,128)S(1)}, f32[64,256]{1,0:T(8,128)S(1)}, u32[]{:S(2)}, u32[]{:S(2)}) collective-permute-start(f32[64,256]{1,0:T(8,128)S(1)} %get-tuple-element.41.refs_0_), channel_id=1, source_target_pairs={{0,4},{1,5},{2,6},{3,7},{4,0},{5,1},{6,2},{7,3},{8,12},{9,13},{10,... | collective-permute-start | bytes 196616 | tf_op jit(solution)/shard_map/ppermute | solution.py:351
  27.0 4.7 %collective-permute-start.14 = (f32[16,256]{1,0:T(8,128)S(1)}, f32[16,256]{1,0:T(8,128)S(1)}, u32[]{:S(2)}, u32[]{:S(2)}) collective-permute-start(f32[16,256]{1,0:T(8,128)S(1)} %get-tuple-element.53), channel_id=1, source_target_pairs={{0,1},{1,0},{2,3},{3,2},{4,5},{5,4},{6,7},{7,6},{8,9},{9,8},{10,11... | collective-permute-start | bytes 49160 | tf_op jit(solution)/shard_map/ppermute | solution.py:346
  27.1 5.9 %collective-permute-start.15 = (f32[16,256]{1,0:T(8,128)S(1)}, f32[16,256]{1,0:T(8,128)S(1)}, u32[]{:S(2)}, u32[]{:S(2)}) collective-permute-start(f32[16,256]{1,0:T(8,128)S(1)} %get-tuple-element.54), channel_id=1, source_target_pairs={{0,2},{1,3},{2,0},{3,1},{4,6},{5,7},{6,4},{7,5},{8,10},{9,11},{10,... | collective-permute-start | bytes 49160 | tf_op jit(solution)/shard_map/ppermute | solution.py:346
  27.9 5.1 %collective-permute-start.16 = (f32[16,256]{1,0:T(8,128)S(1)}, f32[16,256]{1,0:T(8,128)S(1)}, u32[]{:S(2)}, u32[]{:S(2)}) collective-permute-start(f32[16,256]{1,0:T(8,128)S(1)} %get-tuple-element.55), channel_id=1, source_target_pairs={{0,3},{1,2},{2,1},{3,0},{4,7},{5,6},{6,5},{7,4},{8,11},{9,10},{10,... | collective-permute-start | bytes 49160 | tf_op jit(solution)/shard_map/ppermute | solution.py:346
  30.8 3.5 %collective-permute-start.11 = (f32[16,256]{1,0:T(8,128)S(1)}, f32[16,256]{1,0:T(8,128)S(1)}, u32[]{:S(2)}, u32[]{:S(2)}) collective-permute-start(f32[16,256]{1,0:T(8,128)S(1)} %get-tuple-element.49), channel_id=1, source_target_pairs={{0,1},{1,0},{2,3},{3,2},{4,5},{5,4},{6,7},{7,6},{8,9},{9,8},{10,11... | collective-permute-start | bytes 49160 | tf_op jit(solution)/shard_map/ppermute | solution.py:346
  30.8 3.5 %collective-permute-start.12 = (f32[16,256]{1,0:T(8,128)S(1)}, f32[16,256]{1,0:T(8,128)S(1)}, u32[]{:S(2)}, u32[]{:S(2)}) collective-permute-start(f32[16,256]{1,0:T(8,128)S(1)} %get-tuple-element.50), channel_id=1, source_target_pairs={{0,3},{1,2},{2,1},{3,0},{4,7},{5,6},{6,5},{7,4},{8,11},{9,10},{10,... | collective-permute-start | bytes 49160 | tf_op jit(solution)/shard_map/ppermute | solution.py:346
  31.7 3.7 %collective-permute-start.13 = (f32[16,256]{1,0:T(8,128)S(1)}, f32[16,256]{1,0:T(8,128)S(1)}, u32[]{:S(2)}, u32[]{:S(2)}) collective-permute-start(f32[16,256]{1,0:T(8,128)S(1)} %get-tuple-element.51), channel_id=1, source_target_pairs={{0,2},{1,3},{2,0},{3,1},{4,6},{5,7},{6,4},{7,5},{8,10},{9,11},{10,... | collective-permute-start | bytes 49160 | tf_op jit(solution)/shard_map/ppermute | solution.py:346

commit v34 on v28

--- a/solution.py
+++ b/solution.py
@@ -332,12 +332,14 @@
     outs = column_copies(y, out, sems)
     columns, slots = means.shape
     second = own_means(parts, means)
-    for b in range(len(outs)):
-        at = slice(b * BLOCK, (b + 1) * BLOCK)
-        found = tables[0][:, at] if tables else one_hot(row(mask_ids, b, BLOCK), slots)
+    piece = BLOCK // 2
+    for b in range(2 * len(outs)):
+        at = slice(b * piece, (b + 1) * piece)
+        found = tables[0][:, at] if tables else one_hot(row(mask_ids, b, piece), slots)
         spread = dot(second, found)
         y[:, at] = before[:, at] - (spread[:columns] + spread[columns:])
-        outs[b].start()
+        if b % 2:
+            outs[b // 2].start()
     wait_all(outs)
 
 

time: 36.6 us -> 36.6 us (level)
  no operation moved by 1% of the time
where the time goes in v34:
time: 36.6 us; the launch traced here: 36.4 us
  starting transfers between devices  17.7 us (48%)
  Pallas kernels  15.3 us (42%)
  waiting for transfers between devices  3.32 us (9%)
    ppermute x6, starting transfers between devices, far_share(): return [one] + [lax.ppermute(one, 'rows', step) for step in steps]  8.85 us
    ppermute x9, starting transfers between devices, near_exchange(): lax.ppermute(one, 'rows', step)  6.99 us
    pallas_call x4, Pallas kernels, pair_counts(): call(functools.partial(pairs_kernel, pad, start, 1), [array((1, slots, 2...  4.92 us
    pallas_call x1, Pallas kernels, body(): call(functools.partial(sums_kernel, pad, slots // n), [short, message, sh...  3.37 us
    ppermute x6, waiting for transfers between devices, far_share(): return [one] + [lax.ppermute(one, 'rows', step) for step in steps]  2.42 us
    ppermute x2, starting transfers between devices, near_step(): return lax.ppermute(one, 'rows', [(i, i ^ step) for i in range(n)])  1.87 us
    pallas_call x1, Pallas kernels, body(): call(last_kernel, array(whole, F32), [vmem] * (NEAR + 2 + len(spreads[:1]...  1.61 us
    pallas_call x1, Pallas kernels, body(): call(functools.partial(change_kernel, far, part, len(tables)), [of_near,...  1.37 us
  transfers between devices with their start and end apart: 17, of which 5 were waited for; matrix products, arithmetic and copies ran while one was open for 0% of the time, Pallas kernels for 24%

profile of v34, /device:TPU:0, one launch (start us, length us, event | category | flops | bytes accessed | tf_op | source)
XLA Modules:
  0.0 36.4 jit_solution(14718171338923136378)
XLA Ops:
  0.0 3.4 %shard_map.46 = (f32[24,256]{1,0:T(8,128)S(1)}, f32[56,256]{1,0:T(8,128)S(1)}, f32[24,256]{1,0:T(8,128)S(1)}, f32[24,256]{1,0:T(8,128)S(1)}, f32[40,256]{1,0:T(8...) custom-call(f32[64,8192]{1,0:T(8,128)} %refs_0_.1, s32[8,128]{1,0:T(8,128)} %bitcast.4, ...), custom_call_target="tpu_custom_call" | custom-call | flops 1073741824 | bytes 2097152 | tf_op jit(solution)/shard_map/pallas_call | solution.py:397
  3.4 0.5 %collective-permute-start = (f32[56,256]{1,0:T(8,128)S(1)}, f32[56,256]{1,0:T(8,128)S(1)}, u32[]{:S(2)}, u32[]{:S(2)}) collective-permute-start(f32[56,256]{1,0:T(8,128)S(1)} %get-tuple-element.33), channel_id=1, source_target_pairs={{0,1},{1,0},{2,3},{3,2},{4,5},{5,4},{6,7},{7,6},{8,9},{9,8},{10,11... | collective-permute-start | bytes 172040 | tf_op jit(solution)/shard_map/ppermute | solution.py:348
  3.9 2.6 %collective-permute-start.1 = (f32[24,256]{1,0:T(8,128)S(1)}, f32[24,256]{1,0:T(8,128)S(1)}, u32[]{:S(2)}, u32[]{:S(2)}) collective-permute-start(f32[24,256]{1,0:T(8,128)S(1)} %get-tuple-element.34), channel_id=1, source_target_pairs={{0,2},{1,3},{2,0},{3,1},{4,6},{5,7},{6,4},{7,5},{8,10},{9,11},{10,... | collective-permute-start | bytes 73736 | tf_op jit(solution)/shard_map/ppermute | solution.py:348
  6.5 0.1 collective-permute-start.2
  6.6 1.2 %shard_map.47 = (bf16[1,256,512]{2,1,0:T(8,128)(2,1)S(1)}, f32[40,256]{1,0:T(8,128)S(1)}) custom-call(f32[40,256]{1,0:T(8,128)S(1)} %get-tuple-element.36.refs_0_), custom_call_target="tpu_custom_call" | custom-call | flops 134217728 | bytes 262144 | tf_op jit(solution)/shard_map/pallas_call | solution.py:417
  7.8 1.8 %collective-permute-start.6 = (f32[40,256]{1,0:T(8,128)S(1)}, f32[40,256]{1,0:T(8,128)S(1)}, u32[]{:S(2)}, u32[]{:S(2)}) collective-permute-start(f32[40,256]{1,0:T(8,128)S(1)} %get-tuple-element.38), channel_id=1, source_target_pairs={{0,2},{1,3},{2,0},{3,1},{4,6},{5,7},{6,4},{7,5},{8,10},{9,11},{10,... | collective-permute-start | bytes 122888 | tf_op jit(solution)/shard_map/ppermute | solution.py:432
  9.6 0.0 collective-permute-done.1.refs_2_
  9.6 0.2 collective-permute-done.2.refs_3_
  9.7 0.0 collective-permute-done.refs_1_.refs_0_
  9.8 3.7 %collective-permute-start.5 = (f32[72,256]{1,0:T(8,128)S(1)}, f32[72,256]{1,0:T(8,128)S(1)}, u32[]{:S(2)}, u32[]{:S(2)}) collective-permute-start(f32[72,256]{1,0:T(8,128)S(1)} %shard_map.48.own.one.refs_0_), channel_id=1, source_target_pairs={{0,12},{1,13},{2,14},{3,15},{4,8},{5,9},{6,10},{7,11},{8,4},{9,5},... | collective-permute-start | bytes 221192 | tf_op jit(solution)/shard_map/ppermute | solution.py:353
  13.4 0.0 collective-permute-start.4
  13.4 0.8 %collective-permute-start.3 = (f32[72,256]{1,0:T(8,128)S(1)}, f32[72,256]{1,0:T(8,128)S(1)}, u32[]{:S(2)}, u32[]{:S(2)}) collective-permute-start(f32[72,256]{1,0:T(8,128)S(1)} %shard_map.48.own.one.refs_0_), channel_id=1, source_target_pairs={{0,4},{1,5},{2,6},{3,7},{4,0},{5,1},{6,2},{7,3},{8,12},{9,13},{10,... | collective-permute-start | bytes 221192 | tf_op jit(solution)/shard_map/ppermute | solution.py:353
  14.2 0.0 collective-permute-done.6.passed.refs_0_
  14.2 0.3 shard_map.49
  14.5 0.1 collective-permute-start.7
  14.6 1.2 %shard_map.52.refs_8_ = bf16[1,256,512]{2,1,0:T(8,128)(2,1)S(1)} custom-call(f32[40,256]{1,0:T(8,128)S(1)} %collective-permute-done.6.passed.refs_0_), custom_call_target="tpu_custom_call" | custom-call | flops 134217728 | bytes 262144 | tf_op jit(solution)/shard_map/pallas_call | solution.py:417
  15.8 1.2 %shard_map.51.refs_7_ = bf16[1,256,512]{2,1,0:T(8,128)(2,1)S(1)} custom-call(f32[56,256]{1,0:T(8,128)S(1)} %collective-permute-done.refs_1_.refs_0_), custom_call_target="tpu_custom_call" | custom-call | flops 134217728 | bytes 262144 | tf_op jit(solution)/shard_map/pallas_call | solution.py:417
  17.1 0.0 collective-permute-done.7.refs_0_
  17.1 1.2 %shard_map.53.refs_9_ = bf16[1,256,512]{2,1,0:T(8,128)(2,1)S(1)} custom-call(f32[40,256]{1,0:T(8,128)S(1)} %collective-permute-done.7.refs_0_), custom_call_target="tpu_custom_call" | custom-call | flops 134217728 | bytes 262144 | tf_op jit(solution)/shard_map/pallas_call | solution.py:417
  18.3 0.0 collective-permute-done.5.one.refs_3_
  18.3 0.3 shard_map.50.refs_5_.refs_7_
  18.7 1.3 %collective-permute-done.4.refs_2_ = f32[72,256]{1,0:T(8,128)S(1)} collective-permute-done((f32[72,256]{1,0:T(8,128)S(1)}, f32[72,256]{1,0:T(8,128)S(1)}, u32[]{:S(2)}, u32[]{:S(2)}) %collective-permute-start.4) | collective-permute-done | bytes 73760 | tf_op jit(solution)/shard_map/ppermute | solution.py:353
  19.9 0.0 collective-permute-done.3.refs_1_
  19.9 1.4 %shard_map.54 = (f32[64,256]{1,0:T(8,128)S(1)}, f32[64,256]{1,0:T(8,128)S(1)}, f32[2,8,512]{2,1,0:T(8,128)S(1)}, bf16[2,512,512]{2,1,0:T(8,128)(2,1)S(1)}, bf16[2,512,512]{2,1,0:T(8,128)(2,1)S(1)}) custom-call(f32[72,256]{1,0:T(8,128)S(1)} %shard_map.48.own.one.refs_0_, f32[72,256]{1,0:T(8,128)S(1)} %collective-permute-done.3.refs_1_, ...), custom_call_target="tpu_custom_call" | custom-call | flops 134217728 | bytes 262144 | tf_op jit(solution)/shard_map/pallas_call | solution.py:468
  21.3 2.5 %collective-permute-start.10 = (f32[64,256]{1,0:T(8,128)S(1)}, f32[64,256]{1,0:T(8,128)S(1)}, u32[]{:S(2)}, u32[]{:S(2)}) collective-permute-start(f32[64,256]{1,0:T(8,128)S(1)} %get-tuple-element.41.refs_0_), channel_id=1, source_target_pairs={{0,12},{1,13},{2,14},{3,15},{4,8},{5,9},{6,10},{7,11},{8,4},{9,5},... | collective-permute-start | bytes 196616 | tf_op jit(solution)/shard_map/ppermute | solution.py:353
  23.8 0.0 collective-permute-start.9
  23.8 1.9 %collective-permute-start.8 = (f32[64,256]{1,0:T(8,128)S(1)}, f32[64,256]{1,0:T(8,128)S(1)}, u32[]{:S(2)}, u32[]{:S(2)}) collective-permute-start(f32[64,256]{1,0:T(8,128)S(1)} %get-tuple-element.41.refs_0_), channel_id=1, source_target_pairs={{0,4},{1,5},{2,6},{3,7},{4,0},{5,1},{6,2},{7,3},{8,12},{9,13},{10,... | collective-permute-start | bytes 196616 | tf_op jit(solution)/shard_map/ppermute | solution.py:353
  25.7 1.3 %shard_map.55 = (bf16[256,8192]{1,0:T(8,128)(2,1)S(1)}, bf16[256,8192]{1,0:T(8,128)(2,1)S(1)}, f32[16,256]{1,0:T(8,128)S(1)}, f32[16,256]{1,0:T(8,128)S(1)}, f32...) custom-call(s32[64,128]{1,0:T(8,128)S(1)} %get-tuple-element.45.mask_ids.refs_5_, f32[64,256]{1,0:T(8,128)S(1)} %get-tuple-element.46.mean), custom_call_target="tpu_custom_call" | custom-call | flops 536870912 | bytes 8388608 | tf_op jit(solution)/shard_map/pallas_call | solution.py:482
  27.0 0.1 collective-permute-start.14
  27.1 0.8 %collective-permute-start.15 = (f32[16,256]{1,0:T(8,128)S(1)}, f32[16,256]{1,0:T(8,128)S(1)}, u32[]{:S(2)}, u32[]{:S(2)}) collective-permute-start(f32[16,256]{1,0:T(8,128)S(1)} %get-tuple-element.54), channel_id=1, source_target_pairs={{0,2},{1,3},{2,0},{3,1},{4,6},{5,7},{6,4},{7,5},{8,10},{9,11},{10,... | collective-permute-start | bytes 49160 | tf_op jit(solution)/shard_map/ppermute | solution.py:348
  27.9 0.0 collective-permute-done.10.refs_3_
  27.9 1.0 %collective-permute-start.16 = (f32[16,256]{1,0:T(8,128)S(1)}, f32[16,256]{1,0:T(8,128)S(1)}, u32[]{:S(2)}, u32[]{:S(2)}) collective-permute-start(f32[16,256]{1,0:T(8,128)S(1)} %get-tuple-element.55), channel_id=1, source_target_pairs={{0,3},{1,2},{2,1},{3,0},{4,7},{5,6},{6,5},{7,4},{8,11},{9,10},{10,... | collective-permute-start | bytes 49160 | tf_op jit(solution)/shard_map/ppermute | solution.py:348
  28.9 1.1 %collective-permute-done.9.refs_2_ = f32[64,256]{1,0:T(8,128)S(1)} collective-permute-done((f32[64,256]{1,0:T(8,128)S(1)}, f32[64,256]{1,0:T(8,128)S(1)}, u32[]{:S(2)}, u32[]{:S(2)}) %collective-permute-start.9) | collective-permute-done | bytes 65568 | tf_op jit(solution)/shard_map/ppermute | solution.py:353
  30.1 0.0 collective-permute-done.8.refs_1_
  30.1 0.8 %shard_map.56 = (f32[16,256]{1,0:T(8,128)S(1)}, f32[16,256]{1,0:T(8,128)S(1)}, f32[16,256]{1,0:T(8,128)S(1)}, f32[16,256]{1,0:T(8,128)S(1)}) custom-call(f32[64,256]{1,0:T(8,128)S(1)} %get-tuple-element.41.refs_0_, f32[64,256]{1,0:T(8,128)S(1)} %collective-permute-done.8.refs_1_, f32[64,256]{1,0:T(8,128)S(1)} %collective-permute-done.9.refs_2_, ...), custom_call_target="tpu_custom_call" | custom-call | flops 134217728 | bytes 262144 | tf_op jit(solution)/shard_map/pallas_call | solution.py:493
  30.8 0.0 collective-permute-start.11
  30.8 0.8 %collective-permute-start.12 = (f32[16,256]{1,0:T(8,128)S(1)}, f32[16,256]{1,0:T(8,128)S(1)}, u32[]{:S(2)}, u32[]{:S(2)}) collective-permute-start(f32[16,256]{1,0:T(8,128)S(1)} %get-tuple-element.50), channel_id=1, source_target_pairs={{0,2},{1,3},{2,0},{3,1},{4,6},{5,7},{6,4},{7,5},{8,10},{9,11},{10,... | collective-permute-start | bytes 49160 | tf_op jit(solution)/shard_map/ppermute | solution.py:348
  31.6 0.0 collective-permute-done.14.refs_1_
  31.6 1.1 %collective-permute-start.13 = (f32[16,256]{1,0:T(8,128)S(1)}, f32[16,256]{1,0:T(8,128)S(1)}, u32[]{:S(2)}, u32[]{:S(2)}) collective-permute-start(f32[16,256]{1,0:T(8,128)S(1)} %get-tuple-element.51), channel_id=1, source_target_pairs={{0,3},{1,2},{2,1},{3,0},{4,7},{5,6},{6,5},{7,4},{8,11},{9,10},{10,... | collective-permute-start | bytes 49160 | tf_op jit(solution)/shard_map/ppermute | solution.py:348
  32.7 0.0 collective-permute-done.15.refs_2_
  32.7 0.0 collective-permute-done.16.refs_3_
  32.7 1.3 %shard_map.57.refs_4_ = f32[64,8192]{1,0:T(8,128)S(1)} custom-call(f32[16,256]{1,0:T(8,128)S(1)} %get-tuple-element.52.refs_0_, f32[16,256]{1,0:T(8,128)S(1)} %collective-permute-done.14.refs_1_, f32[16,256]{1,0:T(8,128)S(1)} %collective-permute-done.15.refs_2_, f32[16,256]{1,0:T(8,128)S(1)} %collective-permute-done.16.refs_3_, ...), custom_call_target="tpu_custom_call" | custom-call | flops 536870912 | bytes 4194304 | tf_op jit(solution)/shard_map/pallas_call | solution.py:503
  34.1 0.0 collective-permute-done.11.refs_1_
  34.1 0.6 %collective-permute-done.12.refs_2_ = f32[16,256]{1,0:T(8,128)S(1)} collective-permute-done((f32[16,256]{1,0:T(8,128)S(1)}, f32[16,256]{1,0:T(8,128)S(1)}, u32[]{:S(2)}, u32[]{:S(2)}) %collective-permute-start.12) | collective-permute-done | bytes 16416 | tf_op jit(solution)/shard_map/ppermute | solution.py:348
  34.6 0.1 collective-permute-done.13.refs_3_
  34.8 1.6 %shard_map.58 = f32[64,8192]{1,0:T(8,128)} custom-call(f32[16,256]{1,0:T(8,128)S(1)} %get-tuple-element.48.refs_0_, f32[16,256]{1,0:T(8,128)S(1)} %collective-permute-done.11.refs_1_, f32[16,256]{1,0:T(8,128)S(1)} %collective-permute-done.12.refs_2_, f32[16,256]{1,0:T(8,128)S(1)} %collective-permute-done.13.refs_3_, f32[64,8192]{1,0:T(8,128)S(1)} %shard_map.57.refs_4_, ...), custom_call_target="tpu_custom_call" | custom-call | flops 536870912 | bytes 4194304 | tf_op jit(solution)/shard_map/pallas_call | solution.py:512
  (1 shorter events, 0.0 us)
Async XLA Ops:
  3.4 6.4 %collective-permute-start = (f32[56,256]{1,0:T(8,128)S(1)}, f32[56,256]{1,0:T(8,128)S(1)}, u32[]{:S(2)}, u32[]{:S(2)}) collective-permute-start(f32[56,256]{1,0:T(8,128)S(1)} %get-tuple-element.33), channel_id=1, source_target_pairs={{0,1},{1,0},{2,3},{3,2},{4,5},{5,4},{6,7},{7,6},{8,9},{9,8},{10,11... | collective-permute-start | bytes 172040 | tf_op jit(solution)/shard_map/ppermute | solution.py:348
  3.9 5.7 %collective-permute-start.1 = (f32[24,256]{1,0:T(8,128)S(1)}, f32[24,256]{1,0:T(8,128)S(1)}, u32[]{:S(2)}, u32[]{:S(2)}) collective-permute-start(f32[24,256]{1,0:T(8,128)S(1)} %get-tuple-element.34), channel_id=1, source_target_pairs={{0,2},{1,3},{2,0},{3,1},{4,6},{5,7},{6,4},{7,5},{8,10},{9,11},{10,... | collective-permute-start | bytes 73736 | tf_op jit(solution)/shard_map/ppermute | solution.py:348
  6.5 3.3 %collective-permute-start.2 = (f32[24,256]{1,0:T(8,128)S(1)}, f32[24,256]{1,0:T(8,128)S(1)}, u32[]{:S(2)}, u32[]{:S(2)}) collective-permute-start(f32[24,256]{1,0:T(8,128)S(1)} %get-tuple-element.35), channel_id=1, source_target_pairs={{0,3},{1,2},{2,1},{3,0},{4,7},{5,6},{6,5},{7,4},{8,11},{9,10},{10,... | collective-permute-start | bytes 73736 | tf_op jit(solution)/shard_map/ppermute | solution.py:348
  7.8 6.4 %collective-permute-start.6 = (f32[40,256]{1,0:T(8,128)S(1)}, f32[40,256]{1,0:T(8,128)S(1)}, u32[]{:S(2)}, u32[]{:S(2)}) collective-permute-start(f32[40,256]{1,0:T(8,128)S(1)} %get-tuple-element.38), channel_id=1, source_target_pairs={{0,2},{1,3},{2,0},{3,1},{4,6},{5,7},{6,4},{7,5},{8,10},{9,11},{10,... | collective-permute-start | bytes 122888 | tf_op jit(solution)/shard_map/ppermute | solution.py:432
  9.8 8.6 %collective-permute-start.5 = (f32[72,256]{1,0:T(8,128)S(1)}, f32[72,256]{1,0:T(8,128)S(1)}, u32[]{:S(2)}, u32[]{:S(2)}) collective-permute-start(f32[72,256]{1,0:T(8,128)S(1)} %shard_map.48.own.one.refs_0_), channel_id=1, source_target_pairs={{0,12},{1,13},{2,14},{3,15},{4,8},{5,9},{6,10},{7,11},{8,4},{9,5},... | collective-permute-start | bytes 221192 | tf_op jit(solution)/shard_map/ppermute | solution.py:353
  13.4 6.5 %collective-permute-start.4 = (f32[72,256]{1,0:T(8,128)S(1)}, f32[72,256]{1,0:T(8,128)S(1)}, u32[]{:S(2)}, u32[]{:S(2)}) collective-permute-start(f32[72,256]{1,0:T(8,128)S(1)} %shard_map.48.own.one.refs_0_), channel_id=1, source_target_pairs={{0,8},{1,9},{2,10},{3,11},{4,12},{5,13},{6,14},{7,15},{8,0},{9,1},... | collective-permute-start | bytes 221192 | tf_op jit(solution)/shard_map/ppermute | solution.py:353
  13.4 6.5 %collective-permute-start.3 = (f32[72,256]{1,0:T(8,128)S(1)}, f32[72,256]{1,0:T(8,128)S(1)}, u32[]{:S(2)}, u32[]{:S(2)}) collective-permute-start(f32[72,256]{1,0:T(8,128)S(1)} %shard_map.48.own.one.refs_0_), channel_id=1, source_target_pairs={{0,4},{1,5},{2,6},{3,7},{4,0},{5,1},{6,2},{7,3},{8,12},{9,13},{10,... | collective-permute-start | bytes 221192 | tf_op jit(solution)/shard_map/ppermute | solution.py:353
  14.5 2.6 %collective-permute-start.7 = (f32[40,256]{1,0:T(8,128)S(1)}, f32[40,256]{1,0:T(8,128)S(1)}, u32[]{:S(2)}, u32[]{:S(2)}) collective-permute-start(f32[40,256]{1,0:T(8,128)S(1)} %get-tuple-element.40), channel_id=1, source_target_pairs={{0,1},{1,0},{2,3},{3,2},{4,5},{5,4},{6,7},{7,6},{8,9},{9,8},{10,11... | collective-permute-start | bytes 122888 | tf_op jit(solution)/shard_map/ppermute | solution.py:432
  21.3 6.6 %collective-permute-start.10 = (f32[64,256]{1,0:T(8,128)S(1)}, f32[64,256]{1,0:T(8,128)S(1)}, u32[]{:S(2)}, u32[]{:S(2)}) collective-permute-start(f32[64,256]{1,0:T(8,128)S(1)} %get-tuple-element.41.refs_0_), channel_id=1, source_target_pairs={{0,12},{1,13},{2,14},{3,15},{4,8},{5,9},{6,10},{7,11},{8,4},{9,5},... | collective-permute-start | bytes 196616 | tf_op jit(solution)/shard_map/ppermute | solution.py:353
  23.8 6.3 %collective-permute-start.9 = (f32[64,256]{1,0:T(8,128)S(1)}, f32[64,256]{1,0:T(8,128)S(1)}, u32[]{:S(2)}, u32[]{:S(2)}) collective-permute-start(f32[64,256]{1,0:T(8,128)S(1)} %get-tuple-element.41.refs_0_), channel_id=1, source_target_pairs={{0,8},{1,9},{2,10},{3,11},{4,12},{5,13},{6,14},{7,15},{8,0},{9,1},... | collective-permute-start | bytes 196616 | tf_op jit(solution)/shard_map/ppermute | solution.py:353
  23.8 6.3 %collective-permute-start.8 = (f32[64,256]{1,0:T(8,128)S(1)}, f32[64,256]{1,0:T(8,128)S(1)}, u32[]{:S(2)}, u32[]{:S(2)}) collective-permute-start(f32[64,256]{1,0:T(8,128)S(1)} %get-tuple-element.41.refs_0_), channel_id=1, source_target_pairs={{0,4},{1,5},{2,6},{3,7},{4,0},{5,1},{6,2},{7,3},{8,12},{9,13},{10,... | collective-permute-start | bytes 196616 | tf_op jit(solution)/shard_map/ppermute | solution.py:353
  27.0 4.6 %collective-permute-start.14 = (f32[16,256]{1,0:T(8,128)S(1)}, f32[16,256]{1,0:T(8,128)S(1)}, u32[]{:S(2)}, u32[]{:S(2)}) collective-permute-start(f32[16,256]{1,0:T(8,128)S(1)} %get-tuple-element.53), channel_id=1, source_target_pairs={{0,1},{1,0},{2,3},{3,2},{4,5},{5,4},{6,7},{7,6},{8,9},{9,8},{10,11... | collective-permute-start | bytes 49160 | tf_op jit(solution)/shard_map/ppermute | solution.py:348
  27.1 5.7 %collective-permute-start.15 = (f32[16,256]{1,0:T(8,128)S(1)}, f32[16,256]{1,0:T(8,128)S(1)}, u32[]{:S(2)}, u32[]{:S(2)}) collective-permute-start(f32[16,256]{1,0:T(8,128)S(1)} %get-tuple-element.54), channel_id=1, source_target_pairs={{0,2},{1,3},{2,0},{3,1},{4,6},{5,7},{6,4},{7,5},{8,10},{9,11},{10,... | collective-permute-start | bytes 49160 | tf_op jit(solution)/shard_map/ppermute | solution.py:348
  27.9 4.8 %collective-permute-start.16 = (f32[16,256]{1,0:T(8,128)S(1)}, f32[16,256]{1,0:T(8,128)S(1)}, u32[]{:S(2)}, u32[]{:S(2)}) collective-permute-start(f32[16,256]{1,0:T(8,128)S(1)} %get-tuple-element.55), channel_id=1, source_target_pairs={{0,3},{1,2},{2,1},{3,0},{4,7},{5,6},{6,5},{7,4},{8,11},{9,10},{10,... | collective-permute-start | bytes 49160 | tf_op jit(solution)/shard_map/ppermute | solution.py:348
  30.8 3.2 %collective-permute-start.11 = (f32[16,256]{1,0:T(8,128)S(1)}, f32[16,256]{1,0:T(8,128)S(1)}, u32[]{:S(2)}, u32[]{:S(2)}) collective-permute-start(f32[16,256]{1,0:T(8,128)S(1)} %get-tuple-element.49), channel_id=1, source_target_pairs={{0,1},{1,0},{2,3},{3,2},{4,5},{5,4},{6,7},{7,6},{8,9},{9,8},{10,11... | collective-permute-start | bytes 49160 | tf_op jit(solution)/shard_map/ppermute | solution.py:348
  30.8 3.8 %collective-permute-start.12 = (f32[16,256]{1,0:T(8,128)S(1)}, f32[16,256]{1,0:T(8,128)S(1)}, u32[]{:S(2)}, u32[]{:S(2)}) collective-permute-start(f32[16,256]{1,0:T(8,128)S(1)} %get-tuple-element.50), channel_id=1, source_target_pairs={{0,2},{1,3},{2,0},{3,1},{4,6},{5,7},{6,4},{7,5},{8,10},{9,11},{10,... | collective-permute-start | bytes 49160 | tf_op jit(solution)/shard_map/ppermute | solution.py:348
  31.6 3.2 %collective-permute-start.13 = (f32[16,256]{1,0:T(8,128)S(1)}, f32[16,256]{1,0:T(8,128)S(1)}, u32[]{:S(2)}, u32[]{:S(2)}) collective-permute-start(f32[16,256]{1,0:T(8,128)S(1)} %get-tuple-element.51), channel_id=1, source_target_pairs={{0,3},{1,2},{2,1},{3,0},{4,7},{5,6},{6,5},{7,4},{8,11},{9,10},{10,... | collective-permute-start | bytes 49160 | tf_op jit(solution)/shard_map/ppermute | solution.py:348
